TPU v7x, 32 devices: a whole 2x2x4 slice. The times are simulated.
32 devices in a mesh: kx: 4 (over z), ht: 2 (over y), real: 4 (over x, core).
Axes of the slice: x: 2, y: 2, z: 4, core: 2. Of those that a mesh axis runs over, the one named last changes fastest.
Arguments:
- velocity: float32 [3, 4, 16, 512, 128], P(None, 'real', 'kx', 'ht'), may hold values from -6 to 6
- low_index: int32 [8], replicated, may hold values from 0 to 15, as said below
- neighbours: int32 [16, 8], P('kx'), may hold values from 0 to 15, as said below
- owner_map: int32 [64], replicated, may hold values from 0 to 63, each once
- mode_counts: int32 [16], P('kx'), may hold values from 16 to 64
- helmholtz: float32 [64, 512, 512], P(('kx', 'ht')), may hold values from -0.25 to 0.25
Outputs:
- velocity_next: float32 [3, 4, 16, 512, 128], P(None, 'real', 'kx', 'ht')
Inputs may be any that keep to these rules, and one draw needn't show every extreme that they name: `low_index`: distinct values. neighbours[m, j] lies within 4 modes of m, counting circularly over the 16 modes; offsets of + 4 and - 4 both occur.
All inputs are finite; a program needn't handle non-finite values.
Results may differ from a plain program's by a relative error of at most 0.0001.
Values sent between devices are 32-bit elements; how exact they have to be, the bound alone decides.
No kernel may reach another device: no remote copies, remote signals or barrier semaphores. Data moves between devices by JAX's collectives and lax.ppermute only.
A program may use at most 128 MiB of HBM per device.

v0:
```python
import functools

import jax
import jax.numpy as jnp
from jax import lax
from jax.experimental import pallas as pl
from jax.experimental.pallas import tpu as pltpu
from jax.sharding import PartitionSpec as P

dt_step = 0.1


def spanwise_tables(mode_count, point_count):
    column_ids = jnp.arange(2 * mode_count)
    wavenumber = (column_ids // 2).astype(jnp.float32)
    imag_part = column_ids % 2
    positions = 2.0 * jnp.pi * jnp.arange(point_count).astype(jnp.float32) / point_count
    phases = wavenumber[:, None] * positions[None, :]
    forward = jnp.where(imag_part[:, None] == 0, jnp.cos(phases), -jnp.sin(phases)) / jnp.sqrt(
        jnp.float32(mode_count)
    )
    backward = forward.T * (2.0 * mode_count / point_count)
    return (forward, backward)


def nonlinear_rows(fields, low_index, neighbours, mode_counts, forward, backward):
    precision = lax.Precision.HIGH
    realizations, modes, columns = (fields.shape[1], fields.shape[2], fields.shape[4])
    low_select = (low_index[:, None] == jnp.arange(modes)[None, :]).astype(jnp.float32)
    high_mask = 1.0 - jnp.sum(low_select, axis=0)
    high_rows = high_mask[None, None, :, None, None]
    column_mask = ((jnp.arange(columns) // 2)[None, :] < mode_counts[:, None]).astype(jnp.float32)
    physical = jnp.dot(fields, forward, precision=precision)
    low_fields = jnp.take(physical, low_index, axis=2)
    high_low = jnp.zeros_like(physical)
    stresses = []
    for member in range(low_index.shape[0]):
        partner = jnp.take(physical, neighbours[:, member], axis=2)
        low_one = low_fields[:, :, member : member + 1]
        high_low = high_low + low_one * partner[1:2] + partner * low_one[1:2]
        stresses.append(jnp.sum(physical * (partner[1:2] * high_rows), axis=(1, 2)))
    stress = jnp.stack(stresses, axis=1) / realizations
    forcing = jnp.dot(high_low, backward, precision=precision) * high_rows
    low_forcing = jnp.dot(stress, backward, precision=precision)
    low_rows = jnp.einsum("jm,cjyk->cmyk", low_select, low_forcing, precision=lax.Precision.HIGHEST)
    forcing = (forcing + low_rows[:, None]) * column_mask[None, None, :, None, :]
    return fields + dt_step * forcing


def local_plain(velocity, low_index, neighbours, owner_map, mode_counts, helmholtz):
    components, reals_dev, band_modes, rows_ht, columns = velocity.shape
    kz_modes = columns // 2
    forward, backward = spanwise_tables(kz_modes, 4 * kz_modes)
    kx_count, ht_count = (lax.axis_size("kx"), lax.axis_size("ht"))
    real_count = lax.axis_size("real")
    modes, realizations = (band_modes * kx_count, reals_dev * real_count)
    slots_dev = kz_modes // (kx_count * ht_count)
    rows_dev = rows_ht // (kx_count * real_count)
    small = jnp.concatenate([neighbours, mode_counts[:, None]], axis=1)
    small = lax.all_gather(small, "kx", axis=0, tiled=True)
    neighbours, mode_counts = (small[:, :-1], small[:, -1])
    inverse_map = (
        jnp.zeros((kz_modes,), jnp.int32).at[owner_map].set(jnp.arange(kz_modes, dtype=jnp.int32))
    )
    split = velocity.reshape(
        components, reals_dev, band_modes, kx_count * real_count, rows_dev, columns
    )
    split = split.transpose(3, 0, 1, 2, 4, 5)
    split = lax.all_to_all(split, ("kx", "real"), split_axis=0, concat_axis=0, tiled=True)
    fields = split.reshape(
        kx_count, real_count, components, reals_dev, band_modes, rows_dev, columns
    )
    fields = fields.transpose(2, 1, 3, 0, 4, 5, 6).reshape(
        components, realizations, modes, rows_dev, columns
    )
    updated = nonlinear_rows(fields, low_index, neighbours, mode_counts, forward, backward)
    slotted = jnp.take(
        updated.reshape(components, realizations, modes, rows_dev, kz_modes, 2), owner_map, axis=4
    )
    slotted = slotted.reshape(
        components, real_count, reals_dev, modes, rows_dev, kx_count * ht_count, slots_dev, 2
    )
    outgoing = slotted.transpose(5, 1, 6, 2, 0, 3, 7, 4).reshape(
        kx_count * ht_count * real_count, slots_dev, reals_dev * components * modes * 2, rows_dev
    )
    incoming = lax.all_to_all(
        outgoing, ("kx", "ht", "real"), split_axis=0, concat_axis=0, tiled=True
    )
    incoming = incoming.reshape(
        kx_count, ht_count, real_count, slots_dev, reals_dev * components * modes * 2, rows_dev
    )
    incoming = incoming.transpose(3, 4, 1, 0, 2, 5).reshape(
        slots_dev, reals_dev * components * modes * 2, ht_count * rows_ht
    )
    solved = jnp.einsum("syx,snx->sny", helmholtz, incoming, precision=lax.Precision.HIGH)
    solved = solved.reshape(
        slots_dev, reals_dev, components, kx_count, band_modes, 2, ht_count, rows_ht
    )
    solved = solved.transpose(3, 6, 0, 5, 1, 2, 4, 7).reshape(
        kx_count * ht_count, slots_dev * 2, reals_dev * components * band_modes, rows_ht
    )
    returned = lax.all_to_all(solved, ("kx", "ht"), split_axis=0, concat_axis=0, tiled=True)
    restored = returned.reshape(
        kz_modes, 2, reals_dev, components, band_modes, rows_ht
    )
    restored = jnp.take(restored, inverse_map, axis=0)
    return restored.transpose(3, 2, 4, 5, 0, 1).reshape(velocity.shape)


LANES = 128
PIECES = 1
VMEM = pl.BlockSpec(memory_space=pltpu.VMEM)
SMEM = pl.BlockSpec(memory_space=pltpu.SMEM)


def params():
    return pltpu.CompilerParams(vmem_limit_bytes=48 * 1024 * 1024)


def two_parts(value):
    top = value.astype(jnp.bfloat16)
    rest = (value - top.astype(jnp.float32)).astype(jnp.bfloat16)
    return top, rest


def dot(left, right, dims=((1,), (0,))):
    return lax.dot_general(left, right, (dims, ((), ())), preferred_element_type=jnp.float32)


def nonlinear_kernel(
    low_ref, near_ref, block_ref, first_ref, second_ref, back_ref, mask_ref,
    slotted_ref, stress_ref, physical, products, sums, high_ref,
):
    bands, components, band_modes, rows, columns = block_ref.shape
    modes, points = (bands * band_modes, physical.shape[3])
    members, highs = (stress_ref.shape[1], products.shape[1])
    found = jnp.int32(0)
    for mode in range(modes):
        is_low = jnp.int32(0)
        for member in range(members):
            is_low = is_low | (low_ref[member] == mode).astype(jnp.int32)
        high_ref[found] = mode
        found = found + 1 - is_low

    def transform(step, carry):
        band, component = (step // components, step % components)
        top, rest = two_parts(block_ref[band, component].reshape(band_modes * rows, columns))
        both = dot(jnp.concatenate([top, rest], axis=1), first_ref[...])
        fields = both[:, :points] + dot(top, second_ref[...])
        place = pl.ds(band * band_modes, band_modes)
        physical[component, place] = fields.reshape(band_modes, rows, points)
        slotted_ref[component, place] = both[:, points:].reshape(band_modes, rows, columns)
        return carry

    lax.fori_loop(0, bands * components, transform, 0)

    def pairs(step, carry):
        halves = points // LANES
        place = (
            pl.ds(pl.multiple_of((step // halves) * 8, 8), 8),
            pl.ds(pl.multiple_of((step % halves) * LANES, LANES), LANES),
        )

        def one_high(index, totals):
            mode = high_ref[index]
            own = [physical[(c, mode) + place] for c in range(components)]
            result = [jnp.zeros((8, LANES), jnp.float32) for _ in range(components)]
            totals = list(totals)
            for member in range(members):
                low = low_ref[member]
                near = near_ref[mode, member]
                partner = [physical[(c, near) + place] for c in range(components)]
                low_one = [physical[(c, low) + place] for c in range(components)]
                for c in range(components):
                    if c == 1:
                        result[c] = result[c] + low_one[1] * partner[1]
                    else:
                        result[c] = result[c] + (low_one[c] * partner[1] + partner[c] * low_one[1])
                    slot = member * components + c
                    totals[slot] = totals[slot] + own[c] * partner[1]
            for c in range(components):
                products[(c, index) + place] = result[c] * 2.0 if c == 1 else result[c]
            return tuple(totals)

        empty = tuple(jnp.zeros((8, LANES), jnp.float32) for _ in range(members * components))
        totals = lax.fori_loop(0, highs, one_high, empty)
        for member in range(members):
            for c in range(components):
                sums[(c, member) + place] = totals[member * components + c]
        return carry

    lax.fori_loop(0, (rows // 8) * (points // LANES), pairs, 0)

    def inverse(fields):
        top, rest = two_parts(fields)
        both = dot(top, back_ref[...])
        return both[:, :columns] + both[:, columns:] + dot(rest, back_ref[:, :columns])

    def finish(component, carry):
        forcing = inverse(products[component].reshape(highs * rows, points))
        forcing = forcing.reshape(highs, rows, columns)
        for index in range(highs):
            mode = high_ref[index]
            slotted_ref[component, mode] += forcing[index] * mask_ref[mode]
        stress = inverse(sums[component].reshape(members * rows, points))
        stress_ref[component] = stress.reshape(members, rows, columns)
        return carry

    lax.fori_loop(0, components, finish, 0)


def nonlinear(block, low_index, neighbours, tables, mask):
    bands, components, band_modes, rows, columns = block.shape
    members, modes, points = (low_index.shape[0], bands * band_modes, 2 * columns)
    highs = modes - members
    return pl.pallas_call(
        nonlinear_kernel,
        out_shape=(
            jax.ShapeDtypeStruct((components, modes, rows, columns), jnp.float32),
            jax.ShapeDtypeStruct((components, members, rows, columns), jnp.float32),
        ),
        in_specs=[SMEM, SMEM] + [VMEM] * 5,
        out_specs=(VMEM, VMEM),
        scratch_shapes=[
            pltpu.VMEM((components, modes, rows, points), jnp.float32),
            pltpu.VMEM((components, highs, rows, points), jnp.float32),
            pltpu.VMEM((components, members, rows, points), jnp.float32),
            pltpu.SMEM((modes + 1,), jnp.int32),
        ],
        compiler_params=params(),
        name="nonlinear",
    )(low_index, neighbours, block, *tables, mask)


def outgoing_kernel(low_ref, slotted_ref, stress_ref, mask_ref, out_ref, full, *, groups, owners):
    components, modes, rows, columns = slotted_ref.shape
    members = stress_ref.shape[1]
    per_slot = out_ref.shape[0] // (columns // 2)
    full[...] = slotted_ref[...]
    for member in range(members):
        mode = low_ref[member]
        for c in range(components):
            full[c, mode] += stress_ref[c, member] * mask_ref[mode]
    inner = modes // groups
    for c in range(components):
        for part in range(inner):
            tile = jnp.concatenate([full[c, part + inner * g] for g in range(groups)], axis=0)
            turned = tile.T
            band_low, band_mode = (part // owners["band"], part % owners["band"])
            for p in range(2):
                row = ((band_low * 2 + p) * components + c) * owners["band"] + band_mode
                out_ref[pl.ds(row, columns // 2, stride=per_slot), :] = turned[
                    p * (columns // 2) : (p + 1) * (columns // 2)
                ]


def outgoing(slotted, stress, low_index, mask, groups, band_modes):
    components, modes, rows, columns = slotted.shape
    per_slot = (modes // groups) * 2 * components
    return pl.pallas_call(
        functools.partial(outgoing_kernel, groups=groups, owners={"band": band_modes}),
        out_shape=jax.ShapeDtypeStruct((columns // 2 * per_slot, groups * rows), jnp.float32),
        in_specs=[SMEM, VMEM, VMEM, VMEM],
        out_specs=VMEM,
        scratch_shapes=[pltpu.VMEM(slotted.shape, jnp.float32)],
        compiler_params=params(),
        name="outgoing",
    )(low_index, slotted, stress, mask)


def regroup(blocks, rows):
    count = len(blocks)
    lane = lax.broadcasted_iota(jnp.int32, blocks[0].shape, 1) // rows
    step = 1
    while step < count:
        take = (lane & step) == 0
        for i in range(count):
            if i & step == 0:
                here, there = (blocks[i], blocks[i + step])
                blocks[i] = jnp.where(take, here, pltpu.roll(there, step * rows, 1))
                blocks[i + step] = jnp.where(
                    take, pltpu.roll(here, LANES - step * rows, 1), there
                )
        step *= 2
    return blocks


def solve_kernel(*refs, groups, kx_count, ht_count):
    pieces = len(refs) - 2
    block_refs, matrix_ref, out_ref = (refs[:pieces], refs[pieces], refs[pieces + 1])
    rows = LANES // groups
    tiles = []
    for h in range(ht_count):
        for piece in range(pieces):
            for first in range(0, kx_count, groups):
                blocks = [
                    block_refs[piece][(first + g) * ht_count + h, 0] for g in range(groups)
                ]
                tiles.append(jnp.concatenate(regroup(blocks, rows), axis=0))
    top, rest = two_parts(jnp.concatenate(tiles, axis=1))
    count = top.shape[0]
    matrix_top, matrix_rest = two_parts(matrix_ref[0])
    last = ((1,), (1,))
    both = dot(jnp.concatenate([top, rest], axis=0), matrix_top, last)
    solved = both[:count] + both[count:] + dot(top, matrix_rest, last)
    lane_tiles, per_band = out_ref.shape[2:4]
    for band in range(kx_count):
        for tile in range(ht_count * lane_tiles):
            out_ref[band * ht_count + tile // lane_tiles, 0, tile % lane_tiles] = solved[
                band * per_band : (band + 1) * per_band, tile * LANES : (tile + 1) * LANES
            ]


def solve(blocks, helmholtz, groups, kx_count, ht_count):
    owners, slots, per_slot, lanes = blocks[0].shape
    heights = helmholtz.shape[1]
    lane_tiles = heights // ht_count // LANES
    out = (owners, slots, lane_tiles, per_slot * groups // kx_count, LANES)
    return pl.pallas_call(
        functools.partial(solve_kernel, groups=groups, kx_count=kx_count, ht_count=ht_count),
        out_shape=jax.ShapeDtypeStruct(out, jnp.float32),
        grid=(slots,),
        in_specs=[pl.BlockSpec((owners, 1, per_slot, lanes), lambda s: (0, s, 0, 0))] * len(blocks)
        + [pl.BlockSpec((1, heights, heights), lambda s: (s, 0, 0))],
        out_specs=pl.BlockSpec((owners, 1) + out[2:], lambda s: (0, s, 0, 0, 0)),
        compiler_params=params(),
        name="solve",
    )(*blocks, helmholtz)


def restore_kernel(block_ref, order_ref, out_ref):
    components, band_modes, rows, columns = out_ref.shape
    slots = columns // 2
    per_slot = block_ref.shape[0] // slots
    for c in range(components):
        for mode in range(band_modes):
            for tile in range(rows // LANES):
                parts = []
                for p in range(2):
                    row = ((tile * 2 + p) * components + c) * band_modes + mode
                    parts.append(block_ref[pl.ds(row, slots, stride=per_slot), :])
                top, rest = two_parts(jnp.concatenate(parts, axis=0))
                both = jnp.concatenate([top, rest], axis=0)
                out_ref[c, mode, pl.ds(tile * LANES, LANES)] = dot(
                    both, order_ref[...], ((0,), (0,))
                )


def restore(block, order, components, band_modes, rows):
    columns = order.shape[1]
    return pl.pallas_call(
        restore_kernel,
        out_shape=jax.ShapeDtypeStruct((components, band_modes, rows, columns), jnp.float32),
        in_specs=[VMEM, VMEM],
        out_specs=VMEM,
        compiler_params=params(),
        name="restore",
    )(block, order)


def table_parts(value):
    top = lax.reduce_precision(value, 8, 7)
    return top.astype(jnp.bfloat16), (value - top).astype(jnp.bfloat16)


def slot_tables(owner_map, mode_counts, columns, realizations):
    forward, backward = spanwise_tables(columns // 2, 2 * columns)
    slot_columns = (2 * owner_map[None, :] + jnp.arange(2)[:, None]).reshape(columns)
    select = slot_columns[None, :] == jnp.arange(columns)[:, None]
    forward_top, forward_rest = table_parts(forward)
    first = jnp.concatenate([forward_top, select.astype(jnp.bfloat16)], axis=1)
    first = jnp.concatenate([first, first], axis=0)
    slotted_back = jnp.dot(
        backward, select.astype(jnp.float32), precision=lax.Precision.HIGHEST
    )
    back = jnp.concatenate(table_parts(slotted_back), axis=1)
    active = (slot_columns // 2)[None, :] < mode_counts[:, None]
    mask = jnp.where(active, jnp.float32(dt_step), 0.0)[:, None, :]
    order = select.T.astype(jnp.bfloat16)
    order = jnp.concatenate([order, order], axis=0)
    return (first, forward_rest, back), mask, mask / realizations, order


def local(velocity, low_index, neighbours, owner_map, mode_counts, helmholtz):
    components, reals_dev, band_modes, rows_ht, columns = velocity.shape
    kx_count, ht_count = (lax.axis_size("kx"), lax.axis_size("ht"))
    owners, pieces = (kx_count * ht_count, PIECES)
    rows = rows_ht // (kx_count * pieces)
    groups = LANES // rows if rows else 0
    slots = columns // 2 // owners
    if (
        columns != LANES or reals_dev != 1 or rows_ht % LANES or rows % 8 or LANES % rows or kx_count % groups
        or (band_modes * 2 * components) % 8 or slots % 8 or low_index.shape[0] >= kx_count * band_modes
    ):
        return local_plain(velocity, low_index, neighbours, owner_map, mode_counts, helmholtz)
    realizations = lax.axis_size("real")
    small = jnp.concatenate([neighbours, mode_counts[:, None]], axis=1)
    small = lax.all_gather(small, "kx", axis=0, tiled=True)
    neighbours, mode_counts = (small[:, :-1], small[:, -1])
    tables, mask, low_mask, order = slot_tables(owner_map, mode_counts, columns, realizations)
    split = velocity.reshape(components, band_modes, pieces, kx_count, rows, columns)
    received = []
    for piece in range(pieces):
        part = split[:, :, piece].transpose(2, 0, 1, 3, 4)
        part = lax.all_to_all(part, "kx", split_axis=0, concat_axis=0, tiled=True)
        slotted, stress = nonlinear(part, low_index, neighbours, tables, mask)
        stress = lax.psum(stress, "real")
        block = outgoing(slotted, stress, low_index, low_mask, groups, band_modes)
        block = block.reshape(owners, slots, -1, LANES)
        received.append(
            lax.all_to_all(block, ("kx", "ht"), split_axis=0, concat_axis=0, tiled=True)
        )
    solved = solve(received, helmholtz, groups, kx_count, ht_count)
    returned = lax.all_to_all(solved, ("kx", "ht"), split_axis=0, concat_axis=0, tiled=True)
    result = restore(returned.reshape(-1, LANES), order, components, band_modes, rows_ht)
    return result.reshape(velocity.shape)


def solution(mesh):
    in_specs = (
        P(None, "real", "kx", "ht", None),
        P(),
        P("kx", None),
        P(),
        P("kx"),
        P(("kx", "ht"), None, None),
    )
    out_specs = P(None, "real", "kx", "ht", None)
    return jax.shard_map(local, mesh=mesh, in_specs=in_specs, out_specs=out_specs, check_vma=False)
```

profile of v0, /device:TPU:0, one launch (start us, length us, event | category | flops | bytes accessed | tf_op | source)
XLA Modules:
  0.0 208.9 jit_solution(10543714883715808730)
XLA Ops:
  6.5 2.7 %copy.23 = f32[3,4,4,64,128]{4,3,1,0,2:T(8,128)} copy(f32[3,4,4,64,128]{4,3,2,1,0:T(8,128)} %bitcast.18) | data formatting | bytes 3145728 | tf_op jit(solution)/shard_map/squeeze;reshape | solution.py:404
  9.3 0.0 copy-start.8
  9.3 0.0 copy-start.7
  9.3 0.0 copy-start.6
  9.3 6.4 %all-to-all-start = ((f32[4,3,4,64,128]{4,3,2,1,0:T(8,128)}), f32[4,3,4,64,128]{4,3,2,1,0:T(8,128)S(1)}, u32[]{:S(2)}, u32[]{:S(2)}) async-start(f32[4,3,4,64,128]{4,3,2,1,0:T(8,128)} %bitcast.12), calls=%async_computation | async-start | bytes 3145728 | tf_op jit(solution)/shard_map/all_to_all | solution.py:405
  15.7 0.0 all-reduce.2.cloned.1.call-start
  15.7 0.0 copy-done.8
  15.7 0.1 add.54
  15.8 0.0 copy-done.7
  15.8 0.1 copy.16
  15.9 0.0 copy-done.6
  15.9 0.1 add_bitcast_fusion
  16.0 42.0 %all-gather = s32[4,4,9]{2,1,0:T(4,128)S(1)} all-gather(s32[1,4,9]{2,1,0:T(4,128)S(1)} %add_bitcast_fusion), channel_id=1, replica_groups=mesh['kx'=4,'ht'=2,'real'=4] {'kx'}, dimensions={0}, use_global_device_ids=true | all-gather | bytes 720 | tf_op jit(solution)/shard_map/all_gather | solution.py:398
  58.0 0.2 slice_reduce_fusion
  58.2 0.7 reduce-precision_convert_fusion
  59.0 0.7 iota_compare_fusion
  59.7 0.6 fusion.3
  60.3 0.7 broadcast_multiply_fusion
  61.0 0.0 all-to-all-done.block_ref
  61.0 0.0 copy-start.2
  61.0 0.7 copy-done.2
  61.7 0.0 copy-start.3
  61.7 0.7 copy-done.3
  62.3 10.4 %nonlinear.1 = (f32[3,16,64,128]{3,2,1,0:T(8,128)S(1)}, f32[3,8,64,128]{3,2,1,0:T(8,128)S(1)}) custom-call(s32[8]{0:T(128)S(1)} %copy-done.3, s32[16,8]{1,0:T(8,128)S(1)} %bitcast.17, f32[4,3,4,64,128]{4,3,2,1,0:T(8,128)S(1)} %all-to-all-done.block_ref, bf16[256,384]{1,0:T(8,128)(2,1)S(1)} %maximum_maximum_fusion.first_ref, ...), custom_call_target="tpu_custom_call" | custom-call | tf_op jit(solution)/shard_map/nonlinear/pallas_call | solution.py:216
  72.8 0.0 copy-start
  72.8 0.9 copy-done
  73.6 0.0 all-reduce.2.cloned.1.call-update
  73.7 33.0 %all-reduce.2.cloned.1.call-done.stress_ref = f32[3,8,64,128]{3,2,1,0:T(8,128)} async-done(((f32[3,8,64,128]{3,2,1,0:T(8,128)}), f32[3,8,64,128]{3,2,1,0:T(8,128)}) %all-reduce.2.cloned.1.call-update) | async-done | bytes 786448 | tf_op jit(solution)/shard_map/psum | solution.py:407
  106.7 0.0 copy-start.1
  106.7 1.1 copy-done.1
  107.8 0.0 copy-start.4
  107.8 0.7 copy-done.4
  108.5 1.3 outgoing.1
  109.8 41.5 %all_to_all.15.refs_0_ = f32[8,8,48,128]{3,2,1,0:T(8,128)S(1)} all-to-all(f32[8,8,48,128]{3,2,1,0:T(8,128)S(1)} %bitcast.15), channel_id=1, replica_groups=mesh['kx'=4,'ht'=2,'real'=4] {'kx','ht'}, dimensions={0} | all-to-all | bytes 3145728 | tf_op jit(solution)/shard_map/all_to_all | solution.py:411
  151.3 8.6 %solve.1 = f32[8,8,2,24,128]{4,3,2,1,0:T(8,128)} custom-call(f32[8,8,48,128]{3,2,1,0:T(8,128)S(1)} %all_to_all.15.refs_0_, f32[8,512,512]{2,1,0:T(8,128)} %refs_1_.1), custom_call_target="tpu_custom_call" | custom-call | tf_op jit(solution)/shard_map/solve/pallas_call | solution.py:319
  159.9 0.0 copy-start.5
  159.9 3.7 %all-to-all-start.2 = ((f32[8,8,2,24,128]{4,3,2,1,0:T(8,128)}), f32[8,8,2,24,128]{4,3,2,1,0:T(8,128)S(1)}, u32[]{:S(2)}, u32[]{:S(2)}) async-start(f32[8,8,2,24,128]{4,3,2,1,0:T(8,128)} %solve.1), calls=%async_computation.2 | async-start | bytes 3145728 | tf_op jit(solution)/shard_map/all_to_all | solution.py:414
  163.6 0.0 copy-done.5
  163.6 36.4 %all-to-all-done.2 = f32[8,8,2,24,128]{4,3,2,1,0:T(8,128)S(1)} async-done(((f32[8,8,2,24,128]{4,3,2,1,0:T(8,128)}), f32[8,8,2,24,128]{4,3,2,1,0:T(8,128)S(1)}, u32[]{:S(2)}, u32[]{:S(2)}) %all-to-all-start.2) | async-done | bytes 1572896 | tf_op jit(solution)/shard_map/all_to_all | solution.py:414
  200.1 2.0 restore.1
  (9 shorter events, 0.1 us)
Async XLA Ops:
  9.3 6.5 %copy-start.8 = (s32[64]{0:T(128)S(1)}, s32[64]{0:T(128)}, u32[]{:S(2)}) copy-start(s32[64]{0:T(128)} %param.9) | copy-start | bytes 772
  9.3 6.6 %copy-start.7 = (s32[4]{0:T(128)S(1)}, s32[4]{0:T(128)}, u32[]{:S(2)}) copy-start(s32[4]{0:T(128)} %param.10) | copy-start | bytes 52
  9.3 6.7 %copy-start.6 = (s32[4,8]{1,0:T(4,128)S(1)}, s32[4,8]{1,0:T(4,128)}, u32[]{:S(2)}) copy-start(s32[4,8]{1,0:T(4,128)} %param.8) | copy-start | bytes 388
  9.3 51.7 %all-to-all-start = ((f32[4,3,4,64,128]{4,3,2,1,0:T(8,128)}), f32[4,3,4,64,128]{4,3,2,1,0:T(8,128)S(1)}, u32[]{:S(2)}, u32[]{:S(2)}) async-start(f32[4,3,4,64,128]{4,3,2,1,0:T(8,128)} %bitcast.12), calls=%async_computation | async-start | bytes 3145728 | tf_op jit(solution)/shard_map/all_to_all | solution.py:405
  15.7 91.0 %all-reduce.2.cloned.1.call-start = ((), (), s32[]{:S(2)}) async-start(), calls=%async_computation.3 | async-start | bytes 1572864 | tf_op jit(solution)/shard_map/psum | solution.py:407
  61.0 0.7 copy-start.2
  61.7 0.7 copy-start.3
  72.8 0.9 copy-start
  106.7 1.1 copy-start.1
  107.8 0.7 copy-start.4
  159.9 3.7 %copy-start.5 = (pred[128,128]{1,0:T(8,128)(4,1)S(1)}, pred[128,128]{1,0:T(8,128)(4,1)}, u32[]{:S(2)}) copy-start(pred[128,128]{1,0:T(8,128)(4,1)} %get-tuple-element.15) | copy-start | bytes 49156
  159.9 40.2 %all-to-all-start.2 = ((f32[8,8,2,24,128]{4,3,2,1,0:T(8,128)}), f32[8,8,2,24,128]{4,3,2,1,0:T(8,128)S(1)}, u32[]{:S(2)}, u32[]{:S(2)}) async-start(f32[8,8,2,24,128]{4,3,2,1,0:T(8,128)} %solve.1), calls=%async_computation.2 | async-start | bytes 3145728 | tf_op jit(solution)/shard_map/all_to_all | solution.py:414
Sparse Core Ops, SparseCore 0:
  73.8 32.8 all-reduce.1
where the time goes:
time: 210 us; the launch traced here: 209 us
  blocking collectives  83.5 us (40%)
  waiting for transfers between devices  69.5 us (33%)
  Pallas kernels  22.3 us (11%)
  between operations  13.5 us (6%)
  starting transfers between devices  10.2 us (5%)
  local copies, waits for them, and re-layouts  7.11 us (3%)
    all_gather x1, blocking collectives, local(): small = lax.all_gather(small, 'kx', axis=0, tiled=True)  42 us
    all_to_all x1, blocking collectives, local(): lax.all_to_all(block, ('kx', 'ht'), split_axis=0, concat_axis=0, tiled=True)  41.5 us
    all_to_all x1, waiting for transfers between devices, local(): lax.all_to_all(solved, ('kx', 'ht'), split_axis=0, concat_axis=0, tiled=T...  36.4 us
    psum x1, waiting for transfers between devices, local(): stress = lax.psum(stress, 'real')  33 us
    pallas_call x1, Pallas kernels, nonlinear(): pl.pallas_call(nonlinear_kernel, out_shape=(jax.ShapeDtypeStruct((compone...  10.4 us
    pallas_call x1, Pallas kernels, solve(): pl.pallas_call(functools.partial(solve_kernel, groups=groups, kx_count=kx...  8.58 us
    all_to_all x1, starting transfers between devices, local(): part = lax.all_to_all(part, 'kx', split_axis=0, concat_axis=0, tiled=True)  6.45 us
  transfers between devices with their start and end apart: 3, of which 2 were waited for; matrix products, arithmetic and copies ran while one was open for 2% of the time, Pallas kernels for 0%

commit v1 on v0

--- a/solution.py
+++ b/solution.py
@@ -108,7 +108,7 @@
 
 
 LANES = 128
-PIECES = 1
+PIECES = 2
 VMEM = pl.BlockSpec(memory_space=pltpu.VMEM)
 SMEM = pl.BlockSpec(memory_space=pltpu.SMEM)
 
@@ -127,12 +127,73 @@
     return lax.dot_general(left, right, (dims, ((), ())), preferred_element_type=jnp.float32)
 
 
+def pack_kernel(near_ref, count_ref, velocity_ref, out_ref):
+    chunks, rows, columns = (velocity_ref.shape[0], velocity_ref.shape[3], velocity_ref.shape[4])
+    out_ref[0, : chunks * rows] = velocity_ref[:, 0, 0].reshape(chunks * rows, columns)
+    if out_ref.shape[1] == chunks * rows:
+        return
+    shape = (out_ref.shape[1] - chunks * rows, columns)
+    row = lax.broadcasted_iota(jnp.int32, shape, 0)
+    lane = lax.broadcasted_iota(jnp.int32, shape, 1)
+    extra = jnp.zeros(shape, jnp.int32)
+    modes, members = near_ref.shape
+    for mode in range(modes):
+        line = jnp.where(lane == members, count_ref[mode], 0)
+        for member in range(members):
+            line = jnp.where(lane == member, near_ref[mode, member], line)
+        extra = jnp.where(row == mode, line, extra)
+    out_ref[0, chunks * rows :] = extra.astype(jnp.float32)
+
+
+def pack(velocity, neighbours, mode_counts, piece, extra_rows):
+    chunks, pieces, kx_count, rows, columns = velocity.shape
+    total = chunks * rows + extra_rows
+    return pl.pallas_call(
+        pack_kernel,
+        out_shape=jax.ShapeDtypeStruct((kx_count, total, columns), jnp.float32),
+        grid=(kx_count,),
+        in_specs=[
+            SMEM,
+            SMEM,
+            pl.BlockSpec((chunks, 1, 1, rows, columns), lambda k: (0, piece, k, 0, 0)),
+        ],
+        out_specs=pl.BlockSpec((1, total, columns), lambda k: (k, 0, 0)),
+        compiler_params=params(),
+        name="pack",
+    )(neighbours, mode_counts, velocity)
+
+
+def split_matrix_kernel(matrix_ref, top_ref, rest_ref):
+    top, rest = two_parts(matrix_ref[0].T)
+    top_ref[0] = top
+    rest_ref[0] = rest
+
+
+def split_matrix(helmholtz):
+    slots, heights, _ = helmholtz.shape
+    spec = pl.BlockSpec((1, heights, heights), lambda s: (s, 0, 0))
+    shape = jax.ShapeDtypeStruct(helmholtz.shape, jnp.bfloat16)
+    return pl.pallas_call(
+        split_matrix_kernel,
+        out_shape=(shape, shape),
+        grid=(slots,),
+        in_specs=[spec],
+        out_specs=(spec, spec),
+        compiler_params=params(),
+        cost_estimate=pl.CostEstimate(
+            flops=0, bytes_accessed=2 * helmholtz.size * 4, transcendentals=0
+        ),
+        name="split_matrix",
+    )(helmholtz)
+
+
 def nonlinear_kernel(
     low_ref, near_ref, block_ref, first_ref, second_ref, back_ref, mask_ref,
     slotted_ref, stress_ref, physical, products, sums, high_ref,
 ):
-    bands, components, band_modes, rows, columns = block_ref.shape
-    modes, points = (bands * band_modes, physical.shape[3])
+    components, modes, rows, columns = slotted_ref.shape
+    bands, points = (block_ref.shape[0], physical.shape[3])
+    band_modes = modes // bands
     members, highs = (stress_ref.shape[1], products.shape[1])
     found = jnp.int32(0)
     for mode in range(modes):
@@ -144,7 +205,8 @@
 
     def transform(step, carry):
         band, component = (step // components, step % components)
-        top, rest = two_parts(block_ref[band, component].reshape(band_modes * rows, columns))
+        size = band_modes * rows
+        top, rest = two_parts(block_ref[band, pl.ds(pl.multiple_of(component * size, 8), size)])
         both = dot(jnp.concatenate([top, rest], axis=1), first_ref[...])
         fields = both[:, :points] + dot(top, second_ref[...])
         place = pl.ds(band * band_modes, band_modes)
@@ -209,9 +271,9 @@
     lax.fori_loop(0, components, finish, 0)
 
 
-def nonlinear(block, low_index, neighbours, tables, mask):
-    bands, components, band_modes, rows, columns = block.shape
-    members, modes, points = (low_index.shape[0], bands * band_modes, 2 * columns)
+def nonlinear(block, shape, low_index, neighbours, tables, mask):
+    components, modes, rows, columns = shape
+    members, points = (low_index.shape[0], 2 * columns)
     highs = modes - members
     return pl.pallas_call(
         nonlinear_kernel,
@@ -232,7 +294,9 @@
     )(low_index, neighbours, block, *tables, mask)
 
 
-def outgoing_kernel(low_ref, slotted_ref, stress_ref, mask_ref, out_ref, full, *, groups, owners):
+def outgoing_kernel(
+    low_ref, slotted_ref, stress_ref, other_ref, mask_ref, out_ref, full, *, groups, band_modes
+):
     components, modes, rows, columns = slotted_ref.shape
     members = stress_ref.shape[1]
     per_slot = out_ref.shape[0] // (columns // 2)
@@ -240,32 +304,33 @@
     for member in range(members):
         mode = low_ref[member]
         for c in range(components):
-            full[c, mode] += stress_ref[c, member] * mask_ref[mode]
+            stress = stress_ref[c, member] + other_ref[c, member]
+            full[c, mode] += stress * mask_ref[mode]
     inner = modes // groups
     for c in range(components):
         for part in range(inner):
             tile = jnp.concatenate([full[c, part + inner * g] for g in range(groups)], axis=0)
             turned = tile.T
-            band_low, band_mode = (part // owners["band"], part % owners["band"])
+            band_low, band_mode = (part // band_modes, part % band_modes)
             for p in range(2):
-                row = ((band_low * 2 + p) * components + c) * owners["band"] + band_mode
+                row = ((band_low * 2 + p) * components + c) * band_modes + band_mode
                 out_ref[pl.ds(row, columns // 2, stride=per_slot), :] = turned[
                     p * (columns // 2) : (p + 1) * (columns // 2)
                 ]
 
 
-def outgoing(slotted, stress, low_index, mask, groups, band_modes):
+def outgoing(slotted, stress, other, low_index, mask, groups, band_modes):
     components, modes, rows, columns = slotted.shape
     per_slot = (modes // groups) * 2 * components
     return pl.pallas_call(
-        functools.partial(outgoing_kernel, groups=groups, owners={"band": band_modes}),
+        functools.partial(outgoing_kernel, groups=groups, band_modes=band_modes),
         out_shape=jax.ShapeDtypeStruct((columns // 2 * per_slot, groups * rows), jnp.float32),
-        in_specs=[SMEM, VMEM, VMEM, VMEM],
+        in_specs=[SMEM, VMEM, VMEM, VMEM, VMEM],
         out_specs=VMEM,
         scratch_shapes=[pltpu.VMEM(slotted.shape, jnp.float32)],
         compiler_params=params(),
         name="outgoing",
-    )(low_index, slotted, stress, mask)
+    )(low_index, slotted, stress, other, mask)
 
 
 def regroup(blocks, rows):
@@ -286,8 +351,8 @@
 
 
 def solve_kernel(*refs, groups, kx_count, ht_count):
-    pieces = len(refs) - 2
-    block_refs, matrix_ref, out_ref = (refs[:pieces], refs[pieces], refs[pieces + 1])
+    pieces = len(refs) - 3
+    block_refs, (top_ref, rest_ref, out_ref) = (refs[:pieces], refs[pieces:])
     rows = LANES // groups
     tiles = []
     for h in range(ht_count):
@@ -299,10 +364,8 @@
                 tiles.append(jnp.concatenate(regroup(blocks, rows), axis=0))
     top, rest = two_parts(jnp.concatenate(tiles, axis=1))
     count = top.shape[0]
-    matrix_top, matrix_rest = two_parts(matrix_ref[0])
-    last = ((1,), (1,))
-    both = dot(jnp.concatenate([top, rest], axis=0), matrix_top, last)
-    solved = both[:count] + both[count:] + dot(top, matrix_rest, last)
+    both = dot(jnp.concatenate([top, rest], axis=0), top_ref[0])
+    solved = both[:count] + both[count:] + dot(top, rest_ref[0])
     lane_tiles, per_band = out_ref.shape[2:4]
     for band in range(kx_count):
         for tile in range(ht_count * lane_tiles):
@@ -311,9 +374,9 @@
             ]
 
 
-def solve(blocks, helmholtz, groups, kx_count, ht_count):
+def solve(blocks, matrices, groups, kx_count, ht_count):
     owners, slots, per_slot, lanes = blocks[0].shape
-    heights = helmholtz.shape[1]
+    heights = matrices[0].shape[1]
     lane_tiles = heights // ht_count // LANES
     out = (owners, slots, lane_tiles, per_slot * groups // kx_count, LANES)
     return pl.pallas_call(
@@ -321,11 +384,11 @@
         out_shape=jax.ShapeDtypeStruct(out, jnp.float32),
         grid=(slots,),
         in_specs=[pl.BlockSpec((owners, 1, per_slot, lanes), lambda s: (0, s, 0, 0))] * len(blocks)
-        + [pl.BlockSpec((1, heights, heights), lambda s: (s, 0, 0))],
+        + [pl.BlockSpec((1, heights, heights), lambda s: (s, 0, 0))] * 2,
         out_specs=pl.BlockSpec((owners, 1) + out[2:], lambda s: (0, s, 0, 0, 0)),
         compiler_params=params(),
         name="solve",
-    )(*blocks, helmholtz)
+    )(*blocks, *matrices)
 
 
 def restore_kernel(block_ref, order_ref, out_ref):
@@ -363,7 +426,7 @@
     return top.astype(jnp.bfloat16), (value - top).astype(jnp.bfloat16)
 
 
-def slot_tables(owner_map, mode_counts, columns, realizations):
+def slot_tables(owner_map, columns):
     forward, backward = spanwise_tables(columns // 2, 2 * columns)
     slot_columns = (2 * owner_map[None, :] + jnp.arange(2)[:, None]).reshape(columns)
     select = slot_columns[None, :] == jnp.arange(columns)[:, None]
@@ -374,43 +437,60 @@
         backward, select.astype(jnp.float32), precision=lax.Precision.HIGHEST
     )
     back = jnp.concatenate(table_parts(slotted_back), axis=1)
-    active = (slot_columns // 2)[None, :] < mode_counts[:, None]
-    mask = jnp.where(active, jnp.float32(dt_step), 0.0)[:, None, :]
     order = select.T.astype(jnp.bfloat16)
     order = jnp.concatenate([order, order], axis=0)
-    return (first, forward_rest, back), mask, mask / realizations, order
+    return (first, forward_rest, back), order
+
+
+def slot_masks(owner_map, mode_counts, realizations):
+    active = jnp.tile(owner_map, 2)[None, :] < mode_counts[:, None]
+    mask = jnp.where(active, jnp.float32(dt_step), 0.0)[:, None, :]
+    return mask, mask / realizations
 
 
 def local(velocity, low_index, neighbours, owner_map, mode_counts, helmholtz):
     components, reals_dev, band_modes, rows_ht, columns = velocity.shape
     kx_count, ht_count = (lax.axis_size("kx"), lax.axis_size("ht"))
-    owners, pieces = (kx_count * ht_count, PIECES)
+    owners, pieces, real_count = (kx_count * ht_count, PIECES, lax.axis_size("real"))
     rows = rows_ht // (kx_count * pieces)
     groups = LANES // rows if rows else 0
     slots = columns // 2 // owners
     if (
         columns != LANES or reals_dev != 1 or rows_ht % LANES or rows % 8 or LANES % rows or kx_count % groups
         or (band_modes * 2 * components) % 8 or slots % 8 or low_index.shape[0] >= kx_count * band_modes
+        or low_index.shape[0] >= columns or real_count < 2 or real_count & (real_count - 1)
     ):
         return local_plain(velocity, low_index, neighbours, owner_map, mode_counts, helmholtz)
-    realizations = lax.axis_size("real")
-    small = jnp.concatenate([neighbours, mode_counts[:, None]], axis=1)
-    small = lax.all_gather(small, "kx", axis=0, tiled=True)
+    realizations, members = (real_count, low_index.shape[0])
+    chunks, modes = (components * band_modes, band_modes * kx_count)
+    shape = (components, modes, rows, columns)
+    extra_rows = -(-band_modes // 8) * 8
+    split = velocity.reshape(chunks, pieces, kx_count, rows, columns)
+    parts = []
+    for piece in range(pieces):
+        part = pack(split, neighbours, mode_counts, piece, 0 if piece else extra_rows)
+        parts.append(lax.all_to_all(part, "kx", split_axis=0, concat_axis=0, tiled=True))
+    matrices = split_matrix(helmholtz)
+    small = parts[0][:, chunks * rows : chunks * rows + band_modes, : members + 1]
+    small = small.reshape(modes, members + 1).astype(jnp.int32)
     neighbours, mode_counts = (small[:, :-1], small[:, -1])
-    tables, mask, low_mask, order = slot_tables(owner_map, mode_counts, columns, realizations)
-    split = velocity.reshape(components, band_modes, pieces, kx_count, rows, columns)
+    tables, order = slot_tables(owner_map, columns)
+    mask, low_mask = slot_masks(owner_map, mode_counts, realizations)
     received = []
-    for piece in range(pieces):
-        part = split[:, :, piece].transpose(2, 0, 1, 3, 4)
-        part = lax.all_to_all(part, "kx", split_axis=0, concat_axis=0, tiled=True)
-        slotted, stress = nonlinear(part, low_index, neighbours, tables, mask)
-        stress = lax.psum(stress, "real")
-        block = outgoing(slotted, stress, low_index, low_mask, groups, band_modes)
+    for part in parts:
+        slotted, stress = nonlinear(part, shape, low_index, neighbours, tables, mask)
+        step, other = (1, None)
+        while step < realizations:
+            stress = stress if other is None else stress + other
+            exchange = [(i, i ^ step) for i in range(realizations)]
+            other = lax.ppermute(stress, "real", exchange)
+            step *= 2
+        block = outgoing(slotted, stress, other, low_index, low_mask, groups, band_modes)
         block = block.reshape(owners, slots, -1, LANES)
         received.append(
             lax.all_to_all(block, ("kx", "ht"), split_axis=0, concat_axis=0, tiled=True)
         )
-    solved = solve(received, helmholtz, groups, kx_count, ht_count)
+    solved = solve(received, matrices, groups, kx_count, ht_count)
     returned = lax.all_to_all(solved, ("kx", "ht"), split_axis=0, concat_axis=0, tiled=True)
     result = restore(returned.reshape(-1, LANES), order, components, band_modes, rows_ht)
     return result.reshape(velocity.shape)

time: 210 us -> 179 us (0.85)
  blocking collectives: 83.5 us -> 0 us
  waiting for transfers between devices: 69.5 us -> 105 us
  Pallas kernels: 22.3 us -> 40.2 us
  starting transfers between devices: 10.2 us -> 26.4 us
  between operations: 13.5 us -> 0.16 us
    all_to_all x1 -> x4, waiting for transfers between devices: 0.01 us -> 45.1 us  [the longest x2 36 us: local(): lax.all_to_all(part, 'kx', split_axis=0, concat_axis=0, tiled=True)]
    all_gather x1 -> x0, blocking collectives: 42 us -> none  [local(): small = lax.all_gather(small, 'kx', axis=0, tiled=True)]
    all_to_all x1 -> x0, blocking collectives: 41.5 us -> none  [local(): lax.all_to_all(block, ('kx', 'ht'), split_axis=0, concat_axis=0, tiled=True)]
    psum x1 -> x0, waiting for transfers between devices: 33 us -> none  [local(): stress = lax.psum(stress, 'real')]
    ppermute x0 -> x4, waiting for transfers between devices: none -> 22.8 us  [local(): other = lax.ppermute(stress, 'real', exchange)]
    pallas_call x1 -> x5, Pallas kernels: 1.3 us -> 16.4 us  [the longest x1 8.59 us: split_matrix(): pl.pallas_call(split_matrix_kernel, out_shape=(shape, shape), grid=(slots...]
    all_to_all x1 -> x4, starting transfers between devices: 6.45 us -> 19.5 us  [the longest x2 9.81 us: local(): lax.all_to_all(part, 'kx', split_axis=0, concat_axis=0, tiled=True)]
    ppermute x0 -> x4, starting transfers between devices: none -> 3.24 us  [local(): other = lax.ppermute(stress, 'real', exchange)]
  transfers between devices with their start and end apart: 3 -> 9, of which waited for: 2 -> 8; matrix products, arithmetic and copies ran while one was open for 2% -> 1% of each run, Pallas kernels for 0% -> 11%
where the time goes in v1:
time: 179 us; the launch traced here: 178 us
  waiting for transfers between devices  105 us (59%)
  Pallas kernels  40.2 us (22%)
  starting transfers between devices  26.4 us (15%)
  local copies, waits for them, and re-layouts  5.13 us (3%)
    all_to_all x1, waiting for transfers between devices, local(): lax.all_to_all(solved, ('kx', 'ht'), split_axis=0, concat_axis=0, tiled=T...  37.1 us
    all_to_all x2, waiting for transfers between devices, local(): lax.all_to_all(part, 'kx', split_axis=0, concat_axis=0, tiled=True)  36 us
    ppermute x4, waiting for transfers between devices, local(): other = lax.ppermute(stress, 'real', exchange)  22.8 us
    pallas_call x2, Pallas kernels, nonlinear(): pl.pallas_call(nonlinear_kernel, out_shape=(jax.ShapeDtypeStruct((compone...  13.3 us
    all_to_all x2, starting transfers between devices, local(): lax.all_to_all(part, 'kx', split_axis=0, concat_axis=0, tiled=True)  9.81 us
    all_to_all x2, starting transfers between devices, local(): lax.all_to_all(block, ('kx', 'ht'), split_axis=0, concat_axis=0, tiled=True)  9.73 us
    all_to_all x2, waiting for transfers between devices, local(): lax.all_to_all(block, ('kx', 'ht'), split_axis=0, concat_axis=0, tiled=True)  9.11 us
    pallas_call x1, Pallas kernels, split_matrix(): pl.pallas_call(split_matrix_kernel, out_shape=(shape, shape), grid=(slots...  8.59 us
  transfers between devices with their start and end apart: 9, of which 8 were waited for; matrix products, arithmetic and copies ran while one was open for 1% of the time, Pallas kernels for 11%

profile of v1, /device:TPU:0, one launch (start us, length us, event | category | flops | bytes accessed | tf_op | source)
XLA Modules:
  0.0 178.5 jit_solution(3145907786612115617)
XLA Ops:
  0.0 0.0 copy-start
  0.0 1.4 copy-done
  1.4 0.0 copy-start.3
  1.4 0.7 copy-done.3
  2.1 0.0 copy-start.6
  2.1 0.7 copy-done.6
  2.7 0.0 copy-start.1
  2.7 0.0 copy-start.4
  2.8 0.0 copy-start.7
  2.8 2.1 %pack.2 = f32[4,392,128]{2,1,0:T(8,128)} custom-call(s32[4,8]{1,0:T(4,128)S(1)} %copy-done.3, s32[4]{0:T(128)S(1)} %copy-done.6, f32[12,2,4,32,128]{4,3,2,1,0:T(8,128)S(1)} %bitcast.9), custom_call_target="tpu_custom_call" | custom-call | tf_op jit(solution)/shard_map/pack/pallas_call | solution.py:151
  4.9 6.3 %all-to-all-start = ((f32[4,392,128]{2,1,0:T(8,128)}), f32[4,392,128]{2,1,0:T(8,128)S(1)}, u32[]{:S(2)}, u32[]{:S(2)}) async-start(f32[4,392,128]{2,1,0:T(8,128)} %pack.2), calls=%async_computation | async-start | bytes 1605632 | tf_op jit(solution)/shard_map/all_to_all | solution.py:472
  11.2 0.0 copy-done.1
  11.2 0.0 copy-done.4
  11.2 0.0 copy-done.7
  11.2 0.0 copy-start.8
  11.2 2.1 %pack.3 = f32[4,384,128]{2,1,0:T(8,128)} custom-call(s32[4,8]{1,0:T(4,128)S(1)} %copy-done.4, s32[4]{0:T(128)S(1)} %copy-done.7, f32[12,2,4,32,128]{4,3,2,1,0:T(8,128)S(1)} %bitcast.10), custom_call_target="tpu_custom_call" | custom-call | tf_op jit(solution)/shard_map/pack/pallas_call | solution.py:151
  13.3 0.0 copy-done.8
  13.3 0.0 copy-start.5
  13.3 0.1 add.51
  13.4 0.7 reduce-precision_convert_fusion
  14.1 17.5 %all-to-all-done.block_ref = f32[4,392,128]{2,1,0:T(8,128)S(1)} async-done(((f32[4,392,128]{2,1,0:T(8,128)}), f32[4,392,128]{2,1,0:T(8,128)S(1)}, u32[]{:S(2)}, u32[]{:S(2)}) %all-to-all-start) | async-done | bytes 802848 | tf_op jit(solution)/shard_map/all_to_all | solution.py:472
  31.6 3.5 %all-to-all-start.2 = ((f32[4,384,128]{2,1,0:T(8,128)}), f32[4,384,128]{2,1,0:T(8,128)S(1)}, u32[]{:S(2)}, u32[]{:S(2)}) async-start(f32[4,384,128]{2,1,0:T(8,128)} %pack.3), calls=%async_computation.2 | async-start | bytes 1572864 | tf_op jit(solution)/shard_map/all_to_all | solution.py:472
  35.2 0.1 lt.39
  35.3 0.1 iota_compare_fusion
  35.3 0.6 fusion.3
  36.0 0.2 slice_reduce_fusion
  36.1 0.1 broadcast_multiply_fusion
  36.2 18.5 %all-to-all-done.2.block_ref = f32[4,384,128]{2,1,0:T(8,128)S(1)} async-done(((f32[4,384,128]{2,1,0:T(8,128)}), f32[4,384,128]{2,1,0:T(8,128)S(1)}, u32[]{:S(2)}, u32[]{:S(2)}) %all-to-all-start.2) | async-done | bytes 786464 | tf_op jit(solution)/shard_map/all_to_all | solution.py:472
  54.7 0.0 copy-done.5
  54.7 6.6 %nonlinear.3 = (f32[3,16,32,128]{3,2,1,0:T(8,128)S(1)}, f32[3,8,32,128]{3,2,1,0:T(8,128)S(1)}) custom-call(s32[8]{0:T(128)S(1)} %copy-done.5, s32[16,8]{1,0:T(8,128)S(1)} %bitcast.13, f32[4,384,128]{2,1,0:T(8,128)S(1)} %all-to-all-done.2.block_ref, bf16[256,384]{1,0:T(8,128)(2,1)S(1)} %maximum_maximum_fusion.first_ref, ...), custom_call_target="tpu_custom_call" | custom-call | tf_op jit(solution)/shard_map/nonlinear/pallas_call | solution.py:278
  61.4 0.1 collective-permute-start.2
  61.4 1.7 collective-permute-done.2
  63.2 0.1 add.53.stress_ref
  63.2 1.6 collective-permute-start.3
  64.8 9.6 %collective-permute-done.3.other_ref = f32[3,8,32,128]{3,2,1,0:T(8,128)S(1)} collective-permute-done((f32[3,8,32,128]{3,2,1,0:T(8,128)S(1)}, f32[3,8,32,128]{3,2,1,0:T(8,128)S(1)}, u32[]{:S(2)}, u32[]{:S(2)}) %collective-permute-start.3) | collective-permute-done | bytes 393248 | tf_op jit(solution)/shard_map/ppermute | solution.py:486
  74.4 1.8 %outgoing.3 = f32[1536,128]{1,0:T(8,128)} custom-call(s32[8]{0:T(128)S(1)} %copy-done.5, f32[3,16,32,128]{3,2,1,0:T(8,128)S(1)} %get-tuple-element.13.slotted_ref, f32[3,8,32,128]{3,2,1,0:T(8,128)S(1)} %add.53.stress_ref, f32[3,8,32,128]{3,2,1,0:T(8,128)S(1)} %collective-permute-done.3.other_ref, f32[16,1,128]{2,1,0:T(1,128)S(1)} %get-tuple-element.21.mask_ref), custom_call_target="tpu_custom_call" | custom-call | tf_op jit(solution)/shard_map/outgoing/pallas_call | solution.py:325
  76.3 3.7 %all-to-all-start.3 = ((f32[8,8,24,128]{3,2,1,0:T(8,128)}), f32[8,8,24,128]{3,2,1,0:T(8,128)S(1)}, u32[]{:S(2)}, u32[]{:S(2)}) async-start(f32[8,8,24,128]{3,2,1,0:T(8,128)} %bitcast.3), calls=%async_computation.3 | async-start | bytes 1572864 | tf_op jit(solution)/shard_map/all_to_all | solution.py:491
  80.0 6.7 %nonlinear.2 = (f32[3,16,32,128]{3,2,1,0:T(8,128)S(1)}, f32[3,8,32,128]{3,2,1,0:T(8,128)S(1)}) custom-call(s32[8]{0:T(128)S(1)} %copy-done.5, s32[16,8]{1,0:T(8,128)S(1)} %bitcast.14, f32[4,392,128]{2,1,0:T(8,128)S(1)} %all-to-all-done.block_ref, bf16[256,384]{1,0:T(8,128)(2,1)S(1)} %maximum_maximum_fusion.first_ref, ...), custom_call_target="tpu_custom_call" | custom-call | tf_op jit(solution)/shard_map/nonlinear/pallas_call | solution.py:278
  86.7 0.1 collective-permute-start
  86.8 1.7 collective-permute-done
  88.5 0.1 add.52.stress_ref
  88.5 1.5 collective-permute-start.1
  90.0 9.7 %collective-permute-done.1.other_ref = f32[3,8,32,128]{3,2,1,0:T(8,128)S(1)} collective-permute-done((f32[3,8,32,128]{3,2,1,0:T(8,128)S(1)}, f32[3,8,32,128]{3,2,1,0:T(8,128)S(1)}, u32[]{:S(2)}, u32[]{:S(2)}) %collective-permute-start.1) | collective-permute-done | bytes 393248 | tf_op jit(solution)/shard_map/ppermute | solution.py:486
  99.8 1.8 %outgoing.2 = f32[1536,128]{1,0:T(8,128)} custom-call(s32[8]{0:T(128)S(1)} %copy-done.5, f32[3,16,32,128]{3,2,1,0:T(8,128)S(1)} %get-tuple-element.11.slotted_ref, f32[3,8,32,128]{3,2,1,0:T(8,128)S(1)} %add.52.stress_ref, f32[3,8,32,128]{3,2,1,0:T(8,128)S(1)} %collective-permute-done.1.other_ref, f32[16,1,128]{2,1,0:T(1,128)S(1)} %get-tuple-element.21.mask_ref), custom_call_target="tpu_custom_call" | custom-call | tf_op jit(solution)/shard_map/outgoing/pallas_call | solution.py:325
  101.6 0.0 all-to-all-done.3.refs_1_
  101.6 6.0 %all-to-all-start.1 = ((f32[8,8,24,128]{3,2,1,0:T(8,128)}), f32[8,8,24,128]{3,2,1,0:T(8,128)S(1)}, u32[]{:S(2)}, u32[]{:S(2)}) async-start(f32[8,8,24,128]{3,2,1,0:T(8,128)} %bitcast.2), calls=%async_computation.1 | async-start | bytes 1572864 | tf_op jit(solution)/shard_map/all_to_all | solution.py:491
  107.6 8.6 %split_matrix.1 = (bf16[8,512,512]{2,1,0:T(8,128)(2,1)S(1)}, bf16[8,512,512]{2,1,0:T(8,128)(2,1)}) custom-call(f32[8,512,512]{2,1,0:T(8,128)} %matrix_ref.1), custom_call_target="tpu_custom_call" | custom-call | bytes 16777216 | tf_op jit(solution)/shard_map/split_matrix/pallas_call | solution.py:176
  116.1 0.0 copy-start.2
  116.1 2.0 %copy-done.2 = bf16[8,512,512]{2,1,0:T(8,128)(2,1)} copy-done((bf16[8,512,512]{2,1,0:T(8,128)(2,1)}, bf16[8,512,512]{2,1,0:T(8,128)(2,1)S(1)}, u32[]{:S(2)}) %copy-start.2) | copy-done | bytes 4194328
  118.2 9.1 %all-to-all-done.1.refs_0_ = f32[8,8,24,128]{3,2,1,0:T(8,128)S(1)} async-done(((f32[8,8,24,128]{3,2,1,0:T(8,128)}), f32[8,8,24,128]{3,2,1,0:T(8,128)S(1)}, u32[]{:S(2)}, u32[]{:S(2)}) %all-to-all-start.1) | async-done | bytes 786464 | tf_op jit(solution)/shard_map/all_to_all | solution.py:491
  127.3 8.6 %solve.1 = f32[8,8,2,24,128]{4,3,2,1,0:T(8,128)} custom-call(f32[8,8,24,128]{3,2,1,0:T(8,128)S(1)} %all-to-all-done.1.refs_0_, f32[8,8,24,128]{3,2,1,0:T(8,128)S(1)} %all-to-all-done.3.refs_1_, bf16[8,512,512]{2,1,0:T(8,128)(2,1)} %copy-done.2, bf16[8,512,512]{2,1,0:T(8,128)(2,1)} %get-tuple-element.16.refs_3_), custom_call_target="tpu_custom_call" | custom-call | tf_op jit(solution)/shard_map/solve/pallas_call | solution.py:382
  135.8 3.6 %all-to-all-start.4 = ((f32[8,8,2,24,128]{4,3,2,1,0:T(8,128)}), f32[8,8,2,24,128]{4,3,2,1,0:T(8,128)S(1)}, u32[]{:S(2)}, u32[]{:S(2)}) async-start(f32[8,8,2,24,128]{4,3,2,1,0:T(8,128)} %solve.1), calls=%async_computation.4 | async-start | bytes 3145728 | tf_op jit(solution)/shard_map/all_to_all | solution.py:494
  139.4 37.1 %all-to-all-done.4 = f32[8,8,2,24,128]{4,3,2,1,0:T(8,128)S(1)} async-done(((f32[8,8,2,24,128]{4,3,2,1,0:T(8,128)}), f32[8,8,2,24,128]{4,3,2,1,0:T(8,128)S(1)}, u32[]{:S(2)}, u32[]{:S(2)}) %all-to-all-start.4) | async-done | bytes 1572896 | tf_op jit(solution)/shard_map/all_to_all | solution.py:494
  176.5 2.0 %restore.1 = f32[3,4,256,128]{3,2,1,0:T(8,128)} custom-call(f32[3072,128]{1,0:T(8,128)S(1)} %bitcast.11, bf16[256,128]{1,0:T(8,128)(2,1)S(1)} %add_convert_fusion.order_ref), custom_call_target="tpu_custom_call" | custom-call | tf_op jit(solution)/shard_map/restore/pallas_call | solution.py:414
  (10 shorter events, 0.1 us)
Async XLA Ops:
  0.0 1.4 copy-start
  1.4 0.7 copy-start.3
  2.1 0.7 copy-start.6
  2.7 8.4 %copy-start.1 = (f32[3,1,4,256,128]{4,3,2,1,0:T(8,128)S(1)}, f32[3,1,4,256,128]{4,3,2,1,0:T(8,128)}, u32[]{:S(2)}) copy-start(f32[3,1,4,256,128]{4,3,2,1,0:T(8,128)} %param.6) | copy-start | bytes 4718596
  2.7 8.4 %copy-start.4 = (s32[4,8]{1,0:T(4,128)S(1)}, s32[4,8]{1,0:T(4,128)}, u32[]{:S(2)}) copy-start(s32[4,8]{1,0:T(4,128)} %near_ref.3) | copy-start | bytes 388
  2.8 8.4 %copy-start.7 = (s32[4]{0:T(128)S(1)}, s32[4]{0:T(128)}, u32[]{:S(2)}) copy-start(s32[4]{0:T(128)} %count_ref.3) | copy-start | bytes 52
  4.9 26.8 %all-to-all-start = ((f32[4,392,128]{2,1,0:T(8,128)}), f32[4,392,128]{2,1,0:T(8,128)S(1)}, u32[]{:S(2)}, u32[]{:S(2)}) async-start(f32[4,392,128]{2,1,0:T(8,128)} %pack.2), calls=%async_computation | async-start | bytes 1605632 | tf_op jit(solution)/shard_map/all_to_all | solution.py:472
  11.2 2.1 %copy-start.8 = (s32[64]{0:T(128)S(1)}, s32[64]{0:T(128)}, u32[]{:S(2)}) copy-start(s32[64]{0:T(128)} %param.9) | copy-start | bytes 772
  13.3 41.4 %copy-start.5 = (s32[8]{0:T(128)S(1)}, s32[8]{0:T(128)}, u32[]{:S(2)}) copy-start(s32[8]{0:T(128)} %low_ref.7) | copy-start | bytes 100
  31.6 23.1 %all-to-all-start.2 = ((f32[4,384,128]{2,1,0:T(8,128)}), f32[4,384,128]{2,1,0:T(8,128)S(1)}, u32[]{:S(2)}, u32[]{:S(2)}) async-start(f32[4,384,128]{2,1,0:T(8,128)} %pack.3), calls=%async_computation.2 | async-start | bytes 1572864 | tf_op jit(solution)/shard_map/all_to_all | solution.py:472
  61.4 1.8 %collective-permute-start.2 = (f32[3,8,32,128]{3,2,1,0:T(8,128)S(1)}, f32[3,8,32,128]{3,2,1,0:T(8,128)S(1)}, u32[]{:S(2)}, u32[]{:S(2)}) collective-permute-start(f32[3,8,32,128]{3,2,1,0:T(8,128)S(1)} %get-tuple-element.14), channel_id=1, source_target_pairs={{0,1},{1,0},{2,3},{3,2},{4,5},{5,4},{6,7},{7,6},{8,9},{9,8},{10,11... | collective-permute-start | bytes 1179656 | tf_op jit(solution)/shard_map/ppermute | solution.py:486
  63.2 11.2 %collective-permute-start.3 = (f32[3,8,32,128]{3,2,1,0:T(8,128)S(1)}, f32[3,8,32,128]{3,2,1,0:T(8,128)S(1)}, u32[]{:S(2)}, u32[]{:S(2)}) collective-permute-start(f32[3,8,32,128]{3,2,1,0:T(8,128)S(1)} %add.53.stress_ref), channel_id=1, source_target_pairs={{0,2},{1,3},{2,0},{3,1},{4,6},{5,7},{6,4},{7,5},{8,10},{9,11},{10,... | collective-permute-start | bytes 1179656 | tf_op jit(solution)/shard_map/ppermute | solution.py:486
  76.3 25.3 %all-to-all-start.3 = ((f32[8,8,24,128]{3,2,1,0:T(8,128)}), f32[8,8,24,128]{3,2,1,0:T(8,128)S(1)}, u32[]{:S(2)}, u32[]{:S(2)}) async-start(f32[8,8,24,128]{3,2,1,0:T(8,128)} %bitcast.3), calls=%async_computation.3 | async-start | bytes 1572864 | tf_op jit(solution)/shard_map/all_to_all | solution.py:491
  86.7 1.8 %collective-permute-start = (f32[3,8,32,128]{3,2,1,0:T(8,128)S(1)}, f32[3,8,32,128]{3,2,1,0:T(8,128)S(1)}, u32[]{:S(2)}, u32[]{:S(2)}) collective-permute-start(f32[3,8,32,128]{3,2,1,0:T(8,128)S(1)} %get-tuple-element.12), channel_id=1, source_target_pairs={{0,1},{1,0},{2,3},{3,2},{4,5},{5,4},{6,7},{7,6},{8,9},{9,8},{10,11... | collective-permute-start | bytes 1179656 | tf_op jit(solution)/shard_map/ppermute | solution.py:486
  88.5 11.2 %collective-permute-start.1 = (f32[3,8,32,128]{3,2,1,0:T(8,128)S(1)}, f32[3,8,32,128]{3,2,1,0:T(8,128)S(1)}, u32[]{:S(2)}, u32[]{:S(2)}) collective-permute-start(f32[3,8,32,128]{3,2,1,0:T(8,128)S(1)} %add.52.stress_ref), channel_id=1, source_target_pairs={{0,2},{1,3},{2,0},{3,1},{4,6},{5,7},{6,4},{7,5},{8,10},{9,11},{10,... | collective-permute-start | bytes 1179656 | tf_op jit(solution)/shard_map/ppermute | solution.py:486
  101.6 25.7 %all-to-all-start.1 = ((f32[8,8,24,128]{3,2,1,0:T(8,128)}), f32[8,8,24,128]{3,2,1,0:T(8,128)S(1)}, u32[]{:S(2)}, u32[]{:S(2)}) async-start(f32[8,8,24,128]{3,2,1,0:T(8,128)} %bitcast.2), calls=%async_computation.1 | async-start | bytes 1572864 | tf_op jit(solution)/shard_map/all_to_all | solution.py:491
  116.1 2.0 %copy-start.2 = (bf16[8,512,512]{2,1,0:T(8,128)(2,1)}, bf16[8,512,512]{2,1,0:T(8,128)(2,1)S(1)}, u32[]{:S(2)}) copy-start(bf16[8,512,512]{2,1,0:T(8,128)(2,1)S(1)} %get-tuple-element.15.refs_2_) | copy-start | bytes 12582916
  135.8 40.7 %all-to-all-start.4 = ((f32[8,8,2,24,128]{4,3,2,1,0:T(8,128)}), f32[8,8,2,24,128]{4,3,2,1,0:T(8,128)S(1)}, u32[]{:S(2)}, u32[]{:S(2)}) async-start(f32[8,8,2,24,128]{4,3,2,1,0:T(8,128)} %solve.1), calls=%async_computation.4 | async-start | bytes 3145728 | tf_op jit(solution)/shard_map/all_to_all | solution.py:494

commit v2 on v1

--- a/solution.py
+++ b/solution.py
@@ -163,10 +163,11 @@
     )(neighbours, mode_counts, velocity)
 
 
-def split_matrix_kernel(matrix_ref, top_ref, rest_ref):
+def split_matrix_kernel(matrix_ref, top_ref, rest_ref, mark_ref):
     top, rest = two_parts(matrix_ref[0].T)
     top_ref[0] = top
     rest_ref[0] = rest
+    mark_ref[...] = jnp.zeros_like(mark_ref)
 
 
 def split_matrix(helmholtz):
@@ -175,10 +176,10 @@
     shape = jax.ShapeDtypeStruct(helmholtz.shape, jnp.bfloat16)
     return pl.pallas_call(
         split_matrix_kernel,
-        out_shape=(shape, shape),
+        out_shape=(shape, shape, jax.ShapeDtypeStruct((8, LANES), jnp.float32)),
         grid=(slots,),
         in_specs=[spec],
-        out_specs=(spec, spec),
+        out_specs=(spec, spec, pl.BlockSpec((8, LANES), lambda s: (0, 0))),
         compiler_params=params(),
         cost_estimate=pl.CostEstimate(
             flops=0, bytes_accessed=2 * helmholtz.size * 4, transcendentals=0
@@ -188,7 +189,7 @@
 
 
 def nonlinear_kernel(
-    low_ref, near_ref, block_ref, first_ref, second_ref, back_ref, mask_ref,
+    low_ref, near_ref, block_ref, first_ref, second_ref, back_ref, mask_ref, after_ref,
     slotted_ref, stress_ref, physical, products, sums, high_ref,
 ):
     components, modes, rows, columns = slotted_ref.shape
@@ -271,7 +272,7 @@
     lax.fori_loop(0, components, finish, 0)
 
 
-def nonlinear(block, shape, low_index, neighbours, tables, mask):
+def nonlinear(block, shape, low_index, neighbours, tables, mask, after):
     components, modes, rows, columns = shape
     members, points = (low_index.shape[0], 2 * columns)
     highs = modes - members
@@ -281,7 +282,7 @@
             jax.ShapeDtypeStruct((components, modes, rows, columns), jnp.float32),
             jax.ShapeDtypeStruct((components, members, rows, columns), jnp.float32),
         ),
-        in_specs=[SMEM, SMEM] + [VMEM] * 5,
+        in_specs=[SMEM, SMEM] + [VMEM] * 5 + [pl.BlockSpec(memory_space=pl.ANY)],
         out_specs=(VMEM, VMEM),
         scratch_shapes=[
             pltpu.VMEM((components, modes, rows, points), jnp.float32),
@@ -291,7 +292,7 @@
         ],
         compiler_params=params(),
         name="nonlinear",
-    )(low_index, neighbours, block, *tables, mask)
+    )(low_index, neighbours, block, *tables, mask, after)
 
 
 def outgoing_kernel(
@@ -374,8 +375,8 @@
             ]
 
 
-def solve(blocks, matrices, groups, kx_count, ht_count):
-    owners, slots, per_slot, lanes = blocks[0].shape
+def solve(blocks, matrices, groups, kx_count, ht_count, first, slots):
+    owners, _, per_slot, lanes = blocks[0].shape
     heights = matrices[0].shape[1]
     lane_tiles = heights // ht_count // LANES
     out = (owners, slots, lane_tiles, per_slot * groups // kx_count, LANES)
@@ -383,25 +384,29 @@
         functools.partial(solve_kernel, groups=groups, kx_count=kx_count, ht_count=ht_count),
         out_shape=jax.ShapeDtypeStruct(out, jnp.float32),
         grid=(slots,),
-        in_specs=[pl.BlockSpec((owners, 1, per_slot, lanes), lambda s: (0, s, 0, 0))] * len(blocks)
-        + [pl.BlockSpec((1, heights, heights), lambda s: (s, 0, 0))] * 2,
+        in_specs=[
+            pl.BlockSpec((owners, 1, per_slot, lanes), lambda s: (0, first + s, 0, 0))
+        ] * len(blocks)
+        + [pl.BlockSpec((1, heights, heights), lambda s: (first + s, 0, 0))] * 2,
         out_specs=pl.BlockSpec((owners, 1) + out[2:], lambda s: (0, s, 0, 0, 0)),
         compiler_params=params(),
         name="solve",
     )(*blocks, *matrices)
 
 
-def restore_kernel(block_ref, order_ref, out_ref):
+def restore_kernel(*refs):
+    block_refs, (order_ref, out_ref) = (refs[:-2], refs[-2:])
     components, band_modes, rows, columns = out_ref.shape
-    slots = columns // 2
-    per_slot = block_ref.shape[0] // slots
+    slots = columns // 2 // len(block_refs)
+    per_slot = block_refs[0].shape[0] // slots
     for c in range(components):
         for mode in range(band_modes):
             for tile in range(rows // LANES):
                 parts = []
                 for p in range(2):
                     row = ((tile * 2 + p) * components + c) * band_modes + mode
-                    parts.append(block_ref[pl.ds(row, slots, stride=per_slot), :])
+                    for block_ref in block_refs:
+                        parts.append(block_ref[pl.ds(row, slots, stride=per_slot), :])
                 top, rest = two_parts(jnp.concatenate(parts, axis=0))
                 both = jnp.concatenate([top, rest], axis=0)
                 out_ref[c, mode, pl.ds(tile * LANES, LANES)] = dot(
@@ -409,16 +414,16 @@
                 )
 
 
-def restore(block, order, components, band_modes, rows):
+def restore(blocks, order, components, band_modes, rows):
     columns = order.shape[1]
     return pl.pallas_call(
         restore_kernel,
         out_shape=jax.ShapeDtypeStruct((components, band_modes, rows, columns), jnp.float32),
-        in_specs=[VMEM, VMEM],
+        in_specs=[VMEM] * (len(blocks) + 1),
         out_specs=VMEM,
         compiler_params=params(),
         name="restore",
-    )(block, order)
+    )(*blocks, order)
 
 
 def table_parts(value):
@@ -426,7 +431,7 @@
     return top.astype(jnp.bfloat16), (value - top).astype(jnp.bfloat16)
 
 
-def slot_tables(owner_map, columns):
+def slot_tables(owner_map, columns, owners, pieces):
     forward, backward = spanwise_tables(columns // 2, 2 * columns)
     slot_columns = (2 * owner_map[None, :] + jnp.arange(2)[:, None]).reshape(columns)
     select = slot_columns[None, :] == jnp.arange(columns)[:, None]
@@ -437,7 +442,8 @@
         backward, select.astype(jnp.float32), precision=lax.Precision.HIGHEST
     )
     back = jnp.concatenate(table_parts(slotted_back), axis=1)
-    order = select.T.astype(jnp.bfloat16)
+    order = select.T.reshape(2, owners, pieces, -1, columns).transpose(0, 2, 1, 3, 4)
+    order = order.reshape(columns, columns).astype(jnp.bfloat16)
     order = jnp.concatenate([order, order], axis=0)
     return (first, forward_rest, back), order
 
@@ -457,7 +463,7 @@
     slots = columns // 2 // owners
     if (
         columns != LANES or reals_dev != 1 or rows_ht % LANES or rows % 8 or LANES % rows or kx_count % groups
-        or (band_modes * 2 * components) % 8 or slots % 8 or low_index.shape[0] >= kx_count * band_modes
+        or (band_modes * 2 * components) % 8 or slots % 8 or slots // pieces * owners % 8 or low_index.shape[0] >= kx_count * band_modes
         or low_index.shape[0] >= columns or real_count < 2 or real_count & (real_count - 1)
     ):
         return local_plain(velocity, low_index, neighbours, owner_map, mode_counts, helmholtz)
@@ -470,29 +476,34 @@
     for piece in range(pieces):
         part = pack(split, neighbours, mode_counts, piece, 0 if piece else extra_rows)
         parts.append(lax.all_to_all(part, "kx", split_axis=0, concat_axis=0, tiled=True))
-    matrices = split_matrix(helmholtz)
+    *matrices, after = split_matrix(helmholtz)
     small = parts[0][:, chunks * rows : chunks * rows + band_modes, : members + 1]
     small = small.reshape(modes, members + 1).astype(jnp.int32)
     neighbours, mode_counts = (small[:, :-1], small[:, -1])
-    tables, order = slot_tables(owner_map, columns)
+    tables, order = slot_tables(owner_map, columns, owners, pieces)
     mask, low_mask = slot_masks(owner_map, mode_counts, realizations)
     received = []
     for part in parts:
-        slotted, stress = nonlinear(part, shape, low_index, neighbours, tables, mask)
+        slotted, stress = nonlinear(part, shape, low_index, neighbours, tables, mask, after)
         step, other = (1, None)
         while step < realizations:
             stress = stress if other is None else stress + other
             exchange = [(i, i ^ step) for i in range(realizations)]
             other = lax.ppermute(stress, "real", exchange)
             step *= 2
+        after = stress
         block = outgoing(slotted, stress, other, low_index, low_mask, groups, band_modes)
         block = block.reshape(owners, slots, -1, LANES)
         received.append(
             lax.all_to_all(block, ("kx", "ht"), split_axis=0, concat_axis=0, tiled=True)
         )
-    solved = solve(received, matrices, groups, kx_count, ht_count)
-    returned = lax.all_to_all(solved, ("kx", "ht"), split_axis=0, concat_axis=0, tiled=True)
-    result = restore(returned.reshape(-1, LANES), order, components, band_modes, rows_ht)
+    returned = []
+    for piece in range(pieces):
+        count = slots // pieces
+        solved = solve(received, matrices, groups, kx_count, ht_count, piece * count, count)
+        solved = lax.all_to_all(solved, ("kx", "ht"), split_axis=0, concat_axis=0, tiled=True)
+        returned.append(solved.reshape(-1, LANES))
+    result = restore(returned, order, components, band_modes, rows_ht)
     return result.reshape(velocity.shape)
 
 

time: 179 us -> 164 us (0.916)
  waiting for transfers between devices: 105 us -> 62.3 us
  blocking collectives: 0 us -> 25.4 us
    all_to_all x2, waiting for transfers between devices: 36 us -> 4.78 us  [local(): lax.all_to_all(part, 'kx', split_axis=0, concat_axis=0, tiled=True)]
    all_to_all x0 -> x1, blocking collectives: none -> 25.4 us  [local(): lax.all_to_all(block, ('kx', 'ht'), split_axis=0, concat_axis=0, tiled=True)]
    all_to_all x2 -> x1, waiting for transfers between devices: 9.11 us -> 0.01 us  [local(): lax.all_to_all(block, ('kx', 'ht'), split_axis=0, concat_axis=0, tiled=True)]
    all_to_all x2 -> x1, starting transfers between devices: 9.73 us -> 6.01 us  [local(): lax.all_to_all(block, ('kx', 'ht'), split_axis=0, concat_axis=0, tiled=True)]
    all_to_all x1 -> x2, starting transfers between devices: 3.58 us -> 7.13 us  [local(): lax.all_to_all(solved, ('kx', 'ht'), split_axis=0, concat_axis=0, tiled=T...]
    all_to_all x1 -> x2, waiting for transfers between devices: 37.1 us -> 34.8 us  [local(): lax.all_to_all(solved, ('kx', 'ht'), split_axis=0, concat_axis=0, tiled=T...]
    pallas_call x1 -> x2, Pallas kernels: 8.56 us -> 9.76 us  [solve(): pl.pallas_call(functools.partial(solve_kernel, groups=groups, kx_count=kx...]
  transfers between devices with their start and end apart: 9 -> 9, of which waited for: 8 -> 7; matrix products, arithmetic and copies ran while one was open for 1% -> 1% of each run, Pallas kernels for 11% -> 19%
where the time goes in v2:
time: 164 us; the launch traced here: 163 us
  waiting for transfers between devices  62.3 us (38%)
  Pallas kernels  40.6 us (25%)
  starting transfers between devices  26.2 us (16%)
  blocking collectives  25.4 us (15%)
  local copies, waits for them, and re-layouts  6.67 us (4%)
    all_to_all x2, waiting for transfers between devices, local(): lax.all_to_all(solved, ('kx', 'ht'), split_axis=0, concat_axis=0, tiled=T...  34.8 us
    all_to_all x1, blocking collectives, local(): lax.all_to_all(block, ('kx', 'ht'), split_axis=0, concat_axis=0, tiled=True)  25.4 us
    ppermute x4, waiting for transfers between devices, local(): other = lax.ppermute(stress, 'real', exchange)  22.7 us
    pallas_call x2, Pallas kernels, nonlinear(): pl.pallas_call(nonlinear_kernel, out_shape=(jax.ShapeDtypeStruct((compone...  13.4 us
    all_to_all x2, starting transfers between devices, local(): lax.all_to_all(part, 'kx', split_axis=0, concat_axis=0, tiled=True)  9.81 us
    pallas_call x2, Pallas kernels, solve(): pl.pallas_call(functools.partial(solve_kernel, groups=groups, kx_count=kx...  9.76 us
    pallas_call x1, Pallas kernels, split_matrix(): pl.pallas_call(split_matrix_kernel, out_shape=(shape, shape, jax.ShapeDty...  8.61 us
    all_to_all x2, starting transfers between devices, local(): lax.all_to_all(solved, ('kx', 'ht'), split_axis=0, concat_axis=0, tiled=T...  7.13 us
  transfers between devices with their start and end apart: 9, of which 7 were waited for; matrix products, arithmetic and copies ran while one was open for 1% of the time, Pallas kernels for 19%

profile of v2, /device:TPU:0, one launch (start us, length us, event | category | flops | bytes accessed | tf_op | source)
XLA Modules:
  0.0 163.1 jit_solution(4802489758184310537)
XLA Ops:
  0.0 0.0 copy-start.8
  0.0 0.0 copy-start.1
  0.0 1.4 copy-done.1
  1.4 0.0 copy-start.3
  1.4 0.7 copy-done.3
  2.1 0.0 copy-start.6
  2.1 0.7 copy-done.6
  2.8 0.0 copy-start.2
  2.8 2.1 %pack.2 = f32[4,392,128]{2,1,0:T(8,128)} custom-call(s32[4,8]{1,0:T(4,128)S(1)} %copy-done.3, s32[4]{0:T(128)S(1)} %copy-done.6, f32[12,2,4,32,128]{4,3,2,1,0:T(8,128)S(1)} %bitcast.13), custom_call_target="tpu_custom_call" | custom-call | tf_op jit(solution)/shard_map/pack/pallas_call | solution.py:151
  4.9 6.3 %all-to-all-start = ((f32[4,392,128]{2,1,0:T(8,128)}), f32[4,392,128]{2,1,0:T(8,128)S(1)}, u32[]{:S(2)}, u32[]{:S(2)}) async-start(f32[4,392,128]{2,1,0:T(8,128)} %pack.2), calls=%async_computation | async-start | bytes 1605632 | tf_op jit(solution)/shard_map/all_to_all | solution.py:478
  11.2 0.0 copy-done.2
  11.2 0.0 copy-start.4
  11.2 0.7 copy-done.4
  11.9 0.0 copy-start.7
  11.9 0.7 copy-done.7
  12.5 2.1 %pack.3 = f32[4,384,128]{2,1,0:T(8,128)} custom-call(s32[4,8]{1,0:T(4,128)S(1)} %copy-done.4, s32[4]{0:T(128)S(1)} %copy-done.7, f32[12,2,4,32,128]{4,3,2,1,0:T(8,128)S(1)} %bitcast.14), custom_call_target="tpu_custom_call" | custom-call | tf_op jit(solution)/shard_map/pack/pallas_call | solution.py:151
  14.6 0.0 copy-done.8
  14.6 0.1 add.67
  14.7 0.1 lt.39
  14.8 0.0 copy-start.5
  14.8 8.6 %split_matrix.1 = (bf16[8,512,512]{2,1,0:T(8,128)(2,1)S(1)}, bf16[8,512,512]{2,1,0:T(8,128)(2,1)}, f32[8,128]{1,0:T(8,128)S(1)}) custom-call(f32[8,512,512]{2,1,0:T(8,128)} %matrix_ref.1), custom_call_target="tpu_custom_call" | custom-call | bytes 16777216 | tf_op jit(solution)/shard_map/split_matrix/pallas_call | solution.py:177
  23.4 0.0 copy-start
  23.4 2.0 %copy-done = bf16[8,512,512]{2,1,0:T(8,128)(2,1)} copy-done((bf16[8,512,512]{2,1,0:T(8,128)(2,1)}, bf16[8,512,512]{2,1,0:T(8,128)(2,1)S(1)}, u32[]{:S(2)}) %copy-start) | copy-done | bytes 4194328
  25.5 0.7 reduce-precision_convert_fusion
  26.3 0.6 fusion.3
  26.9 4.8 %all-to-all-done.block_ref = f32[4,392,128]{2,1,0:T(8,128)S(1)} async-done(((f32[4,392,128]{2,1,0:T(8,128)}), f32[4,392,128]{2,1,0:T(8,128)S(1)}, u32[]{:S(2)}, u32[]{:S(2)}) %all-to-all-start) | async-done | bytes 802848 | tf_op jit(solution)/shard_map/all_to_all | solution.py:478
  31.6 3.5 %all-to-all-start.2 = ((f32[4,384,128]{2,1,0:T(8,128)}), f32[4,384,128]{2,1,0:T(8,128)S(1)}, u32[]{:S(2)}, u32[]{:S(2)}) async-start(f32[4,384,128]{2,1,0:T(8,128)} %pack.3), calls=%async_computation.2 | async-start | bytes 1572864 | tf_op jit(solution)/shard_map/all_to_all | solution.py:478
  35.1 0.2 slice_reduce_fusion
  35.3 0.1 broadcast_multiply_fusion
  35.4 0.0 copy-done.5
  35.4 6.7 %nonlinear.2 = (f32[3,16,32,128]{3,2,1,0:T(8,128)S(1)}, f32[3,8,32,128]{3,2,1,0:T(8,128)S(1)}) custom-call(s32[8]{0:T(128)S(1)} %copy-done.5, s32[16,8]{1,0:T(8,128)S(1)} %bitcast.19, f32[4,392,128]{2,1,0:T(8,128)S(1)} %all-to-all-done.block_ref, bf16[256,384]{1,0:T(8,128)(2,1)S(1)} %maximum_maximum_fusion.first_ref, ...), custom_call_target="tpu_custom_call" | custom-call | tf_op jit(solution)/shard_map/nonlinear/pallas_call | solution.py:279
  42.1 0.1 collective-permute-start
  42.2 1.7 %collective-permute-done = f32[3,8,32,128]{3,2,1,0:T(8,128)S(1)} collective-permute-done((f32[3,8,32,128]{3,2,1,0:T(8,128)S(1)}, f32[3,8,32,128]{3,2,1,0:T(8,128)S(1)}, u32[]{:S(2)}, u32[]{:S(2)}) %collective-permute-start) | collective-permute-done | bytes 393248 | tf_op jit(solution)/shard_map/ppermute | solution.py:492
  43.9 0.1 add.68.stress_ref.after_ref
  44.0 1.6 collective-permute-start.1
  45.5 9.7 %collective-permute-done.1.other_ref = f32[3,8,32,128]{3,2,1,0:T(8,128)S(1)} collective-permute-done((f32[3,8,32,128]{3,2,1,0:T(8,128)S(1)}, f32[3,8,32,128]{3,2,1,0:T(8,128)S(1)}, u32[]{:S(2)}, u32[]{:S(2)}) %collective-permute-start.1) | collective-permute-done | bytes 393248 | tf_op jit(solution)/shard_map/ppermute | solution.py:492
  55.2 1.8 %outgoing.2 = f32[1536,128]{1,0:T(8,128)} custom-call(s32[8]{0:T(128)S(1)} %copy-done.5, f32[3,16,32,128]{3,2,1,0:T(8,128)S(1)} %get-tuple-element.13.slotted_ref, f32[3,8,32,128]{3,2,1,0:T(8,128)S(1)} %add.68.stress_ref.after_ref, f32[3,8,32,128]{3,2,1,0:T(8,128)S(1)} %collective-permute-done.1.other_ref, f32[16,1,128]{2,1,0:T(1,128)S(1)} %get-tuple-element.23.mask_ref), custom_call_target="tpu_custom_call" | custom-call | tf_op jit(solution)/shard_map/outgoing/pallas_call | solution.py:326
  57.0 0.0 all-to-all-done.2.block_ref
  57.0 6.0 %all-to-all-start.1 = ((f32[8,8,24,128]{3,2,1,0:T(8,128)}), f32[8,8,24,128]{3,2,1,0:T(8,128)S(1)}, u32[]{:S(2)}, u32[]{:S(2)}) async-start(f32[8,8,24,128]{3,2,1,0:T(8,128)} %bitcast.2), calls=%async_computation.1 | async-start | bytes 1572864 | tf_op jit(solution)/shard_map/all_to_all | solution.py:498
  63.0 6.7 %nonlinear.3 = (f32[3,16,32,128]{3,2,1,0:T(8,128)S(1)}, f32[3,8,32,128]{3,2,1,0:T(8,128)S(1)}) custom-call(s32[8]{0:T(128)S(1)} %copy-done.5, s32[16,8]{1,0:T(8,128)S(1)} %bitcast.20, f32[4,384,128]{2,1,0:T(8,128)S(1)} %all-to-all-done.2.block_ref, bf16[256,384]{1,0:T(8,128)(2,1)S(1)} %maximum_maximum_fusion.first_ref, ...), custom_call_target="tpu_custom_call" | custom-call | tf_op jit(solution)/shard_map/nonlinear/pallas_call | solution.py:279
  69.7 0.1 collective-permute-start.2
  69.8 1.7 %collective-permute-done.2 = f32[3,8,32,128]{3,2,1,0:T(8,128)S(1)} collective-permute-done((f32[3,8,32,128]{3,2,1,0:T(8,128)S(1)}, f32[3,8,32,128]{3,2,1,0:T(8,128)S(1)}, u32[]{:S(2)}, u32[]{:S(2)}) %collective-permute-start.2) | collective-permute-done | bytes 393248 | tf_op jit(solution)/shard_map/ppermute | solution.py:492
  71.5 0.1 add.69.stress_ref
  71.6 1.6 collective-permute-start.3
  73.1 9.7 %collective-permute-done.3.other_ref = f32[3,8,32,128]{3,2,1,0:T(8,128)S(1)} collective-permute-done((f32[3,8,32,128]{3,2,1,0:T(8,128)S(1)}, f32[3,8,32,128]{3,2,1,0:T(8,128)S(1)}, u32[]{:S(2)}, u32[]{:S(2)}) %collective-permute-start.3) | collective-permute-done | bytes 393248 | tf_op jit(solution)/shard_map/ppermute | solution.py:492
  82.8 0.9 outgoing.3
  83.7 0.0 all-to-all-done.1.refs_0_
  83.7 25.4 %all_to_all.30.refs_1_ = f32[8,8,24,128]{3,2,1,0:T(8,128)S(1)} all-to-all(f32[8,8,24,128]{3,2,1,0:T(8,128)S(1)} %bitcast.17), channel_id=1, replica_groups=mesh['kx'=4,'ht'=2,'real'=4] {'kx','ht'}, dimensions={0} | all-to-all | bytes 1572864 | tf_op jit(solution)/shard_map/all_to_all | solution.py:498
  109.1 4.8 %solve.2 = f32[8,4,2,24,128]{4,3,2,1,0:T(8,128)} custom-call(f32[8,8,24,128]{3,2,1,0:T(8,128)S(1)} %all-to-all-done.1.refs_0_, f32[8,8,24,128]{3,2,1,0:T(8,128)S(1)} %all_to_all.30.refs_1_, bf16[8,512,512]{2,1,0:T(8,128)(2,1)} %copy-done, bf16[8,512,512]{2,1,0:T(8,128)(2,1)} %get-tuple-element.18.refs_3_), custom_call_target="tpu_custom_call" | custom-call | tf_op jit(solution)/shard_map/solve/pallas_call | solution.py:383
  113.9 3.6 %all-to-all-start.4 = ((f32[8,4,2,24,128]{4,3,2,1,0:T(8,128)}), f32[8,4,2,24,128]{4,3,2,1,0:T(8,128)S(1)}, u32[]{:S(2)}, u32[]{:S(2)}) async-start(f32[8,4,2,24,128]{4,3,2,1,0:T(8,128)} %solve.2), calls=%async_computation.4 | async-start | bytes 1572864 | tf_op jit(solution)/shard_map/all_to_all | solution.py:504
  117.5 4.9 %solve.3 = f32[8,4,2,24,128]{4,3,2,1,0:T(8,128)} custom-call(f32[8,8,24,128]{3,2,1,0:T(8,128)S(1)} %all-to-all-done.1.refs_0_, f32[8,8,24,128]{3,2,1,0:T(8,128)S(1)} %all_to_all.30.refs_1_, bf16[8,512,512]{2,1,0:T(8,128)(2,1)} %copy-done, bf16[8,512,512]{2,1,0:T(8,128)(2,1)} %get-tuple-element.18.refs_3_), custom_call_target="tpu_custom_call" | custom-call | tf_op jit(solution)/shard_map/solve/pallas_call | solution.py:383
  122.4 14.8 %all-to-all-done.4 = f32[8,4,2,24,128]{4,3,2,1,0:T(8,128)S(1)} async-done(((f32[8,4,2,24,128]{4,3,2,1,0:T(8,128)}), f32[8,4,2,24,128]{4,3,2,1,0:T(8,128)S(1)}, u32[]{:S(2)}, u32[]{:S(2)}) %all-to-all-start.4) | async-done | bytes 786464 | tf_op jit(solution)/shard_map/all_to_all | solution.py:504
  137.3 3.5 %all-to-all-start.5 = ((f32[8,4,2,24,128]{4,3,2,1,0:T(8,128)}), f32[8,4,2,24,128]{4,3,2,1,0:T(8,128)S(1)}, u32[]{:S(2)}, u32[]{:S(2)}) async-start(f32[8,4,2,24,128]{4,3,2,1,0:T(8,128)} %solve.3), calls=%async_computation.5 | async-start | bytes 1572864 | tf_op jit(solution)/shard_map/all_to_all | solution.py:504
  140.8 0.1 add.70
  140.9 0.1 add.75
  141.0 0.1 iota_compare_fusion
  141.2 20.0 %all-to-all-done.5 = f32[8,4,2,24,128]{4,3,2,1,0:T(8,128)S(1)} async-done(((f32[8,4,2,24,128]{4,3,2,1,0:T(8,128)}), f32[8,4,2,24,128]{4,3,2,1,0:T(8,128)S(1)}, u32[]{:S(2)}, u32[]{:S(2)}) %all-to-all-start.5) | async-done | bytes 786464 | tf_op jit(solution)/shard_map/all_to_all | solution.py:504
  161.1 2.0 %restore.1 = f32[3,4,256,128]{3,2,1,0:T(8,128)} custom-call(f32[1536,128]{1,0:T(8,128)S(1)} %bitcast.15, f32[1536,128]{1,0:T(8,128)S(1)} %bitcast.16, bf16[256,128]{1,0:T(8,128)(2,1)S(1)} %add_convert_fusion.refs_2_), custom_call_target="tpu_custom_call" | custom-call | tf_op jit(solution)/shard_map/restore/pallas_call | solution.py:419
  (13 shorter events, 0.1 us)
Async XLA Ops:
  0.0 14.6 %copy-start.8 = (s32[64]{0:T(128)S(1)}, s32[64]{0:T(128)}, u32[]{:S(2)}) copy-start(s32[64]{0:T(128)} %param.9) | copy-start | bytes 772
  0.0 1.4 copy-start.1
  1.4 0.7 copy-start.3
  2.1 0.7 copy-start.6
  2.8 8.4 %copy-start.2 = (f32[3,1,4,256,128]{4,3,2,1,0:T(8,128)S(1)}, f32[3,1,4,256,128]{4,3,2,1,0:T(8,128)}, u32[]{:S(2)}) copy-start(f32[3,1,4,256,128]{4,3,2,1,0:T(8,128)} %param.6) | copy-start | bytes 4718596
  4.9 26.8 %all-to-all-start = ((f32[4,392,128]{2,1,0:T(8,128)}), f32[4,392,128]{2,1,0:T(8,128)S(1)}, u32[]{:S(2)}, u32[]{:S(2)}) async-start(f32[4,392,128]{2,1,0:T(8,128)} %pack.2), calls=%async_computation | async-start | bytes 1605632 | tf_op jit(solution)/shard_map/all_to_all | solution.py:478
  11.2 0.7 copy-start.4
  11.9 0.7 copy-start.7
  14.8 20.6 %copy-start.5 = (s32[8]{0:T(128)S(1)}, s32[8]{0:T(128)}, u32[]{:S(2)}) copy-start(s32[8]{0:T(128)} %low_ref.7) | copy-start | bytes 100
  23.4 2.0 %copy-start = (bf16[8,512,512]{2,1,0:T(8,128)(2,1)}, bf16[8,512,512]{2,1,0:T(8,128)(2,1)S(1)}, u32[]{:S(2)}) copy-start(bf16[8,512,512]{2,1,0:T(8,128)(2,1)S(1)} %get-tuple-element.17.refs_2_) | copy-start | bytes 12582916
  31.6 25.4 %all-to-all-start.2 = ((f32[4,384,128]{2,1,0:T(8,128)}), f32[4,384,128]{2,1,0:T(8,128)S(1)}, u32[]{:S(2)}, u32[]{:S(2)}) async-start(f32[4,384,128]{2,1,0:T(8,128)} %pack.3), calls=%async_computation.2 | async-start | bytes 1572864 | tf_op jit(solution)/shard_map/all_to_all | solution.py:478
  42.1 1.8 %collective-permute-start = (f32[3,8,32,128]{3,2,1,0:T(8,128)S(1)}, f32[3,8,32,128]{3,2,1,0:T(8,128)S(1)}, u32[]{:S(2)}, u32[]{:S(2)}) collective-permute-start(f32[3,8,32,128]{3,2,1,0:T(8,128)S(1)} %get-tuple-element.14), channel_id=1, source_target_pairs={{0,1},{1,0},{2,3},{3,2},{4,5},{5,4},{6,7},{7,6},{8,9},{9,8},{10,11... | collective-permute-start | bytes 1179656 | tf_op jit(solution)/shard_map/ppermute | solution.py:492
  44.0 11.2 %collective-permute-start.1 = (f32[3,8,32,128]{3,2,1,0:T(8,128)S(1)}, f32[3,8,32,128]{3,2,1,0:T(8,128)S(1)}, u32[]{:S(2)}, u32[]{:S(2)}) collective-permute-start(f32[3,8,32,128]{3,2,1,0:T(8,128)S(1)} %add.68.stress_ref.after_ref), channel_id=1, source_target_pairs={{0,2},{1,3},{2,0},{3,1},{4,6},{5,7},{6,4},{7,5},{8,10},{9,11},{10,... | collective-permute-start | bytes 1179656 | tf_op jit(solution)/shard_map/ppermute | solution.py:492
  57.0 26.7 %all-to-all-start.1 = ((f32[8,8,24,128]{3,2,1,0:T(8,128)}), f32[8,8,24,128]{3,2,1,0:T(8,128)S(1)}, u32[]{:S(2)}, u32[]{:S(2)}) async-start(f32[8,8,24,128]{3,2,1,0:T(8,128)} %bitcast.2), calls=%async_computation.1 | async-start | bytes 1572864 | tf_op jit(solution)/shard_map/all_to_all | solution.py:498
  69.7 1.8 %collective-permute-start.2 = (f32[3,8,32,128]{3,2,1,0:T(8,128)S(1)}, f32[3,8,32,128]{3,2,1,0:T(8,128)S(1)}, u32[]{:S(2)}, u32[]{:S(2)}) collective-permute-start(f32[3,8,32,128]{3,2,1,0:T(8,128)S(1)} %get-tuple-element.16), channel_id=1, source_target_pairs={{0,1},{1,0},{2,3},{3,2},{4,5},{5,4},{6,7},{7,6},{8,9},{9,8},{10,11... | collective-permute-start | bytes 1179656 | tf_op jit(solution)/shard_map/ppermute | solution.py:492
  71.6 11.2 %collective-permute-start.3 = (f32[3,8,32,128]{3,2,1,0:T(8,128)S(1)}, f32[3,8,32,128]{3,2,1,0:T(8,128)S(1)}, u32[]{:S(2)}, u32[]{:S(2)}) collective-permute-start(f32[3,8,32,128]{3,2,1,0:T(8,128)S(1)} %add.69.stress_ref), channel_id=1, source_target_pairs={{0,2},{1,3},{2,0},{3,1},{4,6},{5,7},{6,4},{7,5},{8,10},{9,11},{10,... | collective-permute-start | bytes 1179656 | tf_op jit(solution)/shard_map/ppermute | solution.py:492
  113.9 23.3 %all-to-all-start.4 = ((f32[8,4,2,24,128]{4,3,2,1,0:T(8,128)}), f32[8,4,2,24,128]{4,3,2,1,0:T(8,128)S(1)}, u32[]{:S(2)}, u32[]{:S(2)}) async-start(f32[8,4,2,24,128]{4,3,2,1,0:T(8,128)} %solve.2), calls=%async_computation.4 | async-start | bytes 1572864 | tf_op jit(solution)/shard_map/all_to_all | solution.py:504
  137.3 23.9 %all-to-all-start.5 = ((f32[8,4,2,24,128]{4,3,2,1,0:T(8,128)}), f32[8,4,2,24,128]{4,3,2,1,0:T(8,128)S(1)}, u32[]{:S(2)}, u32[]{:S(2)}) async-start(f32[8,4,2,24,128]{4,3,2,1,0:T(8,128)} %solve.3), calls=%async_computation.5 | async-start | bytes 1572864 | tf_op jit(solution)/shard_map/all_to_all | solution.py:504

commit v3 on v2

--- a/solution.py
+++ b/solution.py
@@ -127,12 +127,14 @@
     return lax.dot_general(left, right, (dims, ((), ())), preferred_element_type=jnp.float32)
 
 
-def pack_kernel(near_ref, count_ref, velocity_ref, out_ref):
-    chunks, rows, columns = (velocity_ref.shape[0], velocity_ref.shape[3], velocity_ref.shape[4])
-    out_ref[0, : chunks * rows] = velocity_ref[:, 0, 0].reshape(chunks * rows, columns)
-    if out_ref.shape[1] == chunks * rows:
-        return
-    shape = (out_ref.shape[1] - chunks * rows, columns)
+def pack_kernel(near_ref, count_ref, velocity_ref, *out_refs):
+    chunks, pieces, kx_count, rows, columns = velocity_ref.shape
+    own = lax.axis_index("kx")
+    for index, out_ref in enumerate(out_refs):
+        piece, partner = (index // kx_count, own ^ (index % kx_count))
+        for chunk in range(chunks):
+            out_ref[chunk * rows : (chunk + 1) * rows] = velocity_ref[chunk, piece, partner]
+    shape = (out_refs[0].shape[0] - chunks * rows, columns)
     row = lax.broadcasted_iota(jnp.int32, shape, 0)
     lane = lax.broadcasted_iota(jnp.int32, shape, 1)
     extra = jnp.zeros(shape, jnp.int32)
@@ -142,44 +144,56 @@
         for member in range(members):
             line = jnp.where(lane == member, near_ref[mode, member], line)
         extra = jnp.where(row == mode, line, extra)
-    out_ref[0, chunks * rows :] = extra.astype(jnp.float32)
-
-
-def pack(velocity, neighbours, mode_counts, piece, extra_rows):
+    extra = extra.astype(jnp.float32)
+    for out_ref in out_refs[:kx_count]:
+        out_ref[chunks * rows :] = extra
+
+
+def pack(velocity, neighbours, mode_counts, extra_rows):
     chunks, pieces, kx_count, rows, columns = velocity.shape
-    total = chunks * rows + extra_rows
-    return pl.pallas_call(
+    shapes = []
+    for piece in range(pieces):
+        total = chunks * rows + (0 if piece else extra_rows)
+        shapes += [jax.ShapeDtypeStruct((total, columns), jnp.float32)] * kx_count
+    out = pl.pallas_call(
         pack_kernel,
-        out_shape=jax.ShapeDtypeStruct((kx_count, total, columns), jnp.float32),
-        grid=(kx_count,),
-        in_specs=[
-            SMEM,
-            SMEM,
-            pl.BlockSpec((chunks, 1, 1, rows, columns), lambda k: (0, piece, k, 0, 0)),
-        ],
-        out_specs=pl.BlockSpec((1, total, columns), lambda k: (k, 0, 0)),
-        compiler_params=params(),
+        out_shape=tuple(shapes),
+        in_specs=[SMEM, SMEM, VMEM],
+        out_specs=(VMEM,) * len(shapes),
         name="pack",
     )(neighbours, mode_counts, velocity)
-
-
-def split_matrix_kernel(matrix_ref, top_ref, rest_ref, mark_ref):
-    top, rest = two_parts(matrix_ref[0].T)
-    top_ref[0] = top
-    rest_ref[0] = rest
+    return [out[piece * kx_count : (piece + 1) * kx_count] for piece in range(pieces)]
+
+
+def split_matrix_kernel(matrix_ref, top_ref, rest_ref, mark_ref, turned, *, pieces, kx_count):
+    ht_count, heights, width = turned.shape
+    rows = width // (pieces * kx_count)
+    own_kx, own_ht = (lax.axis_index("kx"), lax.axis_index("ht"))
+    for h in range(ht_count):
+        turned[h] = matrix_ref[0, h * width : (h + 1) * width, :].T
+    for block in range(heights // rows):
+        piece, h, k = (
+            block // (ht_count * kx_count), block // kx_count % ht_count, block % kx_count
+        )
+        source = (((own_ht ^ h) * pieces + piece) * kx_count + (own_kx ^ k)) * rows
+        for j in range(ht_count):
+            value = turned[own_ht ^ j, pl.ds(pl.multiple_of(source, rows), rows), :]
+            place = (0, slice(block * rows, (block + 1) * rows), slice(j * width, (j + 1) * width))
+            top_ref[place], rest_ref[place] = two_parts(value)
     mark_ref[...] = jnp.zeros_like(mark_ref)
 
 
-def split_matrix(helmholtz):
+def split_matrix(helmholtz, pieces, kx_count, ht_count):
     slots, heights, _ = helmholtz.shape
     spec = pl.BlockSpec((1, heights, heights), lambda s: (s, 0, 0))
     shape = jax.ShapeDtypeStruct(helmholtz.shape, jnp.bfloat16)
     return pl.pallas_call(
-        split_matrix_kernel,
+        functools.partial(split_matrix_kernel, pieces=pieces, kx_count=kx_count),
         out_shape=(shape, shape, jax.ShapeDtypeStruct((8, LANES), jnp.float32)),
         grid=(slots,),
         in_specs=[spec],
         out_specs=(spec, spec, pl.BlockSpec((8, LANES), lambda s: (0, 0))),
+        scratch_shapes=[pltpu.VMEM((ht_count, heights, heights // ht_count), jnp.float32)],
         compiler_params=params(),
         cost_estimate=pl.CostEstimate(
             flops=0, bytes_accessed=2 * helmholtz.size * 4, transcendentals=0
@@ -188,13 +202,14 @@
     )(helmholtz)
 
 
-def nonlinear_kernel(
-    low_ref, near_ref, block_ref, first_ref, second_ref, back_ref, mask_ref, after_ref,
-    slotted_ref, stress_ref, physical, products, sums, high_ref,
-):
+def nonlinear_kernel(low_ref, near_ref, *refs):
+    block_refs, refs = (refs[:-11], refs[-11:])
+    first_ref, second_ref, back_ref, mask_ref, _, slotted_ref, stress_ref, *scratch = refs
+    physical, products, sums, high_ref = scratch
     components, modes, rows, columns = slotted_ref.shape
-    bands, points = (block_ref.shape[0], physical.shape[3])
+    bands, points = (len(block_refs), physical.shape[3])
     band_modes = modes // bands
+    own = lax.axis_index("kx")
     members, highs = (stress_ref.shape[1], products.shape[1])
     found = jnp.int32(0)
     for mode in range(modes):
@@ -204,18 +219,18 @@
         high_ref[found] = mode
         found = found + 1 - is_low
 
-    def transform(step, carry):
-        band, component = (step // components, step % components)
+    def transform(component, carry):
         size = band_modes * rows
-        top, rest = two_parts(block_ref[band, pl.ds(pl.multiple_of(component * size, 8), size)])
-        both = dot(jnp.concatenate([top, rest], axis=1), first_ref[...])
-        fields = both[:, :points] + dot(top, second_ref[...])
-        place = pl.ds(band * band_modes, band_modes)
-        physical[component, place] = fields.reshape(band_modes, rows, points)
-        slotted_ref[component, place] = both[:, points:].reshape(band_modes, rows, columns)
+        for index, block_ref in enumerate(block_refs):
+            top, rest = two_parts(block_ref[pl.ds(pl.multiple_of(component * size, 8), size)])
+            both = dot(jnp.concatenate([top, rest], axis=1), first_ref[...])
+            fields = both[:, :points] + dot(top, second_ref[...])
+            place = pl.ds((own ^ index) * band_modes, band_modes)
+            physical[component, place] = fields.reshape(band_modes, rows, points)
+            slotted_ref[component, place] = both[:, points:].reshape(band_modes, rows, columns)
         return carry
 
-    lax.fori_loop(0, bands * components, transform, 0)
+    lax.fori_loop(0, components, transform, 0)
 
     def pairs(step, carry):
         halves = points // LANES
@@ -272,7 +287,7 @@
     lax.fori_loop(0, components, finish, 0)
 
 
-def nonlinear(block, shape, low_index, neighbours, tables, mask, after):
+def nonlinear(blocks, shape, low_index, neighbours, tables, mask, after):
     components, modes, rows, columns = shape
     members, points = (low_index.shape[0], 2 * columns)
     highs = modes - members
@@ -282,7 +297,7 @@
             jax.ShapeDtypeStruct((components, modes, rows, columns), jnp.float32),
             jax.ShapeDtypeStruct((components, members, rows, columns), jnp.float32),
         ),
-        in_specs=[SMEM, SMEM] + [VMEM] * 5 + [pl.BlockSpec(memory_space=pl.ANY)],
+        in_specs=[SMEM, SMEM] + [VMEM] * (len(blocks) + 4) + [pl.BlockSpec(memory_space=pl.ANY)],
         out_specs=(VMEM, VMEM),
         scratch_shapes=[
             pltpu.VMEM((components, modes, rows, points), jnp.float32),
@@ -292,15 +307,17 @@
         ],
         compiler_params=params(),
         name="nonlinear",
-    )(low_index, neighbours, block, *tables, mask, after)
+    )(low_index, neighbours, *blocks, *tables, mask, after)
 
 
 def outgoing_kernel(
-    low_ref, slotted_ref, stress_ref, other_ref, mask_ref, out_ref, full, *, groups, band_modes
+    low_ref, slotted_ref, stress_ref, other_ref, mask_ref, *refs, groups, band_modes
 ):
+    out_refs, full = (refs[:-1], refs[-1])
     components, modes, rows, columns = slotted_ref.shape
-    members = stress_ref.shape[1]
-    per_slot = out_ref.shape[0] // (columns // 2)
+    members, owners = (stress_ref.shape[1], len(out_refs))
+    slots = columns // 2 // owners
+    per_slot = out_refs[0].shape[0] // slots
     full[...] = slotted_ref[...]
     for member in range(members):
         mode = low_ref[member]
@@ -315,19 +332,21 @@
             band_low, band_mode = (part // band_modes, part % band_modes)
             for p in range(2):
                 row = ((band_low * 2 + p) * components + c) * band_modes + band_mode
-                out_ref[pl.ds(row, columns // 2, stride=per_slot), :] = turned[
-                    p * (columns // 2) : (p + 1) * (columns // 2)
-                ]
-
-
-def outgoing(slotted, stress, other, low_index, mask, groups, band_modes):
+                for owner in range(owners):
+                    start = (p * owners + owner) * slots
+                    out_refs[owner][pl.ds(row, slots, stride=per_slot), :] = turned[
+                        start : start + slots
+                    ]
+
+
+def outgoing(slotted, stress, other, low_index, mask, groups, band_modes, owners):
     components, modes, rows, columns = slotted.shape
-    per_slot = (modes // groups) * 2 * components
+    total = (columns // 2 // owners) * (modes // groups) * 2 * components
     return pl.pallas_call(
         functools.partial(outgoing_kernel, groups=groups, band_modes=band_modes),
-        out_shape=jax.ShapeDtypeStruct((columns // 2 * per_slot, groups * rows), jnp.float32),
+        out_shape=(jax.ShapeDtypeStruct((total, groups * rows), jnp.float32),) * owners,
         in_specs=[SMEM, VMEM, VMEM, VMEM, VMEM],
-        out_specs=VMEM,
+        out_specs=(VMEM,) * owners,
         scratch_shapes=[pltpu.VMEM(slotted.shape, jnp.float32)],
         compiler_params=params(),
         name="outgoing",
@@ -351,47 +370,70 @@
     return blocks
 
 
-def solve_kernel(*refs, groups, kx_count, ht_count):
-    pieces = len(refs) - 3
-    block_refs, (top_ref, rest_ref, out_ref) = (refs[:pieces], refs[pieces:])
+def solve_kernel(*refs, groups, kx_count, ht_count, started, last):
+    owners = kx_count * ht_count
+    block_refs, (top_ref, rest_ref), refs = (
+        refs[:owners], refs[owners : owners + 2], refs[owners + 2 :]
+    )
     rows = LANES // groups
     tiles = []
     for h in range(ht_count):
-        for piece in range(pieces):
-            for first in range(0, kx_count, groups):
-                blocks = [
-                    block_refs[piece][(first + g) * ht_count + h, 0] for g in range(groups)
-                ]
-                tiles.append(jnp.concatenate(regroup(blocks, rows), axis=0))
+        for first in range(0, kx_count, groups):
+            blocks = [block_refs[(first + g) * ht_count + h][0] for g in range(groups)]
+            tiles.append(jnp.concatenate(regroup(blocks, rows), axis=0))
     top, rest = two_parts(jnp.concatenate(tiles, axis=1))
     count = top.shape[0]
     both = dot(jnp.concatenate([top, rest], axis=0), top_ref[0])
     solved = both[:count] + both[count:] + dot(top, rest_ref[0])
-    lane_tiles, per_band = out_ref.shape[2:4]
-    for band in range(kx_count):
+    if started:
+        solved, refs = (solved + refs[0][0], refs[1:])
+    if not last:
+        refs[0][0] = solved
+        return
+    out_refs, full = (refs[:owners], refs[owners])
+    full[...] = solved
+    own = lax.axis_index("kx")
+    lane_tiles, per_band = out_refs[0].shape[1:3]
+    for k in range(kx_count):
+        band = pl.ds(pl.multiple_of((own ^ k) * per_band, 8), per_band)
         for tile in range(ht_count * lane_tiles):
-            out_ref[band * ht_count + tile // lane_tiles, 0, tile % lane_tiles] = solved[
-                band * per_band : (band + 1) * per_band, tile * LANES : (tile + 1) * LANES
+            out_refs[k * ht_count + tile // lane_tiles][0, tile % lane_tiles] = full[
+                band, tile * LANES : (tile + 1) * LANES
             ]
 
 
-def solve(blocks, matrices, groups, kx_count, ht_count, first, slots):
-    owners, _, per_slot, lanes = blocks[0].shape
-    heights = matrices[0].shape[1]
-    lane_tiles = heights // ht_count // LANES
-    out = (owners, slots, lane_tiles, per_slot * groups // kx_count, LANES)
+def solve(blocks, matrices, piece, pieces, partial, groups, kx_count, ht_count):
+    slots, per_slot, lanes = blocks[0].shape
+    heights, last = (matrices[0].shape[2], piece == pieces - 1)
+    count, owners = (per_slot * groups, kx_count * ht_count)
+    whole = pl.BlockSpec((1, count, heights), lambda s: (s, 0, 0))
+    if last:
+        shape = (slots, heights // ht_count // LANES, count // kx_count, LANES)
+        out_shape = (jax.ShapeDtypeStruct(shape, jnp.float32),) * owners
+        out_specs = (pl.BlockSpec((1,) + shape[1:], lambda s: (s, 0, 0, 0)),) * owners
+        scratch = [pltpu.VMEM((count, heights), jnp.float32)]
+    else:
+        out_shape = jax.ShapeDtypeStruct((slots, count, heights), jnp.float32)
+        out_specs, scratch = (whole, [])
     return pl.pallas_call(
-        functools.partial(solve_kernel, groups=groups, kx_count=kx_count, ht_count=ht_count),
-        out_shape=jax.ShapeDtypeStruct(out, jnp.float32),
+        functools.partial(
+            solve_kernel, groups=groups, kx_count=kx_count, ht_count=ht_count,
+            started=partial is not None, last=last,
+        ),
+        out_shape=out_shape,
         grid=(slots,),
-        in_specs=[
-            pl.BlockSpec((owners, 1, per_slot, lanes), lambda s: (0, first + s, 0, 0))
-        ] * len(blocks)
-        + [pl.BlockSpec((1, heights, heights), lambda s: (first + s, 0, 0))] * 2,
-        out_specs=pl.BlockSpec((owners, 1) + out[2:], lambda s: (0, s, 0, 0, 0)),
+        in_specs=[pl.BlockSpec((1, per_slot, lanes), lambda s: (s, 0, 0))] * owners
+        + [pl.BlockSpec((1, heights // pieces, heights), lambda s: (s, piece, 0))] * 2
+        + ([] if partial is None else [whole]),
+        out_specs=out_specs,
+        scratch_shapes=scratch,
         compiler_params=params(),
+        cost_estimate=pl.CostEstimate(
+            flops=6 * slots * count * heights * heights // pieces,
+            bytes_accessed=slots * heights * heights * 4 // pieces, transcendentals=0,
+        ),
         name="solve",
-    )(*blocks, *matrices)
+    )(*blocks, *matrices, *([] if partial is None else [partial]))
 
 
 def restore_kernel(*refs):
@@ -431,7 +473,7 @@
     return top.astype(jnp.bfloat16), (value - top).astype(jnp.bfloat16)
 
 
-def slot_tables(owner_map, columns, owners, pieces):
+def slot_tables(owner_map, columns):
     forward, backward = spanwise_tables(columns // 2, 2 * columns)
     slot_columns = (2 * owner_map[None, :] + jnp.arange(2)[:, None]).reshape(columns)
     select = slot_columns[None, :] == jnp.arange(columns)[:, None]
@@ -442,8 +484,7 @@
         backward, select.astype(jnp.float32), precision=lax.Precision.HIGHEST
     )
     back = jnp.concatenate(table_parts(slotted_back), axis=1)
-    order = select.T.reshape(2, owners, pieces, -1, columns).transpose(0, 2, 1, 3, 4)
-    order = order.reshape(columns, columns).astype(jnp.bfloat16)
+    order = select.T.astype(jnp.bfloat16)
     order = jnp.concatenate([order, order], axis=0)
     return (first, forward_rest, back), order
 
@@ -454,16 +495,28 @@
     return mask, mask / realizations
 
 
+def partners(count, step):
+    return [(index, index ^ step) for index in range(count)]
+
+
+def exchange(blocks, axes):
+    result = list(blocks)
+    for step in range(len(blocks) - 1, 0, -1):
+        result[step] = lax.ppermute(blocks[step], axes, partners(len(blocks), step))
+    return result
+
+
 def local(velocity, low_index, neighbours, owner_map, mode_counts, helmholtz):
     components, reals_dev, band_modes, rows_ht, columns = velocity.shape
     kx_count, ht_count = (lax.axis_size("kx"), lax.axis_size("ht"))
+    own_kx, own_ht = (lax.axis_index("kx"), lax.axis_index("ht"))
     owners, pieces, real_count = (kx_count * ht_count, PIECES, lax.axis_size("real"))
     rows = rows_ht // (kx_count * pieces)
     groups = LANES // rows if rows else 0
     slots = columns // 2 // owners
     if (
         columns != LANES or reals_dev != 1 or rows_ht % LANES or rows % 8 or LANES % rows or kx_count % groups
-        or (band_modes * 2 * components) % 8 or slots % 8 or slots // pieces * owners % 8 or low_index.shape[0] >= kx_count * band_modes
+        or (band_modes * 2 * components) % 8 or slots % 8 or owners & (owners - 1) or low_index.shape[0] >= kx_count * band_modes
         or low_index.shape[0] >= columns or real_count < 2 or real_count & (real_count - 1)
     ):
         return local_plain(velocity, low_index, neighbours, owner_map, mode_counts, helmholtz)
@@ -472,15 +525,20 @@
     shape = (components, modes, rows, columns)
     extra_rows = -(-band_modes // 8) * 8
     split = velocity.reshape(chunks, pieces, kx_count, rows, columns)
-    parts = []
-    for piece in range(pieces):
-        part = pack(split, neighbours, mode_counts, piece, 0 if piece else extra_rows)
-        parts.append(lax.all_to_all(part, "kx", split_axis=0, concat_axis=0, tiled=True))
-    *matrices, after = split_matrix(helmholtz)
-    small = parts[0][:, chunks * rows : chunks * rows + band_modes, : members + 1]
+    everyone = (own_kx * ht_count + own_ht) ^ jnp.arange(owners)
+    owner_map = owner_map.reshape(owners, slots)[everyone].reshape(-1)
+    parts = [
+        exchange(blocks, "kx") for blocks in pack(split, neighbours, mode_counts, extra_rows)
+    ]
+    *matrices, after = split_matrix(helmholtz, pieces, kx_count, ht_count)
+    small = 0.0
+    for index, block in enumerate(parts[0]):
+        lines = block[chunks * rows : chunks * rows + band_modes, : members + 1]
+        here = (own_kx ^ index) == jnp.arange(kx_count)
+        small = small + jnp.where(here[:, None, None], lines[None], 0.0)
     small = small.reshape(modes, members + 1).astype(jnp.int32)
     neighbours, mode_counts = (small[:, :-1], small[:, -1])
-    tables, order = slot_tables(owner_map, columns, owners, pieces)
+    tables, order = slot_tables(owner_map, columns)
     mask, low_mask = slot_masks(owner_map, mode_counts, realizations)
     received = []
     for part in parts:
@@ -488,21 +546,18 @@
         step, other = (1, None)
         while step < realizations:
             stress = stress if other is None else stress + other
-            exchange = [(i, i ^ step) for i in range(realizations)]
-            other = lax.ppermute(stress, "real", exchange)
+            other = lax.ppermute(stress, "real", partners(realizations, step))
             step *= 2
         after = stress
-        block = outgoing(slotted, stress, other, low_index, low_mask, groups, band_modes)
-        block = block.reshape(owners, slots, -1, LANES)
-        received.append(
-            lax.all_to_all(block, ("kx", "ht"), split_axis=0, concat_axis=0, tiled=True)
+        blocks = outgoing(
+            slotted, stress, other, low_index, low_mask, groups, band_modes, owners
         )
-    returned = []
-    for piece in range(pieces):
-        count = slots // pieces
-        solved = solve(received, matrices, groups, kx_count, ht_count, piece * count, count)
-        solved = lax.all_to_all(solved, ("kx", "ht"), split_axis=0, concat_axis=0, tiled=True)
-        returned.append(solved.reshape(-1, LANES))
+        blocks = [block.reshape(slots, -1, LANES) for block in blocks]
+        received.append(exchange(blocks, ("kx", "ht")))
+    solved = None
+    for piece, blocks in enumerate(received):
+        solved = solve(blocks, matrices, piece, pieces, solved, groups, kx_count, ht_count)
+    returned = [block.reshape(-1, LANES) for block in exchange(solved, ("kx", "ht"))]
     result = restore(returned, order, components, band_modes, rows_ht)
     return result.reshape(velocity.shape)
 

time: 164 us -> 156 us (0.951)
  the two profiles are of different devices: /device:TPU:0 before, /device:TPU:10 now
where the time goes in v3:
time: 156 us; the launch traced here: 155 us
  waiting for transfers between devices  70.1 us (45%)
  starting transfers between devices  39.6 us (25%)
  Pallas kernels  38.4 us (25%)
  local copies, waits for them, and re-layouts  5.13 us (3%)
    ppermute x27, waiting for transfers between devices, exchange(): result[step] = lax.ppermute(blocks[step], axes, partners(len(blocks), step))  57 us
    ppermute x27, starting transfers between devices, exchange(): result[step] = lax.ppermute(blocks[step], axes, partners(len(blocks), step))  38.2 us
    ppermute x4, waiting for transfers between devices, local(): other = lax.ppermute(stress, 'real', partners(realizations, step))  13.2 us
    pallas_call x2, Pallas kernels, solve(): pl.pallas_call(functools.partial(solve_kernel, groups=groups, kx_count=kx...  12.2 us
    pallas_call x2, Pallas kernels, nonlinear(): pl.pallas_call(nonlinear_kernel, out_shape=(jax.ShapeDtypeStruct((compone...  10.7 us
    pallas_call x1, Pallas kernels, split_matrix(): pl.pallas_call(functools.partial(split_matrix_kernel, pieces=pieces, kx_c...  9.06 us
  transfers between devices with their start and end apart: 31, of which 18 were waited for; matrix products, arithmetic and copies ran while one was open for 3% of the time, Pallas kernels for 11%

profile of v3, /device:TPU:10, one launch (start us, length us, event | category | flops | bytes accessed | tf_op | source)
XLA Modules:
  0.0 155.4 jit_solution(1947884418169805163)
XLA Ops:
  0.0 2.7 %pack.1 = (f32[392,128]{1,0:T(8,128)}, f32[392,128]{1,0:T(8,128)}, f32[392,128]{1,0:T(8,128)}, f32[392,128]{1,0:T(8,128)}, f32[384,128]{1,0:T(8,128)}, /*index=5...) custom-call(s32[4,8]{1,0:T(4,128)} %near_ref.1, s32[4]{0:T(128)} %count_ref.1, f32[12,2,4,32,128]{4,3,2,1,0:T(8,128)} %bitcast.61), custom_call_target="tpu_custom_call" | custom-call | tf_op jit(solution)/shard_map/pack/pallas_call | solution.py:158
  2.7 1.6 %collective-permute-start.2 = (f32[392,128]{1,0:T(8,128)}, f32[392,128]{1,0:T(8,128)S(1)}, u32[]{:S(2)}, u32[]{:S(2)}) collective-permute-start(f32[392,128]{1,0:T(8,128)} %get-tuple-element.47), channel_id=1, source_target_pairs={{0,24},{8,16},{16,8},{24,0},{1,25},{9,17},{17,9},{25,1},{2,26},{10... | collective-permute-start | bytes 602120 | tf_op jit(solution)/shard_map/ppermute | solution.py:505
  4.2 1.2 collective-permute-start.1
  5.5 1.2 collective-permute-start
  6.7 0.7 reshape.294
  7.5 0.6 gather_fusion
  8.2 0.1 iota_compare_fusion
  8.3 0.6 fusion.3
  8.9 0.7 reduce-precision_convert_fusion
  9.6 0.7 slice.20
  10.4 0.1 broadcast_in_dim.131
  10.6 0.1 broadcast_in_dim.126
  10.9 0.1 broadcast_in_dim.115
  11.1 9.1 %split_matrix.1 = (bf16[8,512,512]{2,1,0:T(8,128)(2,1)S(1)}, bf16[8,512,512]{2,1,0:T(8,128)(2,1)}, f32[8,128]{1,0:T(8,128)S(1)}) custom-call(f32[8,512,512]{2,1,0:T(8,128)} %matrix_ref.1), custom_call_target="tpu_custom_call" | custom-call | bytes 16777216 | tf_op jit(solution)/shard_map/split_matrix/pallas_call | solution.py:190
  20.2 2.0 %copy-done = bf16[8,512,512]{2,1,0:T(8,128)(2,1)} copy-done((bf16[8,512,512]{2,1,0:T(8,128)(2,1)}, bf16[8,512,512]{2,1,0:T(8,128)(2,1)S(1)}, u32[]{:S(2)}) %copy-start) | copy-done | bytes 4194328
  22.5 0.2 slice_reduce_fusion
  22.6 0.1 broadcast_multiply_fusion
  22.8 5.4 %nonlinear.2 = (f32[3,16,32,128]{3,2,1,0:T(8,128)S(1)}, f32[3,8,32,128]{3,2,1,0:T(8,128)S(1)}) custom-call(s32[8]{0:T(128)S(1)} %copy-done.3, s32[16,8]{1,0:T(8,128)S(1)} %bitcast.43, f32[392,128]{1,0:T(8,128)S(1)} %copy-done.1, f32[392,128]{1,0:T(8,128)S(1)} %collective-permute-done.refs_1_, f32[392,128]{1,0:T(8,128)S(1)} %collective-permute-done.1.refs_2_, ...), custom_call_target="tpu_custom_call" | custom-call | tf_op jit(solution)/shard_map/nonlinear/pallas_call | solution.py:294
  28.2 1.7 %collective-permute-start.3 = (f32[384,128]{1,0:T(8,128)S(1)}, f32[384,128]{1,0:T(8,128)S(1)}, u32[]{:S(2)}, u32[]{:S(2)}) collective-permute-start(f32[384,128]{1,0:T(8,128)S(1)} %copy-done.6), channel_id=1, source_target_pairs={{0,8},{8,0},{16,24},{24,16},{1,9},{9,1},{17,25},{25,17},{2,10},{10... | collective-permute-start | bytes 589832 | tf_op jit(solution)/shard_map/ppermute | solution.py:505
  29.9 1.4 collective-permute-start.4
  31.3 0.5 collective-permute-start.5
  31.9 6.6 %collective-permute-done.3.refs_1_ = f32[384,128]{1,0:T(8,128)S(1)} collective-permute-done((f32[384,128]{1,0:T(8,128)S(1)}, f32[384,128]{1,0:T(8,128)S(1)}, u32[]{:S(2)}, u32[]{:S(2)}) %collective-permute-start.3) | collective-permute-done | bytes 196640 | tf_op jit(solution)/shard_map/ppermute | solution.py:505
  38.5 6.4 %collective-permute-done.4.refs_2_ = f32[384,128]{1,0:T(8,128)S(1)} collective-permute-done((f32[384,128]{1,0:T(8,128)S(1)}, f32[384,128]{1,0:T(8,128)S(1)}, u32[]{:S(2)}, u32[]{:S(2)}) %collective-permute-start.4) | collective-permute-done | bytes 196640 | tf_op jit(solution)/shard_map/ppermute | solution.py:505
  45.0 4.7 %collective-permute-done.5.refs_3_ = f32[384,128]{1,0:T(8,128)S(1)} collective-permute-done((f32[384,128]{1,0:T(8,128)S(1)}, f32[384,128]{1,0:T(8,128)S(1)}, u32[]{:S(2)}, u32[]{:S(2)}) %collective-permute-start.5) | collective-permute-done | bytes 196640 | tf_op jit(solution)/shard_map/ppermute | solution.py:505
  49.7 5.4 %nonlinear.3 = (f32[3,16,32,128]{3,2,1,0:T(8,128)S(1)}, f32[3,8,32,128]{3,2,1,0:T(8,128)S(1)}) custom-call(s32[8]{0:T(128)S(1)} %copy-done.3, s32[16,8]{1,0:T(8,128)S(1)} %bitcast.44, f32[384,128]{1,0:T(8,128)S(1)} %copy-done.2, f32[384,128]{1,0:T(8,128)S(1)} %collective-permute-done.3.refs_1_, f32[384,128]{1,0:T(8,128)S(1)} %collective-permute-done.4.refs_2_, ...), custom_call_target="tpu_custom_call" | custom-call | tf_op jit(solution)/shard_map/nonlinear/pallas_call | solution.py:294
  55.1 0.6 collective-permute-start.16
  55.7 1.1 collective-permute-done.7
  56.9 0.6 collective-permute-start.8
  57.5 9.6 %collective-permute-done.16.other_ref = f32[3,8,32,128]{3,2,1,0:T(8,128)S(1)} collective-permute-done((f32[3,8,32,128]{3,2,1,0:T(8,128)S(1)}, f32[3,8,32,128]{3,2,1,0:T(8,128)S(1)}, u32[]{:S(2)}, u32[]{:S(2)}) %collective-permute-start.16) | collective-permute-done | bytes 393248 | tf_op jit(solution)/shard_map/ppermute | solution.py:549
  67.1 0.9 outgoing.3
  68.0 1.6 %collective-permute-start.17 = (f32[8,24,128]{2,1,0:T(8,128)S(1)}, f32[8,24,128]{2,1,0:T(8,128)S(1)}, u32[]{:S(2)}, u32[]{:S(2)}) collective-permute-start(f32[8,24,128]{2,1,0:T(8,128)S(1)} %bitcast.60), channel_id=1, source_target_pairs={{0,4},{4,0},{8,12},{12,8},{16,20},{20,16},{24,28},{28,24},{1,5},{5... | collective-permute-start | bytes 294920 | tf_op jit(solution)/shard_map/ppermute | solution.py:505
  69.6 1.9 %collective-permute-start.19 = (f32[8,24,128]{2,1,0:T(8,128)S(1)}, f32[8,24,128]{2,1,0:T(8,128)S(1)}, u32[]{:S(2)}, u32[]{:S(2)}) collective-permute-start(f32[8,24,128]{2,1,0:T(8,128)S(1)} %bitcast.58), channel_id=1, source_target_pairs={{0,12},{4,8},{8,4},{12,0},{16,28},{20,24},{24,20},{28,16},{1,13},{... | collective-permute-start | bytes 294920 | tf_op jit(solution)/shard_map/ppermute | solution.py:505
  71.6 1.1 collective-permute-start.20
  72.6 2.4 %collective-permute-done.8.other_ref = f32[3,8,32,128]{3,2,1,0:T(8,128)S(1)} collective-permute-done((f32[3,8,32,128]{3,2,1,0:T(8,128)S(1)}, f32[3,8,32,128]{3,2,1,0:T(8,128)S(1)}, u32[]{:S(2)}, u32[]{:S(2)}) %collective-permute-start.8) | collective-permute-done | bytes 393248 | tf_op jit(solution)/shard_map/ppermute | solution.py:549
  75.1 0.4 collective-permute-start.21
  75.5 0.9 outgoing.2
  76.4 1.6 %collective-permute-start.22 = (f32[8,24,128]{2,1,0:T(8,128)S(1)}, f32[8,24,128]{2,1,0:T(8,128)S(1)}, u32[]{:S(2)}, u32[]{:S(2)}) collective-permute-start(f32[8,24,128]{2,1,0:T(8,128)S(1)} %bitcast.53), channel_id=1, source_target_pairs={{0,24},{4,28},{8,16},{12,20},{16,8},{20,12},{24,0},{28,4},{1,25},{... | collective-permute-start | bytes 294920 | tf_op jit(solution)/shard_map/ppermute | solution.py:505
  78.0 1.1 collective-permute-start.23
  79.1 0.9 collective-permute-start.9
  80.0 5.4 %collective-permute-start.10 = (f32[8,24,128]{2,1,0:T(8,128)S(1)}, f32[8,24,128]{2,1,0:T(8,128)S(1)}, u32[]{:S(2)}, u32[]{:S(2)}) collective-permute-start(f32[8,24,128]{2,1,0:T(8,128)S(1)} %bitcast.55), channel_id=1, source_target_pairs={{0,8},{4,12},{8,0},{12,4},{16,24},{20,28},{24,16},{28,20},{1,9},{5... | collective-permute-start | bytes 294920 | tf_op jit(solution)/shard_map/ppermute | solution.py:505
  85.4 2.9 %collective-permute-start.11 = (f32[8,24,128]{2,1,0:T(8,128)S(1)}, f32[8,24,128]{2,1,0:T(8,128)S(1)}, u32[]{:S(2)}, u32[]{:S(2)}) collective-permute-start(f32[8,24,128]{2,1,0:T(8,128)S(1)} %bitcast.51), channel_id=1, source_target_pairs={{0,12},{4,8},{8,4},{12,0},{16,28},{20,24},{24,20},{28,16},{1,13},{... | collective-permute-start | bytes 294920 | tf_op jit(solution)/shard_map/ppermute | solution.py:505
  88.3 0.9 collective-permute-done.22.refs_6_
  89.2 2.9 %collective-permute-done.23.refs_7_ = f32[8,24,128]{2,1,0:T(8,128)S(1)} collective-permute-done((f32[8,24,128]{2,1,0:T(8,128)S(1)}, f32[8,24,128]{2,1,0:T(8,128)S(1)}, u32[]{:S(2)}, u32[]{:S(2)}) %collective-permute-start.23) | collective-permute-done | bytes 98336 | tf_op jit(solution)/shard_map/ppermute | solution.py:505
  92.1 0.5 collective-permute-start.13
  92.6 0.9 collective-permute-start.14
  93.5 1.5 collective-permute-start.15
  95.0 6.0 %solve.2.refs_10_ = f32[8,96,512]{2,1,0:T(8,128)S(1)} custom-call(f32[8,24,128]{2,1,0:T(8,128)S(1)} %bitcast.46, f32[8,24,128]{2,1,0:T(8,128)S(1)} %collective-permute-done.17.refs_1_, f32[8,24,128]{2,1,0:T(8,128)S(1)} %collective-permute-done.18.refs_2_, f32[8,24,128]{2,1,0:T(8,128)S(1)} %collective-permute-done.19.refs_3_, ...), custom_call_target="tpu_custom_call" | custom-call | flops 603979776 | bytes 4194304 | tf_op jit(solution)/shard_map/solve/pallas_call | solution.py:418
  101.1 1.7 %collective-permute-done.13.refs_5_ = f32[8,24,128]{2,1,0:T(8,128)S(1)} collective-permute-done((f32[8,24,128]{2,1,0:T(8,128)S(1)}, f32[8,24,128]{2,1,0:T(8,128)S(1)}, u32[]{:S(2)}, u32[]{:S(2)}) %collective-permute-start.13) | collective-permute-done | bytes 98336 | tf_op jit(solution)/shard_map/ppermute | solution.py:505
  102.8 2.9 %collective-permute-done.14.refs_6_ = f32[8,24,128]{2,1,0:T(8,128)S(1)} collective-permute-done((f32[8,24,128]{2,1,0:T(8,128)S(1)}, f32[8,24,128]{2,1,0:T(8,128)S(1)}, u32[]{:S(2)}, u32[]{:S(2)}) %collective-permute-start.14) | collective-permute-done | bytes 98336 | tf_op jit(solution)/shard_map/ppermute | solution.py:505
  105.7 2.4 %collective-permute-done.15.refs_7_ = f32[8,24,128]{2,1,0:T(8,128)S(1)} collective-permute-done((f32[8,24,128]{2,1,0:T(8,128)S(1)}, f32[8,24,128]{2,1,0:T(8,128)S(1)}, u32[]{:S(2)}, u32[]{:S(2)}) %collective-permute-start.15) | collective-permute-done | bytes 98336 | tf_op jit(solution)/shard_map/ppermute | solution.py:505
  108.1 6.2 %solve.3 = (f32[8,2,24,128]{3,2,1,0:T(8,128)S(1)}, f32[8,2,24,128]{3,2,1,0:T(8,128)S(1)}, f32[8,2,24,128]{3,2,1,0:T(8,128)S(1)}, f32[8,2,24,128]{3,2,1,0:T(8,128...) custom-call(f32[8,24,128]{2,1,0:T(8,128)S(1)} %bitcast.45, ...), custom_call_target="tpu_custom_call" | custom-call | flops 603979776 | bytes 4194304 | tf_op jit(solution)/shard_map/solve/pallas_call | solution.py:418
  114.3 1.1 collective-permute-start.24
  115.4 2.5 %collective-permute-start.26 = (f32[8,2,24,128]{3,2,1,0:T(8,128)S(1)}, f32[8,2,24,128]{3,2,1,0:T(8,128)S(1)}, u32[]{:S(2)}, u32[]{:S(2)}) collective-permute-start(f32[8,2,24,128]{3,2,1,0:T(8,128)S(1)} %get-tuple-element.78), channel_id=1, source_target_pairs={{0,12},{4,8},{8,4},{12,0},{16,28},{20,24},{24,20},{28,16},{1,13},{... | collective-permute-start | bytes 589832 | tf_op jit(solution)/shard_map/ppermute | solution.py:505
  117.8 1.2 collective-permute-start.27
  119.0 2.2 %collective-permute-start.28 = (f32[8,2,24,128]{3,2,1,0:T(8,128)S(1)}, f32[8,2,24,128]{3,2,1,0:T(8,128)S(1)}, u32[]{:S(2)}, u32[]{:S(2)}) collective-permute-start(f32[8,2,24,128]{3,2,1,0:T(8,128)S(1)} %get-tuple-element.80), channel_id=1, source_target_pairs={{0,20},{4,16},{8,28},{12,24},{16,4},{20,0},{24,12},{28,8},{1,21},{... | collective-permute-start | bytes 589832 | tf_op jit(solution)/shard_map/ppermute | solution.py:505
  121.3 1.8 %collective-permute-start.29 = (f32[8,2,24,128]{3,2,1,0:T(8,128)S(1)}, f32[8,2,24,128]{3,2,1,0:T(8,128)S(1)}, u32[]{:S(2)}, u32[]{:S(2)}) collective-permute-start(f32[8,2,24,128]{3,2,1,0:T(8,128)S(1)} %get-tuple-element.81), channel_id=1, source_target_pairs={{0,24},{4,28},{8,16},{12,20},{16,8},{20,12},{24,0},{28,4},{1,25},{... | collective-permute-start | bytes 589832 | tf_op jit(solution)/shard_map/ppermute | solution.py:505
  123.0 4.5 %collective-permute-done.25 = f32[8,2,24,128]{3,2,1,0:T(8,128)S(1)} collective-permute-done((f32[8,2,24,128]{3,2,1,0:T(8,128)S(1)}, f32[8,2,24,128]{3,2,1,0:T(8,128)S(1)}, u32[]{:S(2)}, u32[]{:S(2)}) %collective-permute-start.25) | collective-permute-done | bytes 196640 | tf_op jit(solution)/shard_map/ppermute | solution.py:505
  127.6 2.1 %collective-permute-start.30 = (f32[8,2,24,128]{3,2,1,0:T(8,128)S(1)}, f32[8,2,24,128]{3,2,1,0:T(8,128)S(1)}, u32[]{:S(2)}, u32[]{:S(2)}) collective-permute-start(f32[8,2,24,128]{3,2,1,0:T(8,128)S(1)} %get-tuple-element.82), channel_id=1, source_target_pairs={{0,28},{4,24},{8,20},{12,16},{16,12},{20,8},{24,4},{28,0},{1,29},{... | collective-permute-start | bytes 589832 | tf_op jit(solution)/shard_map/ppermute | solution.py:505
  129.7 1.1 collective-permute-done.26
  130.8 1.2 collective-permute-done.27
  131.9 13.5 %collective-permute-done.28 = f32[8,2,24,128]{3,2,1,0:T(8,128)S(1)} collective-permute-done((f32[8,2,24,128]{3,2,1,0:T(8,128)S(1)}, f32[8,2,24,128]{3,2,1,0:T(8,128)S(1)}, u32[]{:S(2)}, u32[]{:S(2)}) %collective-permute-start.28) | collective-permute-done | bytes 196640 | tf_op jit(solution)/shard_map/ppermute | solution.py:505
  145.5 5.2 %collective-permute-done.29 = f32[8,2,24,128]{3,2,1,0:T(8,128)S(1)} collective-permute-done((f32[8,2,24,128]{3,2,1,0:T(8,128)S(1)}, f32[8,2,24,128]{3,2,1,0:T(8,128)S(1)}, u32[]{:S(2)}, u32[]{:S(2)}) %collective-permute-start.29) | collective-permute-done | bytes 196640 | tf_op jit(solution)/shard_map/ppermute | solution.py:505
  150.7 2.8 %collective-permute-done.30 = f32[8,2,24,128]{3,2,1,0:T(8,128)S(1)} collective-permute-done((f32[8,2,24,128]{3,2,1,0:T(8,128)S(1)}, f32[8,2,24,128]{3,2,1,0:T(8,128)S(1)}, u32[]{:S(2)}, u32[]{:S(2)}) %collective-permute-start.30) | collective-permute-done | bytes 196640 | tf_op jit(solution)/shard_map/ppermute | solution.py:505
  153.5 2.0 %restore.1 = f32[3,4,256,128]{3,2,1,0:T(8,128)} custom-call(f32[384,128]{1,0:T(8,128)S(1)} %bitcast.35, f32[384,128]{1,0:T(8,128)S(1)} %bitcast.36, f32[384,128]{1,0:T(8,128)S(1)} %bitcast.37, f32[384,128]{1,0:T(8,128)S(1)} %bitcast.38, f32[384,128]{1,0:T(8,128)S(1)} %bitcast.39, f32[384,128]{1,0:T(8,128)S(1)} %bitcast.40, f32[384,128]{1,0:T(8,128)S(1)} %bitcast.41, ...), custom_call_target="tpu_custom_call" | custom-call | tf_op jit(solution)/shard_map/restore/pallas_call | solution.py:461
  (65 shorter events, 1.2 us)
Async XLA Ops:
  2.7 19.6 %collective-permute-start.2 = (f32[392,128]{1,0:T(8,128)}, f32[392,128]{1,0:T(8,128)S(1)}, u32[]{:S(2)}, u32[]{:S(2)}) collective-permute-start(f32[392,128]{1,0:T(8,128)} %get-tuple-element.47), channel_id=1, source_target_pairs={{0,24},{8,16},{16,8},{24,0},{1,25},{9,17},{17,9},{25,1},{2,26},{10... | collective-permute-start | bytes 602120 | tf_op jit(solution)/shard_map/ppermute | solution.py:505
  4.2 18.0 %collective-permute-start.1 = (f32[392,128]{1,0:T(8,128)}, f32[392,128]{1,0:T(8,128)S(1)}, u32[]{:S(2)}, u32[]{:S(2)}) collective-permute-start(f32[392,128]{1,0:T(8,128)} %get-tuple-element.46), channel_id=1, source_target_pairs={{0,16},{8,24},{16,0},{24,8},{1,17},{9,25},{17,1},{25,9},{2,18},{10... | collective-permute-start | bytes 602120 | tf_op jit(solution)/shard_map/ppermute | solution.py:505
  5.5 16.8 %collective-permute-start = (f32[392,128]{1,0:T(8,128)}, f32[392,128]{1,0:T(8,128)S(1)}, u32[]{:S(2)}, u32[]{:S(2)}) collective-permute-start(f32[392,128]{1,0:T(8,128)} %get-tuple-element.45), channel_id=1, source_target_pairs={{0,8},{8,0},{16,24},{24,16},{1,9},{9,1},{17,25},{25,17},{2,10},{10... | collective-permute-start | bytes 602120 | tf_op jit(solution)/shard_map/ppermute | solution.py:505
  11.1 11.6 %copy-start.1 = (f32[392,128]{1,0:T(8,128)S(1)}, f32[392,128]{1,0:T(8,128)}, u32[]{:S(2)}) copy-start(f32[392,128]{1,0:T(8,128)} %get-tuple-element.44.refs_0_) | copy-start | bytes 602116
  11.1 11.6 %copy-start.3 = (s32[8]{0:T(128)S(1)}, s32[8]{0:T(128)}, u32[]{:S(2)}) copy-start(s32[8]{0:T(128)} %low_ref.7) | copy-start | bytes 100
  11.1 17.1 %copy-start.6 = (f32[384,128]{1,0:T(8,128)S(1)}, f32[384,128]{1,0:T(8,128)}, u32[]{:S(2)}) copy-start(f32[384,128]{1,0:T(8,128)} %get-tuple-element.49) | copy-start | bytes 589828
  11.1 18.8 %copy-start.5 = (f32[384,128]{1,0:T(8,128)S(1)}, f32[384,128]{1,0:T(8,128)}, u32[]{:S(2)}) copy-start(f32[384,128]{1,0:T(8,128)} %get-tuple-element.50) | copy-start | bytes 589828
  11.1 20.2 %copy-start.4 = (f32[384,128]{1,0:T(8,128)S(1)}, f32[384,128]{1,0:T(8,128)}, u32[]{:S(2)}) copy-start(f32[384,128]{1,0:T(8,128)} %get-tuple-element.51) | copy-start | bytes 589828
  11.1 38.5 %copy-start.2 = (f32[384,128]{1,0:T(8,128)S(1)}, f32[384,128]{1,0:T(8,128)}, u32[]{:S(2)}) copy-start(f32[384,128]{1,0:T(8,128)} %get-tuple-element.48.refs_0_) | copy-start | bytes 589828
  20.2 2.0 %copy-start = (bf16[8,512,512]{2,1,0:T(8,128)(2,1)}, bf16[8,512,512]{2,1,0:T(8,128)(2,1)S(1)}, u32[]{:S(2)}) copy-start(bf16[8,512,512]{2,1,0:T(8,128)(2,1)S(1)} %get-tuple-element.64.refs_8_) | copy-start | bytes 12582916
  28.1 3.7 %collective-permute-start.6 = (f32[3,8,32,128]{3,2,1,0:T(8,128)S(1)}, f32[3,8,32,128]{3,2,1,0:T(8,128)S(1)}, u32[]{:S(2)}, u32[]{:S(2)}) collective-permute-start(f32[3,8,32,128]{3,2,1,0:T(8,128)S(1)} %get-tuple-element.53), channel_id=1, source_target_pairs={{0,1},{1,0},{2,3},{3,2},{4,5},{5,4},{6,7},{7,6},{8,9},{9,8},{10,11... | collective-permute-start | bytes 1179656 | tf_op jit(solution)/shard_map/ppermute | solution.py:549
  28.2 10.3 %collective-permute-start.3 = (f32[384,128]{1,0:T(8,128)S(1)}, f32[384,128]{1,0:T(8,128)S(1)}, u32[]{:S(2)}, u32[]{:S(2)}) collective-permute-start(f32[384,128]{1,0:T(8,128)S(1)} %copy-done.6), channel_id=1, source_target_pairs={{0,8},{8,0},{16,24},{24,16},{1,9},{9,1},{17,25},{25,17},{2,10},{10... | collective-permute-start | bytes 589832 | tf_op jit(solution)/shard_map/ppermute | solution.py:505
  29.9 15.1 %collective-permute-start.4 = (f32[384,128]{1,0:T(8,128)S(1)}, f32[384,128]{1,0:T(8,128)S(1)}, u32[]{:S(2)}, u32[]{:S(2)}) collective-permute-start(f32[384,128]{1,0:T(8,128)S(1)} %copy-done.5), channel_id=1, source_target_pairs={{0,16},{8,24},{16,0},{24,8},{1,17},{9,25},{17,1},{25,9},{2,18},{10... | collective-permute-start | bytes 589832 | tf_op jit(solution)/shard_map/ppermute | solution.py:505
  31.3 18.4 %collective-permute-start.5 = (f32[384,128]{1,0:T(8,128)S(1)}, f32[384,128]{1,0:T(8,128)S(1)}, u32[]{:S(2)}, u32[]{:S(2)}) collective-permute-start(f32[384,128]{1,0:T(8,128)S(1)} %copy-done.4), channel_id=1, source_target_pairs={{0,24},{8,16},{16,8},{24,0},{1,25},{9,17},{17,9},{25,1},{2,26},{10... | collective-permute-start | bytes 589832 | tf_op jit(solution)/shard_map/ppermute | solution.py:505
  55.0 1.8 %collective-permute-start.7 = (f32[3,8,32,128]{3,2,1,0:T(8,128)S(1)}, f32[3,8,32,128]{3,2,1,0:T(8,128)S(1)}, u32[]{:S(2)}, u32[]{:S(2)}) collective-permute-start(f32[3,8,32,128]{3,2,1,0:T(8,128)S(1)} %get-tuple-element.55), channel_id=1, source_target_pairs={{0,1},{1,0},{2,3},{3,2},{4,5},{5,4},{6,7},{7,6},{8,9},{9,8},{10,11... | collective-permute-start | bytes 1179656 | tf_op jit(solution)/shard_map/ppermute | solution.py:549
  55.1 12.0 %collective-permute-start.16 = (f32[3,8,32,128]{3,2,1,0:T(8,128)S(1)}, f32[3,8,32,128]{3,2,1,0:T(8,128)S(1)}, u32[]{:S(2)}, u32[]{:S(2)}) collective-permute-start(f32[3,8,32,128]{3,2,1,0:T(8,128)S(1)} %add.82.refs_8_.stress_ref), channel_id=1, source_target_pairs={{0,2},{1,3},{2,0},{3,1},{4,6},{5,7},{6,4},{7,5},{8,10},{9,11},{10,... | collective-permute-start | bytes 1179656 | tf_op jit(solution)/shard_map/ppermute | solution.py:549
  56.9 18.2 %collective-permute-start.8 = (f32[3,8,32,128]{3,2,1,0:T(8,128)S(1)}, f32[3,8,32,128]{3,2,1,0:T(8,128)S(1)}, u32[]{:S(2)}, u32[]{:S(2)}) collective-permute-start(f32[3,8,32,128]{3,2,1,0:T(8,128)S(1)} %add.83.stress_ref), channel_id=1, source_target_pairs={{0,2},{1,3},{2,0},{3,1},{4,6},{5,7},{6,4},{7,5},{8,10},{9,11},{10,... | collective-permute-start | bytes 1179656 | tf_op jit(solution)/shard_map/ppermute | solution.py:549
  68.0 8.4 %collective-permute-start.17 = (f32[8,24,128]{2,1,0:T(8,128)S(1)}, f32[8,24,128]{2,1,0:T(8,128)S(1)}, u32[]{:S(2)}, u32[]{:S(2)}) collective-permute-start(f32[8,24,128]{2,1,0:T(8,128)S(1)} %bitcast.60), channel_id=1, source_target_pairs={{0,4},{4,0},{8,12},{12,8},{16,20},{20,16},{24,28},{28,24},{1,5},{5... | collective-permute-start | bytes 294920 | tf_op jit(solution)/shard_map/ppermute | solution.py:505
  69.6 8.4 %collective-permute-start.18 = (f32[8,24,128]{2,1,0:T(8,128)S(1)}, f32[8,24,128]{2,1,0:T(8,128)S(1)}, u32[]{:S(2)}, u32[]{:S(2)}) collective-permute-start(f32[8,24,128]{2,1,0:T(8,128)S(1)} %bitcast.59), channel_id=1, source_target_pairs={{0,8},{4,12},{8,0},{12,4},{16,24},{20,28},{24,16},{28,20},{1,9},{5... | collective-permute-start | bytes 294920 | tf_op jit(solution)/shard_map/ppermute | solution.py:505
  69.6 9.5 %collective-permute-start.19 = (f32[8,24,128]{2,1,0:T(8,128)S(1)}, f32[8,24,128]{2,1,0:T(8,128)S(1)}, u32[]{:S(2)}, u32[]{:S(2)}) collective-permute-start(f32[8,24,128]{2,1,0:T(8,128)S(1)} %bitcast.58), channel_id=1, source_target_pairs={{0,12},{4,8},{8,4},{12,0},{16,28},{20,24},{24,20},{28,16},{1,13},{... | collective-permute-start | bytes 294920 | tf_op jit(solution)/shard_map/ppermute | solution.py:505
  71.6 8.4 %collective-permute-start.20 = (f32[8,24,128]{2,1,0:T(8,128)S(1)}, f32[8,24,128]{2,1,0:T(8,128)S(1)}, u32[]{:S(2)}, u32[]{:S(2)}) collective-permute-start(f32[8,24,128]{2,1,0:T(8,128)S(1)} %bitcast.56), channel_id=1, source_target_pairs={{0,16},{4,20},{8,24},{12,28},{16,0},{20,4},{24,8},{28,12},{1,17},{... | collective-permute-start | bytes 294920 | tf_op jit(solution)/shard_map/ppermute | solution.py:505
  75.1 10.3 %collective-permute-start.21 = (f32[8,24,128]{2,1,0:T(8,128)S(1)}, f32[8,24,128]{2,1,0:T(8,128)S(1)}, u32[]{:S(2)}, u32[]{:S(2)}) collective-permute-start(f32[8,24,128]{2,1,0:T(8,128)S(1)} %bitcast.54), channel_id=1, source_target_pairs={{0,20},{4,16},{8,28},{12,24},{16,4},{20,0},{24,12},{28,8},{1,21},{... | collective-permute-start | bytes 294920 | tf_op jit(solution)/shard_map/ppermute | solution.py:505
  76.4 12.7 %collective-permute-start.22 = (f32[8,24,128]{2,1,0:T(8,128)S(1)}, f32[8,24,128]{2,1,0:T(8,128)S(1)}, u32[]{:S(2)}, u32[]{:S(2)}) collective-permute-start(f32[8,24,128]{2,1,0:T(8,128)S(1)} %bitcast.53), channel_id=1, source_target_pairs={{0,24},{4,28},{8,16},{12,20},{16,8},{20,12},{24,0},{28,4},{1,25},{... | collective-permute-start | bytes 294920 | tf_op jit(solution)/shard_map/ppermute | solution.py:505
  78.0 14.1 %collective-permute-start.23 = (f32[8,24,128]{2,1,0:T(8,128)S(1)}, f32[8,24,128]{2,1,0:T(8,128)S(1)}, u32[]{:S(2)}, u32[]{:S(2)}) collective-permute-start(f32[8,24,128]{2,1,0:T(8,128)S(1)} %bitcast.52), channel_id=1, source_target_pairs={{0,28},{4,24},{8,20},{12,16},{16,12},{20,8},{24,4},{28,0},{1,29},{... | collective-permute-start | bytes 294920 | tf_op jit(solution)/shard_map/ppermute | solution.py:505
  79.1 13.5 %collective-permute-start.9 = (f32[8,24,128]{2,1,0:T(8,128)S(1)}, f32[8,24,128]{2,1,0:T(8,128)S(1)}, u32[]{:S(2)}, u32[]{:S(2)}) collective-permute-start(f32[8,24,128]{2,1,0:T(8,128)S(1)} %bitcast.57), channel_id=1, source_target_pairs={{0,4},{4,0},{8,12},{12,8},{16,20},{20,16},{24,28},{28,24},{1,5},{5... | collective-permute-start | bytes 294920 | tf_op jit(solution)/shard_map/ppermute | solution.py:505
  80.0 13.5 %collective-permute-start.10 = (f32[8,24,128]{2,1,0:T(8,128)S(1)}, f32[8,24,128]{2,1,0:T(8,128)S(1)}, u32[]{:S(2)}, u32[]{:S(2)}) collective-permute-start(f32[8,24,128]{2,1,0:T(8,128)S(1)} %bitcast.55), channel_id=1, source_target_pairs={{0,8},{4,12},{8,0},{12,4},{16,24},{20,28},{24,16},{28,20},{1,9},{5... | collective-permute-start | bytes 294920 | tf_op jit(solution)/shard_map/ppermute | solution.py:505
  85.4 15.7 %collective-permute-start.11 = (f32[8,24,128]{2,1,0:T(8,128)S(1)}, f32[8,24,128]{2,1,0:T(8,128)S(1)}, u32[]{:S(2)}, u32[]{:S(2)}) collective-permute-start(f32[8,24,128]{2,1,0:T(8,128)S(1)} %bitcast.51), channel_id=1, source_target_pairs={{0,12},{4,8},{8,4},{12,0},{16,28},{20,24},{24,20},{28,16},{1,13},{... | collective-permute-start | bytes 294920 | tf_op jit(solution)/shard_map/ppermute | solution.py:505
  89.2 11.9 %collective-permute-start.12 = (f32[8,24,128]{2,1,0:T(8,128)S(1)}, f32[8,24,128]{2,1,0:T(8,128)S(1)}, u32[]{:S(2)}, u32[]{:S(2)}) collective-permute-start(f32[8,24,128]{2,1,0:T(8,128)S(1)} %bitcast.50), channel_id=1, source_target_pairs={{0,16},{4,20},{8,24},{12,28},{16,0},{20,4},{24,8},{28,12},{1,17},{... | collective-permute-start | bytes 294920 | tf_op jit(solution)/shard_map/ppermute | solution.py:505
  92.1 10.7 %collective-permute-start.13 = (f32[8,24,128]{2,1,0:T(8,128)S(1)}, f32[8,24,128]{2,1,0:T(8,128)S(1)}, u32[]{:S(2)}, u32[]{:S(2)}) collective-permute-start(f32[8,24,128]{2,1,0:T(8,128)S(1)} %bitcast.49), channel_id=1, source_target_pairs={{0,20},{4,16},{8,28},{12,24},{16,4},{20,0},{24,12},{28,8},{1,21},{... | collective-permute-start | bytes 294920 | tf_op jit(solution)/shard_map/ppermute | solution.py:505
  92.6 13.1 %collective-permute-start.14 = (f32[8,24,128]{2,1,0:T(8,128)S(1)}, f32[8,24,128]{2,1,0:T(8,128)S(1)}, u32[]{:S(2)}, u32[]{:S(2)}) collective-permute-start(f32[8,24,128]{2,1,0:T(8,128)S(1)} %bitcast.48), channel_id=1, source_target_pairs={{0,24},{4,28},{8,16},{12,20},{16,8},{20,12},{24,0},{28,4},{1,25},{... | collective-permute-start | bytes 294920 | tf_op jit(solution)/shard_map/ppermute | solution.py:505
  93.5 14.6 %collective-permute-start.15 = (f32[8,24,128]{2,1,0:T(8,128)S(1)}, f32[8,24,128]{2,1,0:T(8,128)S(1)}, u32[]{:S(2)}, u32[]{:S(2)}) collective-permute-start(f32[8,24,128]{2,1,0:T(8,128)S(1)} %bitcast.47), channel_id=1, source_target_pairs={{0,28},{4,24},{8,20},{12,16},{16,12},{20,8},{24,4},{28,0},{1,29},{... | collective-permute-start | bytes 294920 | tf_op jit(solution)/shard_map/ppermute | solution.py:505
  114.3 7.0 %collective-permute-start.24 = (f32[8,2,24,128]{3,2,1,0:T(8,128)S(1)}, f32[8,2,24,128]{3,2,1,0:T(8,128)S(1)}, u32[]{:S(2)}, u32[]{:S(2)}) collective-permute-start(f32[8,2,24,128]{3,2,1,0:T(8,128)S(1)} %get-tuple-element.76), channel_id=1, source_target_pairs={{0,4},{4,0},{8,12},{12,8},{16,20},{20,16},{24,28},{28,24},{1,5},{5... | collective-permute-start | bytes 589832 | tf_op jit(solution)/shard_map/ppermute | solution.py:505
  115.4 12.2 %collective-permute-start.25 = (f32[8,2,24,128]{3,2,1,0:T(8,128)S(1)}, f32[8,2,24,128]{3,2,1,0:T(8,128)S(1)}, u32[]{:S(2)}, u32[]{:S(2)}) collective-permute-start(f32[8,2,24,128]{3,2,1,0:T(8,128)S(1)} %get-tuple-element.77), channel_id=1, source_target_pairs={{0,8},{4,12},{8,0},{12,4},{16,24},{20,28},{24,16},{28,20},{1,9},{5... | collective-permute-start | bytes 589832 | tf_op jit(solution)/shard_map/ppermute | solution.py:505
  115.4 15.4 %collective-permute-start.26 = (f32[8,2,24,128]{3,2,1,0:T(8,128)S(1)}, f32[8,2,24,128]{3,2,1,0:T(8,128)S(1)}, u32[]{:S(2)}, u32[]{:S(2)}) collective-permute-start(f32[8,2,24,128]{3,2,1,0:T(8,128)S(1)} %get-tuple-element.78), channel_id=1, source_target_pairs={{0,12},{4,8},{8,4},{12,0},{16,28},{20,24},{24,20},{28,16},{1,13},{... | collective-permute-start | bytes 589832 | tf_op jit(solution)/shard_map/ppermute | solution.py:505
  117.8 14.1 %collective-permute-start.27 = (f32[8,2,24,128]{3,2,1,0:T(8,128)S(1)}, f32[8,2,24,128]{3,2,1,0:T(8,128)S(1)}, u32[]{:S(2)}, u32[]{:S(2)}) collective-permute-start(f32[8,2,24,128]{3,2,1,0:T(8,128)S(1)} %get-tuple-element.79), channel_id=1, source_target_pairs={{0,16},{4,20},{8,24},{12,28},{16,0},{20,4},{24,8},{28,12},{1,17},{... | collective-permute-start | bytes 589832 | tf_op jit(solution)/shard_map/ppermute | solution.py:505
  119.0 26.4 %collective-permute-start.28 = (f32[8,2,24,128]{3,2,1,0:T(8,128)S(1)}, f32[8,2,24,128]{3,2,1,0:T(8,128)S(1)}, u32[]{:S(2)}, u32[]{:S(2)}) collective-permute-start(f32[8,2,24,128]{3,2,1,0:T(8,128)S(1)} %get-tuple-element.80), channel_id=1, source_target_pairs={{0,20},{4,16},{8,28},{12,24},{16,4},{20,0},{24,12},{28,8},{1,21},{... | collective-permute-start | bytes 589832 | tf_op jit(solution)/shard_map/ppermute | solution.py:505
  121.3 29.4 %collective-permute-start.29 = (f32[8,2,24,128]{3,2,1,0:T(8,128)S(1)}, f32[8,2,24,128]{3,2,1,0:T(8,128)S(1)}, u32[]{:S(2)}, u32[]{:S(2)}) collective-permute-start(f32[8,2,24,128]{3,2,1,0:T(8,128)S(1)} %get-tuple-element.81), channel_id=1, source_target_pairs={{0,24},{4,28},{8,16},{12,20},{16,8},{20,12},{24,0},{28,4},{1,25},{... | collective-permute-start | bytes 589832 | tf_op jit(solution)/shard_map/ppermute | solution.py:505
  127.6 25.9 %collective-permute-start.30 = (f32[8,2,24,128]{3,2,1,0:T(8,128)S(1)}, f32[8,2,24,128]{3,2,1,0:T(8,128)S(1)}, u32[]{:S(2)}, u32[]{:S(2)}) collective-permute-start(f32[8,2,24,128]{3,2,1,0:T(8,128)S(1)} %get-tuple-element.82), channel_id=1, source_target_pairs={{0,28},{4,24},{8,20},{12,16},{16,12},{20,8},{24,4},{28,0},{1,29},{... | collective-permute-start | bytes 589832 | tf_op jit(solution)/shard_map/ppermute | solution.py:505

commit v4 on v3

--- a/solution.py
+++ b/solution.py
@@ -117,6 +117,26 @@
     return pltpu.CompilerParams(vmem_limit_bytes=48 * 1024 * 1024)
 
 
+ORDERS = {4: (1, 3, 2), 8: (4, 1, 2, 6, 5, 3, 7)}
+
+
+def steps_of(count):
+    even = ORDERS.get(count, tuple(range(1, count)))
+    odd = list(even)
+    for first in range(0, count - 2, 2):
+        odd[first], odd[first + 1] = (even[first + 1], even[first])
+    return (0,) + tuple(even), (0,) + tuple(odd)
+
+
+def step_at(count, position):
+    even, odd = steps_of(count)
+    return jnp.where(lax.axis_index("real") % 2 == 0, even[position], odd[position])
+
+
+def cost(size):
+    return pl.CostEstimate(flops=0, bytes_accessed=size, transcendentals=0)
+
+
 def two_parts(value):
     top = value.astype(jnp.bfloat16)
     rest = (value - top.astype(jnp.float32)).astype(jnp.bfloat16)
@@ -131,7 +151,7 @@
     chunks, pieces, kx_count, rows, columns = velocity_ref.shape
     own = lax.axis_index("kx")
     for index, out_ref in enumerate(out_refs):
-        piece, partner = (index // kx_count, own ^ (index % kx_count))
+        piece, partner = (index // kx_count, own ^ step_at(kx_count, index % kx_count))
         for chunk in range(chunks):
             out_ref[chunk * rows : (chunk + 1) * rows] = velocity_ref[chunk, piece, partner]
     shape = (out_refs[0].shape[0] - chunks * rows, columns)
@@ -160,6 +180,7 @@
         out_shape=tuple(shapes),
         in_specs=[SMEM, SMEM, VMEM],
         out_specs=(VMEM,) * len(shapes),
+        cost_estimate=cost(8 * velocity.size),
         name="pack",
     )(neighbours, mode_counts, velocity)
     return [out[piece * kx_count : (piece + 1) * kx_count] for piece in range(pieces)]
@@ -168,18 +189,20 @@
 def split_matrix_kernel(matrix_ref, top_ref, rest_ref, mark_ref, turned, *, pieces, kx_count):
     ht_count, heights, width = turned.shape
     rows = width // (pieces * kx_count)
+    owners = kx_count * ht_count
     own_kx, own_ht = (lax.axis_index("kx"), lax.axis_index("ht"))
     for h in range(ht_count):
         turned[h] = matrix_ref[0, h * width : (h + 1) * width, :].T
-    for block in range(heights // rows):
-        piece, h, k = (
-            block // (ht_count * kx_count), block // kx_count % ht_count, block % kx_count
-        )
-        source = (((own_ht ^ h) * pieces + piece) * kx_count + (own_kx ^ k)) * rows
-        for j in range(ht_count):
-            value = turned[own_ht ^ j, pl.ds(pl.multiple_of(source, rows), rows), :]
-            place = (0, slice(block * rows, (block + 1) * rows), slice(j * width, (j + 1) * width))
-            top_ref[place], rest_ref[place] = two_parts(value)
+    for position in range(owners):
+        step = step_at(owners, position)
+        kx, ht = (own_kx ^ (step // ht_count), own_ht ^ (step % ht_count))
+        for piece in range(pieces):
+            source = pl.multiple_of(((ht * pieces + piece) * kx_count + kx) * rows, rows)
+            start = (piece * owners + position) * rows
+            for h in range(ht_count):
+                place = (0, slice(start, start + rows), slice(h * width, (h + 1) * width))
+                value = turned[h, pl.ds(source, rows), :]
+                top_ref[place], rest_ref[place] = two_parts(value)
     mark_ref[...] = jnp.zeros_like(mark_ref)
 
 
@@ -195,9 +218,7 @@
         out_specs=(spec, spec, pl.BlockSpec((8, LANES), lambda s: (0, 0))),
         scratch_shapes=[pltpu.VMEM((ht_count, heights, heights // ht_count), jnp.float32)],
         compiler_params=params(),
-        cost_estimate=pl.CostEstimate(
-            flops=0, bytes_accessed=2 * helmholtz.size * 4, transcendentals=0
-        ),
+        cost_estimate=cost(8 * helmholtz.size),
         name="split_matrix",
     )(helmholtz)
 
@@ -225,7 +246,7 @@
             top, rest = two_parts(block_ref[pl.ds(pl.multiple_of(component * size, 8), size)])
             both = dot(jnp.concatenate([top, rest], axis=1), first_ref[...])
             fields = both[:, :points] + dot(top, second_ref[...])
-            place = pl.ds((own ^ index) * band_modes, band_modes)
+            place = pl.ds((own ^ step_at(bands, index)) * band_modes, band_modes)
             physical[component, place] = fields.reshape(band_modes, rows, points)
             slotted_ref[component, place] = both[:, points:].reshape(band_modes, rows, columns)
         return carry
@@ -269,18 +290,21 @@
 
     lax.fori_loop(0, (rows // 8) * (points // LANES), pairs, 0)
 
-    def inverse(fields):
+    def inverse(fields, start):
         top, rest = two_parts(fields)
-        both = dot(top, back_ref[...])
-        return both[:, :columns] + both[:, columns:] + dot(rest, back_ref[:, :columns])
+        both = dot(top, back_ref[:, start : start + 2 * columns])
+        return (
+            both[:, :columns] + both[:, columns:]
+            + dot(rest, back_ref[:, start : start + columns])
+        )
 
     def finish(component, carry):
-        forcing = inverse(products[component].reshape(highs * rows, points))
+        forcing = inverse(products[component].reshape(highs * rows, points), 0)
         forcing = forcing.reshape(highs, rows, columns)
         for index in range(highs):
             mode = high_ref[index]
             slotted_ref[component, mode] += forcing[index] * mask_ref[mode]
-        stress = inverse(sums[component].reshape(members * rows, points))
+        stress = inverse(sums[component].reshape(members * rows, points), 2 * columns)
         stress_ref[component] = stress.reshape(members, rows, columns)
         return carry
 
@@ -306,6 +330,7 @@
             pltpu.SMEM((modes + 1,), jnp.int32),
         ],
         compiler_params=params(),
+        cost_estimate=cost(8 * components * modes * rows * points * members),
         name="nonlinear",
     )(low_index, neighbours, *blocks, *tables, mask, after)
 
@@ -319,10 +344,18 @@
     slots = columns // 2 // owners
     per_slot = out_refs[0].shape[0] // slots
     full[...] = slotted_ref[...]
+    position = lax.broadcasted_iota(jnp.int32, (rows, columns), 1) // slots % owners
+    odd = lax.axis_index("real") % 2 == 1
+    upper = odd & (position % 2 == 1) & (position < owners - 1)
+    lower = odd & (position % 2 == 0) & (position > 0)
     for member in range(members):
         mode = low_ref[member]
         for c in range(components):
             stress = stress_ref[c, member] + other_ref[c, member]
+            stress = jnp.where(
+                upper, pltpu.roll(stress, columns - slots, 1),
+                jnp.where(lower, pltpu.roll(stress, slots, 1), stress),
+            )
             full[c, mode] += stress * mask_ref[mode]
     inner = modes // groups
     for c in range(components):
@@ -349,6 +382,7 @@
         out_specs=(VMEM,) * owners,
         scratch_shapes=[pltpu.VMEM(slotted.shape, jnp.float32)],
         compiler_params=params(),
+        cost_estimate=cost(8 * slotted.size),
         name="outgoing",
     )(low_index, slotted, stress, other, mask)
 
@@ -377,10 +411,9 @@
     )
     rows = LANES // groups
     tiles = []
-    for h in range(ht_count):
-        for first in range(0, kx_count, groups):
-            blocks = [block_refs[(first + g) * ht_count + h][0] for g in range(groups)]
-            tiles.append(jnp.concatenate(regroup(blocks, rows), axis=0))
+    for first in range(0, owners, groups):
+        blocks = [block_refs[first + g][0] for g in range(groups)]
+        tiles.append(jnp.concatenate(regroup(blocks, rows), axis=0))
     top, rest = two_parts(jnp.concatenate(tiles, axis=1))
     count = top.shape[0]
     both = dot(jnp.concatenate([top, rest], axis=0), top_ref[0])
@@ -391,15 +424,16 @@
         refs[0][0] = solved
         return
     out_refs, full = (refs[:owners], refs[owners])
-    full[...] = solved
-    own = lax.axis_index("kx")
+    for tile in range(full.shape[0]):
+        full[tile] = solved[:, tile * LANES : (tile + 1) * LANES]
+    own_kx, own_ht = (lax.axis_index("kx"), lax.axis_index("ht"))
     lane_tiles, per_band = out_refs[0].shape[1:3]
-    for k in range(kx_count):
-        band = pl.ds(pl.multiple_of((own ^ k) * per_band, 8), per_band)
-        for tile in range(ht_count * lane_tiles):
-            out_refs[k * ht_count + tile // lane_tiles][0, tile % lane_tiles] = full[
-                band, tile * LANES : (tile + 1) * LANES
-            ]
+    for position, out_ref in enumerate(out_refs):
+        step = step_at(owners, position)
+        kx, ht = (own_kx ^ (step // ht_count), own_ht ^ (step % ht_count))
+        band = pl.ds(pl.multiple_of(kx * per_band, 8), per_band)
+        for tile in range(lane_tiles):
+            out_ref[0, tile] = full[ht * lane_tiles + tile, band]
 
 
 def solve(blocks, matrices, piece, pieces, partial, groups, kx_count, ht_count):
@@ -411,7 +445,7 @@
         shape = (slots, heights // ht_count // LANES, count // kx_count, LANES)
         out_shape = (jax.ShapeDtypeStruct(shape, jnp.float32),) * owners
         out_specs = (pl.BlockSpec((1,) + shape[1:], lambda s: (s, 0, 0, 0)),) * owners
-        scratch = [pltpu.VMEM((count, heights), jnp.float32)]
+        scratch = [pltpu.VMEM((heights // LANES, count, LANES), jnp.float32)]
     else:
         out_shape = jax.ShapeDtypeStruct((slots, count, heights), jnp.float32)
         out_specs, scratch = (whole, [])
@@ -464,6 +498,7 @@
         in_specs=[VMEM] * (len(blocks) + 1),
         out_specs=VMEM,
         compiler_params=params(),
+        cost_estimate=cost(8 * components * band_modes * rows * columns),
         name="restore",
     )(*blocks, order)
 
@@ -473,17 +508,23 @@
     return top.astype(jnp.bfloat16), (value - top).astype(jnp.bfloat16)
 
 
-def slot_tables(owner_map, columns):
+def slot_tables(owner_map, even_map, columns):
     forward, backward = spanwise_tables(columns // 2, 2 * columns)
-    slot_columns = (2 * owner_map[None, :] + jnp.arange(2)[:, None]).reshape(columns)
-    select = slot_columns[None, :] == jnp.arange(columns)[:, None]
+    select, even_select = (
+        (2 * order[None, :] + jnp.arange(2)[:, None]).reshape(1, columns)
+        == jnp.arange(columns)[:, None]
+        for order in (owner_map, even_map)
+    )
     forward_top, forward_rest = table_parts(forward)
     first = jnp.concatenate([forward_top, select.astype(jnp.bfloat16)], axis=1)
     first = jnp.concatenate([first, first], axis=0)
-    slotted_back = jnp.dot(
-        backward, select.astype(jnp.float32), precision=lax.Precision.HIGHEST
-    )
-    back = jnp.concatenate(table_parts(slotted_back), axis=1)
+    back = []
+    for chosen in (select, even_select):
+        slotted_back = jnp.dot(
+            backward, chosen.astype(jnp.float32), precision=lax.Precision.HIGHEST
+        )
+        back += table_parts(slotted_back)
+    back = jnp.concatenate(back, axis=1)
     order = select.T.astype(jnp.bfloat16)
     order = jnp.concatenate([order, order], axis=0)
     return (first, forward_rest, back), order
@@ -495,14 +536,17 @@
     return mask, mask / realizations
 
 
-def partners(count, step):
-    return [(index, index ^ step) for index in range(count)]
-
-
 def exchange(blocks, axes):
+    count, realizations = (len(blocks), lax.axis_size("real"))
     result = list(blocks)
-    for step in range(len(blocks) - 1, 0, -1):
-        result[step] = lax.ppermute(blocks[step], axes, partners(len(blocks), step))
+    for position in range(1, count):
+        steps = [order[position] for order in steps_of(count)]
+        pairs = [
+            (index * realizations + r, (index ^ steps[r % 2]) * realizations + r)
+            for index in range(count)
+            for r in range(realizations)
+        ]
+        result[position] = lax.ppermute(blocks[position], axes + ("real",), pairs)
     return result
 
 
@@ -515,7 +559,7 @@
     groups = LANES // rows if rows else 0
     slots = columns // 2 // owners
     if (
-        columns != LANES or reals_dev != 1 or rows_ht % LANES or rows % 8 or LANES % rows or kx_count % groups
+        columns != LANES or reals_dev != 1 or rows_ht % LANES or rows % 8 or LANES % rows or kx_count % groups or kx_count & (kx_count - 1)
         or (band_modes * 2 * components) % 8 or slots % 8 or owners & (owners - 1) or low_index.shape[0] >= kx_count * band_modes
         or low_index.shape[0] >= columns or real_count < 2 or real_count & (real_count - 1)
     ):
@@ -525,20 +569,25 @@
     shape = (components, modes, rows, columns)
     extra_rows = -(-band_modes // 8) * 8
     split = velocity.reshape(chunks, pieces, kx_count, rows, columns)
-    everyone = (own_kx * ht_count + own_ht) ^ jnp.arange(owners)
-    owner_map = owner_map.reshape(owners, slots)[everyone].reshape(-1)
+    owner_map, even_map = (
+        owner_map.reshape(owners, slots)[(own_kx * ht_count + own_ht) ^ order].reshape(-1)
+        for order in (
+            jnp.stack([step_at(owners, position) for position in range(owners)]),
+            jnp.array(steps_of(owners)[0], jnp.int32),
+        )
+    )
     parts = [
-        exchange(blocks, "kx") for blocks in pack(split, neighbours, mode_counts, extra_rows)
+        exchange(blocks, ("kx",)) for blocks in pack(split, neighbours, mode_counts, extra_rows)
     ]
     *matrices, after = split_matrix(helmholtz, pieces, kx_count, ht_count)
     small = 0.0
     for index, block in enumerate(parts[0]):
         lines = block[chunks * rows : chunks * rows + band_modes, : members + 1]
-        here = (own_kx ^ index) == jnp.arange(kx_count)
+        here = (own_kx ^ step_at(kx_count, index)) == jnp.arange(kx_count)
         small = small + jnp.where(here[:, None, None], lines[None], 0.0)
     small = small.reshape(modes, members + 1).astype(jnp.int32)
     neighbours, mode_counts = (small[:, :-1], small[:, -1])
-    tables, order = slot_tables(owner_map, columns)
+    tables, order = slot_tables(owner_map, even_map, columns)
     mask, low_mask = slot_masks(owner_map, mode_counts, realizations)
     received = []
     for part in parts:
@@ -546,9 +595,11 @@
         step, other = (1, None)
         while step < realizations:
             stress = stress if other is None else stress + other
-            other = lax.ppermute(stress, "real", partners(realizations, step))
+            other = lax.ppermute(
+                stress, "real", [(index, index ^ step) for index in range(realizations)]
+            )
             step *= 2
-        after = stress
+        after = other
         blocks = outgoing(
             slotted, stress, other, low_index, low_mask, groups, band_modes, owners
         )

time: 156 us -> 147 us (0.942)
  the two profiles are of different devices: /device:TPU:10 before, /device:TPU:0 now
where the time goes in v4:
time: 147 us; the launch traced here: 146 us
  waiting for transfers between devices  54.9 us (37%)
  starting transfers between devices  42.9 us (29%)
  Pallas kernels  38.8 us (26%)
  local copies, waits for them, and re-layouts  5.97 us (4%)
  other arithmetic  1.76 us (1%)
  matrix products  1.47 us (1%)
    ppermute x27, waiting for transfers between devices, exchange(): result[position] = lax.ppermute(blocks[position], axes + ('real',), pairs)  47.9 us
    ppermute x27, starting transfers between devices, exchange(): result[position] = lax.ppermute(blocks[position], axes + ('real',), pairs)  40.6 us
    pallas_call x2, Pallas kernels, solve(): pl.pallas_call(functools.partial(solve_kernel, groups=groups, kx_count=kx...  12.2 us
    pallas_call x2, Pallas kernels, nonlinear(): pl.pallas_call(nonlinear_kernel, out_shape=(jax.ShapeDtypeStruct((compone...  10.7 us
    pallas_call x1, Pallas kernels, split_matrix(): pl.pallas_call(functools.partial(split_matrix_kernel, pieces=pieces, kx_c...  9.04 us
    ppermute x4, waiting for transfers between devices, local(): lax.ppermute(stress, 'real', [(index, index ^ step) for index in range(re...  6.97 us
  transfers between devices with their start and end apart: 31, of which 14 were waited for; matrix products, arithmetic and copies ran while one was open for 5% of the time, Pallas kernels for 12%

profile of v4, /device:TPU:0, one launch (start us, length us, event | category | flops | bytes accessed | tf_op | source)
XLA Modules:
  0.0 146.1 jit_solution(10601255488094100211)
XLA Ops:
  0.0 2.7 %pack.1 = (f32[392,128]{1,0:T(8,128)}, f32[392,128]{1,0:T(8,128)}, f32[392,128]{1,0:T(8,128)}, f32[392,128]{1,0:T(8,128)}, f32[384,128]{1,0:T(8,128)}, /*index=5...) custom-call(s32[4,8]{1,0:T(4,128)} %near_ref.1, s32[4]{0:T(128)} %count_ref.1, f32[12,2,4,32,128]{4,3,2,1,0:T(8,128)} %bitcast.67), custom_call_target="tpu_custom_call" | custom-call | bytes 3145728 | tf_op jit(solution)/shard_map/pack/pallas_call | solution.py:178
  2.7 3.0 %collective-permute-start = (f32[392,128]{1,0:T(8,128)}, f32[392,128]{1,0:T(8,128)S(1)}, u32[]{:S(2)}, u32[]{:S(2)}) collective-permute-start(f32[392,128]{1,0:T(8,128)} %get-tuple-element.45), channel_id=1, source_target_pairs={{0,8},{1,25},{2,10},{3,27},{8,0},{9,17},{10,2},{11,19},{16,24},{17... | collective-permute-start | bytes 602120 | tf_op jit(solution)/shard_map/ppermute | solution.py:549
  5.7 2.5 %collective-permute-start.1 = (f32[392,128]{1,0:T(8,128)}, f32[392,128]{1,0:T(8,128)S(1)}, u32[]{:S(2)}, u32[]{:S(2)}) collective-permute-start(f32[392,128]{1,0:T(8,128)} %get-tuple-element.46), channel_id=1, source_target_pairs={{0,24},{1,9},{2,26},{3,11},{8,16},{9,1},{10,18},{11,3},{16,8},{17,... | collective-permute-start | bytes 602120 | tf_op jit(solution)/shard_map/ppermute | solution.py:549
  8.2 0.1 collective-permute-start.2
  8.3 0.1 stack.29
  8.5 0.7 reshape.422
  9.2 0.6 gather_fusion
  9.8 0.1 add.123
  9.9 0.1 iota_compare_fusion
  10.0 0.7 reduce-precision_convert_fusion.1
  10.8 0.6 fusion.3
  11.4 0.1 broadcast_in_dim.122
  11.6 0.1 broadcast_in_dim.128
  11.8 0.1 broadcast_in_dim.133
  11.9 0.1 broadcast_in_dim.138
  12.0 0.7 compare_select_fusion.1
  12.7 0.6 gather_fusion.1
  13.5 0.7 reduce-precision_convert_fusion
  14.3 0.7 slice.20
  15.0 9.0 %split_matrix.1 = (bf16[8,512,512]{2,1,0:T(8,128)(2,1)S(1)}, bf16[8,512,512]{2,1,0:T(8,128)(2,1)}, f32[8,128]{1,0:T(8,128)S(1)}) custom-call(f32[8,512,512]{2,1,0:T(8,128)} %matrix_ref.1), custom_call_target="tpu_custom_call" | custom-call | bytes 16777216 | tf_op jit(solution)/shard_map/split_matrix/pallas_call | solution.py:213
  24.1 2.0 %copy-done = bf16[8,512,512]{2,1,0:T(8,128)(2,1)} copy-done((bf16[8,512,512]{2,1,0:T(8,128)(2,1)}, bf16[8,512,512]{2,1,0:T(8,128)(2,1)S(1)}, u32[]{:S(2)}) %copy-start) | copy-done | bytes 4194328
  26.3 0.2 slice_reduce_fusion
  26.5 0.1 broadcast_multiply_fusion
  26.6 5.4 %nonlinear.2 = (f32[3,16,32,128]{3,2,1,0:T(8,128)S(1)}, f32[3,8,32,128]{3,2,1,0:T(8,128)S(1)}) custom-call(s32[8]{0:T(128)S(1)} %copy-done.3, s32[16,8]{1,0:T(8,128)S(1)} %bitcast.49, f32[392,128]{1,0:T(8,128)S(1)} %copy-done.1, f32[392,128]{1,0:T(8,128)S(1)} %collective-permute-done.refs_1_, f32[392,128]{1,0:T(8,128)S(1)} %collective-permute-done.1.refs_2_, ...), custom_call_target="tpu_custom_call" | custom-call | bytes 25165824 | tf_op jit(solution)/shard_map/nonlinear/pallas_call | solution.py:318
  32.1 1.7 %collective-permute-done.6 = f32[3,8,32,128]{3,2,1,0:T(8,128)S(1)} collective-permute-done((f32[3,8,32,128]{3,2,1,0:T(8,128)S(1)}, f32[3,8,32,128]{3,2,1,0:T(8,128)S(1)}, u32[]{:S(2)}, u32[]{:S(2)}) %collective-permute-start.6) | collective-permute-done | bytes 393248 | tf_op jit(solution)/shard_map/ppermute | solution.py:598
  33.8 1.6 %collective-permute-start.7 = (f32[3,8,32,128]{3,2,1,0:T(8,128)S(1)}, f32[3,8,32,128]{3,2,1,0:T(8,128)S(1)}, u32[]{:S(2)}, u32[]{:S(2)}) collective-permute-start(f32[3,8,32,128]{3,2,1,0:T(8,128)S(1)} %add.129.stress_ref), channel_id=1, source_target_pairs={{0,2},{1,3},{2,0},{3,1},{4,6},{5,7},{6,4},{7,5},{8,10},{9,11},{10,... | collective-permute-start | bytes 1179656 | tf_op jit(solution)/shard_map/ppermute | solution.py:598
  35.4 1.8 %collective-permute-start.3 = (f32[384,128]{1,0:T(8,128)S(1)}, f32[384,128]{1,0:T(8,128)S(1)}, u32[]{:S(2)}, u32[]{:S(2)}) collective-permute-start(f32[384,128]{1,0:T(8,128)S(1)} %copy-done.6), channel_id=1, source_target_pairs={{0,8},{1,25},{2,10},{3,27},{8,0},{9,17},{10,2},{11,19},{16,24},{17... | collective-permute-start | bytes 589832 | tf_op jit(solution)/shard_map/ppermute | solution.py:549
  37.2 2.5 %collective-permute-start.4 = (f32[384,128]{1,0:T(8,128)S(1)}, f32[384,128]{1,0:T(8,128)S(1)}, u32[]{:S(2)}, u32[]{:S(2)}) collective-permute-start(f32[384,128]{1,0:T(8,128)S(1)} %copy-done.5), channel_id=1, source_target_pairs={{0,24},{1,9},{2,26},{3,11},{8,16},{9,1},{10,18},{11,3},{16,8},{17,... | collective-permute-start | bytes 589832 | tf_op jit(solution)/shard_map/ppermute | solution.py:549
  39.7 4.7 %collective-permute-done.3.refs_1_ = f32[384,128]{1,0:T(8,128)S(1)} collective-permute-done((f32[384,128]{1,0:T(8,128)S(1)}, f32[384,128]{1,0:T(8,128)S(1)}, u32[]{:S(2)}, u32[]{:S(2)}) %collective-permute-start.3) | collective-permute-done | bytes 196640 | tf_op jit(solution)/shard_map/ppermute | solution.py:549
  44.4 5.4 %collective-permute-done.4.refs_2_ = f32[384,128]{1,0:T(8,128)S(1)} collective-permute-done((f32[384,128]{1,0:T(8,128)S(1)}, f32[384,128]{1,0:T(8,128)S(1)}, u32[]{:S(2)}, u32[]{:S(2)}) %collective-permute-start.4) | collective-permute-done | bytes 196640 | tf_op jit(solution)/shard_map/ppermute | solution.py:549
  49.8 6.1 %collective-permute-done.5.refs_3_ = f32[384,128]{1,0:T(8,128)S(1)} collective-permute-done((f32[384,128]{1,0:T(8,128)S(1)}, f32[384,128]{1,0:T(8,128)S(1)}, u32[]{:S(2)}, u32[]{:S(2)}) %collective-permute-start.5) | collective-permute-done | bytes 196640 | tf_op jit(solution)/shard_map/ppermute | solution.py:549
  55.9 5.4 %nonlinear.3 = (f32[3,16,32,128]{3,2,1,0:T(8,128)S(1)}, f32[3,8,32,128]{3,2,1,0:T(8,128)S(1)}) custom-call(s32[8]{0:T(128)S(1)} %copy-done.3, s32[16,8]{1,0:T(8,128)S(1)} %bitcast.50, f32[384,128]{1,0:T(8,128)S(1)} %copy-done.2, f32[384,128]{1,0:T(8,128)S(1)} %collective-permute-done.3.refs_1_, f32[384,128]{1,0:T(8,128)S(1)} %collective-permute-done.4.refs_2_, ...), custom_call_target="tpu_custom_call" | custom-call | bytes 25165824 | tf_op jit(solution)/shard_map/nonlinear/pallas_call | solution.py:318
  61.4 1.7 %collective-permute-done.8 = f32[3,8,32,128]{3,2,1,0:T(8,128)S(1)} collective-permute-done((f32[3,8,32,128]{3,2,1,0:T(8,128)S(1)}, f32[3,8,32,128]{3,2,1,0:T(8,128)S(1)}, u32[]{:S(2)}, u32[]{:S(2)}) %collective-permute-start.8) | collective-permute-done | bytes 393248 | tf_op jit(solution)/shard_map/ppermute | solution.py:598
  63.2 0.6 collective-permute-start.9
  63.8 1.1 outgoing.3
  64.9 1.6 %collective-permute-start.18 = (f32[8,24,128]{2,1,0:T(8,128)S(1)}, f32[8,24,128]{2,1,0:T(8,128)S(1)}, u32[]{:S(2)}, u32[]{:S(2)}) collective-permute-start(f32[8,24,128]{2,1,0:T(8,128)S(1)} %bitcast.65), channel_id=1, source_target_pairs={{0,4},{1,17},{2,6},{3,19},{4,0},{5,21},{6,2},{7,23},{8,12},{9,25},... | collective-permute-start | bytes 294920 | tf_op jit(solution)/shard_map/ppermute | solution.py:549
  66.5 3.0 %collective-permute-start.19 = (f32[8,24,128]{2,1,0:T(8,128)S(1)}, f32[8,24,128]{2,1,0:T(8,128)S(1)}, u32[]{:S(2)}, u32[]{:S(2)}) collective-permute-start(f32[8,24,128]{2,1,0:T(8,128)S(1)} %bitcast.64), channel_id=1, source_target_pairs={{0,8},{1,25},{2,10},{3,27},{4,12},{5,29},{6,14},{7,31},{8,0},{9,17... | collective-permute-start | bytes 294920 | tf_op jit(solution)/shard_map/ppermute | solution.py:549
  69.5 1.3 collective-permute-start.20
  70.8 3.5 %collective-permute-done.9.other_ref = f32[3,8,32,128]{3,2,1,0:T(8,128)S(1)} collective-permute-done((f32[3,8,32,128]{3,2,1,0:T(8,128)S(1)}, f32[3,8,32,128]{3,2,1,0:T(8,128)S(1)}, u32[]{:S(2)}, u32[]{:S(2)}) %collective-permute-start.9) | collective-permute-done | bytes 393248 | tf_op jit(solution)/shard_map/ppermute | solution.py:598
  74.4 0.5 collective-permute-start.21
  74.9 1.1 outgoing.2
  76.0 3.5 %collective-permute-start.22 = (f32[8,24,128]{2,1,0:T(8,128)S(1)}, f32[8,24,128]{2,1,0:T(8,128)S(1)}, u32[]{:S(2)}, u32[]{:S(2)}) collective-permute-start(f32[8,24,128]{2,1,0:T(8,128)S(1)} %bitcast.59), channel_id=1, source_target_pairs={{0,12},{1,21},{2,14},{3,23},{4,8},{5,17},{6,10},{7,19},{8,4},{9,29... | collective-permute-start | bytes 294920 | tf_op jit(solution)/shard_map/ppermute | solution.py:549
  79.5 2.3 %collective-permute-start.23 = (f32[8,24,128]{2,1,0:T(8,128)S(1)}, f32[8,24,128]{2,1,0:T(8,128)S(1)}, u32[]{:S(2)}, u32[]{:S(2)}) collective-permute-start(f32[8,24,128]{2,1,0:T(8,128)S(1)} %bitcast.58), channel_id=1, source_target_pairs={{0,28},{1,29},{2,30},{3,31},{4,24},{5,25},{6,26},{7,27},{8,20},{9,... | collective-permute-start | bytes 294920 | tf_op jit(solution)/shard_map/ppermute | solution.py:549
  81.8 0.8 collective-permute-start.11
  82.6 1.1 collective-permute-done.21.refs_5_
  83.7 1.7 %collective-permute-start.12 = (f32[8,24,128]{2,1,0:T(8,128)S(1)}, f32[8,24,128]{2,1,0:T(8,128)S(1)}, u32[]{:S(2)}, u32[]{:S(2)}) collective-permute-start(f32[8,24,128]{2,1,0:T(8,128)S(1)} %bitcast.57), channel_id=1, source_target_pairs={{0,8},{1,25},{2,10},{3,27},{4,12},{5,29},{6,14},{7,31},{8,0},{9,17... | collective-permute-start | bytes 294920 | tf_op jit(solution)/shard_map/ppermute | solution.py:549
  85.4 1.4 collective-permute-start.13
  86.7 1.4 collective-permute-done.23.refs_7_
  88.1 4.6 %collective-permute-start.14 = (f32[8,24,128]{2,1,0:T(8,128)S(1)}, f32[8,24,128]{2,1,0:T(8,128)S(1)}, u32[]{:S(2)}, u32[]{:S(2)}) collective-permute-start(f32[8,24,128]{2,1,0:T(8,128)S(1)} %bitcast.55), channel_id=1, source_target_pairs={{0,20},{1,13},{2,22},{3,15},{4,16},{5,9},{6,18},{7,11},{8,28},{9,5... | collective-permute-start | bytes 294920 | tf_op jit(solution)/shard_map/ppermute | solution.py:549
  92.7 1.1 collective-permute-done.10.refs_1_
  93.8 2.0 %collective-permute-start.16 = (f32[8,24,128]{2,1,0:T(8,128)S(1)}, f32[8,24,128]{2,1,0:T(8,128)S(1)}, u32[]{:S(2)}, u32[]{:S(2)}) collective-permute-start(f32[8,24,128]{2,1,0:T(8,128)S(1)} %bitcast.53), channel_id=1, source_target_pairs={{0,28},{1,29},{2,30},{3,31},{4,24},{5,25},{6,26},{7,27},{8,20},{9,... | collective-permute-start | bytes 294920 | tf_op jit(solution)/shard_map/ppermute | solution.py:549
  95.8 6.0 %solve.2.refs_10_ = f32[8,96,512]{2,1,0:T(8,128)S(1)} custom-call(f32[8,24,128]{2,1,0:T(8,128)S(1)} %bitcast.52, f32[8,24,128]{2,1,0:T(8,128)S(1)} %collective-permute-done.17.refs_1_, f32[8,24,128]{2,1,0:T(8,128)S(1)} %collective-permute-done.18.refs_2_, f32[8,24,128]{2,1,0:T(8,128)S(1)} %collective-permute-done.19.refs_3_, ...), custom_call_target="tpu_custom_call" | custom-call | flops 603979776 | bytes 4194304 | tf_op jit(solution)/shard_map/solve/pallas_call | solution.py:452
  101.9 0.7 collective-permute-done.14.refs_5_
  102.6 0.9 collective-permute-done.15.refs_6_
  103.5 6.2 %solve.3 = (f32[8,2,24,128]{3,2,1,0:T(8,128)S(1)}, f32[8,2,24,128]{3,2,1,0:T(8,128)S(1)}, f32[8,2,24,128]{3,2,1,0:T(8,128)S(1)}, f32[8,2,24,128]{3,2,1,0:T(8,128...) custom-call(f32[8,24,128]{2,1,0:T(8,128)S(1)} %bitcast.51, ...), custom_call_target="tpu_custom_call" | custom-call | flops 603979776 | bytes 4194304 | tf_op jit(solution)/shard_map/solve/pallas_call | solution.py:452
  109.7 1.5 %collective-permute-start.24 = (f32[8,2,24,128]{3,2,1,0:T(8,128)S(1)}, f32[8,2,24,128]{3,2,1,0:T(8,128)S(1)}, u32[]{:S(2)}, u32[]{:S(2)}) collective-permute-start(f32[8,2,24,128]{3,2,1,0:T(8,128)S(1)} %get-tuple-element.76), channel_id=1, source_target_pairs={{0,16},{1,5},{2,18},{3,7},{4,20},{5,1},{6,22},{7,3},{8,24},{9,13},... | collective-permute-start | bytes 589832 | tf_op jit(solution)/shard_map/ppermute | solution.py:549
  111.2 1.6 %collective-permute-start.25 = (f32[8,2,24,128]{3,2,1,0:T(8,128)S(1)}, f32[8,2,24,128]{3,2,1,0:T(8,128)S(1)}, u32[]{:S(2)}, u32[]{:S(2)}) collective-permute-start(f32[8,2,24,128]{3,2,1,0:T(8,128)S(1)} %get-tuple-element.77), channel_id=1, source_target_pairs={{0,4},{1,17},{2,6},{3,19},{4,0},{5,21},{6,2},{7,23},{8,12},{9,25},... | collective-permute-start | bytes 589832 | tf_op jit(solution)/shard_map/ppermute | solution.py:549
  112.8 2.3 %collective-permute-start.27 = (f32[8,2,24,128]{3,2,1,0:T(8,128)S(1)}, f32[8,2,24,128]{3,2,1,0:T(8,128)S(1)}, u32[]{:S(2)}, u32[]{:S(2)}) collective-permute-start(f32[8,2,24,128]{3,2,1,0:T(8,128)S(1)} %get-tuple-element.79), channel_id=1, source_target_pairs={{0,24},{1,9},{2,26},{3,11},{4,28},{5,13},{6,30},{7,15},{8,16},{9,1... | collective-permute-start | bytes 589832 | tf_op jit(solution)/shard_map/ppermute | solution.py:549
  115.1 1.1 collective-permute-start.28
  116.2 9.6 %collective-permute-done.24 = f32[8,2,24,128]{3,2,1,0:T(8,128)S(1)} collective-permute-done((f32[8,2,24,128]{3,2,1,0:T(8,128)S(1)}, f32[8,2,24,128]{3,2,1,0:T(8,128)S(1)}, u32[]{:S(2)}, u32[]{:S(2)}) %collective-permute-start.24) | collective-permute-done | bytes 196640 | tf_op jit(solution)/shard_map/ppermute | solution.py:549
  125.7 1.5 %collective-permute-start.30 = (f32[8,2,24,128]{3,2,1,0:T(8,128)S(1)}, f32[8,2,24,128]{3,2,1,0:T(8,128)S(1)}, u32[]{:S(2)}, u32[]{:S(2)}) collective-permute-start(f32[8,2,24,128]{3,2,1,0:T(8,128)S(1)} %get-tuple-element.82), channel_id=1, source_target_pairs={{0,28},{1,29},{2,30},{3,31},{4,24},{5,25},{6,26},{7,27},{8,20},{9,... | collective-permute-start | bytes 589832 | tf_op jit(solution)/shard_map/ppermute | solution.py:549
  127.3 0.8 collective-permute-done.27
  128.1 16.1 %collective-permute-done.28 = f32[8,2,24,128]{3,2,1,0:T(8,128)S(1)} collective-permute-done((f32[8,2,24,128]{3,2,1,0:T(8,128)S(1)}, f32[8,2,24,128]{3,2,1,0:T(8,128)S(1)}, u32[]{:S(2)}, u32[]{:S(2)}) %collective-permute-start.28) | collective-permute-done | bytes 196640 | tf_op jit(solution)/shard_map/ppermute | solution.py:549
  144.2 2.0 %restore.1 = f32[3,4,256,128]{3,2,1,0:T(8,128)} custom-call(f32[384,128]{1,0:T(8,128)S(1)} %bitcast.41, f32[384,128]{1,0:T(8,128)S(1)} %bitcast.42, f32[384,128]{1,0:T(8,128)S(1)} %bitcast.43, f32[384,128]{1,0:T(8,128)S(1)} %bitcast.44, f32[384,128]{1,0:T(8,128)S(1)} %bitcast.45, f32[384,128]{1,0:T(8,128)S(1)} %bitcast.46, f32[384,128]{1,0:T(8,128)S(1)} %bitcast.47, ...), custom_call_target="tpu_custom_call" | custom-call | bytes 3145728 | tf_op jit(solution)/shard_map/restore/pallas_call | solution.py:495
  (74 shorter events, 1.3 us)
Async XLA Ops:
  2.7 23.5 %collective-permute-start = (f32[392,128]{1,0:T(8,128)}, f32[392,128]{1,0:T(8,128)S(1)}, u32[]{:S(2)}, u32[]{:S(2)}) collective-permute-start(f32[392,128]{1,0:T(8,128)} %get-tuple-element.45), channel_id=1, source_target_pairs={{0,8},{1,25},{2,10},{3,27},{8,0},{9,17},{10,2},{11,19},{16,24},{17... | collective-permute-start | bytes 602120 | tf_op jit(solution)/shard_map/ppermute | solution.py:549
  5.7 20.5 %collective-permute-start.1 = (f32[392,128]{1,0:T(8,128)}, f32[392,128]{1,0:T(8,128)S(1)}, u32[]{:S(2)}, u32[]{:S(2)}) collective-permute-start(f32[392,128]{1,0:T(8,128)} %get-tuple-element.46), channel_id=1, source_target_pairs={{0,24},{1,9},{2,26},{3,11},{8,16},{9,1},{10,18},{11,3},{16,8},{17,... | collective-permute-start | bytes 602120 | tf_op jit(solution)/shard_map/ppermute | solution.py:549
  8.2 18.0 %collective-permute-start.2 = (f32[392,128]{1,0:T(8,128)}, f32[392,128]{1,0:T(8,128)S(1)}, u32[]{:S(2)}, u32[]{:S(2)}) collective-permute-start(f32[392,128]{1,0:T(8,128)} %get-tuple-element.47), channel_id=1, source_target_pairs={{0,16},{1,17},{2,18},{3,19},{8,24},{9,25},{10,26},{11,27},{16,0},{... | collective-permute-start | bytes 602120 | tf_op jit(solution)/shard_map/ppermute | solution.py:549
  15.0 11.6 %copy-start.1 = (f32[392,128]{1,0:T(8,128)S(1)}, f32[392,128]{1,0:T(8,128)}, u32[]{:S(2)}) copy-start(f32[392,128]{1,0:T(8,128)} %get-tuple-element.44.refs_0_) | copy-start | bytes 602116
  15.0 11.7 %copy-start.3 = (s32[8]{0:T(128)S(1)}, s32[8]{0:T(128)}, u32[]{:S(2)}) copy-start(s32[8]{0:T(128)} %low_ref.7) | copy-start | bytes 100
  15.0 20.4 %copy-start.6 = (f32[384,128]{1,0:T(8,128)S(1)}, f32[384,128]{1,0:T(8,128)}, u32[]{:S(2)}) copy-start(f32[384,128]{1,0:T(8,128)} %get-tuple-element.49) | copy-start | bytes 589828
  15.0 22.2 %copy-start.5 = (f32[384,128]{1,0:T(8,128)S(1)}, f32[384,128]{1,0:T(8,128)}, u32[]{:S(2)}) copy-start(f32[384,128]{1,0:T(8,128)} %get-tuple-element.50) | copy-start | bytes 589828
  15.0 24.7 %copy-start.4 = (f32[384,128]{1,0:T(8,128)S(1)}, f32[384,128]{1,0:T(8,128)}, u32[]{:S(2)}) copy-start(f32[384,128]{1,0:T(8,128)} %get-tuple-element.51) | copy-start | bytes 589828
  15.0 41.0 %copy-start.2 = (f32[384,128]{1,0:T(8,128)S(1)}, f32[384,128]{1,0:T(8,128)}, u32[]{:S(2)}) copy-start(f32[384,128]{1,0:T(8,128)} %get-tuple-element.48.refs_0_) | copy-start | bytes 589828
  24.1 2.0 %copy-start = (bf16[8,512,512]{2,1,0:T(8,128)(2,1)}, bf16[8,512,512]{2,1,0:T(8,128)(2,1)S(1)}, u32[]{:S(2)}) copy-start(bf16[8,512,512]{2,1,0:T(8,128)(2,1)S(1)} %get-tuple-element.64.refs_8_) | copy-start | bytes 12582916
  32.0 1.8 %collective-permute-start.6 = (f32[3,8,32,128]{3,2,1,0:T(8,128)S(1)}, f32[3,8,32,128]{3,2,1,0:T(8,128)S(1)}, u32[]{:S(2)}, u32[]{:S(2)}) collective-permute-start(f32[3,8,32,128]{3,2,1,0:T(8,128)S(1)} %get-tuple-element.53), channel_id=1, source_target_pairs={{0,1},{1,0},{2,3},{3,2},{4,5},{5,4},{6,7},{7,6},{8,9},{9,8},{10,11... | collective-permute-start | bytes 1179656 | tf_op jit(solution)/shard_map/ppermute | solution.py:598
  33.8 22.1 %collective-permute-start.7 = (f32[3,8,32,128]{3,2,1,0:T(8,128)S(1)}, f32[3,8,32,128]{3,2,1,0:T(8,128)S(1)}, u32[]{:S(2)}, u32[]{:S(2)}) collective-permute-start(f32[3,8,32,128]{3,2,1,0:T(8,128)S(1)} %add.129.stress_ref), channel_id=1, source_target_pairs={{0,2},{1,3},{2,0},{3,1},{4,6},{5,7},{6,4},{7,5},{8,10},{9,11},{10,... | collective-permute-start | bytes 1179656 | tf_op jit(solution)/shard_map/ppermute | solution.py:598
  35.4 9.0 %collective-permute-start.3 = (f32[384,128]{1,0:T(8,128)S(1)}, f32[384,128]{1,0:T(8,128)S(1)}, u32[]{:S(2)}, u32[]{:S(2)}) collective-permute-start(f32[384,128]{1,0:T(8,128)S(1)} %copy-done.6), channel_id=1, source_target_pairs={{0,8},{1,25},{2,10},{3,27},{8,0},{9,17},{10,2},{11,19},{16,24},{17... | collective-permute-start | bytes 589832 | tf_op jit(solution)/shard_map/ppermute | solution.py:549
  37.2 12.6 %collective-permute-start.4 = (f32[384,128]{1,0:T(8,128)S(1)}, f32[384,128]{1,0:T(8,128)S(1)}, u32[]{:S(2)}, u32[]{:S(2)}) collective-permute-start(f32[384,128]{1,0:T(8,128)S(1)} %copy-done.5), channel_id=1, source_target_pairs={{0,24},{1,9},{2,26},{3,11},{8,16},{9,1},{10,18},{11,3},{16,8},{17,... | collective-permute-start | bytes 589832 | tf_op jit(solution)/shard_map/ppermute | solution.py:549
  39.7 16.3 %collective-permute-start.5 = (f32[384,128]{1,0:T(8,128)S(1)}, f32[384,128]{1,0:T(8,128)S(1)}, u32[]{:S(2)}, u32[]{:S(2)}) collective-permute-start(f32[384,128]{1,0:T(8,128)S(1)} %copy-done.4), channel_id=1, source_target_pairs={{0,16},{1,17},{2,18},{3,19},{8,24},{9,25},{10,26},{11,27},{16,0},{... | collective-permute-start | bytes 589832 | tf_op jit(solution)/shard_map/ppermute | solution.py:549
  61.3 1.8 %collective-permute-start.8 = (f32[3,8,32,128]{3,2,1,0:T(8,128)S(1)}, f32[3,8,32,128]{3,2,1,0:T(8,128)S(1)}, u32[]{:S(2)}, u32[]{:S(2)}) collective-permute-start(f32[3,8,32,128]{3,2,1,0:T(8,128)S(1)} %get-tuple-element.55), channel_id=1, source_target_pairs={{0,1},{1,0},{2,3},{3,2},{4,5},{5,4},{6,7},{7,6},{8,9},{9,8},{10,11... | collective-permute-start | bytes 1179656 | tf_op jit(solution)/shard_map/ppermute | solution.py:598
  63.2 11.2 %collective-permute-start.9 = (f32[3,8,32,128]{3,2,1,0:T(8,128)S(1)}, f32[3,8,32,128]{3,2,1,0:T(8,128)S(1)}, u32[]{:S(2)}, u32[]{:S(2)}) collective-permute-start(f32[3,8,32,128]{3,2,1,0:T(8,128)S(1)} %add.130.stress_ref), channel_id=1, source_target_pairs={{0,2},{1,3},{2,0},{3,1},{4,6},{5,7},{6,4},{7,5},{8,10},{9,11},{10,... | collective-permute-start | bytes 1179656 | tf_op jit(solution)/shard_map/ppermute | solution.py:598
  64.9 11.1 %collective-permute-start.17 = (f32[8,24,128]{2,1,0:T(8,128)S(1)}, f32[8,24,128]{2,1,0:T(8,128)S(1)}, u32[]{:S(2)}, u32[]{:S(2)}) collective-permute-start(f32[8,24,128]{2,1,0:T(8,128)S(1)} %bitcast.66), channel_id=1, source_target_pairs={{0,16},{1,5},{2,18},{3,7},{4,20},{5,1},{6,22},{7,3},{8,24},{9,13},... | collective-permute-start | bytes 294920 | tf_op jit(solution)/shard_map/ppermute | solution.py:549
  64.9 14.6 %collective-permute-start.18 = (f32[8,24,128]{2,1,0:T(8,128)S(1)}, f32[8,24,128]{2,1,0:T(8,128)S(1)}, u32[]{:S(2)}, u32[]{:S(2)}) collective-permute-start(f32[8,24,128]{2,1,0:T(8,128)S(1)} %bitcast.65), channel_id=1, source_target_pairs={{0,4},{1,17},{2,6},{3,19},{4,0},{5,21},{6,2},{7,23},{8,12},{9,25},... | collective-permute-start | bytes 294920 | tf_op jit(solution)/shard_map/ppermute | solution.py:549
  66.5 15.3 %collective-permute-start.19 = (f32[8,24,128]{2,1,0:T(8,128)S(1)}, f32[8,24,128]{2,1,0:T(8,128)S(1)}, u32[]{:S(2)}, u32[]{:S(2)}) collective-permute-start(f32[8,24,128]{2,1,0:T(8,128)S(1)} %bitcast.64), channel_id=1, source_target_pairs={{0,8},{1,25},{2,10},{3,27},{4,12},{5,29},{6,14},{7,31},{8,0},{9,17... | collective-permute-start | bytes 294920 | tf_op jit(solution)/shard_map/ppermute | solution.py:549
  69.5 12.3 %collective-permute-start.20 = (f32[8,24,128]{2,1,0:T(8,128)S(1)}, f32[8,24,128]{2,1,0:T(8,128)S(1)}, u32[]{:S(2)}, u32[]{:S(2)}) collective-permute-start(f32[8,24,128]{2,1,0:T(8,128)S(1)} %bitcast.62), channel_id=1, source_target_pairs={{0,24},{1,9},{2,26},{3,11},{4,28},{5,13},{6,30},{7,15},{8,16},{9,1... | collective-permute-start | bytes 294920 | tf_op jit(solution)/shard_map/ppermute | solution.py:549
  74.4 9.3 %collective-permute-start.21 = (f32[8,24,128]{2,1,0:T(8,128)S(1)}, f32[8,24,128]{2,1,0:T(8,128)S(1)}, u32[]{:S(2)}, u32[]{:S(2)}) collective-permute-start(f32[8,24,128]{2,1,0:T(8,128)S(1)} %bitcast.60), channel_id=1, source_target_pairs={{0,20},{1,13},{2,22},{3,15},{4,16},{5,9},{6,18},{7,11},{8,28},{9,5... | collective-permute-start | bytes 294920 | tf_op jit(solution)/shard_map/ppermute | solution.py:549
  76.0 9.4 %collective-permute-start.22 = (f32[8,24,128]{2,1,0:T(8,128)S(1)}, f32[8,24,128]{2,1,0:T(8,128)S(1)}, u32[]{:S(2)}, u32[]{:S(2)}) collective-permute-start(f32[8,24,128]{2,1,0:T(8,128)S(1)} %bitcast.59), channel_id=1, source_target_pairs={{0,12},{1,21},{2,14},{3,23},{4,8},{5,17},{6,10},{7,19},{8,4},{9,29... | collective-permute-start | bytes 294920 | tf_op jit(solution)/shard_map/ppermute | solution.py:549
  79.5 8.6 %collective-permute-start.23 = (f32[8,24,128]{2,1,0:T(8,128)S(1)}, f32[8,24,128]{2,1,0:T(8,128)S(1)}, u32[]{:S(2)}, u32[]{:S(2)}) collective-permute-start(f32[8,24,128]{2,1,0:T(8,128)S(1)} %bitcast.58), channel_id=1, source_target_pairs={{0,28},{1,29},{2,30},{3,31},{4,24},{5,25},{6,26},{7,27},{8,20},{9,... | collective-permute-start | bytes 294920 | tf_op jit(solution)/shard_map/ppermute | solution.py:549
  81.8 12.0 %collective-permute-start.10 = (f32[8,24,128]{2,1,0:T(8,128)S(1)}, f32[8,24,128]{2,1,0:T(8,128)S(1)}, u32[]{:S(2)}, u32[]{:S(2)}) collective-permute-start(f32[8,24,128]{2,1,0:T(8,128)S(1)} %bitcast.63), channel_id=1, source_target_pairs={{0,16},{1,5},{2,18},{3,7},{4,20},{5,1},{6,22},{7,3},{8,24},{9,13},... | collective-permute-start | bytes 294920 | tf_op jit(solution)/shard_map/ppermute | solution.py:549
  81.8 12.0 %collective-permute-start.11 = (f32[8,24,128]{2,1,0:T(8,128)S(1)}, f32[8,24,128]{2,1,0:T(8,128)S(1)}, u32[]{:S(2)}, u32[]{:S(2)}) collective-permute-start(f32[8,24,128]{2,1,0:T(8,128)S(1)} %bitcast.61), channel_id=1, source_target_pairs={{0,4},{1,17},{2,6},{3,19},{4,0},{5,21},{6,2},{7,23},{8,12},{9,25},... | collective-permute-start | bytes 294920 | tf_op jit(solution)/shard_map/ppermute | solution.py:549
  83.7 18.2 %collective-permute-start.12 = (f32[8,24,128]{2,1,0:T(8,128)S(1)}, f32[8,24,128]{2,1,0:T(8,128)S(1)}, u32[]{:S(2)}, u32[]{:S(2)}) collective-permute-start(f32[8,24,128]{2,1,0:T(8,128)S(1)} %bitcast.57), channel_id=1, source_target_pairs={{0,8},{1,25},{2,10},{3,27},{4,12},{5,29},{6,14},{7,31},{8,0},{9,17... | collective-permute-start | bytes 294920 | tf_op jit(solution)/shard_map/ppermute | solution.py:549
  85.4 16.5 %collective-permute-start.13 = (f32[8,24,128]{2,1,0:T(8,128)S(1)}, f32[8,24,128]{2,1,0:T(8,128)S(1)}, u32[]{:S(2)}, u32[]{:S(2)}) collective-permute-start(f32[8,24,128]{2,1,0:T(8,128)S(1)} %bitcast.56), channel_id=1, source_target_pairs={{0,24},{1,9},{2,26},{3,11},{4,28},{5,13},{6,30},{7,15},{8,16},{9,1... | collective-permute-start | bytes 294920 | tf_op jit(solution)/shard_map/ppermute | solution.py:549
  88.1 14.5 %collective-permute-start.14 = (f32[8,24,128]{2,1,0:T(8,128)S(1)}, f32[8,24,128]{2,1,0:T(8,128)S(1)}, u32[]{:S(2)}, u32[]{:S(2)}) collective-permute-start(f32[8,24,128]{2,1,0:T(8,128)S(1)} %bitcast.55), channel_id=1, source_target_pairs={{0,20},{1,13},{2,22},{3,15},{4,16},{5,9},{6,18},{7,11},{8,28},{9,5... | collective-permute-start | bytes 294920 | tf_op jit(solution)/shard_map/ppermute | solution.py:549
  93.8 9.7 %collective-permute-start.15 = (f32[8,24,128]{2,1,0:T(8,128)S(1)}, f32[8,24,128]{2,1,0:T(8,128)S(1)}, u32[]{:S(2)}, u32[]{:S(2)}) collective-permute-start(f32[8,24,128]{2,1,0:T(8,128)S(1)} %bitcast.54), channel_id=1, source_target_pairs={{0,12},{1,21},{2,14},{3,23},{4,8},{5,17},{6,10},{7,19},{8,4},{9,29... | collective-permute-start | bytes 294920 | tf_op jit(solution)/shard_map/ppermute | solution.py:549
  93.8 9.7 %collective-permute-start.16 = (f32[8,24,128]{2,1,0:T(8,128)S(1)}, f32[8,24,128]{2,1,0:T(8,128)S(1)}, u32[]{:S(2)}, u32[]{:S(2)}) collective-permute-start(f32[8,24,128]{2,1,0:T(8,128)S(1)} %bitcast.53), channel_id=1, source_target_pairs={{0,28},{1,29},{2,30},{3,31},{4,24},{5,25},{6,26},{7,27},{8,20},{9,... | collective-permute-start | bytes 294920 | tf_op jit(solution)/shard_map/ppermute | solution.py:549
  109.7 16.1 %collective-permute-start.24 = (f32[8,2,24,128]{3,2,1,0:T(8,128)S(1)}, f32[8,2,24,128]{3,2,1,0:T(8,128)S(1)}, u32[]{:S(2)}, u32[]{:S(2)}) collective-permute-start(f32[8,2,24,128]{3,2,1,0:T(8,128)S(1)} %get-tuple-element.76), channel_id=1, source_target_pairs={{0,16},{1,5},{2,18},{3,7},{4,20},{5,1},{6,22},{7,3},{8,24},{9,13},... | collective-permute-start | bytes 589832 | tf_op jit(solution)/shard_map/ppermute | solution.py:549
  111.2 14.5 %collective-permute-start.25 = (f32[8,2,24,128]{3,2,1,0:T(8,128)S(1)}, f32[8,2,24,128]{3,2,1,0:T(8,128)S(1)}, u32[]{:S(2)}, u32[]{:S(2)}) collective-permute-start(f32[8,2,24,128]{3,2,1,0:T(8,128)S(1)} %get-tuple-element.77), channel_id=1, source_target_pairs={{0,4},{1,17},{2,6},{3,19},{4,0},{5,21},{6,2},{7,23},{8,12},{9,25},... | collective-permute-start | bytes 589832 | tf_op jit(solution)/shard_map/ppermute | solution.py:549
  112.8 14.4 %collective-permute-start.26 = (f32[8,2,24,128]{3,2,1,0:T(8,128)S(1)}, f32[8,2,24,128]{3,2,1,0:T(8,128)S(1)}, u32[]{:S(2)}, u32[]{:S(2)}) collective-permute-start(f32[8,2,24,128]{3,2,1,0:T(8,128)S(1)} %get-tuple-element.78), channel_id=1, source_target_pairs={{0,8},{1,25},{2,10},{3,27},{4,12},{5,29},{6,14},{7,31},{8,0},{9,17... | collective-permute-start | bytes 589832 | tf_op jit(solution)/shard_map/ppermute | solution.py:549
  112.8 15.2 %collective-permute-start.27 = (f32[8,2,24,128]{3,2,1,0:T(8,128)S(1)}, f32[8,2,24,128]{3,2,1,0:T(8,128)S(1)}, u32[]{:S(2)}, u32[]{:S(2)}) collective-permute-start(f32[8,2,24,128]{3,2,1,0:T(8,128)S(1)} %get-tuple-element.79), channel_id=1, source_target_pairs={{0,24},{1,9},{2,26},{3,11},{4,28},{5,13},{6,30},{7,15},{8,16},{9,1... | collective-permute-start | bytes 589832 | tf_op jit(solution)/shard_map/ppermute | solution.py:549
  115.1 29.0 %collective-permute-start.28 = (f32[8,2,24,128]{3,2,1,0:T(8,128)S(1)}, f32[8,2,24,128]{3,2,1,0:T(8,128)S(1)}, u32[]{:S(2)}, u32[]{:S(2)}) collective-permute-start(f32[8,2,24,128]{3,2,1,0:T(8,128)S(1)} %get-tuple-element.80), channel_id=1, source_target_pairs={{0,20},{1,13},{2,22},{3,15},{4,16},{5,9},{6,18},{7,11},{8,28},{9,5... | collective-permute-start | bytes 589832 | tf_op jit(solution)/shard_map/ppermute | solution.py:549
  125.7 18.4 %collective-permute-start.29 = (f32[8,2,24,128]{3,2,1,0:T(8,128)S(1)}, f32[8,2,24,128]{3,2,1,0:T(8,128)S(1)}, u32[]{:S(2)}, u32[]{:S(2)}) collective-permute-start(f32[8,2,24,128]{3,2,1,0:T(8,128)S(1)} %get-tuple-element.81), channel_id=1, source_target_pairs={{0,12},{1,21},{2,14},{3,23},{4,8},{5,17},{6,10},{7,19},{8,4},{9,29... | collective-permute-start | bytes 589832 | tf_op jit(solution)/shard_map/ppermute | solution.py:549
  125.7 18.4 %collective-permute-start.30 = (f32[8,2,24,128]{3,2,1,0:T(8,128)S(1)}, f32[8,2,24,128]{3,2,1,0:T(8,128)S(1)}, u32[]{:S(2)}, u32[]{:S(2)}) collective-permute-start(f32[8,2,24,128]{3,2,1,0:T(8,128)S(1)} %get-tuple-element.82), channel_id=1, source_target_pairs={{0,28},{1,29},{2,30},{3,31},{4,24},{5,25},{6,26},{7,27},{8,20},{9,... | collective-permute-start | bytes 589832 | tf_op jit(solution)/shard_map/ppermute | solution.py:549

commit v5 on v4

--- a/solution.py
+++ b/solution.py
@@ -150,10 +150,13 @@
 def pack_kernel(near_ref, count_ref, velocity_ref, *out_refs):
     chunks, pieces, kx_count, rows, columns = velocity_ref.shape
     own = lax.axis_index("kx")
-    for index, out_ref in enumerate(out_refs):
-        piece, partner = (index // kx_count, own ^ step_at(kx_count, index % kx_count))
+    for index in range(kx_count):
+        partner = own ^ step_at(kx_count, index)
         for chunk in range(chunks):
-            out_ref[chunk * rows : (chunk + 1) * rows] = velocity_ref[chunk, piece, partner]
+            place = slice(chunk * rows, (chunk + 1) * rows)
+            out_refs[index][place] = velocity_ref[chunk, 0, partner]
+            for piece in range(1, pieces):
+                out_refs[kx_count + piece - 1][index, place] = velocity_ref[chunk, piece, index]
     shape = (out_refs[0].shape[0] - chunks * rows, columns)
     row = lax.broadcasted_iota(jnp.int32, shape, 0)
     lane = lax.broadcasted_iota(jnp.int32, shape, 1)
@@ -171,19 +174,18 @@
 
 def pack(velocity, neighbours, mode_counts, extra_rows):
     chunks, pieces, kx_count, rows, columns = velocity.shape
-    shapes = []
-    for piece in range(pieces):
-        total = chunks * rows + (0 if piece else extra_rows)
-        shapes += [jax.ShapeDtypeStruct((total, columns), jnp.float32)] * kx_count
+    size = chunks * rows
+    shapes = [(size + extra_rows, columns)] * kx_count
+    shapes += [(kx_count, size, columns)] * (pieces - 1)
     out = pl.pallas_call(
         pack_kernel,
-        out_shape=tuple(shapes),
+        out_shape=tuple(jax.ShapeDtypeStruct(shape, jnp.float32) for shape in shapes),
         in_specs=[SMEM, SMEM, VMEM],
         out_specs=(VMEM,) * len(shapes),
         cost_estimate=cost(8 * velocity.size),
         name="pack",
     )(neighbours, mode_counts, velocity)
-    return [out[piece * kx_count : (piece + 1) * kx_count] for piece in range(pieces)]
+    return out[:kx_count], out[kx_count:]
 
 
 def split_matrix_kernel(matrix_ref, top_ref, rest_ref, mark_ref, turned, *, pieces, kx_count):
@@ -224,14 +226,20 @@
 
 
 def nonlinear_kernel(low_ref, near_ref, *refs):
-    block_refs, refs = (refs[:-11], refs[-11:])
-    first_ref, second_ref, back_ref, mask_ref, _, slotted_ref, stress_ref, *scratch = refs
-    physical, products, sums, high_ref = scratch
+    block_refs, refs = (refs[:-12], refs[-12:])
+    first_ref, second_ref, back_ref, mask_ref, _, slotted_ref, kept_ref, sent_ref = refs[:8]
+    physical, products, sums, high_ref = refs[8:]
     components, modes, rows, columns = slotted_ref.shape
-    bands, points = (len(block_refs), physical.shape[3])
-    band_modes = modes // bands
-    own = lax.axis_index("kx")
-    members, highs = (stress_ref.shape[1], products.shape[1])
+    if len(block_refs) > 1:
+        bands = len(block_refs)
+        places = [lax.axis_index("kx") ^ step_at(bands, index) for index in range(bands)]
+    else:
+        bands = block_refs[0].shape[0]
+        places = list(range(bands))
+        block_refs = [block_refs[0].at[index] for index in range(bands)]
+    points, band_modes = (physical.shape[3], modes // bands)
+    members, highs = (sums.shape[1], products.shape[1])
+    odd = lax.axis_index("real") % 2 == 1
     found = jnp.int32(0)
     for mode in range(modes):
         is_low = jnp.int32(0)
@@ -246,7 +254,7 @@
             top, rest = two_parts(block_ref[pl.ds(pl.multiple_of(component * size, 8), size)])
             both = dot(jnp.concatenate([top, rest], axis=1), first_ref[...])
             fields = both[:, :points] + dot(top, second_ref[...])
-            place = pl.ds((own ^ step_at(bands, index)) * band_modes, band_modes)
+            place = pl.ds(places[index] * band_modes, band_modes)
             physical[component, place] = fields.reshape(band_modes, rows, points)
             slotted_ref[component, place] = both[:, points:].reshape(band_modes, rows, columns)
         return carry
@@ -305,7 +313,9 @@
             mode = high_ref[index]
             slotted_ref[component, mode] += forcing[index] * mask_ref[mode]
         stress = inverse(sums[component].reshape(members * rows, points), 2 * columns)
-        stress_ref[component] = stress.reshape(members, rows, columns)
+        stress = stress.reshape(2, members // 2, rows, columns)
+        kept_ref[component] = jnp.where(odd, stress[1], stress[0])
+        sent_ref[component] = jnp.where(odd, stress[0], stress[1])
         return carry
 
     lax.fori_loop(0, components, finish, 0)
@@ -319,10 +329,11 @@
         nonlinear_kernel,
         out_shape=(
             jax.ShapeDtypeStruct((components, modes, rows, columns), jnp.float32),
-            jax.ShapeDtypeStruct((components, members, rows, columns), jnp.float32),
+            jax.ShapeDtypeStruct((components, members // 2, rows, columns), jnp.float32),
+            jax.ShapeDtypeStruct((components, members // 2, rows, columns), jnp.float32),
         ),
         in_specs=[SMEM, SMEM] + [VMEM] * (len(blocks) + 4) + [pl.BlockSpec(memory_space=pl.ANY)],
-        out_specs=(VMEM, VMEM),
+        out_specs=(VMEM, VMEM, VMEM),
         scratch_shapes=[
             pltpu.VMEM((components, modes, rows, points), jnp.float32),
             pltpu.VMEM((components, highs, rows, points), jnp.float32),
@@ -336,27 +347,28 @@
 
 
 def outgoing_kernel(
-    low_ref, slotted_ref, stress_ref, other_ref, mask_ref, *refs, groups, band_modes
+    low_ref, slotted_ref, kept_ref, other_ref, mask_ref, *refs, groups, band_modes
 ):
     out_refs, full = (refs[:-1], refs[-1])
     components, modes, rows, columns = slotted_ref.shape
-    members, owners = (stress_ref.shape[1], len(out_refs))
+    half, owners = (kept_ref.shape[1], len(out_refs))
     slots = columns // 2 // owners
     per_slot = out_refs[0].shape[0] // slots
     full[...] = slotted_ref[...]
     position = lax.broadcasted_iota(jnp.int32, (rows, columns), 1) // slots % owners
-    odd = lax.axis_index("real") % 2 == 1
-    upper = odd & (position % 2 == 1) & (position < owners - 1)
-    lower = odd & (position % 2 == 0) & (position > 0)
-    for member in range(members):
-        mode = low_ref[member]
-        for c in range(components):
-            stress = stress_ref[c, member] + other_ref[c, member]
-            stress = jnp.where(
-                upper, pltpu.roll(stress, columns - slots, 1),
-                jnp.where(lower, pltpu.roll(stress, slots, 1), stress),
-            )
-            full[c, mode] += stress * mask_ref[mode]
+    own = lax.axis_index("real") % 2
+    upper = (own == 1) & (position % 2 == 1) & (position < owners - 1)
+    lower = (own == 1) & (position % 2 == 0) & (position > 0)
+    for member in range(half):
+        for part_ref, start in ((kept_ref, own * half), (other_ref, (1 - own) * half)):
+            mode = low_ref[start + member]
+            for c in range(components):
+                stress = part_ref[c, member]
+                stress = jnp.where(
+                    upper, pltpu.roll(stress, columns - slots, 1),
+                    jnp.where(lower, pltpu.roll(stress, slots, 1), stress),
+                )
+                full[c, mode] += stress * mask_ref[mode]
     inner = modes // groups
     for c in range(components):
         for part in range(inner):
@@ -372,7 +384,7 @@
                     ]
 
 
-def outgoing(slotted, stress, other, low_index, mask, groups, band_modes, owners):
+def outgoing(slotted, kept, other, low_index, mask, groups, band_modes, owners):
     components, modes, rows, columns = slotted.shape
     total = (columns // 2 // owners) * (modes // groups) * 2 * components
     return pl.pallas_call(
@@ -384,7 +396,7 @@
         compiler_params=params(),
         cost_estimate=cost(8 * slotted.size),
         name="outgoing",
-    )(low_index, slotted, stress, other, mask)
+    )(low_index, slotted, kept, other, mask)
 
 
 def regroup(blocks, rows):
@@ -550,6 +562,11 @@
     return result
 
 
+def swap(value, step):
+    pairs = [(index, index ^ step) for index in range(lax.axis_size("real"))]
+    return lax.ppermute(value, "real", pairs)
+
+
 def local(velocity, low_index, neighbours, owner_map, mode_counts, helmholtz):
     components, reals_dev, band_modes, rows_ht, columns = velocity.shape
     kx_count, ht_count = (lax.axis_size("kx"), lax.axis_size("ht"))
@@ -561,7 +578,7 @@
     if (
         columns != LANES or reals_dev != 1 or rows_ht % LANES or rows % 8 or LANES % rows or kx_count % groups or kx_count & (kx_count - 1)
         or (band_modes * 2 * components) % 8 or slots % 8 or owners & (owners - 1) or low_index.shape[0] >= kx_count * band_modes
-        or low_index.shape[0] >= columns or real_count < 2 or real_count & (real_count - 1)
+        or low_index.shape[0] >= columns or low_index.shape[0] % 2 or real_count < 2 or real_count & (real_count - 1)
     ):
         return local_plain(velocity, low_index, neighbours, owner_map, mode_counts, helmholtz)
     realizations, members = (real_count, low_index.shape[0])
@@ -576,8 +593,9 @@
             jnp.array(steps_of(owners)[0], jnp.int32),
         )
     )
-    parts = [
-        exchange(blocks, ("kx",)) for blocks in pack(split, neighbours, mode_counts, extra_rows)
+    first_blocks, rest = pack(split, neighbours, mode_counts, extra_rows)
+    parts = [exchange(first_blocks, ("kx",))] + [
+        (lax.all_to_all(block, "kx", split_axis=0, concat_axis=0, tiled=True),) for block in rest
     ]
     *matrices, after = split_matrix(helmholtz, pieces, kx_count, ht_count)
     small = 0.0
@@ -591,17 +609,17 @@
     mask, low_mask = slot_masks(owner_map, mode_counts, realizations)
     received = []
     for part in parts:
-        slotted, stress = nonlinear(part, shape, low_index, neighbours, tables, mask, after)
-        step, other = (1, None)
+        slotted, kept, sent = nonlinear(
+            part, shape, low_index, neighbours, tables, mask, after
+        )
+        kept = kept + swap(sent, 1)
+        step = 2
         while step < realizations:
-            stress = stress if other is None else stress + other
-            other = lax.ppermute(
-                stress, "real", [(index, index ^ step) for index in range(realizations)]
-            )
+            kept = kept + swap(kept, step)
             step *= 2
-        after = other
+        after = swap(kept, 1)
         blocks = outgoing(
-            slotted, stress, other, low_index, low_mask, groups, band_modes, owners
+            slotted, kept, after, low_index, low_mask, groups, band_modes, owners
         )
         blocks = [block.reshape(slots, -1, LANES) for block in blocks]
         received.append(exchange(blocks, ("kx", "ht")))

time: 147 us -> 146 us (level)
  waiting for transfers between devices: 54.9 us -> 48.8 us
  starting transfers between devices: 42.9 us -> 47 us
    ppermute x27 -> x24, waiting for transfers between devices: 47.9 us -> 33.7 us  [exchange(): result[position] = lax.ppermute(blocks[position], axes + ('real',), pairs)]
    ppermute x4 -> x6, waiting for transfers between devices: 6.97 us -> 15.1 us  [swap(): return lax.ppermute(value, 'real', pairs)]
    all_to_all x0 -> x1, starting transfers between devices: none -> 4.19 us  [local(): lax.all_to_all(block, 'kx', split_axis=0, concat_axis=0, tiled=True)]
    ppermute x27 -> x24, starting transfers between devices: 40.6 us -> 39.3 us  [exchange(): result[position] = lax.ppermute(blocks[position], axes + ('real',), pairs)]
    ppermute x4 -> x6, starting transfers between devices: 2.3 us -> 3.52 us  [swap(): return lax.ppermute(value, 'real', pairs)]
  transfers between devices with their start and end apart: 31 -> 31, of which waited for: 14 -> 11; matrix products, arithmetic and copies ran while one was open for 5% -> 5% of each run, Pallas kernels for 12% -> 16%
where the time goes in v5:
time: 146 us; the launch traced here: 144 us
  waiting for transfers between devices  48.8 us (33%)
  starting transfers between devices  47 us (32%)
  Pallas kernels  38.7 us (27%)
  local copies, waits for them, and re-layouts  5.92 us (4%)
  other arithmetic  1.77 us (1%)
  matrix products  1.47 us (1%)
    ppermute x24, starting transfers between devices, exchange(): result[position] = lax.ppermute(blocks[position], axes + ('real',), pairs)  39.3 us
    ppermute x24, waiting for transfers between devices, exchange(): result[position] = lax.ppermute(blocks[position], axes + ('real',), pairs)  33.7 us
    ppermute x6, waiting for transfers between devices, swap(): return lax.ppermute(value, 'real', pairs)  15.1 us
    pallas_call x2, Pallas kernels, solve(): pl.pallas_call(functools.partial(solve_kernel, groups=groups, kx_count=kx...  12.2 us
    pallas_call x2, Pallas kernels, nonlinear(): pl.pallas_call(nonlinear_kernel, out_shape=(jax.ShapeDtypeStruct((compone...  10.7 us
    pallas_call x1, Pallas kernels, split_matrix(): pl.pallas_call(functools.partial(split_matrix_kernel, pieces=pieces, kx_c...  9 us
    all_to_all x1, starting transfers between devices, local(): lax.all_to_all(block, 'kx', split_axis=0, concat_axis=0, tiled=True)  4.19 us
    ppermute x6, starting transfers between devices, swap(): return lax.ppermute(value, 'real', pairs)  3.52 us
  transfers between devices with their start and end apart: 31, of which 11 were waited for; matrix products, arithmetic and copies ran while one was open for 5% of the time, Pallas kernels for 16%

profile of v5, /device:TPU:0, one launch (start us, length us, event | category | flops | bytes accessed | tf_op | source)
XLA Modules:
  0.0 144.0 jit_solution(15575390009396557844)
XLA Ops:
  0.0 2.6 %pack.1 = (f32[392,128]{1,0:T(8,128)}, f32[392,128]{1,0:T(8,128)}, f32[392,128]{1,0:T(8,128)}, f32[392,128]{1,0:T(8,128)}, f32[4,384,128]{2,1,0:T(8,128)}) custom-call(s32[4,8]{1,0:T(4,128)} %near_ref.1, s32[4]{0:T(128)} %count_ref.1, f32[12,2,4,32,128]{4,3,2,1,0:T(8,128)} %bitcast.67), custom_call_target="tpu_custom_call" | custom-call | bytes 3145728 | tf_op jit(solution)/shard_map/pack/pallas_call | solution.py:180
  2.6 4.0 %collective-permute-start.2 = (f32[392,128]{1,0:T(8,128)}, f32[392,128]{1,0:T(8,128)S(1)}, u32[]{:S(2)}, u32[]{:S(2)}) collective-permute-start(f32[392,128]{1,0:T(8,128)} %get-tuple-element.46), channel_id=1, source_target_pairs={{0,16},{1,17},{2,18},{3,19},{8,24},{9,25},{10,26},{11,27},{16,0},{... | collective-permute-start | bytes 602120 | tf_op jit(solution)/shard_map/ppermute | solution.py:561
  6.7 1.3 collective-permute-start.1
  8.0 0.2 collective-permute-start
  8.2 4.2 %all-to-all-start = ((f32[4,384,128]{2,1,0:T(8,128)}), f32[4,384,128]{2,1,0:T(8,128)S(1)}, u32[]{:S(2)}, u32[]{:S(2)}) async-start(f32[4,384,128]{2,1,0:T(8,128)} %get-tuple-element.47), calls=%async_computation | async-start | bytes 1572864 | tf_op jit(solution)/shard_map/all_to_all | solution.py:598
  12.5 0.7 reshape.422
  13.2 0.1 stack.29
  13.3 0.6 gather_fusion
  14.1 0.1 iota_compare_fusion
  14.2 0.6 fusion.3
  14.7 0.7 reduce-precision_convert_fusion.1
  15.5 0.7 compare_select_fusion.1
  16.2 0.6 gather_fusion.1
  16.8 0.1 add.134
  16.9 0.7 reduce-precision_convert_fusion
  17.7 0.7 slice.20
  18.5 0.1 broadcast_in_dim.138
  18.7 0.1 broadcast_in_dim.133
  18.8 0.1 broadcast_in_dim.128
  19.0 0.1 broadcast_in_dim.122
  19.1 0.1 lt.85
  19.2 9.0 %split_matrix.1 = (bf16[8,512,512]{2,1,0:T(8,128)(2,1)S(1)}, bf16[8,512,512]{2,1,0:T(8,128)(2,1)}, f32[8,128]{1,0:T(8,128)S(1)}) custom-call(f32[8,512,512]{2,1,0:T(8,128)} %matrix_ref.1), custom_call_target="tpu_custom_call" | custom-call | bytes 16777216 | tf_op jit(solution)/shard_map/split_matrix/pallas_call | solution.py:215
  28.2 2.0 %copy-done = bf16[8,512,512]{2,1,0:T(8,128)(2,1)} copy-done((bf16[8,512,512]{2,1,0:T(8,128)(2,1)}, bf16[8,512,512]{2,1,0:T(8,128)(2,1)S(1)}, u32[]{:S(2)}) %copy-start) | copy-done | bytes 4194328
  30.4 0.2 slice_reduce_fusion
  30.5 0.1 broadcast_multiply_fusion
  30.7 5.4 %nonlinear.2 = (f32[3,16,32,128]{3,2,1,0:T(8,128)S(1)}, f32[3,4,32,128]{3,2,1,0:T(8,128)S(1)}, f32[3,4,32,128]{3,2,1,0:T(8,128)S(1)}) custom-call(s32[8]{0:T(128)S(1)} %copy-done.2, s32[16,8]{1,0:T(8,128)S(1)} %bitcast.49, f32[392,128]{1,0:T(8,128)S(1)} %copy-done.1, f32[392,128]{1,0:T(8,128)S(1)} %collective-permute-done.refs_1_, ...), custom_call_target="tpu_custom_call" | custom-call | bytes 25165824 | tf_op jit(solution)/shard_map/nonlinear/pallas_call | solution.py:328
  36.1 1.4 collective-permute-done.3
  37.6 1.6 %collective-permute-start.4 = (f32[3,4,32,128]{3,2,1,0:T(8,128)S(1)}, f32[3,4,32,128]{3,2,1,0:T(8,128)S(1)}, u32[]{:S(2)}, u32[]{:S(2)}) collective-permute-start(f32[3,4,32,128]{3,2,1,0:T(8,128)S(1)} %add.135), channel_id=1, source_target_pairs={{0,2},{1,3},{2,0},{3,1},{4,6},{5,7},{6,4},{7,5},{8,10},{9,11},{10,... | collective-permute-start | bytes 589832 | tf_op jit(solution)/shard_map/ppermute | solution.py:567
  39.2 5.5 %collective-permute-done.4 = f32[3,4,32,128]{3,2,1,0:T(8,128)S(1)} collective-permute-done((f32[3,4,32,128]{3,2,1,0:T(8,128)S(1)}, f32[3,4,32,128]{3,2,1,0:T(8,128)S(1)}, u32[]{:S(2)}, u32[]{:S(2)}) %collective-permute-start.4) | collective-permute-done | bytes 196640 | tf_op jit(solution)/shard_map/ppermute | solution.py:567
  44.7 1.4 collective-permute-done.5.refs_5_.other_ref
  46.2 5.4 %nonlinear.3 = (f32[3,16,32,128]{3,2,1,0:T(8,128)S(1)}, f32[3,4,32,128]{3,2,1,0:T(8,128)S(1)}, f32[3,4,32,128]{3,2,1,0:T(8,128)S(1)}) custom-call(s32[8]{0:T(128)S(1)} %copy-done.2, s32[16,8]{1,0:T(8,128)S(1)} %bitcast.50, f32[4,384,128]{2,1,0:T(8,128)S(1)} %all-to-all-done.refs_0_, bf16[256,384]{1,0:T(8,128)(2,1)S(1)} %maximum_maximum_fusion.refs_4_.refs_1_, ...), custom_call_target="tpu_custom_call" | custom-call | bytes 25165824 | tf_op jit(solution)/shard_map/nonlinear/pallas_call | solution.py:328
  51.5 0.2 collective-permute-start.6
  51.7 1.3 collective-permute-done.6
  53.1 1.6 %collective-permute-start.7 = (f32[3,4,32,128]{3,2,1,0:T(8,128)S(1)}, f32[3,4,32,128]{3,2,1,0:T(8,128)S(1)}, u32[]{:S(2)}, u32[]{:S(2)}) collective-permute-start(f32[3,4,32,128]{3,2,1,0:T(8,128)S(1)} %add.137), channel_id=1, source_target_pairs={{0,2},{1,3},{2,0},{3,1},{4,6},{5,7},{6,4},{7,5},{8,10},{9,11},{10,... | collective-permute-start | bytes 589832 | tf_op jit(solution)/shard_map/ppermute | solution.py:567
  54.6 5.5 %collective-permute-done.7 = f32[3,4,32,128]{3,2,1,0:T(8,128)S(1)} collective-permute-done((f32[3,4,32,128]{3,2,1,0:T(8,128)S(1)}, f32[3,4,32,128]{3,2,1,0:T(8,128)S(1)}, u32[]{:S(2)}, u32[]{:S(2)}) %collective-permute-start.7) | collective-permute-done | bytes 196640 | tf_op jit(solution)/shard_map/ppermute | solution.py:567
  60.2 1.1 outgoing.3
  61.3 5.8 %collective-permute-start.16 = (f32[8,24,128]{2,1,0:T(8,128)S(1)}, f32[8,24,128]{2,1,0:T(8,128)S(1)}, u32[]{:S(2)}, u32[]{:S(2)}) collective-permute-start(f32[8,24,128]{2,1,0:T(8,128)S(1)} %bitcast.66), channel_id=1, source_target_pairs={{0,16},{1,5},{2,18},{3,7},{4,20},{5,1},{6,22},{7,3},{8,24},{9,13},... | collective-permute-start | bytes 294920 | tf_op jit(solution)/shard_map/ppermute | solution.py:561
  67.1 1.5 %collective-permute-start.17 = (f32[8,24,128]{2,1,0:T(8,128)S(1)}, f32[8,24,128]{2,1,0:T(8,128)S(1)}, u32[]{:S(2)}, u32[]{:S(2)}) collective-permute-start(f32[8,24,128]{2,1,0:T(8,128)S(1)} %bitcast.65), channel_id=1, source_target_pairs={{0,4},{1,17},{2,6},{3,19},{4,0},{5,21},{6,2},{7,23},{8,12},{9,25},... | collective-permute-start | bytes 294920 | tf_op jit(solution)/shard_map/ppermute | solution.py:561
  68.6 1.5 %collective-permute-start.19 = (f32[8,24,128]{2,1,0:T(8,128)S(1)}, f32[8,24,128]{2,1,0:T(8,128)S(1)}, u32[]{:S(2)}, u32[]{:S(2)}) collective-permute-start(f32[8,24,128]{2,1,0:T(8,128)S(1)} %bitcast.62), channel_id=1, source_target_pairs={{0,24},{1,9},{2,26},{3,11},{4,28},{5,13},{6,30},{7,15},{8,16},{9,1... | collective-permute-start | bytes 294920 | tf_op jit(solution)/shard_map/ppermute | solution.py:561
  70.1 1.9 %collective-permute-start.20 = (f32[8,24,128]{2,1,0:T(8,128)S(1)}, f32[8,24,128]{2,1,0:T(8,128)S(1)}, u32[]{:S(2)}, u32[]{:S(2)}) collective-permute-start(f32[8,24,128]{2,1,0:T(8,128)S(1)} %bitcast.60), channel_id=1, source_target_pairs={{0,20},{1,13},{2,22},{3,15},{4,16},{5,9},{6,18},{7,11},{8,28},{9,5... | collective-permute-start | bytes 294920 | tf_op jit(solution)/shard_map/ppermute | solution.py:561
  72.0 1.1 outgoing.2
  73.1 1.9 %collective-permute-start.21 = (f32[8,24,128]{2,1,0:T(8,128)S(1)}, f32[8,24,128]{2,1,0:T(8,128)S(1)}, u32[]{:S(2)}, u32[]{:S(2)}) collective-permute-start(f32[8,24,128]{2,1,0:T(8,128)S(1)} %bitcast.59), channel_id=1, source_target_pairs={{0,12},{1,21},{2,14},{3,23},{4,8},{5,17},{6,10},{7,19},{8,4},{9,29... | collective-permute-start | bytes 294920 | tf_op jit(solution)/shard_map/ppermute | solution.py:561
  75.0 1.5 %collective-permute-start.22 = (f32[8,24,128]{2,1,0:T(8,128)S(1)}, f32[8,24,128]{2,1,0:T(8,128)S(1)}, u32[]{:S(2)}, u32[]{:S(2)}) collective-permute-start(f32[8,24,128]{2,1,0:T(8,128)S(1)} %bitcast.58), channel_id=1, source_target_pairs={{0,28},{1,29},{2,30},{3,31},{4,24},{5,25},{6,26},{7,27},{8,20},{9,... | collective-permute-start | bytes 294920 | tf_op jit(solution)/shard_map/ppermute | solution.py:561
  76.5 0.5 collective-permute-done.18.refs_3_
  77.0 0.6 collective-permute-start.9
  77.6 2.6 %collective-permute-start.10 = (f32[8,24,128]{2,1,0:T(8,128)S(1)}, f32[8,24,128]{2,1,0:T(8,128)S(1)}, u32[]{:S(2)}, u32[]{:S(2)}) collective-permute-start(f32[8,24,128]{2,1,0:T(8,128)S(1)} %bitcast.61), channel_id=1, source_target_pairs={{0,4},{1,17},{2,6},{3,19},{4,0},{5,21},{6,2},{7,23},{8,12},{9,25},... | collective-permute-start | bytes 294920 | tf_op jit(solution)/shard_map/ppermute | solution.py:561
  80.1 7.3 %collective-permute-done.20.refs_5_ = f32[8,24,128]{2,1,0:T(8,128)S(1)} collective-permute-done((f32[8,24,128]{2,1,0:T(8,128)S(1)}, f32[8,24,128]{2,1,0:T(8,128)S(1)}, u32[]{:S(2)}, u32[]{:S(2)}) %collective-permute-start.20) | collective-permute-done | bytes 98336 | tf_op jit(solution)/shard_map/ppermute | solution.py:561
  87.5 0.4 collective-permute-start.12
  87.8 3.4 %collective-permute-start.13 = (f32[8,24,128]{2,1,0:T(8,128)S(1)}, f32[8,24,128]{2,1,0:T(8,128)S(1)}, u32[]{:S(2)}, u32[]{:S(2)}) collective-permute-start(f32[8,24,128]{2,1,0:T(8,128)S(1)} %bitcast.55), channel_id=1, source_target_pairs={{0,20},{1,13},{2,22},{3,15},{4,16},{5,9},{6,18},{7,11},{8,28},{9,5... | collective-permute-start | bytes 294920 | tf_op jit(solution)/shard_map/ppermute | solution.py:561
  91.2 1.6 %collective-permute-start.14 = (f32[8,24,128]{2,1,0:T(8,128)S(1)}, f32[8,24,128]{2,1,0:T(8,128)S(1)}, u32[]{:S(2)}, u32[]{:S(2)}) collective-permute-start(f32[8,24,128]{2,1,0:T(8,128)S(1)} %bitcast.54), channel_id=1, source_target_pairs={{0,12},{1,21},{2,14},{3,23},{4,8},{5,17},{6,10},{7,19},{8,4},{9,29... | collective-permute-start | bytes 294920 | tf_op jit(solution)/shard_map/ppermute | solution.py:561
  92.8 1.0 collective-permute-start.15
  93.8 6.0 %solve.2.refs_10_ = f32[8,96,512]{2,1,0:T(8,128)S(1)} custom-call(f32[8,24,128]{2,1,0:T(8,128)S(1)} %bitcast.52, f32[8,24,128]{2,1,0:T(8,128)S(1)} %collective-permute-done.16.refs_1_, f32[8,24,128]{2,1,0:T(8,128)S(1)} %collective-permute-done.17.refs_2_, f32[8,24,128]{2,1,0:T(8,128)S(1)} %collective-permute-done.18.refs_3_, ...), custom_call_target="tpu_custom_call" | custom-call | flops 603979776 | bytes 4194304 | tf_op jit(solution)/shard_map/solve/pallas_call | solution.py:464
  99.9 1.6 %collective-permute-done.13.refs_5_ = f32[8,24,128]{2,1,0:T(8,128)S(1)} collective-permute-done((f32[8,24,128]{2,1,0:T(8,128)S(1)}, f32[8,24,128]{2,1,0:T(8,128)S(1)}, u32[]{:S(2)}, u32[]{:S(2)}) %collective-permute-start.13) | collective-permute-done | bytes 98336 | tf_op jit(solution)/shard_map/ppermute | solution.py:561
  101.5 6.2 %solve.3 = (f32[8,2,24,128]{3,2,1,0:T(8,128)S(1)}, f32[8,2,24,128]{3,2,1,0:T(8,128)S(1)}, f32[8,2,24,128]{3,2,1,0:T(8,128)S(1)}, f32[8,2,24,128]{3,2,1,0:T(8,128...) custom-call(f32[8,24,128]{2,1,0:T(8,128)S(1)} %bitcast.51, ...), custom_call_target="tpu_custom_call" | custom-call | flops 603979776 | bytes 4194304 | tf_op jit(solution)/shard_map/solve/pallas_call | solution.py:464
  107.7 2.2 %collective-permute-start.23 = (f32[8,2,24,128]{3,2,1,0:T(8,128)S(1)}, f32[8,2,24,128]{3,2,1,0:T(8,128)S(1)}, u32[]{:S(2)}, u32[]{:S(2)}) collective-permute-start(f32[8,2,24,128]{3,2,1,0:T(8,128)S(1)} %get-tuple-element.74), channel_id=1, source_target_pairs={{0,16},{1,5},{2,18},{3,7},{4,20},{5,1},{6,22},{7,3},{8,24},{9,13},... | collective-permute-start | bytes 589832 | tf_op jit(solution)/shard_map/ppermute | solution.py:561
  109.9 1.3 collective-permute-start.24
  111.2 0.2 collective-permute-start.25
  111.4 2.3 %collective-permute-start.26 = (f32[8,2,24,128]{3,2,1,0:T(8,128)S(1)}, f32[8,2,24,128]{3,2,1,0:T(8,128)S(1)}, u32[]{:S(2)}, u32[]{:S(2)}) collective-permute-start(f32[8,2,24,128]{3,2,1,0:T(8,128)S(1)} %get-tuple-element.77), channel_id=1, source_target_pairs={{0,24},{1,9},{2,26},{3,11},{4,28},{5,13},{6,30},{7,15},{8,16},{9,1... | collective-permute-start | bytes 589832 | tf_op jit(solution)/shard_map/ppermute | solution.py:561
  113.7 1.2 collective-permute-start.27
  114.9 8.1 %collective-permute-done.23 = f32[8,2,24,128]{3,2,1,0:T(8,128)S(1)} collective-permute-done((f32[8,2,24,128]{3,2,1,0:T(8,128)S(1)}, f32[8,2,24,128]{3,2,1,0:T(8,128)S(1)}, u32[]{:S(2)}, u32[]{:S(2)}) %collective-permute-start.23) | collective-permute-done | bytes 196640 | tf_op jit(solution)/shard_map/ppermute | solution.py:561
  123.0 3.0 %collective-permute-start.29 = (f32[8,2,24,128]{3,2,1,0:T(8,128)S(1)}, f32[8,2,24,128]{3,2,1,0:T(8,128)S(1)}, u32[]{:S(2)}, u32[]{:S(2)}) collective-permute-start(f32[8,2,24,128]{3,2,1,0:T(8,128)S(1)} %get-tuple-element.80), channel_id=1, source_target_pairs={{0,28},{1,29},{2,30},{3,31},{4,24},{5,25},{6,26},{7,27},{8,20},{9,... | collective-permute-start | bytes 589832 | tf_op jit(solution)/shard_map/ppermute | solution.py:561
  126.0 0.7 collective-permute-done.26
  126.7 15.3 %collective-permute-done.27 = f32[8,2,24,128]{3,2,1,0:T(8,128)S(1)} collective-permute-done((f32[8,2,24,128]{3,2,1,0:T(8,128)S(1)}, f32[8,2,24,128]{3,2,1,0:T(8,128)S(1)}, u32[]{:S(2)}, u32[]{:S(2)}) %collective-permute-start.27) | collective-permute-done | bytes 196640 | tf_op jit(solution)/shard_map/ppermute | solution.py:561
  142.1 2.0 %restore.1 = f32[3,4,256,128]{3,2,1,0:T(8,128)} custom-call(f32[384,128]{1,0:T(8,128)S(1)} %bitcast.41, f32[384,128]{1,0:T(8,128)S(1)} %bitcast.42, f32[384,128]{1,0:T(8,128)S(1)} %bitcast.43, f32[384,128]{1,0:T(8,128)S(1)} %bitcast.44, f32[384,128]{1,0:T(8,128)S(1)} %bitcast.45, f32[384,128]{1,0:T(8,128)S(1)} %bitcast.46, f32[384,128]{1,0:T(8,128)S(1)} %bitcast.47, ...), custom_call_target="tpu_custom_call" | custom-call | bytes 3145728 | tf_op jit(solution)/shard_map/restore/pallas_call | solution.py:507
  (68 shorter events, 1.2 us)
Async XLA Ops:
  2.6 27.6 %collective-permute-start.2 = (f32[392,128]{1,0:T(8,128)}, f32[392,128]{1,0:T(8,128)S(1)}, u32[]{:S(2)}, u32[]{:S(2)}) collective-permute-start(f32[392,128]{1,0:T(8,128)} %get-tuple-element.46), channel_id=1, source_target_pairs={{0,16},{1,17},{2,18},{3,19},{8,24},{9,25},{10,26},{11,27},{16,0},{... | collective-permute-start | bytes 602120 | tf_op jit(solution)/shard_map/ppermute | solution.py:561
  6.7 23.6 %collective-permute-start.1 = (f32[392,128]{1,0:T(8,128)}, f32[392,128]{1,0:T(8,128)S(1)}, u32[]{:S(2)}, u32[]{:S(2)}) collective-permute-start(f32[392,128]{1,0:T(8,128)} %get-tuple-element.45), channel_id=1, source_target_pairs={{0,24},{1,9},{2,26},{3,11},{8,16},{9,1},{10,18},{11,3},{16,8},{17,... | collective-permute-start | bytes 602120 | tf_op jit(solution)/shard_map/ppermute | solution.py:561
  8.0 22.2 %collective-permute-start = (f32[392,128]{1,0:T(8,128)}, f32[392,128]{1,0:T(8,128)S(1)}, u32[]{:S(2)}, u32[]{:S(2)}) collective-permute-start(f32[392,128]{1,0:T(8,128)} %get-tuple-element.44), channel_id=1, source_target_pairs={{0,8},{1,25},{2,10},{3,27},{8,0},{9,17},{10,2},{11,19},{16,24},{17... | collective-permute-start | bytes 602120 | tf_op jit(solution)/shard_map/ppermute | solution.py:561
  8.2 37.9 %all-to-all-start = ((f32[4,384,128]{2,1,0:T(8,128)}), f32[4,384,128]{2,1,0:T(8,128)S(1)}, u32[]{:S(2)}, u32[]{:S(2)}) async-start(f32[4,384,128]{2,1,0:T(8,128)} %get-tuple-element.47), calls=%async_computation | async-start | bytes 1572864 | tf_op jit(solution)/shard_map/all_to_all | solution.py:598
  19.2 11.5 %copy-start.1 = (f32[392,128]{1,0:T(8,128)S(1)}, f32[392,128]{1,0:T(8,128)}, u32[]{:S(2)}) copy-start(f32[392,128]{1,0:T(8,128)} %get-tuple-element.43.refs_0_) | copy-start | bytes 602116
  19.2 11.5 %copy-start.2 = (s32[8]{0:T(128)S(1)}, s32[8]{0:T(128)}, u32[]{:S(2)}) copy-start(s32[8]{0:T(128)} %low_ref.7) | copy-start | bytes 100
  28.2 2.0 %copy-start = (bf16[8,512,512]{2,1,0:T(8,128)(2,1)}, bf16[8,512,512]{2,1,0:T(8,128)(2,1)S(1)}, u32[]{:S(2)}) copy-start(bf16[8,512,512]{2,1,0:T(8,128)(2,1)S(1)} %get-tuple-element.62.refs_8_) | copy-start | bytes 12582916
  36.1 1.5 %collective-permute-start.3 = (f32[3,4,32,128]{3,2,1,0:T(8,128)S(1)}, f32[3,4,32,128]{3,2,1,0:T(8,128)S(1)}, u32[]{:S(2)}, u32[]{:S(2)}) collective-permute-start(f32[3,4,32,128]{3,2,1,0:T(8,128)S(1)} %get-tuple-element.50), channel_id=1, source_target_pairs={{0,1},{1,0},{2,3},{3,2},{4,5},{5,4},{6,7},{7,6},{8,9},{9,8},{10,11... | collective-permute-start | bytes 589832 | tf_op jit(solution)/shard_map/ppermute | solution.py:567
  37.6 7.0 %collective-permute-start.4 = (f32[3,4,32,128]{3,2,1,0:T(8,128)S(1)}, f32[3,4,32,128]{3,2,1,0:T(8,128)S(1)}, u32[]{:S(2)}, u32[]{:S(2)}) collective-permute-start(f32[3,4,32,128]{3,2,1,0:T(8,128)S(1)} %add.135), channel_id=1, source_target_pairs={{0,2},{1,3},{2,0},{3,1},{4,6},{5,7},{6,4},{7,5},{8,10},{9,11},{10,... | collective-permute-start | bytes 589832 | tf_op jit(solution)/shard_map/ppermute | solution.py:567
  44.6 1.5 %collective-permute-start.5 = (f32[3,4,32,128]{3,2,1,0:T(8,128)S(1)}, f32[3,4,32,128]{3,2,1,0:T(8,128)S(1)}, u32[]{:S(2)}, u32[]{:S(2)}) collective-permute-start(f32[3,4,32,128]{3,2,1,0:T(8,128)S(1)} %add.136.kept_ref), channel_id=1, source_target_pairs={{0,1},{1,0},{2,3},{3,2},{4,5},{5,4},{6,7},{7,6},{8,9},{9,8},{10,11... | collective-permute-start | bytes 589832 | tf_op jit(solution)/shard_map/ppermute | solution.py:567
  51.5 1.5 %collective-permute-start.6 = (f32[3,4,32,128]{3,2,1,0:T(8,128)S(1)}, f32[3,4,32,128]{3,2,1,0:T(8,128)S(1)}, u32[]{:S(2)}, u32[]{:S(2)}) collective-permute-start(f32[3,4,32,128]{3,2,1,0:T(8,128)S(1)} %get-tuple-element.53), channel_id=1, source_target_pairs={{0,1},{1,0},{2,3},{3,2},{4,5},{5,4},{6,7},{7,6},{8,9},{9,8},{10,11... | collective-permute-start | bytes 589832 | tf_op jit(solution)/shard_map/ppermute | solution.py:567
  53.1 7.0 %collective-permute-start.7 = (f32[3,4,32,128]{3,2,1,0:T(8,128)S(1)}, f32[3,4,32,128]{3,2,1,0:T(8,128)S(1)}, u32[]{:S(2)}, u32[]{:S(2)}) collective-permute-start(f32[3,4,32,128]{3,2,1,0:T(8,128)S(1)} %add.137), channel_id=1, source_target_pairs={{0,2},{1,3},{2,0},{3,1},{4,6},{5,7},{6,4},{7,5},{8,10},{9,11},{10,... | collective-permute-start | bytes 589832 | tf_op jit(solution)/shard_map/ppermute | solution.py:567
  60.1 10.0 %collective-permute-start.8 = (f32[3,4,32,128]{3,2,1,0:T(8,128)S(1)}, f32[3,4,32,128]{3,2,1,0:T(8,128)S(1)}, u32[]{:S(2)}, u32[]{:S(2)}) collective-permute-start(f32[3,4,32,128]{3,2,1,0:T(8,128)S(1)} %add.138.kept_ref), channel_id=1, source_target_pairs={{0,1},{1,0},{2,3},{3,2},{4,5},{5,4},{6,7},{7,6},{8,9},{9,8},{10,11... | collective-permute-start | bytes 589832 | tf_op jit(solution)/shard_map/ppermute | solution.py:567
  61.3 11.8 %collective-permute-start.16 = (f32[8,24,128]{2,1,0:T(8,128)S(1)}, f32[8,24,128]{2,1,0:T(8,128)S(1)}, u32[]{:S(2)}, u32[]{:S(2)}) collective-permute-start(f32[8,24,128]{2,1,0:T(8,128)S(1)} %bitcast.66), channel_id=1, source_target_pairs={{0,16},{1,5},{2,18},{3,7},{4,20},{5,1},{6,22},{7,3},{8,24},{9,13},... | collective-permute-start | bytes 294920 | tf_op jit(solution)/shard_map/ppermute | solution.py:561
  67.1 8.0 %collective-permute-start.17 = (f32[8,24,128]{2,1,0:T(8,128)S(1)}, f32[8,24,128]{2,1,0:T(8,128)S(1)}, u32[]{:S(2)}, u32[]{:S(2)}) collective-permute-start(f32[8,24,128]{2,1,0:T(8,128)S(1)} %bitcast.65), channel_id=1, source_target_pairs={{0,4},{1,17},{2,6},{3,19},{4,0},{5,21},{6,2},{7,23},{8,12},{9,25},... | collective-permute-start | bytes 294920 | tf_op jit(solution)/shard_map/ppermute | solution.py:561
  68.6 8.4 %collective-permute-start.18 = (f32[8,24,128]{2,1,0:T(8,128)S(1)}, f32[8,24,128]{2,1,0:T(8,128)S(1)}, u32[]{:S(2)}, u32[]{:S(2)}) collective-permute-start(f32[8,24,128]{2,1,0:T(8,128)S(1)} %bitcast.64), channel_id=1, source_target_pairs={{0,8},{1,25},{2,10},{3,27},{4,12},{5,29},{6,14},{7,31},{8,0},{9,17... | collective-permute-start | bytes 294920 | tf_op jit(solution)/shard_map/ppermute | solution.py:561
  68.6 9.0 %collective-permute-start.19 = (f32[8,24,128]{2,1,0:T(8,128)S(1)}, f32[8,24,128]{2,1,0:T(8,128)S(1)}, u32[]{:S(2)}, u32[]{:S(2)}) collective-permute-start(f32[8,24,128]{2,1,0:T(8,128)S(1)} %bitcast.62), channel_id=1, source_target_pairs={{0,24},{1,9},{2,26},{3,11},{4,28},{5,13},{6,30},{7,15},{8,16},{9,1... | collective-permute-start | bytes 294920 | tf_op jit(solution)/shard_map/ppermute | solution.py:561
  70.1 17.3 %collective-permute-start.20 = (f32[8,24,128]{2,1,0:T(8,128)S(1)}, f32[8,24,128]{2,1,0:T(8,128)S(1)}, u32[]{:S(2)}, u32[]{:S(2)}) collective-permute-start(f32[8,24,128]{2,1,0:T(8,128)S(1)} %bitcast.60), channel_id=1, source_target_pairs={{0,20},{1,13},{2,22},{3,15},{4,16},{5,9},{6,18},{7,11},{8,28},{9,5... | collective-permute-start | bytes 294920 | tf_op jit(solution)/shard_map/ppermute | solution.py:561
  73.1 14.4 %collective-permute-start.21 = (f32[8,24,128]{2,1,0:T(8,128)S(1)}, f32[8,24,128]{2,1,0:T(8,128)S(1)}, u32[]{:S(2)}, u32[]{:S(2)}) collective-permute-start(f32[8,24,128]{2,1,0:T(8,128)S(1)} %bitcast.59), channel_id=1, source_target_pairs={{0,12},{1,21},{2,14},{3,23},{4,8},{5,17},{6,10},{7,19},{8,4},{9,29... | collective-permute-start | bytes 294920 | tf_op jit(solution)/shard_map/ppermute | solution.py:561
  75.0 12.8 %collective-permute-start.22 = (f32[8,24,128]{2,1,0:T(8,128)S(1)}, f32[8,24,128]{2,1,0:T(8,128)S(1)}, u32[]{:S(2)}, u32[]{:S(2)}) collective-permute-start(f32[8,24,128]{2,1,0:T(8,128)S(1)} %bitcast.58), channel_id=1, source_target_pairs={{0,28},{1,29},{2,30},{3,31},{4,24},{5,25},{6,26},{7,27},{8,20},{9,... | collective-permute-start | bytes 294920 | tf_op jit(solution)/shard_map/ppermute | solution.py:561
  77.0 14.2 %collective-permute-start.9 = (f32[8,24,128]{2,1,0:T(8,128)S(1)}, f32[8,24,128]{2,1,0:T(8,128)S(1)}, u32[]{:S(2)}, u32[]{:S(2)}) collective-permute-start(f32[8,24,128]{2,1,0:T(8,128)S(1)} %bitcast.63), channel_id=1, source_target_pairs={{0,16},{1,5},{2,18},{3,7},{4,20},{5,1},{6,22},{7,3},{8,24},{9,13},... | collective-permute-start | bytes 294920 | tf_op jit(solution)/shard_map/ppermute | solution.py:561
  77.6 15.2 %collective-permute-start.10 = (f32[8,24,128]{2,1,0:T(8,128)S(1)}, f32[8,24,128]{2,1,0:T(8,128)S(1)}, u32[]{:S(2)}, u32[]{:S(2)}) collective-permute-start(f32[8,24,128]{2,1,0:T(8,128)S(1)} %bitcast.61), channel_id=1, source_target_pairs={{0,4},{1,17},{2,6},{3,19},{4,0},{5,21},{6,2},{7,23},{8,12},{9,25},... | collective-permute-start | bytes 294920 | tf_op jit(solution)/shard_map/ppermute | solution.py:561
  87.5 12.4 %collective-permute-start.11 = (f32[8,24,128]{2,1,0:T(8,128)S(1)}, f32[8,24,128]{2,1,0:T(8,128)S(1)}, u32[]{:S(2)}, u32[]{:S(2)}) collective-permute-start(f32[8,24,128]{2,1,0:T(8,128)S(1)} %bitcast.57), channel_id=1, source_target_pairs={{0,8},{1,25},{2,10},{3,27},{4,12},{5,29},{6,14},{7,31},{8,0},{9,17... | collective-permute-start | bytes 294920 | tf_op jit(solution)/shard_map/ppermute | solution.py:561
  87.5 12.4 %collective-permute-start.12 = (f32[8,24,128]{2,1,0:T(8,128)S(1)}, f32[8,24,128]{2,1,0:T(8,128)S(1)}, u32[]{:S(2)}, u32[]{:S(2)}) collective-permute-start(f32[8,24,128]{2,1,0:T(8,128)S(1)} %bitcast.56), channel_id=1, source_target_pairs={{0,24},{1,9},{2,26},{3,11},{4,28},{5,13},{6,30},{7,15},{8,16},{9,1... | collective-permute-start | bytes 294920 | tf_op jit(solution)/shard_map/ppermute | solution.py:561
  87.8 13.6 %collective-permute-start.13 = (f32[8,24,128]{2,1,0:T(8,128)S(1)}, f32[8,24,128]{2,1,0:T(8,128)S(1)}, u32[]{:S(2)}, u32[]{:S(2)}) collective-permute-start(f32[8,24,128]{2,1,0:T(8,128)S(1)} %bitcast.55), channel_id=1, source_target_pairs={{0,20},{1,13},{2,22},{3,15},{4,16},{5,9},{6,18},{7,11},{8,28},{9,5... | collective-permute-start | bytes 294920 | tf_op jit(solution)/shard_map/ppermute | solution.py:561
  91.2 10.3 %collective-permute-start.14 = (f32[8,24,128]{2,1,0:T(8,128)S(1)}, f32[8,24,128]{2,1,0:T(8,128)S(1)}, u32[]{:S(2)}, u32[]{:S(2)}) collective-permute-start(f32[8,24,128]{2,1,0:T(8,128)S(1)} %bitcast.54), channel_id=1, source_target_pairs={{0,12},{1,21},{2,14},{3,23},{4,8},{5,17},{6,10},{7,19},{8,4},{9,29... | collective-permute-start | bytes 294920 | tf_op jit(solution)/shard_map/ppermute | solution.py:561
  92.8 8.7 %collective-permute-start.15 = (f32[8,24,128]{2,1,0:T(8,128)S(1)}, f32[8,24,128]{2,1,0:T(8,128)S(1)}, u32[]{:S(2)}, u32[]{:S(2)}) collective-permute-start(f32[8,24,128]{2,1,0:T(8,128)S(1)} %bitcast.53), channel_id=1, source_target_pairs={{0,28},{1,29},{2,30},{3,31},{4,24},{5,25},{6,26},{7,27},{8,20},{9,... | collective-permute-start | bytes 294920 | tf_op jit(solution)/shard_map/ppermute | solution.py:561
  107.7 15.3 %collective-permute-start.23 = (f32[8,2,24,128]{3,2,1,0:T(8,128)S(1)}, f32[8,2,24,128]{3,2,1,0:T(8,128)S(1)}, u32[]{:S(2)}, u32[]{:S(2)}) collective-permute-start(f32[8,2,24,128]{3,2,1,0:T(8,128)S(1)} %get-tuple-element.74), channel_id=1, source_target_pairs={{0,16},{1,5},{2,18},{3,7},{4,20},{5,1},{6,22},{7,3},{8,24},{9,13},... | collective-permute-start | bytes 589832 | tf_op jit(solution)/shard_map/ppermute | solution.py:561
  109.9 13.1 %collective-permute-start.24 = (f32[8,2,24,128]{3,2,1,0:T(8,128)S(1)}, f32[8,2,24,128]{3,2,1,0:T(8,128)S(1)}, u32[]{:S(2)}, u32[]{:S(2)}) collective-permute-start(f32[8,2,24,128]{3,2,1,0:T(8,128)S(1)} %get-tuple-element.75), channel_id=1, source_target_pairs={{0,4},{1,17},{2,6},{3,19},{4,0},{5,21},{6,2},{7,23},{8,12},{9,25},... | collective-permute-start | bytes 589832 | tf_op jit(solution)/shard_map/ppermute | solution.py:561
  111.2 14.8 %collective-permute-start.25 = (f32[8,2,24,128]{3,2,1,0:T(8,128)S(1)}, f32[8,2,24,128]{3,2,1,0:T(8,128)S(1)}, u32[]{:S(2)}, u32[]{:S(2)}) collective-permute-start(f32[8,2,24,128]{3,2,1,0:T(8,128)S(1)} %get-tuple-element.76), channel_id=1, source_target_pairs={{0,8},{1,25},{2,10},{3,27},{4,12},{5,29},{6,14},{7,31},{8,0},{9,17... | collective-permute-start | bytes 589832 | tf_op jit(solution)/shard_map/ppermute | solution.py:561
  111.4 15.4 %collective-permute-start.26 = (f32[8,2,24,128]{3,2,1,0:T(8,128)S(1)}, f32[8,2,24,128]{3,2,1,0:T(8,128)S(1)}, u32[]{:S(2)}, u32[]{:S(2)}) collective-permute-start(f32[8,2,24,128]{3,2,1,0:T(8,128)S(1)} %get-tuple-element.77), channel_id=1, source_target_pairs={{0,24},{1,9},{2,26},{3,11},{4,28},{5,13},{6,30},{7,15},{8,16},{9,1... | collective-permute-start | bytes 589832 | tf_op jit(solution)/shard_map/ppermute | solution.py:561
  113.7 28.4 %collective-permute-start.27 = (f32[8,2,24,128]{3,2,1,0:T(8,128)S(1)}, f32[8,2,24,128]{3,2,1,0:T(8,128)S(1)}, u32[]{:S(2)}, u32[]{:S(2)}) collective-permute-start(f32[8,2,24,128]{3,2,1,0:T(8,128)S(1)} %get-tuple-element.78), channel_id=1, source_target_pairs={{0,20},{1,13},{2,22},{3,15},{4,16},{5,9},{6,18},{7,11},{8,28},{9,5... | collective-permute-start | bytes 589832 | tf_op jit(solution)/shard_map/ppermute | solution.py:561
  123.0 19.1 %collective-permute-start.28 = (f32[8,2,24,128]{3,2,1,0:T(8,128)S(1)}, f32[8,2,24,128]{3,2,1,0:T(8,128)S(1)}, u32[]{:S(2)}, u32[]{:S(2)}) collective-permute-start(f32[8,2,24,128]{3,2,1,0:T(8,128)S(1)} %get-tuple-element.79), channel_id=1, source_target_pairs={{0,12},{1,21},{2,14},{3,23},{4,8},{5,17},{6,10},{7,19},{8,4},{9,29... | collective-permute-start | bytes 589832 | tf_op jit(solution)/shard_map/ppermute | solution.py:561
  123.0 19.1 %collective-permute-start.29 = (f32[8,2,24,128]{3,2,1,0:T(8,128)S(1)}, f32[8,2,24,128]{3,2,1,0:T(8,128)S(1)}, u32[]{:S(2)}, u32[]{:S(2)}) collective-permute-start(f32[8,2,24,128]{3,2,1,0:T(8,128)S(1)} %get-tuple-element.80), channel_id=1, source_target_pairs={{0,28},{1,29},{2,30},{3,31},{4,24},{5,25},{6,26},{7,27},{8,20},{9,... | collective-permute-start | bytes 589832 | tf_op jit(solution)/shard_map/ppermute | solution.py:561

commit v6 on v5

--- a/solution.py
+++ b/solution.py
@@ -2,6 +2,7 @@
 
 import jax
 import jax.numpy as jnp
+import numpy as np
 from jax import lax
 from jax.experimental import pallas as pl
 from jax.experimental.pallas import tpu as pltpu
@@ -130,7 +131,7 @@
 
 def step_at(count, position):
     even, odd = steps_of(count)
-    return jnp.where(lax.axis_index("real") % 2 == 0, even[position], odd[position])
+    return jnp.where((lax.axis_index("real") & 1) == 0, even[position], odd[position])
 
 
 def cost(size):
@@ -188,46 +189,62 @@
     return out[:kx_count], out[kx_count:]
 
 
-def split_matrix_kernel(matrix_ref, top_ref, rest_ref, mark_ref, turned, *, pieces, kx_count):
-    ht_count, heights, width = turned.shape
-    rows = width // (pieces * kx_count)
-    owners = kx_count * ht_count
-    own_kx, own_ht = (lax.axis_index("kx"), lax.axis_index("ht"))
-    for h in range(ht_count):
-        turned[h] = matrix_ref[0, h * width : (h + 1) * width, :].T
-    for position in range(owners):
-        step = step_at(owners, position)
-        kx, ht = (own_kx ^ (step // ht_count), own_ht ^ (step % ht_count))
-        for piece in range(pieces):
-            source = pl.multiple_of(((ht * pieces + piece) * kx_count + kx) * rows, rows)
-            start = (piece * owners + position) * rows
-            for h in range(ht_count):
-                place = (0, slice(start, start + rows), slice(h * width, (h + 1) * width))
-                value = turned[h, pl.ds(source, rows), :]
-                top_ref[place], rest_ref[place] = two_parts(value)
-    mark_ref[...] = jnp.zeros_like(mark_ref)
-
-
-def split_matrix(helmholtz, pieces, kx_count, ht_count):
-    slots, heights, _ = helmholtz.shape
-    spec = pl.BlockSpec((1, heights, heights), lambda s: (s, 0, 0))
-    shape = jax.ShapeDtypeStruct(helmholtz.shape, jnp.bfloat16)
-    return pl.pallas_call(
-        functools.partial(split_matrix_kernel, pieces=pieces, kx_count=kx_count),
-        out_shape=(shape, shape, jax.ShapeDtypeStruct((8, LANES), jnp.float32)),
-        grid=(slots,),
-        in_specs=[spec],
-        out_specs=(spec, spec, pl.BlockSpec((8, LANES), lambda s: (0, 0))),
-        scratch_shapes=[pltpu.VMEM((ht_count, heights, heights // ht_count), jnp.float32)],
+def tables_kernel(owner_ref, top_ref, rest_ref, first_ref, back_ref, order_ref, slot_ref):
+    columns = slot_ref.shape[1]
+    modes = columns // 2
+    lane = lax.broadcasted_iota(jnp.int32, (8, columns), 1)
+    mode = jnp.zeros((8, columns), jnp.int32)
+    for slot in range(modes):
+        mode = jnp.where(lane % modes == slot, owner_ref[slot], mode)
+    slot_ref[...] = mode
+    wanted = 2 * mode + lane // modes
+    row = lax.broadcasted_iota(jnp.int32, (columns, columns), 0)
+    chosen = (row == wanted[:1]).astype(jnp.float32)
+    select = chosen.astype(jnp.bfloat16)
+    points = top_ref.shape[1]
+    for half in range(2):
+        rows = slice(half * columns, (half + 1) * columns)
+        first_ref[rows, :points] = top_ref[...]
+        first_ref[rows, points:] = select
+        order_ref[rows] = chosen.T.astype(jnp.bfloat16)
+    for index, table_ref in enumerate((top_ref, rest_ref)):
+        back = dot(table_ref[...], select, ((0,), (0,))) * (2.0 * modes / points)
+        back_ref[:, index * columns : (index + 1) * columns] = back.astype(jnp.bfloat16)
+
+
+def spanwise_constants(columns, points):
+    mode = np.arange(columns) // 2
+    phase = 2.0 * np.pi * ((mode[:, None] * np.arange(points)[None, :]) % points) / points
+    forward = np.where(np.arange(columns)[:, None] % 2 == 0, np.cos(phase), -np.sin(phase))
+    forward = (forward / np.sqrt(columns // 2)).astype(np.float32)
+    top = forward.astype(jnp.bfloat16)
+    rest = (forward - top.astype(np.float32)).astype(jnp.bfloat16)
+    return jnp.asarray(top), jnp.asarray(rest)
+
+
+def slot_tables(owner_map, columns):
+    points = 2 * columns
+    top, rest = spanwise_constants(columns, points)
+    first, back, order, slot_modes = pl.pallas_call(
+        tables_kernel,
+        out_shape=(
+            jax.ShapeDtypeStruct((2 * columns, points + columns), jnp.bfloat16),
+            jax.ShapeDtypeStruct((points, 2 * columns), jnp.bfloat16),
+            jax.ShapeDtypeStruct((2 * columns, columns), jnp.bfloat16),
+            jax.ShapeDtypeStruct((8, columns), jnp.int32),
+        ),
+        in_specs=[SMEM, VMEM, VMEM],
+        out_specs=(VMEM,) * 4,
         compiler_params=params(),
-        cost_estimate=cost(8 * helmholtz.size),
-        name="split_matrix",
-    )(helmholtz)
-
-
-def nonlinear_kernel(low_ref, near_ref, *refs):
+        cost_estimate=cost(16 * points * columns),
+        name="tables",
+    )(owner_map, top, rest)
+    return (first, rest, back), order, slot_modes
+
+
+def nonlinear_kernel(low_ref, near_ref, count_ref, *refs):
     block_refs, refs = (refs[:-12], refs[-12:])
-    first_ref, second_ref, back_ref, mask_ref, _, slotted_ref, kept_ref, sent_ref = refs[:8]
+    first_ref, second_ref, back_ref, slot_ref, _, slotted_ref, kept_ref, sent_ref = refs[:8]
     physical, products, sums, high_ref = refs[8:]
     components, modes, rows, columns = slotted_ref.shape
     if len(block_refs) > 1:
@@ -239,7 +256,7 @@
         block_refs = [block_refs[0].at[index] for index in range(bands)]
     points, band_modes = (physical.shape[3], modes // bands)
     members, highs = (sums.shape[1], products.shape[1])
-    odd = lax.axis_index("real") % 2 == 1
+    odd = (lax.axis_index("real") & 1) == 1
     found = jnp.int32(0)
     for mode in range(modes):
         is_low = jnp.int32(0)
@@ -298,21 +315,19 @@
 
     lax.fori_loop(0, (rows // 8) * (points // LANES), pairs, 0)
 
-    def inverse(fields, start):
+    def inverse(fields):
         top, rest = two_parts(fields)
-        both = dot(top, back_ref[:, start : start + 2 * columns])
-        return (
-            both[:, :columns] + both[:, columns:]
-            + dot(rest, back_ref[:, start : start + columns])
-        )
+        both = dot(top, back_ref[...])
+        return both[:, :columns] + both[:, columns:] + dot(rest, back_ref[:, :columns])
 
     def finish(component, carry):
-        forcing = inverse(products[component].reshape(highs * rows, points), 0)
+        forcing = inverse(products[component].reshape(highs * rows, points))
         forcing = forcing.reshape(highs, rows, columns)
         for index in range(highs):
             mode = high_ref[index]
-            slotted_ref[component, mode] += forcing[index] * mask_ref[mode]
-        stress = inverse(sums[component].reshape(members * rows, points), 2 * columns)
+            active = slot_ref[:1] < count_ref[mode]
+            slotted_ref[component, mode] += jnp.where(active, forcing[index] * dt_step, 0.0)
+        stress = inverse(sums[component].reshape(members * rows, points))
         stress = stress.reshape(2, members // 2, rows, columns)
         kept_ref[component] = jnp.where(odd, stress[1], stress[0])
         sent_ref[component] = jnp.where(odd, stress[0], stress[1])
@@ -321,7 +336,7 @@
     lax.fori_loop(0, components, finish, 0)
 
 
-def nonlinear(blocks, shape, low_index, neighbours, tables, mask, after):
+def nonlinear(blocks, shape, low_index, neighbours, mode_counts, tables, slot_modes, after):
     components, modes, rows, columns = shape
     members, points = (low_index.shape[0], 2 * columns)
     highs = modes - members
@@ -332,7 +347,7 @@
             jax.ShapeDtypeStruct((components, members // 2, rows, columns), jnp.float32),
             jax.ShapeDtypeStruct((components, members // 2, rows, columns), jnp.float32),
         ),
-        in_specs=[SMEM, SMEM] + [VMEM] * (len(blocks) + 4) + [pl.BlockSpec(memory_space=pl.ANY)],
+        in_specs=[SMEM] * 3 + [VMEM] * (len(blocks) + 4) + [pl.BlockSpec(memory_space=pl.ANY)],
         out_specs=(VMEM, VMEM, VMEM),
         scratch_shapes=[
             pltpu.VMEM((components, modes, rows, points), jnp.float32),
@@ -343,60 +358,71 @@
         compiler_params=params(),
         cost_estimate=cost(8 * components * modes * rows * points * members),
         name="nonlinear",
-    )(low_index, neighbours, *blocks, *tables, mask, after)
+    )(low_index, neighbours, mode_counts, *blocks, *tables, slot_modes, after)
 
 
 def outgoing_kernel(
-    low_ref, slotted_ref, kept_ref, other_ref, mask_ref, *refs, groups, band_modes
+    low_ref, count_ref, slotted_ref, kept_ref, other_ref, slot_ref, *refs,
+    groups, band_modes, owners, scale
 ):
-    out_refs, full = (refs[:-1], refs[-1])
+    out_refs, (full, turned) = (refs[:-2], refs[-2:])
     components, modes, rows, columns = slotted_ref.shape
-    half, owners = (kept_ref.shape[1], len(out_refs))
-    slots = columns // 2 // owners
-    per_slot = out_refs[0].shape[0] // slots
+    half, slots = (kept_ref.shape[1], columns // 2 // owners)
+    per_slot = out_refs[0].shape[0] * len(out_refs) // (columns // 2)
+    own = lax.axis_index("real") & 1
     full[...] = slotted_ref[...]
-    position = lax.broadcasted_iota(jnp.int32, (rows, columns), 1) // slots % owners
-    own = lax.axis_index("real") % 2
-    upper = (own == 1) & (position % 2 == 1) & (position < owners - 1)
-    lower = (own == 1) & (position % 2 == 0) & (position > 0)
     for member in range(half):
         for part_ref, start in ((kept_ref, own * half), (other_ref, (1 - own) * half)):
             mode = low_ref[start + member]
+            active = slot_ref[:1] < count_ref[mode]
             for c in range(components):
-                stress = part_ref[c, member]
-                stress = jnp.where(
-                    upper, pltpu.roll(stress, columns - slots, 1),
-                    jnp.where(lower, pltpu.roll(stress, slots, 1), stress),
-                )
-                full[c, mode] += stress * mask_ref[mode]
+                full[c, mode] += jnp.where(active, part_ref[c, member] * scale, 0.0)
     inner = modes // groups
+    if len(out_refs) > 1:
+        me = lax.axis_index("kx") * lax.axis_size("ht") + lax.axis_index("ht")
+        targets = [me ^ step_at(owners, position) for position in range(owners)]
     for c in range(components):
         for part in range(inner):
             tile = jnp.concatenate([full[c, part + inner * g] for g in range(groups)], axis=0)
-            turned = tile.T
             band_low, band_mode = (part // band_modes, part % band_modes)
+            if len(out_refs) > 1:
+                turned[...] = tile.T
+            else:
+                value = tile.T
             for p in range(2):
                 row = ((band_low * 2 + p) * components + c) * band_modes + band_mode
-                for owner in range(owners):
-                    start = (p * owners + owner) * slots
-                    out_refs[owner][pl.ds(row, slots, stride=per_slot), :] = turned[
-                        start : start + slots
+                if len(out_refs) == 1:
+                    out_refs[0][pl.ds(row, columns // 2, stride=per_slot), :] = value[
+                        p * (columns // 2) : (p + 1) * (columns // 2)
                     ]
-
-
-def outgoing(slotted, kept, other, low_index, mask, groups, band_modes, owners):
+                    continue
+                for out_ref, target in zip(out_refs, targets):
+                    start = pl.multiple_of((p * owners + target) * slots, slots)
+                    out_ref[pl.ds(row, slots, stride=per_slot), :] = turned[pl.ds(start, slots)]
+
+
+def outgoing(
+    slotted, kept, other, low_index, mode_counts, slot_modes, groups, band_modes, owners,
+    realizations, separate,
+):
     components, modes, rows, columns = slotted.shape
-    total = (columns // 2 // owners) * (modes // groups) * 2 * components
+    total, lanes = ((columns // 2) * (modes // groups) * 2 * components, groups * rows)
+    count = owners if separate else 1
     return pl.pallas_call(
-        functools.partial(outgoing_kernel, groups=groups, band_modes=band_modes),
-        out_shape=(jax.ShapeDtypeStruct((total, groups * rows), jnp.float32),) * owners,
-        in_specs=[SMEM, VMEM, VMEM, VMEM, VMEM],
-        out_specs=(VMEM,) * owners,
-        scratch_shapes=[pltpu.VMEM(slotted.shape, jnp.float32)],
+        functools.partial(
+            outgoing_kernel, groups=groups, band_modes=band_modes, owners=owners,
+            scale=dt_step / realizations,
+        ),
+        out_shape=(jax.ShapeDtypeStruct((total // count, lanes), jnp.float32),) * count,
+        in_specs=[SMEM, SMEM] + [VMEM] * 4,
+        out_specs=(VMEM,) * count,
+        scratch_shapes=[
+            pltpu.VMEM(slotted.shape, jnp.float32), pltpu.VMEM((columns, lanes), jnp.float32)
+        ],
         compiler_params=params(),
         cost_estimate=cost(8 * slotted.size),
         name="outgoing",
-    )(low_index, slotted, kept, other, mask)
+    )(low_index, mode_counts, slotted, kept, other, slot_modes)
 
 
 def regroup(blocks, rows):
@@ -416,85 +442,90 @@
     return blocks
 
 
-def solve_kernel(*refs, groups, kx_count, ht_count, started, last):
+def solve_kernel(*refs, groups, kx_count, ht_count, pieces):
     owners = kx_count * ht_count
-    block_refs, (top_ref, rest_ref), refs = (
-        refs[:owners], refs[owners : owners + 2], refs[owners + 2 :]
-    )
-    rows = LANES // groups
-    tiles = []
-    for first in range(0, owners, groups):
-        blocks = [block_refs[first + g][0] for g in range(groups)]
-        tiles.append(jnp.concatenate(regroup(blocks, rows), axis=0))
-    top, rest = two_parts(jnp.concatenate(tiles, axis=1))
-    count = top.shape[0]
-    both = dot(jnp.concatenate([top, rest], axis=0), top_ref[0])
-    solved = both[:count] + both[count:] + dot(top, rest_ref[0])
-    if started:
-        solved, refs = (solved + refs[0][0], refs[1:])
-    if not last:
-        refs[0][0] = solved
-        return
-    out_refs, full = (refs[:owners], refs[owners])
-    for tile in range(full.shape[0]):
-        full[tile] = solved[:, tile * LANES : (tile + 1) * LANES]
+    first_ref, refs = (refs[0], refs[1:])
+    count = owners * (pieces - 1)
+    block_refs, matrix_ref, refs = (refs[:count], refs[count], refs[count + 1 :])
+    out_refs, (matrices, arrived, ordered, full) = (refs[:owners], refs[owners:])
+    slots, heights = (matrix_ref.shape[0], matrix_ref.shape[1])
+    copies = [
+        pltpu.make_async_copy(matrix_ref.at[s], matrices.at[s], arrived.at[s])
+        for s in range(slots)
+    ]
+    for copy in copies:
+        copy.start()
     own_kx, own_ht = (lax.axis_index("kx"), lax.axis_index("ht"))
-    lane_tiles, per_band = out_refs[0].shape[1:3]
-    for position, out_ref in enumerate(out_refs):
+    partners = []
+    for position in range(owners):
         step = step_at(owners, position)
-        kx, ht = (own_kx ^ (step // ht_count), own_ht ^ (step % ht_count))
-        band = pl.ds(pl.multiple_of(kx * per_band, 8), per_band)
-        for tile in range(lane_tiles):
-            out_ref[0, tile] = full[ht * lane_tiles + tile, band]
-
-
-def solve(blocks, matrices, piece, pieces, partial, groups, kx_count, ht_count):
-    slots, per_slot, lanes = blocks[0].shape
-    heights, last = (matrices[0].shape[2], piece == pieces - 1)
-    count, owners = (per_slot * groups, kx_count * ht_count)
-    whole = pl.BlockSpec((1, count, heights), lambda s: (s, 0, 0))
-    if last:
-        shape = (slots, heights // ht_count // LANES, count // kx_count, LANES)
-        out_shape = (jax.ShapeDtypeStruct(shape, jnp.float32),) * owners
-        out_specs = (pl.BlockSpec((1,) + shape[1:], lambda s: (s, 0, 0, 0)),) * owners
-        scratch = [pltpu.VMEM((heights // LANES, count, LANES), jnp.float32)]
-    else:
-        out_shape = jax.ShapeDtypeStruct((slots, count, heights), jnp.float32)
-        out_specs, scratch = (whole, [])
+        partners.append((own_kx ^ (step // ht_count), own_ht ^ (step % ht_count)))
+    for index, block_ref in enumerate(block_refs):
+        kx, ht = partners[index % owners]
+        ordered[index // owners, kx * ht_count + ht] = block_ref[...]
+    rows, (lane_tiles, per_band) = (LANES // groups, out_refs[0].shape[1:3])
+    for s in range(slots):
+        tiles = []
+        for h in range(ht_count):
+            for piece in range(pieces):
+                source = first_ref if piece == 0 else ordered.at[piece - 1]
+                for first in range(0, kx_count, groups):
+                    blocks = [source[(first + g) * ht_count + h, s] for g in range(groups)]
+                    tiles.append(jnp.concatenate(regroup(blocks, rows), axis=0))
+        top, rest = two_parts(jnp.concatenate(tiles, axis=1))
+        count = top.shape[0]
+        copies[s].wait()
+        matrix_top, matrix_rest = two_parts(matrices[s])
+        last = ((1,), (1,))
+        both = dot(matrix_top, jnp.concatenate([top, rest], axis=0), last)
+        solved = both[:, :count] + both[:, count:] + dot(matrix_rest, top, last)
+        for tile in range(heights // LANES):
+            full[s % 2, tile] = solved[tile * LANES : (tile + 1) * LANES].T
+        for out_ref, (kx, ht) in zip(out_refs, partners):
+            band = pl.ds(pl.multiple_of(kx * per_band, 8), per_band)
+            for tile in range(lane_tiles):
+                out_ref[s, tile] = full[s % 2, ht * lane_tiles + tile, band]
+
+
+def solve(first, blocks, helmholtz, pieces, groups, kx_count, ht_count):
+    owners, slots, per_slot, lanes = first.shape
+    heights, count = (helmholtz.shape[1], per_slot * groups)
+    shape = (slots, heights // ht_count // LANES, count // kx_count, LANES)
     return pl.pallas_call(
         functools.partial(
-            solve_kernel, groups=groups, kx_count=kx_count, ht_count=ht_count,
-            started=partial is not None, last=last,
+            solve_kernel, groups=groups, kx_count=kx_count, ht_count=ht_count, pieces=pieces
         ),
-        out_shape=out_shape,
-        grid=(slots,),
-        in_specs=[pl.BlockSpec((1, per_slot, lanes), lambda s: (s, 0, 0))] * owners
-        + [pl.BlockSpec((1, heights // pieces, heights), lambda s: (s, piece, 0))] * 2
-        + ([] if partial is None else [whole]),
-        out_specs=out_specs,
-        scratch_shapes=scratch,
+        out_shape=(jax.ShapeDtypeStruct(shape, jnp.float32),) * owners,
+        in_specs=[VMEM] * (1 + len(blocks)) + [pl.BlockSpec(memory_space=pl.ANY)],
+        out_specs=(VMEM,) * owners,
+        scratch_shapes=[
+            pltpu.VMEM(helmholtz.shape, jnp.float32),
+            pltpu.SemaphoreType.DMA((slots,)),
+            pltpu.VMEM((max(pieces - 1, 1),) + first.shape, jnp.float32),
+            pltpu.VMEM((2, heights // LANES, count, LANES), jnp.float32),
+        ],
         compiler_params=params(),
-        cost_estimate=pl.CostEstimate(
-            flops=6 * slots * count * heights * heights // pieces,
-            bytes_accessed=slots * heights * heights * 4 // pieces, transcendentals=0,
-        ),
+        cost_estimate=cost(4 * helmholtz.size),
         name="solve",
-    )(*blocks, *matrices, *([] if partial is None else [partial]))
-
-
-def restore_kernel(*refs):
-    block_refs, (order_ref, out_ref) = (refs[:-2], refs[-2:])
+    )(first, *blocks, helmholtz)
+
+
+def restore_kernel(*refs, owners, ht_count):
+    block_refs, (order_ref, out_ref, ordered) = (refs[:-3], refs[-3:])
     components, band_modes, rows, columns = out_ref.shape
-    slots = columns // 2 // len(block_refs)
+    slots = columns // 2 // owners
     per_slot = block_refs[0].shape[0] // slots
+    me = lax.axis_index("kx") * ht_count + lax.axis_index("ht")
+    for position, block_ref in enumerate(block_refs):
+        ordered[me ^ step_at(owners, position)] = block_ref[...]
     for c in range(components):
         for mode in range(band_modes):
             for tile in range(rows // LANES):
                 parts = []
                 for p in range(2):
                     row = ((tile * 2 + p) * components + c) * band_modes + mode
-                    for block_ref in block_refs:
-                        parts.append(block_ref[pl.ds(row, slots, stride=per_slot), :])
+                    for owner in range(owners):
+                        parts.append(ordered[owner, pl.ds(row, slots, stride=per_slot), :])
                 top, rest = two_parts(jnp.concatenate(parts, axis=0))
                 both = jnp.concatenate([top, rest], axis=0)
                 out_ref[c, mode, pl.ds(tile * LANES, LANES)] = dot(
@@ -502,50 +533,18 @@
                 )
 
 
-def restore(blocks, order, components, band_modes, rows):
+def restore(blocks, order, components, band_modes, rows, ht_count):
     columns = order.shape[1]
     return pl.pallas_call(
-        restore_kernel,
+        functools.partial(restore_kernel, owners=len(blocks), ht_count=ht_count),
         out_shape=jax.ShapeDtypeStruct((components, band_modes, rows, columns), jnp.float32),
         in_specs=[VMEM] * (len(blocks) + 1),
         out_specs=VMEM,
+        scratch_shapes=[pltpu.VMEM((len(blocks),) + blocks[0].shape, jnp.float32)],
         compiler_params=params(),
         cost_estimate=cost(8 * components * band_modes * rows * columns),
         name="restore",
     )(*blocks, order)
-
-
-def table_parts(value):
-    top = lax.reduce_precision(value, 8, 7)
-    return top.astype(jnp.bfloat16), (value - top).astype(jnp.bfloat16)
-
-
-def slot_tables(owner_map, even_map, columns):
-    forward, backward = spanwise_tables(columns // 2, 2 * columns)
-    select, even_select = (
-        (2 * order[None, :] + jnp.arange(2)[:, None]).reshape(1, columns)
-        == jnp.arange(columns)[:, None]
-        for order in (owner_map, even_map)
-    )
-    forward_top, forward_rest = table_parts(forward)
-    first = jnp.concatenate([forward_top, select.astype(jnp.bfloat16)], axis=1)
-    first = jnp.concatenate([first, first], axis=0)
-    back = []
-    for chosen in (select, even_select):
-        slotted_back = jnp.dot(
-            backward, chosen.astype(jnp.float32), precision=lax.Precision.HIGHEST
-        )
-        back += table_parts(slotted_back)
-    back = jnp.concatenate(back, axis=1)
-    order = select.T.astype(jnp.bfloat16)
-    order = jnp.concatenate([order, order], axis=0)
-    return (first, forward_rest, back), order
-
-
-def slot_masks(owner_map, mode_counts, realizations):
-    active = jnp.tile(owner_map, 2)[None, :] < mode_counts[:, None]
-    mask = jnp.where(active, jnp.float32(dt_step), 0.0)[:, None, :]
-    return mask, mask / realizations
 
 
 def exchange(blocks, axes):
@@ -586,18 +585,11 @@
     shape = (components, modes, rows, columns)
     extra_rows = -(-band_modes // 8) * 8
     split = velocity.reshape(chunks, pieces, kx_count, rows, columns)
-    owner_map, even_map = (
-        owner_map.reshape(owners, slots)[(own_kx * ht_count + own_ht) ^ order].reshape(-1)
-        for order in (
-            jnp.stack([step_at(owners, position) for position in range(owners)]),
-            jnp.array(steps_of(owners)[0], jnp.int32),
-        )
-    )
     first_blocks, rest = pack(split, neighbours, mode_counts, extra_rows)
     parts = [exchange(first_blocks, ("kx",))] + [
         (lax.all_to_all(block, "kx", split_axis=0, concat_axis=0, tiled=True),) for block in rest
     ]
-    *matrices, after = split_matrix(helmholtz, pieces, kx_count, ht_count)
+    tables, order, slot_modes = slot_tables(owner_map, columns)
     small = 0.0
     for index, block in enumerate(parts[0]):
         lines = block[chunks * rows : chunks * rows + band_modes, : members + 1]
@@ -605,29 +597,29 @@
         small = small + jnp.where(here[:, None, None], lines[None], 0.0)
     small = small.reshape(modes, members + 1).astype(jnp.int32)
     neighbours, mode_counts = (small[:, :-1], small[:, -1])
-    tables, order = slot_tables(owner_map, even_map, columns)
-    mask, low_mask = slot_masks(owner_map, mode_counts, realizations)
+    after = slot_modes
     received = []
-    for part in parts:
+    for piece, part in enumerate(parts):
         slotted, kept, sent = nonlinear(
-            part, shape, low_index, neighbours, tables, mask, after
+            part, shape, low_index, neighbours, mode_counts, tables, slot_modes, after
         )
-        kept = kept + swap(sent, 1)
+        kept = after = kept + swap(sent, 1)
         step = 2
         while step < realizations:
             kept = kept + swap(kept, step)
             step *= 2
-        after = swap(kept, 1)
         blocks = outgoing(
-            slotted, kept, after, low_index, low_mask, groups, band_modes, owners
+            slotted, kept, swap(kept, 1), low_index, mode_counts, slot_modes, groups, band_modes,
+            owners, realizations, piece > 0,
         )
-        blocks = [block.reshape(slots, -1, LANES) for block in blocks]
-        received.append(exchange(blocks, ("kx", "ht")))
-    solved = None
-    for piece, blocks in enumerate(received):
-        solved = solve(blocks, matrices, piece, pieces, solved, groups, kx_count, ht_count)
+        if piece:
+            received += exchange([block.reshape(slots, -1, LANES) for block in blocks], ("kx", "ht"))
+        else:
+            block = blocks[0].reshape(owners, slots, -1, LANES)
+            first = lax.all_to_all(block, ("kx", "ht"), split_axis=0, concat_axis=0, tiled=True)
+    solved = solve(first, received, helmholtz, pieces, groups, kx_count, ht_count)
     returned = [block.reshape(-1, LANES) for block in exchange(solved, ("kx", "ht"))]
-    result = restore(returned, order, components, band_modes, rows_ht)
+    result = restore(returned, order, components, band_modes, rows_ht, ht_count)
     return result.reshape(velocity.shape)
 
 

time: 146 us -> 152 us (1.041)
  waiting for transfers between devices: 48.8 us -> 78.5 us
  Pallas kernels: 38.7 us -> 25.9 us
  local copies, waits for them, and re-layouts: 5.92 us -> 0.88 us
  starting transfers between devices: 47 us -> 43.7 us
  other arithmetic: 1.77 us -> 0.21 us
    ppermute x24 -> x17, waiting for transfers between devices: 33.7 us -> 61.9 us  [exchange(): result[position] = lax.ppermute(blocks[position], axes + ('real',), pairs)]
    ppermute x24 -> x17, starting transfers between devices: 39.3 us -> 30.1 us  [exchange(): result[position] = lax.ppermute(blocks[position], axes + ('real',), pairs)]
    pallas_call x2, Pallas kernels: 11 us -> 2.82 us  [the longest x1 2.06 us: restore(): pl.pallas_call(functools.partial(restore_kernel, owners=len(blocks), ht_c...]
    pallas_call x2 -> x1, Pallas kernels: 12.2 us -> 6.81 us  [solve(): pl.pallas_call(functools.partial(solve_kernel, groups=groups, kx_count=kx...]
    all_to_all x0 -> x1, starting transfers between devices: none -> 3.69 us  [local(): lax.all_to_all(block, ('kx', 'ht'), split_axis=0, concat_axis=0, tiled=True)]
    all_to_all x1, starting transfers between devices: 4.19 us -> 6.48 us  [local(): lax.all_to_all(block, 'kx', split_axis=0, concat_axis=0, tiled=True)]
    unnamed x6 -> x16, local copies, waits for them, and re-layouts: 2.03 us -> 0.03 us
    ppermute x6, waiting for transfers between devices: 15.1 us -> 16.6 us  [swap(): return lax.ppermute(value, 'real', pairs)]
  transfers between devices with their start and end apart: 31 -> 25, of which waited for: 11 -> 13; matrix products, arithmetic and copies ran while one was open for 5% -> 1% of each run, Pallas kernels for 16% -> 10%
where the time goes in v6:
time: 152 us; the launch traced here: 149 us
  waiting for transfers between devices  78.5 us (52%)
  starting transfers between devices  43.7 us (29%)
  Pallas kernels  25.9 us (17%)
    ppermute x17, waiting for transfers between devices, exchange(): result[position] = lax.ppermute(blocks[position], axes + ('real',), pairs)  61.9 us
    ppermute x17, starting transfers between devices, exchange(): result[position] = lax.ppermute(blocks[position], axes + ('real',), pairs)  30.1 us
    ppermute x6, waiting for transfers between devices, swap(): return lax.ppermute(value, 'real', pairs)  16.6 us
    pallas_call x2, Pallas kernels, nonlinear(): pl.pallas_call(nonlinear_kernel, out_shape=(jax.ShapeDtypeStruct((compone...  10.7 us
    pallas_call x1, Pallas kernels, solve(): pl.pallas_call(functools.partial(solve_kernel, groups=groups, kx_count=kx...  6.81 us
    all_to_all x1, starting transfers between devices, local(): lax.all_to_all(block, 'kx', split_axis=0, concat_axis=0, tiled=True)  6.48 us
    all_to_all x1, starting transfers between devices, local(): lax.all_to_all(block, ('kx', 'ht'), split_axis=0, concat_axis=0, tiled=True)  3.69 us
    ppermute x6, starting transfers between devices, swap(): return lax.ppermute(value, 'real', pairs)  3.4 us
  transfers between devices with their start and end apart: 25, of which 13 were waited for; matrix products, arithmetic and copies ran while one was open for 1% of the time, Pallas kernels for 10%

profile of v6, /device:TPU:0, one launch (start us, length us, event | category | flops | bytes accessed | tf_op | source)
XLA Modules:
  0.0 149.4 jit_solution(5362096025807866889)
XLA Ops:
  0.0 2.6 %pack.1 = (f32[392,128]{1,0:T(8,128)}, f32[392,128]{1,0:T(8,128)}, f32[392,128]{1,0:T(8,128)}, f32[392,128]{1,0:T(8,128)}, f32[4,384,128]{2,1,0:T(8,128)}) custom-call(s32[4,8]{1,0:T(4,128)} %near_ref.1, s32[4]{0:T(128)} %count_ref.1, f32[12,2,4,32,128]{4,3,2,1,0:T(8,128)} %bitcast.44), custom_call_target="tpu_custom_call" | custom-call | bytes 3145728 | tf_op jit(solution)/shard_map/pack/pallas_call | solution.py:181
  2.7 6.5 %all-to-all-start.1 = ((f32[4,384,128]{2,1,0:T(8,128)}), f32[4,384,128]{2,1,0:T(8,128)S(1)}, u32[]{:S(2)}, u32[]{:S(2)}) async-start(f32[4,384,128]{2,1,0:T(8,128)} %get-tuple-element.46), calls=%async_computation.1 | async-start | bytes 1572864 | tf_op jit(solution)/shard_map/all_to_all | solution.py:590
  9.2 2.0 %collective-permute-start = (f32[392,128]{1,0:T(8,128)S(1)}, f32[392,128]{1,0:T(8,128)S(1)}, u32[]{:S(2)}, u32[]{:S(2)}) collective-permute-start(f32[392,128]{1,0:T(8,128)S(1)} %copy-done.7), channel_id=1, source_target_pairs={{0,8},{1,25},{2,10},{3,27},{8,0},{9,17},{10,2},{11,19},{16,24},{17... | collective-permute-start | bytes 602120 | tf_op jit(solution)/shard_map/ppermute | solution.py:560
  11.2 2.4 %collective-permute-start.1 = (f32[392,128]{1,0:T(8,128)S(1)}, f32[392,128]{1,0:T(8,128)S(1)}, u32[]{:S(2)}, u32[]{:S(2)}) collective-permute-start(f32[392,128]{1,0:T(8,128)S(1)} %copy-done.6), channel_id=1, source_target_pairs={{0,24},{1,9},{2,26},{3,11},{8,16},{9,1},{10,18},{11,3},{16,8},{17,... | collective-permute-start | bytes 602120 | tf_op jit(solution)/shard_map/ppermute | solution.py:560
  13.5 0.1 collective-permute-start.2
  13.6 0.1 broadcast_in_dim.85
  13.7 0.1 broadcast_in_dim.86
  13.8 0.1 broadcast_in_dim.91
  13.9 0.1 broadcast_in_dim.92
  14.0 0.1 broadcast_in_dim.96
  14.0 0.1 broadcast_in_dim.97
  14.1 0.1 broadcast_in_dim.101
  14.2 0.1 broadcast_in_dim.102
  14.3 0.8 tables.1
  15.1 12.3 %collective-permute-done.refs_1_ = f32[392,128]{1,0:T(8,128)S(1)} collective-permute-done((f32[392,128]{1,0:T(8,128)S(1)}, f32[392,128]{1,0:T(8,128)S(1)}, u32[]{:S(2)}, u32[]{:S(2)}) %collective-permute-start) | collective-permute-done | bytes 200736 | tf_op jit(solution)/shard_map/ppermute | solution.py:560
  27.4 8.7 %collective-permute-done.1.refs_2_ = f32[392,128]{1,0:T(8,128)S(1)} collective-permute-done((f32[392,128]{1,0:T(8,128)S(1)}, f32[392,128]{1,0:T(8,128)S(1)}, u32[]{:S(2)}, u32[]{:S(2)}) %collective-permute-start.1) | collective-permute-done | bytes 200736 | tf_op jit(solution)/shard_map/ppermute | solution.py:560
  36.2 10.3 %collective-permute-done.2.refs_3_ = f32[392,128]{1,0:T(8,128)S(1)} collective-permute-done((f32[392,128]{1,0:T(8,128)S(1)}, f32[392,128]{1,0:T(8,128)S(1)}, u32[]{:S(2)}, u32[]{:S(2)}) %collective-permute-start.2) | collective-permute-done | bytes 200736 | tf_op jit(solution)/shard_map/ppermute | solution.py:560
  46.5 0.1 add_convert_fusion
  46.6 0.2 slice_reduce_fusion.count_ref
  46.8 5.4 %nonlinear.2 = (f32[3,16,32,128]{3,2,1,0:T(8,128)S(1)}, f32[3,4,32,128]{3,2,1,0:T(8,128)S(1)}, f32[3,4,32,128]{3,2,1,0:T(8,128)S(1)}) custom-call(s32[8]{0:T(128)S(1)} %copy-done.3, s32[16,8]{1,0:T(8,128)S(1)} %bitcast.34, s32[16]{0:T(128)S(1)} %slice_reduce_fusion.count_ref, f32[392,128]{1,0:T(8,128)S(1)} %copy-done.1, ...), custom_call_target="tpu_custom_call" | custom-call | bytes 25165824 | tf_op jit(solution)/shard_map/nonlinear/pallas_call | solution.py:343
  52.2 0.1 collective-permute-start.3
  52.2 1.4 collective-permute-done.3
  53.7 1.5 %collective-permute-start.4 = (f32[3,4,32,128]{3,2,1,0:T(8,128)S(1)}, f32[3,4,32,128]{3,2,1,0:T(8,128)S(1)}, u32[]{:S(2)}, u32[]{:S(2)}) collective-permute-start(f32[3,4,32,128]{3,2,1,0:T(8,128)S(1)} %add.27.refs_5_), channel_id=1, source_target_pairs={{0,2},{1,3},{2,0},{3,1},{4,6},{5,7},{6,4},{7,5},{8,10},{9,11},{10,... | collective-permute-start | bytes 589832 | tf_op jit(solution)/shard_map/ppermute | solution.py:566
  55.2 5.5 %collective-permute-done.4 = f32[3,4,32,128]{3,2,1,0:T(8,128)S(1)} collective-permute-done((f32[3,4,32,128]{3,2,1,0:T(8,128)S(1)}, f32[3,4,32,128]{3,2,1,0:T(8,128)S(1)}, u32[]{:S(2)}, u32[]{:S(2)}) %collective-permute-start.4) | collective-permute-done | bytes 196640 | tf_op jit(solution)/shard_map/ppermute | solution.py:566
  60.7 0.1 collective-permute-start.5
  60.8 1.4 collective-permute-done.5.other_ref
  62.2 1.8 %outgoing.2 = f32[1536,128]{1,0:T(8,128)} custom-call(s32[8]{0:T(128)S(1)} %copy-done.3, s32[16]{0:T(128)S(1)} %slice_reduce_fusion.count_ref, f32[3,16,32,128]{3,2,1,0:T(8,128)S(1)} %get-tuple-element.43.slotted_ref, f32[3,4,32,128]{3,2,1,0:T(8,128)S(1)} %add.28.kept_ref, f32[3,4,32,128]{3,2,1,0:T(8,128)S(1)} %collective-permute-done.5.other_ref, ...), custom_call_target="tpu_custom_call" | custom-call | bytes 1572864 | tf_op jit(solution)/shard_map/outgoing/pallas_call | solution.py:411
  64.1 0.0 all-to-all-done.1.refs_0_
  64.1 3.7 %all-to-all-start = ((f32[8,8,24,128]{3,2,1,0:T(8,128)}), f32[8,8,24,128]{3,2,1,0:T(8,128)S(1)}, u32[]{:S(2)}, u32[]{:S(2)}) async-start(f32[8,8,24,128]{3,2,1,0:T(8,128)} %bitcast.5), calls=%async_computation | async-start | bytes 1572864 | tf_op jit(solution)/shard_map/all_to_all | solution.py:619
  67.7 5.4 %nonlinear.3 = (f32[3,16,32,128]{3,2,1,0:T(8,128)S(1)}, f32[3,4,32,128]{3,2,1,0:T(8,128)S(1)}, f32[3,4,32,128]{3,2,1,0:T(8,128)S(1)}) custom-call(s32[8]{0:T(128)S(1)} %copy-done.3, s32[16,8]{1,0:T(8,128)S(1)} %bitcast.35, s32[16]{0:T(128)S(1)} %slice_reduce_fusion.count_ref, f32[4,384,128]{2,1,0:T(8,128)S(1)} %all-to-all-done.1.refs_0_, ...), custom_call_target="tpu_custom_call" | custom-call | bytes 25165824 | tf_op jit(solution)/shard_map/nonlinear/pallas_call | solution.py:343
  73.1 0.1 collective-permute-start.6
  73.2 1.4 collective-permute-done.6
  74.7 1.6 %collective-permute-start.7 = (f32[3,4,32,128]{3,2,1,0:T(8,128)S(1)}, f32[3,4,32,128]{3,2,1,0:T(8,128)S(1)}, u32[]{:S(2)}, u32[]{:S(2)}) collective-permute-start(f32[3,4,32,128]{3,2,1,0:T(8,128)S(1)} %add.29), channel_id=1, source_target_pairs={{0,2},{1,3},{2,0},{3,1},{4,6},{5,7},{6,4},{7,5},{8,10},{9,11},{10,... | collective-permute-start | bytes 589832 | tf_op jit(solution)/shard_map/ppermute | solution.py:566
  76.2 5.5 %collective-permute-done.7 = f32[3,4,32,128]{3,2,1,0:T(8,128)S(1)} collective-permute-done((f32[3,4,32,128]{3,2,1,0:T(8,128)S(1)}, f32[3,4,32,128]{3,2,1,0:T(8,128)S(1)}, u32[]{:S(2)}, u32[]{:S(2)}) %collective-permute-start.7) | collective-permute-done | bytes 196640 | tf_op jit(solution)/shard_map/ppermute | solution.py:566
  81.7 0.1 collective-permute-start.8
  81.8 1.4 collective-permute-done.8.other_ref
  83.2 1.1 outgoing.3
  84.3 3.0 %collective-permute-start.9 = (f32[8,24,128]{2,1,0:T(8,128)S(1)}, f32[8,24,128]{2,1,0:T(8,128)S(1)}, u32[]{:S(2)}, u32[]{:S(2)}) collective-permute-start(f32[8,24,128]{2,1,0:T(8,128)S(1)} %bitcast.43), channel_id=1, source_target_pairs={{0,16},{1,5},{2,18},{3,7},{4,20},{5,1},{6,22},{7,3},{8,24},{9,13},... | collective-permute-start | bytes 294920 | tf_op jit(solution)/shard_map/ppermute | solution.py:560
  87.3 1.5 collective-permute-start.10
  88.7 1.5 collective-permute-start.11
  90.2 0.6 collective-permute-start.12
  90.8 1.5 collective-permute-start.13
  92.2 0.0 collective-permute-done.9.refs_2_
  92.2 3.7 %collective-permute-start.14 = (f32[8,24,128]{2,1,0:T(8,128)S(1)}, f32[8,24,128]{2,1,0:T(8,128)S(1)}, u32[]{:S(2)}, u32[]{:S(2)}) collective-permute-start(f32[8,24,128]{2,1,0:T(8,128)S(1)} %bitcast.38), channel_id=1, source_target_pairs={{0,12},{1,21},{2,14},{3,23},{4,8},{5,17},{6,10},{7,19},{8,4},{9,29... | collective-permute-start | bytes 294920 | tf_op jit(solution)/shard_map/ppermute | solution.py:560
  95.9 0.0 collective-permute-done.10.refs_3_
  95.9 3.2 %collective-permute-start.15 = (f32[8,24,128]{2,1,0:T(8,128)S(1)}, f32[8,24,128]{2,1,0:T(8,128)S(1)}, u32[]{:S(2)}, u32[]{:S(2)}) collective-permute-start(f32[8,24,128]{2,1,0:T(8,128)S(1)} %bitcast.37), channel_id=1, source_target_pairs={{0,28},{1,29},{2,30},{3,31},{4,24},{5,25},{6,26},{7,27},{8,20},{9,... | collective-permute-start | bytes 294920 | tf_op jit(solution)/shard_map/ppermute | solution.py:560
  99.1 0.0 collective-permute-done.11.refs_4_
  99.1 0.0 collective-permute-done.12.refs_5_
  99.1 5.9 %collective-permute-done.13.refs_6_ = f32[8,24,128]{2,1,0:T(8,128)S(1)} collective-permute-done((f32[8,24,128]{2,1,0:T(8,128)S(1)}, f32[8,24,128]{2,1,0:T(8,128)S(1)}, u32[]{:S(2)}, u32[]{:S(2)}) %collective-permute-start.13) | collective-permute-done | bytes 98336 | tf_op jit(solution)/shard_map/ppermute | solution.py:560
  105.0 0.0 collective-permute-done.14.refs_7_
  105.0 0.0 collective-permute-done.15.refs_8_
  105.0 0.0 all-to-all-done.refs_0_
  105.0 6.8 %solve.1 = (f32[8,2,24,128]{3,2,1,0:T(8,128)S(1)}, f32[8,2,24,128]{3,2,1,0:T(8,128)S(1)}, f32[8,2,24,128]{3,2,1,0:T(8,128)S(1)}, f32[8,2,24,128]{3,2,1,0:T(8,128...) custom-call(f32[8,8,24,128]{3,2,1,0:T(8,128)S(1)} %all-to-all-done.r, ...), custom_call_target="tpu_custom_call" | custom-call | bytes 8388608 | tf_op jit(solution)/shard_map/solve/pallas_call | solution.py:494
  111.8 4.1 %collective-permute-start.16 = (f32[8,2,24,128]{3,2,1,0:T(8,128)S(1)}, f32[8,2,24,128]{3,2,1,0:T(8,128)S(1)}, u32[]{:S(2)}, u32[]{:S(2)}) collective-permute-start(f32[8,2,24,128]{3,2,1,0:T(8,128)S(1)} %get-tuple-element.59), channel_id=1, source_target_pairs={{0,16},{1,5},{2,18},{3,7},{4,20},{5,1},{6,22},{7,3},{8,24},{9,13},... | collective-permute-start | bytes 589832 | tf_op jit(solution)/shard_map/ppermute | solution.py:560
  115.9 1.0 collective-permute-start.17
  116.9 0.0 collective-permute-start.18
  116.9 1.5 %collective-permute-start.19 = (f32[8,2,24,128]{3,2,1,0:T(8,128)S(1)}, f32[8,2,24,128]{3,2,1,0:T(8,128)S(1)}, u32[]{:S(2)}, u32[]{:S(2)}) collective-permute-start(f32[8,2,24,128]{3,2,1,0:T(8,128)S(1)} %get-tuple-element.62), channel_id=1, source_target_pairs={{0,24},{1,9},{2,26},{3,11},{4,28},{5,13},{6,30},{7,15},{8,16},{9,1... | collective-permute-start | bytes 589832 | tf_op jit(solution)/shard_map/ppermute | solution.py:560
  118.5 2.4 %collective-permute-start.20 = (f32[8,2,24,128]{3,2,1,0:T(8,128)S(1)}, f32[8,2,24,128]{3,2,1,0:T(8,128)S(1)}, u32[]{:S(2)}, u32[]{:S(2)}) collective-permute-start(f32[8,2,24,128]{3,2,1,0:T(8,128)S(1)} %get-tuple-element.63), channel_id=1, source_target_pairs={{0,20},{1,13},{2,22},{3,15},{4,16},{5,9},{6,18},{7,11},{8,28},{9,5... | collective-permute-start | bytes 589832 | tf_op jit(solution)/shard_map/ppermute | solution.py:560
  120.8 8.6 %collective-permute-done.16 = f32[8,2,24,128]{3,2,1,0:T(8,128)S(1)} collective-permute-done((f32[8,2,24,128]{3,2,1,0:T(8,128)S(1)}, f32[8,2,24,128]{3,2,1,0:T(8,128)S(1)}, u32[]{:S(2)}, u32[]{:S(2)}) %collective-permute-start.16) | collective-permute-done | bytes 196640 | tf_op jit(solution)/shard_map/ppermute | solution.py:560
  129.5 1.9 %collective-permute-start.22 = (f32[8,2,24,128]{3,2,1,0:T(8,128)S(1)}, f32[8,2,24,128]{3,2,1,0:T(8,128)S(1)}, u32[]{:S(2)}, u32[]{:S(2)}) collective-permute-start(f32[8,2,24,128]{3,2,1,0:T(8,128)S(1)} %get-tuple-element.65), channel_id=1, source_target_pairs={{0,28},{1,29},{2,30},{3,31},{4,24},{5,25},{6,26},{7,27},{8,20},{9,... | collective-permute-start | bytes 589832 | tf_op jit(solution)/shard_map/ppermute | solution.py:560
  131.3 1.7 %collective-permute-done.18 = f32[8,2,24,128]{3,2,1,0:T(8,128)S(1)} collective-permute-done((f32[8,2,24,128]{3,2,1,0:T(8,128)S(1)}, f32[8,2,24,128]{3,2,1,0:T(8,128)S(1)}, u32[]{:S(2)}, u32[]{:S(2)}) %collective-permute-start.18) | collective-permute-done | bytes 196640 | tf_op jit(solution)/shard_map/ppermute | solution.py:560
  133.1 0.0 collective-permute-done.19
  133.1 14.3 %collective-permute-done.20 = f32[8,2,24,128]{3,2,1,0:T(8,128)S(1)} collective-permute-done((f32[8,2,24,128]{3,2,1,0:T(8,128)S(1)}, f32[8,2,24,128]{3,2,1,0:T(8,128)S(1)}, u32[]{:S(2)}, u32[]{:S(2)}) %collective-permute-start.20) | collective-permute-done | bytes 196640 | tf_op jit(solution)/shard_map/ppermute | solution.py:560
  147.3 2.1 %restore.1 = f32[3,4,256,128]{3,2,1,0:T(8,128)} custom-call(f32[384,128]{1,0:T(8,128)S(1)} %bitcast.26, f32[384,128]{1,0:T(8,128)S(1)} %bitcast.27, f32[384,128]{1,0:T(8,128)S(1)} %bitcast.28, f32[384,128]{1,0:T(8,128)S(1)} %bitcast.29, f32[384,128]{1,0:T(8,128)S(1)} %bitcast.30, f32[384,128]{1,0:T(8,128)S(1)} %bitcast.31, f32[384,128]{1,0:T(8,128)S(1)} %bitcast.32, ...), custom_call_target="tpu_custom_call" | custom-call | bytes 3145728 | tf_op jit(solution)/shard_map/restore/pallas_call | solution.py:538
  (36 shorter events, 0.2 us)
Async XLA Ops:
  0.0 14.3 %copy-start = (bf16[128,256]{1,0:T(8,128)(2,1)S(1)}, bf16[128,256]{1,0:T(8,128)(2,1)}, u32[]{:S(2)}) copy-start(bf16[128,256]{1,0:T(8,128)(2,1)} %constant.22.clone.rest_ref.refs_5_.refs_2_) | copy-start | bytes 196612
  0.0 14.3 %copy-start.2 = (bf16[128,256]{1,0:T(8,128)(2,1)S(1)}, bf16[128,256]{1,0:T(8,128)(2,1)}, u32[]{:S(2)}) copy-start(bf16[128,256]{1,0:T(8,128)(2,1)} %constant.21.clone.top_ref) | copy-start | bytes 196612
  0.0 14.3 %copy-start.4 = (s32[64]{0:T(128)S(1)}, s32[64]{0:T(128)}, u32[]{:S(2)}) copy-start(s32[64]{0:T(128)} %owner_ref.1) | copy-start | bytes 772
  0.0 46.7 %copy-start.3 = (s32[8]{0:T(128)S(1)}, s32[8]{0:T(128)}, u32[]{:S(2)}) copy-start(s32[8]{0:T(128)} %low_ref.7) | copy-start | bytes 100
  2.7 6.5 %copy-start.7 = (f32[392,128]{1,0:T(8,128)S(1)}, f32[392,128]{1,0:T(8,128)}, u32[]{:S(2)}) copy-start(f32[392,128]{1,0:T(8,128)} %get-tuple-element.37) | copy-start | bytes 602116
  2.7 8.5 %copy-start.6 = (f32[392,128]{1,0:T(8,128)S(1)}, f32[392,128]{1,0:T(8,128)}, u32[]{:S(2)}) copy-start(f32[392,128]{1,0:T(8,128)} %get-tuple-element.38) | copy-start | bytes 602116
  2.7 10.9 %copy-start.5 = (f32[392,128]{1,0:T(8,128)S(1)}, f32[392,128]{1,0:T(8,128)}, u32[]{:S(2)}) copy-start(f32[392,128]{1,0:T(8,128)} %get-tuple-element.39) | copy-start | bytes 602116
  2.7 11.6 %copy-start.1 = (f32[392,128]{1,0:T(8,128)S(1)}, f32[392,128]{1,0:T(8,128)}, u32[]{:S(2)}) copy-start(f32[392,128]{1,0:T(8,128)} %get-tuple-element.36.refs_0_) | copy-start | bytes 602116
  2.7 61.4 %all-to-all-start.1 = ((f32[4,384,128]{2,1,0:T(8,128)}), f32[4,384,128]{2,1,0:T(8,128)S(1)}, u32[]{:S(2)}, u32[]{:S(2)}) async-start(f32[4,384,128]{2,1,0:T(8,128)} %get-tuple-element.46), calls=%async_computation.1 | async-start | bytes 1572864 | tf_op jit(solution)/shard_map/all_to_all | solution.py:590
  9.2 18.3 %collective-permute-start = (f32[392,128]{1,0:T(8,128)S(1)}, f32[392,128]{1,0:T(8,128)S(1)}, u32[]{:S(2)}, u32[]{:S(2)}) collective-permute-start(f32[392,128]{1,0:T(8,128)S(1)} %copy-done.7), channel_id=1, source_target_pairs={{0,8},{1,25},{2,10},{3,27},{8,0},{9,17},{10,2},{11,19},{16,24},{17... | collective-permute-start | bytes 602120 | tf_op jit(solution)/shard_map/ppermute | solution.py:560
  11.2 25.0 %collective-permute-start.1 = (f32[392,128]{1,0:T(8,128)S(1)}, f32[392,128]{1,0:T(8,128)S(1)}, u32[]{:S(2)}, u32[]{:S(2)}) collective-permute-start(f32[392,128]{1,0:T(8,128)S(1)} %copy-done.6), channel_id=1, source_target_pairs={{0,24},{1,9},{2,26},{3,11},{8,16},{9,1},{10,18},{11,3},{16,8},{17,... | collective-permute-start | bytes 602120 | tf_op jit(solution)/shard_map/ppermute | solution.py:560
  13.5 32.9 %collective-permute-start.2 = (f32[392,128]{1,0:T(8,128)S(1)}, f32[392,128]{1,0:T(8,128)S(1)}, u32[]{:S(2)}, u32[]{:S(2)}) collective-permute-start(f32[392,128]{1,0:T(8,128)S(1)} %copy-done.5), channel_id=1, source_target_pairs={{0,16},{1,17},{2,18},{3,19},{8,24},{9,25},{10,26},{11,27},{16,0},{... | collective-permute-start | bytes 602120 | tf_op jit(solution)/shard_map/ppermute | solution.py:560
  52.2 1.5 %collective-permute-start.3 = (f32[3,4,32,128]{3,2,1,0:T(8,128)S(1)}, f32[3,4,32,128]{3,2,1,0:T(8,128)S(1)}, u32[]{:S(2)}, u32[]{:S(2)}) collective-permute-start(f32[3,4,32,128]{3,2,1,0:T(8,128)S(1)} %get-tuple-element.45), channel_id=1, source_target_pairs={{0,1},{1,0},{2,3},{3,2},{4,5},{5,4},{6,7},{7,6},{8,9},{9,8},{10,11... | collective-permute-start | bytes 589832 | tf_op jit(solution)/shard_map/ppermute | solution.py:566
  53.7 7.0 %collective-permute-start.4 = (f32[3,4,32,128]{3,2,1,0:T(8,128)S(1)}, f32[3,4,32,128]{3,2,1,0:T(8,128)S(1)}, u32[]{:S(2)}, u32[]{:S(2)}) collective-permute-start(f32[3,4,32,128]{3,2,1,0:T(8,128)S(1)} %add.27.refs_5_), channel_id=1, source_target_pairs={{0,2},{1,3},{2,0},{3,1},{4,6},{5,7},{6,4},{7,5},{8,10},{9,11},{10,... | collective-permute-start | bytes 589832 | tf_op jit(solution)/shard_map/ppermute | solution.py:566
  60.7 1.5 %collective-permute-start.5 = (f32[3,4,32,128]{3,2,1,0:T(8,128)S(1)}, f32[3,4,32,128]{3,2,1,0:T(8,128)S(1)}, u32[]{:S(2)}, u32[]{:S(2)}) collective-permute-start(f32[3,4,32,128]{3,2,1,0:T(8,128)S(1)} %add.28.kept_ref), channel_id=1, source_target_pairs={{0,1},{1,0},{2,3},{3,2},{4,5},{5,4},{6,7},{7,6},{8,9},{9,8},{10,11... | collective-permute-start | bytes 589832 | tf_op jit(solution)/shard_map/ppermute | solution.py:566
  64.1 40.9 %all-to-all-start = ((f32[8,8,24,128]{3,2,1,0:T(8,128)}), f32[8,8,24,128]{3,2,1,0:T(8,128)S(1)}, u32[]{:S(2)}, u32[]{:S(2)}) async-start(f32[8,8,24,128]{3,2,1,0:T(8,128)} %bitcast.5), calls=%async_computation | async-start | bytes 1572864 | tf_op jit(solution)/shard_map/all_to_all | solution.py:619
  73.1 1.5 %collective-permute-start.6 = (f32[3,4,32,128]{3,2,1,0:T(8,128)S(1)}, f32[3,4,32,128]{3,2,1,0:T(8,128)S(1)}, u32[]{:S(2)}, u32[]{:S(2)}) collective-permute-start(f32[3,4,32,128]{3,2,1,0:T(8,128)S(1)} %get-tuple-element.49), channel_id=1, source_target_pairs={{0,1},{1,0},{2,3},{3,2},{4,5},{5,4},{6,7},{7,6},{8,9},{9,8},{10,11... | collective-permute-start | bytes 589832 | tf_op jit(solution)/shard_map/ppermute | solution.py:566
  74.7 7.0 %collective-permute-start.7 = (f32[3,4,32,128]{3,2,1,0:T(8,128)S(1)}, f32[3,4,32,128]{3,2,1,0:T(8,128)S(1)}, u32[]{:S(2)}, u32[]{:S(2)}) collective-permute-start(f32[3,4,32,128]{3,2,1,0:T(8,128)S(1)} %add.29), channel_id=1, source_target_pairs={{0,2},{1,3},{2,0},{3,1},{4,6},{5,7},{6,4},{7,5},{8,10},{9,11},{10,... | collective-permute-start | bytes 589832 | tf_op jit(solution)/shard_map/ppermute | solution.py:566
  81.7 1.5 %collective-permute-start.8 = (f32[3,4,32,128]{3,2,1,0:T(8,128)S(1)}, f32[3,4,32,128]{3,2,1,0:T(8,128)S(1)}, u32[]{:S(2)}, u32[]{:S(2)}) collective-permute-start(f32[3,4,32,128]{3,2,1,0:T(8,128)S(1)} %add.30.kept_ref), channel_id=1, source_target_pairs={{0,1},{1,0},{2,3},{3,2},{4,5},{5,4},{6,7},{7,6},{8,9},{9,8},{10,11... | collective-permute-start | bytes 589832 | tf_op jit(solution)/shard_map/ppermute | solution.py:566
  84.3 7.9 %collective-permute-start.9 = (f32[8,24,128]{2,1,0:T(8,128)S(1)}, f32[8,24,128]{2,1,0:T(8,128)S(1)}, u32[]{:S(2)}, u32[]{:S(2)}) collective-permute-start(f32[8,24,128]{2,1,0:T(8,128)S(1)} %bitcast.43), channel_id=1, source_target_pairs={{0,16},{1,5},{2,18},{3,7},{4,20},{5,1},{6,22},{7,3},{8,24},{9,13},... | collective-permute-start | bytes 294920 | tf_op jit(solution)/shard_map/ppermute | solution.py:560
  87.3 8.7 %collective-permute-start.10 = (f32[8,24,128]{2,1,0:T(8,128)S(1)}, f32[8,24,128]{2,1,0:T(8,128)S(1)}, u32[]{:S(2)}, u32[]{:S(2)}) collective-permute-start(f32[8,24,128]{2,1,0:T(8,128)S(1)} %bitcast.42), channel_id=1, source_target_pairs={{0,4},{1,17},{2,6},{3,19},{4,0},{5,21},{6,2},{7,23},{8,12},{9,25},... | collective-permute-start | bytes 294920 | tf_op jit(solution)/shard_map/ppermute | solution.py:560
  88.7 10.4 %collective-permute-start.11 = (f32[8,24,128]{2,1,0:T(8,128)S(1)}, f32[8,24,128]{2,1,0:T(8,128)S(1)}, u32[]{:S(2)}, u32[]{:S(2)}) collective-permute-start(f32[8,24,128]{2,1,0:T(8,128)S(1)} %bitcast.41), channel_id=1, source_target_pairs={{0,8},{1,25},{2,10},{3,27},{4,12},{5,29},{6,14},{7,31},{8,0},{9,17... | collective-permute-start | bytes 294920 | tf_op jit(solution)/shard_map/ppermute | solution.py:560
  90.2 8.9 %collective-permute-start.12 = (f32[8,24,128]{2,1,0:T(8,128)S(1)}, f32[8,24,128]{2,1,0:T(8,128)S(1)}, u32[]{:S(2)}, u32[]{:S(2)}) collective-permute-start(f32[8,24,128]{2,1,0:T(8,128)S(1)} %bitcast.40), channel_id=1, source_target_pairs={{0,24},{1,9},{2,26},{3,11},{4,28},{5,13},{6,30},{7,15},{8,16},{9,1... | collective-permute-start | bytes 294920 | tf_op jit(solution)/shard_map/ppermute | solution.py:560
  90.8 14.2 %collective-permute-start.13 = (f32[8,24,128]{2,1,0:T(8,128)S(1)}, f32[8,24,128]{2,1,0:T(8,128)S(1)}, u32[]{:S(2)}, u32[]{:S(2)}) collective-permute-start(f32[8,24,128]{2,1,0:T(8,128)S(1)} %bitcast.39), channel_id=1, source_target_pairs={{0,20},{1,13},{2,22},{3,15},{4,16},{5,9},{6,18},{7,11},{8,28},{9,5... | collective-permute-start | bytes 294920 | tf_op jit(solution)/shard_map/ppermute | solution.py:560
  92.2 12.7 %collective-permute-start.14 = (f32[8,24,128]{2,1,0:T(8,128)S(1)}, f32[8,24,128]{2,1,0:T(8,128)S(1)}, u32[]{:S(2)}, u32[]{:S(2)}) collective-permute-start(f32[8,24,128]{2,1,0:T(8,128)S(1)} %bitcast.38), channel_id=1, source_target_pairs={{0,12},{1,21},{2,14},{3,23},{4,8},{5,17},{6,10},{7,19},{8,4},{9,29... | collective-permute-start | bytes 294920 | tf_op jit(solution)/shard_map/ppermute | solution.py:560
  95.9 9.1 %collective-permute-start.15 = (f32[8,24,128]{2,1,0:T(8,128)S(1)}, f32[8,24,128]{2,1,0:T(8,128)S(1)}, u32[]{:S(2)}, u32[]{:S(2)}) collective-permute-start(f32[8,24,128]{2,1,0:T(8,128)S(1)} %bitcast.37), channel_id=1, source_target_pairs={{0,28},{1,29},{2,30},{3,31},{4,24},{5,25},{6,26},{7,27},{8,20},{9,... | collective-permute-start | bytes 294920 | tf_op jit(solution)/shard_map/ppermute | solution.py:560
  111.8 17.6 %collective-permute-start.16 = (f32[8,2,24,128]{3,2,1,0:T(8,128)S(1)}, f32[8,2,24,128]{3,2,1,0:T(8,128)S(1)}, u32[]{:S(2)}, u32[]{:S(2)}) collective-permute-start(f32[8,2,24,128]{3,2,1,0:T(8,128)S(1)} %get-tuple-element.59), channel_id=1, source_target_pairs={{0,16},{1,5},{2,18},{3,7},{4,20},{5,1},{6,22},{7,3},{8,24},{9,13},... | collective-permute-start | bytes 589832 | tf_op jit(solution)/shard_map/ppermute | solution.py:560
  115.9 13.6 %collective-permute-start.17 = (f32[8,2,24,128]{3,2,1,0:T(8,128)S(1)}, f32[8,2,24,128]{3,2,1,0:T(8,128)S(1)}, u32[]{:S(2)}, u32[]{:S(2)}) collective-permute-start(f32[8,2,24,128]{3,2,1,0:T(8,128)S(1)} %get-tuple-element.60), channel_id=1, source_target_pairs={{0,4},{1,17},{2,6},{3,19},{4,0},{5,21},{6,2},{7,23},{8,12},{9,25},... | collective-permute-start | bytes 589832 | tf_op jit(solution)/shard_map/ppermute | solution.py:560
  116.9 16.2 %collective-permute-start.18 = (f32[8,2,24,128]{3,2,1,0:T(8,128)S(1)}, f32[8,2,24,128]{3,2,1,0:T(8,128)S(1)}, u32[]{:S(2)}, u32[]{:S(2)}) collective-permute-start(f32[8,2,24,128]{3,2,1,0:T(8,128)S(1)} %get-tuple-element.61), channel_id=1, source_target_pairs={{0,8},{1,25},{2,10},{3,27},{4,12},{5,29},{6,14},{7,31},{8,0},{9,17... | collective-permute-start | bytes 589832 | tf_op jit(solution)/shard_map/ppermute | solution.py:560
  116.9 16.2 %collective-permute-start.19 = (f32[8,2,24,128]{3,2,1,0:T(8,128)S(1)}, f32[8,2,24,128]{3,2,1,0:T(8,128)S(1)}, u32[]{:S(2)}, u32[]{:S(2)}) collective-permute-start(f32[8,2,24,128]{3,2,1,0:T(8,128)S(1)} %get-tuple-element.62), channel_id=1, source_target_pairs={{0,24},{1,9},{2,26},{3,11},{4,28},{5,13},{6,30},{7,15},{8,16},{9,1... | collective-permute-start | bytes 589832 | tf_op jit(solution)/shard_map/ppermute | solution.py:560
  118.5 28.9 %collective-permute-start.20 = (f32[8,2,24,128]{3,2,1,0:T(8,128)S(1)}, f32[8,2,24,128]{3,2,1,0:T(8,128)S(1)}, u32[]{:S(2)}, u32[]{:S(2)}) collective-permute-start(f32[8,2,24,128]{3,2,1,0:T(8,128)S(1)} %get-tuple-element.63), channel_id=1, source_target_pairs={{0,20},{1,13},{2,22},{3,15},{4,16},{5,9},{6,18},{7,11},{8,28},{9,5... | collective-permute-start | bytes 589832 | tf_op jit(solution)/shard_map/ppermute | solution.py:560
  129.5 17.9 %collective-permute-start.21 = (f32[8,2,24,128]{3,2,1,0:T(8,128)S(1)}, f32[8,2,24,128]{3,2,1,0:T(8,128)S(1)}, u32[]{:S(2)}, u32[]{:S(2)}) collective-permute-start(f32[8,2,24,128]{3,2,1,0:T(8,128)S(1)} %get-tuple-element.64), channel_id=1, source_target_pairs={{0,12},{1,21},{2,14},{3,23},{4,8},{5,17},{6,10},{7,19},{8,4},{9,29... | collective-permute-start | bytes 589832 | tf_op jit(solution)/shard_map/ppermute | solution.py:560
  129.5 17.9 %collective-permute-start.22 = (f32[8,2,24,128]{3,2,1,0:T(8,128)S(1)}, f32[8,2,24,128]{3,2,1,0:T(8,128)S(1)}, u32[]{:S(2)}, u32[]{:S(2)}) collective-permute-start(f32[8,2,24,128]{3,2,1,0:T(8,128)S(1)} %get-tuple-element.65), channel_id=1, source_target_pairs={{0,28},{1,29},{2,30},{3,31},{4,24},{5,25},{6,26},{7,27},{8,20},{9,... | collective-permute-start | bytes 589832 | tf_op jit(solution)/shard_map/ppermute | solution.py:560

commit v7 on v6

--- a/solution.py
+++ b/solution.py
@@ -148,17 +148,9 @@
     return lax.dot_general(left, right, (dims, ((), ())), preferred_element_type=jnp.float32)
 
 
-def pack_kernel(near_ref, count_ref, velocity_ref, *out_refs):
+def pack_kernel(near_ref, count_ref, velocity_ref, first_ref, *out_refs):
     chunks, pieces, kx_count, rows, columns = velocity_ref.shape
-    own = lax.axis_index("kx")
-    for index in range(kx_count):
-        partner = own ^ step_at(kx_count, index)
-        for chunk in range(chunks):
-            place = slice(chunk * rows, (chunk + 1) * rows)
-            out_refs[index][place] = velocity_ref[chunk, 0, partner]
-            for piece in range(1, pieces):
-                out_refs[kx_count + piece - 1][index, place] = velocity_ref[chunk, piece, index]
-    shape = (out_refs[0].shape[0] - chunks * rows, columns)
+    shape = (first_ref.shape[1] - chunks * rows, columns)
     row = lax.broadcasted_iota(jnp.int32, shape, 0)
     lane = lax.broadcasted_iota(jnp.int32, shape, 1)
     extra = jnp.zeros(shape, jnp.int32)
@@ -169,16 +161,24 @@
             line = jnp.where(lane == member, near_ref[mode, member], line)
         extra = jnp.where(row == mode, line, extra)
     extra = extra.astype(jnp.float32)
-    for out_ref in out_refs[:kx_count]:
-        out_ref[chunks * rows :] = extra
+    own = lax.axis_index("kx")
+    for index in range(kx_count):
+        first_ref[index, chunks * rows :] = extra
+        partner = own ^ step_at(kx_count, index)
+        for chunk in range(chunks):
+            place = slice(chunk * rows, (chunk + 1) * rows)
+            first_ref[index, place] = velocity_ref[chunk, 0, index]
+            for piece in range(1, pieces):
+                out_ref = out_refs[(piece - 1) * kx_count + index]
+                out_ref[place] = velocity_ref[chunk, piece, partner]
 
 
 def pack(velocity, neighbours, mode_counts, extra_rows):
     chunks, pieces, kx_count, rows, columns = velocity.shape
     size = chunks * rows
-    shapes = [(size + extra_rows, columns)] * kx_count
-    shapes += [(kx_count, size, columns)] * (pieces - 1)
-    out = pl.pallas_call(
+    shapes = [(kx_count, size + extra_rows, columns)]
+    shapes += [(size, columns)] * (kx_count * (pieces - 1))
+    first, *out = pl.pallas_call(
         pack_kernel,
         out_shape=tuple(jax.ShapeDtypeStruct(shape, jnp.float32) for shape in shapes),
         in_specs=[SMEM, SMEM, VMEM],
@@ -186,7 +186,7 @@
         cost_estimate=cost(8 * velocity.size),
         name="pack",
     )(neighbours, mode_counts, velocity)
-    return out[:kx_count], out[kx_count:]
+    return first, [out[i : i + kx_count] for i in range(0, len(out), kx_count)]
 
 
 def tables_kernel(owner_ref, top_ref, rest_ref, first_ref, back_ref, order_ref, slot_ref):
@@ -585,16 +585,11 @@
     shape = (components, modes, rows, columns)
     extra_rows = -(-band_modes // 8) * 8
     split = velocity.reshape(chunks, pieces, kx_count, rows, columns)
-    first_blocks, rest = pack(split, neighbours, mode_counts, extra_rows)
-    parts = [exchange(first_blocks, ("kx",))] + [
-        (lax.all_to_all(block, "kx", split_axis=0, concat_axis=0, tiled=True),) for block in rest
-    ]
+    block, rest = pack(split, neighbours, mode_counts, extra_rows)
+    block = lax.all_to_all(block, "kx", split_axis=0, concat_axis=0, tiled=True)
+    parts = [(block,)] + [exchange(blocks, ("kx",)) for blocks in rest]
     tables, order, slot_modes = slot_tables(owner_map, columns)
-    small = 0.0
-    for index, block in enumerate(parts[0]):
-        lines = block[chunks * rows : chunks * rows + band_modes, : members + 1]
-        here = (own_kx ^ step_at(kx_count, index)) == jnp.arange(kx_count)
-        small = small + jnp.where(here[:, None, None], lines[None], 0.0)
+    small = block[:, chunks * rows : chunks * rows + band_modes, : members + 1]
     small = small.reshape(modes, members + 1).astype(jnp.int32)
     neighbours, mode_counts = (small[:, :-1], small[:, -1])
     after = slot_modes

time: 152 us -> 169 us (1.11)
  waiting for transfers between devices: 78.5 us -> 103 us
  starting transfers between devices: 43.7 us -> 37.3 us
    all_to_all x1, waiting for transfers between devices: 0.01 us -> 19.7 us  [local(): block = lax.all_to_all(block, 'kx', split_axis=0, concat_axis=0, tiled=True)]
    ppermute x17, starting transfers between devices: 30.1 us -> 23.9 us  [exchange(): result[position] = lax.ppermute(blocks[position], axes + ('real',), pairs)]
    ppermute x17, waiting for transfers between devices: 61.9 us -> 66.6 us  [exchange(): result[position] = lax.ppermute(blocks[position], axes + ('real',), pairs)]
  transfers between devices with their start and end apart: 25 -> 25, of which waited for: 13 -> 16; matrix products, arithmetic and copies ran while one was open for 1% -> 0% of each run, Pallas kernels for 10% -> 4%
where the time goes in v7:
time: 169 us; the launch traced here: 167 us
  waiting for transfers between devices  103 us (61%)
  starting transfers between devices  37.3 us (22%)
  Pallas kernels  25.9 us (15%)
    ppermute x17, waiting for transfers between devices, exchange(): result[position] = lax.ppermute(blocks[position], axes + ('real',), pairs)  66.6 us
    ppermute x17, starting transfers between devices, exchange(): result[position] = lax.ppermute(blocks[position], axes + ('real',), pairs)  23.9 us
    all_to_all x1, waiting for transfers between devices, local(): block = lax.all_to_all(block, 'kx', split_axis=0, concat_axis=0, tiled=True)  19.7 us
    ppermute x6, waiting for transfers between devices, swap(): return lax.ppermute(value, 'real', pairs)  16.6 us
    pallas_call x2, Pallas kernels, nonlinear(): pl.pallas_call(nonlinear_kernel, out_shape=(jax.ShapeDtypeStruct((compone...  10.8 us
    pallas_call x1, Pallas kernels, solve(): pl.pallas_call(functools.partial(solve_kernel, groups=groups, kx_count=kx...  6.82 us
    all_to_all x1, starting transfers between devices, local(): block = lax.all_to_all(block, 'kx', split_axis=0, concat_axis=0, tiled=True)  6.33 us
    all_to_all x1, starting transfers between devices, local(): lax.all_to_all(block, ('kx', 'ht'), split_axis=0, concat_axis=0, tiled=True)  3.69 us
  transfers between devices with their start and end apart: 25, of which 16 were waited for; matrix products, arithmetic and copies ran while one was open for 0% of the time, Pallas kernels for 4%

profile of v7, /device:TPU:0, one launch (start us, length us, event | category | flops | bytes accessed | tf_op | source)
XLA Modules:
  0.0 166.6 jit_solution(2188598580597525199)
XLA Ops:
  0.0 2.6 %pack.1 = (f32[4,392,128]{2,1,0:T(8,128)}, f32[384,128]{1,0:T(8,128)}, f32[384,128]{1,0:T(8,128)}, f32[384,128]{1,0:T(8,128)}, f32[384,128]{1,0:T(8,128)}) custom-call(s32[4,8]{1,0:T(4,128)} %near_ref.1, s32[4]{0:T(128)} %count_ref.1, f32[12,2,4,32,128]{4,3,2,1,0:T(8,128)} %bitcast.42), custom_call_target="tpu_custom_call" | custom-call | bytes 3145728 | tf_op jit(solution)/shard_map/pack/pallas_call | solution.py:181
  2.6 6.3 %all-to-all-start = ((f32[4,392,128]{2,1,0:T(8,128)}), f32[4,392,128]{2,1,0:T(8,128)S(1)}, u32[]{:S(2)}, u32[]{:S(2)}) async-start(f32[4,392,128]{2,1,0:T(8,128)} %get-tuple-element.36), calls=%async_computation | async-start | bytes 1605632 | tf_op jit(solution)/shard_map/all_to_all | solution.py:589
  9.0 0.0 copy-done
  9.0 0.0 copy-done.2
  9.0 0.0 copy-done.4
  9.0 0.8 tables.1
  9.8 19.7 %all-to-all-done.refs_0_ = f32[4,392,128]{2,1,0:T(8,128)S(1)} async-done(((f32[4,392,128]{2,1,0:T(8,128)}), f32[4,392,128]{2,1,0:T(8,128)S(1)}, u32[]{:S(2)}, u32[]{:S(2)}) %all-to-all-start) | async-done | bytes 802848 | tf_op jit(solution)/shard_map/all_to_all | solution.py:589
  29.4 0.2 slice_reduce_fusion.count_ref
  29.6 0.0 copy-done.3
  29.6 5.4 %nonlinear.2 = (f32[3,16,32,128]{3,2,1,0:T(8,128)S(1)}, f32[3,4,32,128]{3,2,1,0:T(8,128)S(1)}, f32[3,4,32,128]{3,2,1,0:T(8,128)S(1)}) custom-call(s32[8]{0:T(128)S(1)} %copy-done.3, s32[16,8]{1,0:T(8,128)S(1)} %bitcast.32, s32[16]{0:T(128)S(1)} %slice_reduce_fusion.count_ref, f32[4,392,128]{2,1,0:T(8,128)S(1)} %all-to-all-done.refs_0_, ...), custom_call_target="tpu_custom_call" | custom-call | bytes 25165824 | tf_op jit(solution)/shard_map/nonlinear/pallas_call | solution.py:343
  35.0 0.1 collective-permute-start
  35.1 1.4 collective-permute-done
  36.6 1.6 collective-permute-start.1
  38.1 5.5 %collective-permute-done.1 = f32[3,4,32,128]{3,2,1,0:T(8,128)S(1)} collective-permute-done((f32[3,4,32,128]{3,2,1,0:T(8,128)S(1)}, f32[3,4,32,128]{3,2,1,0:T(8,128)S(1)}, u32[]{:S(2)}, u32[]{:S(2)}) %collective-permute-start.1) | collective-permute-done | bytes 196640 | tf_op jit(solution)/shard_map/ppermute | solution.py:566
  43.6 0.1 collective-permute-start.2
  43.7 1.4 collective-permute-done.2.other_ref
  45.1 1.8 %outgoing.2 = f32[1536,128]{1,0:T(8,128)} custom-call(s32[8]{0:T(128)S(1)} %copy-done.3, s32[16]{0:T(128)S(1)} %slice_reduce_fusion.count_ref, f32[3,16,32,128]{3,2,1,0:T(8,128)S(1)} %get-tuple-element.40.slotted_ref, f32[3,4,32,128]{3,2,1,0:T(8,128)S(1)} %add.13.kept_ref, f32[3,4,32,128]{3,2,1,0:T(8,128)S(1)} %collective-permute-done.2.other_ref, ...), custom_call_target="tpu_custom_call" | custom-call | bytes 1572864 | tf_op jit(solution)/shard_map/outgoing/pallas_call | solution.py:411
  46.9 3.7 %all-to-all-start.1 = ((f32[8,8,24,128]{3,2,1,0:T(8,128)}), f32[8,8,24,128]{3,2,1,0:T(8,128)S(1)}, u32[]{:S(2)}, u32[]{:S(2)}) async-start(f32[8,8,24,128]{3,2,1,0:T(8,128)} %bitcast.2), calls=%async_computation.1 | async-start | bytes 1572864 | tf_op jit(solution)/shard_map/all_to_all | solution.py:614
  50.6 0.0 copy-done.7
  50.6 2.0 %collective-permute-start.3 = (f32[384,128]{1,0:T(8,128)S(1)}, f32[384,128]{1,0:T(8,128)S(1)}, u32[]{:S(2)}, u32[]{:S(2)}) collective-permute-start(f32[384,128]{1,0:T(8,128)S(1)} %copy-done.7), channel_id=1, source_target_pairs={{0,8},{1,25},{2,10},{3,27},{8,0},{9,17},{10,2},{11,19},{16,24},{17... | collective-permute-start | bytes 589832 | tf_op jit(solution)/shard_map/ppermute | solution.py:560
  52.7 2.4 %collective-permute-start.4 = (f32[384,128]{1,0:T(8,128)S(1)}, f32[384,128]{1,0:T(8,128)S(1)}, u32[]{:S(2)}, u32[]{:S(2)}) collective-permute-start(f32[384,128]{1,0:T(8,128)S(1)} %copy-done.6), channel_id=1, source_target_pairs={{0,24},{1,9},{2,26},{3,11},{8,16},{9,1},{10,18},{11,3},{16,8},{17,... | collective-permute-start | bytes 589832 | tf_op jit(solution)/shard_map/ppermute | solution.py:560
  55.0 0.1 collective-permute-start.5
  55.1 13.9 %collective-permute-done.3.refs_1_ = f32[384,128]{1,0:T(8,128)S(1)} collective-permute-done((f32[384,128]{1,0:T(8,128)S(1)}, f32[384,128]{1,0:T(8,128)S(1)}, u32[]{:S(2)}, u32[]{:S(2)}) %collective-permute-start.3) | collective-permute-done | bytes 196640 | tf_op jit(solution)/shard_map/ppermute | solution.py:560
  69.0 8.4 %collective-permute-done.4.refs_2_ = f32[384,128]{1,0:T(8,128)S(1)} collective-permute-done((f32[384,128]{1,0:T(8,128)S(1)}, f32[384,128]{1,0:T(8,128)S(1)}, u32[]{:S(2)}, u32[]{:S(2)}) %collective-permute-start.4) | collective-permute-done | bytes 196640 | tf_op jit(solution)/shard_map/ppermute | solution.py:560
  77.4 10.6 %collective-permute-done.5.refs_3_ = f32[384,128]{1,0:T(8,128)S(1)} collective-permute-done((f32[384,128]{1,0:T(8,128)S(1)}, f32[384,128]{1,0:T(8,128)S(1)}, u32[]{:S(2)}, u32[]{:S(2)}) %collective-permute-start.5) | collective-permute-done | bytes 196640 | tf_op jit(solution)/shard_map/ppermute | solution.py:560
  88.0 5.4 %nonlinear.3 = (f32[3,16,32,128]{3,2,1,0:T(8,128)S(1)}, f32[3,4,32,128]{3,2,1,0:T(8,128)S(1)}, f32[3,4,32,128]{3,2,1,0:T(8,128)S(1)}) custom-call(s32[8]{0:T(128)S(1)} %copy-done.3, s32[16,8]{1,0:T(8,128)S(1)} %bitcast.33, s32[16]{0:T(128)S(1)} %slice_reduce_fusion.count_ref, f32[384,128]{1,0:T(8,128)S(1)} %copy-done.1, ...), custom_call_target="tpu_custom_call" | custom-call | bytes 25165824 | tf_op jit(solution)/shard_map/nonlinear/pallas_call | solution.py:343
  93.4 0.1 collective-permute-start.6
  93.5 1.4 collective-permute-done.6
  94.9 1.6 collective-permute-start.7
  96.5 5.5 %collective-permute-done.7 = f32[3,4,32,128]{3,2,1,0:T(8,128)S(1)} collective-permute-done((f32[3,4,32,128]{3,2,1,0:T(8,128)S(1)}, f32[3,4,32,128]{3,2,1,0:T(8,128)S(1)}, u32[]{:S(2)}, u32[]{:S(2)}) %collective-permute-start.7) | collective-permute-done | bytes 196640 | tf_op jit(solution)/shard_map/ppermute | solution.py:566
  102.0 0.1 collective-permute-start.8
  102.0 1.4 collective-permute-done.8.other_ref
  103.5 1.1 outgoing.3
  104.6 0.1 collective-permute-start.9
  104.6 1.5 collective-permute-start.10
  106.1 1.9 %collective-permute-start.11 = (f32[8,24,128]{2,1,0:T(8,128)S(1)}, f32[8,24,128]{2,1,0:T(8,128)S(1)}, u32[]{:S(2)}, u32[]{:S(2)}) collective-permute-start(f32[8,24,128]{2,1,0:T(8,128)S(1)} %bitcast.39), channel_id=1, source_target_pairs={{0,8},{1,25},{2,10},{3,27},{4,12},{5,29},{6,14},{7,31},{8,0},{9,17... | collective-permute-start | bytes 294920 | tf_op jit(solution)/shard_map/ppermute | solution.py:560
  108.1 2.4 %collective-permute-start.12 = (f32[8,24,128]{2,1,0:T(8,128)S(1)}, f32[8,24,128]{2,1,0:T(8,128)S(1)}, u32[]{:S(2)}, u32[]{:S(2)}) collective-permute-start(f32[8,24,128]{2,1,0:T(8,128)S(1)} %bitcast.38), channel_id=1, source_target_pairs={{0,24},{1,9},{2,26},{3,11},{4,28},{5,13},{6,30},{7,15},{8,16},{9,1... | collective-permute-start | bytes 294920 | tf_op jit(solution)/shard_map/ppermute | solution.py:560
  110.4 0.0 collective-permute-start.13
  110.4 2.4 %collective-permute-done.9.refs_2_ = f32[8,24,128]{2,1,0:T(8,128)S(1)} collective-permute-done((f32[8,24,128]{2,1,0:T(8,128)S(1)}, f32[8,24,128]{2,1,0:T(8,128)S(1)}, u32[]{:S(2)}, u32[]{:S(2)}) %collective-permute-start.9) | collective-permute-done | bytes 98336 | tf_op jit(solution)/shard_map/ppermute | solution.py:560
  112.8 0.5 collective-permute-start.14
  113.3 0.0 collective-permute-done.10.refs_3_
  113.3 2.7 %collective-permute-start.15 = (f32[8,24,128]{2,1,0:T(8,128)S(1)}, f32[8,24,128]{2,1,0:T(8,128)S(1)}, u32[]{:S(2)}, u32[]{:S(2)}) collective-permute-start(f32[8,24,128]{2,1,0:T(8,128)S(1)} %bitcast.35), channel_id=1, source_target_pairs={{0,28},{1,29},{2,30},{3,31},{4,24},{5,25},{6,26},{7,27},{8,20},{9,... | collective-permute-start | bytes 294920 | tf_op jit(solution)/shard_map/ppermute | solution.py:560
  116.1 0.0 collective-permute-done.11.refs_4_
  116.1 0.3 collective-permute-done.12.refs_5_
  116.4 6.6 %collective-permute-done.13.refs_6_ = f32[8,24,128]{2,1,0:T(8,128)S(1)} collective-permute-done((f32[8,24,128]{2,1,0:T(8,128)S(1)}, f32[8,24,128]{2,1,0:T(8,128)S(1)}, u32[]{:S(2)}, u32[]{:S(2)}) %collective-permute-start.13) | collective-permute-done | bytes 98336 | tf_op jit(solution)/shard_map/ppermute | solution.py:560
  123.0 0.0 collective-permute-done.14.refs_7_
  123.0 0.0 collective-permute-done.15.refs_8_
  123.0 0.0 all-to-all-done.1.refs_0_
  123.0 6.8 %solve.1 = (f32[8,2,24,128]{3,2,1,0:T(8,128)S(1)}, f32[8,2,24,128]{3,2,1,0:T(8,128)S(1)}, f32[8,2,24,128]{3,2,1,0:T(8,128)S(1)}, f32[8,2,24,128]{3,2,1,0:T(8,128...) custom-call(f32[8,8,24,128]{3,2,1,0:T(8,128)S(1)} %all-to-all-done.1, ...), custom_call_target="tpu_custom_call" | custom-call | bytes 8388608 | tf_op jit(solution)/shard_map/solve/pallas_call | solution.py:494
  129.8 3.7 %collective-permute-start.16 = (f32[8,2,24,128]{3,2,1,0:T(8,128)S(1)}, f32[8,2,24,128]{3,2,1,0:T(8,128)S(1)}, u32[]{:S(2)}, u32[]{:S(2)}) collective-permute-start(f32[8,2,24,128]{3,2,1,0:T(8,128)S(1)} %get-tuple-element.59), channel_id=1, source_target_pairs={{0,16},{1,5},{2,18},{3,7},{4,20},{5,1},{6,22},{7,3},{8,24},{9,13},... | collective-permute-start | bytes 589832 | tf_op jit(solution)/shard_map/ppermute | solution.py:560
  133.5 0.8 collective-permute-start.17
  134.3 0.0 collective-permute-start.18
  134.3 1.5 collective-permute-start.19
  135.9 2.6 %collective-permute-start.20 = (f32[8,2,24,128]{3,2,1,0:T(8,128)S(1)}, f32[8,2,24,128]{3,2,1,0:T(8,128)S(1)}, u32[]{:S(2)}, u32[]{:S(2)}) collective-permute-start(f32[8,2,24,128]{3,2,1,0:T(8,128)S(1)} %get-tuple-element.63), channel_id=1, source_target_pairs={{0,20},{1,13},{2,22},{3,15},{4,16},{5,9},{6,18},{7,11},{8,28},{9,5... | collective-permute-start | bytes 589832 | tf_op jit(solution)/shard_map/ppermute | solution.py:560
  138.5 8.0 %collective-permute-done.16 = f32[8,2,24,128]{3,2,1,0:T(8,128)S(1)} collective-permute-done((f32[8,2,24,128]{3,2,1,0:T(8,128)S(1)}, f32[8,2,24,128]{3,2,1,0:T(8,128)S(1)}, u32[]{:S(2)}, u32[]{:S(2)}) %collective-permute-start.16) | collective-permute-done | bytes 196640 | tf_op jit(solution)/shard_map/ppermute | solution.py:560
  146.5 0.0 collective-permute-start.21
  146.5 0.0 collective-permute-done.17
  146.5 1.6 collective-permute-start.22
  148.1 1.2 collective-permute-done.18
  149.3 0.0 collective-permute-done.19
  149.3 15.2 %collective-permute-done.20 = f32[8,2,24,128]{3,2,1,0:T(8,128)S(1)} collective-permute-done((f32[8,2,24,128]{3,2,1,0:T(8,128)S(1)}, f32[8,2,24,128]{3,2,1,0:T(8,128)S(1)}, u32[]{:S(2)}, u32[]{:S(2)}) %collective-permute-start.20) | collective-permute-done | bytes 196640 | tf_op jit(solution)/shard_map/ppermute | solution.py:560
  164.5 0.0 collective-permute-done.21
  164.5 0.0 collective-permute-done.22
  164.5 2.1 %restore.1 = f32[3,4,256,128]{3,2,1,0:T(8,128)} custom-call(f32[384,128]{1,0:T(8,128)S(1)} %bitcast.23, f32[384,128]{1,0:T(8,128)S(1)} %bitcast.24, f32[384,128]{1,0:T(8,128)S(1)} %bitcast.25, f32[384,128]{1,0:T(8,128)S(1)} %bitcast.26, f32[384,128]{1,0:T(8,128)S(1)} %bitcast.27, f32[384,128]{1,0:T(8,128)S(1)} %bitcast.28, f32[384,128]{1,0:T(8,128)S(1)} %bitcast.29, ...), custom_call_target="tpu_custom_call" | custom-call | bytes 3145728 | tf_op jit(solution)/shard_map/restore/pallas_call | solution.py:538
  (16 shorter events, 0.1 us)
Async XLA Ops:
  0.0 9.0 %copy-start = (bf16[128,256]{1,0:T(8,128)(2,1)S(1)}, bf16[128,256]{1,0:T(8,128)(2,1)}, u32[]{:S(2)}) copy-start(bf16[128,256]{1,0:T(8,128)(2,1)} %constant.5.clone.rest_ref.refs_2_.refs_5_) | copy-start | bytes 196612
  0.0 9.0 %copy-start.2 = (bf16[128,256]{1,0:T(8,128)(2,1)S(1)}, bf16[128,256]{1,0:T(8,128)(2,1)}, u32[]{:S(2)}) copy-start(bf16[128,256]{1,0:T(8,128)(2,1)} %constant.4.clone.top_ref) | copy-start | bytes 196612
  0.0 9.0 %copy-start.4 = (s32[64]{0:T(128)S(1)}, s32[64]{0:T(128)}, u32[]{:S(2)}) copy-start(s32[64]{0:T(128)} %owner_ref.1) | copy-start | bytes 772
  0.0 29.6 %copy-start.3 = (s32[8]{0:T(128)S(1)}, s32[8]{0:T(128)}, u32[]{:S(2)}) copy-start(s32[8]{0:T(128)} %low_ref.7) | copy-start | bytes 100
  2.6 26.8 %all-to-all-start = ((f32[4,392,128]{2,1,0:T(8,128)}), f32[4,392,128]{2,1,0:T(8,128)S(1)}, u32[]{:S(2)}, u32[]{:S(2)}) async-start(f32[4,392,128]{2,1,0:T(8,128)} %get-tuple-element.36), calls=%async_computation | async-start | bytes 1605632 | tf_op jit(solution)/shard_map/all_to_all | solution.py:589
  35.0 1.5 collective-permute-start
  36.6 7.0 %collective-permute-start.1 = (f32[3,4,32,128]{3,2,1,0:T(8,128)S(1)}, f32[3,4,32,128]{3,2,1,0:T(8,128)S(1)}, u32[]{:S(2)}, u32[]{:S(2)}) collective-permute-start(f32[3,4,32,128]{3,2,1,0:T(8,128)S(1)} %add.12.refs_8_), channel_id=1, source_target_pairs={{0,2},{1,3},{2,0},{3,1},{4,6},{5,7},{6,4},{7,5},{8,10},{9,11},{10,... | collective-permute-start | bytes 589832 | tf_op jit(solution)/shard_map/ppermute | solution.py:566
  43.6 1.5 collective-permute-start.2
  45.1 5.5 %copy-start.7 = (f32[384,128]{1,0:T(8,128)S(1)}, f32[384,128]{1,0:T(8,128)}, u32[]{:S(2)}) copy-start(f32[384,128]{1,0:T(8,128)} %get-tuple-element.44) | copy-start | bytes 589828
  45.1 7.5 %copy-start.6 = (f32[384,128]{1,0:T(8,128)S(1)}, f32[384,128]{1,0:T(8,128)}, u32[]{:S(2)}) copy-start(f32[384,128]{1,0:T(8,128)} %get-tuple-element.45) | copy-start | bytes 589828
  45.1 9.9 %copy-start.5 = (f32[384,128]{1,0:T(8,128)S(1)}, f32[384,128]{1,0:T(8,128)}, u32[]{:S(2)}) copy-start(f32[384,128]{1,0:T(8,128)} %get-tuple-element.46) | copy-start | bytes 589828
  45.1 42.9 %copy-start.1 = (f32[384,128]{1,0:T(8,128)S(1)}, f32[384,128]{1,0:T(8,128)}, u32[]{:S(2)}) copy-start(f32[384,128]{1,0:T(8,128)} %get-tuple-element.43.refs_0_) | copy-start | bytes 589828
  46.9 76.0 %all-to-all-start.1 = ((f32[8,8,24,128]{3,2,1,0:T(8,128)}), f32[8,8,24,128]{3,2,1,0:T(8,128)S(1)}, u32[]{:S(2)}, u32[]{:S(2)}) async-start(f32[8,8,24,128]{3,2,1,0:T(8,128)} %bitcast.2), calls=%async_computation.1 | async-start | bytes 1572864 | tf_op jit(solution)/shard_map/all_to_all | solution.py:614
  50.6 18.3 %collective-permute-start.3 = (f32[384,128]{1,0:T(8,128)S(1)}, f32[384,128]{1,0:T(8,128)S(1)}, u32[]{:S(2)}, u32[]{:S(2)}) collective-permute-start(f32[384,128]{1,0:T(8,128)S(1)} %copy-done.7), channel_id=1, source_target_pairs={{0,8},{1,25},{2,10},{3,27},{8,0},{9,17},{10,2},{11,19},{16,24},{17... | collective-permute-start | bytes 589832 | tf_op jit(solution)/shard_map/ppermute | solution.py:560
  52.7 24.7 %collective-permute-start.4 = (f32[384,128]{1,0:T(8,128)S(1)}, f32[384,128]{1,0:T(8,128)S(1)}, u32[]{:S(2)}, u32[]{:S(2)}) collective-permute-start(f32[384,128]{1,0:T(8,128)S(1)} %copy-done.6), channel_id=1, source_target_pairs={{0,24},{1,9},{2,26},{3,11},{8,16},{9,1},{10,18},{11,3},{16,8},{17,... | collective-permute-start | bytes 589832 | tf_op jit(solution)/shard_map/ppermute | solution.py:560
  55.0 33.0 %collective-permute-start.5 = (f32[384,128]{1,0:T(8,128)S(1)}, f32[384,128]{1,0:T(8,128)S(1)}, u32[]{:S(2)}, u32[]{:S(2)}) collective-permute-start(f32[384,128]{1,0:T(8,128)S(1)} %copy-done.5), channel_id=1, source_target_pairs={{0,16},{1,17},{2,18},{3,19},{8,24},{9,25},{10,26},{11,27},{16,0},{... | collective-permute-start | bytes 589832 | tf_op jit(solution)/shard_map/ppermute | solution.py:560
  93.4 1.5 collective-permute-start.6
  94.9 7.0 %collective-permute-start.7 = (f32[3,4,32,128]{3,2,1,0:T(8,128)S(1)}, f32[3,4,32,128]{3,2,1,0:T(8,128)S(1)}, u32[]{:S(2)}, u32[]{:S(2)}) collective-permute-start(f32[3,4,32,128]{3,2,1,0:T(8,128)S(1)} %add.14), channel_id=1, source_target_pairs={{0,2},{1,3},{2,0},{3,1},{4,6},{5,7},{6,4},{7,5},{8,10},{9,11},{10,... | collective-permute-start | bytes 589832 | tf_op jit(solution)/shard_map/ppermute | solution.py:566
  102.0 1.5 collective-permute-start.8
  104.6 8.3 %collective-permute-start.9 = (f32[8,24,128]{2,1,0:T(8,128)S(1)}, f32[8,24,128]{2,1,0:T(8,128)S(1)}, u32[]{:S(2)}, u32[]{:S(2)}) collective-permute-start(f32[8,24,128]{2,1,0:T(8,128)S(1)} %bitcast.41), channel_id=1, source_target_pairs={{0,16},{1,5},{2,18},{3,7},{4,20},{5,1},{6,22},{7,3},{8,24},{9,13},... | collective-permute-start | bytes 294920 | tf_op jit(solution)/shard_map/ppermute | solution.py:560
  104.6 8.7 %collective-permute-start.10 = (f32[8,24,128]{2,1,0:T(8,128)S(1)}, f32[8,24,128]{2,1,0:T(8,128)S(1)}, u32[]{:S(2)}, u32[]{:S(2)}) collective-permute-start(f32[8,24,128]{2,1,0:T(8,128)S(1)} %bitcast.40), channel_id=1, source_target_pairs={{0,4},{1,17},{2,6},{3,19},{4,0},{5,21},{6,2},{7,23},{8,12},{9,25},... | collective-permute-start | bytes 294920 | tf_op jit(solution)/shard_map/ppermute | solution.py:560
  106.1 10.0 %collective-permute-start.11 = (f32[8,24,128]{2,1,0:T(8,128)S(1)}, f32[8,24,128]{2,1,0:T(8,128)S(1)}, u32[]{:S(2)}, u32[]{:S(2)}) collective-permute-start(f32[8,24,128]{2,1,0:T(8,128)S(1)} %bitcast.39), channel_id=1, source_target_pairs={{0,8},{1,25},{2,10},{3,27},{4,12},{5,29},{6,14},{7,31},{8,0},{9,17... | collective-permute-start | bytes 294920 | tf_op jit(solution)/shard_map/ppermute | solution.py:560
  108.1 8.3 %collective-permute-start.12 = (f32[8,24,128]{2,1,0:T(8,128)S(1)}, f32[8,24,128]{2,1,0:T(8,128)S(1)}, u32[]{:S(2)}, u32[]{:S(2)}) collective-permute-start(f32[8,24,128]{2,1,0:T(8,128)S(1)} %bitcast.38), channel_id=1, source_target_pairs={{0,24},{1,9},{2,26},{3,11},{4,28},{5,13},{6,30},{7,15},{8,16},{9,1... | collective-permute-start | bytes 294920 | tf_op jit(solution)/shard_map/ppermute | solution.py:560
  110.4 12.5 %collective-permute-start.13 = (f32[8,24,128]{2,1,0:T(8,128)S(1)}, f32[8,24,128]{2,1,0:T(8,128)S(1)}, u32[]{:S(2)}, u32[]{:S(2)}) collective-permute-start(f32[8,24,128]{2,1,0:T(8,128)S(1)} %bitcast.37), channel_id=1, source_target_pairs={{0,20},{1,13},{2,22},{3,15},{4,16},{5,9},{6,18},{7,11},{8,28},{9,5... | collective-permute-start | bytes 294920 | tf_op jit(solution)/shard_map/ppermute | solution.py:560
  112.8 10.1 %collective-permute-start.14 = (f32[8,24,128]{2,1,0:T(8,128)S(1)}, f32[8,24,128]{2,1,0:T(8,128)S(1)}, u32[]{:S(2)}, u32[]{:S(2)}) collective-permute-start(f32[8,24,128]{2,1,0:T(8,128)S(1)} %bitcast.36), channel_id=1, source_target_pairs={{0,12},{1,21},{2,14},{3,23},{4,8},{5,17},{6,10},{7,19},{8,4},{9,29... | collective-permute-start | bytes 294920 | tf_op jit(solution)/shard_map/ppermute | solution.py:560
  113.3 9.6 %collective-permute-start.15 = (f32[8,24,128]{2,1,0:T(8,128)S(1)}, f32[8,24,128]{2,1,0:T(8,128)S(1)}, u32[]{:S(2)}, u32[]{:S(2)}) collective-permute-start(f32[8,24,128]{2,1,0:T(8,128)S(1)} %bitcast.35), channel_id=1, source_target_pairs={{0,28},{1,29},{2,30},{3,31},{4,24},{5,25},{6,26},{7,27},{8,20},{9,... | collective-permute-start | bytes 294920 | tf_op jit(solution)/shard_map/ppermute | solution.py:560
  129.8 16.7 %collective-permute-start.16 = (f32[8,2,24,128]{3,2,1,0:T(8,128)S(1)}, f32[8,2,24,128]{3,2,1,0:T(8,128)S(1)}, u32[]{:S(2)}, u32[]{:S(2)}) collective-permute-start(f32[8,2,24,128]{3,2,1,0:T(8,128)S(1)} %get-tuple-element.59), channel_id=1, source_target_pairs={{0,16},{1,5},{2,18},{3,7},{4,20},{5,1},{6,22},{7,3},{8,24},{9,13},... | collective-permute-start | bytes 589832 | tf_op jit(solution)/shard_map/ppermute | solution.py:560
  133.5 13.0 %collective-permute-start.17 = (f32[8,2,24,128]{3,2,1,0:T(8,128)S(1)}, f32[8,2,24,128]{3,2,1,0:T(8,128)S(1)}, u32[]{:S(2)}, u32[]{:S(2)}) collective-permute-start(f32[8,2,24,128]{3,2,1,0:T(8,128)S(1)} %get-tuple-element.60), channel_id=1, source_target_pairs={{0,4},{1,17},{2,6},{3,19},{4,0},{5,21},{6,2},{7,23},{8,12},{9,25},... | collective-permute-start | bytes 589832 | tf_op jit(solution)/shard_map/ppermute | solution.py:560
  134.3 15.0 %collective-permute-start.18 = (f32[8,2,24,128]{3,2,1,0:T(8,128)S(1)}, f32[8,2,24,128]{3,2,1,0:T(8,128)S(1)}, u32[]{:S(2)}, u32[]{:S(2)}) collective-permute-start(f32[8,2,24,128]{3,2,1,0:T(8,128)S(1)} %get-tuple-element.61), channel_id=1, source_target_pairs={{0,8},{1,25},{2,10},{3,27},{4,12},{5,29},{6,14},{7,31},{8,0},{9,17... | collective-permute-start | bytes 589832 | tf_op jit(solution)/shard_map/ppermute | solution.py:560
  134.3 15.0 %collective-permute-start.19 = (f32[8,2,24,128]{3,2,1,0:T(8,128)S(1)}, f32[8,2,24,128]{3,2,1,0:T(8,128)S(1)}, u32[]{:S(2)}, u32[]{:S(2)}) collective-permute-start(f32[8,2,24,128]{3,2,1,0:T(8,128)S(1)} %get-tuple-element.62), channel_id=1, source_target_pairs={{0,24},{1,9},{2,26},{3,11},{4,28},{5,13},{6,30},{7,15},{8,16},{9,1... | collective-permute-start | bytes 589832 | tf_op jit(solution)/shard_map/ppermute | solution.py:560
  135.9 28.6 %collective-permute-start.20 = (f32[8,2,24,128]{3,2,1,0:T(8,128)S(1)}, f32[8,2,24,128]{3,2,1,0:T(8,128)S(1)}, u32[]{:S(2)}, u32[]{:S(2)}) collective-permute-start(f32[8,2,24,128]{3,2,1,0:T(8,128)S(1)} %get-tuple-element.63), channel_id=1, source_target_pairs={{0,20},{1,13},{2,22},{3,15},{4,16},{5,9},{6,18},{7,11},{8,28},{9,5... | collective-permute-start | bytes 589832 | tf_op jit(solution)/shard_map/ppermute | solution.py:560
  146.5 18.0 %collective-permute-start.21 = (f32[8,2,24,128]{3,2,1,0:T(8,128)S(1)}, f32[8,2,24,128]{3,2,1,0:T(8,128)S(1)}, u32[]{:S(2)}, u32[]{:S(2)}) collective-permute-start(f32[8,2,24,128]{3,2,1,0:T(8,128)S(1)} %get-tuple-element.64), channel_id=1, source_target_pairs={{0,12},{1,21},{2,14},{3,23},{4,8},{5,17},{6,10},{7,19},{8,4},{9,29... | collective-permute-start | bytes 589832 | tf_op jit(solution)/shard_map/ppermute | solution.py:560
  146.5 18.0 %collective-permute-start.22 = (f32[8,2,24,128]{3,2,1,0:T(8,128)S(1)}, f32[8,2,24,128]{3,2,1,0:T(8,128)S(1)}, u32[]{:S(2)}, u32[]{:S(2)}) collective-permute-start(f32[8,2,24,128]{3,2,1,0:T(8,128)S(1)} %get-tuple-element.65), channel_id=1, source_target_pairs={{0,28},{1,29},{2,30},{3,31},{4,24},{5,25},{6,26},{7,27},{8,20},{9,... | collective-permute-start | bytes 589832 | tf_op jit(solution)/shard_map/ppermute | solution.py:560

commit v8 on v6

--- a/solution.py
+++ b/solution.py
@@ -236,7 +236,7 @@
         in_specs=[SMEM, VMEM, VMEM],
         out_specs=(VMEM,) * 4,
         compiler_params=params(),
-        cost_estimate=cost(16 * points * columns),
+        cost_estimate=cost(640 * points * columns),
         name="tables",
     )(owner_map, top, rest)
     return (first, rest, back), order, slot_modes

time: 152 us -> 152 us (level)
  no operation moved by 1% of the time
where the time goes in v8:
time: 152 us; the launch traced here: 149 us
  waiting for transfers between devices  78.5 us (52%)
  starting transfers between devices  43.7 us (29%)
  Pallas kernels  25.9 us (17%)
    ppermute x17, waiting for transfers between devices, exchange(): result[position] = lax.ppermute(blocks[position], axes + ('real',), pairs)  61.9 us
    ppermute x17, starting transfers between devices, exchange(): result[position] = lax.ppermute(blocks[position], axes + ('real',), pairs)  30.2 us
    ppermute x6, waiting for transfers between devices, swap(): return lax.ppermute(value, 'real', pairs)  16.6 us
    pallas_call x2, Pallas kernels, nonlinear(): pl.pallas_call(nonlinear_kernel, out_shape=(jax.ShapeDtypeStruct((compone...  10.8 us
    pallas_call x1, Pallas kernels, solve(): pl.pallas_call(functools.partial(solve_kernel, groups=groups, kx_count=kx...  6.81 us
    all_to_all x1, starting transfers between devices, local(): lax.all_to_all(block, 'kx', split_axis=0, concat_axis=0, tiled=True)  6.48 us
    all_to_all x1, starting transfers between devices, local(): lax.all_to_all(block, ('kx', 'ht'), split_axis=0, concat_axis=0, tiled=True)  3.69 us
    ppermute x6, starting transfers between devices, swap(): return lax.ppermute(value, 'real', pairs)  3.39 us
  transfers between devices with their start and end apart: 25, of which 13 were waited for; matrix products, arithmetic and copies ran while one was open for 1% of the time, Pallas kernels for 10%

profile of v8, /device:TPU:0, one launch (start us, length us, event | category | flops | bytes accessed | tf_op | source)
XLA Modules:
  0.0 149.5 jit_solution(5362096025807866889)
XLA Ops:
  0.0 2.6 %pack.1 = (f32[392,128]{1,0:T(8,128)}, f32[392,128]{1,0:T(8,128)}, f32[392,128]{1,0:T(8,128)}, f32[392,128]{1,0:T(8,128)}, f32[4,384,128]{2,1,0:T(8,128)}) custom-call(s32[4,8]{1,0:T(4,128)} %near_ref.1, s32[4]{0:T(128)} %count_ref.1, f32[12,2,4,32,128]{4,3,2,1,0:T(8,128)} %bitcast.44), custom_call_target="tpu_custom_call" | custom-call | bytes 3145728 | tf_op jit(solution)/shard_map/pack/pallas_call | solution.py:181
  2.7 6.5 %all-to-all-start.1 = ((f32[4,384,128]{2,1,0:T(8,128)}), f32[4,384,128]{2,1,0:T(8,128)S(1)}, u32[]{:S(2)}, u32[]{:S(2)}) async-start(f32[4,384,128]{2,1,0:T(8,128)} %get-tuple-element.46), calls=%async_computation.1 | async-start | bytes 1572864 | tf_op jit(solution)/shard_map/all_to_all | solution.py:590
  9.2 2.0 %collective-permute-start = (f32[392,128]{1,0:T(8,128)S(1)}, f32[392,128]{1,0:T(8,128)S(1)}, u32[]{:S(2)}, u32[]{:S(2)}) collective-permute-start(f32[392,128]{1,0:T(8,128)S(1)} %copy-done.7), channel_id=1, source_target_pairs={{0,8},{1,25},{2,10},{3,27},{8,0},{9,17},{10,2},{11,19},{16,24},{17... | collective-permute-start | bytes 602120 | tf_op jit(solution)/shard_map/ppermute | solution.py:560
  11.2 2.4 %collective-permute-start.1 = (f32[392,128]{1,0:T(8,128)S(1)}, f32[392,128]{1,0:T(8,128)S(1)}, u32[]{:S(2)}, u32[]{:S(2)}) collective-permute-start(f32[392,128]{1,0:T(8,128)S(1)} %copy-done.6), channel_id=1, source_target_pairs={{0,24},{1,9},{2,26},{3,11},{8,16},{9,1},{10,18},{11,3},{16,8},{17,... | collective-permute-start | bytes 602120 | tf_op jit(solution)/shard_map/ppermute | solution.py:560
  13.5 0.1 collective-permute-start.2
  13.6 0.1 broadcast_in_dim.85
  13.7 0.1 broadcast_in_dim.86
  13.8 0.1 broadcast_in_dim.91
  13.9 0.1 broadcast_in_dim.92
  14.0 0.1 broadcast_in_dim.96
  14.0 0.1 broadcast_in_dim.97
  14.1 0.1 broadcast_in_dim.101
  14.2 0.1 broadcast_in_dim.102
  14.3 0.8 tables.1
  15.1 12.3 %collective-permute-done.refs_1_ = f32[392,128]{1,0:T(8,128)S(1)} collective-permute-done((f32[392,128]{1,0:T(8,128)S(1)}, f32[392,128]{1,0:T(8,128)S(1)}, u32[]{:S(2)}, u32[]{:S(2)}) %collective-permute-start) | collective-permute-done | bytes 200736 | tf_op jit(solution)/shard_map/ppermute | solution.py:560
  27.4 8.7 %collective-permute-done.1.refs_2_ = f32[392,128]{1,0:T(8,128)S(1)} collective-permute-done((f32[392,128]{1,0:T(8,128)S(1)}, f32[392,128]{1,0:T(8,128)S(1)}, u32[]{:S(2)}, u32[]{:S(2)}) %collective-permute-start.1) | collective-permute-done | bytes 200736 | tf_op jit(solution)/shard_map/ppermute | solution.py:560
  36.2 10.3 %collective-permute-done.2.refs_3_ = f32[392,128]{1,0:T(8,128)S(1)} collective-permute-done((f32[392,128]{1,0:T(8,128)S(1)}, f32[392,128]{1,0:T(8,128)S(1)}, u32[]{:S(2)}, u32[]{:S(2)}) %collective-permute-start.2) | collective-permute-done | bytes 200736 | tf_op jit(solution)/shard_map/ppermute | solution.py:560
  46.5 0.1 add_convert_fusion
  46.6 0.2 slice_reduce_fusion.count_ref
  46.8 5.4 %nonlinear.2 = (f32[3,16,32,128]{3,2,1,0:T(8,128)S(1)}, f32[3,4,32,128]{3,2,1,0:T(8,128)S(1)}, f32[3,4,32,128]{3,2,1,0:T(8,128)S(1)}) custom-call(s32[8]{0:T(128)S(1)} %copy-done.3, s32[16,8]{1,0:T(8,128)S(1)} %bitcast.34, s32[16]{0:T(128)S(1)} %slice_reduce_fusion.count_ref, f32[392,128]{1,0:T(8,128)S(1)} %copy-done.1, ...), custom_call_target="tpu_custom_call" | custom-call | bytes 25165824 | tf_op jit(solution)/shard_map/nonlinear/pallas_call | solution.py:343
  52.2 0.1 collective-permute-start.3
  52.2 1.4 collective-permute-done.3
  53.7 1.5 %collective-permute-start.4 = (f32[3,4,32,128]{3,2,1,0:T(8,128)S(1)}, f32[3,4,32,128]{3,2,1,0:T(8,128)S(1)}, u32[]{:S(2)}, u32[]{:S(2)}) collective-permute-start(f32[3,4,32,128]{3,2,1,0:T(8,128)S(1)} %add.27.refs_5_), channel_id=1, source_target_pairs={{0,2},{1,3},{2,0},{3,1},{4,6},{5,7},{6,4},{7,5},{8,10},{9,11},{10,... | collective-permute-start | bytes 589832 | tf_op jit(solution)/shard_map/ppermute | solution.py:566
  55.2 5.5 %collective-permute-done.4 = f32[3,4,32,128]{3,2,1,0:T(8,128)S(1)} collective-permute-done((f32[3,4,32,128]{3,2,1,0:T(8,128)S(1)}, f32[3,4,32,128]{3,2,1,0:T(8,128)S(1)}, u32[]{:S(2)}, u32[]{:S(2)}) %collective-permute-start.4) | collective-permute-done | bytes 196640 | tf_op jit(solution)/shard_map/ppermute | solution.py:566
  60.7 0.1 collective-permute-start.5
  60.8 1.4 collective-permute-done.5.other_ref
  62.2 1.8 %outgoing.2 = f32[1536,128]{1,0:T(8,128)} custom-call(s32[8]{0:T(128)S(1)} %copy-done.3, s32[16]{0:T(128)S(1)} %slice_reduce_fusion.count_ref, f32[3,16,32,128]{3,2,1,0:T(8,128)S(1)} %get-tuple-element.43.slotted_ref, f32[3,4,32,128]{3,2,1,0:T(8,128)S(1)} %add.28.kept_ref, f32[3,4,32,128]{3,2,1,0:T(8,128)S(1)} %collective-permute-done.5.other_ref, ...), custom_call_target="tpu_custom_call" | custom-call | bytes 1572864 | tf_op jit(solution)/shard_map/outgoing/pallas_call | solution.py:411
  64.1 0.0 all-to-all-done.1.refs_0_
  64.1 3.7 %all-to-all-start = ((f32[8,8,24,128]{3,2,1,0:T(8,128)}), f32[8,8,24,128]{3,2,1,0:T(8,128)S(1)}, u32[]{:S(2)}, u32[]{:S(2)}) async-start(f32[8,8,24,128]{3,2,1,0:T(8,128)} %bitcast.5), calls=%async_computation | async-start | bytes 1572864 | tf_op jit(solution)/shard_map/all_to_all | solution.py:619
  67.7 5.4 %nonlinear.3 = (f32[3,16,32,128]{3,2,1,0:T(8,128)S(1)}, f32[3,4,32,128]{3,2,1,0:T(8,128)S(1)}, f32[3,4,32,128]{3,2,1,0:T(8,128)S(1)}) custom-call(s32[8]{0:T(128)S(1)} %copy-done.3, s32[16,8]{1,0:T(8,128)S(1)} %bitcast.35, s32[16]{0:T(128)S(1)} %slice_reduce_fusion.count_ref, f32[4,384,128]{2,1,0:T(8,128)S(1)} %all-to-all-done.1.refs_0_, ...), custom_call_target="tpu_custom_call" | custom-call | bytes 25165824 | tf_op jit(solution)/shard_map/nonlinear/pallas_call | solution.py:343
  73.1 0.1 collective-permute-start.6
  73.2 1.4 collective-permute-done.6
  74.7 1.6 %collective-permute-start.7 = (f32[3,4,32,128]{3,2,1,0:T(8,128)S(1)}, f32[3,4,32,128]{3,2,1,0:T(8,128)S(1)}, u32[]{:S(2)}, u32[]{:S(2)}) collective-permute-start(f32[3,4,32,128]{3,2,1,0:T(8,128)S(1)} %add.29), channel_id=1, source_target_pairs={{0,2},{1,3},{2,0},{3,1},{4,6},{5,7},{6,4},{7,5},{8,10},{9,11},{10,... | collective-permute-start | bytes 589832 | tf_op jit(solution)/shard_map/ppermute | solution.py:566
  76.2 5.5 %collective-permute-done.7 = f32[3,4,32,128]{3,2,1,0:T(8,128)S(1)} collective-permute-done((f32[3,4,32,128]{3,2,1,0:T(8,128)S(1)}, f32[3,4,32,128]{3,2,1,0:T(8,128)S(1)}, u32[]{:S(2)}, u32[]{:S(2)}) %collective-permute-start.7) | collective-permute-done | bytes 196640 | tf_op jit(solution)/shard_map/ppermute | solution.py:566
  81.7 0.1 collective-permute-start.8
  81.8 1.4 collective-permute-done.8.other_ref
  83.2 1.1 outgoing.3
  84.3 3.0 %collective-permute-start.9 = (f32[8,24,128]{2,1,0:T(8,128)S(1)}, f32[8,24,128]{2,1,0:T(8,128)S(1)}, u32[]{:S(2)}, u32[]{:S(2)}) collective-permute-start(f32[8,24,128]{2,1,0:T(8,128)S(1)} %bitcast.43), channel_id=1, source_target_pairs={{0,16},{1,5},{2,18},{3,7},{4,20},{5,1},{6,22},{7,3},{8,24},{9,13},... | collective-permute-start | bytes 294920 | tf_op jit(solution)/shard_map/ppermute | solution.py:560
  87.3 1.5 collective-permute-start.10
  88.7 1.5 collective-permute-start.11
  90.2 0.6 collective-permute-start.12
  90.8 1.5 collective-permute-start.13
  92.2 0.0 collective-permute-done.9.refs_2_
  92.2 3.7 %collective-permute-start.14 = (f32[8,24,128]{2,1,0:T(8,128)S(1)}, f32[8,24,128]{2,1,0:T(8,128)S(1)}, u32[]{:S(2)}, u32[]{:S(2)}) collective-permute-start(f32[8,24,128]{2,1,0:T(8,128)S(1)} %bitcast.38), channel_id=1, source_target_pairs={{0,12},{1,21},{2,14},{3,23},{4,8},{5,17},{6,10},{7,19},{8,4},{9,29... | collective-permute-start | bytes 294920 | tf_op jit(solution)/shard_map/ppermute | solution.py:560
  95.9 0.0 collective-permute-done.10.refs_3_
  95.9 3.2 %collective-permute-start.15 = (f32[8,24,128]{2,1,0:T(8,128)S(1)}, f32[8,24,128]{2,1,0:T(8,128)S(1)}, u32[]{:S(2)}, u32[]{:S(2)}) collective-permute-start(f32[8,24,128]{2,1,0:T(8,128)S(1)} %bitcast.37), channel_id=1, source_target_pairs={{0,28},{1,29},{2,30},{3,31},{4,24},{5,25},{6,26},{7,27},{8,20},{9,... | collective-permute-start | bytes 294920 | tf_op jit(solution)/shard_map/ppermute | solution.py:560
  99.1 0.0 collective-permute-done.11.refs_4_
  99.1 0.0 collective-permute-done.12.refs_5_
  99.1 5.9 %collective-permute-done.13.refs_6_ = f32[8,24,128]{2,1,0:T(8,128)S(1)} collective-permute-done((f32[8,24,128]{2,1,0:T(8,128)S(1)}, f32[8,24,128]{2,1,0:T(8,128)S(1)}, u32[]{:S(2)}, u32[]{:S(2)}) %collective-permute-start.13) | collective-permute-done | bytes 98336 | tf_op jit(solution)/shard_map/ppermute | solution.py:560
  105.0 0.0 collective-permute-done.14.refs_7_
  105.0 0.0 collective-permute-done.15.refs_8_
  105.0 0.0 all-to-all-done.refs_0_
  105.0 6.8 %solve.1 = (f32[8,2,24,128]{3,2,1,0:T(8,128)S(1)}, f32[8,2,24,128]{3,2,1,0:T(8,128)S(1)}, f32[8,2,24,128]{3,2,1,0:T(8,128)S(1)}, f32[8,2,24,128]{3,2,1,0:T(8,128...) custom-call(f32[8,8,24,128]{3,2,1,0:T(8,128)S(1)} %all-to-all-done.r, ...), custom_call_target="tpu_custom_call" | custom-call | bytes 8388608 | tf_op jit(solution)/shard_map/solve/pallas_call | solution.py:494
  111.8 4.1 %collective-permute-start.16 = (f32[8,2,24,128]{3,2,1,0:T(8,128)S(1)}, f32[8,2,24,128]{3,2,1,0:T(8,128)S(1)}, u32[]{:S(2)}, u32[]{:S(2)}) collective-permute-start(f32[8,2,24,128]{3,2,1,0:T(8,128)S(1)} %get-tuple-element.59), channel_id=1, source_target_pairs={{0,16},{1,5},{2,18},{3,7},{4,20},{5,1},{6,22},{7,3},{8,24},{9,13},... | collective-permute-start | bytes 589832 | tf_op jit(solution)/shard_map/ppermute | solution.py:560
  115.9 1.0 collective-permute-start.17
  116.9 0.0 collective-permute-start.18
  116.9 1.5 %collective-permute-start.19 = (f32[8,2,24,128]{3,2,1,0:T(8,128)S(1)}, f32[8,2,24,128]{3,2,1,0:T(8,128)S(1)}, u32[]{:S(2)}, u32[]{:S(2)}) collective-permute-start(f32[8,2,24,128]{3,2,1,0:T(8,128)S(1)} %get-tuple-element.62), channel_id=1, source_target_pairs={{0,24},{1,9},{2,26},{3,11},{4,28},{5,13},{6,30},{7,15},{8,16},{9,1... | collective-permute-start | bytes 589832 | tf_op jit(solution)/shard_map/ppermute | solution.py:560
  118.5 2.4 %collective-permute-start.20 = (f32[8,2,24,128]{3,2,1,0:T(8,128)S(1)}, f32[8,2,24,128]{3,2,1,0:T(8,128)S(1)}, u32[]{:S(2)}, u32[]{:S(2)}) collective-permute-start(f32[8,2,24,128]{3,2,1,0:T(8,128)S(1)} %get-tuple-element.63), channel_id=1, source_target_pairs={{0,20},{1,13},{2,22},{3,15},{4,16},{5,9},{6,18},{7,11},{8,28},{9,5... | collective-permute-start | bytes 589832 | tf_op jit(solution)/shard_map/ppermute | solution.py:560
  120.9 8.6 %collective-permute-done.16 = f32[8,2,24,128]{3,2,1,0:T(8,128)S(1)} collective-permute-done((f32[8,2,24,128]{3,2,1,0:T(8,128)S(1)}, f32[8,2,24,128]{3,2,1,0:T(8,128)S(1)}, u32[]{:S(2)}, u32[]{:S(2)}) %collective-permute-start.16) | collective-permute-done | bytes 196640 | tf_op jit(solution)/shard_map/ppermute | solution.py:560
  129.5 0.0 collective-permute-start.21
  129.5 1.8 %collective-permute-start.22 = (f32[8,2,24,128]{3,2,1,0:T(8,128)S(1)}, f32[8,2,24,128]{3,2,1,0:T(8,128)S(1)}, u32[]{:S(2)}, u32[]{:S(2)}) collective-permute-start(f32[8,2,24,128]{3,2,1,0:T(8,128)S(1)} %get-tuple-element.65), channel_id=1, source_target_pairs={{0,28},{1,29},{2,30},{3,31},{4,24},{5,25},{6,26},{7,27},{8,20},{9,... | collective-permute-start | bytes 589832 | tf_op jit(solution)/shard_map/ppermute | solution.py:560
  131.3 1.7 %collective-permute-done.18 = f32[8,2,24,128]{3,2,1,0:T(8,128)S(1)} collective-permute-done((f32[8,2,24,128]{3,2,1,0:T(8,128)S(1)}, f32[8,2,24,128]{3,2,1,0:T(8,128)S(1)}, u32[]{:S(2)}, u32[]{:S(2)}) %collective-permute-start.18) | collective-permute-done | bytes 196640 | tf_op jit(solution)/shard_map/ppermute | solution.py:560
  133.1 14.3 %collective-permute-done.20 = f32[8,2,24,128]{3,2,1,0:T(8,128)S(1)} collective-permute-done((f32[8,2,24,128]{3,2,1,0:T(8,128)S(1)}, f32[8,2,24,128]{3,2,1,0:T(8,128)S(1)}, u32[]{:S(2)}, u32[]{:S(2)}) %collective-permute-start.20) | collective-permute-done | bytes 196640 | tf_op jit(solution)/shard_map/ppermute | solution.py:560
  147.4 2.1 %restore.1 = f32[3,4,256,128]{3,2,1,0:T(8,128)} custom-call(f32[384,128]{1,0:T(8,128)S(1)} %bitcast.26, f32[384,128]{1,0:T(8,128)S(1)} %bitcast.27, f32[384,128]{1,0:T(8,128)S(1)} %bitcast.28, f32[384,128]{1,0:T(8,128)S(1)} %bitcast.29, f32[384,128]{1,0:T(8,128)S(1)} %bitcast.30, f32[384,128]{1,0:T(8,128)S(1)} %bitcast.31, f32[384,128]{1,0:T(8,128)S(1)} %bitcast.32, ...), custom_call_target="tpu_custom_call" | custom-call | bytes 3145728 | tf_op jit(solution)/shard_map/restore/pallas_call | solution.py:538
  (36 shorter events, 0.2 us)
Async XLA Ops:
  0.0 14.3 %copy-start = (bf16[128,256]{1,0:T(8,128)(2,1)S(1)}, bf16[128,256]{1,0:T(8,128)(2,1)}, u32[]{:S(2)}) copy-start(bf16[128,256]{1,0:T(8,128)(2,1)} %constant.22.clone.rest_ref.refs_5_.refs_2_) | copy-start | bytes 196612
  0.0 14.3 %copy-start.2 = (bf16[128,256]{1,0:T(8,128)(2,1)S(1)}, bf16[128,256]{1,0:T(8,128)(2,1)}, u32[]{:S(2)}) copy-start(bf16[128,256]{1,0:T(8,128)(2,1)} %constant.21.clone.top_ref) | copy-start | bytes 196612
  0.0 14.3 %copy-start.4 = (s32[64]{0:T(128)S(1)}, s32[64]{0:T(128)}, u32[]{:S(2)}) copy-start(s32[64]{0:T(128)} %owner_ref.1) | copy-start | bytes 772
  0.0 46.7 %copy-start.3 = (s32[8]{0:T(128)S(1)}, s32[8]{0:T(128)}, u32[]{:S(2)}) copy-start(s32[8]{0:T(128)} %low_ref.7) | copy-start | bytes 100
  2.7 6.5 %copy-start.7 = (f32[392,128]{1,0:T(8,128)S(1)}, f32[392,128]{1,0:T(8,128)}, u32[]{:S(2)}) copy-start(f32[392,128]{1,0:T(8,128)} %get-tuple-element.37) | copy-start | bytes 602116
  2.7 8.5 %copy-start.6 = (f32[392,128]{1,0:T(8,128)S(1)}, f32[392,128]{1,0:T(8,128)}, u32[]{:S(2)}) copy-start(f32[392,128]{1,0:T(8,128)} %get-tuple-element.38) | copy-start | bytes 602116
  2.7 10.9 %copy-start.5 = (f32[392,128]{1,0:T(8,128)S(1)}, f32[392,128]{1,0:T(8,128)}, u32[]{:S(2)}) copy-start(f32[392,128]{1,0:T(8,128)} %get-tuple-element.39) | copy-start | bytes 602116
  2.7 11.6 %copy-start.1 = (f32[392,128]{1,0:T(8,128)S(1)}, f32[392,128]{1,0:T(8,128)}, u32[]{:S(2)}) copy-start(f32[392,128]{1,0:T(8,128)} %get-tuple-element.36.refs_0_) | copy-start | bytes 602116
  2.7 61.4 %all-to-all-start.1 = ((f32[4,384,128]{2,1,0:T(8,128)}), f32[4,384,128]{2,1,0:T(8,128)S(1)}, u32[]{:S(2)}, u32[]{:S(2)}) async-start(f32[4,384,128]{2,1,0:T(8,128)} %get-tuple-element.46), calls=%async_computation.1 | async-start | bytes 1572864 | tf_op jit(solution)/shard_map/all_to_all | solution.py:590
  9.2 18.3 %collective-permute-start = (f32[392,128]{1,0:T(8,128)S(1)}, f32[392,128]{1,0:T(8,128)S(1)}, u32[]{:S(2)}, u32[]{:S(2)}) collective-permute-start(f32[392,128]{1,0:T(8,128)S(1)} %copy-done.7), channel_id=1, source_target_pairs={{0,8},{1,25},{2,10},{3,27},{8,0},{9,17},{10,2},{11,19},{16,24},{17... | collective-permute-start | bytes 602120 | tf_op jit(solution)/shard_map/ppermute | solution.py:560
  11.2 25.0 %collective-permute-start.1 = (f32[392,128]{1,0:T(8,128)S(1)}, f32[392,128]{1,0:T(8,128)S(1)}, u32[]{:S(2)}, u32[]{:S(2)}) collective-permute-start(f32[392,128]{1,0:T(8,128)S(1)} %copy-done.6), channel_id=1, source_target_pairs={{0,24},{1,9},{2,26},{3,11},{8,16},{9,1},{10,18},{11,3},{16,8},{17,... | collective-permute-start | bytes 602120 | tf_op jit(solution)/shard_map/ppermute | solution.py:560
  13.5 32.9 %collective-permute-start.2 = (f32[392,128]{1,0:T(8,128)S(1)}, f32[392,128]{1,0:T(8,128)S(1)}, u32[]{:S(2)}, u32[]{:S(2)}) collective-permute-start(f32[392,128]{1,0:T(8,128)S(1)} %copy-done.5), channel_id=1, source_target_pairs={{0,16},{1,17},{2,18},{3,19},{8,24},{9,25},{10,26},{11,27},{16,0},{... | collective-permute-start | bytes 602120 | tf_op jit(solution)/shard_map/ppermute | solution.py:560
  52.2 1.5 %collective-permute-start.3 = (f32[3,4,32,128]{3,2,1,0:T(8,128)S(1)}, f32[3,4,32,128]{3,2,1,0:T(8,128)S(1)}, u32[]{:S(2)}, u32[]{:S(2)}) collective-permute-start(f32[3,4,32,128]{3,2,1,0:T(8,128)S(1)} %get-tuple-element.45), channel_id=1, source_target_pairs={{0,1},{1,0},{2,3},{3,2},{4,5},{5,4},{6,7},{7,6},{8,9},{9,8},{10,11... | collective-permute-start | bytes 589832 | tf_op jit(solution)/shard_map/ppermute | solution.py:566
  53.7 7.0 %collective-permute-start.4 = (f32[3,4,32,128]{3,2,1,0:T(8,128)S(1)}, f32[3,4,32,128]{3,2,1,0:T(8,128)S(1)}, u32[]{:S(2)}, u32[]{:S(2)}) collective-permute-start(f32[3,4,32,128]{3,2,1,0:T(8,128)S(1)} %add.27.refs_5_), channel_id=1, source_target_pairs={{0,2},{1,3},{2,0},{3,1},{4,6},{5,7},{6,4},{7,5},{8,10},{9,11},{10,... | collective-permute-start | bytes 589832 | tf_op jit(solution)/shard_map/ppermute | solution.py:566
  60.7 1.5 %collective-permute-start.5 = (f32[3,4,32,128]{3,2,1,0:T(8,128)S(1)}, f32[3,4,32,128]{3,2,1,0:T(8,128)S(1)}, u32[]{:S(2)}, u32[]{:S(2)}) collective-permute-start(f32[3,4,32,128]{3,2,1,0:T(8,128)S(1)} %add.28.kept_ref), channel_id=1, source_target_pairs={{0,1},{1,0},{2,3},{3,2},{4,5},{5,4},{6,7},{7,6},{8,9},{9,8},{10,11... | collective-permute-start | bytes 589832 | tf_op jit(solution)/shard_map/ppermute | solution.py:566
  64.1 40.9 %all-to-all-start = ((f32[8,8,24,128]{3,2,1,0:T(8,128)}), f32[8,8,24,128]{3,2,1,0:T(8,128)S(1)}, u32[]{:S(2)}, u32[]{:S(2)}) async-start(f32[8,8,24,128]{3,2,1,0:T(8,128)} %bitcast.5), calls=%async_computation | async-start | bytes 1572864 | tf_op jit(solution)/shard_map/all_to_all | solution.py:619
  73.1 1.5 %collective-permute-start.6 = (f32[3,4,32,128]{3,2,1,0:T(8,128)S(1)}, f32[3,4,32,128]{3,2,1,0:T(8,128)S(1)}, u32[]{:S(2)}, u32[]{:S(2)}) collective-permute-start(f32[3,4,32,128]{3,2,1,0:T(8,128)S(1)} %get-tuple-element.49), channel_id=1, source_target_pairs={{0,1},{1,0},{2,3},{3,2},{4,5},{5,4},{6,7},{7,6},{8,9},{9,8},{10,11... | collective-permute-start | bytes 589832 | tf_op jit(solution)/shard_map/ppermute | solution.py:566
  74.7 7.0 %collective-permute-start.7 = (f32[3,4,32,128]{3,2,1,0:T(8,128)S(1)}, f32[3,4,32,128]{3,2,1,0:T(8,128)S(1)}, u32[]{:S(2)}, u32[]{:S(2)}) collective-permute-start(f32[3,4,32,128]{3,2,1,0:T(8,128)S(1)} %add.29), channel_id=1, source_target_pairs={{0,2},{1,3},{2,0},{3,1},{4,6},{5,7},{6,4},{7,5},{8,10},{9,11},{10,... | collective-permute-start | bytes 589832 | tf_op jit(solution)/shard_map/ppermute | solution.py:566
  81.7 1.5 %collective-permute-start.8 = (f32[3,4,32,128]{3,2,1,0:T(8,128)S(1)}, f32[3,4,32,128]{3,2,1,0:T(8,128)S(1)}, u32[]{:S(2)}, u32[]{:S(2)}) collective-permute-start(f32[3,4,32,128]{3,2,1,0:T(8,128)S(1)} %add.30.kept_ref), channel_id=1, source_target_pairs={{0,1},{1,0},{2,3},{3,2},{4,5},{5,4},{6,7},{7,6},{8,9},{9,8},{10,11... | collective-permute-start | bytes 589832 | tf_op jit(solution)/shard_map/ppermute | solution.py:566
  84.3 7.9 %collective-permute-start.9 = (f32[8,24,128]{2,1,0:T(8,128)S(1)}, f32[8,24,128]{2,1,0:T(8,128)S(1)}, u32[]{:S(2)}, u32[]{:S(2)}) collective-permute-start(f32[8,24,128]{2,1,0:T(8,128)S(1)} %bitcast.43), channel_id=1, source_target_pairs={{0,16},{1,5},{2,18},{3,7},{4,20},{5,1},{6,22},{7,3},{8,24},{9,13},... | collective-permute-start | bytes 294920 | tf_op jit(solution)/shard_map/ppermute | solution.py:560
  87.3 8.7 %collective-permute-start.10 = (f32[8,24,128]{2,1,0:T(8,128)S(1)}, f32[8,24,128]{2,1,0:T(8,128)S(1)}, u32[]{:S(2)}, u32[]{:S(2)}) collective-permute-start(f32[8,24,128]{2,1,0:T(8,128)S(1)} %bitcast.42), channel_id=1, source_target_pairs={{0,4},{1,17},{2,6},{3,19},{4,0},{5,21},{6,2},{7,23},{8,12},{9,25},... | collective-permute-start | bytes 294920 | tf_op jit(solution)/shard_map/ppermute | solution.py:560
  88.7 10.4 %collective-permute-start.11 = (f32[8,24,128]{2,1,0:T(8,128)S(1)}, f32[8,24,128]{2,1,0:T(8,128)S(1)}, u32[]{:S(2)}, u32[]{:S(2)}) collective-permute-start(f32[8,24,128]{2,1,0:T(8,128)S(1)} %bitcast.41), channel_id=1, source_target_pairs={{0,8},{1,25},{2,10},{3,27},{4,12},{5,29},{6,14},{7,31},{8,0},{9,17... | collective-permute-start | bytes 294920 | tf_op jit(solution)/shard_map/ppermute | solution.py:560
  90.2 8.9 %collective-permute-start.12 = (f32[8,24,128]{2,1,0:T(8,128)S(1)}, f32[8,24,128]{2,1,0:T(8,128)S(1)}, u32[]{:S(2)}, u32[]{:S(2)}) collective-permute-start(f32[8,24,128]{2,1,0:T(8,128)S(1)} %bitcast.40), channel_id=1, source_target_pairs={{0,24},{1,9},{2,26},{3,11},{4,28},{5,13},{6,30},{7,15},{8,16},{9,1... | collective-permute-start | bytes 294920 | tf_op jit(solution)/shard_map/ppermute | solution.py:560
  90.8 14.2 %collective-permute-start.13 = (f32[8,24,128]{2,1,0:T(8,128)S(1)}, f32[8,24,128]{2,1,0:T(8,128)S(1)}, u32[]{:S(2)}, u32[]{:S(2)}) collective-permute-start(f32[8,24,128]{2,1,0:T(8,128)S(1)} %bitcast.39), channel_id=1, source_target_pairs={{0,20},{1,13},{2,22},{3,15},{4,16},{5,9},{6,18},{7,11},{8,28},{9,5... | collective-permute-start | bytes 294920 | tf_op jit(solution)/shard_map/ppermute | solution.py:560
  92.2 12.7 %collective-permute-start.14 = (f32[8,24,128]{2,1,0:T(8,128)S(1)}, f32[8,24,128]{2,1,0:T(8,128)S(1)}, u32[]{:S(2)}, u32[]{:S(2)}) collective-permute-start(f32[8,24,128]{2,1,0:T(8,128)S(1)} %bitcast.38), channel_id=1, source_target_pairs={{0,12},{1,21},{2,14},{3,23},{4,8},{5,17},{6,10},{7,19},{8,4},{9,29... | collective-permute-start | bytes 294920 | tf_op jit(solution)/shard_map/ppermute | solution.py:560
  95.9 9.1 %collective-permute-start.15 = (f32[8,24,128]{2,1,0:T(8,128)S(1)}, f32[8,24,128]{2,1,0:T(8,128)S(1)}, u32[]{:S(2)}, u32[]{:S(2)}) collective-permute-start(f32[8,24,128]{2,1,0:T(8,128)S(1)} %bitcast.37), channel_id=1, source_target_pairs={{0,28},{1,29},{2,30},{3,31},{4,24},{5,25},{6,26},{7,27},{8,20},{9,... | collective-permute-start | bytes 294920 | tf_op jit(solution)/shard_map/ppermute | solution.py:560
  111.8 17.7 %collective-permute-start.16 = (f32[8,2,24,128]{3,2,1,0:T(8,128)S(1)}, f32[8,2,24,128]{3,2,1,0:T(8,128)S(1)}, u32[]{:S(2)}, u32[]{:S(2)}) collective-permute-start(f32[8,2,24,128]{3,2,1,0:T(8,128)S(1)} %get-tuple-element.59), channel_id=1, source_target_pairs={{0,16},{1,5},{2,18},{3,7},{4,20},{5,1},{6,22},{7,3},{8,24},{9,13},... | collective-permute-start | bytes 589832 | tf_op jit(solution)/shard_map/ppermute | solution.py:560
  115.9 13.6 %collective-permute-start.17 = (f32[8,2,24,128]{3,2,1,0:T(8,128)S(1)}, f32[8,2,24,128]{3,2,1,0:T(8,128)S(1)}, u32[]{:S(2)}, u32[]{:S(2)}) collective-permute-start(f32[8,2,24,128]{3,2,1,0:T(8,128)S(1)} %get-tuple-element.60), channel_id=1, source_target_pairs={{0,4},{1,17},{2,6},{3,19},{4,0},{5,21},{6,2},{7,23},{8,12},{9,25},... | collective-permute-start | bytes 589832 | tf_op jit(solution)/shard_map/ppermute | solution.py:560
  116.9 16.2 %collective-permute-start.18 = (f32[8,2,24,128]{3,2,1,0:T(8,128)S(1)}, f32[8,2,24,128]{3,2,1,0:T(8,128)S(1)}, u32[]{:S(2)}, u32[]{:S(2)}) collective-permute-start(f32[8,2,24,128]{3,2,1,0:T(8,128)S(1)} %get-tuple-element.61), channel_id=1, source_target_pairs={{0,8},{1,25},{2,10},{3,27},{4,12},{5,29},{6,14},{7,31},{8,0},{9,17... | collective-permute-start | bytes 589832 | tf_op jit(solution)/shard_map/ppermute | solution.py:560
  116.9 16.2 %collective-permute-start.19 = (f32[8,2,24,128]{3,2,1,0:T(8,128)S(1)}, f32[8,2,24,128]{3,2,1,0:T(8,128)S(1)}, u32[]{:S(2)}, u32[]{:S(2)}) collective-permute-start(f32[8,2,24,128]{3,2,1,0:T(8,128)S(1)} %get-tuple-element.62), channel_id=1, source_target_pairs={{0,24},{1,9},{2,26},{3,11},{4,28},{5,13},{6,30},{7,15},{8,16},{9,1... | collective-permute-start | bytes 589832 | tf_op jit(solution)/shard_map/ppermute | solution.py:560
  118.5 28.9 %collective-permute-start.20 = (f32[8,2,24,128]{3,2,1,0:T(8,128)S(1)}, f32[8,2,24,128]{3,2,1,0:T(8,128)S(1)}, u32[]{:S(2)}, u32[]{:S(2)}) collective-permute-start(f32[8,2,24,128]{3,2,1,0:T(8,128)S(1)} %get-tuple-element.63), channel_id=1, source_target_pairs={{0,20},{1,13},{2,22},{3,15},{4,16},{5,9},{6,18},{7,11},{8,28},{9,5... | collective-permute-start | bytes 589832 | tf_op jit(solution)/shard_map/ppermute | solution.py:560
  129.5 17.9 %collective-permute-start.21 = (f32[8,2,24,128]{3,2,1,0:T(8,128)S(1)}, f32[8,2,24,128]{3,2,1,0:T(8,128)S(1)}, u32[]{:S(2)}, u32[]{:S(2)}) collective-permute-start(f32[8,2,24,128]{3,2,1,0:T(8,128)S(1)} %get-tuple-element.64), channel_id=1, source_target_pairs={{0,12},{1,21},{2,14},{3,23},{4,8},{5,17},{6,10},{7,19},{8,4},{9,29... | collective-permute-start | bytes 589832 | tf_op jit(solution)/shard_map/ppermute | solution.py:560
  129.5 17.9 %collective-permute-start.22 = (f32[8,2,24,128]{3,2,1,0:T(8,128)S(1)}, f32[8,2,24,128]{3,2,1,0:T(8,128)S(1)}, u32[]{:S(2)}, u32[]{:S(2)}) collective-permute-start(f32[8,2,24,128]{3,2,1,0:T(8,128)S(1)} %get-tuple-element.65), channel_id=1, source_target_pairs={{0,28},{1,29},{2,30},{3,31},{4,24},{5,25},{6,26},{7,27},{8,20},{9,... | collective-permute-start | bytes 589832 | tf_op jit(solution)/shard_map/ppermute | solution.py:560

commit v9 on v6

--- a/solution.py
+++ b/solution.py
@@ -148,16 +148,8 @@
     return lax.dot_general(left, right, (dims, ((), ())), preferred_element_type=jnp.float32)
 
 
-def pack_kernel(near_ref, count_ref, velocity_ref, *out_refs):
-    chunks, pieces, kx_count, rows, columns = velocity_ref.shape
-    own = lax.axis_index("kx")
-    for index in range(kx_count):
-        partner = own ^ step_at(kx_count, index)
-        for chunk in range(chunks):
-            place = slice(chunk * rows, (chunk + 1) * rows)
-            out_refs[index][place] = velocity_ref[chunk, 0, partner]
-            for piece in range(1, pieces):
-                out_refs[kx_count + piece - 1][index, place] = velocity_ref[chunk, piece, index]
+def pack_first_kernel(near_ref, count_ref, velocity_ref, *out_refs):
+    chunks, _, kx_count, rows, columns = velocity_ref.shape
     shape = (out_refs[0].shape[0] - chunks * rows, columns)
     row = lax.broadcasted_iota(jnp.int32, shape, 0)
     lane = lax.broadcasted_iota(jnp.int32, shape, 1)
@@ -169,24 +161,55 @@
             line = jnp.where(lane == member, near_ref[mode, member], line)
         extra = jnp.where(row == mode, line, extra)
     extra = extra.astype(jnp.float32)
-    for out_ref in out_refs[:kx_count]:
+    own = lax.axis_index("kx")
+    for index, out_ref in enumerate(out_refs):
+        partner = own ^ step_at(kx_count, index)
+        for chunk in range(chunks):
+            out_ref[chunk * rows : (chunk + 1) * rows] = velocity_ref[chunk, 0, partner]
         out_ref[chunks * rows :] = extra
 
 
-def pack(velocity, neighbours, mode_counts, extra_rows):
-    chunks, pieces, kx_count, rows, columns = velocity.shape
-    size = chunks * rows
-    shapes = [(size + extra_rows, columns)] * kx_count
-    shapes += [(kx_count, size, columns)] * (pieces - 1)
-    out = pl.pallas_call(
+def pack_first(velocity, neighbours, mode_counts, extra_rows):
+    chunks, _, kx_count, rows, columns = velocity.shape
+    shape = jax.ShapeDtypeStruct((chunks * rows + extra_rows, columns), jnp.float32)
+    return pl.pallas_call(
+        pack_first_kernel,
+        out_shape=(shape,) * kx_count,
+        grid=(1,),
+        in_specs=[
+            SMEM,
+            SMEM,
+            pl.BlockSpec((chunks, 1, kx_count, rows, columns), lambda i: (0, 0, 0, 0, 0)),
+        ],
+        out_specs=(pl.BlockSpec(shape.shape, lambda i: (0, 0)),) * kx_count,
+        cost_estimate=cost(4 * velocity.size),
+        name="pack_first",
+    )(neighbours, mode_counts, velocity)
+
+
+def pack_kernel(velocity_ref, _, out_ref):
+    chunks, _, kx_count, rows, columns = velocity_ref.shape
+    for index in range(kx_count):
+        for chunk in range(chunks):
+            place = slice(chunk * rows, (chunk + 1) * rows)
+            out_ref[index, place] = velocity_ref[chunk, 0, index]
+
+
+def pack(velocity, piece, after):
+    chunks, _, kx_count, rows, columns = velocity.shape
+    shape = (kx_count, chunks * rows, columns)
+    return pl.pallas_call(
         pack_kernel,
-        out_shape=tuple(jax.ShapeDtypeStruct(shape, jnp.float32) for shape in shapes),
-        in_specs=[SMEM, SMEM, VMEM],
-        out_specs=(VMEM,) * len(shapes),
-        cost_estimate=cost(8 * velocity.size),
+        out_shape=jax.ShapeDtypeStruct(shape, jnp.float32),
+        grid=(1,),
+        in_specs=[
+            pl.BlockSpec((chunks, 1, kx_count, rows, columns), lambda i: (0, piece, 0, 0, 0)),
+            pl.BlockSpec(memory_space=pl.ANY),
+        ],
+        out_specs=pl.BlockSpec(shape, lambda i: (0, 0, 0)),
+        cost_estimate=cost(4 * velocity.size),
         name="pack",
-    )(neighbours, mode_counts, velocity)
-    return out[:kx_count], out[kx_count:]
+    )(velocity, after)
 
 
 def tables_kernel(owner_ref, top_ref, rest_ref, first_ref, back_ref, order_ref, slot_ref):
@@ -585,10 +608,12 @@
     shape = (components, modes, rows, columns)
     extra_rows = -(-band_modes // 8) * 8
     split = velocity.reshape(chunks, pieces, kx_count, rows, columns)
-    first_blocks, rest = pack(split, neighbours, mode_counts, extra_rows)
-    parts = [exchange(first_blocks, ("kx",))] + [
-        (lax.all_to_all(block, "kx", split_axis=0, concat_axis=0, tiled=True),) for block in rest
-    ]
+    blocks = pack_first(split, neighbours, mode_counts, extra_rows)
+    parts = [exchange(blocks, ("kx",))]
+    for piece in range(1, pieces):
+        block = pack(split, piece, parts[0][1])
+        block = lax.all_to_all(block, "kx", split_axis=0, concat_axis=0, tiled=True)
+        parts.append((block,))
     tables, order, slot_modes = slot_tables(owner_map, columns)
     small = 0.0
     for index, block in enumerate(parts[0]):

time: 152 us -> 137 us (0.901)
  waiting for transfers between devices: 78.5 us -> 52.9 us
  starting transfers between devices: 43.7 us -> 52 us
  Pallas kernels: 25.9 us -> 27.5 us
    ppermute x17, waiting for transfers between devices: 61.9 us -> 36.2 us  [exchange(): result[position] = lax.ppermute(blocks[position], axes + ('real',), pairs)]
    all_to_all x1, starting transfers between devices: 3.69 us -> 7.83 us  [local(): lax.all_to_all(block, ('kx', 'ht'), split_axis=0, concat_axis=0, tiled=True)]
    all_to_all x1, starting transfers between devices: 6.48 us -> 9.53 us  [local(): block = lax.all_to_all(block, 'kx', split_axis=0, concat_axis=0, tiled=True)]
    pallas_call x1 -> x2, Pallas kernels: 2.65 us -> 4.16 us  [the longest x1 2.1 us: pack_first(): pl.pallas_call(pack_first_kernel, out_shape=(shape,) * kx_count, grid=(1,...]
  transfers between devices with their start and end apart: 25 -> 25, of which waited for: 13 -> 12; matrix products, arithmetic and copies ran while one was open for 1% -> 1% of each run, Pallas kernels for 10% -> 12%
where the time goes in v9:
time: 137 us; the launch traced here: 134 us
  waiting for transfers between devices  52.9 us (39%)
  starting transfers between devices  52 us (38%)
  Pallas kernels  27.5 us (20%)
  local copies, waits for them, and re-layouts  1.56 us (1%)
    ppermute x17, waiting for transfers between devices, exchange(): result[position] = lax.ppermute(blocks[position], axes + ('real',), pairs)  36.2 us
    ppermute x17, starting transfers between devices, exchange(): result[position] = lax.ppermute(blocks[position], axes + ('real',), pairs)  31.3 us
    ppermute x6, waiting for transfers between devices, swap(): return lax.ppermute(value, 'real', pairs)  16.6 us
    pallas_call x2, Pallas kernels, nonlinear(): pl.pallas_call(nonlinear_kernel, out_shape=(jax.ShapeDtypeStruct((compone...  10.8 us
    all_to_all x1, starting transfers between devices, local(): block = lax.all_to_all(block, 'kx', split_axis=0, concat_axis=0, tiled=True)  9.53 us
    all_to_all x1, starting transfers between devices, local(): lax.all_to_all(block, ('kx', 'ht'), split_axis=0, concat_axis=0, tiled=True)  7.83 us
    pallas_call x1, Pallas kernels, solve(): pl.pallas_call(functools.partial(solve_kernel, groups=groups, kx_count=kx...  6.85 us
    ppermute x6, starting transfers between devices, swap(): return lax.ppermute(value, 'real', pairs)  3.4 us
  transfers between devices with their start and end apart: 25, of which 12 were waited for; matrix products, arithmetic and copies ran while one was open for 1% of the time, Pallas kernels for 12%

profile of v9, /device:TPU:0, one launch (start us, length us, event | category | flops | bytes accessed | tf_op | source)
XLA Modules:
  0.0 134.4 jit_solution(5759823291128220141)
XLA Ops:
  0.0 2.1 %pack_first.1 = (f32[392,128]{1,0:T(8,128)}, f32[392,128]{1,0:T(8,128)}, f32[392,128]{1,0:T(8,128)}, f32[392,128]{1,0:T(8,128)}) custom-call(s32[4,8]{1,0:T(4,128)} %near_ref.1, s32[4]{0:T(128)} %count_ref.1, f32[12,2,4,32,128]{4,3,2,1,0:T(8,128)} %bitcast.44), custom_call_target="tpu_custom_call" | custom-call | bytes 1572864 | tf_op jit(solution)/shard_map/pack_first/pallas_call | solution.py:175
  2.1 3.0 %collective-permute-start = (f32[392,128]{1,0:T(8,128)}, f32[392,128]{1,0:T(8,128)S(1)}, u32[]{:S(2)}, u32[]{:S(2)}) collective-permute-start(f32[392,128]{1,0:T(8,128)} %get-tuple-element.36), channel_id=1, source_target_pairs={{0,8},{1,25},{2,10},{3,27},{8,0},{9,17},{10,2},{11,19},{16,24},{17... | collective-permute-start | bytes 602120 | tf_op jit(solution)/shard_map/ppermute | solution.py:583
  5.1 2.5 %collective-permute-start.1 = (f32[392,128]{1,0:T(8,128)}, f32[392,128]{1,0:T(8,128)S(1)}, u32[]{:S(2)}, u32[]{:S(2)}) collective-permute-start(f32[392,128]{1,0:T(8,128)} %get-tuple-element.37), channel_id=1, source_target_pairs={{0,24},{1,9},{2,26},{3,11},{8,16},{9,1},{10,18},{11,3},{16,8},{17,... | collective-permute-start | bytes 602120 | tf_op jit(solution)/shard_map/ppermute | solution.py:583
  7.6 0.1 collective-permute-start.2
  7.7 0.0 copy-start.4
  7.7 0.0 copy-start.6
  7.8 0.0 copy-start.5
  7.8 4.2 %collective-permute-done.refs_1_._ = f32[392,128]{1,0:T(8,128)S(1)} collective-permute-done((f32[392,128]{1,0:T(8,128)}, f32[392,128]{1,0:T(8,128)S(1)}, u32[]{:S(2)}, u32[]{:S(2)}) %collective-permute-start) | collective-permute-done | bytes 200736 | tf_op jit(solution)/shard_map/ppermute | solution.py:583
  11.9 0.7 copy-done
  12.6 2.1 %pack.1 = f32[4,384,128]{2,1,0:T(8,128)} custom-call(f32[12,2,4,32,128]{4,3,2,1,0:T(8,128)} %bitcast.45, f32[392,128]{1,0:T(8,128)} %copy-done), custom_call_target="tpu_custom_call" | custom-call | bytes 1572864 | tf_op jit(solution)/shard_map/pack/pallas_call | solution.py:201
  14.7 9.5 %all-to-all-start.1 = ((f32[4,384,128]{2,1,0:T(8,128)}), f32[4,384,128]{2,1,0:T(8,128)S(1)}, u32[]{:S(2)}, u32[]{:S(2)}) async-start(f32[4,384,128]{2,1,0:T(8,128)} %pack.1), calls=%async_computation.1 | async-start | bytes 1572864 | tf_op jit(solution)/shard_map/all_to_all | solution.py:615
  24.2 0.1 broadcast_in_dim.85
  24.3 0.1 broadcast_in_dim.86
  24.4 0.1 broadcast_in_dim.91
  24.4 0.1 broadcast_in_dim.92
  24.5 0.1 broadcast_in_dim.96
  24.6 0.1 broadcast_in_dim.97
  24.7 0.1 broadcast_in_dim.101
  24.8 0.1 broadcast_in_dim.102
  24.9 0.8 tables.1
  25.7 1.6 %collective-permute-done.2.refs_3_ = f32[392,128]{1,0:T(8,128)S(1)} collective-permute-done((f32[392,128]{1,0:T(8,128)}, f32[392,128]{1,0:T(8,128)S(1)}, u32[]{:S(2)}, u32[]{:S(2)}) %collective-permute-start.2) | collective-permute-done | bytes 200736 | tf_op jit(solution)/shard_map/ppermute | solution.py:583
  27.3 0.1 add_convert_fusion
  27.4 0.2 slice_reduce_fusion.count_ref
  27.6 5.4 %nonlinear.2 = (f32[3,16,32,128]{3,2,1,0:T(8,128)S(1)}, f32[3,4,32,128]{3,2,1,0:T(8,128)S(1)}, f32[3,4,32,128]{3,2,1,0:T(8,128)S(1)}) custom-call(s32[8]{0:T(128)S(1)} %copy-done.5, s32[16,8]{1,0:T(8,128)S(1)} %bitcast.34, s32[16]{0:T(128)S(1)} %slice_reduce_fusion.count_ref, f32[392,128]{1,0:T(8,128)S(1)} %copy-done.3, f32[392,128]{1,0:T(8,128)S(1)} %copy-done.1, ...), custom_call_target="tpu_custom_call" | custom-call | bytes 25165824 | tf_op jit(solution)/shard_map/nonlinear/pallas_call | solution.py:366
  33.0 0.1 collective-permute-start.3
  33.1 1.4 %collective-permute-done.3 = f32[3,4,32,128]{3,2,1,0:T(8,128)S(1)} collective-permute-done((f32[3,4,32,128]{3,2,1,0:T(8,128)S(1)}, f32[3,4,32,128]{3,2,1,0:T(8,128)S(1)}, u32[]{:S(2)}, u32[]{:S(2)}) %collective-permute-start.3) | collective-permute-done | bytes 196640 | tf_op jit(solution)/shard_map/ppermute | solution.py:589
  34.5 1.6 %collective-permute-start.4 = (f32[3,4,32,128]{3,2,1,0:T(8,128)S(1)}, f32[3,4,32,128]{3,2,1,0:T(8,128)S(1)}, u32[]{:S(2)}, u32[]{:S(2)}) collective-permute-start(f32[3,4,32,128]{3,2,1,0:T(8,128)S(1)} %add.27.refs_5_), channel_id=1, source_target_pairs={{0,2},{1,3},{2,0},{3,1},{4,6},{5,7},{6,4},{7,5},{8,10},{9,11},{10,... | collective-permute-start | bytes 589832 | tf_op jit(solution)/shard_map/ppermute | solution.py:589
  36.1 5.5 %collective-permute-done.4 = f32[3,4,32,128]{3,2,1,0:T(8,128)S(1)} collective-permute-done((f32[3,4,32,128]{3,2,1,0:T(8,128)S(1)}, f32[3,4,32,128]{3,2,1,0:T(8,128)S(1)}, u32[]{:S(2)}, u32[]{:S(2)}) %collective-permute-start.4) | collective-permute-done | bytes 196640 | tf_op jit(solution)/shard_map/ppermute | solution.py:589
  41.6 0.1 collective-permute-start.5
  41.6 1.4 %collective-permute-done.5.other_ref = f32[3,4,32,128]{3,2,1,0:T(8,128)S(1)} collective-permute-done((f32[3,4,32,128]{3,2,1,0:T(8,128)S(1)}, f32[3,4,32,128]{3,2,1,0:T(8,128)S(1)}, u32[]{:S(2)}, u32[]{:S(2)}) %collective-permute-start.5) | collective-permute-done | bytes 196640 | tf_op jit(solution)/shard_map/ppermute | solution.py:589
  43.1 1.8 %outgoing.2 = f32[1536,128]{1,0:T(8,128)} custom-call(s32[8]{0:T(128)S(1)} %copy-done.5, s32[16]{0:T(128)S(1)} %slice_reduce_fusion.count_ref, f32[3,16,32,128]{3,2,1,0:T(8,128)S(1)} %get-tuple-element.42.slotted_ref, f32[3,4,32,128]{3,2,1,0:T(8,128)S(1)} %add.28.kept_ref, f32[3,4,32,128]{3,2,1,0:T(8,128)S(1)} %collective-permute-done.5.other_ref, ...), custom_call_target="tpu_custom_call" | custom-call | bytes 1572864 | tf_op jit(solution)/shard_map/outgoing/pallas_call | solution.py:434
  44.9 7.8 %all-to-all-start = ((f32[8,8,24,128]{3,2,1,0:T(8,128)}), f32[8,8,24,128]{3,2,1,0:T(8,128)S(1)}, u32[]{:S(2)}, u32[]{:S(2)}) async-start(f32[8,8,24,128]{3,2,1,0:T(8,128)} %bitcast.5), calls=%async_computation | async-start | bytes 1572864 | tf_op jit(solution)/shard_map/all_to_all | solution.py:644
  52.7 5.4 %nonlinear.3 = (f32[3,16,32,128]{3,2,1,0:T(8,128)S(1)}, f32[3,4,32,128]{3,2,1,0:T(8,128)S(1)}, f32[3,4,32,128]{3,2,1,0:T(8,128)S(1)}) custom-call(s32[8]{0:T(128)S(1)} %copy-done.5, s32[16,8]{1,0:T(8,128)S(1)} %bitcast.35, s32[16]{0:T(128)S(1)} %slice_reduce_fusion.count_ref, f32[4,384,128]{2,1,0:T(8,128)S(1)} %all-to-all-done.1.refs_0_, ...), custom_call_target="tpu_custom_call" | custom-call | bytes 25165824 | tf_op jit(solution)/shard_map/nonlinear/pallas_call | solution.py:366
  58.1 0.1 collective-permute-start.6
  58.2 1.4 %collective-permute-done.6 = f32[3,4,32,128]{3,2,1,0:T(8,128)S(1)} collective-permute-done((f32[3,4,32,128]{3,2,1,0:T(8,128)S(1)}, f32[3,4,32,128]{3,2,1,0:T(8,128)S(1)}, u32[]{:S(2)}, u32[]{:S(2)}) %collective-permute-start.6) | collective-permute-done | bytes 196640 | tf_op jit(solution)/shard_map/ppermute | solution.py:589
  59.6 1.6 %collective-permute-start.7 = (f32[3,4,32,128]{3,2,1,0:T(8,128)S(1)}, f32[3,4,32,128]{3,2,1,0:T(8,128)S(1)}, u32[]{:S(2)}, u32[]{:S(2)}) collective-permute-start(f32[3,4,32,128]{3,2,1,0:T(8,128)S(1)} %add.29), channel_id=1, source_target_pairs={{0,2},{1,3},{2,0},{3,1},{4,6},{5,7},{6,4},{7,5},{8,10},{9,11},{10,... | collective-permute-start | bytes 589832 | tf_op jit(solution)/shard_map/ppermute | solution.py:589
  61.2 5.5 %collective-permute-done.7 = f32[3,4,32,128]{3,2,1,0:T(8,128)S(1)} collective-permute-done((f32[3,4,32,128]{3,2,1,0:T(8,128)S(1)}, f32[3,4,32,128]{3,2,1,0:T(8,128)S(1)}, u32[]{:S(2)}, u32[]{:S(2)}) %collective-permute-start.7) | collective-permute-done | bytes 196640 | tf_op jit(solution)/shard_map/ppermute | solution.py:589
  66.7 0.1 collective-permute-start.8
  66.8 1.4 %collective-permute-done.8.other_ref = f32[3,4,32,128]{3,2,1,0:T(8,128)S(1)} collective-permute-done((f32[3,4,32,128]{3,2,1,0:T(8,128)S(1)}, f32[3,4,32,128]{3,2,1,0:T(8,128)S(1)}, u32[]{:S(2)}, u32[]{:S(2)}) %collective-permute-start.8) | collective-permute-done | bytes 196640 | tf_op jit(solution)/shard_map/ppermute | solution.py:589
  68.2 1.1 outgoing.3
  69.3 3.0 %collective-permute-start.9 = (f32[8,24,128]{2,1,0:T(8,128)S(1)}, f32[8,24,128]{2,1,0:T(8,128)S(1)}, u32[]{:S(2)}, u32[]{:S(2)}) collective-permute-start(f32[8,24,128]{2,1,0:T(8,128)S(1)} %bitcast.43), channel_id=1, source_target_pairs={{0,16},{1,5},{2,18},{3,7},{4,20},{5,1},{6,22},{7,3},{8,24},{9,13},... | collective-permute-start | bytes 294920 | tf_op jit(solution)/shard_map/ppermute | solution.py:583
  72.3 1.5 %collective-permute-start.10 = (f32[8,24,128]{2,1,0:T(8,128)S(1)}, f32[8,24,128]{2,1,0:T(8,128)S(1)}, u32[]{:S(2)}, u32[]{:S(2)}) collective-permute-start(f32[8,24,128]{2,1,0:T(8,128)S(1)} %bitcast.42), channel_id=1, source_target_pairs={{0,4},{1,17},{2,6},{3,19},{4,0},{5,21},{6,2},{7,23},{8,12},{9,25},... | collective-permute-start | bytes 294920 | tf_op jit(solution)/shard_map/ppermute | solution.py:583
  73.7 1.5 %collective-permute-start.11 = (f32[8,24,128]{2,1,0:T(8,128)S(1)}, f32[8,24,128]{2,1,0:T(8,128)S(1)}, u32[]{:S(2)}, u32[]{:S(2)}) collective-permute-start(f32[8,24,128]{2,1,0:T(8,128)S(1)} %bitcast.41), channel_id=1, source_target_pairs={{0,8},{1,25},{2,10},{3,27},{4,12},{5,29},{6,14},{7,31},{8,0},{9,17... | collective-permute-start | bytes 294920 | tf_op jit(solution)/shard_map/ppermute | solution.py:583
  75.2 0.6 collective-permute-start.12
  75.7 1.5 %collective-permute-start.13 = (f32[8,24,128]{2,1,0:T(8,128)S(1)}, f32[8,24,128]{2,1,0:T(8,128)S(1)}, u32[]{:S(2)}, u32[]{:S(2)}) collective-permute-start(f32[8,24,128]{2,1,0:T(8,128)S(1)} %bitcast.39), channel_id=1, source_target_pairs={{0,20},{1,13},{2,22},{3,15},{4,16},{5,9},{6,18},{7,11},{8,28},{9,5... | collective-permute-start | bytes 294920 | tf_op jit(solution)/shard_map/ppermute | solution.py:583
  77.2 3.7 %collective-permute-start.14 = (f32[8,24,128]{2,1,0:T(8,128)S(1)}, f32[8,24,128]{2,1,0:T(8,128)S(1)}, u32[]{:S(2)}, u32[]{:S(2)}) collective-permute-start(f32[8,24,128]{2,1,0:T(8,128)S(1)} %bitcast.38), channel_id=1, source_target_pairs={{0,12},{1,21},{2,14},{3,23},{4,8},{5,17},{6,10},{7,19},{8,4},{9,29... | collective-permute-start | bytes 294920 | tf_op jit(solution)/shard_map/ppermute | solution.py:583
  80.9 0.0 collective-permute-done.10.refs_3_
  80.9 3.2 %collective-permute-start.15 = (f32[8,24,128]{2,1,0:T(8,128)S(1)}, f32[8,24,128]{2,1,0:T(8,128)S(1)}, u32[]{:S(2)}, u32[]{:S(2)}) collective-permute-start(f32[8,24,128]{2,1,0:T(8,128)S(1)} %bitcast.37), channel_id=1, source_target_pairs={{0,28},{1,29},{2,30},{3,31},{4,24},{5,25},{6,26},{7,27},{8,20},{9,... | collective-permute-start | bytes 294920 | tf_op jit(solution)/shard_map/ppermute | solution.py:583
  84.1 5.9 %collective-permute-done.13.refs_6_ = f32[8,24,128]{2,1,0:T(8,128)S(1)} collective-permute-done((f32[8,24,128]{2,1,0:T(8,128)S(1)}, f32[8,24,128]{2,1,0:T(8,128)S(1)}, u32[]{:S(2)}, u32[]{:S(2)}) %collective-permute-start.13) | collective-permute-done | bytes 98336 | tf_op jit(solution)/shard_map/ppermute | solution.py:583
  90.0 0.0 collective-permute-done.15.refs_8_
  90.0 0.0 all-to-all-done.refs_0_
  90.0 6.9 %solve.1 = (f32[8,2,24,128]{3,2,1,0:T(8,128)S(1)}, f32[8,2,24,128]{3,2,1,0:T(8,128)S(1)}, f32[8,2,24,128]{3,2,1,0:T(8,128)S(1)}, f32[8,2,24,128]{3,2,1,0:T(8,128...) custom-call(f32[8,8,24,128]{3,2,1,0:T(8,128)S(1)} %all-to-all-done.r, ...), custom_call_target="tpu_custom_call" | custom-call | bytes 8388608 | tf_op jit(solution)/shard_map/solve/pallas_call | solution.py:517
  96.8 4.1 %collective-permute-start.16 = (f32[8,2,24,128]{3,2,1,0:T(8,128)S(1)}, f32[8,2,24,128]{3,2,1,0:T(8,128)S(1)}, u32[]{:S(2)}, u32[]{:S(2)}) collective-permute-start(f32[8,2,24,128]{3,2,1,0:T(8,128)S(1)} %get-tuple-element.57), channel_id=1, source_target_pairs={{0,16},{1,5},{2,18},{3,7},{4,20},{5,1},{6,22},{7,3},{8,24},{9,13},... | collective-permute-start | bytes 589832 | tf_op jit(solution)/shard_map/ppermute | solution.py:583
  100.9 1.0 collective-permute-start.17
  101.9 0.0 collective-permute-start.18
  101.9 1.5 %collective-permute-start.19 = (f32[8,2,24,128]{3,2,1,0:T(8,128)S(1)}, f32[8,2,24,128]{3,2,1,0:T(8,128)S(1)}, u32[]{:S(2)}, u32[]{:S(2)}) collective-permute-start(f32[8,2,24,128]{3,2,1,0:T(8,128)S(1)} %get-tuple-element.60), channel_id=1, source_target_pairs={{0,24},{1,9},{2,26},{3,11},{4,28},{5,13},{6,30},{7,15},{8,16},{9,1... | collective-permute-start | bytes 589832 | tf_op jit(solution)/shard_map/ppermute | solution.py:583
  103.4 2.4 %collective-permute-start.20 = (f32[8,2,24,128]{3,2,1,0:T(8,128)S(1)}, f32[8,2,24,128]{3,2,1,0:T(8,128)S(1)}, u32[]{:S(2)}, u32[]{:S(2)}) collective-permute-start(f32[8,2,24,128]{3,2,1,0:T(8,128)S(1)} %get-tuple-element.61), channel_id=1, source_target_pairs={{0,20},{1,13},{2,22},{3,15},{4,16},{5,9},{6,18},{7,11},{8,28},{9,5... | collective-permute-start | bytes 589832 | tf_op jit(solution)/shard_map/ppermute | solution.py:583
  105.9 8.6 %collective-permute-done.16 = f32[8,2,24,128]{3,2,1,0:T(8,128)S(1)} collective-permute-done((f32[8,2,24,128]{3,2,1,0:T(8,128)S(1)}, f32[8,2,24,128]{3,2,1,0:T(8,128)S(1)}, u32[]{:S(2)}, u32[]{:S(2)}) %collective-permute-start.16) | collective-permute-done | bytes 196640 | tf_op jit(solution)/shard_map/ppermute | solution.py:583
  114.5 1.8 %collective-permute-start.22 = (f32[8,2,24,128]{3,2,1,0:T(8,128)S(1)}, f32[8,2,24,128]{3,2,1,0:T(8,128)S(1)}, u32[]{:S(2)}, u32[]{:S(2)}) collective-permute-start(f32[8,2,24,128]{3,2,1,0:T(8,128)S(1)} %get-tuple-element.63), channel_id=1, source_target_pairs={{0,28},{1,29},{2,30},{3,31},{4,24},{5,25},{6,26},{7,27},{8,20},{9,... | collective-permute-start | bytes 589832 | tf_op jit(solution)/shard_map/ppermute | solution.py:583
  116.3 1.7 %collective-permute-done.18 = f32[8,2,24,128]{3,2,1,0:T(8,128)S(1)} collective-permute-done((f32[8,2,24,128]{3,2,1,0:T(8,128)S(1)}, f32[8,2,24,128]{3,2,1,0:T(8,128)S(1)}, u32[]{:S(2)}, u32[]{:S(2)}) %collective-permute-start.18) | collective-permute-done | bytes 196640 | tf_op jit(solution)/shard_map/ppermute | solution.py:583
  118.0 14.3 %collective-permute-done.20 = f32[8,2,24,128]{3,2,1,0:T(8,128)S(1)} collective-permute-done((f32[8,2,24,128]{3,2,1,0:T(8,128)S(1)}, f32[8,2,24,128]{3,2,1,0:T(8,128)S(1)}, u32[]{:S(2)}, u32[]{:S(2)}) %collective-permute-start.20) | collective-permute-done | bytes 196640 | tf_op jit(solution)/shard_map/ppermute | solution.py:583
  132.3 0.0 collective-permute-done.21
  132.3 0.0 collective-permute-done.22
  132.3 2.1 %restore.1 = f32[3,4,256,128]{3,2,1,0:T(8,128)} custom-call(f32[384,128]{1,0:T(8,128)S(1)} %bitcast.26, f32[384,128]{1,0:T(8,128)S(1)} %bitcast.27, f32[384,128]{1,0:T(8,128)S(1)} %bitcast.28, f32[384,128]{1,0:T(8,128)S(1)} %bitcast.29, f32[384,128]{1,0:T(8,128)S(1)} %bitcast.30, f32[384,128]{1,0:T(8,128)S(1)} %bitcast.31, f32[384,128]{1,0:T(8,128)S(1)} %bitcast.32, ...), custom_call_target="tpu_custom_call" | custom-call | bytes 3145728 | tf_op jit(solution)/shard_map/restore/pallas_call | solution.py:561
  (35 shorter events, 0.2 us)
Async XLA Ops:
  2.1 9.8 %collective-permute-start = (f32[392,128]{1,0:T(8,128)}, f32[392,128]{1,0:T(8,128)S(1)}, u32[]{:S(2)}, u32[]{:S(2)}) collective-permute-start(f32[392,128]{1,0:T(8,128)} %get-tuple-element.36), channel_id=1, source_target_pairs={{0,8},{1,25},{2,10},{3,27},{8,0},{9,17},{10,2},{11,19},{16,24},{17... | collective-permute-start | bytes 602120 | tf_op jit(solution)/shard_map/ppermute | solution.py:583
  5.1 20.6 %collective-permute-start.1 = (f32[392,128]{1,0:T(8,128)}, f32[392,128]{1,0:T(8,128)S(1)}, u32[]{:S(2)}, u32[]{:S(2)}) collective-permute-start(f32[392,128]{1,0:T(8,128)} %get-tuple-element.37), channel_id=1, source_target_pairs={{0,24},{1,9},{2,26},{3,11},{8,16},{9,1},{10,18},{11,3},{16,8},{17,... | collective-permute-start | bytes 602120 | tf_op jit(solution)/shard_map/ppermute | solution.py:583
  7.6 19.7 %collective-permute-start.2 = (f32[392,128]{1,0:T(8,128)}, f32[392,128]{1,0:T(8,128)S(1)}, u32[]{:S(2)}, u32[]{:S(2)}) collective-permute-start(f32[392,128]{1,0:T(8,128)} %get-tuple-element.38), channel_id=1, source_target_pairs={{0,16},{1,17},{2,18},{3,19},{8,24},{9,25},{10,26},{11,27},{16,0},{... | collective-permute-start | bytes 602120 | tf_op jit(solution)/shard_map/ppermute | solution.py:583
  7.7 17.2 %copy-start.3 = (f32[392,128]{1,0:T(8,128)S(1)}, f32[392,128]{1,0:T(8,128)}, u32[]{:S(2)}) copy-start(f32[392,128]{1,0:T(8,128)} %get-tuple-element.35.refs_0_) | copy-start | bytes 602116
  7.7 17.2 %copy-start.2 = (bf16[128,256]{1,0:T(8,128)(2,1)S(1)}, bf16[128,256]{1,0:T(8,128)(2,1)}, u32[]{:S(2)}) copy-start(bf16[128,256]{1,0:T(8,128)(2,1)} %constant.22.clone.rest_ref.refs_5_.refs_2_) | copy-start | bytes 196612
  7.7 17.2 %copy-start.4 = (bf16[128,256]{1,0:T(8,128)(2,1)S(1)}, bf16[128,256]{1,0:T(8,128)(2,1)}, u32[]{:S(2)}) copy-start(bf16[128,256]{1,0:T(8,128)(2,1)} %constant.21.clone.top_ref) | copy-start | bytes 196612
  7.7 17.2 %copy-start.6 = (s32[64]{0:T(128)S(1)}, s32[64]{0:T(128)}, u32[]{:S(2)}) copy-start(s32[64]{0:T(128)} %owner_ref.1) | copy-start | bytes 772
  7.8 19.8 %copy-start.5 = (s32[8]{0:T(128)S(1)}, s32[8]{0:T(128)}, u32[]{:S(2)}) copy-start(s32[8]{0:T(128)} %low_ref.7) | copy-start | bytes 100
  11.9 0.7 copy-start
  14.7 11.0 %copy-start.1 = (f32[392,128]{1,0:T(8,128)S(1)}, f32[392,128]{1,0:T(8,128)}, u32[]{:S(2)}) copy-start(f32[392,128]{1,0:T(8,128)} %copy-done) | copy-start | bytes 602116
  14.7 30.2 %all-to-all-start.1 = ((f32[4,384,128]{2,1,0:T(8,128)}), f32[4,384,128]{2,1,0:T(8,128)S(1)}, u32[]{:S(2)}, u32[]{:S(2)}) async-start(f32[4,384,128]{2,1,0:T(8,128)} %pack.1), calls=%async_computation.1 | async-start | bytes 1572864 | tf_op jit(solution)/shard_map/all_to_all | solution.py:615
  33.0 1.5 %collective-permute-start.3 = (f32[3,4,32,128]{3,2,1,0:T(8,128)S(1)}, f32[3,4,32,128]{3,2,1,0:T(8,128)S(1)}, u32[]{:S(2)}, u32[]{:S(2)}) collective-permute-start(f32[3,4,32,128]{3,2,1,0:T(8,128)S(1)} %get-tuple-element.44), channel_id=1, source_target_pairs={{0,1},{1,0},{2,3},{3,2},{4,5},{5,4},{6,7},{7,6},{8,9},{9,8},{10,11... | collective-permute-start | bytes 589832 | tf_op jit(solution)/shard_map/ppermute | solution.py:589
  34.5 7.0 %collective-permute-start.4 = (f32[3,4,32,128]{3,2,1,0:T(8,128)S(1)}, f32[3,4,32,128]{3,2,1,0:T(8,128)S(1)}, u32[]{:S(2)}, u32[]{:S(2)}) collective-permute-start(f32[3,4,32,128]{3,2,1,0:T(8,128)S(1)} %add.27.refs_5_), channel_id=1, source_target_pairs={{0,2},{1,3},{2,0},{3,1},{4,6},{5,7},{6,4},{7,5},{8,10},{9,11},{10,... | collective-permute-start | bytes 589832 | tf_op jit(solution)/shard_map/ppermute | solution.py:589
  41.6 1.5 %collective-permute-start.5 = (f32[3,4,32,128]{3,2,1,0:T(8,128)S(1)}, f32[3,4,32,128]{3,2,1,0:T(8,128)S(1)}, u32[]{:S(2)}, u32[]{:S(2)}) collective-permute-start(f32[3,4,32,128]{3,2,1,0:T(8,128)S(1)} %add.28.kept_ref), channel_id=1, source_target_pairs={{0,1},{1,0},{2,3},{3,2},{4,5},{5,4},{6,7},{7,6},{8,9},{9,8},{10,11... | collective-permute-start | bytes 589832 | tf_op jit(solution)/shard_map/ppermute | solution.py:589
  44.9 45.1 %all-to-all-start = ((f32[8,8,24,128]{3,2,1,0:T(8,128)}), f32[8,8,24,128]{3,2,1,0:T(8,128)S(1)}, u32[]{:S(2)}, u32[]{:S(2)}) async-start(f32[8,8,24,128]{3,2,1,0:T(8,128)} %bitcast.5), calls=%async_computation | async-start | bytes 1572864 | tf_op jit(solution)/shard_map/all_to_all | solution.py:644
  58.1 1.5 %collective-permute-start.6 = (f32[3,4,32,128]{3,2,1,0:T(8,128)S(1)}, f32[3,4,32,128]{3,2,1,0:T(8,128)S(1)}, u32[]{:S(2)}, u32[]{:S(2)}) collective-permute-start(f32[3,4,32,128]{3,2,1,0:T(8,128)S(1)} %get-tuple-element.47), channel_id=1, source_target_pairs={{0,1},{1,0},{2,3},{3,2},{4,5},{5,4},{6,7},{7,6},{8,9},{9,8},{10,11... | collective-permute-start | bytes 589832 | tf_op jit(solution)/shard_map/ppermute | solution.py:589
  59.6 7.0 %collective-permute-start.7 = (f32[3,4,32,128]{3,2,1,0:T(8,128)S(1)}, f32[3,4,32,128]{3,2,1,0:T(8,128)S(1)}, u32[]{:S(2)}, u32[]{:S(2)}) collective-permute-start(f32[3,4,32,128]{3,2,1,0:T(8,128)S(1)} %add.29), channel_id=1, source_target_pairs={{0,2},{1,3},{2,0},{3,1},{4,6},{5,7},{6,4},{7,5},{8,10},{9,11},{10,... | collective-permute-start | bytes 589832 | tf_op jit(solution)/shard_map/ppermute | solution.py:589
  66.7 1.5 %collective-permute-start.8 = (f32[3,4,32,128]{3,2,1,0:T(8,128)S(1)}, f32[3,4,32,128]{3,2,1,0:T(8,128)S(1)}, u32[]{:S(2)}, u32[]{:S(2)}) collective-permute-start(f32[3,4,32,128]{3,2,1,0:T(8,128)S(1)} %add.30.kept_ref), channel_id=1, source_target_pairs={{0,1},{1,0},{2,3},{3,2},{4,5},{5,4},{6,7},{7,6},{8,9},{9,8},{10,11... | collective-permute-start | bytes 589832 | tf_op jit(solution)/shard_map/ppermute | solution.py:589
  69.3 7.9 %collective-permute-start.9 = (f32[8,24,128]{2,1,0:T(8,128)S(1)}, f32[8,24,128]{2,1,0:T(8,128)S(1)}, u32[]{:S(2)}, u32[]{:S(2)}) collective-permute-start(f32[8,24,128]{2,1,0:T(8,128)S(1)} %bitcast.43), channel_id=1, source_target_pairs={{0,16},{1,5},{2,18},{3,7},{4,20},{5,1},{6,22},{7,3},{8,24},{9,13},... | collective-permute-start | bytes 294920 | tf_op jit(solution)/shard_map/ppermute | solution.py:583
  72.3 8.7 %collective-permute-start.10 = (f32[8,24,128]{2,1,0:T(8,128)S(1)}, f32[8,24,128]{2,1,0:T(8,128)S(1)}, u32[]{:S(2)}, u32[]{:S(2)}) collective-permute-start(f32[8,24,128]{2,1,0:T(8,128)S(1)} %bitcast.42), channel_id=1, source_target_pairs={{0,4},{1,17},{2,6},{3,19},{4,0},{5,21},{6,2},{7,23},{8,12},{9,25},... | collective-permute-start | bytes 294920 | tf_op jit(solution)/shard_map/ppermute | solution.py:583
  73.7 10.4 %collective-permute-start.11 = (f32[8,24,128]{2,1,0:T(8,128)S(1)}, f32[8,24,128]{2,1,0:T(8,128)S(1)}, u32[]{:S(2)}, u32[]{:S(2)}) collective-permute-start(f32[8,24,128]{2,1,0:T(8,128)S(1)} %bitcast.41), channel_id=1, source_target_pairs={{0,8},{1,25},{2,10},{3,27},{4,12},{5,29},{6,14},{7,31},{8,0},{9,17... | collective-permute-start | bytes 294920 | tf_op jit(solution)/shard_map/ppermute | solution.py:583
  75.2 8.9 %collective-permute-start.12 = (f32[8,24,128]{2,1,0:T(8,128)S(1)}, f32[8,24,128]{2,1,0:T(8,128)S(1)}, u32[]{:S(2)}, u32[]{:S(2)}) collective-permute-start(f32[8,24,128]{2,1,0:T(8,128)S(1)} %bitcast.40), channel_id=1, source_target_pairs={{0,24},{1,9},{2,26},{3,11},{4,28},{5,13},{6,30},{7,15},{8,16},{9,1... | collective-permute-start | bytes 294920 | tf_op jit(solution)/shard_map/ppermute | solution.py:583
  75.7 14.2 %collective-permute-start.13 = (f32[8,24,128]{2,1,0:T(8,128)S(1)}, f32[8,24,128]{2,1,0:T(8,128)S(1)}, u32[]{:S(2)}, u32[]{:S(2)}) collective-permute-start(f32[8,24,128]{2,1,0:T(8,128)S(1)} %bitcast.39), channel_id=1, source_target_pairs={{0,20},{1,13},{2,22},{3,15},{4,16},{5,9},{6,18},{7,11},{8,28},{9,5... | collective-permute-start | bytes 294920 | tf_op jit(solution)/shard_map/ppermute | solution.py:583
  77.2 12.7 %collective-permute-start.14 = (f32[8,24,128]{2,1,0:T(8,128)S(1)}, f32[8,24,128]{2,1,0:T(8,128)S(1)}, u32[]{:S(2)}, u32[]{:S(2)}) collective-permute-start(f32[8,24,128]{2,1,0:T(8,128)S(1)} %bitcast.38), channel_id=1, source_target_pairs={{0,12},{1,21},{2,14},{3,23},{4,8},{5,17},{6,10},{7,19},{8,4},{9,29... | collective-permute-start | bytes 294920 | tf_op jit(solution)/shard_map/ppermute | solution.py:583
  80.9 9.0 %collective-permute-start.15 = (f32[8,24,128]{2,1,0:T(8,128)S(1)}, f32[8,24,128]{2,1,0:T(8,128)S(1)}, u32[]{:S(2)}, u32[]{:S(2)}) collective-permute-start(f32[8,24,128]{2,1,0:T(8,128)S(1)} %bitcast.37), channel_id=1, source_target_pairs={{0,28},{1,29},{2,30},{3,31},{4,24},{5,25},{6,26},{7,27},{8,20},{9,... | collective-permute-start | bytes 294920 | tf_op jit(solution)/shard_map/ppermute | solution.py:583
  96.8 17.7 %collective-permute-start.16 = (f32[8,2,24,128]{3,2,1,0:T(8,128)S(1)}, f32[8,2,24,128]{3,2,1,0:T(8,128)S(1)}, u32[]{:S(2)}, u32[]{:S(2)}) collective-permute-start(f32[8,2,24,128]{3,2,1,0:T(8,128)S(1)} %get-tuple-element.57), channel_id=1, source_target_pairs={{0,16},{1,5},{2,18},{3,7},{4,20},{5,1},{6,22},{7,3},{8,24},{9,13},... | collective-permute-start | bytes 589832 | tf_op jit(solution)/shard_map/ppermute | solution.py:583
  100.9 13.6 %collective-permute-start.17 = (f32[8,2,24,128]{3,2,1,0:T(8,128)S(1)}, f32[8,2,24,128]{3,2,1,0:T(8,128)S(1)}, u32[]{:S(2)}, u32[]{:S(2)}) collective-permute-start(f32[8,2,24,128]{3,2,1,0:T(8,128)S(1)} %get-tuple-element.58), channel_id=1, source_target_pairs={{0,4},{1,17},{2,6},{3,19},{4,0},{5,21},{6,2},{7,23},{8,12},{9,25},... | collective-permute-start | bytes 589832 | tf_op jit(solution)/shard_map/ppermute | solution.py:583
  101.9 16.2 %collective-permute-start.18 = (f32[8,2,24,128]{3,2,1,0:T(8,128)S(1)}, f32[8,2,24,128]{3,2,1,0:T(8,128)S(1)}, u32[]{:S(2)}, u32[]{:S(2)}) collective-permute-start(f32[8,2,24,128]{3,2,1,0:T(8,128)S(1)} %get-tuple-element.59), channel_id=1, source_target_pairs={{0,8},{1,25},{2,10},{3,27},{4,12},{5,29},{6,14},{7,31},{8,0},{9,17... | collective-permute-start | bytes 589832 | tf_op jit(solution)/shard_map/ppermute | solution.py:583
  101.9 16.2 %collective-permute-start.19 = (f32[8,2,24,128]{3,2,1,0:T(8,128)S(1)}, f32[8,2,24,128]{3,2,1,0:T(8,128)S(1)}, u32[]{:S(2)}, u32[]{:S(2)}) collective-permute-start(f32[8,2,24,128]{3,2,1,0:T(8,128)S(1)} %get-tuple-element.60), channel_id=1, source_target_pairs={{0,24},{1,9},{2,26},{3,11},{4,28},{5,13},{6,30},{7,15},{8,16},{9,1... | collective-permute-start | bytes 589832 | tf_op jit(solution)/shard_map/ppermute | solution.py:583
  103.4 28.9 %collective-permute-start.20 = (f32[8,2,24,128]{3,2,1,0:T(8,128)S(1)}, f32[8,2,24,128]{3,2,1,0:T(8,128)S(1)}, u32[]{:S(2)}, u32[]{:S(2)}) collective-permute-start(f32[8,2,24,128]{3,2,1,0:T(8,128)S(1)} %get-tuple-element.61), channel_id=1, source_target_pairs={{0,20},{1,13},{2,22},{3,15},{4,16},{5,9},{6,18},{7,11},{8,28},{9,5... | collective-permute-start | bytes 589832 | tf_op jit(solution)/shard_map/ppermute | solution.py:583
  114.5 17.8 %collective-permute-start.21 = (f32[8,2,24,128]{3,2,1,0:T(8,128)S(1)}, f32[8,2,24,128]{3,2,1,0:T(8,128)S(1)}, u32[]{:S(2)}, u32[]{:S(2)}) collective-permute-start(f32[8,2,24,128]{3,2,1,0:T(8,128)S(1)} %get-tuple-element.62), channel_id=1, source_target_pairs={{0,12},{1,21},{2,14},{3,23},{4,8},{5,17},{6,10},{7,19},{8,4},{9,29... | collective-permute-start | bytes 589832 | tf_op jit(solution)/shard_map/ppermute | solution.py:583
  114.5 17.8 %collective-permute-start.22 = (f32[8,2,24,128]{3,2,1,0:T(8,128)S(1)}, f32[8,2,24,128]{3,2,1,0:T(8,128)S(1)}, u32[]{:S(2)}, u32[]{:S(2)}) collective-permute-start(f32[8,2,24,128]{3,2,1,0:T(8,128)S(1)} %get-tuple-element.63), channel_id=1, source_target_pairs={{0,28},{1,29},{2,30},{3,31},{4,24},{5,25},{6,26},{7,27},{8,20},{9,... | collective-permute-start | bytes 589832 | tf_op jit(solution)/shard_map/ppermute | solution.py:583

commit v10 on v9

--- a/solution.py
+++ b/solution.py
@@ -265,10 +265,35 @@
     return (first, rest, back), order, slot_modes
 
 
-def nonlinear_kernel(low_ref, near_ref, count_ref, *refs):
-    block_refs, refs = (refs[:-12], refs[-12:])
-    first_ref, second_ref, back_ref, slot_ref, _, slotted_ref, kept_ref, sent_ref = refs[:8]
-    physical, products, sums, high_ref = refs[8:]
+def list_high(low_ref, high_ref, modes):
+    found = jnp.int32(0)
+    for mode in range(modes):
+        is_low = jnp.int32(0)
+        for member in range(low_ref.shape[0]):
+            is_low = is_low | (low_ref[member] == mode).astype(jnp.int32)
+        high_ref[found] = mode
+        found = found + 1 - is_low
+
+
+def tile_at(step, points):
+    halves = points // LANES
+    return (
+        pl.ds(pl.multiple_of((step // halves) * 8, 8), 8),
+        pl.ds(pl.multiple_of((step % halves) * LANES, LANES), LANES),
+    )
+
+
+def inverse(fields, back_ref):
+    columns = back_ref.shape[1] // 2
+    top, rest = two_parts(fields)
+    both = dot(top, back_ref[...])
+    return both[:, :columns] + both[:, columns:] + dot(rest, back_ref[:, :columns])
+
+
+def stress_kernel(low_ref, near_ref, *refs):
+    block_refs, refs = (refs[:-10], refs[-10:])
+    first_ref, second_ref, back_ref, _ = refs[:4]
+    slotted_ref, physical, kept_ref, sent_ref, sums, high_ref = refs[4:]
     components, modes, rows, columns = slotted_ref.shape
     if len(block_refs) > 1:
         bands = len(block_refs)
@@ -278,122 +303,147 @@
         places = list(range(bands))
         block_refs = [block_refs[0].at[index] for index in range(bands)]
     points, band_modes = (physical.shape[3], modes // bands)
-    members, highs = (sums.shape[1], products.shape[1])
+    members = sums.shape[1]
     odd = (lax.axis_index("real") & 1) == 1
-    found = jnp.int32(0)
-    for mode in range(modes):
-        is_low = jnp.int32(0)
-        for member in range(members):
-            is_low = is_low | (low_ref[member] == mode).astype(jnp.int32)
-        high_ref[found] = mode
-        found = found + 1 - is_low
-
-    def transform(component, carry):
-        size = band_modes * rows
-        for index, block_ref in enumerate(block_refs):
-            top, rest = two_parts(block_ref[pl.ds(pl.multiple_of(component * size, 8), size)])
-            both = dot(jnp.concatenate([top, rest], axis=1), first_ref[...])
-            fields = both[:, :points] + dot(top, second_ref[...])
+    list_high(low_ref, high_ref, modes)
+    size = band_modes * rows
+    for c in range(components):
+        joined = [block_ref[c * size : (c + 1) * size] for block_ref in block_refs]
+        top, rest = two_parts(jnp.concatenate(joined, axis=0))
+        both = dot(jnp.concatenate([top, rest], axis=1), first_ref[...])
+        fields = both[:, :points] + dot(top, second_ref[...])
+        for index in range(bands):
             place = pl.ds(places[index] * band_modes, band_modes)
-            physical[component, place] = fields.reshape(band_modes, rows, points)
-            slotted_ref[component, place] = both[:, points:].reshape(band_modes, rows, columns)
-        return carry
-
-    lax.fori_loop(0, components, transform, 0)
+            part = slice(index * size, (index + 1) * size)
+            physical[c, place] = fields[part].reshape(band_modes, rows, points)
+            slotted_ref[c, place] = both[part, points:].reshape(band_modes, rows, columns)
 
     def pairs(step, carry):
-        halves = points // LANES
-        place = (
-            pl.ds(pl.multiple_of((step // halves) * 8, 8), 8),
-            pl.ds(pl.multiple_of((step % halves) * LANES, LANES), LANES),
-        )
+        place = tile_at(step, points)
 
         def one_high(index, totals):
             mode = high_ref[index]
             own = [physical[(c, mode) + place] for c in range(components)]
-            result = [jnp.zeros((8, LANES), jnp.float32) for _ in range(components)]
             totals = list(totals)
             for member in range(members):
-                low = low_ref[member]
-                near = near_ref[mode, member]
-                partner = [physical[(c, near) + place] for c in range(components)]
-                low_one = [physical[(c, low) + place] for c in range(components)]
+                partner = physical[(1, near_ref[mode, member]) + place]
                 for c in range(components):
-                    if c == 1:
-                        result[c] = result[c] + low_one[1] * partner[1]
-                    else:
-                        result[c] = result[c] + (low_one[c] * partner[1] + partner[c] * low_one[1])
                     slot = member * components + c
-                    totals[slot] = totals[slot] + own[c] * partner[1]
-            for c in range(components):
-                products[(c, index) + place] = result[c] * 2.0 if c == 1 else result[c]
+                    totals[slot] = totals[slot] + own[c] * partner
             return tuple(totals)
 
         empty = tuple(jnp.zeros((8, LANES), jnp.float32) for _ in range(members * components))
-        totals = lax.fori_loop(0, highs, one_high, empty)
+        totals = lax.fori_loop(0, modes - members, one_high, empty)
         for member in range(members):
             for c in range(components):
                 sums[(c, member) + place] = totals[member * components + c]
         return carry
 
     lax.fori_loop(0, (rows // 8) * (points // LANES), pairs, 0)
-
-    def inverse(fields):
-        top, rest = two_parts(fields)
-        both = dot(top, back_ref[...])
-        return both[:, :columns] + both[:, columns:] + dot(rest, back_ref[:, :columns])
-
-    def finish(component, carry):
-        forcing = inverse(products[component].reshape(highs * rows, points))
-        forcing = forcing.reshape(highs, rows, columns)
-        for index in range(highs):
-            mode = high_ref[index]
-            active = slot_ref[:1] < count_ref[mode]
-            slotted_ref[component, mode] += jnp.where(active, forcing[index] * dt_step, 0.0)
-        stress = inverse(sums[component].reshape(members * rows, points))
-        stress = stress.reshape(2, members // 2, rows, columns)
-        kept_ref[component] = jnp.where(odd, stress[1], stress[0])
-        sent_ref[component] = jnp.where(odd, stress[0], stress[1])
-        return carry
-
-    lax.fori_loop(0, components, finish, 0)
-
-
-def nonlinear(blocks, shape, low_index, neighbours, mode_counts, tables, slot_modes, after):
+    stress = inverse(sums[...].reshape(components * members * rows, points), back_ref)
+    stress = stress.reshape(components, 2, members // 2, rows, columns)
+    kept_ref[...] = jnp.where(odd, stress[:, 1], stress[:, 0])
+    sent_ref[...] = jnp.where(odd, stress[:, 0], stress[:, 1])
+
+
+def stress_terms(blocks, shape, low_index, neighbours, tables, after):
     components, modes, rows, columns = shape
     members, points = (low_index.shape[0], 2 * columns)
-    highs = modes - members
+    half = jax.ShapeDtypeStruct((components, members // 2, rows, columns), jnp.float32)
     return pl.pallas_call(
-        nonlinear_kernel,
+        stress_kernel,
         out_shape=(
-            jax.ShapeDtypeStruct((components, modes, rows, columns), jnp.float32),
-            jax.ShapeDtypeStruct((components, members // 2, rows, columns), jnp.float32),
-            jax.ShapeDtypeStruct((components, members // 2, rows, columns), jnp.float32),
+            jax.ShapeDtypeStruct(shape, jnp.float32),
+            jax.ShapeDtypeStruct((components, modes, rows, points), jnp.float32),
+            half,
+            half,
         ),
-        in_specs=[SMEM] * 3 + [VMEM] * (len(blocks) + 4) + [pl.BlockSpec(memory_space=pl.ANY)],
-        out_specs=(VMEM, VMEM, VMEM),
+        in_specs=[SMEM] * 2 + [VMEM] * (len(blocks) + 3) + [pl.BlockSpec(memory_space=pl.ANY)],
+        out_specs=(VMEM,) * 4,
         scratch_shapes=[
-            pltpu.VMEM((components, modes, rows, points), jnp.float32),
-            pltpu.VMEM((components, highs, rows, points), jnp.float32),
             pltpu.VMEM((components, members, rows, points), jnp.float32),
             pltpu.SMEM((modes + 1,), jnp.int32),
         ],
         compiler_params=params(),
-        cost_estimate=cost(8 * components * modes * rows * points * members),
-        name="nonlinear",
-    )(low_index, neighbours, mode_counts, *blocks, *tables, slot_modes, after)
+        cost_estimate=cost(4 * components * modes * rows * points * members),
+        name="stress",
+    )(low_index, neighbours, *blocks, *tables, after)
+
+
+def products_kernel(
+    low_ref, near_ref, count_ref, physical, back_ref, slot_ref, out_ref, products, high_ref
+):
+    components, modes, rows, points = physical.shape
+    members, highs = (low_ref.shape[0], out_ref.shape[1])
+    list_high(low_ref, high_ref, modes)
+
+    def pairs(step, carry):
+        place = tile_at(step, points)
+        low = [
+            [physical[(c, low_ref[member]) + place] for c in range(components)]
+            for member in range(members)
+        ]
+
+        def one_high(index, inner):
+            mode = high_ref[index]
+            result = [jnp.zeros((8, LANES), jnp.float32) for _ in range(components)]
+            for member in range(members):
+                near = near_ref[mode, member]
+                partner = [physical[(c, near) + place] for c in range(components)]
+                for c in range(components):
+                    if c == 1:
+                        result[c] = result[c] + low[member][1] * partner[1]
+                    else:
+                        result[c] = result[c] + (
+                            low[member][c] * partner[1] + partner[c] * low[member][1]
+                        )
+            for c in range(components):
+                products[(c, index) + place] = result[c] * 2.0 if c == 1 else result[c]
+            return inner
+
+        lax.fori_loop(0, highs, one_high, 0)
+        return carry
+
+    lax.fori_loop(0, (rows // 8) * (points // LANES), pairs, 0)
+    forcing = inverse(products[...].reshape(components * highs * rows, points), back_ref)
+    forcing = forcing.reshape(out_ref.shape)
+    for index in range(highs):
+        active = slot_ref[:1] < count_ref[high_ref[index]]
+        out_ref[:, index] = jnp.where(active, forcing[:, index] * dt_step, 0.0)
+
+
+def high_terms(physical, low_index, neighbours, mode_counts, back, slot_modes):
+    components, modes, rows, points = physical.shape
+    highs = modes - low_index.shape[0]
+    return pl.pallas_call(
+        products_kernel,
+        out_shape=jax.ShapeDtypeStruct((components, highs, rows, points // 2), jnp.float32),
+        in_specs=[SMEM] * 3 + [VMEM] * 3,
+        out_specs=VMEM,
+        scratch_shapes=[
+            pltpu.VMEM((components, highs, rows, points), jnp.float32),
+            pltpu.SMEM((modes + 1,), jnp.int32),
+        ],
+        compiler_params=params(),
+        cost_estimate=cost(4 * physical.size * low_index.shape[0]),
+        name="products",
+    )(low_index, neighbours, mode_counts, physical, back, slot_modes)
 
 
 def outgoing_kernel(
-    low_ref, count_ref, slotted_ref, kept_ref, other_ref, slot_ref, *refs,
+    low_ref, count_ref, slotted_ref, forcing_ref, kept_ref, other_ref, slot_ref, *refs,
     groups, band_modes, owners, scale
 ):
-    out_refs, (full, turned) = (refs[:-2], refs[-2:])
+    out_refs, (full, turned, high_ref) = (refs[:-3], refs[-3:])
     components, modes, rows, columns = slotted_ref.shape
     half, slots = (kept_ref.shape[1], columns // 2 // owners)
     per_slot = out_refs[0].shape[0] * len(out_refs) // (columns // 2)
     own = lax.axis_index("real") & 1
+    list_high(low_ref, high_ref, modes)
     full[...] = slotted_ref[...]
+    for index in range(forcing_ref.shape[1]):
+        for c in range(components):
+            full[c, high_ref[index]] += forcing_ref[c, index]
     for member in range(half):
         for part_ref, start in ((kept_ref, own * half), (other_ref, (1 - own) * half)):
             mode = low_ref[start + member]
@@ -425,7 +475,7 @@
 
 
 def outgoing(
-    slotted, kept, other, low_index, mode_counts, slot_modes, groups, band_modes, owners,
+    slotted, forcing, kept, other, low_index, mode_counts, slot_modes, groups, band_modes, owners,
     realizations, separate,
 ):
     components, modes, rows, columns = slotted.shape
@@ -437,15 +487,16 @@
             scale=dt_step / realizations,
         ),
         out_shape=(jax.ShapeDtypeStruct((total // count, lanes), jnp.float32),) * count,
-        in_specs=[SMEM, SMEM] + [VMEM] * 4,
+        in_specs=[SMEM, SMEM] + [VMEM] * 5,
         out_specs=(VMEM,) * count,
         scratch_shapes=[
-            pltpu.VMEM(slotted.shape, jnp.float32), pltpu.VMEM((columns, lanes), jnp.float32)
+            pltpu.VMEM(slotted.shape, jnp.float32), pltpu.VMEM((columns, lanes), jnp.float32),
+            pltpu.SMEM((modes + 1,), jnp.int32),
         ],
         compiler_params=params(),
         cost_estimate=cost(8 * slotted.size),
         name="outgoing",
-    )(low_index, mode_counts, slotted, kept, other, slot_modes)
+    )(low_index, mode_counts, slotted, forcing, kept, other, slot_modes)
 
 
 def regroup(blocks, rows):
@@ -625,16 +676,17 @@
     after = slot_modes
     received = []
     for piece, part in enumerate(parts):
-        slotted, kept, sent = nonlinear(
-            part, shape, low_index, neighbours, mode_counts, tables, slot_modes, after
+        slotted, physical, kept, sent = stress_terms(
+            part, shape, low_index, neighbours, tables, after
         )
+        forcing = high_terms(physical, low_index, neighbours, mode_counts, tables[2], slot_modes)
         kept = after = kept + swap(sent, 1)
         step = 2
         while step < realizations:
             kept = kept + swap(kept, step)
             step *= 2
         blocks = outgoing(
-            slotted, kept, swap(kept, 1), low_index, mode_counts, slot_modes, groups, band_modes,
+            slotted, forcing, kept, swap(kept, 1), low_index, mode_counts, slot_modes, groups, band_modes,
             owners, realizations, piece > 0,
         )
         if piece:

time: 137 us -> 136 us (level)
  waiting for transfers between devices: 52.9 us -> 47.8 us
  Pallas kernels: 27.5 us -> 29.8 us
  starting transfers between devices: 52 us -> 54.2 us
    ppermute x6, waiting for transfers between devices: 16.6 us -> 13.6 us  [swap(): return lax.ppermute(value, 'real', pairs)]
    pallas_call x2 -> x4, Pallas kernels: 10.8 us -> 12.9 us  [the longest x2 6.93 us: stress_terms(): pl.pallas_call(stress_kernel, out_shape=(jax.ShapeDtypeStruct(shape, jnp....]
    ppermute x17, waiting for transfers between devices: 36.2 us -> 34.2 us  [exchange(): result[position] = lax.ppermute(blocks[position], axes + ('real',), pairs)]
    ppermute x17, starting transfers between devices: 31.3 us -> 33.2 us  [exchange(): result[position] = lax.ppermute(blocks[position], axes + ('real',), pairs)]
  transfers between devices with their start and end apart: 25 -> 25, of which waited for: 12 -> 10; matrix products, arithmetic and copies ran while one was open for 1% -> 1% of each run, Pallas kernels for 12% -> 14%
where the time goes in v10:
time: 136 us; the launch traced here: 134 us
  starting transfers between devices  54.2 us (40%)
  waiting for transfers between devices  47.8 us (35%)
  Pallas kernels  29.8 us (22%)
  local copies, waits for them, and re-layouts  1.56 us (1%)
    ppermute x17, waiting for transfers between devices, exchange(): result[position] = lax.ppermute(blocks[position], axes + ('real',), pairs)  34.2 us
    ppermute x17, starting transfers between devices, exchange(): result[position] = lax.ppermute(blocks[position], axes + ('real',), pairs)  33.2 us
    ppermute x6, waiting for transfers between devices, swap(): return lax.ppermute(value, 'real', pairs)  13.6 us
    all_to_all x1, starting transfers between devices, local(): block = lax.all_to_all(block, 'kx', split_axis=0, concat_axis=0, tiled=True)  9.53 us
    all_to_all x1, starting transfers between devices, local(): lax.all_to_all(block, ('kx', 'ht'), split_axis=0, concat_axis=0, tiled=True)  7.83 us
    pallas_call x2, Pallas kernels, stress_terms(): pl.pallas_call(stress_kernel, out_shape=(jax.ShapeDtypeStruct(shape, jnp....  6.93 us
    pallas_call x1, Pallas kernels, solve(): pl.pallas_call(functools.partial(solve_kernel, groups=groups, kx_count=kx...  6.8 us
    pallas_call x2, Pallas kernels, high_terms(): pl.pallas_call(products_kernel, out_shape=jax.ShapeDtypeStruct((component...  6.01 us
  transfers between devices with their start and end apart: 25, of which 10 were waited for; matrix products, arithmetic and copies ran while one was open for 1% of the time, Pallas kernels for 14%

profile of v10, /device:TPU:0, one launch (start us, length us, event | category | flops | bytes accessed | tf_op | source)
XLA Modules:
  0.0 133.8 jit_solution(5753456151558791964)
XLA Ops:
  0.0 2.1 %pack_first.1 = (f32[392,128]{1,0:T(8,128)}, f32[392,128]{1,0:T(8,128)}, f32[392,128]{1,0:T(8,128)}, f32[392,128]{1,0:T(8,128)}) custom-call(s32[4,8]{1,0:T(4,128)} %near_ref.1, s32[4]{0:T(128)} %count_ref.1, f32[12,2,4,32,128]{4,3,2,1,0:T(8,128)} %bitcast.46), custom_call_target="tpu_custom_call" | custom-call | bytes 1572864 | tf_op jit(solution)/shard_map/pack_first/pallas_call | solution.py:175
  2.1 3.0 %collective-permute-start = (f32[392,128]{1,0:T(8,128)}, f32[392,128]{1,0:T(8,128)S(1)}, u32[]{:S(2)}, u32[]{:S(2)}) collective-permute-start(f32[392,128]{1,0:T(8,128)} %get-tuple-element.38), channel_id=1, source_target_pairs={{0,8},{1,25},{2,10},{3,27},{8,0},{9,17},{10,2},{11,19},{16,24},{17... | collective-permute-start | bytes 602120 | tf_op jit(solution)/shard_map/ppermute | solution.py:634
  5.1 2.5 %collective-permute-start.1 = (f32[392,128]{1,0:T(8,128)}, f32[392,128]{1,0:T(8,128)S(1)}, u32[]{:S(2)}, u32[]{:S(2)}) collective-permute-start(f32[392,128]{1,0:T(8,128)} %get-tuple-element.39), channel_id=1, source_target_pairs={{0,24},{1,9},{2,26},{3,11},{8,16},{9,1},{10,18},{11,3},{16,8},{17,... | collective-permute-start | bytes 602120 | tf_op jit(solution)/shard_map/ppermute | solution.py:634
  7.6 0.1 collective-permute-start.2
  7.7 0.0 copy-start.5
  7.7 4.2 %collective-permute-done.refs_1_._ = f32[392,128]{1,0:T(8,128)S(1)} collective-permute-done((f32[392,128]{1,0:T(8,128)}, f32[392,128]{1,0:T(8,128)S(1)}, u32[]{:S(2)}, u32[]{:S(2)}) %collective-permute-start) | collective-permute-done | bytes 200736 | tf_op jit(solution)/shard_map/ppermute | solution.py:634
  11.9 0.7 copy-done
  12.6 2.1 %pack.1 = f32[4,384,128]{2,1,0:T(8,128)} custom-call(f32[12,2,4,32,128]{4,3,2,1,0:T(8,128)} %bitcast.47, f32[392,128]{1,0:T(8,128)} %copy-done), custom_call_target="tpu_custom_call" | custom-call | bytes 1572864 | tf_op jit(solution)/shard_map/pack/pallas_call | solution.py:201
  14.7 9.5 %all-to-all-start.1 = ((f32[4,384,128]{2,1,0:T(8,128)}), f32[4,384,128]{2,1,0:T(8,128)S(1)}, u32[]{:S(2)}, u32[]{:S(2)}) async-start(f32[4,384,128]{2,1,0:T(8,128)} %pack.1), calls=%async_computation.1 | async-start | bytes 1572864 | tf_op jit(solution)/shard_map/all_to_all | solution.py:666
  24.2 0.1 broadcast_in_dim.85
  24.3 0.1 broadcast_in_dim.86
  24.4 0.1 broadcast_in_dim.91
  24.5 0.1 broadcast_in_dim.92
  24.6 0.1 broadcast_in_dim.96
  24.6 0.1 broadcast_in_dim.97
  24.7 0.1 broadcast_in_dim.101
  24.8 0.1 broadcast_in_dim.102
  24.9 0.8 tables.1
  25.7 1.6 %collective-permute-done.2.refs_3_ = f32[392,128]{1,0:T(8,128)S(1)} collective-permute-done((f32[392,128]{1,0:T(8,128)}, f32[392,128]{1,0:T(8,128)S(1)}, u32[]{:S(2)}, u32[]{:S(2)}) %collective-permute-start.2) | collective-permute-done | bytes 200736 | tf_op jit(solution)/shard_map/ppermute | solution.py:634
  27.3 0.1 add_convert_fusion
  27.4 3.5 %stress.2 = (f32[3,16,32,128]{3,2,1,0:T(8,128)S(1)}, f32[3,16,32,256]{3,2,1,0:T(8,128)S(1)}, f32[3,4,32,128]{3,2,1,0:T(8,128)S(1)}, f32[3,4,32,128]{3,2,1,0:T(8,128)S(1)}) custom-call(s32[8]{0:T(128)S(1)} %copy-done.5, s32[16,8]{1,0:T(8,128)S(1)} %bitcast.26, f32[392,128]{1,0:T(8,128)S(1)} %copy-done.3, f32[392,128]{1,0:T(8,128)S(1)} %copy-done.1, ...), custom_call_target="tpu_custom_call" | custom-call | bytes 12582912 | tf_op jit(solution)/shard_map/stress/pallas_call | solution.py:353
  30.9 0.1 collective-permute-start.3
  31.0 1.4 %collective-permute-done.3 = f32[3,4,32,128]{3,2,1,0:T(8,128)S(1)} collective-permute-done((f32[3,4,32,128]{3,2,1,0:T(8,128)S(1)}, f32[3,4,32,128]{3,2,1,0:T(8,128)S(1)}, u32[]{:S(2)}, u32[]{:S(2)}) %collective-permute-start.3) | collective-permute-done | bytes 196640 | tf_op jit(solution)/shard_map/ppermute | solution.py:640
  32.4 1.6 %collective-permute-start.4 = (f32[3,4,32,128]{3,2,1,0:T(8,128)S(1)}, f32[3,4,32,128]{3,2,1,0:T(8,128)S(1)}, u32[]{:S(2)}, u32[]{:S(2)}) collective-permute-start(f32[3,4,32,128]{3,2,1,0:T(8,128)S(1)} %add.27.refs_4_), channel_id=1, source_target_pairs={{0,2},{1,3},{2,0},{3,1},{4,6},{5,7},{6,4},{7,5},{8,10},{9,11},{10,... | collective-permute-start | bytes 589832 | tf_op jit(solution)/shard_map/ppermute | solution.py:640
  34.0 5.4 %collective-permute-done.4 = f32[3,4,32,128]{3,2,1,0:T(8,128)S(1)} collective-permute-done((f32[3,4,32,128]{3,2,1,0:T(8,128)S(1)}, f32[3,4,32,128]{3,2,1,0:T(8,128)S(1)}, u32[]{:S(2)}, u32[]{:S(2)}) %collective-permute-start.4) | collective-permute-done | bytes 196640 | tf_op jit(solution)/shard_map/ppermute | solution.py:640
  39.5 0.1 collective-permute-start.5
  39.5 0.2 slice_reduce_fusion.count_ref
  39.7 3.0 %products.2.forcing_ref = f32[3,8,32,128]{3,2,1,0:T(8,128)S(1)} custom-call(s32[8]{0:T(128)S(1)} %copy-done.5, s32[16,8]{1,0:T(8,128)S(1)} %bitcast.27, s32[16]{0:T(128)S(1)} %slice_reduce_fusion.count_ref, f32[3,16,32,256]{3,2,1,0:T(8,128)S(1)} %get-tuple-element.45.physical, bf16[256,256]{1,0:T(8,128)(2,1)S(1)} %get-tuple-element.42.refs_6_.back_ref.refs_3_, ...), custom_call_target="tpu_custom_call" | custom-call | bytes 12582912 | tf_op jit(solution)/shard_map/products/pallas_call | solution.py:418
  42.7 0.0 collective-permute-done.5.other_ref
  42.7 1.9 %outgoing.2 = f32[1536,128]{1,0:T(8,128)} custom-call(s32[8]{0:T(128)S(1)} %copy-done.5, s32[16]{0:T(128)S(1)} %slice_reduce_fusion.count_ref, f32[3,16,32,128]{3,2,1,0:T(8,128)S(1)} %get-tuple-element.44.slotted_ref, f32[3,8,32,128]{3,2,1,0:T(8,128)S(1)} %products.2.forcing_ref, f32[3,4,32,128]{3,2,1,0:T(8,128)S(1)} %add.28.kept_ref, ...), custom_call_target="tpu_custom_call" | custom-call | bytes 1572864 | tf_op jit(solution)/shard_map/outgoing/pallas_call | solution.py:484
  44.6 7.8 %all-to-all-start = ((f32[8,8,24,128]{3,2,1,0:T(8,128)}), f32[8,8,24,128]{3,2,1,0:T(8,128)S(1)}, u32[]{:S(2)}, u32[]{:S(2)}) async-start(f32[8,8,24,128]{3,2,1,0:T(8,128)} %bitcast.5), calls=%async_computation | async-start | bytes 1572864 | tf_op jit(solution)/shard_map/all_to_all | solution.py:696
  52.5 3.5 %stress.3 = (f32[3,16,32,128]{3,2,1,0:T(8,128)S(1)}, f32[3,16,32,256]{3,2,1,0:T(8,128)S(1)}, f32[3,4,32,128]{3,2,1,0:T(8,128)S(1)}, f32[3,4,32,128]{3,2,1,0:T(8,128)S(1)}) custom-call(s32[8]{0:T(128)S(1)} %copy-done.5, s32[16,8]{1,0:T(8,128)S(1)} %bitcast.28, f32[4,384,128]{2,1,0:T(8,128)S(1)} %all-to-all-done.1.refs_0_, ...), custom_call_target="tpu_custom_call" | custom-call | bytes 12582912 | tf_op jit(solution)/shard_map/stress/pallas_call | solution.py:353
  56.0 0.3 collective-permute-start.6
  56.2 1.2 collective-permute-done.6
  57.5 1.6 %collective-permute-start.7 = (f32[3,4,32,128]{3,2,1,0:T(8,128)S(1)}, f32[3,4,32,128]{3,2,1,0:T(8,128)S(1)}, u32[]{:S(2)}, u32[]{:S(2)}) collective-permute-start(f32[3,4,32,128]{3,2,1,0:T(8,128)S(1)} %add.29), channel_id=1, source_target_pairs={{0,2},{1,3},{2,0},{3,1},{4,6},{5,7},{6,4},{7,5},{8,10},{9,11},{10,... | collective-permute-start | bytes 589832 | tf_op jit(solution)/shard_map/ppermute | solution.py:640
  59.0 5.5 %collective-permute-done.7 = f32[3,4,32,128]{3,2,1,0:T(8,128)S(1)} collective-permute-done((f32[3,4,32,128]{3,2,1,0:T(8,128)S(1)}, f32[3,4,32,128]{3,2,1,0:T(8,128)S(1)}, u32[]{:S(2)}, u32[]{:S(2)}) %collective-permute-start.7) | collective-permute-done | bytes 196640 | tf_op jit(solution)/shard_map/ppermute | solution.py:640
  64.6 0.1 collective-permute-start.8
  64.7 3.0 %products.3.forcing_ref = f32[3,8,32,128]{3,2,1,0:T(8,128)S(1)} custom-call(s32[8]{0:T(128)S(1)} %copy-done.5, s32[16,8]{1,0:T(8,128)S(1)} %bitcast.29, s32[16]{0:T(128)S(1)} %slice_reduce_fusion.count_ref, f32[3,16,32,256]{3,2,1,0:T(8,128)S(1)} %get-tuple-element.49.physical, bf16[256,256]{1,0:T(8,128)(2,1)S(1)} %get-tuple-element.42.refs_6_.back_ref.refs_3_, ...), custom_call_target="tpu_custom_call" | custom-call | bytes 12582912 | tf_op jit(solution)/shard_map/products/pallas_call | solution.py:418
  67.7 0.0 collective-permute-done.8.other_ref
  67.7 1.2 outgoing.3
  68.9 2.9 %collective-permute-start.9 = (f32[8,24,128]{2,1,0:T(8,128)S(1)}, f32[8,24,128]{2,1,0:T(8,128)S(1)}, u32[]{:S(2)}, u32[]{:S(2)}) collective-permute-start(f32[8,24,128]{2,1,0:T(8,128)S(1)} %bitcast.45), channel_id=1, source_target_pairs={{0,16},{1,5},{2,18},{3,7},{4,20},{5,1},{6,22},{7,3},{8,24},{9,13},... | collective-permute-start | bytes 294920 | tf_op jit(solution)/shard_map/ppermute | solution.py:634
  71.8 1.5 %collective-permute-start.10 = (f32[8,24,128]{2,1,0:T(8,128)S(1)}, f32[8,24,128]{2,1,0:T(8,128)S(1)}, u32[]{:S(2)}, u32[]{:S(2)}) collective-permute-start(f32[8,24,128]{2,1,0:T(8,128)S(1)} %bitcast.44), channel_id=1, source_target_pairs={{0,4},{1,17},{2,6},{3,19},{4,0},{5,21},{6,2},{7,23},{8,12},{9,25},... | collective-permute-start | bytes 294920 | tf_op jit(solution)/shard_map/ppermute | solution.py:634
  73.3 1.5 %collective-permute-start.11 = (f32[8,24,128]{2,1,0:T(8,128)S(1)}, f32[8,24,128]{2,1,0:T(8,128)S(1)}, u32[]{:S(2)}, u32[]{:S(2)}) collective-permute-start(f32[8,24,128]{2,1,0:T(8,128)S(1)} %bitcast.43), channel_id=1, source_target_pairs={{0,8},{1,25},{2,10},{3,27},{4,12},{5,29},{6,14},{7,31},{8,0},{9,17... | collective-permute-start | bytes 294920 | tf_op jit(solution)/shard_map/ppermute | solution.py:634
  74.7 0.6 collective-permute-start.12
  75.3 1.5 %collective-permute-start.13 = (f32[8,24,128]{2,1,0:T(8,128)S(1)}, f32[8,24,128]{2,1,0:T(8,128)S(1)}, u32[]{:S(2)}, u32[]{:S(2)}) collective-permute-start(f32[8,24,128]{2,1,0:T(8,128)S(1)} %bitcast.41), channel_id=1, source_target_pairs={{0,20},{1,13},{2,22},{3,15},{4,16},{5,9},{6,18},{7,11},{8,28},{9,5... | collective-permute-start | bytes 294920 | tf_op jit(solution)/shard_map/ppermute | solution.py:634
  76.8 4.3 %collective-permute-start.14 = (f32[8,24,128]{2,1,0:T(8,128)S(1)}, f32[8,24,128]{2,1,0:T(8,128)S(1)}, u32[]{:S(2)}, u32[]{:S(2)}) collective-permute-start(f32[8,24,128]{2,1,0:T(8,128)S(1)} %bitcast.40), channel_id=1, source_target_pairs={{0,12},{1,21},{2,14},{3,23},{4,8},{5,17},{6,10},{7,19},{8,4},{9,29... | collective-permute-start | bytes 294920 | tf_op jit(solution)/shard_map/ppermute | solution.py:634
  81.1 0.0 collective-permute-done.10.refs_3_
  81.1 3.2 %collective-permute-start.15 = (f32[8,24,128]{2,1,0:T(8,128)S(1)}, f32[8,24,128]{2,1,0:T(8,128)S(1)}, u32[]{:S(2)}, u32[]{:S(2)}) collective-permute-start(f32[8,24,128]{2,1,0:T(8,128)S(1)} %bitcast.39), channel_id=1, source_target_pairs={{0,28},{1,29},{2,30},{3,31},{4,24},{5,25},{6,26},{7,27},{8,20},{9,... | collective-permute-start | bytes 294920 | tf_op jit(solution)/shard_map/ppermute | solution.py:634
  84.3 0.0 collective-permute-done.11.refs_4_
  84.3 0.0 collective-permute-done.12.refs_5_
  84.3 5.2 %collective-permute-done.13.refs_6_ = f32[8,24,128]{2,1,0:T(8,128)S(1)} collective-permute-done((f32[8,24,128]{2,1,0:T(8,128)S(1)}, f32[8,24,128]{2,1,0:T(8,128)S(1)}, u32[]{:S(2)}, u32[]{:S(2)}) %collective-permute-start.13) | collective-permute-done | bytes 98336 | tf_op jit(solution)/shard_map/ppermute | solution.py:634
  89.5 0.0 collective-permute-done.14.refs_7_
  89.5 0.0 collective-permute-done.15.refs_8_
  89.5 6.8 %solve.1 = (f32[8,2,24,128]{3,2,1,0:T(8,128)S(1)}, f32[8,2,24,128]{3,2,1,0:T(8,128)S(1)}, f32[8,2,24,128]{3,2,1,0:T(8,128)S(1)}, f32[8,2,24,128]{3,2,1,0:T(8,128...) custom-call(f32[8,8,24,128]{3,2,1,0:T(8,128)S(1)} %all-to-all-done.r, ...), custom_call_target="tpu_custom_call" | custom-call | bytes 8388608 | tf_op jit(solution)/shard_map/solve/pallas_call | solution.py:568
  96.3 4.5 %collective-permute-start.16 = (f32[8,2,24,128]{3,2,1,0:T(8,128)S(1)}, f32[8,2,24,128]{3,2,1,0:T(8,128)S(1)}, u32[]{:S(2)}, u32[]{:S(2)}) collective-permute-start(f32[8,2,24,128]{3,2,1,0:T(8,128)S(1)} %get-tuple-element.61), channel_id=1, source_target_pairs={{0,16},{1,5},{2,18},{3,7},{4,20},{5,1},{6,22},{7,3},{8,24},{9,13},... | collective-permute-start | bytes 589832 | tf_op jit(solution)/shard_map/ppermute | solution.py:634
  100.8 0.7 collective-permute-start.17
  101.5 0.5 collective-permute-start.18
  102.0 1.1 collective-permute-start.19
  103.0 2.7 %collective-permute-start.20 = (f32[8,2,24,128]{3,2,1,0:T(8,128)S(1)}, f32[8,2,24,128]{3,2,1,0:T(8,128)S(1)}, u32[]{:S(2)}, u32[]{:S(2)}) collective-permute-start(f32[8,2,24,128]{3,2,1,0:T(8,128)S(1)} %get-tuple-element.65), channel_id=1, source_target_pairs={{0,20},{1,13},{2,22},{3,15},{4,16},{5,9},{6,18},{7,11},{8,28},{9,5... | collective-permute-start | bytes 589832 | tf_op jit(solution)/shard_map/ppermute | solution.py:634
  105.8 8.5 %collective-permute-done.16 = f32[8,2,24,128]{3,2,1,0:T(8,128)S(1)} collective-permute-done((f32[8,2,24,128]{3,2,1,0:T(8,128)S(1)}, f32[8,2,24,128]{3,2,1,0:T(8,128)S(1)}, u32[]{:S(2)}, u32[]{:S(2)}) %collective-permute-start.16) | collective-permute-done | bytes 196640 | tf_op jit(solution)/shard_map/ppermute | solution.py:634
  114.3 2.8 %collective-permute-start.22 = (f32[8,2,24,128]{3,2,1,0:T(8,128)S(1)}, f32[8,2,24,128]{3,2,1,0:T(8,128)S(1)}, u32[]{:S(2)}, u32[]{:S(2)}) collective-permute-start(f32[8,2,24,128]{3,2,1,0:T(8,128)S(1)} %get-tuple-element.67), channel_id=1, source_target_pairs={{0,28},{1,29},{2,30},{3,31},{4,24},{5,25},{6,26},{7,27},{8,20},{9,... | collective-permute-start | bytes 589832 | tf_op jit(solution)/shard_map/ppermute | solution.py:634
  117.1 0.6 collective-permute-done.18
  117.7 14.1 %collective-permute-done.20 = f32[8,2,24,128]{3,2,1,0:T(8,128)S(1)} collective-permute-done((f32[8,2,24,128]{3,2,1,0:T(8,128)S(1)}, f32[8,2,24,128]{3,2,1,0:T(8,128)S(1)}, u32[]{:S(2)}, u32[]{:S(2)}) %collective-permute-start.20) | collective-permute-done | bytes 196640 | tf_op jit(solution)/shard_map/ppermute | solution.py:634
  131.7 2.1 %restore.1 = f32[3,4,256,128]{3,2,1,0:T(8,128)} custom-call(f32[384,128]{1,0:T(8,128)S(1)} %bitcast.30, f32[384,128]{1,0:T(8,128)S(1)} %bitcast.31, f32[384,128]{1,0:T(8,128)S(1)} %bitcast.32, f32[384,128]{1,0:T(8,128)S(1)} %bitcast.33, f32[384,128]{1,0:T(8,128)S(1)} %bitcast.34, f32[384,128]{1,0:T(8,128)S(1)} %bitcast.35, f32[384,128]{1,0:T(8,128)S(1)} %bitcast.36, ...), custom_call_target="tpu_custom_call" | custom-call | bytes 3145728 | tf_op jit(solution)/shard_map/restore/pallas_call | solution.py:612
  (37 shorter events, 0.2 us)
Async XLA Ops:
  2.1 9.8 %collective-permute-start = (f32[392,128]{1,0:T(8,128)}, f32[392,128]{1,0:T(8,128)S(1)}, u32[]{:S(2)}, u32[]{:S(2)}) collective-permute-start(f32[392,128]{1,0:T(8,128)} %get-tuple-element.38), channel_id=1, source_target_pairs={{0,8},{1,25},{2,10},{3,27},{8,0},{9,17},{10,2},{11,19},{16,24},{17... | collective-permute-start | bytes 602120 | tf_op jit(solution)/shard_map/ppermute | solution.py:634
  5.1 20.6 %collective-permute-start.1 = (f32[392,128]{1,0:T(8,128)}, f32[392,128]{1,0:T(8,128)S(1)}, u32[]{:S(2)}, u32[]{:S(2)}) collective-permute-start(f32[392,128]{1,0:T(8,128)} %get-tuple-element.39), channel_id=1, source_target_pairs={{0,24},{1,9},{2,26},{3,11},{8,16},{9,1},{10,18},{11,3},{16,8},{17,... | collective-permute-start | bytes 602120 | tf_op jit(solution)/shard_map/ppermute | solution.py:634
  7.6 19.7 %collective-permute-start.2 = (f32[392,128]{1,0:T(8,128)}, f32[392,128]{1,0:T(8,128)S(1)}, u32[]{:S(2)}, u32[]{:S(2)}) collective-permute-start(f32[392,128]{1,0:T(8,128)} %get-tuple-element.40), channel_id=1, source_target_pairs={{0,16},{1,17},{2,18},{3,19},{8,24},{9,25},{10,26},{11,27},{16,0},{... | collective-permute-start | bytes 602120 | tf_op jit(solution)/shard_map/ppermute | solution.py:634
  7.7 17.2 %copy-start.3 = (f32[392,128]{1,0:T(8,128)S(1)}, f32[392,128]{1,0:T(8,128)}, u32[]{:S(2)}) copy-start(f32[392,128]{1,0:T(8,128)} %get-tuple-element.37.refs_0_) | copy-start | bytes 602116
  7.7 17.2 %copy-start.2 = (bf16[128,256]{1,0:T(8,128)(2,1)S(1)}, bf16[128,256]{1,0:T(8,128)(2,1)}, u32[]{:S(2)}) copy-start(bf16[128,256]{1,0:T(8,128)(2,1)} %constant.22.clone.rest_ref.refs_5_.refs_2_) | copy-start | bytes 196612
  7.7 17.2 %copy-start.4 = (bf16[128,256]{1,0:T(8,128)(2,1)S(1)}, bf16[128,256]{1,0:T(8,128)(2,1)}, u32[]{:S(2)}) copy-start(bf16[128,256]{1,0:T(8,128)(2,1)} %constant.21.clone.top_ref) | copy-start | bytes 196612
  7.7 17.2 %copy-start.6 = (s32[64]{0:T(128)S(1)}, s32[64]{0:T(128)}, u32[]{:S(2)}) copy-start(s32[64]{0:T(128)} %owner_ref.1) | copy-start | bytes 772
  7.7 19.7 %copy-start.5 = (s32[8]{0:T(128)S(1)}, s32[8]{0:T(128)}, u32[]{:S(2)}) copy-start(s32[8]{0:T(128)} %low_ref.11) | copy-start | bytes 100
  11.9 0.7 copy-start
  14.7 11.0 %copy-start.1 = (f32[392,128]{1,0:T(8,128)S(1)}, f32[392,128]{1,0:T(8,128)}, u32[]{:S(2)}) copy-start(f32[392,128]{1,0:T(8,128)} %copy-done) | copy-start | bytes 602116
  14.7 30.0 %all-to-all-start.1 = ((f32[4,384,128]{2,1,0:T(8,128)}), f32[4,384,128]{2,1,0:T(8,128)S(1)}, u32[]{:S(2)}, u32[]{:S(2)}) async-start(f32[4,384,128]{2,1,0:T(8,128)} %pack.1), calls=%async_computation.1 | async-start | bytes 1572864 | tf_op jit(solution)/shard_map/all_to_all | solution.py:666
  30.9 1.5 %collective-permute-start.3 = (f32[3,4,32,128]{3,2,1,0:T(8,128)S(1)}, f32[3,4,32,128]{3,2,1,0:T(8,128)S(1)}, u32[]{:S(2)}, u32[]{:S(2)}) collective-permute-start(f32[3,4,32,128]{3,2,1,0:T(8,128)S(1)} %get-tuple-element.47), channel_id=1, source_target_pairs={{0,1},{1,0},{2,3},{3,2},{4,5},{5,4},{6,7},{7,6},{8,9},{9,8},{10,11... | collective-permute-start | bytes 589832 | tf_op jit(solution)/shard_map/ppermute | solution.py:640
  32.4 7.0 %collective-permute-start.4 = (f32[3,4,32,128]{3,2,1,0:T(8,128)S(1)}, f32[3,4,32,128]{3,2,1,0:T(8,128)S(1)}, u32[]{:S(2)}, u32[]{:S(2)}) collective-permute-start(f32[3,4,32,128]{3,2,1,0:T(8,128)S(1)} %add.27.refs_4_), channel_id=1, source_target_pairs={{0,2},{1,3},{2,0},{3,1},{4,6},{5,7},{6,4},{7,5},{8,10},{9,11},{10,... | collective-permute-start | bytes 589832 | tf_op jit(solution)/shard_map/ppermute | solution.py:640
  39.5 3.3 %collective-permute-start.5 = (f32[3,4,32,128]{3,2,1,0:T(8,128)S(1)}, f32[3,4,32,128]{3,2,1,0:T(8,128)S(1)}, u32[]{:S(2)}, u32[]{:S(2)}) collective-permute-start(f32[3,4,32,128]{3,2,1,0:T(8,128)S(1)} %add.28.kept_ref), channel_id=1, source_target_pairs={{0,1},{1,0},{2,3},{3,2},{4,5},{5,4},{6,7},{7,6},{8,9},{9,8},{10,11... | collective-permute-start | bytes 589832 | tf_op jit(solution)/shard_map/ppermute | solution.py:640
  44.6 44.9 %all-to-all-start = ((f32[8,8,24,128]{3,2,1,0:T(8,128)}), f32[8,8,24,128]{3,2,1,0:T(8,128)S(1)}, u32[]{:S(2)}, u32[]{:S(2)}) async-start(f32[8,8,24,128]{3,2,1,0:T(8,128)} %bitcast.5), calls=%async_computation | async-start | bytes 1572864 | tf_op jit(solution)/shard_map/all_to_all | solution.py:696
  56.0 1.5 %collective-permute-start.6 = (f32[3,4,32,128]{3,2,1,0:T(8,128)S(1)}, f32[3,4,32,128]{3,2,1,0:T(8,128)S(1)}, u32[]{:S(2)}, u32[]{:S(2)}) collective-permute-start(f32[3,4,32,128]{3,2,1,0:T(8,128)S(1)} %get-tuple-element.51), channel_id=1, source_target_pairs={{0,1},{1,0},{2,3},{3,2},{4,5},{5,4},{6,7},{7,6},{8,9},{9,8},{10,11... | collective-permute-start | bytes 589832 | tf_op jit(solution)/shard_map/ppermute | solution.py:640
  57.5 7.1 %collective-permute-start.7 = (f32[3,4,32,128]{3,2,1,0:T(8,128)S(1)}, f32[3,4,32,128]{3,2,1,0:T(8,128)S(1)}, u32[]{:S(2)}, u32[]{:S(2)}) collective-permute-start(f32[3,4,32,128]{3,2,1,0:T(8,128)S(1)} %add.29), channel_id=1, source_target_pairs={{0,2},{1,3},{2,0},{3,1},{4,6},{5,7},{6,4},{7,5},{8,10},{9,11},{10,... | collective-permute-start | bytes 589832 | tf_op jit(solution)/shard_map/ppermute | solution.py:640
  64.6 3.1 %collective-permute-start.8 = (f32[3,4,32,128]{3,2,1,0:T(8,128)S(1)}, f32[3,4,32,128]{3,2,1,0:T(8,128)S(1)}, u32[]{:S(2)}, u32[]{:S(2)}) collective-permute-start(f32[3,4,32,128]{3,2,1,0:T(8,128)S(1)} %add.30.kept_ref), channel_id=1, source_target_pairs={{0,1},{1,0},{2,3},{3,2},{4,5},{5,4},{6,7},{7,6},{8,9},{9,8},{10,11... | collective-permute-start | bytes 589832 | tf_op jit(solution)/shard_map/ppermute | solution.py:640
  68.9 7.9 %collective-permute-start.9 = (f32[8,24,128]{2,1,0:T(8,128)S(1)}, f32[8,24,128]{2,1,0:T(8,128)S(1)}, u32[]{:S(2)}, u32[]{:S(2)}) collective-permute-start(f32[8,24,128]{2,1,0:T(8,128)S(1)} %bitcast.45), channel_id=1, source_target_pairs={{0,16},{1,5},{2,18},{3,7},{4,20},{5,1},{6,22},{7,3},{8,24},{9,13},... | collective-permute-start | bytes 294920 | tf_op jit(solution)/shard_map/ppermute | solution.py:634
  71.8 9.3 %collective-permute-start.10 = (f32[8,24,128]{2,1,0:T(8,128)S(1)}, f32[8,24,128]{2,1,0:T(8,128)S(1)}, u32[]{:S(2)}, u32[]{:S(2)}) collective-permute-start(f32[8,24,128]{2,1,0:T(8,128)S(1)} %bitcast.44), channel_id=1, source_target_pairs={{0,4},{1,17},{2,6},{3,19},{4,0},{5,21},{6,2},{7,23},{8,12},{9,25},... | collective-permute-start | bytes 294920 | tf_op jit(solution)/shard_map/ppermute | solution.py:634
  73.3 11.0 %collective-permute-start.11 = (f32[8,24,128]{2,1,0:T(8,128)S(1)}, f32[8,24,128]{2,1,0:T(8,128)S(1)}, u32[]{:S(2)}, u32[]{:S(2)}) collective-permute-start(f32[8,24,128]{2,1,0:T(8,128)S(1)} %bitcast.43), channel_id=1, source_target_pairs={{0,8},{1,25},{2,10},{3,27},{4,12},{5,29},{6,14},{7,31},{8,0},{9,17... | collective-permute-start | bytes 294920 | tf_op jit(solution)/shard_map/ppermute | solution.py:634
  74.7 9.5 %collective-permute-start.12 = (f32[8,24,128]{2,1,0:T(8,128)S(1)}, f32[8,24,128]{2,1,0:T(8,128)S(1)}, u32[]{:S(2)}, u32[]{:S(2)}) collective-permute-start(f32[8,24,128]{2,1,0:T(8,128)S(1)} %bitcast.42), channel_id=1, source_target_pairs={{0,24},{1,9},{2,26},{3,11},{4,28},{5,13},{6,30},{7,15},{8,16},{9,1... | collective-permute-start | bytes 294920 | tf_op jit(solution)/shard_map/ppermute | solution.py:634
  75.3 14.2 %collective-permute-start.13 = (f32[8,24,128]{2,1,0:T(8,128)S(1)}, f32[8,24,128]{2,1,0:T(8,128)S(1)}, u32[]{:S(2)}, u32[]{:S(2)}) collective-permute-start(f32[8,24,128]{2,1,0:T(8,128)S(1)} %bitcast.41), channel_id=1, source_target_pairs={{0,20},{1,13},{2,22},{3,15},{4,16},{5,9},{6,18},{7,11},{8,28},{9,5... | collective-permute-start | bytes 294920 | tf_op jit(solution)/shard_map/ppermute | solution.py:634
  76.8 12.7 %collective-permute-start.14 = (f32[8,24,128]{2,1,0:T(8,128)S(1)}, f32[8,24,128]{2,1,0:T(8,128)S(1)}, u32[]{:S(2)}, u32[]{:S(2)}) collective-permute-start(f32[8,24,128]{2,1,0:T(8,128)S(1)} %bitcast.40), channel_id=1, source_target_pairs={{0,12},{1,21},{2,14},{3,23},{4,8},{5,17},{6,10},{7,19},{8,4},{9,29... | collective-permute-start | bytes 294920 | tf_op jit(solution)/shard_map/ppermute | solution.py:634
  81.1 8.4 %collective-permute-start.15 = (f32[8,24,128]{2,1,0:T(8,128)S(1)}, f32[8,24,128]{2,1,0:T(8,128)S(1)}, u32[]{:S(2)}, u32[]{:S(2)}) collective-permute-start(f32[8,24,128]{2,1,0:T(8,128)S(1)} %bitcast.39), channel_id=1, source_target_pairs={{0,28},{1,29},{2,30},{3,31},{4,24},{5,25},{6,26},{7,27},{8,20},{9,... | collective-permute-start | bytes 294920 | tf_op jit(solution)/shard_map/ppermute | solution.py:634
  96.3 17.9 %collective-permute-start.16 = (f32[8,2,24,128]{3,2,1,0:T(8,128)S(1)}, f32[8,2,24,128]{3,2,1,0:T(8,128)S(1)}, u32[]{:S(2)}, u32[]{:S(2)}) collective-permute-start(f32[8,2,24,128]{3,2,1,0:T(8,128)S(1)} %get-tuple-element.61), channel_id=1, source_target_pairs={{0,16},{1,5},{2,18},{3,7},{4,20},{5,1},{6,22},{7,3},{8,24},{9,13},... | collective-permute-start | bytes 589832 | tf_op jit(solution)/shard_map/ppermute | solution.py:634
  100.8 13.5 %collective-permute-start.17 = (f32[8,2,24,128]{3,2,1,0:T(8,128)S(1)}, f32[8,2,24,128]{3,2,1,0:T(8,128)S(1)}, u32[]{:S(2)}, u32[]{:S(2)}) collective-permute-start(f32[8,2,24,128]{3,2,1,0:T(8,128)S(1)} %get-tuple-element.62), channel_id=1, source_target_pairs={{0,4},{1,17},{2,6},{3,19},{4,0},{5,21},{6,2},{7,23},{8,12},{9,25},... | collective-permute-start | bytes 589832 | tf_op jit(solution)/shard_map/ppermute | solution.py:634
  101.5 16.2 %collective-permute-start.18 = (f32[8,2,24,128]{3,2,1,0:T(8,128)S(1)}, f32[8,2,24,128]{3,2,1,0:T(8,128)S(1)}, u32[]{:S(2)}, u32[]{:S(2)}) collective-permute-start(f32[8,2,24,128]{3,2,1,0:T(8,128)S(1)} %get-tuple-element.63), channel_id=1, source_target_pairs={{0,8},{1,25},{2,10},{3,27},{4,12},{5,29},{6,14},{7,31},{8,0},{9,17... | collective-permute-start | bytes 589832 | tf_op jit(solution)/shard_map/ppermute | solution.py:634
  102.0 15.7 %collective-permute-start.19 = (f32[8,2,24,128]{3,2,1,0:T(8,128)S(1)}, f32[8,2,24,128]{3,2,1,0:T(8,128)S(1)}, u32[]{:S(2)}, u32[]{:S(2)}) collective-permute-start(f32[8,2,24,128]{3,2,1,0:T(8,128)S(1)} %get-tuple-element.64), channel_id=1, source_target_pairs={{0,24},{1,9},{2,26},{3,11},{4,28},{5,13},{6,30},{7,15},{8,16},{9,1... | collective-permute-start | bytes 589832 | tf_op jit(solution)/shard_map/ppermute | solution.py:634
  103.0 28.7 %collective-permute-start.20 = (f32[8,2,24,128]{3,2,1,0:T(8,128)S(1)}, f32[8,2,24,128]{3,2,1,0:T(8,128)S(1)}, u32[]{:S(2)}, u32[]{:S(2)}) collective-permute-start(f32[8,2,24,128]{3,2,1,0:T(8,128)S(1)} %get-tuple-element.65), channel_id=1, source_target_pairs={{0,20},{1,13},{2,22},{3,15},{4,16},{5,9},{6,18},{7,11},{8,28},{9,5... | collective-permute-start | bytes 589832 | tf_op jit(solution)/shard_map/ppermute | solution.py:634
  114.3 17.5 %collective-permute-start.21 = (f32[8,2,24,128]{3,2,1,0:T(8,128)S(1)}, f32[8,2,24,128]{3,2,1,0:T(8,128)S(1)}, u32[]{:S(2)}, u32[]{:S(2)}) collective-permute-start(f32[8,2,24,128]{3,2,1,0:T(8,128)S(1)} %get-tuple-element.66), channel_id=1, source_target_pairs={{0,12},{1,21},{2,14},{3,23},{4,8},{5,17},{6,10},{7,19},{8,4},{9,29... | collective-permute-start | bytes 589832 | tf_op jit(solution)/shard_map/ppermute | solution.py:634
  114.3 17.5 %collective-permute-start.22 = (f32[8,2,24,128]{3,2,1,0:T(8,128)S(1)}, f32[8,2,24,128]{3,2,1,0:T(8,128)S(1)}, u32[]{:S(2)}, u32[]{:S(2)}) collective-permute-start(f32[8,2,24,128]{3,2,1,0:T(8,128)S(1)} %get-tuple-element.67), channel_id=1, source_target_pairs={{0,28},{1,29},{2,30},{3,31},{4,24},{5,25},{6,26},{7,27},{8,20},{9,... | collective-permute-start | bytes 589832 | tf_op jit(solution)/shard_map/ppermute | solution.py:634

commit v11 on v10

--- a/solution.py
+++ b/solution.py
@@ -635,6 +635,22 @@
     return result
 
 
+def sum_kernel(first_ref, second_ref, _, out_ref):
+    out_ref[...] = first_ref[...] + second_ref[...]
+
+
+def ordered_sum(first, second, after):
+    return pl.pallas_call(
+        sum_kernel,
+        out_shape=jax.ShapeDtypeStruct(first.shape, jnp.float32),
+        in_specs=[VMEM, VMEM, pl.BlockSpec(memory_space=pl.ANY)],
+        out_specs=VMEM,
+        compiler_params=params(),
+        cost_estimate=cost(12 * first.size),
+        name="ordered_sum",
+    )(first, second, after)
+
+
 def swap(value, step):
     pairs = [(index, index ^ step) for index in range(lax.axis_size("real"))]
     return lax.ppermute(value, "real", pairs)
@@ -683,7 +699,7 @@
         kept = after = kept + swap(sent, 1)
         step = 2
         while step < realizations:
-            kept = kept + swap(kept, step)
+            kept = ordered_sum(kept, swap(kept, step), forcing)
             step *= 2
         blocks = outgoing(
             slotted, forcing, kept, swap(kept, 1), low_index, mode_counts, slot_modes, groups, band_modes,

time: 136 us -> 133 us (0.978)
  starting transfers between devices: 54.2 us -> 47.2 us
  waiting for transfers between devices: 47.8 us -> 52.4 us
    ppermute x17, waiting for transfers between devices: 34.2 us -> 41.9 us  [exchange(): result[position] = lax.ppermute(blocks[position], axes + ('real',), pairs)]
    ppermute x17, starting transfers between devices: 33.2 us -> 26.4 us  [exchange(): result[position] = lax.ppermute(blocks[position], axes + ('real',), pairs)]
    ppermute x6, waiting for transfers between devices: 13.6 us -> 10.4 us  [swap(): return lax.ppermute(value, 'real', pairs)]
  transfers between devices with their start and end apart: 25 -> 25, of which waited for: 10 -> 13; matrix products, arithmetic and copies ran while one was open for 1% -> 1% of each run, Pallas kernels for 14% -> 14%
where the time goes in v11:
time: 133 us; the launch traced here: 131 us
  waiting for transfers between devices  52.4 us (39%)
  starting transfers between devices  47.2 us (35%)
  Pallas kernels  29.9 us (22%)
  local copies, waits for them, and re-layouts  1.56 us (1%)
    ppermute x17, waiting for transfers between devices, exchange(): result[position] = lax.ppermute(blocks[position], axes + ('real',), pairs)  41.9 us
    ppermute x17, starting transfers between devices, exchange(): result[position] = lax.ppermute(blocks[position], axes + ('real',), pairs)  26.4 us
    ppermute x6, waiting for transfers between devices, swap(): return lax.ppermute(value, 'real', pairs)  10.4 us
    all_to_all x1, starting transfers between devices, local(): block = lax.all_to_all(block, 'kx', split_axis=0, concat_axis=0, tiled=True)  9.53 us
    all_to_all x1, starting transfers between devices, local(): lax.all_to_all(block, ('kx', 'ht'), split_axis=0, concat_axis=0, tiled=True)  7.83 us
    pallas_call x2, Pallas kernels, stress_terms(): pl.pallas_call(stress_kernel, out_shape=(jax.ShapeDtypeStruct(shape, jnp....  6.93 us
    pallas_call x1, Pallas kernels, solve(): pl.pallas_call(functools.partial(solve_kernel, groups=groups, kx_count=kx...  6.85 us
    pallas_call x2, Pallas kernels, high_terms(): pl.pallas_call(products_kernel, out_shape=jax.ShapeDtypeStruct((component...  6 us
  transfers between devices with their start and end apart: 25, of which 13 were waited for; matrix products, arithmetic and copies ran while one was open for 1% of the time, Pallas kernels for 14%

profile of v11, /device:TPU:0, one launch (start us, length us, event | category | flops | bytes accessed | tf_op | source)
XLA Modules:
  0.0 131.3 jit_solution(10882257727859381997)
XLA Ops:
  0.0 2.1 %pack_first.1 = (f32[392,128]{1,0:T(8,128)}, f32[392,128]{1,0:T(8,128)}, f32[392,128]{1,0:T(8,128)}, f32[392,128]{1,0:T(8,128)}) custom-call(s32[4,8]{1,0:T(4,128)} %near_ref.1, s32[4]{0:T(128)} %count_ref.1, f32[12,2,4,32,128]{4,3,2,1,0:T(8,128)} %bitcast.46), custom_call_target="tpu_custom_call" | custom-call | bytes 1572864 | tf_op jit(solution)/shard_map/pack_first/pallas_call | solution.py:175
  2.1 3.0 %collective-permute-start = (f32[392,128]{1,0:T(8,128)}, f32[392,128]{1,0:T(8,128)S(1)}, u32[]{:S(2)}, u32[]{:S(2)}) collective-permute-start(f32[392,128]{1,0:T(8,128)} %get-tuple-element.38), channel_id=1, source_target_pairs={{0,8},{1,25},{2,10},{3,27},{8,0},{9,17},{10,2},{11,19},{16,24},{17... | collective-permute-start | bytes 602120 | tf_op jit(solution)/shard_map/ppermute | solution.py:634
  5.1 2.5 %collective-permute-start.1 = (f32[392,128]{1,0:T(8,128)}, f32[392,128]{1,0:T(8,128)S(1)}, u32[]{:S(2)}, u32[]{:S(2)}) collective-permute-start(f32[392,128]{1,0:T(8,128)} %get-tuple-element.39), channel_id=1, source_target_pairs={{0,24},{1,9},{2,26},{3,11},{8,16},{9,1},{10,18},{11,3},{16,8},{17,... | collective-permute-start | bytes 602120 | tf_op jit(solution)/shard_map/ppermute | solution.py:634
  7.6 0.1 collective-permute-start.2
  7.7 0.0 copy-start.5
  7.7 4.2 %collective-permute-done.refs_1_._ = f32[392,128]{1,0:T(8,128)S(1)} collective-permute-done((f32[392,128]{1,0:T(8,128)}, f32[392,128]{1,0:T(8,128)S(1)}, u32[]{:S(2)}, u32[]{:S(2)}) %collective-permute-start) | collective-permute-done | bytes 200736 | tf_op jit(solution)/shard_map/ppermute | solution.py:634
  11.9 0.7 copy-done
  12.6 2.1 %pack.1 = f32[4,384,128]{2,1,0:T(8,128)} custom-call(f32[12,2,4,32,128]{4,3,2,1,0:T(8,128)} %bitcast.47, f32[392,128]{1,0:T(8,128)} %copy-done), custom_call_target="tpu_custom_call" | custom-call | bytes 1572864 | tf_op jit(solution)/shard_map/pack/pallas_call | solution.py:201
  14.7 9.5 %all-to-all-start.1 = ((f32[4,384,128]{2,1,0:T(8,128)}), f32[4,384,128]{2,1,0:T(8,128)S(1)}, u32[]{:S(2)}, u32[]{:S(2)}) async-start(f32[4,384,128]{2,1,0:T(8,128)} %pack.1), calls=%async_computation.1 | async-start | bytes 1572864 | tf_op jit(solution)/shard_map/all_to_all | solution.py:682
  24.2 0.1 broadcast_in_dim.85
  24.3 0.1 broadcast_in_dim.86
  24.4 0.1 broadcast_in_dim.91
  24.5 0.1 broadcast_in_dim.92
  24.6 0.1 broadcast_in_dim.96
  24.6 0.1 broadcast_in_dim.97
  24.7 0.1 broadcast_in_dim.101
  24.8 0.1 broadcast_in_dim.102
  24.9 0.8 tables.1
  25.7 0.0 collective-permute-done.1.refs_2_
  25.7 1.6 %collective-permute-done.2.refs_3_ = f32[392,128]{1,0:T(8,128)S(1)} collective-permute-done((f32[392,128]{1,0:T(8,128)}, f32[392,128]{1,0:T(8,128)S(1)}, u32[]{:S(2)}, u32[]{:S(2)}) %collective-permute-start.2) | collective-permute-done | bytes 200736 | tf_op jit(solution)/shard_map/ppermute | solution.py:634
  27.3 0.1 add_convert_fusion
  27.4 3.5 %stress.2 = (f32[3,16,32,128]{3,2,1,0:T(8,128)S(1)}, f32[3,16,32,256]{3,2,1,0:T(8,128)S(1)}, f32[3,4,32,128]{3,2,1,0:T(8,128)S(1)}, f32[3,4,32,128]{3,2,1,0:T(8,128)S(1)}) custom-call(s32[8]{0:T(128)S(1)} %copy-done.5, s32[16,8]{1,0:T(8,128)S(1)} %bitcast.26, f32[392,128]{1,0:T(8,128)S(1)} %copy-done.3, f32[392,128]{1,0:T(8,128)S(1)} %copy-done.1, ...), custom_call_target="tpu_custom_call" | custom-call | bytes 12582912 | tf_op jit(solution)/shard_map/stress/pallas_call | solution.py:353
  30.9 0.1 collective-permute-start.3
  31.0 1.4 %collective-permute-done.3 = f32[3,4,32,128]{3,2,1,0:T(8,128)S(1)} collective-permute-done((f32[3,4,32,128]{3,2,1,0:T(8,128)S(1)}, f32[3,4,32,128]{3,2,1,0:T(8,128)S(1)}, u32[]{:S(2)}, u32[]{:S(2)}) %collective-permute-start.3) | collective-permute-done | bytes 196640 | tf_op jit(solution)/shard_map/ppermute | solution.py:656
  32.4 1.6 %collective-permute-start.4 = (f32[3,4,32,128]{3,2,1,0:T(8,128)S(1)}, f32[3,4,32,128]{3,2,1,0:T(8,128)S(1)}, u32[]{:S(2)}, u32[]{:S(2)}) collective-permute-start(f32[3,4,32,128]{3,2,1,0:T(8,128)S(1)} %add.21.first_ref.refs_4_), channel_id=1, source_target_pairs={{0,2},{1,3},{2,0},{3,1},{4,6},{5,7},{6,4},{7,5},{8,10},{9,11},{10,... | collective-permute-start | bytes 589832 | tf_op jit(solution)/shard_map/ppermute | solution.py:656
  34.0 0.2 slice_reduce_fusion.count_ref
  34.2 3.0 %products.2._.forcing_ref = f32[3,8,32,128]{3,2,1,0:T(8,128)S(1)} custom-call(s32[8]{0:T(128)S(1)} %copy-done.5, s32[16,8]{1,0:T(8,128)S(1)} %bitcast.27, s32[16]{0:T(128)S(1)} %slice_reduce_fusion.count_ref, f32[3,16,32,256]{3,2,1,0:T(8,128)S(1)} %get-tuple-element.45.physical, bf16[256,256]{1,0:T(8,128)(2,1)S(1)} %get-tuple-element.42.refs_6_.back_ref.refs_3_, ...), custom_call_target="tpu_custom_call" | custom-call | bytes 12582912 | tf_op jit(solution)/shard_map/products/pallas_call | solution.py:418
  37.2 2.3 %collective-permute-done.4.second_ref = f32[3,4,32,128]{3,2,1,0:T(8,128)S(1)} collective-permute-done((f32[3,4,32,128]{3,2,1,0:T(8,128)S(1)}, f32[3,4,32,128]{3,2,1,0:T(8,128)S(1)}, u32[]{:S(2)}, u32[]{:S(2)}) %collective-permute-start.4) | collective-permute-done | bytes 196640 | tf_op jit(solution)/shard_map/ppermute | solution.py:656
  39.5 0.1 collective-permute-start.5
  39.5 1.4 %collective-permute-done.5.other_ref = f32[3,4,32,128]{3,2,1,0:T(8,128)S(1)} collective-permute-done((f32[3,4,32,128]{3,2,1,0:T(8,128)S(1)}, f32[3,4,32,128]{3,2,1,0:T(8,128)S(1)}, u32[]{:S(2)}, u32[]{:S(2)}) %collective-permute-start.5) | collective-permute-done | bytes 196640 | tf_op jit(solution)/shard_map/ppermute | solution.py:656
  41.0 1.9 %outgoing.2 = f32[1536,128]{1,0:T(8,128)} custom-call(s32[8]{0:T(128)S(1)} %copy-done.5, s32[16]{0:T(128)S(1)} %slice_reduce_fusion.count_ref, f32[3,16,32,128]{3,2,1,0:T(8,128)S(1)} %get-tuple-element.44.slotted_ref, f32[3,8,32,128]{3,2,1,0:T(8,128)S(1)} %products.2._.forcing_ref, f32[3,4,32,128]{3,2,1,0:T(8,128)S(1)} %ordered_sum.2.kept_ref, ...), custom_call_target="tpu_custom_call" | custom-call | bytes 1572864 | tf_op jit(solution)/shard_map/outgoing/pallas_call | solution.py:484
  42.9 7.8 %all-to-all-start = ((f32[8,8,24,128]{3,2,1,0:T(8,128)}), f32[8,8,24,128]{3,2,1,0:T(8,128)S(1)}, u32[]{:S(2)}, u32[]{:S(2)}) async-start(f32[8,8,24,128]{3,2,1,0:T(8,128)} %bitcast.5), calls=%async_computation | async-start | bytes 1572864 | tf_op jit(solution)/shard_map/all_to_all | solution.py:712
  50.7 3.5 %stress.3 = (f32[3,16,32,128]{3,2,1,0:T(8,128)S(1)}, f32[3,16,32,256]{3,2,1,0:T(8,128)S(1)}, f32[3,4,32,128]{3,2,1,0:T(8,128)S(1)}, f32[3,4,32,128]{3,2,1,0:T(8,128)S(1)}) custom-call(s32[8]{0:T(128)S(1)} %copy-done.5, s32[16,8]{1,0:T(8,128)S(1)} %bitcast.28, f32[4,384,128]{2,1,0:T(8,128)S(1)} %all-to-all-done.1.refs_0_, ...), custom_call_target="tpu_custom_call" | custom-call | bytes 12582912 | tf_op jit(solution)/shard_map/stress/pallas_call | solution.py:353
  54.2 0.1 collective-permute-start.6
  54.2 1.4 %collective-permute-done.6 = f32[3,4,32,128]{3,2,1,0:T(8,128)S(1)} collective-permute-done((f32[3,4,32,128]{3,2,1,0:T(8,128)S(1)}, f32[3,4,32,128]{3,2,1,0:T(8,128)S(1)}, u32[]{:S(2)}, u32[]{:S(2)}) %collective-permute-start.6) | collective-permute-done | bytes 196640 | tf_op jit(solution)/shard_map/ppermute | solution.py:656
  55.7 1.6 %collective-permute-start.7 = (f32[3,4,32,128]{3,2,1,0:T(8,128)S(1)}, f32[3,4,32,128]{3,2,1,0:T(8,128)S(1)}, u32[]{:S(2)}, u32[]{:S(2)}) collective-permute-start(f32[3,4,32,128]{3,2,1,0:T(8,128)S(1)} %add.22.first_ref), channel_id=1, source_target_pairs={{0,2},{1,3},{2,0},{3,1},{4,6},{5,7},{6,4},{7,5},{8,10},{9,11},{10,... | collective-permute-start | bytes 589832 | tf_op jit(solution)/shard_map/ppermute | solution.py:656
  57.3 3.0 %products.3._.forcing_ref = f32[3,8,32,128]{3,2,1,0:T(8,128)S(1)} custom-call(s32[8]{0:T(128)S(1)} %copy-done.5, s32[16,8]{1,0:T(8,128)S(1)} %bitcast.29, s32[16]{0:T(128)S(1)} %slice_reduce_fusion.count_ref, f32[3,16,32,256]{3,2,1,0:T(8,128)S(1)} %get-tuple-element.49.physical, bf16[256,256]{1,0:T(8,128)(2,1)S(1)} %get-tuple-element.42.refs_6_.back_ref.refs_3_, ...), custom_call_target="tpu_custom_call" | custom-call | bytes 12582912 | tf_op jit(solution)/shard_map/products/pallas_call | solution.py:418
  60.3 2.5 %collective-permute-done.7.second_ref = f32[3,4,32,128]{3,2,1,0:T(8,128)S(1)} collective-permute-done((f32[3,4,32,128]{3,2,1,0:T(8,128)S(1)}, f32[3,4,32,128]{3,2,1,0:T(8,128)S(1)}, u32[]{:S(2)}, u32[]{:S(2)}) %collective-permute-start.7) | collective-permute-done | bytes 196640 | tf_op jit(solution)/shard_map/ppermute | solution.py:656
  62.7 0.1 collective-permute-start.8
  62.8 1.4 %collective-permute-done.8.other_ref = f32[3,4,32,128]{3,2,1,0:T(8,128)S(1)} collective-permute-done((f32[3,4,32,128]{3,2,1,0:T(8,128)S(1)}, f32[3,4,32,128]{3,2,1,0:T(8,128)S(1)}, u32[]{:S(2)}, u32[]{:S(2)}) %collective-permute-start.8) | collective-permute-done | bytes 196640 | tf_op jit(solution)/shard_map/ppermute | solution.py:656
  64.3 1.2 outgoing.3
  65.4 3.0 %collective-permute-start.9 = (f32[8,24,128]{2,1,0:T(8,128)S(1)}, f32[8,24,128]{2,1,0:T(8,128)S(1)}, u32[]{:S(2)}, u32[]{:S(2)}) collective-permute-start(f32[8,24,128]{2,1,0:T(8,128)S(1)} %bitcast.45), channel_id=1, source_target_pairs={{0,16},{1,5},{2,18},{3,7},{4,20},{5,1},{6,22},{7,3},{8,24},{9,13},... | collective-permute-start | bytes 294920 | tf_op jit(solution)/shard_map/ppermute | solution.py:634
  68.4 1.5 %collective-permute-start.10 = (f32[8,24,128]{2,1,0:T(8,128)S(1)}, f32[8,24,128]{2,1,0:T(8,128)S(1)}, u32[]{:S(2)}, u32[]{:S(2)}) collective-permute-start(f32[8,24,128]{2,1,0:T(8,128)S(1)} %bitcast.44), channel_id=1, source_target_pairs={{0,4},{1,17},{2,6},{3,19},{4,0},{5,21},{6,2},{7,23},{8,12},{9,25},... | collective-permute-start | bytes 294920 | tf_op jit(solution)/shard_map/ppermute | solution.py:634
  69.9 1.5 %collective-permute-start.11 = (f32[8,24,128]{2,1,0:T(8,128)S(1)}, f32[8,24,128]{2,1,0:T(8,128)S(1)}, u32[]{:S(2)}, u32[]{:S(2)}) collective-permute-start(f32[8,24,128]{2,1,0:T(8,128)S(1)} %bitcast.43), channel_id=1, source_target_pairs={{0,8},{1,25},{2,10},{3,27},{4,12},{5,29},{6,14},{7,31},{8,0},{9,17... | collective-permute-start | bytes 294920 | tf_op jit(solution)/shard_map/ppermute | solution.py:634
  71.4 0.6 collective-permute-start.12
  71.9 1.5 %collective-permute-start.13 = (f32[8,24,128]{2,1,0:T(8,128)S(1)}, f32[8,24,128]{2,1,0:T(8,128)S(1)}, u32[]{:S(2)}, u32[]{:S(2)}) collective-permute-start(f32[8,24,128]{2,1,0:T(8,128)S(1)} %bitcast.41), channel_id=1, source_target_pairs={{0,20},{1,13},{2,22},{3,15},{4,16},{5,9},{6,18},{7,11},{8,28},{9,5... | collective-permute-start | bytes 294920 | tf_op jit(solution)/shard_map/ppermute | solution.py:634
  73.4 3.3 %collective-permute-done.9.refs_2_ = f32[8,24,128]{2,1,0:T(8,128)S(1)} collective-permute-done((f32[8,24,128]{2,1,0:T(8,128)S(1)}, f32[8,24,128]{2,1,0:T(8,128)S(1)}, u32[]{:S(2)}, u32[]{:S(2)}) %collective-permute-start.9) | collective-permute-done | bytes 98336 | tf_op jit(solution)/shard_map/ppermute | solution.py:634
  76.7 0.4 collective-permute-start.14
  77.1 0.0 collective-permute-done.10.refs_3_
  77.1 3.2 %collective-permute-start.15 = (f32[8,24,128]{2,1,0:T(8,128)S(1)}, f32[8,24,128]{2,1,0:T(8,128)S(1)}, u32[]{:S(2)}, u32[]{:S(2)}) collective-permute-start(f32[8,24,128]{2,1,0:T(8,128)S(1)} %bitcast.39), channel_id=1, source_target_pairs={{0,28},{1,29},{2,30},{3,31},{4,24},{5,25},{6,26},{7,27},{8,20},{9,... | collective-permute-start | bytes 294920 | tf_op jit(solution)/shard_map/ppermute | solution.py:634
  80.3 0.0 collective-permute-done.11.refs_4_
  80.3 0.0 collective-permute-done.12.refs_5_
  80.3 7.5 %collective-permute-done.13.refs_6_ = f32[8,24,128]{2,1,0:T(8,128)S(1)} collective-permute-done((f32[8,24,128]{2,1,0:T(8,128)S(1)}, f32[8,24,128]{2,1,0:T(8,128)S(1)}, u32[]{:S(2)}, u32[]{:S(2)}) %collective-permute-start.13) | collective-permute-done | bytes 98336 | tf_op jit(solution)/shard_map/ppermute | solution.py:634
  87.8 0.0 collective-permute-done.14.refs_7_
  87.8 6.8 %solve.1 = (f32[8,2,24,128]{3,2,1,0:T(8,128)S(1)}, f32[8,2,24,128]{3,2,1,0:T(8,128)S(1)}, f32[8,2,24,128]{3,2,1,0:T(8,128)S(1)}, f32[8,2,24,128]{3,2,1,0:T(8,128...) custom-call(f32[8,8,24,128]{3,2,1,0:T(8,128)S(1)} %all-to-all-done.r, ...), custom_call_target="tpu_custom_call" | custom-call | bytes 8388608 | tf_op jit(solution)/shard_map/solve/pallas_call | solution.py:568
  94.7 2.4 %collective-permute-start.16 = (f32[8,2,24,128]{3,2,1,0:T(8,128)S(1)}, f32[8,2,24,128]{3,2,1,0:T(8,128)S(1)}, u32[]{:S(2)}, u32[]{:S(2)}) collective-permute-start(f32[8,2,24,128]{3,2,1,0:T(8,128)S(1)} %get-tuple-element.61), channel_id=1, source_target_pairs={{0,16},{1,5},{2,18},{3,7},{4,20},{5,1},{6,22},{7,3},{8,24},{9,13},... | collective-permute-start | bytes 589832 | tf_op jit(solution)/shard_map/ppermute | solution.py:634
  97.1 1.0 collective-permute-start.17
  98.1 2.7 %collective-permute-start.19 = (f32[8,2,24,128]{3,2,1,0:T(8,128)S(1)}, f32[8,2,24,128]{3,2,1,0:T(8,128)S(1)}, u32[]{:S(2)}, u32[]{:S(2)}) collective-permute-start(f32[8,2,24,128]{3,2,1,0:T(8,128)S(1)} %get-tuple-element.64), channel_id=1, source_target_pairs={{0,24},{1,9},{2,26},{3,11},{4,28},{5,13},{6,30},{7,15},{8,16},{9,1... | collective-permute-start | bytes 589832 | tf_op jit(solution)/shard_map/ppermute | solution.py:634
  100.8 1.3 collective-permute-start.20
  102.0 8.6 %collective-permute-done.16 = f32[8,2,24,128]{3,2,1,0:T(8,128)S(1)} collective-permute-done((f32[8,2,24,128]{3,2,1,0:T(8,128)S(1)}, f32[8,2,24,128]{3,2,1,0:T(8,128)S(1)}, u32[]{:S(2)}, u32[]{:S(2)}) %collective-permute-start.16) | collective-permute-done | bytes 196640 | tf_op jit(solution)/shard_map/ppermute | solution.py:634
  110.6 1.9 %collective-permute-start.22 = (f32[8,2,24,128]{3,2,1,0:T(8,128)S(1)}, f32[8,2,24,128]{3,2,1,0:T(8,128)S(1)}, u32[]{:S(2)}, u32[]{:S(2)}) collective-permute-start(f32[8,2,24,128]{3,2,1,0:T(8,128)S(1)} %get-tuple-element.67), channel_id=1, source_target_pairs={{0,28},{1,29},{2,30},{3,31},{4,24},{5,25},{6,26},{7,27},{8,20},{9,... | collective-permute-start | bytes 589832 | tf_op jit(solution)/shard_map/ppermute | solution.py:634
  112.5 1.7 %collective-permute-done.18 = f32[8,2,24,128]{3,2,1,0:T(8,128)S(1)} collective-permute-done((f32[8,2,24,128]{3,2,1,0:T(8,128)S(1)}, f32[8,2,24,128]{3,2,1,0:T(8,128)S(1)}, u32[]{:S(2)}, u32[]{:S(2)}) %collective-permute-start.18) | collective-permute-done | bytes 196640 | tf_op jit(solution)/shard_map/ppermute | solution.py:634
  114.2 15.0 %collective-permute-done.20 = f32[8,2,24,128]{3,2,1,0:T(8,128)S(1)} collective-permute-done((f32[8,2,24,128]{3,2,1,0:T(8,128)S(1)}, f32[8,2,24,128]{3,2,1,0:T(8,128)S(1)}, u32[]{:S(2)}, u32[]{:S(2)}) %collective-permute-start.20) | collective-permute-done | bytes 196640 | tf_op jit(solution)/shard_map/ppermute | solution.py:634
  129.3 2.1 %restore.1 = f32[3,4,256,128]{3,2,1,0:T(8,128)} custom-call(f32[384,128]{1,0:T(8,128)S(1)} %bitcast.30, f32[384,128]{1,0:T(8,128)S(1)} %bitcast.31, f32[384,128]{1,0:T(8,128)S(1)} %bitcast.32, f32[384,128]{1,0:T(8,128)S(1)} %bitcast.33, f32[384,128]{1,0:T(8,128)S(1)} %bitcast.34, f32[384,128]{1,0:T(8,128)S(1)} %bitcast.35, f32[384,128]{1,0:T(8,128)S(1)} %bitcast.36, ...), custom_call_target="tpu_custom_call" | custom-call | bytes 3145728 | tf_op jit(solution)/shard_map/restore/pallas_call | solution.py:612
  (37 shorter events, 0.2 us)
Async XLA Ops:
  2.1 9.8 %collective-permute-start = (f32[392,128]{1,0:T(8,128)}, f32[392,128]{1,0:T(8,128)S(1)}, u32[]{:S(2)}, u32[]{:S(2)}) collective-permute-start(f32[392,128]{1,0:T(8,128)} %get-tuple-element.38), channel_id=1, source_target_pairs={{0,8},{1,25},{2,10},{3,27},{8,0},{9,17},{10,2},{11,19},{16,24},{17... | collective-permute-start | bytes 602120 | tf_op jit(solution)/shard_map/ppermute | solution.py:634
  5.1 20.6 %collective-permute-start.1 = (f32[392,128]{1,0:T(8,128)}, f32[392,128]{1,0:T(8,128)S(1)}, u32[]{:S(2)}, u32[]{:S(2)}) collective-permute-start(f32[392,128]{1,0:T(8,128)} %get-tuple-element.39), channel_id=1, source_target_pairs={{0,24},{1,9},{2,26},{3,11},{8,16},{9,1},{10,18},{11,3},{16,8},{17,... | collective-permute-start | bytes 602120 | tf_op jit(solution)/shard_map/ppermute | solution.py:634
  7.6 19.7 %collective-permute-start.2 = (f32[392,128]{1,0:T(8,128)}, f32[392,128]{1,0:T(8,128)S(1)}, u32[]{:S(2)}, u32[]{:S(2)}) collective-permute-start(f32[392,128]{1,0:T(8,128)} %get-tuple-element.40), channel_id=1, source_target_pairs={{0,16},{1,17},{2,18},{3,19},{8,24},{9,25},{10,26},{11,27},{16,0},{... | collective-permute-start | bytes 602120 | tf_op jit(solution)/shard_map/ppermute | solution.py:634
  7.7 17.2 %copy-start.3 = (f32[392,128]{1,0:T(8,128)S(1)}, f32[392,128]{1,0:T(8,128)}, u32[]{:S(2)}) copy-start(f32[392,128]{1,0:T(8,128)} %get-tuple-element.37.refs_0_) | copy-start | bytes 602116
  7.7 17.2 %copy-start.2 = (bf16[128,256]{1,0:T(8,128)(2,1)S(1)}, bf16[128,256]{1,0:T(8,128)(2,1)}, u32[]{:S(2)}) copy-start(bf16[128,256]{1,0:T(8,128)(2,1)} %constant.22.clone.rest_ref.refs_5_.refs_2_) | copy-start | bytes 196612
  7.7 17.2 %copy-start.4 = (bf16[128,256]{1,0:T(8,128)(2,1)S(1)}, bf16[128,256]{1,0:T(8,128)(2,1)}, u32[]{:S(2)}) copy-start(bf16[128,256]{1,0:T(8,128)(2,1)} %constant.21.clone.top_ref) | copy-start | bytes 196612
  7.7 17.2 %copy-start.6 = (s32[64]{0:T(128)S(1)}, s32[64]{0:T(128)}, u32[]{:S(2)}) copy-start(s32[64]{0:T(128)} %owner_ref.1) | copy-start | bytes 772
  7.7 19.7 %copy-start.5 = (s32[8]{0:T(128)S(1)}, s32[8]{0:T(128)}, u32[]{:S(2)}) copy-start(s32[8]{0:T(128)} %low_ref.11) | copy-start | bytes 100
  11.9 0.7 copy-start
  14.7 11.0 %copy-start.1 = (f32[392,128]{1,0:T(8,128)S(1)}, f32[392,128]{1,0:T(8,128)}, u32[]{:S(2)}) copy-start(f32[392,128]{1,0:T(8,128)} %copy-done) | copy-start | bytes 602116
  14.7 28.2 %all-to-all-start.1 = ((f32[4,384,128]{2,1,0:T(8,128)}), f32[4,384,128]{2,1,0:T(8,128)S(1)}, u32[]{:S(2)}, u32[]{:S(2)}) async-start(f32[4,384,128]{2,1,0:T(8,128)} %pack.1), calls=%async_computation.1 | async-start | bytes 1572864 | tf_op jit(solution)/shard_map/all_to_all | solution.py:682
  30.9 1.5 %collective-permute-start.3 = (f32[3,4,32,128]{3,2,1,0:T(8,128)S(1)}, f32[3,4,32,128]{3,2,1,0:T(8,128)S(1)}, u32[]{:S(2)}, u32[]{:S(2)}) collective-permute-start(f32[3,4,32,128]{3,2,1,0:T(8,128)S(1)} %get-tuple-element.47), channel_id=1, source_target_pairs={{0,1},{1,0},{2,3},{3,2},{4,5},{5,4},{6,7},{7,6},{8,9},{9,8},{10,11... | collective-permute-start | bytes 589832 | tf_op jit(solution)/shard_map/ppermute | solution.py:656
  32.4 7.0 %collective-permute-start.4 = (f32[3,4,32,128]{3,2,1,0:T(8,128)S(1)}, f32[3,4,32,128]{3,2,1,0:T(8,128)S(1)}, u32[]{:S(2)}, u32[]{:S(2)}) collective-permute-start(f32[3,4,32,128]{3,2,1,0:T(8,128)S(1)} %add.21.first_ref.refs_4_), channel_id=1, source_target_pairs={{0,2},{1,3},{2,0},{3,1},{4,6},{5,7},{6,4},{7,5},{8,10},{9,11},{10,... | collective-permute-start | bytes 589832 | tf_op jit(solution)/shard_map/ppermute | solution.py:656
  39.5 1.5 %collective-permute-start.5 = (f32[3,4,32,128]{3,2,1,0:T(8,128)S(1)}, f32[3,4,32,128]{3,2,1,0:T(8,128)S(1)}, u32[]{:S(2)}, u32[]{:S(2)}) collective-permute-start(f32[3,4,32,128]{3,2,1,0:T(8,128)S(1)} %ordered_sum.2.kept_ref), channel_id=1, source_target_pairs={{0,1},{1,0},{2,3},{3,2},{4,5},{5,4},{6,7},{7,6},{8,9},{9,8},{10,11... | collective-permute-start | bytes 589832 | tf_op jit(solution)/shard_map/ppermute | solution.py:656
  42.9 45.0 %all-to-all-start = ((f32[8,8,24,128]{3,2,1,0:T(8,128)}), f32[8,8,24,128]{3,2,1,0:T(8,128)S(1)}, u32[]{:S(2)}, u32[]{:S(2)}) async-start(f32[8,8,24,128]{3,2,1,0:T(8,128)} %bitcast.5), calls=%async_computation | async-start | bytes 1572864 | tf_op jit(solution)/shard_map/all_to_all | solution.py:712
  54.2 1.5 %collective-permute-start.6 = (f32[3,4,32,128]{3,2,1,0:T(8,128)S(1)}, f32[3,4,32,128]{3,2,1,0:T(8,128)S(1)}, u32[]{:S(2)}, u32[]{:S(2)}) collective-permute-start(f32[3,4,32,128]{3,2,1,0:T(8,128)S(1)} %get-tuple-element.51), channel_id=1, source_target_pairs={{0,1},{1,0},{2,3},{3,2},{4,5},{5,4},{6,7},{7,6},{8,9},{9,8},{10,11... | collective-permute-start | bytes 589832 | tf_op jit(solution)/shard_map/ppermute | solution.py:656
  55.7 7.0 %collective-permute-start.7 = (f32[3,4,32,128]{3,2,1,0:T(8,128)S(1)}, f32[3,4,32,128]{3,2,1,0:T(8,128)S(1)}, u32[]{:S(2)}, u32[]{:S(2)}) collective-permute-start(f32[3,4,32,128]{3,2,1,0:T(8,128)S(1)} %add.22.first_ref), channel_id=1, source_target_pairs={{0,2},{1,3},{2,0},{3,1},{4,6},{5,7},{6,4},{7,5},{8,10},{9,11},{10,... | collective-permute-start | bytes 589832 | tf_op jit(solution)/shard_map/ppermute | solution.py:656
  62.7 1.5 %collective-permute-start.8 = (f32[3,4,32,128]{3,2,1,0:T(8,128)S(1)}, f32[3,4,32,128]{3,2,1,0:T(8,128)S(1)}, u32[]{:S(2)}, u32[]{:S(2)}) collective-permute-start(f32[3,4,32,128]{3,2,1,0:T(8,128)S(1)} %ordered_sum.3.kept_ref), channel_id=1, source_target_pairs={{0,1},{1,0},{2,3},{3,2},{4,5},{5,4},{6,7},{7,6},{8,9},{9,8},{10,11... | collective-permute-start | bytes 589832 | tf_op jit(solution)/shard_map/ppermute | solution.py:656
  65.4 11.2 %collective-permute-start.9 = (f32[8,24,128]{2,1,0:T(8,128)S(1)}, f32[8,24,128]{2,1,0:T(8,128)S(1)}, u32[]{:S(2)}, u32[]{:S(2)}) collective-permute-start(f32[8,24,128]{2,1,0:T(8,128)S(1)} %bitcast.45), channel_id=1, source_target_pairs={{0,16},{1,5},{2,18},{3,7},{4,20},{5,1},{6,22},{7,3},{8,24},{9,13},... | collective-permute-start | bytes 294920 | tf_op jit(solution)/shard_map/ppermute | solution.py:634
  68.4 8.7 %collective-permute-start.10 = (f32[8,24,128]{2,1,0:T(8,128)S(1)}, f32[8,24,128]{2,1,0:T(8,128)S(1)}, u32[]{:S(2)}, u32[]{:S(2)}) collective-permute-start(f32[8,24,128]{2,1,0:T(8,128)S(1)} %bitcast.44), channel_id=1, source_target_pairs={{0,4},{1,17},{2,6},{3,19},{4,0},{5,21},{6,2},{7,23},{8,12},{9,25},... | collective-permute-start | bytes 294920 | tf_op jit(solution)/shard_map/ppermute | solution.py:634
  69.9 10.4 %collective-permute-start.11 = (f32[8,24,128]{2,1,0:T(8,128)S(1)}, f32[8,24,128]{2,1,0:T(8,128)S(1)}, u32[]{:S(2)}, u32[]{:S(2)}) collective-permute-start(f32[8,24,128]{2,1,0:T(8,128)S(1)} %bitcast.43), channel_id=1, source_target_pairs={{0,8},{1,25},{2,10},{3,27},{4,12},{5,29},{6,14},{7,31},{8,0},{9,17... | collective-permute-start | bytes 294920 | tf_op jit(solution)/shard_map/ppermute | solution.py:634
  71.4 8.9 %collective-permute-start.12 = (f32[8,24,128]{2,1,0:T(8,128)S(1)}, f32[8,24,128]{2,1,0:T(8,128)S(1)}, u32[]{:S(2)}, u32[]{:S(2)}) collective-permute-start(f32[8,24,128]{2,1,0:T(8,128)S(1)} %bitcast.42), channel_id=1, source_target_pairs={{0,24},{1,9},{2,26},{3,11},{4,28},{5,13},{6,30},{7,15},{8,16},{9,1... | collective-permute-start | bytes 294920 | tf_op jit(solution)/shard_map/ppermute | solution.py:634
  71.9 15.9 %collective-permute-start.13 = (f32[8,24,128]{2,1,0:T(8,128)S(1)}, f32[8,24,128]{2,1,0:T(8,128)S(1)}, u32[]{:S(2)}, u32[]{:S(2)}) collective-permute-start(f32[8,24,128]{2,1,0:T(8,128)S(1)} %bitcast.41), channel_id=1, source_target_pairs={{0,20},{1,13},{2,22},{3,15},{4,16},{5,9},{6,18},{7,11},{8,28},{9,5... | collective-permute-start | bytes 294920 | tf_op jit(solution)/shard_map/ppermute | solution.py:634
  76.7 11.1 %collective-permute-start.14 = (f32[8,24,128]{2,1,0:T(8,128)S(1)}, f32[8,24,128]{2,1,0:T(8,128)S(1)}, u32[]{:S(2)}, u32[]{:S(2)}) collective-permute-start(f32[8,24,128]{2,1,0:T(8,128)S(1)} %bitcast.40), channel_id=1, source_target_pairs={{0,12},{1,21},{2,14},{3,23},{4,8},{5,17},{6,10},{7,19},{8,4},{9,29... | collective-permute-start | bytes 294920 | tf_op jit(solution)/shard_map/ppermute | solution.py:634
  77.1 10.7 %collective-permute-start.15 = (f32[8,24,128]{2,1,0:T(8,128)S(1)}, f32[8,24,128]{2,1,0:T(8,128)S(1)}, u32[]{:S(2)}, u32[]{:S(2)}) collective-permute-start(f32[8,24,128]{2,1,0:T(8,128)S(1)} %bitcast.39), channel_id=1, source_target_pairs={{0,28},{1,29},{2,30},{3,31},{4,24},{5,25},{6,26},{7,27},{8,20},{9,... | collective-permute-start | bytes 294920 | tf_op jit(solution)/shard_map/ppermute | solution.py:634
  94.7 15.9 %collective-permute-start.16 = (f32[8,2,24,128]{3,2,1,0:T(8,128)S(1)}, f32[8,2,24,128]{3,2,1,0:T(8,128)S(1)}, u32[]{:S(2)}, u32[]{:S(2)}) collective-permute-start(f32[8,2,24,128]{3,2,1,0:T(8,128)S(1)} %get-tuple-element.61), channel_id=1, source_target_pairs={{0,16},{1,5},{2,18},{3,7},{4,20},{5,1},{6,22},{7,3},{8,24},{9,13},... | collective-permute-start | bytes 589832 | tf_op jit(solution)/shard_map/ppermute | solution.py:634
  97.1 13.5 %collective-permute-start.17 = (f32[8,2,24,128]{3,2,1,0:T(8,128)S(1)}, f32[8,2,24,128]{3,2,1,0:T(8,128)S(1)}, u32[]{:S(2)}, u32[]{:S(2)}) collective-permute-start(f32[8,2,24,128]{3,2,1,0:T(8,128)S(1)} %get-tuple-element.62), channel_id=1, source_target_pairs={{0,4},{1,17},{2,6},{3,19},{4,0},{5,21},{6,2},{7,23},{8,12},{9,25},... | collective-permute-start | bytes 589832 | tf_op jit(solution)/shard_map/ppermute | solution.py:634
  98.1 16.2 %collective-permute-start.18 = (f32[8,2,24,128]{3,2,1,0:T(8,128)S(1)}, f32[8,2,24,128]{3,2,1,0:T(8,128)S(1)}, u32[]{:S(2)}, u32[]{:S(2)}) collective-permute-start(f32[8,2,24,128]{3,2,1,0:T(8,128)S(1)} %get-tuple-element.63), channel_id=1, source_target_pairs={{0,8},{1,25},{2,10},{3,27},{4,12},{5,29},{6,14},{7,31},{8,0},{9,17... | collective-permute-start | bytes 589832 | tf_op jit(solution)/shard_map/ppermute | solution.py:634
  98.1 16.2 %collective-permute-start.19 = (f32[8,2,24,128]{3,2,1,0:T(8,128)S(1)}, f32[8,2,24,128]{3,2,1,0:T(8,128)S(1)}, u32[]{:S(2)}, u32[]{:S(2)}) collective-permute-start(f32[8,2,24,128]{3,2,1,0:T(8,128)S(1)} %get-tuple-element.64), channel_id=1, source_target_pairs={{0,24},{1,9},{2,26},{3,11},{4,28},{5,13},{6,30},{7,15},{8,16},{9,1... | collective-permute-start | bytes 589832 | tf_op jit(solution)/shard_map/ppermute | solution.py:634
  100.8 28.5 %collective-permute-start.20 = (f32[8,2,24,128]{3,2,1,0:T(8,128)S(1)}, f32[8,2,24,128]{3,2,1,0:T(8,128)S(1)}, u32[]{:S(2)}, u32[]{:S(2)}) collective-permute-start(f32[8,2,24,128]{3,2,1,0:T(8,128)S(1)} %get-tuple-element.65), channel_id=1, source_target_pairs={{0,20},{1,13},{2,22},{3,15},{4,16},{5,9},{6,18},{7,11},{8,28},{9,5... | collective-permute-start | bytes 589832 | tf_op jit(solution)/shard_map/ppermute | solution.py:634
  110.6 18.6 %collective-permute-start.21 = (f32[8,2,24,128]{3,2,1,0:T(8,128)S(1)}, f32[8,2,24,128]{3,2,1,0:T(8,128)S(1)}, u32[]{:S(2)}, u32[]{:S(2)}) collective-permute-start(f32[8,2,24,128]{3,2,1,0:T(8,128)S(1)} %get-tuple-element.66), channel_id=1, source_target_pairs={{0,12},{1,21},{2,14},{3,23},{4,8},{5,17},{6,10},{7,19},{8,4},{9,29... | collective-permute-start | bytes 589832 | tf_op jit(solution)/shard_map/ppermute | solution.py:634
  110.6 18.6 %collective-permute-start.22 = (f32[8,2,24,128]{3,2,1,0:T(8,128)S(1)}, f32[8,2,24,128]{3,2,1,0:T(8,128)S(1)}, u32[]{:S(2)}, u32[]{:S(2)}) collective-permute-start(f32[8,2,24,128]{3,2,1,0:T(8,128)S(1)} %get-tuple-element.67), channel_id=1, source_target_pairs={{0,28},{1,29},{2,30},{3,31},{4,24},{5,25},{6,26},{7,27},{8,20},{9,... | collective-permute-start | bytes 589832 | tf_op jit(solution)/shard_map/ppermute | solution.py:634

commit v12 on v11

--- a/solution.py
+++ b/solution.py
@@ -521,14 +521,8 @@
     first_ref, refs = (refs[0], refs[1:])
     count = owners * (pieces - 1)
     block_refs, matrix_ref, refs = (refs[:count], refs[count], refs[count + 1 :])
-    out_refs, (matrices, arrived, ordered, full) = (refs[:owners], refs[owners:])
+    out_refs, (ordered, full) = (refs[:owners], refs[owners:])
     slots, heights = (matrix_ref.shape[0], matrix_ref.shape[1])
-    copies = [
-        pltpu.make_async_copy(matrix_ref.at[s], matrices.at[s], arrived.at[s])
-        for s in range(slots)
-    ]
-    for copy in copies:
-        copy.start()
     own_kx, own_ht = (lax.axis_index("kx"), lax.axis_index("ht"))
     partners = []
     for position in range(owners):
@@ -546,15 +540,18 @@
                 for first in range(0, kx_count, groups):
                     blocks = [source[(first + g) * ht_count + h, s] for g in range(groups)]
                     tiles.append(jnp.concatenate(regroup(blocks, rows), axis=0))
-        top, rest = two_parts(jnp.concatenate(tiles, axis=1))
-        count = top.shape[0]
-        copies[s].wait()
-        matrix_top, matrix_rest = two_parts(matrices[s])
+        fields = jnp.concatenate(tiles, axis=1)
+        count = fields.shape[0]
+        spare = -count % LANES
+        if spare:
+            fields = jnp.concatenate([fields, jnp.zeros((spare, heights), jnp.float32)], axis=0)
+        top, rest = two_parts(fields)
+        matrix_top, matrix_rest = two_parts(matrix_ref[s])
         last = ((1,), (1,))
         both = dot(matrix_top, jnp.concatenate([top, rest], axis=0), last)
-        solved = both[:, :count] + both[:, count:] + dot(matrix_rest, top, last)
+        solved = both[:, : count + spare] + both[:, count + spare :] + dot(matrix_rest, top, last)
         for tile in range(heights // LANES):
-            full[s % 2, tile] = solved[tile * LANES : (tile + 1) * LANES].T
+            full[s % 2, tile] = solved[tile * LANES : (tile + 1) * LANES].T[:count]
         for out_ref, (kx, ht) in zip(out_refs, partners):
             band = pl.ds(pl.multiple_of(kx * per_band, 8), per_band)
             for tile in range(lane_tiles):
@@ -570,11 +567,9 @@
             solve_kernel, groups=groups, kx_count=kx_count, ht_count=ht_count, pieces=pieces
         ),
         out_shape=(jax.ShapeDtypeStruct(shape, jnp.float32),) * owners,
-        in_specs=[VMEM] * (1 + len(blocks)) + [pl.BlockSpec(memory_space=pl.ANY)],
+        in_specs=[VMEM] * (2 + len(blocks)),
         out_specs=(VMEM,) * owners,
         scratch_shapes=[
-            pltpu.VMEM(helmholtz.shape, jnp.float32),
-            pltpu.SemaphoreType.DMA((slots,)),
             pltpu.VMEM((max(pieces - 1, 1),) + first.shape, jnp.float32),
             pltpu.VMEM((2, heights // LANES, count, LANES), jnp.float32),
         ],

time: 133 us -> 132 us (level)
  no operation moved by 1% of the time
where the time goes in v12:
time: 132 us; the launch traced here: 131 us
  waiting for transfers between devices  52.3 us (40%)
  starting transfers between devices  47.2 us (36%)
  Pallas kernels  29.2 us (22%)
  local copies, waits for them, and re-layouts  1.56 us (1%)
    ppermute x17, waiting for transfers between devices, exchange(): result[position] = lax.ppermute(blocks[position], axes + ('real',), pairs)  41.9 us
    ppermute x17, starting transfers between devices, exchange(): result[position] = lax.ppermute(blocks[position], axes + ('real',), pairs)  26.4 us
    ppermute x6, waiting for transfers between devices, swap(): return lax.ppermute(value, 'real', pairs)  10.4 us
    all_to_all x1, starting transfers between devices, local(): block = lax.all_to_all(block, 'kx', split_axis=0, concat_axis=0, tiled=True)  9.53 us
    all_to_all x1, starting transfers between devices, local(): lax.all_to_all(block, ('kx', 'ht'), split_axis=0, concat_axis=0, tiled=True)  7.83 us
    pallas_call x2, Pallas kernels, stress_terms(): pl.pallas_call(stress_kernel, out_shape=(jax.ShapeDtypeStruct(shape, jnp....  6.94 us
    pallas_call x1, Pallas kernels, solve(): pl.pallas_call(functools.partial(solve_kernel, groups=groups, kx_count=kx...  6.14 us
    pallas_call x2, Pallas kernels, high_terms(): pl.pallas_call(products_kernel, out_shape=jax.ShapeDtypeStruct((component...  6 us
  transfers between devices with their start and end apart: 25, of which 13 were waited for; matrix products, arithmetic and copies ran while one was open for 1% of the time, Pallas kernels for 14%

profile of v12, /device:TPU:0, one launch (start us, length us, event | category | flops | bytes accessed | tf_op | source)
XLA Modules:
  0.0 130.6 jit_solution(8259420051889873048)
XLA Ops:
  0.0 2.1 %pack_first.1 = (f32[392,128]{1,0:T(8,128)}, f32[392,128]{1,0:T(8,128)}, f32[392,128]{1,0:T(8,128)}, f32[392,128]{1,0:T(8,128)}) custom-call(s32[4,8]{1,0:T(4,128)} %near_ref.1, s32[4]{0:T(128)} %count_ref.1, f32[12,2,4,32,128]{4,3,2,1,0:T(8,128)} %bitcast.46), custom_call_target="tpu_custom_call" | custom-call | bytes 1572864 | tf_op jit(solution)/shard_map/pack_first/pallas_call | solution.py:175
  2.1 3.0 %collective-permute-start = (f32[392,128]{1,0:T(8,128)}, f32[392,128]{1,0:T(8,128)S(1)}, u32[]{:S(2)}, u32[]{:S(2)}) collective-permute-start(f32[392,128]{1,0:T(8,128)} %get-tuple-element.38), channel_id=1, source_target_pairs={{0,8},{1,25},{2,10},{3,27},{8,0},{9,17},{10,2},{11,19},{16,24},{17... | collective-permute-start | bytes 602120 | tf_op jit(solution)/shard_map/ppermute | solution.py:629
  5.1 2.5 %collective-permute-start.1 = (f32[392,128]{1,0:T(8,128)}, f32[392,128]{1,0:T(8,128)S(1)}, u32[]{:S(2)}, u32[]{:S(2)}) collective-permute-start(f32[392,128]{1,0:T(8,128)} %get-tuple-element.39), channel_id=1, source_target_pairs={{0,24},{1,9},{2,26},{3,11},{8,16},{9,1},{10,18},{11,3},{16,8},{17,... | collective-permute-start | bytes 602120 | tf_op jit(solution)/shard_map/ppermute | solution.py:629
  7.6 0.1 collective-permute-start.2
  7.7 0.0 copy-start.5
  7.7 4.2 %collective-permute-done.refs_1_._ = f32[392,128]{1,0:T(8,128)S(1)} collective-permute-done((f32[392,128]{1,0:T(8,128)}, f32[392,128]{1,0:T(8,128)S(1)}, u32[]{:S(2)}, u32[]{:S(2)}) %collective-permute-start) | collective-permute-done | bytes 200736 | tf_op jit(solution)/shard_map/ppermute | solution.py:629
  11.9 0.7 copy-done
  12.6 2.1 %pack.1 = f32[4,384,128]{2,1,0:T(8,128)} custom-call(f32[12,2,4,32,128]{4,3,2,1,0:T(8,128)} %bitcast.47, f32[392,128]{1,0:T(8,128)} %copy-done), custom_call_target="tpu_custom_call" | custom-call | bytes 1572864 | tf_op jit(solution)/shard_map/pack/pallas_call | solution.py:201
  14.7 9.5 %all-to-all-start.1 = ((f32[4,384,128]{2,1,0:T(8,128)}), f32[4,384,128]{2,1,0:T(8,128)S(1)}, u32[]{:S(2)}, u32[]{:S(2)}) async-start(f32[4,384,128]{2,1,0:T(8,128)} %pack.1), calls=%async_computation.1 | async-start | bytes 1572864 | tf_op jit(solution)/shard_map/all_to_all | solution.py:677
  24.2 0.1 broadcast_in_dim.85
  24.3 0.1 broadcast_in_dim.86
  24.4 0.1 broadcast_in_dim.91
  24.5 0.1 broadcast_in_dim.92
  24.6 0.1 broadcast_in_dim.96
  24.6 0.1 broadcast_in_dim.97
  24.7 0.1 broadcast_in_dim.101
  24.8 0.1 broadcast_in_dim.102
  24.9 0.8 tables.1
  25.7 0.0 collective-permute-done.1.refs_2_
  25.7 1.6 %collective-permute-done.2.refs_3_ = f32[392,128]{1,0:T(8,128)S(1)} collective-permute-done((f32[392,128]{1,0:T(8,128)}, f32[392,128]{1,0:T(8,128)S(1)}, u32[]{:S(2)}, u32[]{:S(2)}) %collective-permute-start.2) | collective-permute-done | bytes 200736 | tf_op jit(solution)/shard_map/ppermute | solution.py:629
  27.3 0.1 add_convert_fusion
  27.4 3.5 %stress.2 = (f32[3,16,32,128]{3,2,1,0:T(8,128)S(1)}, f32[3,16,32,256]{3,2,1,0:T(8,128)S(1)}, f32[3,4,32,128]{3,2,1,0:T(8,128)S(1)}, f32[3,4,32,128]{3,2,1,0:T(8,128)S(1)}) custom-call(s32[8]{0:T(128)S(1)} %copy-done.5, s32[16,8]{1,0:T(8,128)S(1)} %bitcast.26, f32[392,128]{1,0:T(8,128)S(1)} %copy-done.3, f32[392,128]{1,0:T(8,128)S(1)} %copy-done.1, ...), custom_call_target="tpu_custom_call" | custom-call | bytes 12582912 | tf_op jit(solution)/shard_map/stress/pallas_call | solution.py:353
  30.9 0.1 collective-permute-start.3
  31.0 1.4 %collective-permute-done.3 = f32[3,4,32,128]{3,2,1,0:T(8,128)S(1)} collective-permute-done((f32[3,4,32,128]{3,2,1,0:T(8,128)S(1)}, f32[3,4,32,128]{3,2,1,0:T(8,128)S(1)}, u32[]{:S(2)}, u32[]{:S(2)}) %collective-permute-start.3) | collective-permute-done | bytes 196640 | tf_op jit(solution)/shard_map/ppermute | solution.py:651
  32.4 1.6 %collective-permute-start.4 = (f32[3,4,32,128]{3,2,1,0:T(8,128)S(1)}, f32[3,4,32,128]{3,2,1,0:T(8,128)S(1)}, u32[]{:S(2)}, u32[]{:S(2)}) collective-permute-start(f32[3,4,32,128]{3,2,1,0:T(8,128)S(1)} %add.21.first_ref.refs_4_), channel_id=1, source_target_pairs={{0,2},{1,3},{2,0},{3,1},{4,6},{5,7},{6,4},{7,5},{8,10},{9,11},{10,... | collective-permute-start | bytes 589832 | tf_op jit(solution)/shard_map/ppermute | solution.py:651
  34.0 0.2 slice_reduce_fusion.count_ref
  34.2 3.0 %products.2._.forcing_ref = f32[3,8,32,128]{3,2,1,0:T(8,128)S(1)} custom-call(s32[8]{0:T(128)S(1)} %copy-done.5, s32[16,8]{1,0:T(8,128)S(1)} %bitcast.27, s32[16]{0:T(128)S(1)} %slice_reduce_fusion.count_ref, f32[3,16,32,256]{3,2,1,0:T(8,128)S(1)} %get-tuple-element.45.physical, bf16[256,256]{1,0:T(8,128)(2,1)S(1)} %get-tuple-element.42.refs_6_.back_ref.refs_3_, ...), custom_call_target="tpu_custom_call" | custom-call | bytes 12582912 | tf_op jit(solution)/shard_map/products/pallas_call | solution.py:418
  37.2 2.3 %collective-permute-done.4.second_ref = f32[3,4,32,128]{3,2,1,0:T(8,128)S(1)} collective-permute-done((f32[3,4,32,128]{3,2,1,0:T(8,128)S(1)}, f32[3,4,32,128]{3,2,1,0:T(8,128)S(1)}, u32[]{:S(2)}, u32[]{:S(2)}) %collective-permute-start.4) | collective-permute-done | bytes 196640 | tf_op jit(solution)/shard_map/ppermute | solution.py:651
  39.5 0.1 collective-permute-start.5
  39.5 1.4 %collective-permute-done.5.other_ref = f32[3,4,32,128]{3,2,1,0:T(8,128)S(1)} collective-permute-done((f32[3,4,32,128]{3,2,1,0:T(8,128)S(1)}, f32[3,4,32,128]{3,2,1,0:T(8,128)S(1)}, u32[]{:S(2)}, u32[]{:S(2)}) %collective-permute-start.5) | collective-permute-done | bytes 196640 | tf_op jit(solution)/shard_map/ppermute | solution.py:651
  41.0 1.9 %outgoing.2 = f32[1536,128]{1,0:T(8,128)} custom-call(s32[8]{0:T(128)S(1)} %copy-done.5, s32[16]{0:T(128)S(1)} %slice_reduce_fusion.count_ref, f32[3,16,32,128]{3,2,1,0:T(8,128)S(1)} %get-tuple-element.44.slotted_ref, f32[3,8,32,128]{3,2,1,0:T(8,128)S(1)} %products.2._.forcing_ref, f32[3,4,32,128]{3,2,1,0:T(8,128)S(1)} %ordered_sum.2.kept_ref, ...), custom_call_target="tpu_custom_call" | custom-call | bytes 1572864 | tf_op jit(solution)/shard_map/outgoing/pallas_call | solution.py:484
  42.9 0.0 all-to-all-done.1.refs_0_
  42.9 7.8 %all-to-all-start = ((f32[8,8,24,128]{3,2,1,0:T(8,128)}), f32[8,8,24,128]{3,2,1,0:T(8,128)S(1)}, u32[]{:S(2)}, u32[]{:S(2)}) async-start(f32[8,8,24,128]{3,2,1,0:T(8,128)} %bitcast.5), calls=%async_computation | async-start | bytes 1572864 | tf_op jit(solution)/shard_map/all_to_all | solution.py:707
  50.7 3.5 %stress.3 = (f32[3,16,32,128]{3,2,1,0:T(8,128)S(1)}, f32[3,16,32,256]{3,2,1,0:T(8,128)S(1)}, f32[3,4,32,128]{3,2,1,0:T(8,128)S(1)}, f32[3,4,32,128]{3,2,1,0:T(8,128)S(1)}) custom-call(s32[8]{0:T(128)S(1)} %copy-done.5, s32[16,8]{1,0:T(8,128)S(1)} %bitcast.28, f32[4,384,128]{2,1,0:T(8,128)S(1)} %all-to-all-done.1.refs_0_, ...), custom_call_target="tpu_custom_call" | custom-call | bytes 12582912 | tf_op jit(solution)/shard_map/stress/pallas_call | solution.py:353
  54.2 0.1 collective-permute-start.6
  54.2 1.4 %collective-permute-done.6 = f32[3,4,32,128]{3,2,1,0:T(8,128)S(1)} collective-permute-done((f32[3,4,32,128]{3,2,1,0:T(8,128)S(1)}, f32[3,4,32,128]{3,2,1,0:T(8,128)S(1)}, u32[]{:S(2)}, u32[]{:S(2)}) %collective-permute-start.6) | collective-permute-done | bytes 196640 | tf_op jit(solution)/shard_map/ppermute | solution.py:651
  55.7 1.6 %collective-permute-start.7 = (f32[3,4,32,128]{3,2,1,0:T(8,128)S(1)}, f32[3,4,32,128]{3,2,1,0:T(8,128)S(1)}, u32[]{:S(2)}, u32[]{:S(2)}) collective-permute-start(f32[3,4,32,128]{3,2,1,0:T(8,128)S(1)} %add.22.first_ref), channel_id=1, source_target_pairs={{0,2},{1,3},{2,0},{3,1},{4,6},{5,7},{6,4},{7,5},{8,10},{9,11},{10,... | collective-permute-start | bytes 589832 | tf_op jit(solution)/shard_map/ppermute | solution.py:651
  57.3 3.0 %products.3._.forcing_ref = f32[3,8,32,128]{3,2,1,0:T(8,128)S(1)} custom-call(s32[8]{0:T(128)S(1)} %copy-done.5, s32[16,8]{1,0:T(8,128)S(1)} %bitcast.29, s32[16]{0:T(128)S(1)} %slice_reduce_fusion.count_ref, f32[3,16,32,256]{3,2,1,0:T(8,128)S(1)} %get-tuple-element.49.physical, bf16[256,256]{1,0:T(8,128)(2,1)S(1)} %get-tuple-element.42.refs_6_.back_ref.refs_3_, ...), custom_call_target="tpu_custom_call" | custom-call | bytes 12582912 | tf_op jit(solution)/shard_map/products/pallas_call | solution.py:418
  60.3 2.4 %collective-permute-done.7.second_ref = f32[3,4,32,128]{3,2,1,0:T(8,128)S(1)} collective-permute-done((f32[3,4,32,128]{3,2,1,0:T(8,128)S(1)}, f32[3,4,32,128]{3,2,1,0:T(8,128)S(1)}, u32[]{:S(2)}, u32[]{:S(2)}) %collective-permute-start.7) | collective-permute-done | bytes 196640 | tf_op jit(solution)/shard_map/ppermute | solution.py:651
  62.7 0.1 collective-permute-start.8
  62.8 1.4 %collective-permute-done.8.other_ref = f32[3,4,32,128]{3,2,1,0:T(8,128)S(1)} collective-permute-done((f32[3,4,32,128]{3,2,1,0:T(8,128)S(1)}, f32[3,4,32,128]{3,2,1,0:T(8,128)S(1)}, u32[]{:S(2)}, u32[]{:S(2)}) %collective-permute-start.8) | collective-permute-done | bytes 196640 | tf_op jit(solution)/shard_map/ppermute | solution.py:651
  64.3 1.2 outgoing.3
  65.4 3.0 %collective-permute-start.9 = (f32[8,24,128]{2,1,0:T(8,128)S(1)}, f32[8,24,128]{2,1,0:T(8,128)S(1)}, u32[]{:S(2)}, u32[]{:S(2)}) collective-permute-start(f32[8,24,128]{2,1,0:T(8,128)S(1)} %bitcast.45), channel_id=1, source_target_pairs={{0,16},{1,5},{2,18},{3,7},{4,20},{5,1},{6,22},{7,3},{8,24},{9,13},... | collective-permute-start | bytes 294920 | tf_op jit(solution)/shard_map/ppermute | solution.py:629
  68.4 1.5 %collective-permute-start.10 = (f32[8,24,128]{2,1,0:T(8,128)S(1)}, f32[8,24,128]{2,1,0:T(8,128)S(1)}, u32[]{:S(2)}, u32[]{:S(2)}) collective-permute-start(f32[8,24,128]{2,1,0:T(8,128)S(1)} %bitcast.44), channel_id=1, source_target_pairs={{0,4},{1,17},{2,6},{3,19},{4,0},{5,21},{6,2},{7,23},{8,12},{9,25},... | collective-permute-start | bytes 294920 | tf_op jit(solution)/shard_map/ppermute | solution.py:629
  69.9 1.5 %collective-permute-start.11 = (f32[8,24,128]{2,1,0:T(8,128)S(1)}, f32[8,24,128]{2,1,0:T(8,128)S(1)}, u32[]{:S(2)}, u32[]{:S(2)}) collective-permute-start(f32[8,24,128]{2,1,0:T(8,128)S(1)} %bitcast.43), channel_id=1, source_target_pairs={{0,8},{1,25},{2,10},{3,27},{4,12},{5,29},{6,14},{7,31},{8,0},{9,17... | collective-permute-start | bytes 294920 | tf_op jit(solution)/shard_map/ppermute | solution.py:629
  71.4 0.6 collective-permute-start.12
  71.9 1.5 %collective-permute-start.13 = (f32[8,24,128]{2,1,0:T(8,128)S(1)}, f32[8,24,128]{2,1,0:T(8,128)S(1)}, u32[]{:S(2)}, u32[]{:S(2)}) collective-permute-start(f32[8,24,128]{2,1,0:T(8,128)S(1)} %bitcast.41), channel_id=1, source_target_pairs={{0,20},{1,13},{2,22},{3,15},{4,16},{5,9},{6,18},{7,11},{8,28},{9,5... | collective-permute-start | bytes 294920 | tf_op jit(solution)/shard_map/ppermute | solution.py:629
  73.4 3.3 %collective-permute-done.9.refs_2_ = f32[8,24,128]{2,1,0:T(8,128)S(1)} collective-permute-done((f32[8,24,128]{2,1,0:T(8,128)S(1)}, f32[8,24,128]{2,1,0:T(8,128)S(1)}, u32[]{:S(2)}, u32[]{:S(2)}) %collective-permute-start.9) | collective-permute-done | bytes 98336 | tf_op jit(solution)/shard_map/ppermute | solution.py:629
  76.7 0.4 collective-permute-start.14
  77.1 3.2 %collective-permute-start.15 = (f32[8,24,128]{2,1,0:T(8,128)S(1)}, f32[8,24,128]{2,1,0:T(8,128)S(1)}, u32[]{:S(2)}, u32[]{:S(2)}) collective-permute-start(f32[8,24,128]{2,1,0:T(8,128)S(1)} %bitcast.39), channel_id=1, source_target_pairs={{0,28},{1,29},{2,30},{3,31},{4,24},{5,25},{6,26},{7,27},{8,20},{9,... | collective-permute-start | bytes 294920 | tf_op jit(solution)/shard_map/ppermute | solution.py:629
  80.3 0.0 collective-permute-done.11.refs_4_
  80.3 0.0 collective-permute-done.12.refs_5_
  80.3 7.5 %collective-permute-done.13.refs_6_ = f32[8,24,128]{2,1,0:T(8,128)S(1)} collective-permute-done((f32[8,24,128]{2,1,0:T(8,128)S(1)}, f32[8,24,128]{2,1,0:T(8,128)S(1)}, u32[]{:S(2)}, u32[]{:S(2)}) %collective-permute-start.13) | collective-permute-done | bytes 98336 | tf_op jit(solution)/shard_map/ppermute | solution.py:629
  87.8 0.0 collective-permute-done.14.refs_7_
  87.8 6.1 %solve.1 = (f32[8,2,24,128]{3,2,1,0:T(8,128)S(1)}, f32[8,2,24,128]{3,2,1,0:T(8,128)S(1)}, f32[8,2,24,128]{3,2,1,0:T(8,128)S(1)}, f32[8,2,24,128]{3,2,1,0:T(8,128...) custom-call(f32[8,8,24,128]{3,2,1,0:T(8,128)S(1)} %all-to-all-done.r, ...), custom_call_target="tpu_custom_call" | custom-call | bytes 8388608 | tf_op jit(solution)/shard_map/solve/pallas_call | solution.py:565
  94.0 2.4 %collective-permute-start.16 = (f32[8,2,24,128]{3,2,1,0:T(8,128)S(1)}, f32[8,2,24,128]{3,2,1,0:T(8,128)S(1)}, u32[]{:S(2)}, u32[]{:S(2)}) collective-permute-start(f32[8,2,24,128]{3,2,1,0:T(8,128)S(1)} %get-tuple-element.61), channel_id=1, source_target_pairs={{0,16},{1,5},{2,18},{3,7},{4,20},{5,1},{6,22},{7,3},{8,24},{9,13},... | collective-permute-start | bytes 589832 | tf_op jit(solution)/shard_map/ppermute | solution.py:629
  96.3 1.0 collective-permute-start.17
  97.4 2.7 %collective-permute-start.19 = (f32[8,2,24,128]{3,2,1,0:T(8,128)S(1)}, f32[8,2,24,128]{3,2,1,0:T(8,128)S(1)}, u32[]{:S(2)}, u32[]{:S(2)}) collective-permute-start(f32[8,2,24,128]{3,2,1,0:T(8,128)S(1)} %get-tuple-element.64), channel_id=1, source_target_pairs={{0,24},{1,9},{2,26},{3,11},{4,28},{5,13},{6,30},{7,15},{8,16},{9,1... | collective-permute-start | bytes 589832 | tf_op jit(solution)/shard_map/ppermute | solution.py:629
  100.1 1.2 collective-permute-start.20
  101.3 8.6 %collective-permute-done.16 = f32[8,2,24,128]{3,2,1,0:T(8,128)S(1)} collective-permute-done((f32[8,2,24,128]{3,2,1,0:T(8,128)S(1)}, f32[8,2,24,128]{3,2,1,0:T(8,128)S(1)}, u32[]{:S(2)}, u32[]{:S(2)}) %collective-permute-start.16) | collective-permute-done | bytes 196640 | tf_op jit(solution)/shard_map/ppermute | solution.py:629
  109.9 1.9 %collective-permute-start.22 = (f32[8,2,24,128]{3,2,1,0:T(8,128)S(1)}, f32[8,2,24,128]{3,2,1,0:T(8,128)S(1)}, u32[]{:S(2)}, u32[]{:S(2)}) collective-permute-start(f32[8,2,24,128]{3,2,1,0:T(8,128)S(1)} %get-tuple-element.67), channel_id=1, source_target_pairs={{0,28},{1,29},{2,30},{3,31},{4,24},{5,25},{6,26},{7,27},{8,20},{9,... | collective-permute-start | bytes 589832 | tf_op jit(solution)/shard_map/ppermute | solution.py:629
  111.9 1.7 %collective-permute-done.18 = f32[8,2,24,128]{3,2,1,0:T(8,128)S(1)} collective-permute-done((f32[8,2,24,128]{3,2,1,0:T(8,128)S(1)}, f32[8,2,24,128]{3,2,1,0:T(8,128)S(1)}, u32[]{:S(2)}, u32[]{:S(2)}) %collective-permute-start.18) | collective-permute-done | bytes 196640 | tf_op jit(solution)/shard_map/ppermute | solution.py:629
  113.5 15.0 %collective-permute-done.20 = f32[8,2,24,128]{3,2,1,0:T(8,128)S(1)} collective-permute-done((f32[8,2,24,128]{3,2,1,0:T(8,128)S(1)}, f32[8,2,24,128]{3,2,1,0:T(8,128)S(1)}, u32[]{:S(2)}, u32[]{:S(2)}) %collective-permute-start.20) | collective-permute-done | bytes 196640 | tf_op jit(solution)/shard_map/ppermute | solution.py:629
  128.5 2.1 %restore.1 = f32[3,4,256,128]{3,2,1,0:T(8,128)} custom-call(f32[384,128]{1,0:T(8,128)S(1)} %bitcast.30, f32[384,128]{1,0:T(8,128)S(1)} %bitcast.31, f32[384,128]{1,0:T(8,128)S(1)} %bitcast.32, f32[384,128]{1,0:T(8,128)S(1)} %bitcast.33, f32[384,128]{1,0:T(8,128)S(1)} %bitcast.34, f32[384,128]{1,0:T(8,128)S(1)} %bitcast.35, f32[384,128]{1,0:T(8,128)S(1)} %bitcast.36, ...), custom_call_target="tpu_custom_call" | custom-call | bytes 3145728 | tf_op jit(solution)/shard_map/restore/pallas_call | solution.py:607
  (37 shorter events, 0.2 us)
Async XLA Ops:
  2.1 9.8 %collective-permute-start = (f32[392,128]{1,0:T(8,128)}, f32[392,128]{1,0:T(8,128)S(1)}, u32[]{:S(2)}, u32[]{:S(2)}) collective-permute-start(f32[392,128]{1,0:T(8,128)} %get-tuple-element.38), channel_id=1, source_target_pairs={{0,8},{1,25},{2,10},{3,27},{8,0},{9,17},{10,2},{11,19},{16,24},{17... | collective-permute-start | bytes 602120 | tf_op jit(solution)/shard_map/ppermute | solution.py:629
  5.1 20.6 %collective-permute-start.1 = (f32[392,128]{1,0:T(8,128)}, f32[392,128]{1,0:T(8,128)S(1)}, u32[]{:S(2)}, u32[]{:S(2)}) collective-permute-start(f32[392,128]{1,0:T(8,128)} %get-tuple-element.39), channel_id=1, source_target_pairs={{0,24},{1,9},{2,26},{3,11},{8,16},{9,1},{10,18},{11,3},{16,8},{17,... | collective-permute-start | bytes 602120 | tf_op jit(solution)/shard_map/ppermute | solution.py:629
  7.6 19.7 %collective-permute-start.2 = (f32[392,128]{1,0:T(8,128)}, f32[392,128]{1,0:T(8,128)S(1)}, u32[]{:S(2)}, u32[]{:S(2)}) collective-permute-start(f32[392,128]{1,0:T(8,128)} %get-tuple-element.40), channel_id=1, source_target_pairs={{0,16},{1,17},{2,18},{3,19},{8,24},{9,25},{10,26},{11,27},{16,0},{... | collective-permute-start | bytes 602120 | tf_op jit(solution)/shard_map/ppermute | solution.py:629
  7.7 17.2 %copy-start.3 = (f32[392,128]{1,0:T(8,128)S(1)}, f32[392,128]{1,0:T(8,128)}, u32[]{:S(2)}) copy-start(f32[392,128]{1,0:T(8,128)} %get-tuple-element.37.refs_0_) | copy-start | bytes 602116
  7.7 17.2 %copy-start.2 = (bf16[128,256]{1,0:T(8,128)(2,1)S(1)}, bf16[128,256]{1,0:T(8,128)(2,1)}, u32[]{:S(2)}) copy-start(bf16[128,256]{1,0:T(8,128)(2,1)} %constant.22.clone.rest_ref.refs_5_.refs_2_) | copy-start | bytes 196612
  7.7 17.2 %copy-start.4 = (bf16[128,256]{1,0:T(8,128)(2,1)S(1)}, bf16[128,256]{1,0:T(8,128)(2,1)}, u32[]{:S(2)}) copy-start(bf16[128,256]{1,0:T(8,128)(2,1)} %constant.21.clone.top_ref) | copy-start | bytes 196612
  7.7 17.2 %copy-start.6 = (s32[64]{0:T(128)S(1)}, s32[64]{0:T(128)}, u32[]{:S(2)}) copy-start(s32[64]{0:T(128)} %owner_ref.1) | copy-start | bytes 772
  7.7 19.7 %copy-start.5 = (s32[8]{0:T(128)S(1)}, s32[8]{0:T(128)}, u32[]{:S(2)}) copy-start(s32[8]{0:T(128)} %low_ref.11) | copy-start | bytes 100
  11.9 0.7 copy-start
  14.7 11.0 %copy-start.1 = (f32[392,128]{1,0:T(8,128)S(1)}, f32[392,128]{1,0:T(8,128)}, u32[]{:S(2)}) copy-start(f32[392,128]{1,0:T(8,128)} %copy-done) | copy-start | bytes 602116
  14.7 28.2 %all-to-all-start.1 = ((f32[4,384,128]{2,1,0:T(8,128)}), f32[4,384,128]{2,1,0:T(8,128)S(1)}, u32[]{:S(2)}, u32[]{:S(2)}) async-start(f32[4,384,128]{2,1,0:T(8,128)} %pack.1), calls=%async_computation.1 | async-start | bytes 1572864 | tf_op jit(solution)/shard_map/all_to_all | solution.py:677
  30.9 1.5 %collective-permute-start.3 = (f32[3,4,32,128]{3,2,1,0:T(8,128)S(1)}, f32[3,4,32,128]{3,2,1,0:T(8,128)S(1)}, u32[]{:S(2)}, u32[]{:S(2)}) collective-permute-start(f32[3,4,32,128]{3,2,1,0:T(8,128)S(1)} %get-tuple-element.47), channel_id=1, source_target_pairs={{0,1},{1,0},{2,3},{3,2},{4,5},{5,4},{6,7},{7,6},{8,9},{9,8},{10,11... | collective-permute-start | bytes 589832 | tf_op jit(solution)/shard_map/ppermute | solution.py:651
  32.4 7.0 %collective-permute-start.4 = (f32[3,4,32,128]{3,2,1,0:T(8,128)S(1)}, f32[3,4,32,128]{3,2,1,0:T(8,128)S(1)}, u32[]{:S(2)}, u32[]{:S(2)}) collective-permute-start(f32[3,4,32,128]{3,2,1,0:T(8,128)S(1)} %add.21.first_ref.refs_4_), channel_id=1, source_target_pairs={{0,2},{1,3},{2,0},{3,1},{4,6},{5,7},{6,4},{7,5},{8,10},{9,11},{10,... | collective-permute-start | bytes 589832 | tf_op jit(solution)/shard_map/ppermute | solution.py:651
  39.5 1.5 %collective-permute-start.5 = (f32[3,4,32,128]{3,2,1,0:T(8,128)S(1)}, f32[3,4,32,128]{3,2,1,0:T(8,128)S(1)}, u32[]{:S(2)}, u32[]{:S(2)}) collective-permute-start(f32[3,4,32,128]{3,2,1,0:T(8,128)S(1)} %ordered_sum.2.kept_ref), channel_id=1, source_target_pairs={{0,1},{1,0},{2,3},{3,2},{4,5},{5,4},{6,7},{7,6},{8,9},{9,8},{10,11... | collective-permute-start | bytes 589832 | tf_op jit(solution)/shard_map/ppermute | solution.py:651
  42.9 44.9 %all-to-all-start = ((f32[8,8,24,128]{3,2,1,0:T(8,128)}), f32[8,8,24,128]{3,2,1,0:T(8,128)S(1)}, u32[]{:S(2)}, u32[]{:S(2)}) async-start(f32[8,8,24,128]{3,2,1,0:T(8,128)} %bitcast.5), calls=%async_computation | async-start | bytes 1572864 | tf_op jit(solution)/shard_map/all_to_all | solution.py:707
  54.2 1.5 %collective-permute-start.6 = (f32[3,4,32,128]{3,2,1,0:T(8,128)S(1)}, f32[3,4,32,128]{3,2,1,0:T(8,128)S(1)}, u32[]{:S(2)}, u32[]{:S(2)}) collective-permute-start(f32[3,4,32,128]{3,2,1,0:T(8,128)S(1)} %get-tuple-element.51), channel_id=1, source_target_pairs={{0,1},{1,0},{2,3},{3,2},{4,5},{5,4},{6,7},{7,6},{8,9},{9,8},{10,11... | collective-permute-start | bytes 589832 | tf_op jit(solution)/shard_map/ppermute | solution.py:651
  55.7 7.0 %collective-permute-start.7 = (f32[3,4,32,128]{3,2,1,0:T(8,128)S(1)}, f32[3,4,32,128]{3,2,1,0:T(8,128)S(1)}, u32[]{:S(2)}, u32[]{:S(2)}) collective-permute-start(f32[3,4,32,128]{3,2,1,0:T(8,128)S(1)} %add.22.first_ref), channel_id=1, source_target_pairs={{0,2},{1,3},{2,0},{3,1},{4,6},{5,7},{6,4},{7,5},{8,10},{9,11},{10,... | collective-permute-start | bytes 589832 | tf_op jit(solution)/shard_map/ppermute | solution.py:651
  62.7 1.5 %collective-permute-start.8 = (f32[3,4,32,128]{3,2,1,0:T(8,128)S(1)}, f32[3,4,32,128]{3,2,1,0:T(8,128)S(1)}, u32[]{:S(2)}, u32[]{:S(2)}) collective-permute-start(f32[3,4,32,128]{3,2,1,0:T(8,128)S(1)} %ordered_sum.3.kept_ref), channel_id=1, source_target_pairs={{0,1},{1,0},{2,3},{3,2},{4,5},{5,4},{6,7},{7,6},{8,9},{9,8},{10,11... | collective-permute-start | bytes 589832 | tf_op jit(solution)/shard_map/ppermute | solution.py:651
  65.4 11.2 %collective-permute-start.9 = (f32[8,24,128]{2,1,0:T(8,128)S(1)}, f32[8,24,128]{2,1,0:T(8,128)S(1)}, u32[]{:S(2)}, u32[]{:S(2)}) collective-permute-start(f32[8,24,128]{2,1,0:T(8,128)S(1)} %bitcast.45), channel_id=1, source_target_pairs={{0,16},{1,5},{2,18},{3,7},{4,20},{5,1},{6,22},{7,3},{8,24},{9,13},... | collective-permute-start | bytes 294920 | tf_op jit(solution)/shard_map/ppermute | solution.py:629
  68.4 8.7 %collective-permute-start.10 = (f32[8,24,128]{2,1,0:T(8,128)S(1)}, f32[8,24,128]{2,1,0:T(8,128)S(1)}, u32[]{:S(2)}, u32[]{:S(2)}) collective-permute-start(f32[8,24,128]{2,1,0:T(8,128)S(1)} %bitcast.44), channel_id=1, source_target_pairs={{0,4},{1,17},{2,6},{3,19},{4,0},{5,21},{6,2},{7,23},{8,12},{9,25},... | collective-permute-start | bytes 294920 | tf_op jit(solution)/shard_map/ppermute | solution.py:629
  69.9 10.4 %collective-permute-start.11 = (f32[8,24,128]{2,1,0:T(8,128)S(1)}, f32[8,24,128]{2,1,0:T(8,128)S(1)}, u32[]{:S(2)}, u32[]{:S(2)}) collective-permute-start(f32[8,24,128]{2,1,0:T(8,128)S(1)} %bitcast.43), channel_id=1, source_target_pairs={{0,8},{1,25},{2,10},{3,27},{4,12},{5,29},{6,14},{7,31},{8,0},{9,17... | collective-permute-start | bytes 294920 | tf_op jit(solution)/shard_map/ppermute | solution.py:629
  71.4 8.9 %collective-permute-start.12 = (f32[8,24,128]{2,1,0:T(8,128)S(1)}, f32[8,24,128]{2,1,0:T(8,128)S(1)}, u32[]{:S(2)}, u32[]{:S(2)}) collective-permute-start(f32[8,24,128]{2,1,0:T(8,128)S(1)} %bitcast.42), channel_id=1, source_target_pairs={{0,24},{1,9},{2,26},{3,11},{4,28},{5,13},{6,30},{7,15},{8,16},{9,1... | collective-permute-start | bytes 294920 | tf_op jit(solution)/shard_map/ppermute | solution.py:629
  71.9 15.9 %collective-permute-start.13 = (f32[8,24,128]{2,1,0:T(8,128)S(1)}, f32[8,24,128]{2,1,0:T(8,128)S(1)}, u32[]{:S(2)}, u32[]{:S(2)}) collective-permute-start(f32[8,24,128]{2,1,0:T(8,128)S(1)} %bitcast.41), channel_id=1, source_target_pairs={{0,20},{1,13},{2,22},{3,15},{4,16},{5,9},{6,18},{7,11},{8,28},{9,5... | collective-permute-start | bytes 294920 | tf_op jit(solution)/shard_map/ppermute | solution.py:629
  76.7 11.1 %collective-permute-start.14 = (f32[8,24,128]{2,1,0:T(8,128)S(1)}, f32[8,24,128]{2,1,0:T(8,128)S(1)}, u32[]{:S(2)}, u32[]{:S(2)}) collective-permute-start(f32[8,24,128]{2,1,0:T(8,128)S(1)} %bitcast.40), channel_id=1, source_target_pairs={{0,12},{1,21},{2,14},{3,23},{4,8},{5,17},{6,10},{7,19},{8,4},{9,29... | collective-permute-start | bytes 294920 | tf_op jit(solution)/shard_map/ppermute | solution.py:629
  77.1 10.7 %collective-permute-start.15 = (f32[8,24,128]{2,1,0:T(8,128)S(1)}, f32[8,24,128]{2,1,0:T(8,128)S(1)}, u32[]{:S(2)}, u32[]{:S(2)}) collective-permute-start(f32[8,24,128]{2,1,0:T(8,128)S(1)} %bitcast.39), channel_id=1, source_target_pairs={{0,28},{1,29},{2,30},{3,31},{4,24},{5,25},{6,26},{7,27},{8,20},{9,... | collective-permute-start | bytes 294920 | tf_op jit(solution)/shard_map/ppermute | solution.py:629
  94.0 15.9 %collective-permute-start.16 = (f32[8,2,24,128]{3,2,1,0:T(8,128)S(1)}, f32[8,2,24,128]{3,2,1,0:T(8,128)S(1)}, u32[]{:S(2)}, u32[]{:S(2)}) collective-permute-start(f32[8,2,24,128]{3,2,1,0:T(8,128)S(1)} %get-tuple-element.61), channel_id=1, source_target_pairs={{0,16},{1,5},{2,18},{3,7},{4,20},{5,1},{6,22},{7,3},{8,24},{9,13},... | collective-permute-start | bytes 589832 | tf_op jit(solution)/shard_map/ppermute | solution.py:629
  96.3 13.6 %collective-permute-start.17 = (f32[8,2,24,128]{3,2,1,0:T(8,128)S(1)}, f32[8,2,24,128]{3,2,1,0:T(8,128)S(1)}, u32[]{:S(2)}, u32[]{:S(2)}) collective-permute-start(f32[8,2,24,128]{3,2,1,0:T(8,128)S(1)} %get-tuple-element.62), channel_id=1, source_target_pairs={{0,4},{1,17},{2,6},{3,19},{4,0},{5,21},{6,2},{7,23},{8,12},{9,25},... | collective-permute-start | bytes 589832 | tf_op jit(solution)/shard_map/ppermute | solution.py:629
  97.4 16.2 %collective-permute-start.18 = (f32[8,2,24,128]{3,2,1,0:T(8,128)S(1)}, f32[8,2,24,128]{3,2,1,0:T(8,128)S(1)}, u32[]{:S(2)}, u32[]{:S(2)}) collective-permute-start(f32[8,2,24,128]{3,2,1,0:T(8,128)S(1)} %get-tuple-element.63), channel_id=1, source_target_pairs={{0,8},{1,25},{2,10},{3,27},{4,12},{5,29},{6,14},{7,31},{8,0},{9,17... | collective-permute-start | bytes 589832 | tf_op jit(solution)/shard_map/ppermute | solution.py:629
  97.4 16.2 %collective-permute-start.19 = (f32[8,2,24,128]{3,2,1,0:T(8,128)S(1)}, f32[8,2,24,128]{3,2,1,0:T(8,128)S(1)}, u32[]{:S(2)}, u32[]{:S(2)}) collective-permute-start(f32[8,2,24,128]{3,2,1,0:T(8,128)S(1)} %get-tuple-element.64), channel_id=1, source_target_pairs={{0,24},{1,9},{2,26},{3,11},{4,28},{5,13},{6,30},{7,15},{8,16},{9,1... | collective-permute-start | bytes 589832 | tf_op jit(solution)/shard_map/ppermute | solution.py:629
  100.1 28.5 %collective-permute-start.20 = (f32[8,2,24,128]{3,2,1,0:T(8,128)S(1)}, f32[8,2,24,128]{3,2,1,0:T(8,128)S(1)}, u32[]{:S(2)}, u32[]{:S(2)}) collective-permute-start(f32[8,2,24,128]{3,2,1,0:T(8,128)S(1)} %get-tuple-element.65), channel_id=1, source_target_pairs={{0,20},{1,13},{2,22},{3,15},{4,16},{5,9},{6,18},{7,11},{8,28},{9,5... | collective-permute-start | bytes 589832 | tf_op jit(solution)/shard_map/ppermute | solution.py:629
  109.9 18.6 %collective-permute-start.21 = (f32[8,2,24,128]{3,2,1,0:T(8,128)S(1)}, f32[8,2,24,128]{3,2,1,0:T(8,128)S(1)}, u32[]{:S(2)}, u32[]{:S(2)}) collective-permute-start(f32[8,2,24,128]{3,2,1,0:T(8,128)S(1)} %get-tuple-element.66), channel_id=1, source_target_pairs={{0,12},{1,21},{2,14},{3,23},{4,8},{5,17},{6,10},{7,19},{8,4},{9,29... | collective-permute-start | bytes 589832 | tf_op jit(solution)/shard_map/ppermute | solution.py:629
  109.9 18.6 %collective-permute-start.22 = (f32[8,2,24,128]{3,2,1,0:T(8,128)S(1)}, f32[8,2,24,128]{3,2,1,0:T(8,128)S(1)}, u32[]{:S(2)}, u32[]{:S(2)}) collective-permute-start(f32[8,2,24,128]{3,2,1,0:T(8,128)S(1)} %get-tuple-element.67), channel_id=1, source_target_pairs={{0,28},{1,29},{2,30},{3,31},{4,24},{5,25},{6,26},{7,27},{8,20},{9,... | collective-permute-start | bytes 589832 | tf_op jit(solution)/shard_map/ppermute | solution.py:629

commit v13 on v12

--- a/solution.py
+++ b/solution.py
@@ -516,13 +516,43 @@
     return blocks
 
 
+def split_kernel(matrix_ref, top_ref, rest_ref):
+    top_ref[...], rest_ref[...] = two_parts(matrix_ref[...])
+
+
+def split_matrix(helmholtz):
+    slots, heights, _ = helmholtz.shape
+    spec = pl.BlockSpec((1, heights, heights), lambda s: (s, 0, 0))
+    shape = jax.ShapeDtypeStruct(helmholtz.shape, jnp.bfloat16)
+    return pl.pallas_call(
+        split_kernel,
+        out_shape=(shape, shape),
+        grid=(slots,),
+        in_specs=[spec],
+        out_specs=(spec, spec),
+        compiler_params=params(),
+        cost_estimate=cost(8 * helmholtz.size),
+        name="split_matrix",
+    )(helmholtz)
+
+
 def solve_kernel(*refs, groups, kx_count, ht_count, pieces):
     owners = kx_count * ht_count
     first_ref, refs = (refs[0], refs[1:])
     count = owners * (pieces - 1)
-    block_refs, matrix_ref, refs = (refs[:count], refs[count], refs[count + 1 :])
-    out_refs, (ordered, full) = (refs[:owners], refs[owners:])
-    slots, heights = (matrix_ref.shape[0], matrix_ref.shape[1])
+    block_refs, part_refs, refs = (refs[:count], refs[count : count + 2], refs[count + 2 :])
+    out_refs, (matrices, arrived, ordered, full) = (refs[:owners], refs[owners:])
+    slots, heights = part_refs[0].shape[:2]
+    copies = [
+        [
+            pltpu.make_async_copy(part_ref.at[s], matrices.at[i, s], arrived.at[i, s])
+            for i, part_ref in enumerate(part_refs)
+        ]
+        for s in range(slots)
+    ]
+    for pair in copies:
+        for copy in pair:
+            copy.start()
     own_kx, own_ht = (lax.axis_index("kx"), lax.axis_index("ht"))
     partners = []
     for position in range(owners):
@@ -546,7 +576,9 @@
         if spare:
             fields = jnp.concatenate([fields, jnp.zeros((spare, heights), jnp.float32)], axis=0)
         top, rest = two_parts(fields)
-        matrix_top, matrix_rest = two_parts(matrix_ref[s])
+        for copy in copies[s]:
+            copy.wait()
+        matrix_top, matrix_rest = (matrices[0, s], matrices[1, s])
         last = ((1,), (1,))
         both = dot(matrix_top, jnp.concatenate([top, rest], axis=0), last)
         solved = both[:, : count + spare] + both[:, count + spare :] + dot(matrix_rest, top, last)
@@ -558,25 +590,27 @@
                 out_ref[s, tile] = full[s % 2, ht * lane_tiles + tile, band]
 
 
-def solve(first, blocks, helmholtz, pieces, groups, kx_count, ht_count):
+def solve(first, blocks, parts, pieces, groups, kx_count, ht_count):
     owners, slots, per_slot, lanes = first.shape
-    heights, count = (helmholtz.shape[1], per_slot * groups)
+    heights, count = (parts[0].shape[1], per_slot * groups)
     shape = (slots, heights // ht_count // LANES, count // kx_count, LANES)
     return pl.pallas_call(
         functools.partial(
             solve_kernel, groups=groups, kx_count=kx_count, ht_count=ht_count, pieces=pieces
         ),
         out_shape=(jax.ShapeDtypeStruct(shape, jnp.float32),) * owners,
-        in_specs=[VMEM] * (2 + len(blocks)),
+        in_specs=[VMEM] * (1 + len(blocks)) + [pl.BlockSpec(memory_space=pl.ANY)] * 2,
         out_specs=(VMEM,) * owners,
         scratch_shapes=[
+            pltpu.VMEM((2,) + parts[0].shape, jnp.bfloat16),
+            pltpu.SemaphoreType.DMA((2, slots)),
             pltpu.VMEM((max(pieces - 1, 1),) + first.shape, jnp.float32),
             pltpu.VMEM((2, heights // LANES, count, LANES), jnp.float32),
         ],
         compiler_params=params(),
-        cost_estimate=cost(4 * helmholtz.size),
+        cost_estimate=cost(4 * parts[0].size),
         name="solve",
-    )(first, *blocks, helmholtz)
+    )(first, *blocks, *parts)
 
 
 def restore_kernel(*refs, owners, ht_count):
@@ -705,7 +739,7 @@
         else:
             block = blocks[0].reshape(owners, slots, -1, LANES)
             first = lax.all_to_all(block, ("kx", "ht"), split_axis=0, concat_axis=0, tiled=True)
-    solved = solve(first, received, helmholtz, pieces, groups, kx_count, ht_count)
+    solved = solve(first, received, split_matrix(helmholtz), pieces, groups, kx_count, ht_count)
     returned = [block.reshape(-1, LANES) for block in exchange(solved, ("kx", "ht"))]
     result = restore(returned, order, components, band_modes, rows_ht, ht_count)
     return result.reshape(velocity.shape)

time: 132 us -> 132 us (level)
  waiting for transfers between devices: 52.3 us -> 39.7 us
  Pallas kernels: 29.2 us -> 36.8 us
  starting transfers between devices: 47.2 us -> 50.6 us
  local copies, waits for them, and re-layouts: 1.56 us -> 3.59 us
    ppermute x17, waiting for transfers between devices: 41.9 us -> 29.3 us  [exchange(): result[position] = lax.ppermute(blocks[position], axes + ('real',), pairs)]
    pallas_call x0 -> x1, Pallas kernels: none -> 7.92 us  [split_matrix(): pl.pallas_call(split_kernel, out_shape=(shape, shape), grid=(slots,), in_...]
    ppermute x17, starting transfers between devices: 26.4 us -> 29.8 us  [exchange(): result[position] = lax.ppermute(blocks[position], axes + ('real',), pairs)]
    unnamed x14 -> x16, local copies, waits for them, and re-layouts: 0.7 us -> 2.74 us
  transfers between devices with their start and end apart: 25 -> 25, of which waited for: 13 -> 12; matrix products, arithmetic and copies ran while one was open for 1% -> 1% of each run, Pallas kernels for 14% -> 20%
where the time goes in v13:
time: 132 us; the launch traced here: 131 us
  starting transfers between devices  50.6 us (38%)
  waiting for transfers between devices  39.7 us (30%)
  Pallas kernels  36.8 us (28%)
  local copies, waits for them, and re-layouts  3.59 us (3%)
    ppermute x17, starting transfers between devices, exchange(): result[position] = lax.ppermute(blocks[position], axes + ('real',), pairs)  29.8 us
    ppermute x17, waiting for transfers between devices, exchange(): result[position] = lax.ppermute(blocks[position], axes + ('real',), pairs)  29.3 us
    ppermute x6, waiting for transfers between devices, swap(): return lax.ppermute(value, 'real', pairs)  10.4 us
    all_to_all x1, starting transfers between devices, local(): block = lax.all_to_all(block, 'kx', split_axis=0, concat_axis=0, tiled=True)  9.53 us
    pallas_call x1, Pallas kernels, split_matrix(): pl.pallas_call(split_kernel, out_shape=(shape, shape), grid=(slots,), in_...  7.92 us
    all_to_all x1, starting transfers between devices, local(): lax.all_to_all(block, ('kx', 'ht'), split_axis=0, concat_axis=0, tiled=True)  7.83 us
    pallas_call x2, Pallas kernels, stress_terms(): pl.pallas_call(stress_kernel, out_shape=(jax.ShapeDtypeStruct(shape, jnp....  6.94 us
    pallas_call x2, Pallas kernels, high_terms(): pl.pallas_call(products_kernel, out_shape=jax.ShapeDtypeStruct((component...  6.01 us
  transfers between devices with their start and end apart: 25, of which 12 were waited for; matrix products, arithmetic and copies ran while one was open for 1% of the time, Pallas kernels for 20%

profile of v13, /device:TPU:0, one launch (start us, length us, event | category | flops | bytes accessed | tf_op | source)
XLA Modules:
  0.0 131.1 jit_solution(7703523165609624341)
XLA Ops:
  0.0 2.1 %pack_first.1 = (f32[392,128]{1,0:T(8,128)}, f32[392,128]{1,0:T(8,128)}, f32[392,128]{1,0:T(8,128)}, f32[392,128]{1,0:T(8,128)}) custom-call(s32[4,8]{1,0:T(4,128)} %near_ref.1, s32[4]{0:T(128)} %count_ref.1, f32[12,2,4,32,128]{4,3,2,1,0:T(8,128)} %bitcast.46), custom_call_target="tpu_custom_call" | custom-call | bytes 1572864 | tf_op jit(solution)/shard_map/pack_first/pallas_call | solution.py:175
  2.1 3.0 %collective-permute-start = (f32[392,128]{1,0:T(8,128)}, f32[392,128]{1,0:T(8,128)S(1)}, u32[]{:S(2)}, u32[]{:S(2)}) collective-permute-start(f32[392,128]{1,0:T(8,128)} %get-tuple-element.40), channel_id=1, source_target_pairs={{0,8},{1,25},{2,10},{3,27},{8,0},{9,17},{10,2},{11,19},{16,24},{17... | collective-permute-start | bytes 602120 | tf_op jit(solution)/shard_map/ppermute | solution.py:663
  5.1 2.5 %collective-permute-start.1 = (f32[392,128]{1,0:T(8,128)}, f32[392,128]{1,0:T(8,128)S(1)}, u32[]{:S(2)}, u32[]{:S(2)}) collective-permute-start(f32[392,128]{1,0:T(8,128)} %get-tuple-element.41), channel_id=1, source_target_pairs={{0,24},{1,9},{2,26},{3,11},{8,16},{9,1},{10,18},{11,3},{16,8},{17,... | collective-permute-start | bytes 602120 | tf_op jit(solution)/shard_map/ppermute | solution.py:663
  7.6 0.1 collective-permute-start.2
  7.7 0.0 copy-start.6
  7.7 4.2 %collective-permute-done.refs_1_._ = f32[392,128]{1,0:T(8,128)S(1)} collective-permute-done((f32[392,128]{1,0:T(8,128)}, f32[392,128]{1,0:T(8,128)S(1)}, u32[]{:S(2)}, u32[]{:S(2)}) %collective-permute-start) | collective-permute-done | bytes 200736 | tf_op jit(solution)/shard_map/ppermute | solution.py:663
  11.9 0.7 copy-done.1
  12.6 2.1 %pack.1 = f32[4,384,128]{2,1,0:T(8,128)} custom-call(f32[12,2,4,32,128]{4,3,2,1,0:T(8,128)} %bitcast.47, f32[392,128]{1,0:T(8,128)} %copy-done.1), custom_call_target="tpu_custom_call" | custom-call | bytes 1572864 | tf_op jit(solution)/shard_map/pack/pallas_call | solution.py:201
  14.7 9.5 %all-to-all-start.1 = ((f32[4,384,128]{2,1,0:T(8,128)}), f32[4,384,128]{2,1,0:T(8,128)S(1)}, u32[]{:S(2)}, u32[]{:S(2)}) async-start(f32[4,384,128]{2,1,0:T(8,128)} %pack.1), calls=%async_computation.1 | async-start | bytes 1572864 | tf_op jit(solution)/shard_map/all_to_all | solution.py:711
  24.2 0.1 broadcast_in_dim.85
  24.3 0.1 broadcast_in_dim.86
  24.4 0.1 broadcast_in_dim.91
  24.5 0.1 broadcast_in_dim.92
  24.6 0.1 broadcast_in_dim.96
  24.6 0.1 broadcast_in_dim.97
  24.7 0.1 broadcast_in_dim.101
  24.8 0.1 broadcast_in_dim.102
  24.9 0.8 tables.1
  25.7 0.0 collective-permute-done.1.refs_2_
  25.7 1.5 %collective-permute-done.2.refs_3_ = f32[392,128]{1,0:T(8,128)S(1)} collective-permute-done((f32[392,128]{1,0:T(8,128)}, f32[392,128]{1,0:T(8,128)S(1)}, u32[]{:S(2)}, u32[]{:S(2)}) %collective-permute-start.2) | collective-permute-done | bytes 200736 | tf_op jit(solution)/shard_map/ppermute | solution.py:663
  27.3 0.1 add_convert_fusion
  27.4 3.5 %stress.2 = (f32[3,16,32,128]{3,2,1,0:T(8,128)S(1)}, f32[3,16,32,256]{3,2,1,0:T(8,128)S(1)}, f32[3,4,32,128]{3,2,1,0:T(8,128)S(1)}, f32[3,4,32,128]{3,2,1,0:T(8,128)S(1)}) custom-call(s32[8]{0:T(128)S(1)} %copy-done.6, s32[16,8]{1,0:T(8,128)S(1)} %bitcast.26, f32[392,128]{1,0:T(8,128)S(1)} %copy-done.4, f32[392,128]{1,0:T(8,128)S(1)} %copy-done.2, ...), custom_call_target="tpu_custom_call" | custom-call | bytes 12582912 | tf_op jit(solution)/shard_map/stress/pallas_call | solution.py:353
  30.9 0.1 collective-permute-start.3
  31.0 1.4 %collective-permute-done.3 = f32[3,4,32,128]{3,2,1,0:T(8,128)S(1)} collective-permute-done((f32[3,4,32,128]{3,2,1,0:T(8,128)S(1)}, f32[3,4,32,128]{3,2,1,0:T(8,128)S(1)}, u32[]{:S(2)}, u32[]{:S(2)}) %collective-permute-start.3) | collective-permute-done | bytes 196640 | tf_op jit(solution)/shard_map/ppermute | solution.py:685
  32.4 1.6 %collective-permute-start.4 = (f32[3,4,32,128]{3,2,1,0:T(8,128)S(1)}, f32[3,4,32,128]{3,2,1,0:T(8,128)S(1)}, u32[]{:S(2)}, u32[]{:S(2)}) collective-permute-start(f32[3,4,32,128]{3,2,1,0:T(8,128)S(1)} %add.21.first_ref.refs_4_), channel_id=1, source_target_pairs={{0,2},{1,3},{2,0},{3,1},{4,6},{5,7},{6,4},{7,5},{8,10},{9,11},{10,... | collective-permute-start | bytes 589832 | tf_op jit(solution)/shard_map/ppermute | solution.py:685
  34.0 0.2 slice_reduce_fusion.count_ref
  34.2 3.0 %products.2._.forcing_ref = f32[3,8,32,128]{3,2,1,0:T(8,128)S(1)} custom-call(s32[8]{0:T(128)S(1)} %copy-done.6, s32[16,8]{1,0:T(8,128)S(1)} %bitcast.27, s32[16]{0:T(128)S(1)} %slice_reduce_fusion.count_ref, f32[3,16,32,256]{3,2,1,0:T(8,128)S(1)} %get-tuple-element.47.physical, bf16[256,256]{1,0:T(8,128)(2,1)S(1)} %get-tuple-element.44.refs_6_.back_ref.refs_3_, ...), custom_call_target="tpu_custom_call" | custom-call | bytes 12582912 | tf_op jit(solution)/shard_map/products/pallas_call | solution.py:418
  37.2 2.3 %collective-permute-done.4.second_ref = f32[3,4,32,128]{3,2,1,0:T(8,128)S(1)} collective-permute-done((f32[3,4,32,128]{3,2,1,0:T(8,128)S(1)}, f32[3,4,32,128]{3,2,1,0:T(8,128)S(1)}, u32[]{:S(2)}, u32[]{:S(2)}) %collective-permute-start.4) | collective-permute-done | bytes 196640 | tf_op jit(solution)/shard_map/ppermute | solution.py:685
  39.5 0.1 collective-permute-start.5
  39.5 1.4 %collective-permute-done.5.other_ref = f32[3,4,32,128]{3,2,1,0:T(8,128)S(1)} collective-permute-done((f32[3,4,32,128]{3,2,1,0:T(8,128)S(1)}, f32[3,4,32,128]{3,2,1,0:T(8,128)S(1)}, u32[]{:S(2)}, u32[]{:S(2)}) %collective-permute-start.5) | collective-permute-done | bytes 196640 | tf_op jit(solution)/shard_map/ppermute | solution.py:685
  41.0 1.9 %outgoing.2 = f32[1536,128]{1,0:T(8,128)} custom-call(s32[8]{0:T(128)S(1)} %copy-done.6, s32[16]{0:T(128)S(1)} %slice_reduce_fusion.count_ref, f32[3,16,32,128]{3,2,1,0:T(8,128)S(1)} %get-tuple-element.46.slotted_ref, f32[3,8,32,128]{3,2,1,0:T(8,128)S(1)} %products.2._.forcing_ref, f32[3,4,32,128]{3,2,1,0:T(8,128)S(1)} %ordered_sum.2.kept_ref, ...), custom_call_target="tpu_custom_call" | custom-call | bytes 1572864 | tf_op jit(solution)/shard_map/outgoing/pallas_call | solution.py:484
  42.9 7.8 %all-to-all-start = ((f32[8,8,24,128]{3,2,1,0:T(8,128)}), f32[8,8,24,128]{3,2,1,0:T(8,128)S(1)}, u32[]{:S(2)}, u32[]{:S(2)}) async-start(f32[8,8,24,128]{3,2,1,0:T(8,128)} %bitcast.5), calls=%async_computation | async-start | bytes 1572864 | tf_op jit(solution)/shard_map/all_to_all | solution.py:741
  50.7 3.5 %stress.3 = (f32[3,16,32,128]{3,2,1,0:T(8,128)S(1)}, f32[3,16,32,256]{3,2,1,0:T(8,128)S(1)}, f32[3,4,32,128]{3,2,1,0:T(8,128)S(1)}, f32[3,4,32,128]{3,2,1,0:T(8,128)S(1)}) custom-call(s32[8]{0:T(128)S(1)} %copy-done.6, s32[16,8]{1,0:T(8,128)S(1)} %bitcast.28, f32[4,384,128]{2,1,0:T(8,128)S(1)} %all-to-all-done.1.refs_0_, ...), custom_call_target="tpu_custom_call" | custom-call | bytes 12582912 | tf_op jit(solution)/shard_map/stress/pallas_call | solution.py:353
  54.2 0.1 collective-permute-start.6
  54.2 1.4 %collective-permute-done.6 = f32[3,4,32,128]{3,2,1,0:T(8,128)S(1)} collective-permute-done((f32[3,4,32,128]{3,2,1,0:T(8,128)S(1)}, f32[3,4,32,128]{3,2,1,0:T(8,128)S(1)}, u32[]{:S(2)}, u32[]{:S(2)}) %collective-permute-start.6) | collective-permute-done | bytes 196640 | tf_op jit(solution)/shard_map/ppermute | solution.py:685
  55.7 1.6 %collective-permute-start.7 = (f32[3,4,32,128]{3,2,1,0:T(8,128)S(1)}, f32[3,4,32,128]{3,2,1,0:T(8,128)S(1)}, u32[]{:S(2)}, u32[]{:S(2)}) collective-permute-start(f32[3,4,32,128]{3,2,1,0:T(8,128)S(1)} %add.22.first_ref), channel_id=1, source_target_pairs={{0,2},{1,3},{2,0},{3,1},{4,6},{5,7},{6,4},{7,5},{8,10},{9,11},{10,... | collective-permute-start | bytes 589832 | tf_op jit(solution)/shard_map/ppermute | solution.py:685
  57.3 3.0 %products.3._.forcing_ref = f32[3,8,32,128]{3,2,1,0:T(8,128)S(1)} custom-call(s32[8]{0:T(128)S(1)} %copy-done.6, s32[16,8]{1,0:T(8,128)S(1)} %bitcast.29, s32[16]{0:T(128)S(1)} %slice_reduce_fusion.count_ref, f32[3,16,32,256]{3,2,1,0:T(8,128)S(1)} %get-tuple-element.51.physical, bf16[256,256]{1,0:T(8,128)(2,1)S(1)} %get-tuple-element.44.refs_6_.back_ref.refs_3_, ...), custom_call_target="tpu_custom_call" | custom-call | bytes 12582912 | tf_op jit(solution)/shard_map/products/pallas_call | solution.py:418
  60.3 2.4 %collective-permute-done.7.second_ref = f32[3,4,32,128]{3,2,1,0:T(8,128)S(1)} collective-permute-done((f32[3,4,32,128]{3,2,1,0:T(8,128)S(1)}, f32[3,4,32,128]{3,2,1,0:T(8,128)S(1)}, u32[]{:S(2)}, u32[]{:S(2)}) %collective-permute-start.7) | collective-permute-done | bytes 196640 | tf_op jit(solution)/shard_map/ppermute | solution.py:685
  62.8 0.1 collective-permute-start.8
  62.8 1.4 %collective-permute-done.8.other_ref = f32[3,4,32,128]{3,2,1,0:T(8,128)S(1)} collective-permute-done((f32[3,4,32,128]{3,2,1,0:T(8,128)S(1)}, f32[3,4,32,128]{3,2,1,0:T(8,128)S(1)}, u32[]{:S(2)}, u32[]{:S(2)}) %collective-permute-start.8) | collective-permute-done | bytes 196640 | tf_op jit(solution)/shard_map/ppermute | solution.py:685
  64.3 1.2 outgoing.3
  65.4 3.0 %collective-permute-start.9 = (f32[8,24,128]{2,1,0:T(8,128)S(1)}, f32[8,24,128]{2,1,0:T(8,128)S(1)}, u32[]{:S(2)}, u32[]{:S(2)}) collective-permute-start(f32[8,24,128]{2,1,0:T(8,128)S(1)} %bitcast.45), channel_id=1, source_target_pairs={{0,16},{1,5},{2,18},{3,7},{4,20},{5,1},{6,22},{7,3},{8,24},{9,13},... | collective-permute-start | bytes 294920 | tf_op jit(solution)/shard_map/ppermute | solution.py:663
  68.4 1.5 %collective-permute-start.10 = (f32[8,24,128]{2,1,0:T(8,128)S(1)}, f32[8,24,128]{2,1,0:T(8,128)S(1)}, u32[]{:S(2)}, u32[]{:S(2)}) collective-permute-start(f32[8,24,128]{2,1,0:T(8,128)S(1)} %bitcast.44), channel_id=1, source_target_pairs={{0,4},{1,17},{2,6},{3,19},{4,0},{5,21},{6,2},{7,23},{8,12},{9,25},... | collective-permute-start | bytes 294920 | tf_op jit(solution)/shard_map/ppermute | solution.py:663
  69.9 1.5 %collective-permute-start.11 = (f32[8,24,128]{2,1,0:T(8,128)S(1)}, f32[8,24,128]{2,1,0:T(8,128)S(1)}, u32[]{:S(2)}, u32[]{:S(2)}) collective-permute-start(f32[8,24,128]{2,1,0:T(8,128)S(1)} %bitcast.43), channel_id=1, source_target_pairs={{0,8},{1,25},{2,10},{3,27},{4,12},{5,29},{6,14},{7,31},{8,0},{9,17... | collective-permute-start | bytes 294920 | tf_op jit(solution)/shard_map/ppermute | solution.py:663
  71.4 0.6 collective-permute-start.12
  71.9 1.5 %collective-permute-start.13 = (f32[8,24,128]{2,1,0:T(8,128)S(1)}, f32[8,24,128]{2,1,0:T(8,128)S(1)}, u32[]{:S(2)}, u32[]{:S(2)}) collective-permute-start(f32[8,24,128]{2,1,0:T(8,128)S(1)} %bitcast.41), channel_id=1, source_target_pairs={{0,20},{1,13},{2,22},{3,15},{4,16},{5,9},{6,18},{7,11},{8,28},{9,5... | collective-permute-start | bytes 294920 | tf_op jit(solution)/shard_map/ppermute | solution.py:663
  73.4 3.3 %collective-permute-done.9.refs_2_ = f32[8,24,128]{2,1,0:T(8,128)S(1)} collective-permute-done((f32[8,24,128]{2,1,0:T(8,128)S(1)}, f32[8,24,128]{2,1,0:T(8,128)S(1)}, u32[]{:S(2)}, u32[]{:S(2)}) %collective-permute-start.9) | collective-permute-done | bytes 98336 | tf_op jit(solution)/shard_map/ppermute | solution.py:663
  76.7 0.4 collective-permute-start.14
  77.1 0.0 collective-permute-done.10.refs_3_
  77.1 3.1 %collective-permute-start.15 = (f32[8,24,128]{2,1,0:T(8,128)S(1)}, f32[8,24,128]{2,1,0:T(8,128)S(1)}, u32[]{:S(2)}, u32[]{:S(2)}) collective-permute-start(f32[8,24,128]{2,1,0:T(8,128)S(1)} %bitcast.39), channel_id=1, source_target_pairs={{0,28},{1,29},{2,30},{3,31},{4,24},{5,25},{6,26},{7,27},{8,20},{9,... | collective-permute-start | bytes 294920 | tf_op jit(solution)/shard_map/ppermute | solution.py:663
  80.2 7.9 %split_matrix.1 = (bf16[8,512,512]{2,1,0:T(8,128)(2,1)S(1)}, bf16[8,512,512]{2,1,0:T(8,128)(2,1)}) custom-call(f32[8,512,512]{2,1,0:T(8,128)} %matrix_ref.1), custom_call_target="tpu_custom_call" | custom-call | bytes 16777216 | tf_op jit(solution)/shard_map/split_matrix/pallas_call | solution.py:527
  88.1 2.0 %copy-done = bf16[8,512,512]{2,1,0:T(8,128)(2,1)} copy-done((bf16[8,512,512]{2,1,0:T(8,128)(2,1)}, bf16[8,512,512]{2,1,0:T(8,128)(2,1)S(1)}, u32[]{:S(2)}) %copy-start) | copy-done | bytes 4194328
  90.1 0.0 collective-permute-done.14.refs_7_
  90.2 5.8 %solve.1 = (f32[8,2,24,128]{3,2,1,0:T(8,128)S(1)}, f32[8,2,24,128]{3,2,1,0:T(8,128)S(1)}, f32[8,2,24,128]{3,2,1,0:T(8,128)S(1)}, f32[8,2,24,128]{3,2,1,0:T(8,128...) custom-call(f32[8,8,24,128]{3,2,1,0:T(8,128)S(1)} %all-to-all-done.r, ...), custom_call_target="tpu_custom_call" | custom-call | bytes 8388608 | tf_op jit(solution)/shard_map/solve/pallas_call | solution.py:597
  96.0 1.0 collective-permute-start.16
  97.0 5.4 %collective-permute-start.17 = (f32[8,2,24,128]{3,2,1,0:T(8,128)S(1)}, f32[8,2,24,128]{3,2,1,0:T(8,128)S(1)}, u32[]{:S(2)}, u32[]{:S(2)}) collective-permute-start(f32[8,2,24,128]{3,2,1,0:T(8,128)S(1)} %get-tuple-element.66), channel_id=1, source_target_pairs={{0,4},{1,17},{2,6},{3,19},{4,0},{5,21},{6,2},{7,23},{8,12},{9,25},... | collective-permute-start | bytes 589832 | tf_op jit(solution)/shard_map/ppermute | solution.py:663
  102.4 1.5 %collective-permute-start.19 = (f32[8,2,24,128]{3,2,1,0:T(8,128)S(1)}, f32[8,2,24,128]{3,2,1,0:T(8,128)S(1)}, u32[]{:S(2)}, u32[]{:S(2)}) collective-permute-start(f32[8,2,24,128]{3,2,1,0:T(8,128)S(1)} %get-tuple-element.68), channel_id=1, source_target_pairs={{0,24},{1,9},{2,26},{3,11},{4,28},{5,13},{6,30},{7,15},{8,16},{9,1... | collective-permute-start | bytes 589832 | tf_op jit(solution)/shard_map/ppermute | solution.py:663
  103.9 1.4 %collective-permute-start.20 = (f32[8,2,24,128]{3,2,1,0:T(8,128)S(1)}, f32[8,2,24,128]{3,2,1,0:T(8,128)S(1)}, u32[]{:S(2)}, u32[]{:S(2)}) collective-permute-start(f32[8,2,24,128]{3,2,1,0:T(8,128)S(1)} %get-tuple-element.69), channel_id=1, source_target_pairs={{0,20},{1,13},{2,22},{3,15},{4,16},{5,9},{6,18},{7,11},{8,28},{9,5... | collective-permute-start | bytes 589832 | tf_op jit(solution)/shard_map/ppermute | solution.py:663
  105.3 3.7 %collective-permute-done.16 = f32[8,2,24,128]{3,2,1,0:T(8,128)S(1)} collective-permute-done((f32[8,2,24,128]{3,2,1,0:T(8,128)S(1)}, f32[8,2,24,128]{3,2,1,0:T(8,128)S(1)}, u32[]{:S(2)}, u32[]{:S(2)}) %collective-permute-start.16) | collective-permute-done | bytes 196640 | tf_op jit(solution)/shard_map/ppermute | solution.py:663
  109.0 0.7 collective-permute-start.21
  109.7 2.8 %collective-permute-start.22 = (f32[8,2,24,128]{3,2,1,0:T(8,128)S(1)}, f32[8,2,24,128]{3,2,1,0:T(8,128)S(1)}, u32[]{:S(2)}, u32[]{:S(2)}) collective-permute-start(f32[8,2,24,128]{3,2,1,0:T(8,128)S(1)} %get-tuple-element.71), channel_id=1, source_target_pairs={{0,28},{1,29},{2,30},{3,31},{4,24},{5,25},{6,26},{7,27},{8,20},{9,... | collective-permute-start | bytes 589832 | tf_op jit(solution)/shard_map/ppermute | solution.py:663
  112.5 3.7 %collective-permute-done.19 = f32[8,2,24,128]{3,2,1,0:T(8,128)S(1)} collective-permute-done((f32[8,2,24,128]{3,2,1,0:T(8,128)S(1)}, f32[8,2,24,128]{3,2,1,0:T(8,128)S(1)}, u32[]{:S(2)}, u32[]{:S(2)}) %collective-permute-start.19) | collective-permute-done | bytes 196640 | tf_op jit(solution)/shard_map/ppermute | solution.py:663
  116.2 12.8 %collective-permute-done.20 = f32[8,2,24,128]{3,2,1,0:T(8,128)S(1)} collective-permute-done((f32[8,2,24,128]{3,2,1,0:T(8,128)S(1)}, f32[8,2,24,128]{3,2,1,0:T(8,128)S(1)}, u32[]{:S(2)}, u32[]{:S(2)}) %collective-permute-start.20) | collective-permute-done | bytes 196640 | tf_op jit(solution)/shard_map/ppermute | solution.py:663
  129.1 2.1 %restore.1 = f32[3,4,256,128]{3,2,1,0:T(8,128)} custom-call(f32[384,128]{1,0:T(8,128)S(1)} %bitcast.30, f32[384,128]{1,0:T(8,128)S(1)} %bitcast.31, f32[384,128]{1,0:T(8,128)S(1)} %bitcast.32, f32[384,128]{1,0:T(8,128)S(1)} %bitcast.33, f32[384,128]{1,0:T(8,128)S(1)} %bitcast.34, f32[384,128]{1,0:T(8,128)S(1)} %bitcast.35, f32[384,128]{1,0:T(8,128)S(1)} %bitcast.36, ...), custom_call_target="tpu_custom_call" | custom-call | bytes 3145728 | tf_op jit(solution)/shard_map/restore/pallas_call | solution.py:641
  (40 shorter events, 0.2 us)
Async XLA Ops:
  2.1 9.8 %collective-permute-start = (f32[392,128]{1,0:T(8,128)}, f32[392,128]{1,0:T(8,128)S(1)}, u32[]{:S(2)}, u32[]{:S(2)}) collective-permute-start(f32[392,128]{1,0:T(8,128)} %get-tuple-element.40), channel_id=1, source_target_pairs={{0,8},{1,25},{2,10},{3,27},{8,0},{9,17},{10,2},{11,19},{16,24},{17... | collective-permute-start | bytes 602120 | tf_op jit(solution)/shard_map/ppermute | solution.py:663
  5.1 20.6 %collective-permute-start.1 = (f32[392,128]{1,0:T(8,128)}, f32[392,128]{1,0:T(8,128)S(1)}, u32[]{:S(2)}, u32[]{:S(2)}) collective-permute-start(f32[392,128]{1,0:T(8,128)} %get-tuple-element.41), channel_id=1, source_target_pairs={{0,24},{1,9},{2,26},{3,11},{8,16},{9,1},{10,18},{11,3},{16,8},{17,... | collective-permute-start | bytes 602120 | tf_op jit(solution)/shard_map/ppermute | solution.py:663
  7.6 19.7 %collective-permute-start.2 = (f32[392,128]{1,0:T(8,128)}, f32[392,128]{1,0:T(8,128)S(1)}, u32[]{:S(2)}, u32[]{:S(2)}) collective-permute-start(f32[392,128]{1,0:T(8,128)} %get-tuple-element.42), channel_id=1, source_target_pairs={{0,16},{1,17},{2,18},{3,19},{8,24},{9,25},{10,26},{11,27},{16,0},{... | collective-permute-start | bytes 602120 | tf_op jit(solution)/shard_map/ppermute | solution.py:663
  7.7 17.2 %copy-start.4 = (f32[392,128]{1,0:T(8,128)S(1)}, f32[392,128]{1,0:T(8,128)}, u32[]{:S(2)}) copy-start(f32[392,128]{1,0:T(8,128)} %get-tuple-element.39.refs_0_) | copy-start | bytes 602116
  7.7 17.2 %copy-start.3 = (bf16[128,256]{1,0:T(8,128)(2,1)S(1)}, bf16[128,256]{1,0:T(8,128)(2,1)}, u32[]{:S(2)}) copy-start(bf16[128,256]{1,0:T(8,128)(2,1)} %constant.22.clone.rest_ref.refs_5_.refs_2_) | copy-start | bytes 196612
  7.7 17.2 %copy-start.5 = (bf16[128,256]{1,0:T(8,128)(2,1)S(1)}, bf16[128,256]{1,0:T(8,128)(2,1)}, u32[]{:S(2)}) copy-start(bf16[128,256]{1,0:T(8,128)(2,1)} %constant.21.clone.top_ref) | copy-start | bytes 196612
  7.7 17.2 %copy-start.7 = (s32[64]{0:T(128)S(1)}, s32[64]{0:T(128)}, u32[]{:S(2)}) copy-start(s32[64]{0:T(128)} %owner_ref.1) | copy-start | bytes 772
  7.7 19.7 %copy-start.6 = (s32[8]{0:T(128)S(1)}, s32[8]{0:T(128)}, u32[]{:S(2)}) copy-start(s32[8]{0:T(128)} %low_ref.11) | copy-start | bytes 100
  11.9 0.7 copy-start.1
  14.7 11.0 %copy-start.2 = (f32[392,128]{1,0:T(8,128)S(1)}, f32[392,128]{1,0:T(8,128)}, u32[]{:S(2)}) copy-start(f32[392,128]{1,0:T(8,128)} %copy-done.1) | copy-start | bytes 602116
  14.7 28.2 %all-to-all-start.1 = ((f32[4,384,128]{2,1,0:T(8,128)}), f32[4,384,128]{2,1,0:T(8,128)S(1)}, u32[]{:S(2)}, u32[]{:S(2)}) async-start(f32[4,384,128]{2,1,0:T(8,128)} %pack.1), calls=%async_computation.1 | async-start | bytes 1572864 | tf_op jit(solution)/shard_map/all_to_all | solution.py:711
  30.9 1.5 %collective-permute-start.3 = (f32[3,4,32,128]{3,2,1,0:T(8,128)S(1)}, f32[3,4,32,128]{3,2,1,0:T(8,128)S(1)}, u32[]{:S(2)}, u32[]{:S(2)}) collective-permute-start(f32[3,4,32,128]{3,2,1,0:T(8,128)S(1)} %get-tuple-element.49), channel_id=1, source_target_pairs={{0,1},{1,0},{2,3},{3,2},{4,5},{5,4},{6,7},{7,6},{8,9},{9,8},{10,11... | collective-permute-start | bytes 589832 | tf_op jit(solution)/shard_map/ppermute | solution.py:685
  32.4 7.0 %collective-permute-start.4 = (f32[3,4,32,128]{3,2,1,0:T(8,128)S(1)}, f32[3,4,32,128]{3,2,1,0:T(8,128)S(1)}, u32[]{:S(2)}, u32[]{:S(2)}) collective-permute-start(f32[3,4,32,128]{3,2,1,0:T(8,128)S(1)} %add.21.first_ref.refs_4_), channel_id=1, source_target_pairs={{0,2},{1,3},{2,0},{3,1},{4,6},{5,7},{6,4},{7,5},{8,10},{9,11},{10,... | collective-permute-start | bytes 589832 | tf_op jit(solution)/shard_map/ppermute | solution.py:685
  39.5 1.5 %collective-permute-start.5 = (f32[3,4,32,128]{3,2,1,0:T(8,128)S(1)}, f32[3,4,32,128]{3,2,1,0:T(8,128)S(1)}, u32[]{:S(2)}, u32[]{:S(2)}) collective-permute-start(f32[3,4,32,128]{3,2,1,0:T(8,128)S(1)} %ordered_sum.2.kept_ref), channel_id=1, source_target_pairs={{0,1},{1,0},{2,3},{3,2},{4,5},{5,4},{6,7},{7,6},{8,9},{9,8},{10,11... | collective-permute-start | bytes 589832 | tf_op jit(solution)/shard_map/ppermute | solution.py:685
  42.9 47.3 %all-to-all-start = ((f32[8,8,24,128]{3,2,1,0:T(8,128)}), f32[8,8,24,128]{3,2,1,0:T(8,128)S(1)}, u32[]{:S(2)}, u32[]{:S(2)}) async-start(f32[8,8,24,128]{3,2,1,0:T(8,128)} %bitcast.5), calls=%async_computation | async-start | bytes 1572864 | tf_op jit(solution)/shard_map/all_to_all | solution.py:741
  54.2 1.5 %collective-permute-start.6 = (f32[3,4,32,128]{3,2,1,0:T(8,128)S(1)}, f32[3,4,32,128]{3,2,1,0:T(8,128)S(1)}, u32[]{:S(2)}, u32[]{:S(2)}) collective-permute-start(f32[3,4,32,128]{3,2,1,0:T(8,128)S(1)} %get-tuple-element.53), channel_id=1, source_target_pairs={{0,1},{1,0},{2,3},{3,2},{4,5},{5,4},{6,7},{7,6},{8,9},{9,8},{10,11... | collective-permute-start | bytes 589832 | tf_op jit(solution)/shard_map/ppermute | solution.py:685
  55.7 7.0 %collective-permute-start.7 = (f32[3,4,32,128]{3,2,1,0:T(8,128)S(1)}, f32[3,4,32,128]{3,2,1,0:T(8,128)S(1)}, u32[]{:S(2)}, u32[]{:S(2)}) collective-permute-start(f32[3,4,32,128]{3,2,1,0:T(8,128)S(1)} %add.22.first_ref), channel_id=1, source_target_pairs={{0,2},{1,3},{2,0},{3,1},{4,6},{5,7},{6,4},{7,5},{8,10},{9,11},{10,... | collective-permute-start | bytes 589832 | tf_op jit(solution)/shard_map/ppermute | solution.py:685
  62.8 1.5 %collective-permute-start.8 = (f32[3,4,32,128]{3,2,1,0:T(8,128)S(1)}, f32[3,4,32,128]{3,2,1,0:T(8,128)S(1)}, u32[]{:S(2)}, u32[]{:S(2)}) collective-permute-start(f32[3,4,32,128]{3,2,1,0:T(8,128)S(1)} %ordered_sum.3.kept_ref), channel_id=1, source_target_pairs={{0,1},{1,0},{2,3},{3,2},{4,5},{5,4},{6,7},{7,6},{8,9},{9,8},{10,11... | collective-permute-start | bytes 589832 | tf_op jit(solution)/shard_map/ppermute | solution.py:685
  65.4 11.2 %collective-permute-start.9 = (f32[8,24,128]{2,1,0:T(8,128)S(1)}, f32[8,24,128]{2,1,0:T(8,128)S(1)}, u32[]{:S(2)}, u32[]{:S(2)}) collective-permute-start(f32[8,24,128]{2,1,0:T(8,128)S(1)} %bitcast.45), channel_id=1, source_target_pairs={{0,16},{1,5},{2,18},{3,7},{4,20},{5,1},{6,22},{7,3},{8,24},{9,13},... | collective-permute-start | bytes 294920 | tf_op jit(solution)/shard_map/ppermute | solution.py:663
  68.4 8.7 %collective-permute-start.10 = (f32[8,24,128]{2,1,0:T(8,128)S(1)}, f32[8,24,128]{2,1,0:T(8,128)S(1)}, u32[]{:S(2)}, u32[]{:S(2)}) collective-permute-start(f32[8,24,128]{2,1,0:T(8,128)S(1)} %bitcast.44), channel_id=1, source_target_pairs={{0,4},{1,17},{2,6},{3,19},{4,0},{5,21},{6,2},{7,23},{8,12},{9,25},... | collective-permute-start | bytes 294920 | tf_op jit(solution)/shard_map/ppermute | solution.py:663
  69.9 20.2 %collective-permute-start.11 = (f32[8,24,128]{2,1,0:T(8,128)S(1)}, f32[8,24,128]{2,1,0:T(8,128)S(1)}, u32[]{:S(2)}, u32[]{:S(2)}) collective-permute-start(f32[8,24,128]{2,1,0:T(8,128)S(1)} %bitcast.43), channel_id=1, source_target_pairs={{0,8},{1,25},{2,10},{3,27},{4,12},{5,29},{6,14},{7,31},{8,0},{9,17... | collective-permute-start | bytes 294920 | tf_op jit(solution)/shard_map/ppermute | solution.py:663
  71.4 18.8 %collective-permute-start.12 = (f32[8,24,128]{2,1,0:T(8,128)S(1)}, f32[8,24,128]{2,1,0:T(8,128)S(1)}, u32[]{:S(2)}, u32[]{:S(2)}) collective-permute-start(f32[8,24,128]{2,1,0:T(8,128)S(1)} %bitcast.42), channel_id=1, source_target_pairs={{0,24},{1,9},{2,26},{3,11},{4,28},{5,13},{6,30},{7,15},{8,16},{9,1... | collective-permute-start | bytes 294920 | tf_op jit(solution)/shard_map/ppermute | solution.py:663
  71.9 18.2 %collective-permute-start.13 = (f32[8,24,128]{2,1,0:T(8,128)S(1)}, f32[8,24,128]{2,1,0:T(8,128)S(1)}, u32[]{:S(2)}, u32[]{:S(2)}) collective-permute-start(f32[8,24,128]{2,1,0:T(8,128)S(1)} %bitcast.41), channel_id=1, source_target_pairs={{0,20},{1,13},{2,22},{3,15},{4,16},{5,9},{6,18},{7,11},{8,28},{9,5... | collective-permute-start | bytes 294920 | tf_op jit(solution)/shard_map/ppermute | solution.py:663
  76.7 13.5 %collective-permute-start.14 = (f32[8,24,128]{2,1,0:T(8,128)S(1)}, f32[8,24,128]{2,1,0:T(8,128)S(1)}, u32[]{:S(2)}, u32[]{:S(2)}) collective-permute-start(f32[8,24,128]{2,1,0:T(8,128)S(1)} %bitcast.40), channel_id=1, source_target_pairs={{0,12},{1,21},{2,14},{3,23},{4,8},{5,17},{6,10},{7,19},{8,4},{9,29... | collective-permute-start | bytes 294920 | tf_op jit(solution)/shard_map/ppermute | solution.py:663
  77.1 13.1 %collective-permute-start.15 = (f32[8,24,128]{2,1,0:T(8,128)S(1)}, f32[8,24,128]{2,1,0:T(8,128)S(1)}, u32[]{:S(2)}, u32[]{:S(2)}) collective-permute-start(f32[8,24,128]{2,1,0:T(8,128)S(1)} %bitcast.39), channel_id=1, source_target_pairs={{0,28},{1,29},{2,30},{3,31},{4,24},{5,25},{6,26},{7,27},{8,20},{9,... | collective-permute-start | bytes 294920 | tf_op jit(solution)/shard_map/ppermute | solution.py:663
  88.1 2.0 %copy-start = (bf16[8,512,512]{2,1,0:T(8,128)(2,1)}, bf16[8,512,512]{2,1,0:T(8,128)(2,1)S(1)}, u32[]{:S(2)}) copy-start(bf16[8,512,512]{2,1,0:T(8,128)(2,1)S(1)} %get-tuple-element.62.refs_9_) | copy-start | bytes 12582916
  96.0 13.0 %collective-permute-start.16 = (f32[8,2,24,128]{3,2,1,0:T(8,128)S(1)}, f32[8,2,24,128]{3,2,1,0:T(8,128)S(1)}, u32[]{:S(2)}, u32[]{:S(2)}) collective-permute-start(f32[8,2,24,128]{3,2,1,0:T(8,128)S(1)} %get-tuple-element.65), channel_id=1, source_target_pairs={{0,16},{1,5},{2,18},{3,7},{4,20},{5,1},{6,22},{7,3},{8,24},{9,13},... | collective-permute-start | bytes 589832 | tf_op jit(solution)/shard_map/ppermute | solution.py:663
  97.0 12.7 %collective-permute-start.17 = (f32[8,2,24,128]{3,2,1,0:T(8,128)S(1)}, f32[8,2,24,128]{3,2,1,0:T(8,128)S(1)}, u32[]{:S(2)}, u32[]{:S(2)}) collective-permute-start(f32[8,2,24,128]{3,2,1,0:T(8,128)S(1)} %get-tuple-element.66), channel_id=1, source_target_pairs={{0,4},{1,17},{2,6},{3,19},{4,0},{5,21},{6,2},{7,23},{8,12},{9,25},... | collective-permute-start | bytes 589832 | tf_op jit(solution)/shard_map/ppermute | solution.py:663
  102.3 10.1 %collective-permute-start.18 = (f32[8,2,24,128]{3,2,1,0:T(8,128)S(1)}, f32[8,2,24,128]{3,2,1,0:T(8,128)S(1)}, u32[]{:S(2)}, u32[]{:S(2)}) collective-permute-start(f32[8,2,24,128]{3,2,1,0:T(8,128)S(1)} %get-tuple-element.67), channel_id=1, source_target_pairs={{0,8},{1,25},{2,10},{3,27},{4,12},{5,29},{6,14},{7,31},{8,0},{9,17... | collective-permute-start | bytes 589832 | tf_op jit(solution)/shard_map/ppermute | solution.py:663
  102.4 13.9 %collective-permute-start.19 = (f32[8,2,24,128]{3,2,1,0:T(8,128)S(1)}, f32[8,2,24,128]{3,2,1,0:T(8,128)S(1)}, u32[]{:S(2)}, u32[]{:S(2)}) collective-permute-start(f32[8,2,24,128]{3,2,1,0:T(8,128)S(1)} %get-tuple-element.68), channel_id=1, source_target_pairs={{0,24},{1,9},{2,26},{3,11},{4,28},{5,13},{6,30},{7,15},{8,16},{9,1... | collective-permute-start | bytes 589832 | tf_op jit(solution)/shard_map/ppermute | solution.py:663
  103.9 25.2 %collective-permute-start.20 = (f32[8,2,24,128]{3,2,1,0:T(8,128)S(1)}, f32[8,2,24,128]{3,2,1,0:T(8,128)S(1)}, u32[]{:S(2)}, u32[]{:S(2)}) collective-permute-start(f32[8,2,24,128]{3,2,1,0:T(8,128)S(1)} %get-tuple-element.69), channel_id=1, source_target_pairs={{0,20},{1,13},{2,22},{3,15},{4,16},{5,9},{6,18},{7,11},{8,28},{9,5... | collective-permute-start | bytes 589832 | tf_op jit(solution)/shard_map/ppermute | solution.py:663
  109.0 20.1 %collective-permute-start.21 = (f32[8,2,24,128]{3,2,1,0:T(8,128)S(1)}, f32[8,2,24,128]{3,2,1,0:T(8,128)S(1)}, u32[]{:S(2)}, u32[]{:S(2)}) collective-permute-start(f32[8,2,24,128]{3,2,1,0:T(8,128)S(1)} %get-tuple-element.70), channel_id=1, source_target_pairs={{0,12},{1,21},{2,14},{3,23},{4,8},{5,17},{6,10},{7,19},{8,4},{9,29... | collective-permute-start | bytes 589832 | tf_op jit(solution)/shard_map/ppermute | solution.py:663
  109.7 19.4 %collective-permute-start.22 = (f32[8,2,24,128]{3,2,1,0:T(8,128)S(1)}, f32[8,2,24,128]{3,2,1,0:T(8,128)S(1)}, u32[]{:S(2)}, u32[]{:S(2)}) collective-permute-start(f32[8,2,24,128]{3,2,1,0:T(8,128)S(1)} %get-tuple-element.71), channel_id=1, source_target_pairs={{0,28},{1,29},{2,30},{3,31},{4,24},{5,25},{6,26},{7,27},{8,20},{9,... | collective-permute-start | bytes 589832 | tf_op jit(solution)/shard_map/ppermute | solution.py:663

commit v14 on v11

--- a/solution.py
+++ b/solution.py
@@ -527,7 +527,8 @@
         pltpu.make_async_copy(matrix_ref.at[s], matrices.at[s], arrived.at[s])
         for s in range(slots)
     ]
-    for copy in copies:
+    ahead = 2
+    for copy in copies[:ahead]:
         copy.start()
     own_kx, own_ht = (lax.axis_index("kx"), lax.axis_index("ht"))
     partners = []
@@ -546,15 +547,21 @@
                 for first in range(0, kx_count, groups):
                     blocks = [source[(first + g) * ht_count + h, s] for g in range(groups)]
                     tiles.append(jnp.concatenate(regroup(blocks, rows), axis=0))
-        top, rest = two_parts(jnp.concatenate(tiles, axis=1))
-        count = top.shape[0]
+        fields = jnp.concatenate(tiles, axis=1)
+        count = fields.shape[0]
+        spare = -count % LANES
+        if spare:
+            fields = jnp.concatenate([fields, jnp.zeros((spare, heights), jnp.float32)], axis=0)
+        top, rest = two_parts(fields)
         copies[s].wait()
+        if s + ahead < slots:
+            copies[s + ahead].start()
         matrix_top, matrix_rest = two_parts(matrices[s])
         last = ((1,), (1,))
         both = dot(matrix_top, jnp.concatenate([top, rest], axis=0), last)
-        solved = both[:, :count] + both[:, count:] + dot(matrix_rest, top, last)
+        solved = both[:, : count + spare] + both[:, count + spare :] + dot(matrix_rest, top, last)
         for tile in range(heights // LANES):
-            full[s % 2, tile] = solved[tile * LANES : (tile + 1) * LANES].T
+            full[s % 2, tile] = solved[tile * LANES : (tile + 1) * LANES].T[:count]
         for out_ref, (kx, ht) in zip(out_refs, partners):
             band = pl.ds(pl.multiple_of(kx * per_band, 8), per_band)
             for tile in range(lane_tiles):

time: 133 us -> 132 us (level)
  no operation moved by 1% of the time
where the time goes in v14:
time: 132 us; the launch traced here: 131 us
  waiting for transfers between devices  52.6 us (40%)
  starting transfers between devices  46.9 us (36%)
  Pallas kernels  29.4 us (22%)
  local copies, waits for them, and re-layouts  1.56 us (1%)
    ppermute x17, waiting for transfers between devices, exchange(): result[position] = lax.ppermute(blocks[position], axes + ('real',), pairs)  42.2 us
    ppermute x17, starting transfers between devices, exchange(): result[position] = lax.ppermute(blocks[position], axes + ('real',), pairs)  26.1 us
    ppermute x6, waiting for transfers between devices, swap(): return lax.ppermute(value, 'real', pairs)  10.4 us
    all_to_all x1, starting transfers between devices, local(): block = lax.all_to_all(block, 'kx', split_axis=0, concat_axis=0, tiled=True)  9.53 us
    all_to_all x1, starting transfers between devices, local(): lax.all_to_all(block, ('kx', 'ht'), split_axis=0, concat_axis=0, tiled=True)  7.83 us
    pallas_call x2, Pallas kernels, stress_terms(): pl.pallas_call(stress_kernel, out_shape=(jax.ShapeDtypeStruct(shape, jnp....  6.94 us
    pallas_call x1, Pallas kernels, solve(): pl.pallas_call(functools.partial(solve_kernel, groups=groups, kx_count=kx...  6.36 us
    pallas_call x2, Pallas kernels, high_terms(): pl.pallas_call(products_kernel, out_shape=jax.ShapeDtypeStruct((component...  6 us
  transfers between devices with their start and end apart: 25, of which 13 were waited for; matrix products, arithmetic and copies ran while one was open for 1% of the time, Pallas kernels for 14%

profile of v14, /device:TPU:0, one launch (start us, length us, event | category | flops | bytes accessed | tf_op | source)
XLA Modules:
  0.0 130.8 jit_solution(736999672084874979)
XLA Ops:
  0.0 2.1 %pack_first.1 = (f32[392,128]{1,0:T(8,128)}, f32[392,128]{1,0:T(8,128)}, f32[392,128]{1,0:T(8,128)}, f32[392,128]{1,0:T(8,128)}) custom-call(s32[4,8]{1,0:T(4,128)} %near_ref.1, s32[4]{0:T(128)} %count_ref.1, f32[12,2,4,32,128]{4,3,2,1,0:T(8,128)} %bitcast.46), custom_call_target="tpu_custom_call" | custom-call | bytes 1572864 | tf_op jit(solution)/shard_map/pack_first/pallas_call | solution.py:175
  2.1 3.0 %collective-permute-start = (f32[392,128]{1,0:T(8,128)}, f32[392,128]{1,0:T(8,128)S(1)}, u32[]{:S(2)}, u32[]{:S(2)}) collective-permute-start(f32[392,128]{1,0:T(8,128)} %get-tuple-element.38), channel_id=1, source_target_pairs={{0,8},{1,25},{2,10},{3,27},{8,0},{9,17},{10,2},{11,19},{16,24},{17... | collective-permute-start | bytes 602120 | tf_op jit(solution)/shard_map/ppermute | solution.py:641
  5.1 2.5 %collective-permute-start.1 = (f32[392,128]{1,0:T(8,128)}, f32[392,128]{1,0:T(8,128)S(1)}, u32[]{:S(2)}, u32[]{:S(2)}) collective-permute-start(f32[392,128]{1,0:T(8,128)} %get-tuple-element.39), channel_id=1, source_target_pairs={{0,24},{1,9},{2,26},{3,11},{8,16},{9,1},{10,18},{11,3},{16,8},{17,... | collective-permute-start | bytes 602120 | tf_op jit(solution)/shard_map/ppermute | solution.py:641
  7.6 0.1 collective-permute-start.2
  7.7 0.0 copy-start.5
  7.7 4.2 %collective-permute-done.refs_1_._ = f32[392,128]{1,0:T(8,128)S(1)} collective-permute-done((f32[392,128]{1,0:T(8,128)}, f32[392,128]{1,0:T(8,128)S(1)}, u32[]{:S(2)}, u32[]{:S(2)}) %collective-permute-start) | collective-permute-done | bytes 200736 | tf_op jit(solution)/shard_map/ppermute | solution.py:641
  11.9 0.7 copy-done
  12.6 2.1 %pack.1 = f32[4,384,128]{2,1,0:T(8,128)} custom-call(f32[12,2,4,32,128]{4,3,2,1,0:T(8,128)} %bitcast.47, f32[392,128]{1,0:T(8,128)} %copy-done), custom_call_target="tpu_custom_call" | custom-call | bytes 1572864 | tf_op jit(solution)/shard_map/pack/pallas_call | solution.py:201
  14.7 9.5 %all-to-all-start.1 = ((f32[4,384,128]{2,1,0:T(8,128)}), f32[4,384,128]{2,1,0:T(8,128)S(1)}, u32[]{:S(2)}, u32[]{:S(2)}) async-start(f32[4,384,128]{2,1,0:T(8,128)} %pack.1), calls=%async_computation.1 | async-start | bytes 1572864 | tf_op jit(solution)/shard_map/all_to_all | solution.py:689
  24.2 0.1 broadcast_in_dim.85
  24.3 0.1 broadcast_in_dim.86
  24.4 0.1 broadcast_in_dim.91
  24.5 0.1 broadcast_in_dim.92
  24.6 0.1 broadcast_in_dim.96
  24.6 0.1 broadcast_in_dim.97
  24.7 0.1 broadcast_in_dim.101
  24.8 0.1 broadcast_in_dim.102
  24.9 0.8 tables.1
  25.7 1.6 %collective-permute-done.2.refs_3_ = f32[392,128]{1,0:T(8,128)S(1)} collective-permute-done((f32[392,128]{1,0:T(8,128)}, f32[392,128]{1,0:T(8,128)S(1)}, u32[]{:S(2)}, u32[]{:S(2)}) %collective-permute-start.2) | collective-permute-done | bytes 200736 | tf_op jit(solution)/shard_map/ppermute | solution.py:641
  27.3 0.1 add_convert_fusion
  27.4 3.5 %stress.2 = (f32[3,16,32,128]{3,2,1,0:T(8,128)S(1)}, f32[3,16,32,256]{3,2,1,0:T(8,128)S(1)}, f32[3,4,32,128]{3,2,1,0:T(8,128)S(1)}, f32[3,4,32,128]{3,2,1,0:T(8,128)S(1)}) custom-call(s32[8]{0:T(128)S(1)} %copy-done.5, s32[16,8]{1,0:T(8,128)S(1)} %bitcast.26, f32[392,128]{1,0:T(8,128)S(1)} %copy-done.3, f32[392,128]{1,0:T(8,128)S(1)} %copy-done.1, ...), custom_call_target="tpu_custom_call" | custom-call | bytes 12582912 | tf_op jit(solution)/shard_map/stress/pallas_call | solution.py:353
  30.9 0.1 collective-permute-start.3
  31.0 1.4 %collective-permute-done.3 = f32[3,4,32,128]{3,2,1,0:T(8,128)S(1)} collective-permute-done((f32[3,4,32,128]{3,2,1,0:T(8,128)S(1)}, f32[3,4,32,128]{3,2,1,0:T(8,128)S(1)}, u32[]{:S(2)}, u32[]{:S(2)}) %collective-permute-start.3) | collective-permute-done | bytes 196640 | tf_op jit(solution)/shard_map/ppermute | solution.py:663
  32.4 1.6 %collective-permute-start.4 = (f32[3,4,32,128]{3,2,1,0:T(8,128)S(1)}, f32[3,4,32,128]{3,2,1,0:T(8,128)S(1)}, u32[]{:S(2)}, u32[]{:S(2)}) collective-permute-start(f32[3,4,32,128]{3,2,1,0:T(8,128)S(1)} %add.21.first_ref.refs_4_), channel_id=1, source_target_pairs={{0,2},{1,3},{2,0},{3,1},{4,6},{5,7},{6,4},{7,5},{8,10},{9,11},{10,... | collective-permute-start | bytes 589832 | tf_op jit(solution)/shard_map/ppermute | solution.py:663
  34.0 0.2 slice_reduce_fusion.count_ref
  34.2 3.0 %products.2._.forcing_ref = f32[3,8,32,128]{3,2,1,0:T(8,128)S(1)} custom-call(s32[8]{0:T(128)S(1)} %copy-done.5, s32[16,8]{1,0:T(8,128)S(1)} %bitcast.27, s32[16]{0:T(128)S(1)} %slice_reduce_fusion.count_ref, f32[3,16,32,256]{3,2,1,0:T(8,128)S(1)} %get-tuple-element.45.physical, bf16[256,256]{1,0:T(8,128)(2,1)S(1)} %get-tuple-element.42.refs_6_.back_ref.refs_3_, ...), custom_call_target="tpu_custom_call" | custom-call | bytes 12582912 | tf_op jit(solution)/shard_map/products/pallas_call | solution.py:418
  37.2 2.3 %collective-permute-done.4.second_ref = f32[3,4,32,128]{3,2,1,0:T(8,128)S(1)} collective-permute-done((f32[3,4,32,128]{3,2,1,0:T(8,128)S(1)}, f32[3,4,32,128]{3,2,1,0:T(8,128)S(1)}, u32[]{:S(2)}, u32[]{:S(2)}) %collective-permute-start.4) | collective-permute-done | bytes 196640 | tf_op jit(solution)/shard_map/ppermute | solution.py:663
  39.5 0.1 collective-permute-start.5
  39.5 1.4 %collective-permute-done.5.other_ref = f32[3,4,32,128]{3,2,1,0:T(8,128)S(1)} collective-permute-done((f32[3,4,32,128]{3,2,1,0:T(8,128)S(1)}, f32[3,4,32,128]{3,2,1,0:T(8,128)S(1)}, u32[]{:S(2)}, u32[]{:S(2)}) %collective-permute-start.5) | collective-permute-done | bytes 196640 | tf_op jit(solution)/shard_map/ppermute | solution.py:663
  41.0 1.9 %outgoing.2 = f32[1536,128]{1,0:T(8,128)} custom-call(s32[8]{0:T(128)S(1)} %copy-done.5, s32[16]{0:T(128)S(1)} %slice_reduce_fusion.count_ref, f32[3,16,32,128]{3,2,1,0:T(8,128)S(1)} %get-tuple-element.44.slotted_ref, f32[3,8,32,128]{3,2,1,0:T(8,128)S(1)} %products.2._.forcing_ref, f32[3,4,32,128]{3,2,1,0:T(8,128)S(1)} %ordered_sum.2.kept_ref, ...), custom_call_target="tpu_custom_call" | custom-call | bytes 1572864 | tf_op jit(solution)/shard_map/outgoing/pallas_call | solution.py:484
  42.9 0.0 all-to-all-done.1.refs_0_
  42.9 7.8 %all-to-all-start = ((f32[8,8,24,128]{3,2,1,0:T(8,128)}), f32[8,8,24,128]{3,2,1,0:T(8,128)S(1)}, u32[]{:S(2)}, u32[]{:S(2)}) async-start(f32[8,8,24,128]{3,2,1,0:T(8,128)} %bitcast.5), calls=%async_computation | async-start | bytes 1572864 | tf_op jit(solution)/shard_map/all_to_all | solution.py:719
  50.7 3.5 %stress.3 = (f32[3,16,32,128]{3,2,1,0:T(8,128)S(1)}, f32[3,16,32,256]{3,2,1,0:T(8,128)S(1)}, f32[3,4,32,128]{3,2,1,0:T(8,128)S(1)}, f32[3,4,32,128]{3,2,1,0:T(8,128)S(1)}) custom-call(s32[8]{0:T(128)S(1)} %copy-done.5, s32[16,8]{1,0:T(8,128)S(1)} %bitcast.28, f32[4,384,128]{2,1,0:T(8,128)S(1)} %all-to-all-done.1.refs_0_, ...), custom_call_target="tpu_custom_call" | custom-call | bytes 12582912 | tf_op jit(solution)/shard_map/stress/pallas_call | solution.py:353
  54.2 0.1 collective-permute-start.6
  54.3 1.4 %collective-permute-done.6 = f32[3,4,32,128]{3,2,1,0:T(8,128)S(1)} collective-permute-done((f32[3,4,32,128]{3,2,1,0:T(8,128)S(1)}, f32[3,4,32,128]{3,2,1,0:T(8,128)S(1)}, u32[]{:S(2)}, u32[]{:S(2)}) %collective-permute-start.6) | collective-permute-done | bytes 196640 | tf_op jit(solution)/shard_map/ppermute | solution.py:663
  55.7 1.6 %collective-permute-start.7 = (f32[3,4,32,128]{3,2,1,0:T(8,128)S(1)}, f32[3,4,32,128]{3,2,1,0:T(8,128)S(1)}, u32[]{:S(2)}, u32[]{:S(2)}) collective-permute-start(f32[3,4,32,128]{3,2,1,0:T(8,128)S(1)} %add.22.first_ref), channel_id=1, source_target_pairs={{0,2},{1,3},{2,0},{3,1},{4,6},{5,7},{6,4},{7,5},{8,10},{9,11},{10,... | collective-permute-start | bytes 589832 | tf_op jit(solution)/shard_map/ppermute | solution.py:663
  57.3 3.0 %products.3._.forcing_ref = f32[3,8,32,128]{3,2,1,0:T(8,128)S(1)} custom-call(s32[8]{0:T(128)S(1)} %copy-done.5, s32[16,8]{1,0:T(8,128)S(1)} %bitcast.29, s32[16]{0:T(128)S(1)} %slice_reduce_fusion.count_ref, f32[3,16,32,256]{3,2,1,0:T(8,128)S(1)} %get-tuple-element.49.physical, bf16[256,256]{1,0:T(8,128)(2,1)S(1)} %get-tuple-element.42.refs_6_.back_ref.refs_3_, ...), custom_call_target="tpu_custom_call" | custom-call | bytes 12582912 | tf_op jit(solution)/shard_map/products/pallas_call | solution.py:418
  60.3 2.4 %collective-permute-done.7.second_ref = f32[3,4,32,128]{3,2,1,0:T(8,128)S(1)} collective-permute-done((f32[3,4,32,128]{3,2,1,0:T(8,128)S(1)}, f32[3,4,32,128]{3,2,1,0:T(8,128)S(1)}, u32[]{:S(2)}, u32[]{:S(2)}) %collective-permute-start.7) | collective-permute-done | bytes 196640 | tf_op jit(solution)/shard_map/ppermute | solution.py:663
  62.8 0.1 collective-permute-start.8
  62.8 1.4 %collective-permute-done.8.other_ref = f32[3,4,32,128]{3,2,1,0:T(8,128)S(1)} collective-permute-done((f32[3,4,32,128]{3,2,1,0:T(8,128)S(1)}, f32[3,4,32,128]{3,2,1,0:T(8,128)S(1)}, u32[]{:S(2)}, u32[]{:S(2)}) %collective-permute-start.8) | collective-permute-done | bytes 196640 | tf_op jit(solution)/shard_map/ppermute | solution.py:663
  64.3 1.2 outgoing.3
  65.5 3.0 %collective-permute-start.9 = (f32[8,24,128]{2,1,0:T(8,128)S(1)}, f32[8,24,128]{2,1,0:T(8,128)S(1)}, u32[]{:S(2)}, u32[]{:S(2)}) collective-permute-start(f32[8,24,128]{2,1,0:T(8,128)S(1)} %bitcast.45), channel_id=1, source_target_pairs={{0,16},{1,5},{2,18},{3,7},{4,20},{5,1},{6,22},{7,3},{8,24},{9,13},... | collective-permute-start | bytes 294920 | tf_op jit(solution)/shard_map/ppermute | solution.py:641
  68.4 1.5 %collective-permute-start.10 = (f32[8,24,128]{2,1,0:T(8,128)S(1)}, f32[8,24,128]{2,1,0:T(8,128)S(1)}, u32[]{:S(2)}, u32[]{:S(2)}) collective-permute-start(f32[8,24,128]{2,1,0:T(8,128)S(1)} %bitcast.44), channel_id=1, source_target_pairs={{0,4},{1,17},{2,6},{3,19},{4,0},{5,21},{6,2},{7,23},{8,12},{9,25},... | collective-permute-start | bytes 294920 | tf_op jit(solution)/shard_map/ppermute | solution.py:641
  69.9 1.5 %collective-permute-start.11 = (f32[8,24,128]{2,1,0:T(8,128)S(1)}, f32[8,24,128]{2,1,0:T(8,128)S(1)}, u32[]{:S(2)}, u32[]{:S(2)}) collective-permute-start(f32[8,24,128]{2,1,0:T(8,128)S(1)} %bitcast.43), channel_id=1, source_target_pairs={{0,8},{1,25},{2,10},{3,27},{4,12},{5,29},{6,14},{7,31},{8,0},{9,17... | collective-permute-start | bytes 294920 | tf_op jit(solution)/shard_map/ppermute | solution.py:641
  71.4 0.6 collective-permute-start.12
  71.9 1.5 %collective-permute-start.13 = (f32[8,24,128]{2,1,0:T(8,128)S(1)}, f32[8,24,128]{2,1,0:T(8,128)S(1)}, u32[]{:S(2)}, u32[]{:S(2)}) collective-permute-start(f32[8,24,128]{2,1,0:T(8,128)S(1)} %bitcast.41), channel_id=1, source_target_pairs={{0,20},{1,13},{2,22},{3,15},{4,16},{5,9},{6,18},{7,11},{8,28},{9,5... | collective-permute-start | bytes 294920 | tf_op jit(solution)/shard_map/ppermute | solution.py:641
  73.4 3.3 %collective-permute-done.9.refs_2_ = f32[8,24,128]{2,1,0:T(8,128)S(1)} collective-permute-done((f32[8,24,128]{2,1,0:T(8,128)S(1)}, f32[8,24,128]{2,1,0:T(8,128)S(1)}, u32[]{:S(2)}, u32[]{:S(2)}) %collective-permute-start.9) | collective-permute-done | bytes 98336 | tf_op jit(solution)/shard_map/ppermute | solution.py:641
  76.7 0.4 collective-permute-start.14
  77.1 0.0 collective-permute-done.10.refs_3_
  77.1 3.1 %collective-permute-start.15 = (f32[8,24,128]{2,1,0:T(8,128)S(1)}, f32[8,24,128]{2,1,0:T(8,128)S(1)}, u32[]{:S(2)}, u32[]{:S(2)}) collective-permute-start(f32[8,24,128]{2,1,0:T(8,128)S(1)} %bitcast.39), channel_id=1, source_target_pairs={{0,28},{1,29},{2,30},{3,31},{4,24},{5,25},{6,26},{7,27},{8,20},{9,... | collective-permute-start | bytes 294920 | tf_op jit(solution)/shard_map/ppermute | solution.py:641
  80.2 0.0 collective-permute-done.11.refs_4_
  80.2 7.6 %collective-permute-done.13.refs_6_ = f32[8,24,128]{2,1,0:T(8,128)S(1)} collective-permute-done((f32[8,24,128]{2,1,0:T(8,128)S(1)}, f32[8,24,128]{2,1,0:T(8,128)S(1)}, u32[]{:S(2)}, u32[]{:S(2)}) %collective-permute-start.13) | collective-permute-done | bytes 98336 | tf_op jit(solution)/shard_map/ppermute | solution.py:641
  87.8 0.0 collective-permute-done.14.refs_7_
  87.8 0.0 collective-permute-done.15.refs_8_
  87.8 6.4 %solve.1 = (f32[8,2,24,128]{3,2,1,0:T(8,128)S(1)}, f32[8,2,24,128]{3,2,1,0:T(8,128)S(1)}, f32[8,2,24,128]{3,2,1,0:T(8,128)S(1)}, f32[8,2,24,128]{3,2,1,0:T(8,128...) custom-call(f32[8,8,24,128]{3,2,1,0:T(8,128)S(1)} %all-to-all-done.r, ...), custom_call_target="tpu_custom_call" | custom-call | bytes 8388608 | tf_op jit(solution)/shard_map/solve/pallas_call | solution.py:575
  94.2 2.4 %collective-permute-start.16 = (f32[8,2,24,128]{3,2,1,0:T(8,128)S(1)}, f32[8,2,24,128]{3,2,1,0:T(8,128)S(1)}, u32[]{:S(2)}, u32[]{:S(2)}) collective-permute-start(f32[8,2,24,128]{3,2,1,0:T(8,128)S(1)} %get-tuple-element.61), channel_id=1, source_target_pairs={{0,16},{1,5},{2,18},{3,7},{4,20},{5,1},{6,22},{7,3},{8,24},{9,13},... | collective-permute-start | bytes 589832 | tf_op jit(solution)/shard_map/ppermute | solution.py:641
  96.6 1.1 collective-permute-start.17
  97.7 2.6 %collective-permute-start.19 = (f32[8,2,24,128]{3,2,1,0:T(8,128)S(1)}, f32[8,2,24,128]{3,2,1,0:T(8,128)S(1)}, u32[]{:S(2)}, u32[]{:S(2)}) collective-permute-start(f32[8,2,24,128]{3,2,1,0:T(8,128)S(1)} %get-tuple-element.64), channel_id=1, source_target_pairs={{0,24},{1,9},{2,26},{3,11},{4,28},{5,13},{6,30},{7,15},{8,16},{9,1... | collective-permute-start | bytes 589832 | tf_op jit(solution)/shard_map/ppermute | solution.py:641
  100.3 1.3 collective-permute-start.20
  101.6 8.7 %collective-permute-done.16 = f32[8,2,24,128]{3,2,1,0:T(8,128)S(1)} collective-permute-done((f32[8,2,24,128]{3,2,1,0:T(8,128)S(1)}, f32[8,2,24,128]{3,2,1,0:T(8,128)S(1)}, u32[]{:S(2)}, u32[]{:S(2)}) %collective-permute-start.16) | collective-permute-done | bytes 196640 | tf_op jit(solution)/shard_map/ppermute | solution.py:641
  110.2 1.7 %collective-permute-start.22 = (f32[8,2,24,128]{3,2,1,0:T(8,128)S(1)}, f32[8,2,24,128]{3,2,1,0:T(8,128)S(1)}, u32[]{:S(2)}, u32[]{:S(2)}) collective-permute-start(f32[8,2,24,128]{3,2,1,0:T(8,128)S(1)} %get-tuple-element.67), channel_id=1, source_target_pairs={{0,28},{1,29},{2,30},{3,31},{4,24},{5,25},{6,26},{7,27},{8,20},{9,... | collective-permute-start | bytes 589832 | tf_op jit(solution)/shard_map/ppermute | solution.py:641
  111.9 2.0 %collective-permute-done.18 = f32[8,2,24,128]{3,2,1,0:T(8,128)S(1)} collective-permute-done((f32[8,2,24,128]{3,2,1,0:T(8,128)S(1)}, f32[8,2,24,128]{3,2,1,0:T(8,128)S(1)}, u32[]{:S(2)}, u32[]{:S(2)}) %collective-permute-start.18) | collective-permute-done | bytes 196640 | tf_op jit(solution)/shard_map/ppermute | solution.py:641
  113.9 14.9 %collective-permute-done.20 = f32[8,2,24,128]{3,2,1,0:T(8,128)S(1)} collective-permute-done((f32[8,2,24,128]{3,2,1,0:T(8,128)S(1)}, f32[8,2,24,128]{3,2,1,0:T(8,128)S(1)}, u32[]{:S(2)}, u32[]{:S(2)}) %collective-permute-start.20) | collective-permute-done | bytes 196640 | tf_op jit(solution)/shard_map/ppermute | solution.py:641
  128.8 2.1 %restore.1 = f32[3,4,256,128]{3,2,1,0:T(8,128)} custom-call(f32[384,128]{1,0:T(8,128)S(1)} %bitcast.30, f32[384,128]{1,0:T(8,128)S(1)} %bitcast.31, f32[384,128]{1,0:T(8,128)S(1)} %bitcast.32, f32[384,128]{1,0:T(8,128)S(1)} %bitcast.33, f32[384,128]{1,0:T(8,128)S(1)} %bitcast.34, f32[384,128]{1,0:T(8,128)S(1)} %bitcast.35, f32[384,128]{1,0:T(8,128)S(1)} %bitcast.36, ...), custom_call_target="tpu_custom_call" | custom-call | bytes 3145728 | tf_op jit(solution)/shard_map/restore/pallas_call | solution.py:619
  (37 shorter events, 0.2 us)
Async XLA Ops:
  2.1 9.8 %collective-permute-start = (f32[392,128]{1,0:T(8,128)}, f32[392,128]{1,0:T(8,128)S(1)}, u32[]{:S(2)}, u32[]{:S(2)}) collective-permute-start(f32[392,128]{1,0:T(8,128)} %get-tuple-element.38), channel_id=1, source_target_pairs={{0,8},{1,25},{2,10},{3,27},{8,0},{9,17},{10,2},{11,19},{16,24},{17... | collective-permute-start | bytes 602120 | tf_op jit(solution)/shard_map/ppermute | solution.py:641
  5.1 20.6 %collective-permute-start.1 = (f32[392,128]{1,0:T(8,128)}, f32[392,128]{1,0:T(8,128)S(1)}, u32[]{:S(2)}, u32[]{:S(2)}) collective-permute-start(f32[392,128]{1,0:T(8,128)} %get-tuple-element.39), channel_id=1, source_target_pairs={{0,24},{1,9},{2,26},{3,11},{8,16},{9,1},{10,18},{11,3},{16,8},{17,... | collective-permute-start | bytes 602120 | tf_op jit(solution)/shard_map/ppermute | solution.py:641
  7.6 19.7 %collective-permute-start.2 = (f32[392,128]{1,0:T(8,128)}, f32[392,128]{1,0:T(8,128)S(1)}, u32[]{:S(2)}, u32[]{:S(2)}) collective-permute-start(f32[392,128]{1,0:T(8,128)} %get-tuple-element.40), channel_id=1, source_target_pairs={{0,16},{1,17},{2,18},{3,19},{8,24},{9,25},{10,26},{11,27},{16,0},{... | collective-permute-start | bytes 602120 | tf_op jit(solution)/shard_map/ppermute | solution.py:641
  7.7 17.2 %copy-start.3 = (f32[392,128]{1,0:T(8,128)S(1)}, f32[392,128]{1,0:T(8,128)}, u32[]{:S(2)}) copy-start(f32[392,128]{1,0:T(8,128)} %get-tuple-element.37.refs_0_) | copy-start | bytes 602116
  7.7 17.2 %copy-start.2 = (bf16[128,256]{1,0:T(8,128)(2,1)S(1)}, bf16[128,256]{1,0:T(8,128)(2,1)}, u32[]{:S(2)}) copy-start(bf16[128,256]{1,0:T(8,128)(2,1)} %constant.22.clone.rest_ref.refs_5_.refs_2_) | copy-start | bytes 196612
  7.7 17.2 %copy-start.4 = (bf16[128,256]{1,0:T(8,128)(2,1)S(1)}, bf16[128,256]{1,0:T(8,128)(2,1)}, u32[]{:S(2)}) copy-start(bf16[128,256]{1,0:T(8,128)(2,1)} %constant.21.clone.top_ref) | copy-start | bytes 196612
  7.7 17.2 %copy-start.6 = (s32[64]{0:T(128)S(1)}, s32[64]{0:T(128)}, u32[]{:S(2)}) copy-start(s32[64]{0:T(128)} %owner_ref.1) | copy-start | bytes 772
  7.7 19.7 %copy-start.5 = (s32[8]{0:T(128)S(1)}, s32[8]{0:T(128)}, u32[]{:S(2)}) copy-start(s32[8]{0:T(128)} %low_ref.11) | copy-start | bytes 100
  11.9 0.7 copy-start
  14.7 11.0 %copy-start.1 = (f32[392,128]{1,0:T(8,128)S(1)}, f32[392,128]{1,0:T(8,128)}, u32[]{:S(2)}) copy-start(f32[392,128]{1,0:T(8,128)} %copy-done) | copy-start | bytes 602116
  14.7 28.2 %all-to-all-start.1 = ((f32[4,384,128]{2,1,0:T(8,128)}), f32[4,384,128]{2,1,0:T(8,128)S(1)}, u32[]{:S(2)}, u32[]{:S(2)}) async-start(f32[4,384,128]{2,1,0:T(8,128)} %pack.1), calls=%async_computation.1 | async-start | bytes 1572864 | tf_op jit(solution)/shard_map/all_to_all | solution.py:689
  30.9 1.5 %collective-permute-start.3 = (f32[3,4,32,128]{3,2,1,0:T(8,128)S(1)}, f32[3,4,32,128]{3,2,1,0:T(8,128)S(1)}, u32[]{:S(2)}, u32[]{:S(2)}) collective-permute-start(f32[3,4,32,128]{3,2,1,0:T(8,128)S(1)} %get-tuple-element.47), channel_id=1, source_target_pairs={{0,1},{1,0},{2,3},{3,2},{4,5},{5,4},{6,7},{7,6},{8,9},{9,8},{10,11... | collective-permute-start | bytes 589832 | tf_op jit(solution)/shard_map/ppermute | solution.py:663
  32.4 7.0 %collective-permute-start.4 = (f32[3,4,32,128]{3,2,1,0:T(8,128)S(1)}, f32[3,4,32,128]{3,2,1,0:T(8,128)S(1)}, u32[]{:S(2)}, u32[]{:S(2)}) collective-permute-start(f32[3,4,32,128]{3,2,1,0:T(8,128)S(1)} %add.21.first_ref.refs_4_), channel_id=1, source_target_pairs={{0,2},{1,3},{2,0},{3,1},{4,6},{5,7},{6,4},{7,5},{8,10},{9,11},{10,... | collective-permute-start | bytes 589832 | tf_op jit(solution)/shard_map/ppermute | solution.py:663
  39.5 1.5 %collective-permute-start.5 = (f32[3,4,32,128]{3,2,1,0:T(8,128)S(1)}, f32[3,4,32,128]{3,2,1,0:T(8,128)S(1)}, u32[]{:S(2)}, u32[]{:S(2)}) collective-permute-start(f32[3,4,32,128]{3,2,1,0:T(8,128)S(1)} %ordered_sum.2.kept_ref), channel_id=1, source_target_pairs={{0,1},{1,0},{2,3},{3,2},{4,5},{5,4},{6,7},{7,6},{8,9},{9,8},{10,11... | collective-permute-start | bytes 589832 | tf_op jit(solution)/shard_map/ppermute | solution.py:663
  42.9 44.9 %all-to-all-start = ((f32[8,8,24,128]{3,2,1,0:T(8,128)}), f32[8,8,24,128]{3,2,1,0:T(8,128)S(1)}, u32[]{:S(2)}, u32[]{:S(2)}) async-start(f32[8,8,24,128]{3,2,1,0:T(8,128)} %bitcast.5), calls=%async_computation | async-start | bytes 1572864 | tf_op jit(solution)/shard_map/all_to_all | solution.py:719
  54.2 1.5 %collective-permute-start.6 = (f32[3,4,32,128]{3,2,1,0:T(8,128)S(1)}, f32[3,4,32,128]{3,2,1,0:T(8,128)S(1)}, u32[]{:S(2)}, u32[]{:S(2)}) collective-permute-start(f32[3,4,32,128]{3,2,1,0:T(8,128)S(1)} %get-tuple-element.51), channel_id=1, source_target_pairs={{0,1},{1,0},{2,3},{3,2},{4,5},{5,4},{6,7},{7,6},{8,9},{9,8},{10,11... | collective-permute-start | bytes 589832 | tf_op jit(solution)/shard_map/ppermute | solution.py:663
  55.7 7.0 %collective-permute-start.7 = (f32[3,4,32,128]{3,2,1,0:T(8,128)S(1)}, f32[3,4,32,128]{3,2,1,0:T(8,128)S(1)}, u32[]{:S(2)}, u32[]{:S(2)}) collective-permute-start(f32[3,4,32,128]{3,2,1,0:T(8,128)S(1)} %add.22.first_ref), channel_id=1, source_target_pairs={{0,2},{1,3},{2,0},{3,1},{4,6},{5,7},{6,4},{7,5},{8,10},{9,11},{10,... | collective-permute-start | bytes 589832 | tf_op jit(solution)/shard_map/ppermute | solution.py:663
  62.8 1.5 %collective-permute-start.8 = (f32[3,4,32,128]{3,2,1,0:T(8,128)S(1)}, f32[3,4,32,128]{3,2,1,0:T(8,128)S(1)}, u32[]{:S(2)}, u32[]{:S(2)}) collective-permute-start(f32[3,4,32,128]{3,2,1,0:T(8,128)S(1)} %ordered_sum.3.kept_ref), channel_id=1, source_target_pairs={{0,1},{1,0},{2,3},{3,2},{4,5},{5,4},{6,7},{7,6},{8,9},{9,8},{10,11... | collective-permute-start | bytes 589832 | tf_op jit(solution)/shard_map/ppermute | solution.py:663
  65.5 11.2 %collective-permute-start.9 = (f32[8,24,128]{2,1,0:T(8,128)S(1)}, f32[8,24,128]{2,1,0:T(8,128)S(1)}, u32[]{:S(2)}, u32[]{:S(2)}) collective-permute-start(f32[8,24,128]{2,1,0:T(8,128)S(1)} %bitcast.45), channel_id=1, source_target_pairs={{0,16},{1,5},{2,18},{3,7},{4,20},{5,1},{6,22},{7,3},{8,24},{9,13},... | collective-permute-start | bytes 294920 | tf_op jit(solution)/shard_map/ppermute | solution.py:641
  68.4 8.7 %collective-permute-start.10 = (f32[8,24,128]{2,1,0:T(8,128)S(1)}, f32[8,24,128]{2,1,0:T(8,128)S(1)}, u32[]{:S(2)}, u32[]{:S(2)}) collective-permute-start(f32[8,24,128]{2,1,0:T(8,128)S(1)} %bitcast.44), channel_id=1, source_target_pairs={{0,4},{1,17},{2,6},{3,19},{4,0},{5,21},{6,2},{7,23},{8,12},{9,25},... | collective-permute-start | bytes 294920 | tf_op jit(solution)/shard_map/ppermute | solution.py:641
  69.9 10.3 %collective-permute-start.11 = (f32[8,24,128]{2,1,0:T(8,128)S(1)}, f32[8,24,128]{2,1,0:T(8,128)S(1)}, u32[]{:S(2)}, u32[]{:S(2)}) collective-permute-start(f32[8,24,128]{2,1,0:T(8,128)S(1)} %bitcast.43), channel_id=1, source_target_pairs={{0,8},{1,25},{2,10},{3,27},{4,12},{5,29},{6,14},{7,31},{8,0},{9,17... | collective-permute-start | bytes 294920 | tf_op jit(solution)/shard_map/ppermute | solution.py:641
  71.4 8.8 %collective-permute-start.12 = (f32[8,24,128]{2,1,0:T(8,128)S(1)}, f32[8,24,128]{2,1,0:T(8,128)S(1)}, u32[]{:S(2)}, u32[]{:S(2)}) collective-permute-start(f32[8,24,128]{2,1,0:T(8,128)S(1)} %bitcast.42), channel_id=1, source_target_pairs={{0,24},{1,9},{2,26},{3,11},{4,28},{5,13},{6,30},{7,15},{8,16},{9,1... | collective-permute-start | bytes 294920 | tf_op jit(solution)/shard_map/ppermute | solution.py:641
  71.9 15.9 %collective-permute-start.13 = (f32[8,24,128]{2,1,0:T(8,128)S(1)}, f32[8,24,128]{2,1,0:T(8,128)S(1)}, u32[]{:S(2)}, u32[]{:S(2)}) collective-permute-start(f32[8,24,128]{2,1,0:T(8,128)S(1)} %bitcast.41), channel_id=1, source_target_pairs={{0,20},{1,13},{2,22},{3,15},{4,16},{5,9},{6,18},{7,11},{8,28},{9,5... | collective-permute-start | bytes 294920 | tf_op jit(solution)/shard_map/ppermute | solution.py:641
  76.7 11.1 %collective-permute-start.14 = (f32[8,24,128]{2,1,0:T(8,128)S(1)}, f32[8,24,128]{2,1,0:T(8,128)S(1)}, u32[]{:S(2)}, u32[]{:S(2)}) collective-permute-start(f32[8,24,128]{2,1,0:T(8,128)S(1)} %bitcast.40), channel_id=1, source_target_pairs={{0,12},{1,21},{2,14},{3,23},{4,8},{5,17},{6,10},{7,19},{8,4},{9,29... | collective-permute-start | bytes 294920 | tf_op jit(solution)/shard_map/ppermute | solution.py:641
  77.1 10.7 %collective-permute-start.15 = (f32[8,24,128]{2,1,0:T(8,128)S(1)}, f32[8,24,128]{2,1,0:T(8,128)S(1)}, u32[]{:S(2)}, u32[]{:S(2)}) collective-permute-start(f32[8,24,128]{2,1,0:T(8,128)S(1)} %bitcast.39), channel_id=1, source_target_pairs={{0,28},{1,29},{2,30},{3,31},{4,24},{5,25},{6,26},{7,27},{8,20},{9,... | collective-permute-start | bytes 294920 | tf_op jit(solution)/shard_map/ppermute | solution.py:641
  94.2 16.0 %collective-permute-start.16 = (f32[8,2,24,128]{3,2,1,0:T(8,128)S(1)}, f32[8,2,24,128]{3,2,1,0:T(8,128)S(1)}, u32[]{:S(2)}, u32[]{:S(2)}) collective-permute-start(f32[8,2,24,128]{3,2,1,0:T(8,128)S(1)} %get-tuple-element.61), channel_id=1, source_target_pairs={{0,16},{1,5},{2,18},{3,7},{4,20},{5,1},{6,22},{7,3},{8,24},{9,13},... | collective-permute-start | bytes 589832 | tf_op jit(solution)/shard_map/ppermute | solution.py:641
  96.6 13.6 %collective-permute-start.17 = (f32[8,2,24,128]{3,2,1,0:T(8,128)S(1)}, f32[8,2,24,128]{3,2,1,0:T(8,128)S(1)}, u32[]{:S(2)}, u32[]{:S(2)}) collective-permute-start(f32[8,2,24,128]{3,2,1,0:T(8,128)S(1)} %get-tuple-element.62), channel_id=1, source_target_pairs={{0,4},{1,17},{2,6},{3,19},{4,0},{5,21},{6,2},{7,23},{8,12},{9,25},... | collective-permute-start | bytes 589832 | tf_op jit(solution)/shard_map/ppermute | solution.py:641
  97.7 16.2 %collective-permute-start.18 = (f32[8,2,24,128]{3,2,1,0:T(8,128)S(1)}, f32[8,2,24,128]{3,2,1,0:T(8,128)S(1)}, u32[]{:S(2)}, u32[]{:S(2)}) collective-permute-start(f32[8,2,24,128]{3,2,1,0:T(8,128)S(1)} %get-tuple-element.63), channel_id=1, source_target_pairs={{0,8},{1,25},{2,10},{3,27},{4,12},{5,29},{6,14},{7,31},{8,0},{9,17... | collective-permute-start | bytes 589832 | tf_op jit(solution)/shard_map/ppermute | solution.py:641
  97.7 16.2 %collective-permute-start.19 = (f32[8,2,24,128]{3,2,1,0:T(8,128)S(1)}, f32[8,2,24,128]{3,2,1,0:T(8,128)S(1)}, u32[]{:S(2)}, u32[]{:S(2)}) collective-permute-start(f32[8,2,24,128]{3,2,1,0:T(8,128)S(1)} %get-tuple-element.64), channel_id=1, source_target_pairs={{0,24},{1,9},{2,26},{3,11},{4,28},{5,13},{6,30},{7,15},{8,16},{9,1... | collective-permute-start | bytes 589832 | tf_op jit(solution)/shard_map/ppermute | solution.py:641
  100.3 28.5 %collective-permute-start.20 = (f32[8,2,24,128]{3,2,1,0:T(8,128)S(1)}, f32[8,2,24,128]{3,2,1,0:T(8,128)S(1)}, u32[]{:S(2)}, u32[]{:S(2)}) collective-permute-start(f32[8,2,24,128]{3,2,1,0:T(8,128)S(1)} %get-tuple-element.65), channel_id=1, source_target_pairs={{0,20},{1,13},{2,22},{3,15},{4,16},{5,9},{6,18},{7,11},{8,28},{9,5... | collective-permute-start | bytes 589832 | tf_op jit(solution)/shard_map/ppermute | solution.py:641
  110.2 18.5 %collective-permute-start.21 = (f32[8,2,24,128]{3,2,1,0:T(8,128)S(1)}, f32[8,2,24,128]{3,2,1,0:T(8,128)S(1)}, u32[]{:S(2)}, u32[]{:S(2)}) collective-permute-start(f32[8,2,24,128]{3,2,1,0:T(8,128)S(1)} %get-tuple-element.66), channel_id=1, source_target_pairs={{0,12},{1,21},{2,14},{3,23},{4,8},{5,17},{6,10},{7,19},{8,4},{9,29... | collective-permute-start | bytes 589832 | tf_op jit(solution)/shard_map/ppermute | solution.py:641
  110.2 18.5 %collective-permute-start.22 = (f32[8,2,24,128]{3,2,1,0:T(8,128)S(1)}, f32[8,2,24,128]{3,2,1,0:T(8,128)S(1)}, u32[]{:S(2)}, u32[]{:S(2)}) collective-permute-start(f32[8,2,24,128]{3,2,1,0:T(8,128)S(1)} %get-tuple-element.67), channel_id=1, source_target_pairs={{0,28},{1,29},{2,30},{3,31},{4,24},{5,25},{6,26},{7,27},{8,20},{9,... | collective-permute-start | bytes 589832 | tf_op jit(solution)/shard_map/ppermute | solution.py:641

commit v15 on v12

--- a/solution.py
+++ b/solution.py
@@ -516,40 +516,75 @@
     return blocks
 
 
-def solve_kernel(*refs, groups, kx_count, ht_count, pieces):
-    owners = kx_count * ht_count
-    first_ref, refs = (refs[0], refs[1:])
-    count = owners * (pieces - 1)
-    block_refs, matrix_ref, refs = (refs[:count], refs[count], refs[count + 1 :])
-    out_refs, (ordered, full) = (refs[:owners], refs[owners:])
-    slots, heights = (matrix_ref.shape[0], matrix_ref.shape[1])
+def solve_kernel(*refs, groups, kx_count, ht_count, pieces, piece):
+    owners, last = (kx_count * ht_count, piece == pieces - 1)
     own_kx, own_ht = (lax.axis_index("kx"), lax.axis_index("ht"))
     partners = []
     for position in range(owners):
         step = step_at(owners, position)
         partners.append((own_kx ^ (step // ht_count), own_ht ^ (step % ht_count)))
-    for index, block_ref in enumerate(block_refs):
-        kx, ht = partners[index % owners]
-        ordered[index // owners, kx * ht_count + ht] = block_ref[...]
-    rows, (lane_tiles, per_band) = (LANES // groups, out_refs[0].shape[1:3])
+    refs = list(refs)
+    matrices = refs.pop()
+    arrived = refs.pop()
+    source = refs.pop(0)
+    if piece:
+        ordered = refs.pop()
+        blocks = [source] + [refs.pop(0) for _ in range(owners - 1)]
+        for block_ref, (kx, ht) in zip(blocks, partners):
+            ordered[kx * ht_count + ht] = block_ref[...]
+        source = ordered
+    matrix_ref = refs.pop(0)
+    slots, heights = (matrix_ref.shape[0], matrix_ref.shape[1])
+    width = heights // ht_count // pieces
+    copies = [
+        [
+            pltpu.make_async_copy(
+                matrix_ref.at[s, :, pl.ds((h * pieces + piece) * width, width)],
+                matrices.at[s, h],
+                arrived.at[s, h],
+            )
+            for h in range(ht_count)
+        ]
+        for s in range(slots)
+    ]
+    ahead = min(3, slots)
+    for s in range(ahead):
+        for copy in copies[s]:
+            copy.start()
+    partial_ref = refs.pop(0) if piece else None
+    if last:
+        out_refs, full = (refs[:owners], refs[owners])
+        lane_tiles, per_band = out_refs[0].shape[1:3]
+    rows = LANES // groups
     for s in range(slots):
         tiles = []
         for h in range(ht_count):
-            for piece in range(pieces):
-                source = first_ref if piece == 0 else ordered.at[piece - 1]
-                for first in range(0, kx_count, groups):
-                    blocks = [source[(first + g) * ht_count + h, s] for g in range(groups)]
-                    tiles.append(jnp.concatenate(regroup(blocks, rows), axis=0))
+            for first in range(0, kx_count, groups):
+                blocks = [source[(first + g) * ht_count + h, s] for g in range(groups)]
+                tiles.append(jnp.concatenate(regroup(blocks, rows), axis=0))
         fields = jnp.concatenate(tiles, axis=1)
         count = fields.shape[0]
         spare = -count % LANES
         if spare:
-            fields = jnp.concatenate([fields, jnp.zeros((spare, heights), jnp.float32)], axis=0)
+            empty = jnp.zeros((spare, fields.shape[1]), jnp.float32)
+            fields = jnp.concatenate([fields, empty], axis=0)
         top, rest = two_parts(fields)
-        matrix_top, matrix_rest = two_parts(matrix_ref[s])
-        last = ((1,), (1,))
-        both = dot(matrix_top, jnp.concatenate([top, rest], axis=0), last)
-        solved = both[:, : count + spare] + both[:, count + spare :] + dot(matrix_rest, top, last)
+        for copy in copies[s]:
+            copy.wait()
+        if s + ahead < slots:
+            for copy in copies[s + ahead]:
+                copy.start()
+        matrix = jnp.concatenate([matrices[s, h] for h in range(ht_count)], axis=1)
+        matrix_top, matrix_rest = two_parts(matrix)
+        contract = ((1,), (1,))
+        both = dot(matrix_top, jnp.concatenate([top, rest], axis=0), contract)
+        solved = both[:, : count + spare] + both[:, count + spare :]
+        solved = solved + dot(matrix_rest, top, contract)
+        if piece:
+            solved = solved + partial_ref[s]
+        if not last:
+            refs[0][s] = solved
+            continue
         for tile in range(heights // LANES):
             full[s % 2, tile] = solved[tile * LANES : (tile + 1) * LANES].T[:count]
         for out_ref, (kx, ht) in zip(out_refs, partners):
@@ -558,25 +593,39 @@
                 out_ref[s, tile] = full[s % 2, ht * lane_tiles + tile, band]
 
 
-def solve(first, blocks, helmholtz, pieces, groups, kx_count, ht_count):
-    owners, slots, per_slot, lanes = first.shape
-    heights, count = (helmholtz.shape[1], per_slot * groups)
-    shape = (slots, heights // ht_count // LANES, count // kx_count, LANES)
+def solve(blocks, helmholtz, piece, pieces, partial, groups, kx_count, ht_count):
+    slots, per_slot, _ = blocks[0].shape[-3:]
+    heights, owners, last = (helmholtz.shape[1], kx_count * ht_count, piece == pieces - 1)
+    count = per_slot * groups
+    scratch = []
+    if last:
+        shape = (slots, heights // ht_count // LANES, count // kx_count, LANES)
+        out_shape = (jax.ShapeDtypeStruct(shape, jnp.float32),) * owners
+        scratch.append(pltpu.VMEM((2, heights // LANES, count, LANES), jnp.float32))
+    else:
+        padded = -(-count // LANES) * LANES
+        out_shape = jax.ShapeDtypeStruct((slots, heights, padded), jnp.float32)
+    if piece:
+        scratch.append(pltpu.VMEM((owners,) + blocks[0].shape, jnp.float32))
+    width = heights // ht_count // pieces
+    scratch += [
+        pltpu.SemaphoreType.DMA((slots, ht_count)),
+        pltpu.VMEM((slots, ht_count, heights, width), jnp.float32),
+    ]
+    started = [] if partial is None else [partial]
     return pl.pallas_call(
         functools.partial(
-            solve_kernel, groups=groups, kx_count=kx_count, ht_count=ht_count, pieces=pieces
+            solve_kernel, groups=groups, kx_count=kx_count, ht_count=ht_count, pieces=pieces,
+            piece=piece,
         ),
-        out_shape=(jax.ShapeDtypeStruct(shape, jnp.float32),) * owners,
-        in_specs=[VMEM] * (2 + len(blocks)),
-        out_specs=(VMEM,) * owners,
-        scratch_shapes=[
-            pltpu.VMEM((max(pieces - 1, 1),) + first.shape, jnp.float32),
-            pltpu.VMEM((2, heights // LANES, count, LANES), jnp.float32),
-        ],
+        out_shape=out_shape,
+        in_specs=[VMEM] * len(blocks) + [pl.BlockSpec(memory_space=pl.ANY)] + [VMEM] * len(started),
+        out_specs=(VMEM,) * owners if last else VMEM,
+        scratch_shapes=scratch,
         compiler_params=params(),
-        cost_estimate=cost(4 * helmholtz.size),
+        cost_estimate=cost(8 * helmholtz.size // pieces),
         name="solve",
-    )(first, *blocks, helmholtz)
+    )(*blocks, helmholtz, *started)
 
 
 def restore_kernel(*refs, owners, ht_count):
@@ -701,11 +750,15 @@
             owners, realizations, piece > 0,
         )
         if piece:
-            received += exchange([block.reshape(slots, -1, LANES) for block in blocks], ("kx", "ht"))
+            blocks = [block.reshape(slots, -1, LANES) for block in blocks]
+            received.append(exchange(blocks, ("kx", "ht")))
         else:
             block = blocks[0].reshape(owners, slots, -1, LANES)
-            first = lax.all_to_all(block, ("kx", "ht"), split_axis=0, concat_axis=0, tiled=True)
-    solved = solve(first, received, helmholtz, pieces, groups, kx_count, ht_count)
+            block = lax.all_to_all(block, ("kx", "ht"), split_axis=0, concat_axis=0, tiled=True)
+            received.append([block])
+    solved = None
+    for piece, blocks in enumerate(received):
+        solved = solve(blocks, helmholtz, piece, pieces, solved, groups, kx_count, ht_count)
     returned = [block.reshape(-1, LANES) for block in exchange(solved, ("kx", "ht"))]
     result = restore(returned, order, components, band_modes, rows_ht, ht_count)
     return result.reshape(velocity.shape)

time: 132 us -> 131 us (level)
  waiting for transfers between devices: 52.3 us -> 48.5 us
  Pallas kernels: 29.2 us -> 31.7 us
    ppermute x17, waiting for transfers between devices: 41.9 us -> 38.1 us  [exchange(): result[position] = lax.ppermute(blocks[position], axes + ('real',), pairs)]
    pallas_call x1 -> x2, Pallas kernels: 6.14 us -> 8.62 us  [solve(): pl.pallas_call(functools.partial(solve_kernel, groups=groups, kx_count=kx...]
  transfers between devices with their start and end apart: 25 -> 25, of which waited for: 13 -> 13; matrix products, arithmetic and copies ran while one was open for 1% -> 1% of each run, Pallas kernels for 14% -> 18%
where the time goes in v15:
time: 131 us; the launch traced here: 129 us
  waiting for transfers between devices  48.5 us (37%)
  starting transfers between devices  46.9 us (36%)
  Pallas kernels  31.7 us (24%)
  local copies, waits for them, and re-layouts  1.56 us (1%)
    ppermute x17, waiting for transfers between devices, exchange(): result[position] = lax.ppermute(blocks[position], axes + ('real',), pairs)  38.1 us
    ppermute x17, starting transfers between devices, exchange(): result[position] = lax.ppermute(blocks[position], axes + ('real',), pairs)  26.1 us
    ppermute x6, waiting for transfers between devices, swap(): return lax.ppermute(value, 'real', pairs)  10.4 us
    all_to_all x1, starting transfers between devices, local(): block = lax.all_to_all(block, 'kx', split_axis=0, concat_axis=0, tiled=True)  9.53 us
    pallas_call x2, Pallas kernels, solve(): pl.pallas_call(functools.partial(solve_kernel, groups=groups, kx_count=kx...  8.62 us
    all_to_all x1, starting transfers between devices, local(): lax.all_to_all(block, ('kx', 'ht'), split_axis=0, concat_axis=0, tiled=True)  7.83 us
    pallas_call x2, Pallas kernels, stress_terms(): pl.pallas_call(stress_kernel, out_shape=(jax.ShapeDtypeStruct(shape, jnp....  6.94 us
    pallas_call x2, Pallas kernels, high_terms(): pl.pallas_call(products_kernel, out_shape=jax.ShapeDtypeStruct((component...  6 us
  transfers between devices with their start and end apart: 25, of which 13 were waited for; matrix products, arithmetic and copies ran while one was open for 1% of the time, Pallas kernels for 18%

profile of v15, /device:TPU:0, one launch (start us, length us, event | category | flops | bytes accessed | tf_op | source)
XLA Modules:
  0.0 129.0 jit_solution(4183153361484591538)
XLA Ops:
  0.0 2.1 %pack_first.1 = (f32[392,128]{1,0:T(8,128)}, f32[392,128]{1,0:T(8,128)}, f32[392,128]{1,0:T(8,128)}, f32[392,128]{1,0:T(8,128)}) custom-call(s32[4,8]{1,0:T(4,128)} %near_ref.1, s32[4]{0:T(128)} %count_ref.1, f32[12,2,4,32,128]{4,3,2,1,0:T(8,128)} %bitcast.46), custom_call_target="tpu_custom_call" | custom-call | bytes 1572864 | tf_op jit(solution)/shard_map/pack_first/pallas_call | solution.py:175
  2.1 3.0 %collective-permute-start = (f32[392,128]{1,0:T(8,128)}, f32[392,128]{1,0:T(8,128)S(1)}, u32[]{:S(2)}, u32[]{:S(2)}) collective-permute-start(f32[392,128]{1,0:T(8,128)} %get-tuple-element.38), channel_id=1, source_target_pairs={{0,8},{1,25},{2,10},{3,27},{8,0},{9,17},{10,2},{11,19},{16,24},{17... | collective-permute-start | bytes 602120 | tf_op jit(solution)/shard_map/ppermute | solution.py:678
  5.1 2.5 %collective-permute-start.1 = (f32[392,128]{1,0:T(8,128)}, f32[392,128]{1,0:T(8,128)S(1)}, u32[]{:S(2)}, u32[]{:S(2)}) collective-permute-start(f32[392,128]{1,0:T(8,128)} %get-tuple-element.39), channel_id=1, source_target_pairs={{0,24},{1,9},{2,26},{3,11},{8,16},{9,1},{10,18},{11,3},{16,8},{17,... | collective-permute-start | bytes 602120 | tf_op jit(solution)/shard_map/ppermute | solution.py:678
  7.6 0.1 collective-permute-start.2
  7.7 0.0 copy-start.5
  7.7 4.2 %collective-permute-done._.refs_1_ = f32[392,128]{1,0:T(8,128)S(1)} collective-permute-done((f32[392,128]{1,0:T(8,128)}, f32[392,128]{1,0:T(8,128)S(1)}, u32[]{:S(2)}, u32[]{:S(2)}) %collective-permute-start) | collective-permute-done | bytes 200736 | tf_op jit(solution)/shard_map/ppermute | solution.py:678
  11.9 0.7 copy-done
  12.6 2.1 %pack.1 = f32[4,384,128]{2,1,0:T(8,128)} custom-call(f32[12,2,4,32,128]{4,3,2,1,0:T(8,128)} %bitcast.47, f32[392,128]{1,0:T(8,128)} %copy-done), custom_call_target="tpu_custom_call" | custom-call | bytes 1572864 | tf_op jit(solution)/shard_map/pack/pallas_call | solution.py:201
  14.7 9.5 %all-to-all-start = ((f32[4,384,128]{2,1,0:T(8,128)}), f32[4,384,128]{2,1,0:T(8,128)S(1)}, u32[]{:S(2)}, u32[]{:S(2)}) async-start(f32[4,384,128]{2,1,0:T(8,128)} %pack.1), calls=%async_computation | async-start | bytes 1572864 | tf_op jit(solution)/shard_map/all_to_all | solution.py:726
  24.2 0.1 broadcast_in_dim.85
  24.3 0.1 broadcast_in_dim.86
  24.4 0.1 broadcast_in_dim.91
  24.5 0.1 broadcast_in_dim.92
  24.6 0.1 broadcast_in_dim.96
  24.6 0.1 broadcast_in_dim.97
  24.7 0.1 broadcast_in_dim.101
  24.8 0.1 broadcast_in_dim.102
  24.9 0.8 tables.1
  25.7 0.0 collective-permute-done.1.refs_2_
  25.7 1.6 %collective-permute-done.2.refs_3_ = f32[392,128]{1,0:T(8,128)S(1)} collective-permute-done((f32[392,128]{1,0:T(8,128)}, f32[392,128]{1,0:T(8,128)S(1)}, u32[]{:S(2)}, u32[]{:S(2)}) %collective-permute-start.2) | collective-permute-done | bytes 200736 | tf_op jit(solution)/shard_map/ppermute | solution.py:678
  27.3 0.1 add_convert_fusion
  27.4 3.5 %stress.2 = (f32[3,16,32,128]{3,2,1,0:T(8,128)S(1)}, f32[3,16,32,256]{3,2,1,0:T(8,128)S(1)}, f32[3,4,32,128]{3,2,1,0:T(8,128)S(1)}, f32[3,4,32,128]{3,2,1,0:T(8,128)S(1)}) custom-call(s32[8]{0:T(128)S(1)} %copy-done.5, s32[16,8]{1,0:T(8,128)S(1)} %bitcast.26, f32[392,128]{1,0:T(8,128)S(1)} %copy-done.3, f32[392,128]{1,0:T(8,128)S(1)} %copy-done.1, ...), custom_call_target="tpu_custom_call" | custom-call | bytes 12582912 | tf_op jit(solution)/shard_map/stress/pallas_call | solution.py:353
  30.9 0.1 collective-permute-start.3
  31.0 1.4 %collective-permute-done.3 = f32[3,4,32,128]{3,2,1,0:T(8,128)S(1)} collective-permute-done((f32[3,4,32,128]{3,2,1,0:T(8,128)S(1)}, f32[3,4,32,128]{3,2,1,0:T(8,128)S(1)}, u32[]{:S(2)}, u32[]{:S(2)}) %collective-permute-start.3) | collective-permute-done | bytes 196640 | tf_op jit(solution)/shard_map/ppermute | solution.py:700
  32.4 1.6 %collective-permute-start.14 = (f32[3,4,32,128]{3,2,1,0:T(8,128)S(1)}, f32[3,4,32,128]{3,2,1,0:T(8,128)S(1)}, u32[]{:S(2)}, u32[]{:S(2)}) collective-permute-start(f32[3,4,32,128]{3,2,1,0:T(8,128)S(1)} %add.21.refs_4_.first_ref), channel_id=1, source_target_pairs={{0,2},{1,3},{2,0},{3,1},{4,6},{5,7},{6,4},{7,5},{8,10},{9,11},{10,... | collective-permute-start | bytes 589832 | tf_op jit(solution)/shard_map/ppermute | solution.py:700
  34.0 0.2 slice_reduce_fusion.count_ref
  34.2 3.0 %products.3._.forcing_ref = f32[3,8,32,128]{3,2,1,0:T(8,128)S(1)} custom-call(s32[8]{0:T(128)S(1)} %copy-done.5, s32[16,8]{1,0:T(8,128)S(1)} %bitcast.27, s32[16]{0:T(128)S(1)} %slice_reduce_fusion.count_ref, f32[3,16,32,256]{3,2,1,0:T(8,128)S(1)} %get-tuple-element.59.physical, bf16[256,256]{1,0:T(8,128)(2,1)S(1)} %get-tuple-element.42.refs_6_.refs_3_.back_ref, ...), custom_call_target="tpu_custom_call" | custom-call | bytes 12582912 | tf_op jit(solution)/shard_map/products/pallas_call | solution.py:418
  37.2 2.3 %collective-permute-done.14.second_ref = f32[3,4,32,128]{3,2,1,0:T(8,128)S(1)} collective-permute-done((f32[3,4,32,128]{3,2,1,0:T(8,128)S(1)}, f32[3,4,32,128]{3,2,1,0:T(8,128)S(1)}, u32[]{:S(2)}, u32[]{:S(2)}) %collective-permute-start.14) | collective-permute-done | bytes 196640 | tf_op jit(solution)/shard_map/ppermute | solution.py:700
  39.5 0.1 collective-permute-start.15
  39.6 1.4 %collective-permute-done.15.other_ref = f32[3,4,32,128]{3,2,1,0:T(8,128)S(1)} collective-permute-done((f32[3,4,32,128]{3,2,1,0:T(8,128)S(1)}, f32[3,4,32,128]{3,2,1,0:T(8,128)S(1)}, u32[]{:S(2)}, u32[]{:S(2)}) %collective-permute-start.15) | collective-permute-done | bytes 196640 | tf_op jit(solution)/shard_map/ppermute | solution.py:700
  41.0 1.9 %outgoing.3 = f32[1536,128]{1,0:T(8,128)} custom-call(s32[8]{0:T(128)S(1)} %copy-done.5, s32[16]{0:T(128)S(1)} %slice_reduce_fusion.count_ref, f32[3,16,32,128]{3,2,1,0:T(8,128)S(1)} %get-tuple-element.58.slotted_ref, f32[3,8,32,128]{3,2,1,0:T(8,128)S(1)} %products.3._.forcing_ref, f32[3,4,32,128]{3,2,1,0:T(8,128)S(1)} %ordered_sum.3.kept_ref, ...), custom_call_target="tpu_custom_call" | custom-call | bytes 1572864 | tf_op jit(solution)/shard_map/outgoing/pallas_call | solution.py:484
  42.9 7.8 %all-to-all-start.1 = ((f32[8,8,24,128]{3,2,1,0:T(8,128)}), f32[8,8,24,128]{3,2,1,0:T(8,128)S(1)}, u32[]{:S(2)}, u32[]{:S(2)}) async-start(f32[8,8,24,128]{3,2,1,0:T(8,128)} %bitcast.13), calls=%async_computation.1 | async-start | bytes 1572864 | tf_op jit(solution)/shard_map/all_to_all | solution.py:757
  50.7 3.5 %stress.3 = (f32[3,16,32,128]{3,2,1,0:T(8,128)S(1)}, f32[3,16,32,256]{3,2,1,0:T(8,128)S(1)}, f32[3,4,32,128]{3,2,1,0:T(8,128)S(1)}, f32[3,4,32,128]{3,2,1,0:T(8,128)S(1)}) custom-call(s32[8]{0:T(128)S(1)} %copy-done.5, s32[16,8]{1,0:T(8,128)S(1)} %bitcast.28, f32[4,384,128]{2,1,0:T(8,128)S(1)} %all-to-all-done.refs_0_, ...), custom_call_target="tpu_custom_call" | custom-call | bytes 12582912 | tf_op jit(solution)/shard_map/stress/pallas_call | solution.py:353
  54.2 0.1 collective-permute-start.4
  54.3 1.4 %collective-permute-done.4 = f32[3,4,32,128]{3,2,1,0:T(8,128)S(1)} collective-permute-done((f32[3,4,32,128]{3,2,1,0:T(8,128)S(1)}, f32[3,4,32,128]{3,2,1,0:T(8,128)S(1)}, u32[]{:S(2)}, u32[]{:S(2)}) %collective-permute-start.4) | collective-permute-done | bytes 196640 | tf_op jit(solution)/shard_map/ppermute | solution.py:700
  55.7 1.6 %collective-permute-start.5 = (f32[3,4,32,128]{3,2,1,0:T(8,128)S(1)}, f32[3,4,32,128]{3,2,1,0:T(8,128)S(1)}, u32[]{:S(2)}, u32[]{:S(2)}) collective-permute-start(f32[3,4,32,128]{3,2,1,0:T(8,128)S(1)} %add.22.first_ref), channel_id=1, source_target_pairs={{0,2},{1,3},{2,0},{3,1},{4,6},{5,7},{6,4},{7,5},{8,10},{9,11},{10,... | collective-permute-start | bytes 589832 | tf_op jit(solution)/shard_map/ppermute | solution.py:700
  57.3 3.0 %products.2._.forcing_ref = f32[3,8,32,128]{3,2,1,0:T(8,128)S(1)} custom-call(s32[8]{0:T(128)S(1)} %copy-done.5, s32[16,8]{1,0:T(8,128)S(1)} %bitcast.29, s32[16]{0:T(128)S(1)} %slice_reduce_fusion.count_ref, f32[3,16,32,256]{3,2,1,0:T(8,128)S(1)} %get-tuple-element.47.physical, bf16[256,256]{1,0:T(8,128)(2,1)S(1)} %get-tuple-element.42.refs_6_.refs_3_.back_ref, ...), custom_call_target="tpu_custom_call" | custom-call | bytes 12582912 | tf_op jit(solution)/shard_map/products/pallas_call | solution.py:418
  60.3 2.4 %collective-permute-done.5.second_ref = f32[3,4,32,128]{3,2,1,0:T(8,128)S(1)} collective-permute-done((f32[3,4,32,128]{3,2,1,0:T(8,128)S(1)}, f32[3,4,32,128]{3,2,1,0:T(8,128)S(1)}, u32[]{:S(2)}, u32[]{:S(2)}) %collective-permute-start.5) | collective-permute-done | bytes 196640 | tf_op jit(solution)/shard_map/ppermute | solution.py:700
  62.8 0.1 collective-permute-start.6
  62.8 1.4 %collective-permute-done.6.other_ref = f32[3,4,32,128]{3,2,1,0:T(8,128)S(1)} collective-permute-done((f32[3,4,32,128]{3,2,1,0:T(8,128)S(1)}, f32[3,4,32,128]{3,2,1,0:T(8,128)S(1)}, u32[]{:S(2)}, u32[]{:S(2)}) %collective-permute-start.6) | collective-permute-done | bytes 196640 | tf_op jit(solution)/shard_map/ppermute | solution.py:700
  64.3 1.2 outgoing.2
  65.5 3.0 %collective-permute-start.7 = (f32[8,24,128]{2,1,0:T(8,128)S(1)}, f32[8,24,128]{2,1,0:T(8,128)S(1)}, u32[]{:S(2)}, u32[]{:S(2)}) collective-permute-start(f32[8,24,128]{2,1,0:T(8,128)S(1)} %bitcast.45), channel_id=1, source_target_pairs={{0,16},{1,5},{2,18},{3,7},{4,20},{5,1},{6,22},{7,3},{8,24},{9,13},... | collective-permute-start | bytes 294920 | tf_op jit(solution)/shard_map/ppermute | solution.py:678
  68.5 1.5 %collective-permute-start.8 = (f32[8,24,128]{2,1,0:T(8,128)S(1)}, f32[8,24,128]{2,1,0:T(8,128)S(1)}, u32[]{:S(2)}, u32[]{:S(2)}) collective-permute-start(f32[8,24,128]{2,1,0:T(8,128)S(1)} %bitcast.44), channel_id=1, source_target_pairs={{0,4},{1,17},{2,6},{3,19},{4,0},{5,21},{6,2},{7,23},{8,12},{9,25},... | collective-permute-start | bytes 294920 | tf_op jit(solution)/shard_map/ppermute | solution.py:678
  69.9 1.5 %collective-permute-start.9 = (f32[8,24,128]{2,1,0:T(8,128)S(1)}, f32[8,24,128]{2,1,0:T(8,128)S(1)}, u32[]{:S(2)}, u32[]{:S(2)}) collective-permute-start(f32[8,24,128]{2,1,0:T(8,128)S(1)} %bitcast.43), channel_id=1, source_target_pairs={{0,8},{1,25},{2,10},{3,27},{4,12},{5,29},{6,14},{7,31},{8,0},{9,17... | collective-permute-start | bytes 294920 | tf_op jit(solution)/shard_map/ppermute | solution.py:678
  71.4 0.6 collective-permute-start.10
  71.9 1.5 %collective-permute-start.11 = (f32[8,24,128]{2,1,0:T(8,128)S(1)}, f32[8,24,128]{2,1,0:T(8,128)S(1)}, u32[]{:S(2)}, u32[]{:S(2)}) collective-permute-start(f32[8,24,128]{2,1,0:T(8,128)S(1)} %bitcast.41), channel_id=1, source_target_pairs={{0,20},{1,13},{2,22},{3,15},{4,16},{5,9},{6,18},{7,11},{8,28},{9,5... | collective-permute-start | bytes 294920 | tf_op jit(solution)/shard_map/ppermute | solution.py:678
  73.4 3.3 %collective-permute-done.7.refs_1_ = f32[8,24,128]{2,1,0:T(8,128)S(1)} collective-permute-done((f32[8,24,128]{2,1,0:T(8,128)S(1)}, f32[8,24,128]{2,1,0:T(8,128)S(1)}, u32[]{:S(2)}, u32[]{:S(2)}) %collective-permute-start.7) | collective-permute-done | bytes 98336 | tf_op jit(solution)/shard_map/ppermute | solution.py:678
  76.7 0.4 collective-permute-start.12
  77.1 3.1 %collective-permute-start.13 = (f32[8,24,128]{2,1,0:T(8,128)S(1)}, f32[8,24,128]{2,1,0:T(8,128)S(1)}, u32[]{:S(2)}, u32[]{:S(2)}) collective-permute-start(f32[8,24,128]{2,1,0:T(8,128)S(1)} %bitcast.39), channel_id=1, source_target_pairs={{0,28},{1,29},{2,30},{3,31},{4,24},{5,25},{6,26},{7,27},{8,20},{9,... | collective-permute-start | bytes 294920 | tf_op jit(solution)/shard_map/ppermute | solution.py:678
  80.2 0.0 all-to-all-done.1.refs_0_
  80.2 4.1 %solve.2.refs_9_ = f32[8,512,128]{2,1,0:T(8,128)S(1)} custom-call(f32[8,8,24,128]{3,2,1,0:T(8,128)S(1)} %all-to-all-done.1.refs_0_, f32[8,512,512]{2,1,0:T(8,128)} %refs_8_.1), custom_call_target="tpu_custom_call" | custom-call | bytes 8388608 | tf_op jit(solution)/shard_map/solve/pallas_call | solution.py:616
  84.3 0.0 collective-permute-done.9.refs_3_
  84.3 3.5 %collective-permute-done.11.refs_5_ = f32[8,24,128]{2,1,0:T(8,128)S(1)} collective-permute-done((f32[8,24,128]{2,1,0:T(8,128)S(1)}, f32[8,24,128]{2,1,0:T(8,128)S(1)}, u32[]{:S(2)}, u32[]{:S(2)}) %collective-permute-start.11) | collective-permute-done | bytes 98336 | tf_op jit(solution)/shard_map/ppermute | solution.py:678
  87.8 0.0 collective-permute-done.12.refs_6_
  87.8 4.6 %solve.3 = (f32[8,2,24,128]{3,2,1,0:T(8,128)S(1)}, f32[8,2,24,128]{3,2,1,0:T(8,128)S(1)}, f32[8,2,24,128]{3,2,1,0:T(8,128)S(1)}, f32[8,2,24,128]{3,2,1,0:T(8,128...) custom-call(f32[8,24,128]{2,1,0:T(8,128)S(1)} %bitcast.38, ...), custom_call_target="tpu_custom_call" | custom-call | bytes 8388608 | tf_op jit(solution)/shard_map/solve/pallas_call | solution.py:616
  92.4 2.4 %collective-permute-start.16 = (f32[8,2,24,128]{3,2,1,0:T(8,128)S(1)}, f32[8,2,24,128]{3,2,1,0:T(8,128)S(1)}, u32[]{:S(2)}, u32[]{:S(2)}) collective-permute-start(f32[8,2,24,128]{3,2,1,0:T(8,128)S(1)} %get-tuple-element.61), channel_id=1, source_target_pairs={{0,16},{1,5},{2,18},{3,7},{4,20},{5,1},{6,22},{7,3},{8,24},{9,13},... | collective-permute-start | bytes 589832 | tf_op jit(solution)/shard_map/ppermute | solution.py:678
  94.8 1.1 collective-permute-start.17
  95.9 2.6 %collective-permute-start.19 = (f32[8,2,24,128]{3,2,1,0:T(8,128)S(1)}, f32[8,2,24,128]{3,2,1,0:T(8,128)S(1)}, u32[]{:S(2)}, u32[]{:S(2)}) collective-permute-start(f32[8,2,24,128]{3,2,1,0:T(8,128)S(1)} %get-tuple-element.64), channel_id=1, source_target_pairs={{0,24},{1,9},{2,26},{3,11},{4,28},{5,13},{6,30},{7,15},{8,16},{9,1... | collective-permute-start | bytes 589832 | tf_op jit(solution)/shard_map/ppermute | solution.py:678
  98.5 1.3 collective-permute-start.20
  99.8 8.7 %collective-permute-done.16 = f32[8,2,24,128]{3,2,1,0:T(8,128)S(1)} collective-permute-done((f32[8,2,24,128]{3,2,1,0:T(8,128)S(1)}, f32[8,2,24,128]{3,2,1,0:T(8,128)S(1)}, u32[]{:S(2)}, u32[]{:S(2)}) %collective-permute-start.16) | collective-permute-done | bytes 196640 | tf_op jit(solution)/shard_map/ppermute | solution.py:678
  108.4 1.7 %collective-permute-start.22 = (f32[8,2,24,128]{3,2,1,0:T(8,128)S(1)}, f32[8,2,24,128]{3,2,1,0:T(8,128)S(1)}, u32[]{:S(2)}, u32[]{:S(2)}) collective-permute-start(f32[8,2,24,128]{3,2,1,0:T(8,128)S(1)} %get-tuple-element.67), channel_id=1, source_target_pairs={{0,28},{1,29},{2,30},{3,31},{4,24},{5,25},{6,26},{7,27},{8,20},{9,... | collective-permute-start | bytes 589832 | tf_op jit(solution)/shard_map/ppermute | solution.py:678
  110.1 1.9 %collective-permute-done.18 = f32[8,2,24,128]{3,2,1,0:T(8,128)S(1)} collective-permute-done((f32[8,2,24,128]{3,2,1,0:T(8,128)S(1)}, f32[8,2,24,128]{3,2,1,0:T(8,128)S(1)}, u32[]{:S(2)}, u32[]{:S(2)}) %collective-permute-start.18) | collective-permute-done | bytes 196640 | tf_op jit(solution)/shard_map/ppermute | solution.py:678
  112.1 14.9 %collective-permute-done.20 = f32[8,2,24,128]{3,2,1,0:T(8,128)S(1)} collective-permute-done((f32[8,2,24,128]{3,2,1,0:T(8,128)S(1)}, f32[8,2,24,128]{3,2,1,0:T(8,128)S(1)}, u32[]{:S(2)}, u32[]{:S(2)}) %collective-permute-start.20) | collective-permute-done | bytes 196640 | tf_op jit(solution)/shard_map/ppermute | solution.py:678
  127.0 2.1 %restore.1 = f32[3,4,256,128]{3,2,1,0:T(8,128)} custom-call(f32[384,128]{1,0:T(8,128)S(1)} %bitcast.30, f32[384,128]{1,0:T(8,128)S(1)} %bitcast.31, f32[384,128]{1,0:T(8,128)S(1)} %bitcast.32, f32[384,128]{1,0:T(8,128)S(1)} %bitcast.33, f32[384,128]{1,0:T(8,128)S(1)} %bitcast.34, f32[384,128]{1,0:T(8,128)S(1)} %bitcast.35, f32[384,128]{1,0:T(8,128)S(1)} %bitcast.36, ...), custom_call_target="tpu_custom_call" | custom-call | bytes 3145728 | tf_op jit(solution)/shard_map/restore/pallas_call | solution.py:656
  (38 shorter events, 0.2 us)
Async XLA Ops:
  2.1 9.8 %collective-permute-start = (f32[392,128]{1,0:T(8,128)}, f32[392,128]{1,0:T(8,128)S(1)}, u32[]{:S(2)}, u32[]{:S(2)}) collective-permute-start(f32[392,128]{1,0:T(8,128)} %get-tuple-element.38), channel_id=1, source_target_pairs={{0,8},{1,25},{2,10},{3,27},{8,0},{9,17},{10,2},{11,19},{16,24},{17... | collective-permute-start | bytes 602120 | tf_op jit(solution)/shard_map/ppermute | solution.py:678
  5.1 20.6 %collective-permute-start.1 = (f32[392,128]{1,0:T(8,128)}, f32[392,128]{1,0:T(8,128)S(1)}, u32[]{:S(2)}, u32[]{:S(2)}) collective-permute-start(f32[392,128]{1,0:T(8,128)} %get-tuple-element.39), channel_id=1, source_target_pairs={{0,24},{1,9},{2,26},{3,11},{8,16},{9,1},{10,18},{11,3},{16,8},{17,... | collective-permute-start | bytes 602120 | tf_op jit(solution)/shard_map/ppermute | solution.py:678
  7.6 19.7 %collective-permute-start.2 = (f32[392,128]{1,0:T(8,128)}, f32[392,128]{1,0:T(8,128)S(1)}, u32[]{:S(2)}, u32[]{:S(2)}) collective-permute-start(f32[392,128]{1,0:T(8,128)} %get-tuple-element.40), channel_id=1, source_target_pairs={{0,16},{1,17},{2,18},{3,19},{8,24},{9,25},{10,26},{11,27},{16,0},{... | collective-permute-start | bytes 602120 | tf_op jit(solution)/shard_map/ppermute | solution.py:678
  7.7 17.2 %copy-start.3 = (f32[392,128]{1,0:T(8,128)S(1)}, f32[392,128]{1,0:T(8,128)}, u32[]{:S(2)}) copy-start(f32[392,128]{1,0:T(8,128)} %get-tuple-element.37.refs_0_) | copy-start | bytes 602116
  7.7 17.2 %copy-start.2 = (bf16[128,256]{1,0:T(8,128)(2,1)S(1)}, bf16[128,256]{1,0:T(8,128)(2,1)}, u32[]{:S(2)}) copy-start(bf16[128,256]{1,0:T(8,128)(2,1)} %constant.22.clone.rest_ref.refs_5_.refs_2_) | copy-start | bytes 196612
  7.7 17.2 %copy-start.4 = (bf16[128,256]{1,0:T(8,128)(2,1)S(1)}, bf16[128,256]{1,0:T(8,128)(2,1)}, u32[]{:S(2)}) copy-start(bf16[128,256]{1,0:T(8,128)(2,1)} %constant.21.clone.top_ref) | copy-start | bytes 196612
  7.7 17.2 %copy-start.6 = (s32[64]{0:T(128)S(1)}, s32[64]{0:T(128)}, u32[]{:S(2)}) copy-start(s32[64]{0:T(128)} %owner_ref.1) | copy-start | bytes 772
  7.7 19.7 %copy-start.5 = (s32[8]{0:T(128)S(1)}, s32[8]{0:T(128)}, u32[]{:S(2)}) copy-start(s32[8]{0:T(128)} %low_ref.11) | copy-start | bytes 100
  11.9 0.7 copy-start
  14.7 11.0 %copy-start.1 = (f32[392,128]{1,0:T(8,128)S(1)}, f32[392,128]{1,0:T(8,128)}, u32[]{:S(2)}) copy-start(f32[392,128]{1,0:T(8,128)} %copy-done) | copy-start | bytes 602116
  14.7 28.2 %all-to-all-start = ((f32[4,384,128]{2,1,0:T(8,128)}), f32[4,384,128]{2,1,0:T(8,128)S(1)}, u32[]{:S(2)}, u32[]{:S(2)}) async-start(f32[4,384,128]{2,1,0:T(8,128)} %pack.1), calls=%async_computation | async-start | bytes 1572864 | tf_op jit(solution)/shard_map/all_to_all | solution.py:726
  30.9 1.5 %collective-permute-start.3 = (f32[3,4,32,128]{3,2,1,0:T(8,128)S(1)}, f32[3,4,32,128]{3,2,1,0:T(8,128)S(1)}, u32[]{:S(2)}, u32[]{:S(2)}) collective-permute-start(f32[3,4,32,128]{3,2,1,0:T(8,128)S(1)} %get-tuple-element.45), channel_id=1, source_target_pairs={{0,1},{1,0},{2,3},{3,2},{4,5},{5,4},{6,7},{7,6},{8,9},{9,8},{10,11... | collective-permute-start | bytes 589832 | tf_op jit(solution)/shard_map/ppermute | solution.py:700
  32.4 7.0 %collective-permute-start.14 = (f32[3,4,32,128]{3,2,1,0:T(8,128)S(1)}, f32[3,4,32,128]{3,2,1,0:T(8,128)S(1)}, u32[]{:S(2)}, u32[]{:S(2)}) collective-permute-start(f32[3,4,32,128]{3,2,1,0:T(8,128)S(1)} %add.21.refs_4_.first_ref), channel_id=1, source_target_pairs={{0,2},{1,3},{2,0},{3,1},{4,6},{5,7},{6,4},{7,5},{8,10},{9,11},{10,... | collective-permute-start | bytes 589832 | tf_op jit(solution)/shard_map/ppermute | solution.py:700
  39.5 1.5 %collective-permute-start.15 = (f32[3,4,32,128]{3,2,1,0:T(8,128)S(1)}, f32[3,4,32,128]{3,2,1,0:T(8,128)S(1)}, u32[]{:S(2)}, u32[]{:S(2)}) collective-permute-start(f32[3,4,32,128]{3,2,1,0:T(8,128)S(1)} %ordered_sum.3.kept_ref), channel_id=1, source_target_pairs={{0,1},{1,0},{2,3},{3,2},{4,5},{5,4},{6,7},{7,6},{8,9},{9,8},{10,11... | collective-permute-start | bytes 589832 | tf_op jit(solution)/shard_map/ppermute | solution.py:700
  42.9 37.3 %all-to-all-start.1 = ((f32[8,8,24,128]{3,2,1,0:T(8,128)}), f32[8,8,24,128]{3,2,1,0:T(8,128)S(1)}, u32[]{:S(2)}, u32[]{:S(2)}) async-start(f32[8,8,24,128]{3,2,1,0:T(8,128)} %bitcast.13), calls=%async_computation.1 | async-start | bytes 1572864 | tf_op jit(solution)/shard_map/all_to_all | solution.py:757
  54.2 1.5 %collective-permute-start.4 = (f32[3,4,32,128]{3,2,1,0:T(8,128)S(1)}, f32[3,4,32,128]{3,2,1,0:T(8,128)S(1)}, u32[]{:S(2)}, u32[]{:S(2)}) collective-permute-start(f32[3,4,32,128]{3,2,1,0:T(8,128)S(1)} %get-tuple-element.49), channel_id=1, source_target_pairs={{0,1},{1,0},{2,3},{3,2},{4,5},{5,4},{6,7},{7,6},{8,9},{9,8},{10,11... | collective-permute-start | bytes 589832 | tf_op jit(solution)/shard_map/ppermute | solution.py:700
  55.7 7.0 %collective-permute-start.5 = (f32[3,4,32,128]{3,2,1,0:T(8,128)S(1)}, f32[3,4,32,128]{3,2,1,0:T(8,128)S(1)}, u32[]{:S(2)}, u32[]{:S(2)}) collective-permute-start(f32[3,4,32,128]{3,2,1,0:T(8,128)S(1)} %add.22.first_ref), channel_id=1, source_target_pairs={{0,2},{1,3},{2,0},{3,1},{4,6},{5,7},{6,4},{7,5},{8,10},{9,11},{10,... | collective-permute-start | bytes 589832 | tf_op jit(solution)/shard_map/ppermute | solution.py:700
  62.8 1.5 %collective-permute-start.6 = (f32[3,4,32,128]{3,2,1,0:T(8,128)S(1)}, f32[3,4,32,128]{3,2,1,0:T(8,128)S(1)}, u32[]{:S(2)}, u32[]{:S(2)}) collective-permute-start(f32[3,4,32,128]{3,2,1,0:T(8,128)S(1)} %ordered_sum.2.kept_ref), channel_id=1, source_target_pairs={{0,1},{1,0},{2,3},{3,2},{4,5},{5,4},{6,7},{7,6},{8,9},{9,8},{10,11... | collective-permute-start | bytes 589832 | tf_op jit(solution)/shard_map/ppermute | solution.py:700
  65.5 11.2 %collective-permute-start.7 = (f32[8,24,128]{2,1,0:T(8,128)S(1)}, f32[8,24,128]{2,1,0:T(8,128)S(1)}, u32[]{:S(2)}, u32[]{:S(2)}) collective-permute-start(f32[8,24,128]{2,1,0:T(8,128)S(1)} %bitcast.45), channel_id=1, source_target_pairs={{0,16},{1,5},{2,18},{3,7},{4,20},{5,1},{6,22},{7,3},{8,24},{9,13},... | collective-permute-start | bytes 294920 | tf_op jit(solution)/shard_map/ppermute | solution.py:678
  68.5 8.7 %collective-permute-start.8 = (f32[8,24,128]{2,1,0:T(8,128)S(1)}, f32[8,24,128]{2,1,0:T(8,128)S(1)}, u32[]{:S(2)}, u32[]{:S(2)}) collective-permute-start(f32[8,24,128]{2,1,0:T(8,128)S(1)} %bitcast.44), channel_id=1, source_target_pairs={{0,4},{1,17},{2,6},{3,19},{4,0},{5,21},{6,2},{7,23},{8,12},{9,25},... | collective-permute-start | bytes 294920 | tf_op jit(solution)/shard_map/ppermute | solution.py:678
  69.9 14.4 %collective-permute-start.9 = (f32[8,24,128]{2,1,0:T(8,128)S(1)}, f32[8,24,128]{2,1,0:T(8,128)S(1)}, u32[]{:S(2)}, u32[]{:S(2)}) collective-permute-start(f32[8,24,128]{2,1,0:T(8,128)S(1)} %bitcast.43), channel_id=1, source_target_pairs={{0,8},{1,25},{2,10},{3,27},{4,12},{5,29},{6,14},{7,31},{8,0},{9,17... | collective-permute-start | bytes 294920 | tf_op jit(solution)/shard_map/ppermute | solution.py:678
  71.4 12.9 %collective-permute-start.10 = (f32[8,24,128]{2,1,0:T(8,128)S(1)}, f32[8,24,128]{2,1,0:T(8,128)S(1)}, u32[]{:S(2)}, u32[]{:S(2)}) collective-permute-start(f32[8,24,128]{2,1,0:T(8,128)S(1)} %bitcast.42), channel_id=1, source_target_pairs={{0,24},{1,9},{2,26},{3,11},{4,28},{5,13},{6,30},{7,15},{8,16},{9,1... | collective-permute-start | bytes 294920 | tf_op jit(solution)/shard_map/ppermute | solution.py:678
  71.9 15.9 %collective-permute-start.11 = (f32[8,24,128]{2,1,0:T(8,128)S(1)}, f32[8,24,128]{2,1,0:T(8,128)S(1)}, u32[]{:S(2)}, u32[]{:S(2)}) collective-permute-start(f32[8,24,128]{2,1,0:T(8,128)S(1)} %bitcast.41), channel_id=1, source_target_pairs={{0,20},{1,13},{2,22},{3,15},{4,16},{5,9},{6,18},{7,11},{8,28},{9,5... | collective-permute-start | bytes 294920 | tf_op jit(solution)/shard_map/ppermute | solution.py:678
  76.7 11.1 %collective-permute-start.12 = (f32[8,24,128]{2,1,0:T(8,128)S(1)}, f32[8,24,128]{2,1,0:T(8,128)S(1)}, u32[]{:S(2)}, u32[]{:S(2)}) collective-permute-start(f32[8,24,128]{2,1,0:T(8,128)S(1)} %bitcast.40), channel_id=1, source_target_pairs={{0,12},{1,21},{2,14},{3,23},{4,8},{5,17},{6,10},{7,19},{8,4},{9,29... | collective-permute-start | bytes 294920 | tf_op jit(solution)/shard_map/ppermute | solution.py:678
  77.1 10.7 %collective-permute-start.13 = (f32[8,24,128]{2,1,0:T(8,128)S(1)}, f32[8,24,128]{2,1,0:T(8,128)S(1)}, u32[]{:S(2)}, u32[]{:S(2)}) collective-permute-start(f32[8,24,128]{2,1,0:T(8,128)S(1)} %bitcast.39), channel_id=1, source_target_pairs={{0,28},{1,29},{2,30},{3,31},{4,24},{5,25},{6,26},{7,27},{8,20},{9,... | collective-permute-start | bytes 294920 | tf_op jit(solution)/shard_map/ppermute | solution.py:678
  92.4 16.0 %collective-permute-start.16 = (f32[8,2,24,128]{3,2,1,0:T(8,128)S(1)}, f32[8,2,24,128]{3,2,1,0:T(8,128)S(1)}, u32[]{:S(2)}, u32[]{:S(2)}) collective-permute-start(f32[8,2,24,128]{3,2,1,0:T(8,128)S(1)} %get-tuple-element.61), channel_id=1, source_target_pairs={{0,16},{1,5},{2,18},{3,7},{4,20},{5,1},{6,22},{7,3},{8,24},{9,13},... | collective-permute-start | bytes 589832 | tf_op jit(solution)/shard_map/ppermute | solution.py:678
  94.8 13.6 %collective-permute-start.17 = (f32[8,2,24,128]{3,2,1,0:T(8,128)S(1)}, f32[8,2,24,128]{3,2,1,0:T(8,128)S(1)}, u32[]{:S(2)}, u32[]{:S(2)}) collective-permute-start(f32[8,2,24,128]{3,2,1,0:T(8,128)S(1)} %get-tuple-element.62), channel_id=1, source_target_pairs={{0,4},{1,17},{2,6},{3,19},{4,0},{5,21},{6,2},{7,23},{8,12},{9,25},... | collective-permute-start | bytes 589832 | tf_op jit(solution)/shard_map/ppermute | solution.py:678
  95.9 16.2 %collective-permute-start.18 = (f32[8,2,24,128]{3,2,1,0:T(8,128)S(1)}, f32[8,2,24,128]{3,2,1,0:T(8,128)S(1)}, u32[]{:S(2)}, u32[]{:S(2)}) collective-permute-start(f32[8,2,24,128]{3,2,1,0:T(8,128)S(1)} %get-tuple-element.63), channel_id=1, source_target_pairs={{0,8},{1,25},{2,10},{3,27},{4,12},{5,29},{6,14},{7,31},{8,0},{9,17... | collective-permute-start | bytes 589832 | tf_op jit(solution)/shard_map/ppermute | solution.py:678
  95.9 16.2 %collective-permute-start.19 = (f32[8,2,24,128]{3,2,1,0:T(8,128)S(1)}, f32[8,2,24,128]{3,2,1,0:T(8,128)S(1)}, u32[]{:S(2)}, u32[]{:S(2)}) collective-permute-start(f32[8,2,24,128]{3,2,1,0:T(8,128)S(1)} %get-tuple-element.64), channel_id=1, source_target_pairs={{0,24},{1,9},{2,26},{3,11},{4,28},{5,13},{6,30},{7,15},{8,16},{9,1... | collective-permute-start | bytes 589832 | tf_op jit(solution)/shard_map/ppermute | solution.py:678
  98.5 28.5 %collective-permute-start.20 = (f32[8,2,24,128]{3,2,1,0:T(8,128)S(1)}, f32[8,2,24,128]{3,2,1,0:T(8,128)S(1)}, u32[]{:S(2)}, u32[]{:S(2)}) collective-permute-start(f32[8,2,24,128]{3,2,1,0:T(8,128)S(1)} %get-tuple-element.65), channel_id=1, source_target_pairs={{0,20},{1,13},{2,22},{3,15},{4,16},{5,9},{6,18},{7,11},{8,28},{9,5... | collective-permute-start | bytes 589832 | tf_op jit(solution)/shard_map/ppermute | solution.py:678
  108.4 18.5 %collective-permute-start.21 = (f32[8,2,24,128]{3,2,1,0:T(8,128)S(1)}, f32[8,2,24,128]{3,2,1,0:T(8,128)S(1)}, u32[]{:S(2)}, u32[]{:S(2)}) collective-permute-start(f32[8,2,24,128]{3,2,1,0:T(8,128)S(1)} %get-tuple-element.66), channel_id=1, source_target_pairs={{0,12},{1,21},{2,14},{3,23},{4,8},{5,17},{6,10},{7,19},{8,4},{9,29... | collective-permute-start | bytes 589832 | tf_op jit(solution)/shard_map/ppermute | solution.py:678
  108.4 18.5 %collective-permute-start.22 = (f32[8,2,24,128]{3,2,1,0:T(8,128)S(1)}, f32[8,2,24,128]{3,2,1,0:T(8,128)S(1)}, u32[]{:S(2)}, u32[]{:S(2)}) collective-permute-start(f32[8,2,24,128]{3,2,1,0:T(8,128)S(1)} %get-tuple-element.67), channel_id=1, source_target_pairs={{0,28},{1,29},{2,30},{3,31},{4,24},{5,25},{6,26},{7,27},{8,20},{9,... | collective-permute-start | bytes 589832 | tf_op jit(solution)/shard_map/ppermute | solution.py:678

commit v16 on v15

--- a/solution.py
+++ b/solution.py
@@ -187,7 +187,7 @@
     )(neighbours, mode_counts, velocity)
 
 
-def pack_kernel(velocity_ref, _, out_ref):
+def pack_kernel(velocity_ref, out_ref):
     chunks, _, kx_count, rows, columns = velocity_ref.shape
     for index in range(kx_count):
         for chunk in range(chunks):
@@ -195,7 +195,7 @@
             out_ref[index, place] = velocity_ref[chunk, 0, index]
 
 
-def pack(velocity, piece, after):
+def pack(velocity, piece):
     chunks, _, kx_count, rows, columns = velocity.shape
     shape = (kx_count, chunks * rows, columns)
     return pl.pallas_call(
@@ -204,12 +204,27 @@
         grid=(1,),
         in_specs=[
             pl.BlockSpec((chunks, 1, kx_count, rows, columns), lambda i: (0, piece, 0, 0, 0)),
-            pl.BlockSpec(memory_space=pl.ANY),
         ],
         out_specs=pl.BlockSpec(shape, lambda i: (0, 0, 0)),
         cost_estimate=cost(4 * velocity.size),
         name="pack",
-    )(velocity, after)
+    )(velocity)
+
+
+def hand_on_kernel(value_ref, after_ref, out_ref):
+    pass
+
+
+def hand_on(value, after):
+    return pl.pallas_call(
+        hand_on_kernel,
+        out_shape=jax.ShapeDtypeStruct(value.shape, value.dtype),
+        in_specs=[pl.BlockSpec(memory_space=pl.ANY)] * 2,
+        out_specs=pl.BlockSpec(memory_space=pl.ANY),
+        input_output_aliases={0: 0},
+        cost_estimate=cost(0),
+        name="hand_on",
+    )(value, after)
 
 
 def tables_kernel(owner_ref, top_ref, rest_ref, first_ref, back_ref, order_ref, slot_ref):
@@ -722,7 +737,7 @@
     blocks = pack_first(split, neighbours, mode_counts, extra_rows)
     parts = [exchange(blocks, ("kx",))]
     for piece in range(1, pieces):
-        block = pack(split, piece, parts[0][1])
+        block = hand_on(pack(split, piece), parts[0][min(2, kx_count - 1)])
         block = lax.all_to_all(block, "kx", split_axis=0, concat_axis=0, tiled=True)
         parts.append((block,))
     tables, order, slot_modes = slot_tables(owner_map, columns)

time: 131 us -> 130 us (level)
  no operation moved by 1% of the time
where the time goes in v16:
time: 130 us; the launch traced here: 129 us
  starting transfers between devices  47.6 us (37%)
  waiting for transfers between devices  47.4 us (36%)
  Pallas kernels  31.7 us (24%)
  local copies, waits for them, and re-layouts  1.56 us (1%)
    ppermute x17, waiting for transfers between devices, exchange(): result[position] = lax.ppermute(blocks[position], axes + ('real',), pairs)  37 us
    ppermute x17, starting transfers between devices, exchange(): result[position] = lax.ppermute(blocks[position], axes + ('real',), pairs)  26.4 us
    all_to_all x1, starting transfers between devices, local(): block = lax.all_to_all(block, 'kx', split_axis=0, concat_axis=0, tiled=True)  10.8 us
    ppermute x6, waiting for transfers between devices, swap(): return lax.ppermute(value, 'real', pairs)  10.4 us
    pallas_call x2, Pallas kernels, solve(): pl.pallas_call(functools.partial(solve_kernel, groups=groups, kx_count=kx...  8.62 us
    pallas_call x2, Pallas kernels, stress_terms(): pl.pallas_call(stress_kernel, out_shape=(jax.ShapeDtypeStruct(shape, jnp....  6.94 us
    all_to_all x1, starting transfers between devices, local(): lax.all_to_all(block, ('kx', 'ht'), split_axis=0, concat_axis=0, tiled=True)  6.91 us
    pallas_call x2, Pallas kernels, high_terms(): pl.pallas_call(products_kernel, out_shape=jax.ShapeDtypeStruct((component...  6 us
  transfers between devices with their start and end apart: 25, of which 13 were waited for; matrix products, arithmetic and copies ran while one was open for 1% of the time, Pallas kernels for 18%

profile of v16, /device:TPU:0, one launch (start us, length us, event | category | flops | bytes accessed | tf_op | source)
XLA Modules:
  0.0 128.6 jit_solution(3133351592852768781)
XLA Ops:
  0.0 2.1 %pack_first.1 = (f32[392,128]{1,0:T(8,128)}, f32[392,128]{1,0:T(8,128)}, f32[392,128]{1,0:T(8,128)}, f32[392,128]{1,0:T(8,128)}) custom-call(s32[4,8]{1,0:T(4,128)} %near_ref.1, s32[4]{0:T(128)} %count_ref.1, f32[12,2,4,32,128]{4,3,2,1,0:T(8,128)} %bitcast.46), custom_call_target="tpu_custom_call" | custom-call | bytes 1572864 | tf_op jit(solution)/shard_map/pack_first/pallas_call | solution.py:175
  2.1 5.0 %collective-permute-start.1 = (f32[392,128]{1,0:T(8,128)}, f32[392,128]{1,0:T(8,128)S(1)}, u32[]{:S(2)}, u32[]{:S(2)}) collective-permute-start(f32[392,128]{1,0:T(8,128)} %get-tuple-element.39), channel_id=1, source_target_pairs={{0,24},{1,9},{2,26},{3,11},{8,16},{9,1},{10,18},{11,3},{16,8},{17,... | collective-permute-start | bytes 602120 | tf_op jit(solution)/shard_map/ppermute | solution.py:693
  7.2 0.0 collective-permute-start
  7.2 0.6 collective-permute-start.2
  7.7 2.1 %pack.1.value_ref = f32[4,384,128]{2,1,0:T(8,128)} custom-call(f32[12,2,4,32,128]{4,3,2,1,0:T(8,128)} %bitcast.47), custom_call_target="tpu_custom_call" | custom-call | bytes 1572864 | tf_op jit(solution)/shard_map/pack/pallas_call | solution.py:201
  9.8 0.0 copy-start.5
  9.8 3.5 %collective-permute-done.1.after_ref.refs_2_ = f32[392,128]{1,0:T(8,128)S(1)} collective-permute-done((f32[392,128]{1,0:T(8,128)}, f32[392,128]{1,0:T(8,128)S(1)}, u32[]{:S(2)}, u32[]{:S(2)}) %collective-permute-start.1) | collective-permute-done | bytes 200736 | tf_op jit(solution)/shard_map/ppermute | solution.py:693
  13.3 0.7 copy-done
  14.0 10.8 %all-to-all-start = ((f32[4,384,128]{2,1,0:T(8,128)}), f32[4,384,128]{2,1,0:T(8,128)S(1)}, u32[]{:S(2)}, u32[]{:S(2)}) async-start(f32[4,384,128]{2,1,0:T(8,128)} %hand_on.1), calls=%async_computation | async-start | bytes 1572864 | tf_op jit(solution)/shard_map/all_to_all | solution.py:741
  24.8 0.1 broadcast_in_dim.85
  24.8 0.1 broadcast_in_dim.86
  24.9 0.1 broadcast_in_dim.91
  25.0 0.1 broadcast_in_dim.92
  25.1 0.1 broadcast_in_dim.96
  25.2 0.1 broadcast_in_dim.97
  25.3 0.1 broadcast_in_dim.101
  25.4 0.1 broadcast_in_dim.102
  25.5 0.8 tables.1
  26.3 0.0 collective-permute-done.refs_1_
  26.3 1.5 %collective-permute-done.2.refs_3_ = f32[392,128]{1,0:T(8,128)S(1)} collective-permute-done((f32[392,128]{1,0:T(8,128)}, f32[392,128]{1,0:T(8,128)S(1)}, u32[]{:S(2)}, u32[]{:S(2)}) %collective-permute-start.2) | collective-permute-done | bytes 200736 | tf_op jit(solution)/shard_map/ppermute | solution.py:693
  27.8 0.1 add_convert_fusion
  27.9 3.5 %stress.2 = (f32[3,16,32,128]{3,2,1,0:T(8,128)S(1)}, f32[3,16,32,256]{3,2,1,0:T(8,128)S(1)}, f32[3,4,32,128]{3,2,1,0:T(8,128)S(1)}, f32[3,4,32,128]{3,2,1,0:T(8,128)S(1)}) custom-call(s32[8]{0:T(128)S(1)} %copy-done.5, s32[16,8]{1,0:T(8,128)S(1)} %bitcast.26, f32[392,128]{1,0:T(8,128)S(1)} %copy-done.3, f32[392,128]{1,0:T(8,128)S(1)} %collective-permute-done.refs_1_, ...), custom_call_target="tpu_custom_call" | custom-call | bytes 12582912 | tf_op jit(solution)/shard_map/stress/pallas_call | solution.py:368
  31.4 0.1 collective-permute-start.3
  31.5 1.4 %collective-permute-done.3 = f32[3,4,32,128]{3,2,1,0:T(8,128)S(1)} collective-permute-done((f32[3,4,32,128]{3,2,1,0:T(8,128)S(1)}, f32[3,4,32,128]{3,2,1,0:T(8,128)S(1)}, u32[]{:S(2)}, u32[]{:S(2)}) %collective-permute-start.3) | collective-permute-done | bytes 196640 | tf_op jit(solution)/shard_map/ppermute | solution.py:715
  32.9 1.6 %collective-permute-start.14 = (f32[3,4,32,128]{3,2,1,0:T(8,128)S(1)}, f32[3,4,32,128]{3,2,1,0:T(8,128)S(1)}, u32[]{:S(2)}, u32[]{:S(2)}) collective-permute-start(f32[3,4,32,128]{3,2,1,0:T(8,128)S(1)} %add.21.refs_4_.first_ref), channel_id=1, source_target_pairs={{0,2},{1,3},{2,0},{3,1},{4,6},{5,7},{6,4},{7,5},{8,10},{9,11},{10,... | collective-permute-start | bytes 589832 | tf_op jit(solution)/shard_map/ppermute | solution.py:715
  34.5 0.2 slice_reduce_fusion.count_ref
  34.7 3.0 %products.3._.forcing_ref = f32[3,8,32,128]{3,2,1,0:T(8,128)S(1)} custom-call(s32[8]{0:T(128)S(1)} %copy-done.5, s32[16,8]{1,0:T(8,128)S(1)} %bitcast.27, s32[16]{0:T(128)S(1)} %slice_reduce_fusion.count_ref, f32[3,16,32,256]{3,2,1,0:T(8,128)S(1)} %get-tuple-element.59.physical, bf16[256,256]{1,0:T(8,128)(2,1)S(1)} %get-tuple-element.42.refs_6_.refs_3_.back_ref, ...), custom_call_target="tpu_custom_call" | custom-call | bytes 12582912 | tf_op jit(solution)/shard_map/products/pallas_call | solution.py:433
  37.7 2.3 %collective-permute-done.14.second_ref = f32[3,4,32,128]{3,2,1,0:T(8,128)S(1)} collective-permute-done((f32[3,4,32,128]{3,2,1,0:T(8,128)S(1)}, f32[3,4,32,128]{3,2,1,0:T(8,128)S(1)}, u32[]{:S(2)}, u32[]{:S(2)}) %collective-permute-start.14) | collective-permute-done | bytes 196640 | tf_op jit(solution)/shard_map/ppermute | solution.py:715
  39.9 0.1 collective-permute-start.15
  40.0 1.4 %collective-permute-done.15.other_ref = f32[3,4,32,128]{3,2,1,0:T(8,128)S(1)} collective-permute-done((f32[3,4,32,128]{3,2,1,0:T(8,128)S(1)}, f32[3,4,32,128]{3,2,1,0:T(8,128)S(1)}, u32[]{:S(2)}, u32[]{:S(2)}) %collective-permute-start.15) | collective-permute-done | bytes 196640 | tf_op jit(solution)/shard_map/ppermute | solution.py:715
  41.5 1.9 %outgoing.3 = f32[1536,128]{1,0:T(8,128)} custom-call(s32[8]{0:T(128)S(1)} %copy-done.5, s32[16]{0:T(128)S(1)} %slice_reduce_fusion.count_ref, f32[3,16,32,128]{3,2,1,0:T(8,128)S(1)} %get-tuple-element.58.slotted_ref, f32[3,8,32,128]{3,2,1,0:T(8,128)S(1)} %products.3._.forcing_ref, f32[3,4,32,128]{3,2,1,0:T(8,128)S(1)} %ordered_sum.3.kept_ref, ...), custom_call_target="tpu_custom_call" | custom-call | bytes 1572864 | tf_op jit(solution)/shard_map/outgoing/pallas_call | solution.py:499
  43.4 0.0 all-to-all-done.refs_0_
  43.4 6.9 %all-to-all-start.1 = ((f32[8,8,24,128]{3,2,1,0:T(8,128)}), f32[8,8,24,128]{3,2,1,0:T(8,128)S(1)}, u32[]{:S(2)}, u32[]{:S(2)}) async-start(f32[8,8,24,128]{3,2,1,0:T(8,128)} %bitcast.13), calls=%async_computation.1 | async-start | bytes 1572864 | tf_op jit(solution)/shard_map/all_to_all | solution.py:772
  50.3 3.5 %stress.3 = (f32[3,16,32,128]{3,2,1,0:T(8,128)S(1)}, f32[3,16,32,256]{3,2,1,0:T(8,128)S(1)}, f32[3,4,32,128]{3,2,1,0:T(8,128)S(1)}, f32[3,4,32,128]{3,2,1,0:T(8,128)S(1)}) custom-call(s32[8]{0:T(128)S(1)} %copy-done.5, s32[16,8]{1,0:T(8,128)S(1)} %bitcast.28, f32[4,384,128]{2,1,0:T(8,128)S(1)} %all-to-all-done.refs_0_, ...), custom_call_target="tpu_custom_call" | custom-call | bytes 12582912 | tf_op jit(solution)/shard_map/stress/pallas_call | solution.py:368
  53.7 0.1 collective-permute-start.4
  53.8 1.4 %collective-permute-done.4 = f32[3,4,32,128]{3,2,1,0:T(8,128)S(1)} collective-permute-done((f32[3,4,32,128]{3,2,1,0:T(8,128)S(1)}, f32[3,4,32,128]{3,2,1,0:T(8,128)S(1)}, u32[]{:S(2)}, u32[]{:S(2)}) %collective-permute-start.4) | collective-permute-done | bytes 196640 | tf_op jit(solution)/shard_map/ppermute | solution.py:715
  55.3 1.6 %collective-permute-start.5 = (f32[3,4,32,128]{3,2,1,0:T(8,128)S(1)}, f32[3,4,32,128]{3,2,1,0:T(8,128)S(1)}, u32[]{:S(2)}, u32[]{:S(2)}) collective-permute-start(f32[3,4,32,128]{3,2,1,0:T(8,128)S(1)} %add.22.first_ref), channel_id=1, source_target_pairs={{0,2},{1,3},{2,0},{3,1},{4,6},{5,7},{6,4},{7,5},{8,10},{9,11},{10,... | collective-permute-start | bytes 589832 | tf_op jit(solution)/shard_map/ppermute | solution.py:715
  56.8 3.0 %products.2._.forcing_ref = f32[3,8,32,128]{3,2,1,0:T(8,128)S(1)} custom-call(s32[8]{0:T(128)S(1)} %copy-done.5, s32[16,8]{1,0:T(8,128)S(1)} %bitcast.29, s32[16]{0:T(128)S(1)} %slice_reduce_fusion.count_ref, f32[3,16,32,256]{3,2,1,0:T(8,128)S(1)} %get-tuple-element.47.physical, bf16[256,256]{1,0:T(8,128)(2,1)S(1)} %get-tuple-element.42.refs_6_.refs_3_.back_ref, ...), custom_call_target="tpu_custom_call" | custom-call | bytes 12582912 | tf_op jit(solution)/shard_map/products/pallas_call | solution.py:433
  59.8 2.5 %collective-permute-done.5.second_ref = f32[3,4,32,128]{3,2,1,0:T(8,128)S(1)} collective-permute-done((f32[3,4,32,128]{3,2,1,0:T(8,128)S(1)}, f32[3,4,32,128]{3,2,1,0:T(8,128)S(1)}, u32[]{:S(2)}, u32[]{:S(2)}) %collective-permute-start.5) | collective-permute-done | bytes 196640 | tf_op jit(solution)/shard_map/ppermute | solution.py:715
  62.3 0.1 collective-permute-start.6
  62.4 1.4 %collective-permute-done.6.other_ref = f32[3,4,32,128]{3,2,1,0:T(8,128)S(1)} collective-permute-done((f32[3,4,32,128]{3,2,1,0:T(8,128)S(1)}, f32[3,4,32,128]{3,2,1,0:T(8,128)S(1)}, u32[]{:S(2)}, u32[]{:S(2)}) %collective-permute-start.6) | collective-permute-done | bytes 196640 | tf_op jit(solution)/shard_map/ppermute | solution.py:715
  63.8 1.2 outgoing.2
  65.0 3.0 %collective-permute-start.7 = (f32[8,24,128]{2,1,0:T(8,128)S(1)}, f32[8,24,128]{2,1,0:T(8,128)S(1)}, u32[]{:S(2)}, u32[]{:S(2)}) collective-permute-start(f32[8,24,128]{2,1,0:T(8,128)S(1)} %bitcast.45), channel_id=1, source_target_pairs={{0,16},{1,5},{2,18},{3,7},{4,20},{5,1},{6,22},{7,3},{8,24},{9,13},... | collective-permute-start | bytes 294920 | tf_op jit(solution)/shard_map/ppermute | solution.py:693
  68.0 1.5 %collective-permute-start.8 = (f32[8,24,128]{2,1,0:T(8,128)S(1)}, f32[8,24,128]{2,1,0:T(8,128)S(1)}, u32[]{:S(2)}, u32[]{:S(2)}) collective-permute-start(f32[8,24,128]{2,1,0:T(8,128)S(1)} %bitcast.44), channel_id=1, source_target_pairs={{0,4},{1,17},{2,6},{3,19},{4,0},{5,21},{6,2},{7,23},{8,12},{9,25},... | collective-permute-start | bytes 294920 | tf_op jit(solution)/shard_map/ppermute | solution.py:693
  69.5 1.5 %collective-permute-start.9 = (f32[8,24,128]{2,1,0:T(8,128)S(1)}, f32[8,24,128]{2,1,0:T(8,128)S(1)}, u32[]{:S(2)}, u32[]{:S(2)}) collective-permute-start(f32[8,24,128]{2,1,0:T(8,128)S(1)} %bitcast.43), channel_id=1, source_target_pairs={{0,8},{1,25},{2,10},{3,27},{4,12},{5,29},{6,14},{7,31},{8,0},{9,17... | collective-permute-start | bytes 294920 | tf_op jit(solution)/shard_map/ppermute | solution.py:693
  70.9 0.6 collective-permute-start.10
  71.5 1.5 %collective-permute-start.11 = (f32[8,24,128]{2,1,0:T(8,128)S(1)}, f32[8,24,128]{2,1,0:T(8,128)S(1)}, u32[]{:S(2)}, u32[]{:S(2)}) collective-permute-start(f32[8,24,128]{2,1,0:T(8,128)S(1)} %bitcast.41), channel_id=1, source_target_pairs={{0,20},{1,13},{2,22},{3,15},{4,16},{5,9},{6,18},{7,11},{8,28},{9,5... | collective-permute-start | bytes 294920 | tf_op jit(solution)/shard_map/ppermute | solution.py:693
  73.0 3.3 %collective-permute-done.7.refs_1_ = f32[8,24,128]{2,1,0:T(8,128)S(1)} collective-permute-done((f32[8,24,128]{2,1,0:T(8,128)S(1)}, f32[8,24,128]{2,1,0:T(8,128)S(1)}, u32[]{:S(2)}, u32[]{:S(2)}) %collective-permute-start.7) | collective-permute-done | bytes 98336 | tf_op jit(solution)/shard_map/ppermute | solution.py:693
  76.2 0.4 collective-permute-start.12
  76.7 0.0 collective-permute-done.8.refs_2_
  76.7 3.2 %collective-permute-start.13 = (f32[8,24,128]{2,1,0:T(8,128)S(1)}, f32[8,24,128]{2,1,0:T(8,128)S(1)}, u32[]{:S(2)}, u32[]{:S(2)}) collective-permute-start(f32[8,24,128]{2,1,0:T(8,128)S(1)} %bitcast.39), channel_id=1, source_target_pairs={{0,28},{1,29},{2,30},{3,31},{4,24},{5,25},{6,26},{7,27},{8,20},{9,... | collective-permute-start | bytes 294920 | tf_op jit(solution)/shard_map/ppermute | solution.py:693
  79.8 0.0 all-to-all-done.1.refs_0_
  79.8 4.1 %solve.2.refs_9_ = f32[8,512,128]{2,1,0:T(8,128)S(1)} custom-call(f32[8,8,24,128]{3,2,1,0:T(8,128)S(1)} %all-to-all-done.1.refs_0_, f32[8,512,512]{2,1,0:T(8,128)} %refs_8_.1), custom_call_target="tpu_custom_call" | custom-call | bytes 8388608 | tf_op jit(solution)/shard_map/solve/pallas_call | solution.py:631
  83.9 3.4 %collective-permute-done.11.refs_5_ = f32[8,24,128]{2,1,0:T(8,128)S(1)} collective-permute-done((f32[8,24,128]{2,1,0:T(8,128)S(1)}, f32[8,24,128]{2,1,0:T(8,128)S(1)}, u32[]{:S(2)}, u32[]{:S(2)}) %collective-permute-start.11) | collective-permute-done | bytes 98336 | tf_op jit(solution)/shard_map/ppermute | solution.py:693
  87.4 4.6 %solve.3 = (f32[8,2,24,128]{3,2,1,0:T(8,128)S(1)}, f32[8,2,24,128]{3,2,1,0:T(8,128)S(1)}, f32[8,2,24,128]{3,2,1,0:T(8,128)S(1)}, f32[8,2,24,128]{3,2,1,0:T(8,128...) custom-call(f32[8,24,128]{2,1,0:T(8,128)S(1)} %bitcast.38, ...), custom_call_target="tpu_custom_call" | custom-call | bytes 8388608 | tf_op jit(solution)/shard_map/solve/pallas_call | solution.py:631
  91.9 2.4 %collective-permute-start.16 = (f32[8,2,24,128]{3,2,1,0:T(8,128)S(1)}, f32[8,2,24,128]{3,2,1,0:T(8,128)S(1)}, u32[]{:S(2)}, u32[]{:S(2)}) collective-permute-start(f32[8,2,24,128]{3,2,1,0:T(8,128)S(1)} %get-tuple-element.61), channel_id=1, source_target_pairs={{0,16},{1,5},{2,18},{3,7},{4,20},{5,1},{6,22},{7,3},{8,24},{9,13},... | collective-permute-start | bytes 589832 | tf_op jit(solution)/shard_map/ppermute | solution.py:693
  94.3 1.0 collective-permute-start.17
  95.4 2.7 %collective-permute-start.19 = (f32[8,2,24,128]{3,2,1,0:T(8,128)S(1)}, f32[8,2,24,128]{3,2,1,0:T(8,128)S(1)}, u32[]{:S(2)}, u32[]{:S(2)}) collective-permute-start(f32[8,2,24,128]{3,2,1,0:T(8,128)S(1)} %get-tuple-element.64), channel_id=1, source_target_pairs={{0,24},{1,9},{2,26},{3,11},{4,28},{5,13},{6,30},{7,15},{8,16},{9,1... | collective-permute-start | bytes 589832 | tf_op jit(solution)/shard_map/ppermute | solution.py:693
  98.1 1.2 collective-permute-start.20
  99.3 8.6 %collective-permute-done.16 = f32[8,2,24,128]{3,2,1,0:T(8,128)S(1)} collective-permute-done((f32[8,2,24,128]{3,2,1,0:T(8,128)S(1)}, f32[8,2,24,128]{3,2,1,0:T(8,128)S(1)}, u32[]{:S(2)}, u32[]{:S(2)}) %collective-permute-start.16) | collective-permute-done | bytes 196640 | tf_op jit(solution)/shard_map/ppermute | solution.py:693
  107.9 1.9 %collective-permute-start.22 = (f32[8,2,24,128]{3,2,1,0:T(8,128)S(1)}, f32[8,2,24,128]{3,2,1,0:T(8,128)S(1)}, u32[]{:S(2)}, u32[]{:S(2)}) collective-permute-start(f32[8,2,24,128]{3,2,1,0:T(8,128)S(1)} %get-tuple-element.67), channel_id=1, source_target_pairs={{0,28},{1,29},{2,30},{3,31},{4,24},{5,25},{6,26},{7,27},{8,20},{9,... | collective-permute-start | bytes 589832 | tf_op jit(solution)/shard_map/ppermute | solution.py:693
  109.8 1.7 %collective-permute-done.18 = f32[8,2,24,128]{3,2,1,0:T(8,128)S(1)} collective-permute-done((f32[8,2,24,128]{3,2,1,0:T(8,128)S(1)}, f32[8,2,24,128]{3,2,1,0:T(8,128)S(1)}, u32[]{:S(2)}, u32[]{:S(2)}) %collective-permute-start.18) | collective-permute-done | bytes 196640 | tf_op jit(solution)/shard_map/ppermute | solution.py:693
  111.5 15.0 %collective-permute-done.20 = f32[8,2,24,128]{3,2,1,0:T(8,128)S(1)} collective-permute-done((f32[8,2,24,128]{3,2,1,0:T(8,128)S(1)}, f32[8,2,24,128]{3,2,1,0:T(8,128)S(1)}, u32[]{:S(2)}, u32[]{:S(2)}) %collective-permute-start.20) | collective-permute-done | bytes 196640 | tf_op jit(solution)/shard_map/ppermute | solution.py:693
  126.5 2.1 %restore.1 = f32[3,4,256,128]{3,2,1,0:T(8,128)} custom-call(f32[384,128]{1,0:T(8,128)S(1)} %bitcast.30, f32[384,128]{1,0:T(8,128)S(1)} %bitcast.31, f32[384,128]{1,0:T(8,128)S(1)} %bitcast.32, f32[384,128]{1,0:T(8,128)S(1)} %bitcast.33, f32[384,128]{1,0:T(8,128)S(1)} %bitcast.34, f32[384,128]{1,0:T(8,128)S(1)} %bitcast.35, f32[384,128]{1,0:T(8,128)S(1)} %bitcast.36, ...), custom_call_target="tpu_custom_call" | custom-call | bytes 3145728 | tf_op jit(solution)/shard_map/restore/pallas_call | solution.py:671
  (39 shorter events, 0.2 us)
Async XLA Ops:
  2.1 11.2 %collective-permute-start.1 = (f32[392,128]{1,0:T(8,128)}, f32[392,128]{1,0:T(8,128)S(1)}, u32[]{:S(2)}, u32[]{:S(2)}) collective-permute-start(f32[392,128]{1,0:T(8,128)} %get-tuple-element.39), channel_id=1, source_target_pairs={{0,24},{1,9},{2,26},{3,11},{8,16},{9,1},{10,18},{11,3},{16,8},{17,... | collective-permute-start | bytes 602120 | tf_op jit(solution)/shard_map/ppermute | solution.py:693
  7.2 19.1 %collective-permute-start = (f32[392,128]{1,0:T(8,128)}, f32[392,128]{1,0:T(8,128)S(1)}, u32[]{:S(2)}, u32[]{:S(2)}) collective-permute-start(f32[392,128]{1,0:T(8,128)} %get-tuple-element.38), channel_id=1, source_target_pairs={{0,8},{1,25},{2,10},{3,27},{8,0},{9,17},{10,2},{11,19},{16,24},{17... | collective-permute-start | bytes 602120 | tf_op jit(solution)/shard_map/ppermute | solution.py:693
  7.2 20.6 %collective-permute-start.2 = (f32[392,128]{1,0:T(8,128)}, f32[392,128]{1,0:T(8,128)S(1)}, u32[]{:S(2)}, u32[]{:S(2)}) collective-permute-start(f32[392,128]{1,0:T(8,128)} %get-tuple-element.40), channel_id=1, source_target_pairs={{0,16},{1,17},{2,18},{3,19},{8,24},{9,25},{10,26},{11,27},{16,0},{... | collective-permute-start | bytes 602120 | tf_op jit(solution)/shard_map/ppermute | solution.py:693
  9.8 15.6 %copy-start.3 = (f32[392,128]{1,0:T(8,128)S(1)}, f32[392,128]{1,0:T(8,128)}, u32[]{:S(2)}) copy-start(f32[392,128]{1,0:T(8,128)} %get-tuple-element.37.refs_0_) | copy-start | bytes 602116
  9.8 15.6 %copy-start.2 = (bf16[128,256]{1,0:T(8,128)(2,1)S(1)}, bf16[128,256]{1,0:T(8,128)(2,1)}, u32[]{:S(2)}) copy-start(bf16[128,256]{1,0:T(8,128)(2,1)} %constant.22.clone.rest_ref.refs_5_.refs_2_) | copy-start | bytes 196612
  9.8 15.6 %copy-start.4 = (bf16[128,256]{1,0:T(8,128)(2,1)S(1)}, bf16[128,256]{1,0:T(8,128)(2,1)}, u32[]{:S(2)}) copy-start(bf16[128,256]{1,0:T(8,128)(2,1)} %constant.21.clone.top_ref) | copy-start | bytes 196612
  9.8 15.7 %copy-start.6 = (s32[64]{0:T(128)S(1)}, s32[64]{0:T(128)}, u32[]{:S(2)}) copy-start(s32[64]{0:T(128)} %owner_ref.1) | copy-start | bytes 772
  9.8 18.1 %copy-start.5 = (s32[8]{0:T(128)S(1)}, s32[8]{0:T(128)}, u32[]{:S(2)}) copy-start(s32[8]{0:T(128)} %low_ref.11) | copy-start | bytes 100
  13.3 0.7 copy-start
  14.0 12.3 %copy-start.1 = (f32[392,128]{1,0:T(8,128)S(1)}, f32[392,128]{1,0:T(8,128)}, u32[]{:S(2)}) copy-start(f32[392,128]{1,0:T(8,128)} %copy-done) | copy-start | bytes 602116
  14.0 29.4 %all-to-all-start = ((f32[4,384,128]{2,1,0:T(8,128)}), f32[4,384,128]{2,1,0:T(8,128)S(1)}, u32[]{:S(2)}, u32[]{:S(2)}) async-start(f32[4,384,128]{2,1,0:T(8,128)} %hand_on.1), calls=%async_computation | async-start | bytes 1572864 | tf_op jit(solution)/shard_map/all_to_all | solution.py:741
  31.4 1.5 %collective-permute-start.3 = (f32[3,4,32,128]{3,2,1,0:T(8,128)S(1)}, f32[3,4,32,128]{3,2,1,0:T(8,128)S(1)}, u32[]{:S(2)}, u32[]{:S(2)}) collective-permute-start(f32[3,4,32,128]{3,2,1,0:T(8,128)S(1)} %get-tuple-element.45), channel_id=1, source_target_pairs={{0,1},{1,0},{2,3},{3,2},{4,5},{5,4},{6,7},{7,6},{8,9},{9,8},{10,11... | collective-permute-start | bytes 589832 | tf_op jit(solution)/shard_map/ppermute | solution.py:715
  32.9 7.0 %collective-permute-start.14 = (f32[3,4,32,128]{3,2,1,0:T(8,128)S(1)}, f32[3,4,32,128]{3,2,1,0:T(8,128)S(1)}, u32[]{:S(2)}, u32[]{:S(2)}) collective-permute-start(f32[3,4,32,128]{3,2,1,0:T(8,128)S(1)} %add.21.refs_4_.first_ref), channel_id=1, source_target_pairs={{0,2},{1,3},{2,0},{3,1},{4,6},{5,7},{6,4},{7,5},{8,10},{9,11},{10,... | collective-permute-start | bytes 589832 | tf_op jit(solution)/shard_map/ppermute | solution.py:715
  39.9 1.5 %collective-permute-start.15 = (f32[3,4,32,128]{3,2,1,0:T(8,128)S(1)}, f32[3,4,32,128]{3,2,1,0:T(8,128)S(1)}, u32[]{:S(2)}, u32[]{:S(2)}) collective-permute-start(f32[3,4,32,128]{3,2,1,0:T(8,128)S(1)} %ordered_sum.3.kept_ref), channel_id=1, source_target_pairs={{0,1},{1,0},{2,3},{3,2},{4,5},{5,4},{6,7},{7,6},{8,9},{9,8},{10,11... | collective-permute-start | bytes 589832 | tf_op jit(solution)/shard_map/ppermute | solution.py:715
  43.4 36.5 %all-to-all-start.1 = ((f32[8,8,24,128]{3,2,1,0:T(8,128)}), f32[8,8,24,128]{3,2,1,0:T(8,128)S(1)}, u32[]{:S(2)}, u32[]{:S(2)}) async-start(f32[8,8,24,128]{3,2,1,0:T(8,128)} %bitcast.13), calls=%async_computation.1 | async-start | bytes 1572864 | tf_op jit(solution)/shard_map/all_to_all | solution.py:772
  53.7 1.5 %collective-permute-start.4 = (f32[3,4,32,128]{3,2,1,0:T(8,128)S(1)}, f32[3,4,32,128]{3,2,1,0:T(8,128)S(1)}, u32[]{:S(2)}, u32[]{:S(2)}) collective-permute-start(f32[3,4,32,128]{3,2,1,0:T(8,128)S(1)} %get-tuple-element.49), channel_id=1, source_target_pairs={{0,1},{1,0},{2,3},{3,2},{4,5},{5,4},{6,7},{7,6},{8,9},{9,8},{10,11... | collective-permute-start | bytes 589832 | tf_op jit(solution)/shard_map/ppermute | solution.py:715
  55.3 7.0 %collective-permute-start.5 = (f32[3,4,32,128]{3,2,1,0:T(8,128)S(1)}, f32[3,4,32,128]{3,2,1,0:T(8,128)S(1)}, u32[]{:S(2)}, u32[]{:S(2)}) collective-permute-start(f32[3,4,32,128]{3,2,1,0:T(8,128)S(1)} %add.22.first_ref), channel_id=1, source_target_pairs={{0,2},{1,3},{2,0},{3,1},{4,6},{5,7},{6,4},{7,5},{8,10},{9,11},{10,... | collective-permute-start | bytes 589832 | tf_op jit(solution)/shard_map/ppermute | solution.py:715
  62.3 1.5 %collective-permute-start.6 = (f32[3,4,32,128]{3,2,1,0:T(8,128)S(1)}, f32[3,4,32,128]{3,2,1,0:T(8,128)S(1)}, u32[]{:S(2)}, u32[]{:S(2)}) collective-permute-start(f32[3,4,32,128]{3,2,1,0:T(8,128)S(1)} %ordered_sum.2.kept_ref), channel_id=1, source_target_pairs={{0,1},{1,0},{2,3},{3,2},{4,5},{5,4},{6,7},{7,6},{8,9},{9,8},{10,11... | collective-permute-start | bytes 589832 | tf_op jit(solution)/shard_map/ppermute | solution.py:715
  65.0 11.2 %collective-permute-start.7 = (f32[8,24,128]{2,1,0:T(8,128)S(1)}, f32[8,24,128]{2,1,0:T(8,128)S(1)}, u32[]{:S(2)}, u32[]{:S(2)}) collective-permute-start(f32[8,24,128]{2,1,0:T(8,128)S(1)} %bitcast.45), channel_id=1, source_target_pairs={{0,16},{1,5},{2,18},{3,7},{4,20},{5,1},{6,22},{7,3},{8,24},{9,13},... | collective-permute-start | bytes 294920 | tf_op jit(solution)/shard_map/ppermute | solution.py:693
  68.0 8.7 %collective-permute-start.8 = (f32[8,24,128]{2,1,0:T(8,128)S(1)}, f32[8,24,128]{2,1,0:T(8,128)S(1)}, u32[]{:S(2)}, u32[]{:S(2)}) collective-permute-start(f32[8,24,128]{2,1,0:T(8,128)S(1)} %bitcast.44), channel_id=1, source_target_pairs={{0,4},{1,17},{2,6},{3,19},{4,0},{5,21},{6,2},{7,23},{8,12},{9,25},... | collective-permute-start | bytes 294920 | tf_op jit(solution)/shard_map/ppermute | solution.py:693
  69.5 14.5 %collective-permute-start.9 = (f32[8,24,128]{2,1,0:T(8,128)S(1)}, f32[8,24,128]{2,1,0:T(8,128)S(1)}, u32[]{:S(2)}, u32[]{:S(2)}) collective-permute-start(f32[8,24,128]{2,1,0:T(8,128)S(1)} %bitcast.43), channel_id=1, source_target_pairs={{0,8},{1,25},{2,10},{3,27},{4,12},{5,29},{6,14},{7,31},{8,0},{9,17... | collective-permute-start | bytes 294920 | tf_op jit(solution)/shard_map/ppermute | solution.py:693
  70.9 13.0 %collective-permute-start.10 = (f32[8,24,128]{2,1,0:T(8,128)S(1)}, f32[8,24,128]{2,1,0:T(8,128)S(1)}, u32[]{:S(2)}, u32[]{:S(2)}) collective-permute-start(f32[8,24,128]{2,1,0:T(8,128)S(1)} %bitcast.42), channel_id=1, source_target_pairs={{0,24},{1,9},{2,26},{3,11},{4,28},{5,13},{6,30},{7,15},{8,16},{9,1... | collective-permute-start | bytes 294920 | tf_op jit(solution)/shard_map/ppermute | solution.py:693
  71.5 15.9 %collective-permute-start.11 = (f32[8,24,128]{2,1,0:T(8,128)S(1)}, f32[8,24,128]{2,1,0:T(8,128)S(1)}, u32[]{:S(2)}, u32[]{:S(2)}) collective-permute-start(f32[8,24,128]{2,1,0:T(8,128)S(1)} %bitcast.41), channel_id=1, source_target_pairs={{0,20},{1,13},{2,22},{3,15},{4,16},{5,9},{6,18},{7,11},{8,28},{9,5... | collective-permute-start | bytes 294920 | tf_op jit(solution)/shard_map/ppermute | solution.py:693
  76.2 11.1 %collective-permute-start.12 = (f32[8,24,128]{2,1,0:T(8,128)S(1)}, f32[8,24,128]{2,1,0:T(8,128)S(1)}, u32[]{:S(2)}, u32[]{:S(2)}) collective-permute-start(f32[8,24,128]{2,1,0:T(8,128)S(1)} %bitcast.40), channel_id=1, source_target_pairs={{0,12},{1,21},{2,14},{3,23},{4,8},{5,17},{6,10},{7,19},{8,4},{9,29... | collective-permute-start | bytes 294920 | tf_op jit(solution)/shard_map/ppermute | solution.py:693
  76.7 10.7 %collective-permute-start.13 = (f32[8,24,128]{2,1,0:T(8,128)S(1)}, f32[8,24,128]{2,1,0:T(8,128)S(1)}, u32[]{:S(2)}, u32[]{:S(2)}) collective-permute-start(f32[8,24,128]{2,1,0:T(8,128)S(1)} %bitcast.39), channel_id=1, source_target_pairs={{0,28},{1,29},{2,30},{3,31},{4,24},{5,25},{6,26},{7,27},{8,20},{9,... | collective-permute-start | bytes 294920 | tf_op jit(solution)/shard_map/ppermute | solution.py:693
  91.9 15.9 %collective-permute-start.16 = (f32[8,2,24,128]{3,2,1,0:T(8,128)S(1)}, f32[8,2,24,128]{3,2,1,0:T(8,128)S(1)}, u32[]{:S(2)}, u32[]{:S(2)}) collective-permute-start(f32[8,2,24,128]{3,2,1,0:T(8,128)S(1)} %get-tuple-element.61), channel_id=1, source_target_pairs={{0,16},{1,5},{2,18},{3,7},{4,20},{5,1},{6,22},{7,3},{8,24},{9,13},... | collective-permute-start | bytes 589832 | tf_op jit(solution)/shard_map/ppermute | solution.py:693
  94.3 13.6 %collective-permute-start.17 = (f32[8,2,24,128]{3,2,1,0:T(8,128)S(1)}, f32[8,2,24,128]{3,2,1,0:T(8,128)S(1)}, u32[]{:S(2)}, u32[]{:S(2)}) collective-permute-start(f32[8,2,24,128]{3,2,1,0:T(8,128)S(1)} %get-tuple-element.62), channel_id=1, source_target_pairs={{0,4},{1,17},{2,6},{3,19},{4,0},{5,21},{6,2},{7,23},{8,12},{9,25},... | collective-permute-start | bytes 589832 | tf_op jit(solution)/shard_map/ppermute | solution.py:693
  95.4 16.2 %collective-permute-start.18 = (f32[8,2,24,128]{3,2,1,0:T(8,128)S(1)}, f32[8,2,24,128]{3,2,1,0:T(8,128)S(1)}, u32[]{:S(2)}, u32[]{:S(2)}) collective-permute-start(f32[8,2,24,128]{3,2,1,0:T(8,128)S(1)} %get-tuple-element.63), channel_id=1, source_target_pairs={{0,8},{1,25},{2,10},{3,27},{4,12},{5,29},{6,14},{7,31},{8,0},{9,17... | collective-permute-start | bytes 589832 | tf_op jit(solution)/shard_map/ppermute | solution.py:693
  95.4 16.2 %collective-permute-start.19 = (f32[8,2,24,128]{3,2,1,0:T(8,128)S(1)}, f32[8,2,24,128]{3,2,1,0:T(8,128)S(1)}, u32[]{:S(2)}, u32[]{:S(2)}) collective-permute-start(f32[8,2,24,128]{3,2,1,0:T(8,128)S(1)} %get-tuple-element.64), channel_id=1, source_target_pairs={{0,24},{1,9},{2,26},{3,11},{4,28},{5,13},{6,30},{7,15},{8,16},{9,1... | collective-permute-start | bytes 589832 | tf_op jit(solution)/shard_map/ppermute | solution.py:693
  98.1 28.5 %collective-permute-start.20 = (f32[8,2,24,128]{3,2,1,0:T(8,128)S(1)}, f32[8,2,24,128]{3,2,1,0:T(8,128)S(1)}, u32[]{:S(2)}, u32[]{:S(2)}) collective-permute-start(f32[8,2,24,128]{3,2,1,0:T(8,128)S(1)} %get-tuple-element.65), channel_id=1, source_target_pairs={{0,20},{1,13},{2,22},{3,15},{4,16},{5,9},{6,18},{7,11},{8,28},{9,5... | collective-permute-start | bytes 589832 | tf_op jit(solution)/shard_map/ppermute | solution.py:693
  107.9 18.6 %collective-permute-start.21 = (f32[8,2,24,128]{3,2,1,0:T(8,128)S(1)}, f32[8,2,24,128]{3,2,1,0:T(8,128)S(1)}, u32[]{:S(2)}, u32[]{:S(2)}) collective-permute-start(f32[8,2,24,128]{3,2,1,0:T(8,128)S(1)} %get-tuple-element.66), channel_id=1, source_target_pairs={{0,12},{1,21},{2,14},{3,23},{4,8},{5,17},{6,10},{7,19},{8,4},{9,29... | collective-permute-start | bytes 589832 | tf_op jit(solution)/shard_map/ppermute | solution.py:693
  107.9 18.6 %collective-permute-start.22 = (f32[8,2,24,128]{3,2,1,0:T(8,128)S(1)}, f32[8,2,24,128]{3,2,1,0:T(8,128)S(1)}, u32[]{:S(2)}, u32[]{:S(2)}) collective-permute-start(f32[8,2,24,128]{3,2,1,0:T(8,128)S(1)} %get-tuple-element.67), channel_id=1, source_target_pairs={{0,28},{1,29},{2,30},{3,31},{4,24},{5,25},{6,26},{7,27},{8,20},{9,... | collective-permute-start | bytes 589832 | tf_op jit(solution)/shard_map/ppermute | solution.py:693

commit v17 on v16

--- a/solution.py
+++ b/solution.py
@@ -148,8 +148,22 @@
     return lax.dot_general(left, right, (dims, ((), ())), preferred_element_type=jnp.float32)
 
 
-def pack_first_kernel(near_ref, count_ref, velocity_ref, *out_refs):
+def pack_first_kernel(near_ref, count_ref, velocity_ref, *refs):
+    out_refs, arrived = (refs[:-1], refs[-1])
     chunks, _, kx_count, rows, columns = velocity_ref.shape
+    own = lax.axis_index("kx")
+    copies = []
+    for index, out_ref in enumerate(out_refs):
+        partner = own ^ step_at(kx_count, index)
+        for chunk in range(chunks):
+            copies.append(
+                pltpu.make_async_copy(
+                    velocity_ref.at[chunk, 0, partner],
+                    out_ref.at[pl.ds(chunk * rows, rows)],
+                    arrived.at[index, chunk],
+                )
+            )
+            copies[-1].start()
     shape = (out_refs[0].shape[0] - chunks * rows, columns)
     row = lax.broadcasted_iota(jnp.int32, shape, 0)
     lane = lax.broadcasted_iota(jnp.int32, shape, 1)
@@ -161,12 +175,10 @@
             line = jnp.where(lane == member, near_ref[mode, member], line)
         extra = jnp.where(row == mode, line, extra)
     extra = extra.astype(jnp.float32)
-    own = lax.axis_index("kx")
-    for index, out_ref in enumerate(out_refs):
-        partner = own ^ step_at(kx_count, index)
-        for chunk in range(chunks):
-            out_ref[chunk * rows : (chunk + 1) * rows] = velocity_ref[chunk, 0, partner]
+    for out_ref in out_refs:
         out_ref[chunks * rows :] = extra
+    for copy in copies:
+        copy.wait()
 
 
 def pack_first(velocity, neighbours, mode_counts, extra_rows):
@@ -175,13 +187,9 @@
     return pl.pallas_call(
         pack_first_kernel,
         out_shape=(shape,) * kx_count,
-        grid=(1,),
-        in_specs=[
-            SMEM,
-            SMEM,
-            pl.BlockSpec((chunks, 1, kx_count, rows, columns), lambda i: (0, 0, 0, 0, 0)),
-        ],
-        out_specs=(pl.BlockSpec(shape.shape, lambda i: (0, 0)),) * kx_count,
+        in_specs=[SMEM, SMEM, pl.BlockSpec(memory_space=pl.ANY)],
+        out_specs=(VMEM,) * kx_count,
+        scratch_shapes=[pltpu.SemaphoreType.DMA((kx_count, chunks))],
         cost_estimate=cost(4 * velocity.size),
         name="pack_first",
     )(neighbours, mode_counts, velocity)
@@ -539,6 +547,7 @@
         step = step_at(owners, position)
         partners.append((own_kx ^ (step // ht_count), own_ht ^ (step % ht_count)))
     refs = list(refs)
+    operands = refs.pop()
     matrices = refs.pop()
     arrived = refs.pop()
     source = refs.pop(0)
@@ -562,14 +571,11 @@
         ]
         for s in range(slots)
     ]
-    ahead = min(3, slots)
-    for s in range(ahead):
+    batch = max(slots // 2, 1)
+    for s in range(batch):
         for copy in copies[s]:
             copy.start()
     partial_ref = refs.pop(0) if piece else None
-    if last:
-        out_refs, full = (refs[:owners], refs[owners])
-        lane_tiles, per_band = out_refs[0].shape[1:3]
     rows = LANES // groups
     for s in range(slots):
         tiles = []
@@ -583,42 +589,52 @@
         if spare:
             empty = jnp.zeros((spare, fields.shape[1]), jnp.float32)
             fields = jnp.concatenate([fields, empty], axis=0)
-        top, rest = two_parts(fields)
-        for copy in copies[s]:
-            copy.wait()
-        if s + ahead < slots:
-            for copy in copies[s + ahead]:
-                copy.start()
+        operands[s] = jnp.concatenate(two_parts(fields), axis=0)
+    padded = count + spare
+    for s in range(slots):
+        if s % batch == 0:
+            for t in range(s, min(s + batch, slots)):
+                for copy in copies[t]:
+                    copy.wait()
+            for t in range(s + batch, min(s + 2 * batch, slots)):
+                for copy in copies[t]:
+                    copy.start()
         matrix = jnp.concatenate([matrices[s, h] for h in range(ht_count)], axis=1)
         matrix_top, matrix_rest = two_parts(matrix)
         contract = ((1,), (1,))
-        both = dot(matrix_top, jnp.concatenate([top, rest], axis=0), contract)
-        solved = both[:, : count + spare] + both[:, count + spare :]
-        solved = solved + dot(matrix_rest, top, contract)
+        both = dot(matrix_top, operands[s], contract)
+        solved = both[:, :padded] + both[:, padded:]
+        solved = solved + dot(matrix_rest, operands[s, :padded], contract)
         if piece:
             solved = solved + partial_ref[s]
         if not last:
             refs[0][s] = solved
             continue
+        full = refs[owners]
         for tile in range(heights // LANES):
-            full[s % 2, tile] = solved[tile * LANES : (tile + 1) * LANES].T[:count]
-        for out_ref, (kx, ht) in zip(out_refs, partners):
-            band = pl.ds(pl.multiple_of(kx * per_band, 8), per_band)
+            full[s, tile] = solved[tile * LANES : (tile + 1) * LANES].T[:count]
+    if not last:
+        return
+    out_refs = refs[:owners]
+    lane_tiles, per_band = out_refs[0].shape[1:3]
+    for out_ref, (kx, ht) in zip(out_refs, partners):
+        band = pl.ds(pl.multiple_of(kx * per_band, 8), per_band)
+        for s in range(slots):
             for tile in range(lane_tiles):
-                out_ref[s, tile] = full[s % 2, ht * lane_tiles + tile, band]
+                out_ref[s, tile] = full[s, ht * lane_tiles + tile, band]
 
 
 def solve(blocks, helmholtz, piece, pieces, partial, groups, kx_count, ht_count):
     slots, per_slot, _ = blocks[0].shape[-3:]
     heights, owners, last = (helmholtz.shape[1], kx_count * ht_count, piece == pieces - 1)
     count = per_slot * groups
+    padded = -(-count // LANES) * LANES
     scratch = []
     if last:
         shape = (slots, heights // ht_count // LANES, count // kx_count, LANES)
         out_shape = (jax.ShapeDtypeStruct(shape, jnp.float32),) * owners
-        scratch.append(pltpu.VMEM((2, heights // LANES, count, LANES), jnp.float32))
+        scratch.append(pltpu.VMEM((slots, heights // LANES, count, LANES), jnp.float32))
     else:
-        padded = -(-count // LANES) * LANES
         out_shape = jax.ShapeDtypeStruct((slots, heights, padded), jnp.float32)
     if piece:
         scratch.append(pltpu.VMEM((owners,) + blocks[0].shape, jnp.float32))
@@ -626,6 +642,7 @@
     scratch += [
         pltpu.SemaphoreType.DMA((slots, ht_count)),
         pltpu.VMEM((slots, ht_count, heights, width), jnp.float32),
+        pltpu.VMEM((slots, 2 * padded, ht_count * width), jnp.bfloat16),
     ]
     started = [] if partial is None else [partial]
     return pl.pallas_call(

time: 130 us -> 132 us (1.015)
  Pallas kernels: 31.7 us -> 34.1 us
    pallas_call x2, Pallas kernels: 8.62 us -> 9.97 us  [solve(): pl.pallas_call(functools.partial(solve_kernel, groups=groups, kx_count=kx...]
where the time goes in v17:
time: 132 us; the launch traced here: 130 us
  starting transfers between devices  47.5 us (36%)
  waiting for transfers between devices  46.6 us (35%)
  Pallas kernels  34.1 us (26%)
  local copies, waits for them, and re-layouts  1.56 us (1%)
    ppermute x17, waiting for transfers between devices, exchange(): result[position] = lax.ppermute(blocks[position], axes + ('real',), pairs)  36.2 us
    ppermute x17, starting transfers between devices, exchange(): result[position] = lax.ppermute(blocks[position], axes + ('real',), pairs)  26.3 us
    all_to_all x1, starting transfers between devices, local(): block = lax.all_to_all(block, 'kx', split_axis=0, concat_axis=0, tiled=True)  10.8 us
    ppermute x6, waiting for transfers between devices, swap(): return lax.ppermute(value, 'real', pairs)  10.4 us
    pallas_call x2, Pallas kernels, solve(): pl.pallas_call(functools.partial(solve_kernel, groups=groups, kx_count=kx...  9.97 us
    pallas_call x2, Pallas kernels, stress_terms(): pl.pallas_call(stress_kernel, out_shape=(jax.ShapeDtypeStruct(shape, jnp....  6.94 us
    all_to_all x1, starting transfers between devices, local(): lax.all_to_all(block, ('kx', 'ht'), split_axis=0, concat_axis=0, tiled=True)  6.91 us
    pallas_call x2, Pallas kernels, high_terms(): pl.pallas_call(products_kernel, out_shape=jax.ShapeDtypeStruct((component...  6 us
  transfers between devices with their start and end apart: 25, of which 13 were waited for; matrix products, arithmetic and copies ran while one was open for 1% of the time, Pallas kernels for 18%

profile of v17, /device:TPU:0, one launch (start us, length us, event | category | flops | bytes accessed | tf_op | source)
XLA Modules:
  0.0 130.1 jit_solution(12259363836198819422)
XLA Ops:
  0.0 3.1 %pack_first.1 = (f32[392,128]{1,0:T(8,128)}, f32[392,128]{1,0:T(8,128)}, f32[392,128]{1,0:T(8,128)}, f32[392,128]{1,0:T(8,128)}) custom-call(s32[4,8]{1,0:T(4,128)} %near_ref.1, s32[4]{0:T(128)} %count_ref.1, f32[12,2,4,32,128]{4,3,2,1,0:T(8,128)} %bitcast.46), custom_call_target="tpu_custom_call" | custom-call | bytes 1572864 | tf_op jit(solution)/shard_map/pack_first/pallas_call | solution.py:187
  3.1 5.1 %collective-permute-start.1 = (f32[392,128]{1,0:T(8,128)}, f32[392,128]{1,0:T(8,128)S(1)}, u32[]{:S(2)}, u32[]{:S(2)}) collective-permute-start(f32[392,128]{1,0:T(8,128)} %get-tuple-element.39), channel_id=1, source_target_pairs={{0,24},{1,9},{2,26},{3,11},{8,16},{9,1},{10,18},{11,3},{16,8},{17,... | collective-permute-start | bytes 602120 | tf_op jit(solution)/shard_map/ppermute | solution.py:710
  8.3 0.6 collective-permute-start.2
  8.9 2.1 %pack.1.value_ref = f32[4,384,128]{2,1,0:T(8,128)} custom-call(f32[12,2,4,32,128]{4,3,2,1,0:T(8,128)} %bitcast.47), custom_call_target="tpu_custom_call" | custom-call | bytes 1572864 | tf_op jit(solution)/shard_map/pack/pallas_call | solution.py:209
  11.0 0.0 copy-start.5
  11.0 3.4 %collective-permute-done.1.after_ref.refs_2_ = f32[392,128]{1,0:T(8,128)S(1)} collective-permute-done((f32[392,128]{1,0:T(8,128)}, f32[392,128]{1,0:T(8,128)S(1)}, u32[]{:S(2)}, u32[]{:S(2)}) %collective-permute-start.1) | collective-permute-done | bytes 200736 | tf_op jit(solution)/shard_map/ppermute | solution.py:710
  14.4 0.7 copy-done
  15.1 10.8 %all-to-all-start = ((f32[4,384,128]{2,1,0:T(8,128)}), f32[4,384,128]{2,1,0:T(8,128)S(1)}, u32[]{:S(2)}, u32[]{:S(2)}) async-start(f32[4,384,128]{2,1,0:T(8,128)} %hand_on.1), calls=%async_computation | async-start | bytes 1572864 | tf_op jit(solution)/shard_map/all_to_all | solution.py:758
  25.8 0.1 broadcast_in_dim.85
  25.9 0.1 broadcast_in_dim.86
  26.0 0.1 broadcast_in_dim.91
  26.1 0.1 broadcast_in_dim.92
  26.2 0.1 broadcast_in_dim.96
  26.3 0.1 broadcast_in_dim.97
  26.4 0.1 broadcast_in_dim.101
  26.4 0.1 broadcast_in_dim.102
  26.6 0.8 tables.1
  27.3 0.0 collective-permute-done.refs_1_
  27.4 1.5 %collective-permute-done.2.refs_3_ = f32[392,128]{1,0:T(8,128)S(1)} collective-permute-done((f32[392,128]{1,0:T(8,128)}, f32[392,128]{1,0:T(8,128)S(1)}, u32[]{:S(2)}, u32[]{:S(2)}) %collective-permute-start.2) | collective-permute-done | bytes 200736 | tf_op jit(solution)/shard_map/ppermute | solution.py:710
  28.9 0.1 add_convert_fusion
  29.0 3.5 %stress.2 = (f32[3,16,32,128]{3,2,1,0:T(8,128)S(1)}, f32[3,16,32,256]{3,2,1,0:T(8,128)S(1)}, f32[3,4,32,128]{3,2,1,0:T(8,128)S(1)}, f32[3,4,32,128]{3,2,1,0:T(8,128)S(1)}) custom-call(s32[8]{0:T(128)S(1)} %copy-done.5, s32[16,8]{1,0:T(8,128)S(1)} %bitcast.26, f32[392,128]{1,0:T(8,128)S(1)} %copy-done.3, f32[392,128]{1,0:T(8,128)S(1)} %collective-permute-done.refs_1_, ...), custom_call_target="tpu_custom_call" | custom-call | bytes 12582912 | tf_op jit(solution)/shard_map/stress/pallas_call | solution.py:376
  32.4 0.1 collective-permute-start.3
  32.6 1.4 %collective-permute-done.3 = f32[3,4,32,128]{3,2,1,0:T(8,128)S(1)} collective-permute-done((f32[3,4,32,128]{3,2,1,0:T(8,128)S(1)}, f32[3,4,32,128]{3,2,1,0:T(8,128)S(1)}, u32[]{:S(2)}, u32[]{:S(2)}) %collective-permute-start.3) | collective-permute-done | bytes 196640 | tf_op jit(solution)/shard_map/ppermute | solution.py:732
  34.0 1.6 %collective-permute-start.14 = (f32[3,4,32,128]{3,2,1,0:T(8,128)S(1)}, f32[3,4,32,128]{3,2,1,0:T(8,128)S(1)}, u32[]{:S(2)}, u32[]{:S(2)}) collective-permute-start(f32[3,4,32,128]{3,2,1,0:T(8,128)S(1)} %add.21.refs_4_.first_ref), channel_id=1, source_target_pairs={{0,2},{1,3},{2,0},{3,1},{4,6},{5,7},{6,4},{7,5},{8,10},{9,11},{10,... | collective-permute-start | bytes 589832 | tf_op jit(solution)/shard_map/ppermute | solution.py:732
  35.5 0.2 slice_reduce_fusion.count_ref
  35.7 3.0 %products.3._.forcing_ref = f32[3,8,32,128]{3,2,1,0:T(8,128)S(1)} custom-call(s32[8]{0:T(128)S(1)} %copy-done.5, s32[16,8]{1,0:T(8,128)S(1)} %bitcast.27, s32[16]{0:T(128)S(1)} %slice_reduce_fusion.count_ref, f32[3,16,32,256]{3,2,1,0:T(8,128)S(1)} %get-tuple-element.59.physical, bf16[256,256]{1,0:T(8,128)(2,1)S(1)} %get-tuple-element.42.refs_6_.refs_3_.back_ref, ...), custom_call_target="tpu_custom_call" | custom-call | bytes 12582912 | tf_op jit(solution)/shard_map/products/pallas_call | solution.py:441
  38.7 2.3 %collective-permute-done.14.second_ref = f32[3,4,32,128]{3,2,1,0:T(8,128)S(1)} collective-permute-done((f32[3,4,32,128]{3,2,1,0:T(8,128)S(1)}, f32[3,4,32,128]{3,2,1,0:T(8,128)S(1)}, u32[]{:S(2)}, u32[]{:S(2)}) %collective-permute-start.14) | collective-permute-done | bytes 196640 | tf_op jit(solution)/shard_map/ppermute | solution.py:732
  41.0 0.1 collective-permute-start.15
  41.1 1.4 %collective-permute-done.15.other_ref = f32[3,4,32,128]{3,2,1,0:T(8,128)S(1)} collective-permute-done((f32[3,4,32,128]{3,2,1,0:T(8,128)S(1)}, f32[3,4,32,128]{3,2,1,0:T(8,128)S(1)}, u32[]{:S(2)}, u32[]{:S(2)}) %collective-permute-start.15) | collective-permute-done | bytes 196640 | tf_op jit(solution)/shard_map/ppermute | solution.py:732
  42.5 1.9 %outgoing.3 = f32[1536,128]{1,0:T(8,128)} custom-call(s32[8]{0:T(128)S(1)} %copy-done.5, s32[16]{0:T(128)S(1)} %slice_reduce_fusion.count_ref, f32[3,16,32,128]{3,2,1,0:T(8,128)S(1)} %get-tuple-element.58.slotted_ref, f32[3,8,32,128]{3,2,1,0:T(8,128)S(1)} %products.3._.forcing_ref, f32[3,4,32,128]{3,2,1,0:T(8,128)S(1)} %ordered_sum.3.kept_ref, ...), custom_call_target="tpu_custom_call" | custom-call | bytes 1572864 | tf_op jit(solution)/shard_map/outgoing/pallas_call | solution.py:507
  44.4 0.0 all-to-all-done.refs_0_
  44.4 6.9 %all-to-all-start.1 = ((f32[8,8,24,128]{3,2,1,0:T(8,128)}), f32[8,8,24,128]{3,2,1,0:T(8,128)S(1)}, u32[]{:S(2)}, u32[]{:S(2)}) async-start(f32[8,8,24,128]{3,2,1,0:T(8,128)} %bitcast.13), calls=%async_computation.1 | async-start | bytes 1572864 | tf_op jit(solution)/shard_map/all_to_all | solution.py:789
  51.3 3.5 %stress.3 = (f32[3,16,32,128]{3,2,1,0:T(8,128)S(1)}, f32[3,16,32,256]{3,2,1,0:T(8,128)S(1)}, f32[3,4,32,128]{3,2,1,0:T(8,128)S(1)}, f32[3,4,32,128]{3,2,1,0:T(8,128)S(1)}) custom-call(s32[8]{0:T(128)S(1)} %copy-done.5, s32[16,8]{1,0:T(8,128)S(1)} %bitcast.28, f32[4,384,128]{2,1,0:T(8,128)S(1)} %all-to-all-done.refs_0_, ...), custom_call_target="tpu_custom_call" | custom-call | bytes 12582912 | tf_op jit(solution)/shard_map/stress/pallas_call | solution.py:376
  54.8 0.1 collective-permute-start.4
  54.9 1.4 %collective-permute-done.4 = f32[3,4,32,128]{3,2,1,0:T(8,128)S(1)} collective-permute-done((f32[3,4,32,128]{3,2,1,0:T(8,128)S(1)}, f32[3,4,32,128]{3,2,1,0:T(8,128)S(1)}, u32[]{:S(2)}, u32[]{:S(2)}) %collective-permute-start.4) | collective-permute-done | bytes 196640 | tf_op jit(solution)/shard_map/ppermute | solution.py:732
  56.4 1.5 %collective-permute-start.5 = (f32[3,4,32,128]{3,2,1,0:T(8,128)S(1)}, f32[3,4,32,128]{3,2,1,0:T(8,128)S(1)}, u32[]{:S(2)}, u32[]{:S(2)}) collective-permute-start(f32[3,4,32,128]{3,2,1,0:T(8,128)S(1)} %add.22.first_ref), channel_id=1, source_target_pairs={{0,2},{1,3},{2,0},{3,1},{4,6},{5,7},{6,4},{7,5},{8,10},{9,11},{10,... | collective-permute-start | bytes 589832 | tf_op jit(solution)/shard_map/ppermute | solution.py:732
  57.9 3.0 %products.2._.forcing_ref = f32[3,8,32,128]{3,2,1,0:T(8,128)S(1)} custom-call(s32[8]{0:T(128)S(1)} %copy-done.5, s32[16,8]{1,0:T(8,128)S(1)} %bitcast.29, s32[16]{0:T(128)S(1)} %slice_reduce_fusion.count_ref, f32[3,16,32,256]{3,2,1,0:T(8,128)S(1)} %get-tuple-element.47.physical, bf16[256,256]{1,0:T(8,128)(2,1)S(1)} %get-tuple-element.42.refs_6_.refs_3_.back_ref, ...), custom_call_target="tpu_custom_call" | custom-call | bytes 12582912 | tf_op jit(solution)/shard_map/products/pallas_call | solution.py:441
  60.9 2.5 %collective-permute-done.5.second_ref = f32[3,4,32,128]{3,2,1,0:T(8,128)S(1)} collective-permute-done((f32[3,4,32,128]{3,2,1,0:T(8,128)S(1)}, f32[3,4,32,128]{3,2,1,0:T(8,128)S(1)}, u32[]{:S(2)}, u32[]{:S(2)}) %collective-permute-start.5) | collective-permute-done | bytes 196640 | tf_op jit(solution)/shard_map/ppermute | solution.py:732
  63.4 0.1 collective-permute-start.6
  63.5 1.4 %collective-permute-done.6.other_ref = f32[3,4,32,128]{3,2,1,0:T(8,128)S(1)} collective-permute-done((f32[3,4,32,128]{3,2,1,0:T(8,128)S(1)}, f32[3,4,32,128]{3,2,1,0:T(8,128)S(1)}, u32[]{:S(2)}, u32[]{:S(2)}) %collective-permute-start.6) | collective-permute-done | bytes 196640 | tf_op jit(solution)/shard_map/ppermute | solution.py:732
  64.9 1.2 outgoing.2
  66.1 3.0 %collective-permute-start.7 = (f32[8,24,128]{2,1,0:T(8,128)S(1)}, f32[8,24,128]{2,1,0:T(8,128)S(1)}, u32[]{:S(2)}, u32[]{:S(2)}) collective-permute-start(f32[8,24,128]{2,1,0:T(8,128)S(1)} %bitcast.45), channel_id=1, source_target_pairs={{0,16},{1,5},{2,18},{3,7},{4,20},{5,1},{6,22},{7,3},{8,24},{9,13},... | collective-permute-start | bytes 294920 | tf_op jit(solution)/shard_map/ppermute | solution.py:710
  69.1 1.5 %collective-permute-start.8 = (f32[8,24,128]{2,1,0:T(8,128)S(1)}, f32[8,24,128]{2,1,0:T(8,128)S(1)}, u32[]{:S(2)}, u32[]{:S(2)}) collective-permute-start(f32[8,24,128]{2,1,0:T(8,128)S(1)} %bitcast.44), channel_id=1, source_target_pairs={{0,4},{1,17},{2,6},{3,19},{4,0},{5,21},{6,2},{7,23},{8,12},{9,25},... | collective-permute-start | bytes 294920 | tf_op jit(solution)/shard_map/ppermute | solution.py:710
  70.5 1.5 %collective-permute-start.9 = (f32[8,24,128]{2,1,0:T(8,128)S(1)}, f32[8,24,128]{2,1,0:T(8,128)S(1)}, u32[]{:S(2)}, u32[]{:S(2)}) collective-permute-start(f32[8,24,128]{2,1,0:T(8,128)S(1)} %bitcast.43), channel_id=1, source_target_pairs={{0,8},{1,25},{2,10},{3,27},{4,12},{5,29},{6,14},{7,31},{8,0},{9,17... | collective-permute-start | bytes 294920 | tf_op jit(solution)/shard_map/ppermute | solution.py:710
  72.0 0.6 collective-permute-start.10
  72.6 1.5 %collective-permute-start.11 = (f32[8,24,128]{2,1,0:T(8,128)S(1)}, f32[8,24,128]{2,1,0:T(8,128)S(1)}, u32[]{:S(2)}, u32[]{:S(2)}) collective-permute-start(f32[8,24,128]{2,1,0:T(8,128)S(1)} %bitcast.41), channel_id=1, source_target_pairs={{0,20},{1,13},{2,22},{3,15},{4,16},{5,9},{6,18},{7,11},{8,28},{9,5... | collective-permute-start | bytes 294920 | tf_op jit(solution)/shard_map/ppermute | solution.py:710
  74.0 3.3 %collective-permute-done.7.refs_1_ = f32[8,24,128]{2,1,0:T(8,128)S(1)} collective-permute-done((f32[8,24,128]{2,1,0:T(8,128)S(1)}, f32[8,24,128]{2,1,0:T(8,128)S(1)}, u32[]{:S(2)}, u32[]{:S(2)}) %collective-permute-start.7) | collective-permute-done | bytes 98336 | tf_op jit(solution)/shard_map/ppermute | solution.py:710
  77.3 0.4 collective-permute-start.12
  77.8 0.0 collective-permute-done.8.refs_2_
  77.8 3.2 %collective-permute-start.13 = (f32[8,24,128]{2,1,0:T(8,128)S(1)}, f32[8,24,128]{2,1,0:T(8,128)S(1)}, u32[]{:S(2)}, u32[]{:S(2)}) collective-permute-start(f32[8,24,128]{2,1,0:T(8,128)S(1)} %bitcast.39), channel_id=1, source_target_pairs={{0,28},{1,29},{2,30},{3,31},{4,24},{5,25},{6,26},{7,27},{8,20},{9,... | collective-permute-start | bytes 294920 | tf_op jit(solution)/shard_map/ppermute | solution.py:710
  80.9 0.0 all-to-all-done.1.refs_0_
  80.9 5.0 %solve.2.refs_9_ = f32[8,512,128]{2,1,0:T(8,128)S(1)} custom-call(f32[8,8,24,128]{3,2,1,0:T(8,128)S(1)} %all-to-all-done.1.refs_0_, f32[8,512,512]{2,1,0:T(8,128)} %refs_8_.1), custom_call_target="tpu_custom_call" | custom-call | bytes 8388608 | tf_op jit(solution)/shard_map/solve/pallas_call | solution.py:648
  85.9 0.0 collective-permute-done.9.refs_3_
  85.9 2.5 %collective-permute-done.11.refs_5_ = f32[8,24,128]{2,1,0:T(8,128)S(1)} collective-permute-done((f32[8,24,128]{2,1,0:T(8,128)S(1)}, f32[8,24,128]{2,1,0:T(8,128)S(1)}, u32[]{:S(2)}, u32[]{:S(2)}) %collective-permute-start.11) | collective-permute-done | bytes 98336 | tf_op jit(solution)/shard_map/ppermute | solution.py:710
  88.5 5.0 %solve.3 = (f32[8,2,24,128]{3,2,1,0:T(8,128)S(1)}, f32[8,2,24,128]{3,2,1,0:T(8,128)S(1)}, f32[8,2,24,128]{3,2,1,0:T(8,128)S(1)}, f32[8,2,24,128]{3,2,1,0:T(8,128...) custom-call(f32[8,24,128]{2,1,0:T(8,128)S(1)} %bitcast.38, ...), custom_call_target="tpu_custom_call" | custom-call | bytes 8388608 | tf_op jit(solution)/shard_map/solve/pallas_call | solution.py:648
  93.5 2.4 %collective-permute-start.16 = (f32[8,2,24,128]{3,2,1,0:T(8,128)S(1)}, f32[8,2,24,128]{3,2,1,0:T(8,128)S(1)}, u32[]{:S(2)}, u32[]{:S(2)}) collective-permute-start(f32[8,2,24,128]{3,2,1,0:T(8,128)S(1)} %get-tuple-element.61), channel_id=1, source_target_pairs={{0,16},{1,5},{2,18},{3,7},{4,20},{5,1},{6,22},{7,3},{8,24},{9,13},... | collective-permute-start | bytes 589832 | tf_op jit(solution)/shard_map/ppermute | solution.py:710
  95.9 1.3 %collective-permute-start.17 = (f32[8,2,24,128]{3,2,1,0:T(8,128)S(1)}, f32[8,2,24,128]{3,2,1,0:T(8,128)S(1)}, u32[]{:S(2)}, u32[]{:S(2)}) collective-permute-start(f32[8,2,24,128]{3,2,1,0:T(8,128)S(1)} %get-tuple-element.62), channel_id=1, source_target_pairs={{0,4},{1,17},{2,6},{3,19},{4,0},{5,21},{6,2},{7,23},{8,12},{9,25},... | collective-permute-start | bytes 589832 | tf_op jit(solution)/shard_map/ppermute | solution.py:710
  97.2 2.4 %collective-permute-start.19 = (f32[8,2,24,128]{3,2,1,0:T(8,128)S(1)}, f32[8,2,24,128]{3,2,1,0:T(8,128)S(1)}, u32[]{:S(2)}, u32[]{:S(2)}) collective-permute-start(f32[8,2,24,128]{3,2,1,0:T(8,128)S(1)} %get-tuple-element.64), channel_id=1, source_target_pairs={{0,24},{1,9},{2,26},{3,11},{4,28},{5,13},{6,30},{7,15},{8,16},{9,1... | collective-permute-start | bytes 589832 | tf_op jit(solution)/shard_map/ppermute | solution.py:710
  99.6 1.2 collective-permute-start.20
  100.8 8.6 %collective-permute-done.16 = f32[8,2,24,128]{3,2,1,0:T(8,128)S(1)} collective-permute-done((f32[8,2,24,128]{3,2,1,0:T(8,128)S(1)}, f32[8,2,24,128]{3,2,1,0:T(8,128)S(1)}, u32[]{:S(2)}, u32[]{:S(2)}) %collective-permute-start.16) | collective-permute-done | bytes 196640 | tf_op jit(solution)/shard_map/ppermute | solution.py:710
  109.4 1.7 %collective-permute-start.22 = (f32[8,2,24,128]{3,2,1,0:T(8,128)S(1)}, f32[8,2,24,128]{3,2,1,0:T(8,128)S(1)}, u32[]{:S(2)}, u32[]{:S(2)}) collective-permute-start(f32[8,2,24,128]{3,2,1,0:T(8,128)S(1)} %get-tuple-element.67), channel_id=1, source_target_pairs={{0,28},{1,29},{2,30},{3,31},{4,24},{5,25},{6,26},{7,27},{8,20},{9,... | collective-permute-start | bytes 589832 | tf_op jit(solution)/shard_map/ppermute | solution.py:710
  111.1 2.3 %collective-permute-done.18 = f32[8,2,24,128]{3,2,1,0:T(8,128)S(1)} collective-permute-done((f32[8,2,24,128]{3,2,1,0:T(8,128)S(1)}, f32[8,2,24,128]{3,2,1,0:T(8,128)S(1)}, u32[]{:S(2)}, u32[]{:S(2)}) %collective-permute-start.18) | collective-permute-done | bytes 196640 | tf_op jit(solution)/shard_map/ppermute | solution.py:710
  113.4 14.6 %collective-permute-done.20 = f32[8,2,24,128]{3,2,1,0:T(8,128)S(1)} collective-permute-done((f32[8,2,24,128]{3,2,1,0:T(8,128)S(1)}, f32[8,2,24,128]{3,2,1,0:T(8,128)S(1)}, u32[]{:S(2)}, u32[]{:S(2)}) %collective-permute-start.20) | collective-permute-done | bytes 196640 | tf_op jit(solution)/shard_map/ppermute | solution.py:710
  128.0 2.1 %restore.1 = f32[3,4,256,128]{3,2,1,0:T(8,128)} custom-call(f32[384,128]{1,0:T(8,128)S(1)} %bitcast.30, f32[384,128]{1,0:T(8,128)S(1)} %bitcast.31, f32[384,128]{1,0:T(8,128)S(1)} %bitcast.32, f32[384,128]{1,0:T(8,128)S(1)} %bitcast.33, f32[384,128]{1,0:T(8,128)S(1)} %bitcast.34, f32[384,128]{1,0:T(8,128)S(1)} %bitcast.35, f32[384,128]{1,0:T(8,128)S(1)} %bitcast.36, ...), custom_call_target="tpu_custom_call" | custom-call | bytes 3145728 | tf_op jit(solution)/shard_map/restore/pallas_call | solution.py:688
  (39 shorter events, 0.2 us)
Async XLA Ops:
  3.1 11.2 %collective-permute-start.1 = (f32[392,128]{1,0:T(8,128)}, f32[392,128]{1,0:T(8,128)S(1)}, u32[]{:S(2)}, u32[]{:S(2)}) collective-permute-start(f32[392,128]{1,0:T(8,128)} %get-tuple-element.39), channel_id=1, source_target_pairs={{0,24},{1,9},{2,26},{3,11},{8,16},{9,1},{10,18},{11,3},{16,8},{17,... | collective-permute-start | bytes 602120 | tf_op jit(solution)/shard_map/ppermute | solution.py:710
  8.3 19.1 %collective-permute-start = (f32[392,128]{1,0:T(8,128)}, f32[392,128]{1,0:T(8,128)S(1)}, u32[]{:S(2)}, u32[]{:S(2)}) collective-permute-start(f32[392,128]{1,0:T(8,128)} %get-tuple-element.38), channel_id=1, source_target_pairs={{0,8},{1,25},{2,10},{3,27},{8,0},{9,17},{10,2},{11,19},{16,24},{17... | collective-permute-start | bytes 602120 | tf_op jit(solution)/shard_map/ppermute | solution.py:710
  8.3 20.6 %collective-permute-start.2 = (f32[392,128]{1,0:T(8,128)}, f32[392,128]{1,0:T(8,128)S(1)}, u32[]{:S(2)}, u32[]{:S(2)}) collective-permute-start(f32[392,128]{1,0:T(8,128)} %get-tuple-element.40), channel_id=1, source_target_pairs={{0,16},{1,17},{2,18},{3,19},{8,24},{9,25},{10,26},{11,27},{16,0},{... | collective-permute-start | bytes 602120 | tf_op jit(solution)/shard_map/ppermute | solution.py:710
  11.0 15.6 %copy-start.3 = (f32[392,128]{1,0:T(8,128)S(1)}, f32[392,128]{1,0:T(8,128)}, u32[]{:S(2)}) copy-start(f32[392,128]{1,0:T(8,128)} %get-tuple-element.37.refs_0_) | copy-start | bytes 602116
  11.0 15.6 %copy-start.2 = (bf16[128,256]{1,0:T(8,128)(2,1)S(1)}, bf16[128,256]{1,0:T(8,128)(2,1)}, u32[]{:S(2)}) copy-start(bf16[128,256]{1,0:T(8,128)(2,1)} %constant.22.clone.rest_ref.refs_5_.refs_2_) | copy-start | bytes 196612
  11.0 15.6 %copy-start.4 = (bf16[128,256]{1,0:T(8,128)(2,1)S(1)}, bf16[128,256]{1,0:T(8,128)(2,1)}, u32[]{:S(2)}) copy-start(bf16[128,256]{1,0:T(8,128)(2,1)} %constant.21.clone.top_ref) | copy-start | bytes 196612
  11.0 15.6 %copy-start.6 = (s32[64]{0:T(128)S(1)}, s32[64]{0:T(128)}, u32[]{:S(2)}) copy-start(s32[64]{0:T(128)} %owner_ref.1) | copy-start | bytes 772
  11.0 18.0 %copy-start.5 = (s32[8]{0:T(128)S(1)}, s32[8]{0:T(128)}, u32[]{:S(2)}) copy-start(s32[8]{0:T(128)} %low_ref.11) | copy-start | bytes 100
  14.4 0.7 copy-start
  15.1 12.3 %copy-start.1 = (f32[392,128]{1,0:T(8,128)S(1)}, f32[392,128]{1,0:T(8,128)}, u32[]{:S(2)}) copy-start(f32[392,128]{1,0:T(8,128)} %copy-done) | copy-start | bytes 602116
  15.1 29.4 %all-to-all-start = ((f32[4,384,128]{2,1,0:T(8,128)}), f32[4,384,128]{2,1,0:T(8,128)S(1)}, u32[]{:S(2)}, u32[]{:S(2)}) async-start(f32[4,384,128]{2,1,0:T(8,128)} %hand_on.1), calls=%async_computation | async-start | bytes 1572864 | tf_op jit(solution)/shard_map/all_to_all | solution.py:758
  32.4 1.5 %collective-permute-start.3 = (f32[3,4,32,128]{3,2,1,0:T(8,128)S(1)}, f32[3,4,32,128]{3,2,1,0:T(8,128)S(1)}, u32[]{:S(2)}, u32[]{:S(2)}) collective-permute-start(f32[3,4,32,128]{3,2,1,0:T(8,128)S(1)} %get-tuple-element.45), channel_id=1, source_target_pairs={{0,1},{1,0},{2,3},{3,2},{4,5},{5,4},{6,7},{7,6},{8,9},{9,8},{10,11... | collective-permute-start | bytes 589832 | tf_op jit(solution)/shard_map/ppermute | solution.py:732
  34.0 7.0 %collective-permute-start.14 = (f32[3,4,32,128]{3,2,1,0:T(8,128)S(1)}, f32[3,4,32,128]{3,2,1,0:T(8,128)S(1)}, u32[]{:S(2)}, u32[]{:S(2)}) collective-permute-start(f32[3,4,32,128]{3,2,1,0:T(8,128)S(1)} %add.21.refs_4_.first_ref), channel_id=1, source_target_pairs={{0,2},{1,3},{2,0},{3,1},{4,6},{5,7},{6,4},{7,5},{8,10},{9,11},{10,... | collective-permute-start | bytes 589832 | tf_op jit(solution)/shard_map/ppermute | solution.py:732
  41.0 1.5 %collective-permute-start.15 = (f32[3,4,32,128]{3,2,1,0:T(8,128)S(1)}, f32[3,4,32,128]{3,2,1,0:T(8,128)S(1)}, u32[]{:S(2)}, u32[]{:S(2)}) collective-permute-start(f32[3,4,32,128]{3,2,1,0:T(8,128)S(1)} %ordered_sum.3.kept_ref), channel_id=1, source_target_pairs={{0,1},{1,0},{2,3},{3,2},{4,5},{5,4},{6,7},{7,6},{8,9},{9,8},{10,11... | collective-permute-start | bytes 589832 | tf_op jit(solution)/shard_map/ppermute | solution.py:732
  44.4 36.5 %all-to-all-start.1 = ((f32[8,8,24,128]{3,2,1,0:T(8,128)}), f32[8,8,24,128]{3,2,1,0:T(8,128)S(1)}, u32[]{:S(2)}, u32[]{:S(2)}) async-start(f32[8,8,24,128]{3,2,1,0:T(8,128)} %bitcast.13), calls=%async_computation.1 | async-start | bytes 1572864 | tf_op jit(solution)/shard_map/all_to_all | solution.py:789
  54.8 1.5 %collective-permute-start.4 = (f32[3,4,32,128]{3,2,1,0:T(8,128)S(1)}, f32[3,4,32,128]{3,2,1,0:T(8,128)S(1)}, u32[]{:S(2)}, u32[]{:S(2)}) collective-permute-start(f32[3,4,32,128]{3,2,1,0:T(8,128)S(1)} %get-tuple-element.49), channel_id=1, source_target_pairs={{0,1},{1,0},{2,3},{3,2},{4,5},{5,4},{6,7},{7,6},{8,9},{9,8},{10,11... | collective-permute-start | bytes 589832 | tf_op jit(solution)/shard_map/ppermute | solution.py:732
  56.4 7.0 %collective-permute-start.5 = (f32[3,4,32,128]{3,2,1,0:T(8,128)S(1)}, f32[3,4,32,128]{3,2,1,0:T(8,128)S(1)}, u32[]{:S(2)}, u32[]{:S(2)}) collective-permute-start(f32[3,4,32,128]{3,2,1,0:T(8,128)S(1)} %add.22.first_ref), channel_id=1, source_target_pairs={{0,2},{1,3},{2,0},{3,1},{4,6},{5,7},{6,4},{7,5},{8,10},{9,11},{10,... | collective-permute-start | bytes 589832 | tf_op jit(solution)/shard_map/ppermute | solution.py:732
  63.4 1.5 %collective-permute-start.6 = (f32[3,4,32,128]{3,2,1,0:T(8,128)S(1)}, f32[3,4,32,128]{3,2,1,0:T(8,128)S(1)}, u32[]{:S(2)}, u32[]{:S(2)}) collective-permute-start(f32[3,4,32,128]{3,2,1,0:T(8,128)S(1)} %ordered_sum.2.kept_ref), channel_id=1, source_target_pairs={{0,1},{1,0},{2,3},{3,2},{4,5},{5,4},{6,7},{7,6},{8,9},{9,8},{10,11... | collective-permute-start | bytes 589832 | tf_op jit(solution)/shard_map/ppermute | solution.py:732
  66.1 11.2 %collective-permute-start.7 = (f32[8,24,128]{2,1,0:T(8,128)S(1)}, f32[8,24,128]{2,1,0:T(8,128)S(1)}, u32[]{:S(2)}, u32[]{:S(2)}) collective-permute-start(f32[8,24,128]{2,1,0:T(8,128)S(1)} %bitcast.45), channel_id=1, source_target_pairs={{0,16},{1,5},{2,18},{3,7},{4,20},{5,1},{6,22},{7,3},{8,24},{9,13},... | collective-permute-start | bytes 294920 | tf_op jit(solution)/shard_map/ppermute | solution.py:710
  69.1 8.7 %collective-permute-start.8 = (f32[8,24,128]{2,1,0:T(8,128)S(1)}, f32[8,24,128]{2,1,0:T(8,128)S(1)}, u32[]{:S(2)}, u32[]{:S(2)}) collective-permute-start(f32[8,24,128]{2,1,0:T(8,128)S(1)} %bitcast.44), channel_id=1, source_target_pairs={{0,4},{1,17},{2,6},{3,19},{4,0},{5,21},{6,2},{7,23},{8,12},{9,25},... | collective-permute-start | bytes 294920 | tf_op jit(solution)/shard_map/ppermute | solution.py:710
  70.5 15.4 %collective-permute-start.9 = (f32[8,24,128]{2,1,0:T(8,128)S(1)}, f32[8,24,128]{2,1,0:T(8,128)S(1)}, u32[]{:S(2)}, u32[]{:S(2)}) collective-permute-start(f32[8,24,128]{2,1,0:T(8,128)S(1)} %bitcast.43), channel_id=1, source_target_pairs={{0,8},{1,25},{2,10},{3,27},{4,12},{5,29},{6,14},{7,31},{8,0},{9,17... | collective-permute-start | bytes 294920 | tf_op jit(solution)/shard_map/ppermute | solution.py:710
  72.0 13.9 %collective-permute-start.10 = (f32[8,24,128]{2,1,0:T(8,128)S(1)}, f32[8,24,128]{2,1,0:T(8,128)S(1)}, u32[]{:S(2)}, u32[]{:S(2)}) collective-permute-start(f32[8,24,128]{2,1,0:T(8,128)S(1)} %bitcast.42), channel_id=1, source_target_pairs={{0,24},{1,9},{2,26},{3,11},{4,28},{5,13},{6,30},{7,15},{8,16},{9,1... | collective-permute-start | bytes 294920 | tf_op jit(solution)/shard_map/ppermute | solution.py:710
  72.6 15.9 %collective-permute-start.11 = (f32[8,24,128]{2,1,0:T(8,128)S(1)}, f32[8,24,128]{2,1,0:T(8,128)S(1)}, u32[]{:S(2)}, u32[]{:S(2)}) collective-permute-start(f32[8,24,128]{2,1,0:T(8,128)S(1)} %bitcast.41), channel_id=1, source_target_pairs={{0,20},{1,13},{2,22},{3,15},{4,16},{5,9},{6,18},{7,11},{8,28},{9,5... | collective-permute-start | bytes 294920 | tf_op jit(solution)/shard_map/ppermute | solution.py:710
  77.3 11.1 %collective-permute-start.12 = (f32[8,24,128]{2,1,0:T(8,128)S(1)}, f32[8,24,128]{2,1,0:T(8,128)S(1)}, u32[]{:S(2)}, u32[]{:S(2)}) collective-permute-start(f32[8,24,128]{2,1,0:T(8,128)S(1)} %bitcast.40), channel_id=1, source_target_pairs={{0,12},{1,21},{2,14},{3,23},{4,8},{5,17},{6,10},{7,19},{8,4},{9,29... | collective-permute-start | bytes 294920 | tf_op jit(solution)/shard_map/ppermute | solution.py:710
  77.8 10.7 %collective-permute-start.13 = (f32[8,24,128]{2,1,0:T(8,128)S(1)}, f32[8,24,128]{2,1,0:T(8,128)S(1)}, u32[]{:S(2)}, u32[]{:S(2)}) collective-permute-start(f32[8,24,128]{2,1,0:T(8,128)S(1)} %bitcast.39), channel_id=1, source_target_pairs={{0,28},{1,29},{2,30},{3,31},{4,24},{5,25},{6,26},{7,27},{8,20},{9,... | collective-permute-start | bytes 294920 | tf_op jit(solution)/shard_map/ppermute | solution.py:710
  93.5 15.9 %collective-permute-start.16 = (f32[8,2,24,128]{3,2,1,0:T(8,128)S(1)}, f32[8,2,24,128]{3,2,1,0:T(8,128)S(1)}, u32[]{:S(2)}, u32[]{:S(2)}) collective-permute-start(f32[8,2,24,128]{3,2,1,0:T(8,128)S(1)} %get-tuple-element.61), channel_id=1, source_target_pairs={{0,16},{1,5},{2,18},{3,7},{4,20},{5,1},{6,22},{7,3},{8,24},{9,13},... | collective-permute-start | bytes 589832 | tf_op jit(solution)/shard_map/ppermute | solution.py:710
  95.9 13.5 %collective-permute-start.17 = (f32[8,2,24,128]{3,2,1,0:T(8,128)S(1)}, f32[8,2,24,128]{3,2,1,0:T(8,128)S(1)}, u32[]{:S(2)}, u32[]{:S(2)}) collective-permute-start(f32[8,2,24,128]{3,2,1,0:T(8,128)S(1)} %get-tuple-element.62), channel_id=1, source_target_pairs={{0,4},{1,17},{2,6},{3,19},{4,0},{5,21},{6,2},{7,23},{8,12},{9,25},... | collective-permute-start | bytes 589832 | tf_op jit(solution)/shard_map/ppermute | solution.py:710
  97.2 16.2 %collective-permute-start.18 = (f32[8,2,24,128]{3,2,1,0:T(8,128)S(1)}, f32[8,2,24,128]{3,2,1,0:T(8,128)S(1)}, u32[]{:S(2)}, u32[]{:S(2)}) collective-permute-start(f32[8,2,24,128]{3,2,1,0:T(8,128)S(1)} %get-tuple-element.63), channel_id=1, source_target_pairs={{0,8},{1,25},{2,10},{3,27},{4,12},{5,29},{6,14},{7,31},{8,0},{9,17... | collective-permute-start | bytes 589832 | tf_op jit(solution)/shard_map/ppermute | solution.py:710
  97.2 16.2 %collective-permute-start.19 = (f32[8,2,24,128]{3,2,1,0:T(8,128)S(1)}, f32[8,2,24,128]{3,2,1,0:T(8,128)S(1)}, u32[]{:S(2)}, u32[]{:S(2)}) collective-permute-start(f32[8,2,24,128]{3,2,1,0:T(8,128)S(1)} %get-tuple-element.64), channel_id=1, source_target_pairs={{0,24},{1,9},{2,26},{3,11},{4,28},{5,13},{6,30},{7,15},{8,16},{9,1... | collective-permute-start | bytes 589832 | tf_op jit(solution)/shard_map/ppermute | solution.py:710
  99.6 28.5 %collective-permute-start.20 = (f32[8,2,24,128]{3,2,1,0:T(8,128)S(1)}, f32[8,2,24,128]{3,2,1,0:T(8,128)S(1)}, u32[]{:S(2)}, u32[]{:S(2)}) collective-permute-start(f32[8,2,24,128]{3,2,1,0:T(8,128)S(1)} %get-tuple-element.65), channel_id=1, source_target_pairs={{0,20},{1,13},{2,22},{3,15},{4,16},{5,9},{6,18},{7,11},{8,28},{9,5... | collective-permute-start | bytes 589832 | tf_op jit(solution)/shard_map/ppermute | solution.py:710
  109.4 18.6 %collective-permute-start.21 = (f32[8,2,24,128]{3,2,1,0:T(8,128)S(1)}, f32[8,2,24,128]{3,2,1,0:T(8,128)S(1)}, u32[]{:S(2)}, u32[]{:S(2)}) collective-permute-start(f32[8,2,24,128]{3,2,1,0:T(8,128)S(1)} %get-tuple-element.66), channel_id=1, source_target_pairs={{0,12},{1,21},{2,14},{3,23},{4,8},{5,17},{6,10},{7,19},{8,4},{9,29... | collective-permute-start | bytes 589832 | tf_op jit(solution)/shard_map/ppermute | solution.py:710
  109.4 18.6 %collective-permute-start.22 = (f32[8,2,24,128]{3,2,1,0:T(8,128)S(1)}, f32[8,2,24,128]{3,2,1,0:T(8,128)S(1)}, u32[]{:S(2)}, u32[]{:S(2)}) collective-permute-start(f32[8,2,24,128]{3,2,1,0:T(8,128)S(1)} %get-tuple-element.67), channel_id=1, source_target_pairs={{0,28},{1,29},{2,30},{3,31},{4,24},{5,25},{6,26},{7,27},{8,20},{9,... | collective-permute-start | bytes 589832 | tf_op jit(solution)/shard_map/ppermute | solution.py:710

commit v18 on v16

--- a/solution.py
+++ b/solution.py
@@ -118,15 +118,15 @@
     return pltpu.CompilerParams(vmem_limit_bytes=48 * 1024 * 1024)
 
 
-ORDERS = {4: (1, 3, 2), 8: (4, 1, 2, 6, 5, 3, 7)}
+ORDERS = {
+    4: ((1, 3, 2), (3, 1, 2)),
+    8: ((4, 1, 6, 2, 5, 3, 7), (5, 4, 1, 6, 2, 7, 3)),
+}
 
 
 def steps_of(count):
-    even = ORDERS.get(count, tuple(range(1, count)))
-    odd = list(even)
-    for first in range(0, count - 2, 2):
-        odd[first], odd[first + 1] = (even[first + 1], even[first])
-    return (0,) + tuple(even), (0,) + tuple(odd)
+    even, odd = ORDERS.get(count, (tuple(range(1, count)),) * 2)
+    return (0,) + even, (0,) + odd
 
 
 def step_at(count, position):

time: 130 us -> 131 us (level)
  waiting for transfers between devices: 47.4 us -> 51.6 us
  starting transfers between devices: 47.6 us -> 44.7 us
    ppermute x17, waiting for transfers between devices: 37 us -> 41.2 us  [exchange(): result[position] = lax.ppermute(blocks[position], axes + ('real',), pairs)]
    ppermute x17, starting transfers between devices: 26.4 us -> 23.6 us  [exchange(): result[position] = lax.ppermute(blocks[position], axes + ('real',), pairs)]
  transfers between devices with their start and end apart: 25 -> 25, of which waited for: 13 -> 14; matrix products, arithmetic and copies ran while one was open for 1% -> 1% of each run, Pallas kernels for 18% -> 18%
where the time goes in v18:
time: 131 us; the launch traced here: 130 us
  waiting for transfers between devices  51.6 us (39%)
  starting transfers between devices  44.7 us (34%)
  Pallas kernels  31.7 us (24%)
  local copies, waits for them, and re-layouts  1.56 us (1%)
    ppermute x17, waiting for transfers between devices, exchange(): result[position] = lax.ppermute(blocks[position], axes + ('real',), pairs)  41.2 us
    ppermute x17, starting transfers between devices, exchange(): result[position] = lax.ppermute(blocks[position], axes + ('real',), pairs)  23.6 us
    all_to_all x1, starting transfers between devices, local(): block = lax.all_to_all(block, 'kx', split_axis=0, concat_axis=0, tiled=True)  10.8 us
    ppermute x6, waiting for transfers between devices, swap(): return lax.ppermute(value, 'real', pairs)  10.4 us
    pallas_call x2, Pallas kernels, solve(): pl.pallas_call(functools.partial(solve_kernel, groups=groups, kx_count=kx...  8.62 us
    pallas_call x2, Pallas kernels, stress_terms(): pl.pallas_call(stress_kernel, out_shape=(jax.ShapeDtypeStruct(shape, jnp....  6.94 us
    all_to_all x1, starting transfers between devices, local(): lax.all_to_all(block, ('kx', 'ht'), split_axis=0, concat_axis=0, tiled=True)  6.91 us
    pallas_call x2, Pallas kernels, high_terms(): pl.pallas_call(products_kernel, out_shape=jax.ShapeDtypeStruct((component...  6 us
  transfers between devices with their start and end apart: 25, of which 14 were waited for; matrix products, arithmetic and copies ran while one was open for 1% of the time, Pallas kernels for 18%

profile of v18, /device:TPU:0, one launch (start us, length us, event | category | flops | bytes accessed | tf_op | source)
XLA Modules:
  0.0 130.0 jit_solution(571990086473803544)
XLA Ops:
  0.0 2.1 %pack_first.1 = (f32[392,128]{1,0:T(8,128)}, f32[392,128]{1,0:T(8,128)}, f32[392,128]{1,0:T(8,128)}, f32[392,128]{1,0:T(8,128)}) custom-call(s32[4,8]{1,0:T(4,128)} %near_ref.1, s32[4]{0:T(128)} %count_ref.1, f32[12,2,4,32,128]{4,3,2,1,0:T(8,128)} %bitcast.46), custom_call_target="tpu_custom_call" | custom-call | bytes 1572864 | tf_op jit(solution)/shard_map/pack_first/pallas_call | solution.py:175
  2.1 5.0 %collective-permute-start.1 = (f32[392,128]{1,0:T(8,128)}, f32[392,128]{1,0:T(8,128)S(1)}, u32[]{:S(2)}, u32[]{:S(2)}) collective-permute-start(f32[392,128]{1,0:T(8,128)} %get-tuple-element.39), channel_id=1, source_target_pairs={{0,24},{1,9},{2,26},{3,11},{8,16},{9,1},{10,18},{11,3},{16,8},{17,... | collective-permute-start | bytes 602120 | tf_op jit(solution)/shard_map/ppermute | solution.py:693
  7.2 0.0 collective-permute-start
  7.2 0.6 collective-permute-start.2
  7.7 2.1 %pack.1.value_ref = f32[4,384,128]{2,1,0:T(8,128)} custom-call(f32[12,2,4,32,128]{4,3,2,1,0:T(8,128)} %bitcast.47), custom_call_target="tpu_custom_call" | custom-call | bytes 1572864 | tf_op jit(solution)/shard_map/pack/pallas_call | solution.py:201
  9.8 0.0 copy-start.5
  9.8 3.5 %collective-permute-done.1.after_ref.refs_2_ = f32[392,128]{1,0:T(8,128)S(1)} collective-permute-done((f32[392,128]{1,0:T(8,128)}, f32[392,128]{1,0:T(8,128)S(1)}, u32[]{:S(2)}, u32[]{:S(2)}) %collective-permute-start.1) | collective-permute-done | bytes 200736 | tf_op jit(solution)/shard_map/ppermute | solution.py:693
  13.3 0.7 copy-done
  14.0 10.8 %all-to-all-start = ((f32[4,384,128]{2,1,0:T(8,128)}), f32[4,384,128]{2,1,0:T(8,128)S(1)}, u32[]{:S(2)}, u32[]{:S(2)}) async-start(f32[4,384,128]{2,1,0:T(8,128)} %hand_on.1), calls=%async_computation | async-start | bytes 1572864 | tf_op jit(solution)/shard_map/all_to_all | solution.py:741
  24.8 0.1 broadcast_in_dim.85
  24.8 0.1 broadcast_in_dim.86
  24.9 0.1 broadcast_in_dim.91
  25.0 0.1 broadcast_in_dim.92
  25.1 0.1 broadcast_in_dim.96
  25.2 0.1 broadcast_in_dim.97
  25.3 0.1 broadcast_in_dim.101
  25.4 0.1 broadcast_in_dim.102
  25.5 0.8 tables.1
  26.3 0.0 collective-permute-done.refs_1_
  26.3 1.5 %collective-permute-done.2.refs_3_ = f32[392,128]{1,0:T(8,128)S(1)} collective-permute-done((f32[392,128]{1,0:T(8,128)}, f32[392,128]{1,0:T(8,128)S(1)}, u32[]{:S(2)}, u32[]{:S(2)}) %collective-permute-start.2) | collective-permute-done | bytes 200736 | tf_op jit(solution)/shard_map/ppermute | solution.py:693
  27.8 0.1 add_convert_fusion
  27.9 3.5 %stress.2 = (f32[3,16,32,128]{3,2,1,0:T(8,128)S(1)}, f32[3,16,32,256]{3,2,1,0:T(8,128)S(1)}, f32[3,4,32,128]{3,2,1,0:T(8,128)S(1)}, f32[3,4,32,128]{3,2,1,0:T(8,128)S(1)}) custom-call(s32[8]{0:T(128)S(1)} %copy-done.5, s32[16,8]{1,0:T(8,128)S(1)} %bitcast.26, f32[392,128]{1,0:T(8,128)S(1)} %copy-done.3, f32[392,128]{1,0:T(8,128)S(1)} %collective-permute-done.refs_1_, ...), custom_call_target="tpu_custom_call" | custom-call | bytes 12582912 | tf_op jit(solution)/shard_map/stress/pallas_call | solution.py:368
  31.4 0.1 collective-permute-start.3
  31.5 1.4 %collective-permute-done.3 = f32[3,4,32,128]{3,2,1,0:T(8,128)S(1)} collective-permute-done((f32[3,4,32,128]{3,2,1,0:T(8,128)S(1)}, f32[3,4,32,128]{3,2,1,0:T(8,128)S(1)}, u32[]{:S(2)}, u32[]{:S(2)}) %collective-permute-start.3) | collective-permute-done | bytes 196640 | tf_op jit(solution)/shard_map/ppermute | solution.py:715
  32.9 1.6 %collective-permute-start.14 = (f32[3,4,32,128]{3,2,1,0:T(8,128)S(1)}, f32[3,4,32,128]{3,2,1,0:T(8,128)S(1)}, u32[]{:S(2)}, u32[]{:S(2)}) collective-permute-start(f32[3,4,32,128]{3,2,1,0:T(8,128)S(1)} %add.21.refs_4_.first_ref), channel_id=1, source_target_pairs={{0,2},{1,3},{2,0},{3,1},{4,6},{5,7},{6,4},{7,5},{8,10},{9,11},{10,... | collective-permute-start | bytes 589832 | tf_op jit(solution)/shard_map/ppermute | solution.py:715
  34.5 0.2 slice_reduce_fusion.count_ref
  34.7 3.0 %products.3._.forcing_ref = f32[3,8,32,128]{3,2,1,0:T(8,128)S(1)} custom-call(s32[8]{0:T(128)S(1)} %copy-done.5, s32[16,8]{1,0:T(8,128)S(1)} %bitcast.27, s32[16]{0:T(128)S(1)} %slice_reduce_fusion.count_ref, f32[3,16,32,256]{3,2,1,0:T(8,128)S(1)} %get-tuple-element.59.physical, bf16[256,256]{1,0:T(8,128)(2,1)S(1)} %get-tuple-element.42.refs_6_.refs_3_.back_ref, ...), custom_call_target="tpu_custom_call" | custom-call | bytes 12582912 | tf_op jit(solution)/shard_map/products/pallas_call | solution.py:433
  37.7 2.3 %collective-permute-done.14.second_ref = f32[3,4,32,128]{3,2,1,0:T(8,128)S(1)} collective-permute-done((f32[3,4,32,128]{3,2,1,0:T(8,128)S(1)}, f32[3,4,32,128]{3,2,1,0:T(8,128)S(1)}, u32[]{:S(2)}, u32[]{:S(2)}) %collective-permute-start.14) | collective-permute-done | bytes 196640 | tf_op jit(solution)/shard_map/ppermute | solution.py:715
  39.9 0.1 collective-permute-start.15
  40.0 1.4 %collective-permute-done.15.other_ref = f32[3,4,32,128]{3,2,1,0:T(8,128)S(1)} collective-permute-done((f32[3,4,32,128]{3,2,1,0:T(8,128)S(1)}, f32[3,4,32,128]{3,2,1,0:T(8,128)S(1)}, u32[]{:S(2)}, u32[]{:S(2)}) %collective-permute-start.15) | collective-permute-done | bytes 196640 | tf_op jit(solution)/shard_map/ppermute | solution.py:715
  41.5 1.9 %outgoing.3 = f32[1536,128]{1,0:T(8,128)} custom-call(s32[8]{0:T(128)S(1)} %copy-done.5, s32[16]{0:T(128)S(1)} %slice_reduce_fusion.count_ref, f32[3,16,32,128]{3,2,1,0:T(8,128)S(1)} %get-tuple-element.58.slotted_ref, f32[3,8,32,128]{3,2,1,0:T(8,128)S(1)} %products.3._.forcing_ref, f32[3,4,32,128]{3,2,1,0:T(8,128)S(1)} %ordered_sum.3.kept_ref, ...), custom_call_target="tpu_custom_call" | custom-call | bytes 1572864 | tf_op jit(solution)/shard_map/outgoing/pallas_call | solution.py:499
  43.4 0.0 all-to-all-done.refs_0_
  43.4 6.9 %all-to-all-start.1 = ((f32[8,8,24,128]{3,2,1,0:T(8,128)}), f32[8,8,24,128]{3,2,1,0:T(8,128)S(1)}, u32[]{:S(2)}, u32[]{:S(2)}) async-start(f32[8,8,24,128]{3,2,1,0:T(8,128)} %bitcast.13), calls=%async_computation.1 | async-start | bytes 1572864 | tf_op jit(solution)/shard_map/all_to_all | solution.py:772
  50.3 3.5 %stress.3 = (f32[3,16,32,128]{3,2,1,0:T(8,128)S(1)}, f32[3,16,32,256]{3,2,1,0:T(8,128)S(1)}, f32[3,4,32,128]{3,2,1,0:T(8,128)S(1)}, f32[3,4,32,128]{3,2,1,0:T(8,128)S(1)}) custom-call(s32[8]{0:T(128)S(1)} %copy-done.5, s32[16,8]{1,0:T(8,128)S(1)} %bitcast.28, f32[4,384,128]{2,1,0:T(8,128)S(1)} %all-to-all-done.refs_0_, ...), custom_call_target="tpu_custom_call" | custom-call | bytes 12582912 | tf_op jit(solution)/shard_map/stress/pallas_call | solution.py:368
  53.7 0.1 collective-permute-start.4
  53.8 1.4 %collective-permute-done.4 = f32[3,4,32,128]{3,2,1,0:T(8,128)S(1)} collective-permute-done((f32[3,4,32,128]{3,2,1,0:T(8,128)S(1)}, f32[3,4,32,128]{3,2,1,0:T(8,128)S(1)}, u32[]{:S(2)}, u32[]{:S(2)}) %collective-permute-start.4) | collective-permute-done | bytes 196640 | tf_op jit(solution)/shard_map/ppermute | solution.py:715
  55.3 1.6 %collective-permute-start.5 = (f32[3,4,32,128]{3,2,1,0:T(8,128)S(1)}, f32[3,4,32,128]{3,2,1,0:T(8,128)S(1)}, u32[]{:S(2)}, u32[]{:S(2)}) collective-permute-start(f32[3,4,32,128]{3,2,1,0:T(8,128)S(1)} %add.22.first_ref), channel_id=1, source_target_pairs={{0,2},{1,3},{2,0},{3,1},{4,6},{5,7},{6,4},{7,5},{8,10},{9,11},{10,... | collective-permute-start | bytes 589832 | tf_op jit(solution)/shard_map/ppermute | solution.py:715
  56.8 3.0 %products.2._.forcing_ref = f32[3,8,32,128]{3,2,1,0:T(8,128)S(1)} custom-call(s32[8]{0:T(128)S(1)} %copy-done.5, s32[16,8]{1,0:T(8,128)S(1)} %bitcast.29, s32[16]{0:T(128)S(1)} %slice_reduce_fusion.count_ref, f32[3,16,32,256]{3,2,1,0:T(8,128)S(1)} %get-tuple-element.47.physical, bf16[256,256]{1,0:T(8,128)(2,1)S(1)} %get-tuple-element.42.refs_6_.refs_3_.back_ref, ...), custom_call_target="tpu_custom_call" | custom-call | bytes 12582912 | tf_op jit(solution)/shard_map/products/pallas_call | solution.py:433
  59.8 2.5 %collective-permute-done.5.second_ref = f32[3,4,32,128]{3,2,1,0:T(8,128)S(1)} collective-permute-done((f32[3,4,32,128]{3,2,1,0:T(8,128)S(1)}, f32[3,4,32,128]{3,2,1,0:T(8,128)S(1)}, u32[]{:S(2)}, u32[]{:S(2)}) %collective-permute-start.5) | collective-permute-done | bytes 196640 | tf_op jit(solution)/shard_map/ppermute | solution.py:715
  62.3 0.1 collective-permute-start.6
  62.4 1.4 %collective-permute-done.6.other_ref = f32[3,4,32,128]{3,2,1,0:T(8,128)S(1)} collective-permute-done((f32[3,4,32,128]{3,2,1,0:T(8,128)S(1)}, f32[3,4,32,128]{3,2,1,0:T(8,128)S(1)}, u32[]{:S(2)}, u32[]{:S(2)}) %collective-permute-start.6) | collective-permute-done | bytes 196640 | tf_op jit(solution)/shard_map/ppermute | solution.py:715
  63.8 1.2 outgoing.2
  65.0 3.0 %collective-permute-start.7 = (f32[8,24,128]{2,1,0:T(8,128)S(1)}, f32[8,24,128]{2,1,0:T(8,128)S(1)}, u32[]{:S(2)}, u32[]{:S(2)}) collective-permute-start(f32[8,24,128]{2,1,0:T(8,128)S(1)} %bitcast.45), channel_id=1, source_target_pairs={{0,16},{1,21},{2,18},{3,23},{4,20},{5,17},{6,22},{7,19},{8,24},{9,... | collective-permute-start | bytes 294920 | tf_op jit(solution)/shard_map/ppermute | solution.py:693
  68.0 1.5 %collective-permute-start.8 = (f32[8,24,128]{2,1,0:T(8,128)S(1)}, f32[8,24,128]{2,1,0:T(8,128)S(1)}, u32[]{:S(2)}, u32[]{:S(2)}) collective-permute-start(f32[8,24,128]{2,1,0:T(8,128)S(1)} %bitcast.44), channel_id=1, source_target_pairs={{0,4},{1,17},{2,6},{3,19},{4,0},{5,21},{6,2},{7,23},{8,12},{9,25},... | collective-permute-start | bytes 294920 | tf_op jit(solution)/shard_map/ppermute | solution.py:693
  69.5 1.5 %collective-permute-start.9 = (f32[8,24,128]{2,1,0:T(8,128)S(1)}, f32[8,24,128]{2,1,0:T(8,128)S(1)}, u32[]{:S(2)}, u32[]{:S(2)}) collective-permute-start(f32[8,24,128]{2,1,0:T(8,128)S(1)} %bitcast.43), channel_id=1, source_target_pairs={{0,24},{1,5},{2,26},{3,7},{4,28},{5,1},{6,30},{7,3},{8,16},{9,13},... | collective-permute-start | bytes 294920 | tf_op jit(solution)/shard_map/ppermute | solution.py:693
  70.9 0.0 collective-permute-start.10
  70.9 2.9 %collective-permute-start.11 = (f32[8,24,128]{2,1,0:T(8,128)S(1)}, f32[8,24,128]{2,1,0:T(8,128)S(1)}, u32[]{:S(2)}, u32[]{:S(2)}) collective-permute-start(f32[8,24,128]{2,1,0:T(8,128)S(1)} %bitcast.41), channel_id=1, source_target_pairs={{0,20},{1,9},{2,22},{3,11},{4,16},{5,13},{6,18},{7,15},{8,28},{9,1... | collective-permute-start | bytes 294920 | tf_op jit(solution)/shard_map/ppermute | solution.py:693
  73.9 5.9 %collective-permute-done.7.refs_1_ = f32[8,24,128]{2,1,0:T(8,128)S(1)} collective-permute-done((f32[8,24,128]{2,1,0:T(8,128)S(1)}, f32[8,24,128]{2,1,0:T(8,128)S(1)}, u32[]{:S(2)}, u32[]{:S(2)}) %collective-permute-start.7) | collective-permute-done | bytes 98336 | tf_op jit(solution)/shard_map/ppermute | solution.py:693
  79.8 0.0 collective-permute-start.12
  79.8 2.2 %collective-permute-start.13 = (f32[8,24,128]{2,1,0:T(8,128)S(1)}, f32[8,24,128]{2,1,0:T(8,128)S(1)}, u32[]{:S(2)}, u32[]{:S(2)}) collective-permute-start(f32[8,24,128]{2,1,0:T(8,128)S(1)} %bitcast.39), channel_id=1, source_target_pairs={{0,28},{1,13},{2,30},{3,15},{4,24},{5,9},{6,26},{7,11},{8,20},{9,5... | collective-permute-start | bytes 294920 | tf_op jit(solution)/shard_map/ppermute | solution.py:693
  82.0 4.1 %solve.2.refs_9_ = f32[8,512,128]{2,1,0:T(8,128)S(1)} custom-call(f32[8,8,24,128]{3,2,1,0:T(8,128)S(1)} %all-to-all-done.1.refs_0_, f32[8,512,512]{2,1,0:T(8,128)} %refs_8_.1), custom_call_target="tpu_custom_call" | custom-call | bytes 8388608 | tf_op jit(solution)/shard_map/solve/pallas_call | solution.py:631
  86.1 0.5 collective-permute-done.11.refs_5_
  86.6 1.8 %collective-permute-done.12.refs_6_ = f32[8,24,128]{2,1,0:T(8,128)S(1)} collective-permute-done((f32[8,24,128]{2,1,0:T(8,128)S(1)}, f32[8,24,128]{2,1,0:T(8,128)S(1)}, u32[]{:S(2)}, u32[]{:S(2)}) %collective-permute-start.12) | collective-permute-done | bytes 98336 | tf_op jit(solution)/shard_map/ppermute | solution.py:693
  88.4 4.5 %solve.3 = (f32[8,2,24,128]{3,2,1,0:T(8,128)S(1)}, f32[8,2,24,128]{3,2,1,0:T(8,128)S(1)}, f32[8,2,24,128]{3,2,1,0:T(8,128)S(1)}, f32[8,2,24,128]{3,2,1,0:T(8,128...) custom-call(f32[8,24,128]{2,1,0:T(8,128)S(1)} %bitcast.38, ...), custom_call_target="tpu_custom_call" | custom-call | bytes 8388608 | tf_op jit(solution)/shard_map/solve/pallas_call | solution.py:631
  92.9 0.7 collective-permute-start.16
  93.6 1.8 %collective-permute-start.17 = (f32[8,2,24,128]{3,2,1,0:T(8,128)S(1)}, f32[8,2,24,128]{3,2,1,0:T(8,128)S(1)}, u32[]{:S(2)}, u32[]{:S(2)}) collective-permute-start(f32[8,2,24,128]{3,2,1,0:T(8,128)S(1)} %get-tuple-element.62), channel_id=1, source_target_pairs={{0,4},{1,17},{2,6},{3,19},{4,0},{5,21},{6,2},{7,23},{8,12},{9,25},... | collective-permute-start | bytes 589832 | tf_op jit(solution)/shard_map/ppermute | solution.py:693
  95.4 1.4 %collective-permute-start.18 = (f32[8,2,24,128]{3,2,1,0:T(8,128)S(1)}, f32[8,2,24,128]{3,2,1,0:T(8,128)S(1)}, u32[]{:S(2)}, u32[]{:S(2)}) collective-permute-start(f32[8,2,24,128]{3,2,1,0:T(8,128)S(1)} %get-tuple-element.63), channel_id=1, source_target_pairs={{0,24},{1,5},{2,26},{3,7},{4,28},{5,1},{6,30},{7,3},{8,16},{9,13},... | collective-permute-start | bytes 589832 | tf_op jit(solution)/shard_map/ppermute | solution.py:693
  96.8 0.6 collective-permute-start.19
  97.4 2.1 %collective-permute-start.20 = (f32[8,2,24,128]{3,2,1,0:T(8,128)S(1)}, f32[8,2,24,128]{3,2,1,0:T(8,128)S(1)}, u32[]{:S(2)}, u32[]{:S(2)}) collective-permute-start(f32[8,2,24,128]{3,2,1,0:T(8,128)S(1)} %get-tuple-element.65), channel_id=1, source_target_pairs={{0,20},{1,9},{2,22},{3,11},{4,16},{5,13},{6,18},{7,15},{8,28},{9,1... | collective-permute-start | bytes 589832 | tf_op jit(solution)/shard_map/ppermute | solution.py:693
  99.5 13.9 %collective-permute-done.16 = f32[8,2,24,128]{3,2,1,0:T(8,128)S(1)} collective-permute-done((f32[8,2,24,128]{3,2,1,0:T(8,128)S(1)}, f32[8,2,24,128]{3,2,1,0:T(8,128)S(1)}, u32[]{:S(2)}, u32[]{:S(2)}) %collective-permute-start.16) | collective-permute-done | bytes 196640 | tf_op jit(solution)/shard_map/ppermute | solution.py:693
  113.4 0.4 collective-permute-start.22
  113.8 13.3 %collective-permute-done.20 = f32[8,2,24,128]{3,2,1,0:T(8,128)S(1)} collective-permute-done((f32[8,2,24,128]{3,2,1,0:T(8,128)S(1)}, f32[8,2,24,128]{3,2,1,0:T(8,128)S(1)}, u32[]{:S(2)}, u32[]{:S(2)}) %collective-permute-start.20) | collective-permute-done | bytes 196640 | tf_op jit(solution)/shard_map/ppermute | solution.py:693
  127.0 1.0 collective-permute-done.21
  128.0 2.1 %restore.1 = f32[3,4,256,128]{3,2,1,0:T(8,128)} custom-call(f32[384,128]{1,0:T(8,128)S(1)} %bitcast.30, f32[384,128]{1,0:T(8,128)S(1)} %bitcast.31, f32[384,128]{1,0:T(8,128)S(1)} %bitcast.32, f32[384,128]{1,0:T(8,128)S(1)} %bitcast.33, f32[384,128]{1,0:T(8,128)S(1)} %bitcast.34, f32[384,128]{1,0:T(8,128)S(1)} %bitcast.35, f32[384,128]{1,0:T(8,128)S(1)} %bitcast.36, ...), custom_call_target="tpu_custom_call" | custom-call | bytes 3145728 | tf_op jit(solution)/shard_map/restore/pallas_call | solution.py:671
  (39 shorter events, 0.2 us)
Async XLA Ops:
  2.1 11.2 %collective-permute-start.1 = (f32[392,128]{1,0:T(8,128)}, f32[392,128]{1,0:T(8,128)S(1)}, u32[]{:S(2)}, u32[]{:S(2)}) collective-permute-start(f32[392,128]{1,0:T(8,128)} %get-tuple-element.39), channel_id=1, source_target_pairs={{0,24},{1,9},{2,26},{3,11},{8,16},{9,1},{10,18},{11,3},{16,8},{17,... | collective-permute-start | bytes 602120 | tf_op jit(solution)/shard_map/ppermute | solution.py:693
  7.2 19.1 %collective-permute-start = (f32[392,128]{1,0:T(8,128)}, f32[392,128]{1,0:T(8,128)S(1)}, u32[]{:S(2)}, u32[]{:S(2)}) collective-permute-start(f32[392,128]{1,0:T(8,128)} %get-tuple-element.38), channel_id=1, source_target_pairs={{0,8},{1,25},{2,10},{3,27},{8,0},{9,17},{10,2},{11,19},{16,24},{17... | collective-permute-start | bytes 602120 | tf_op jit(solution)/shard_map/ppermute | solution.py:693
  7.2 20.6 %collective-permute-start.2 = (f32[392,128]{1,0:T(8,128)}, f32[392,128]{1,0:T(8,128)S(1)}, u32[]{:S(2)}, u32[]{:S(2)}) collective-permute-start(f32[392,128]{1,0:T(8,128)} %get-tuple-element.40), channel_id=1, source_target_pairs={{0,16},{1,17},{2,18},{3,19},{8,24},{9,25},{10,26},{11,27},{16,0},{... | collective-permute-start | bytes 602120 | tf_op jit(solution)/shard_map/ppermute | solution.py:693
  9.8 15.6 %copy-start.3 = (f32[392,128]{1,0:T(8,128)S(1)}, f32[392,128]{1,0:T(8,128)}, u32[]{:S(2)}) copy-start(f32[392,128]{1,0:T(8,128)} %get-tuple-element.37.refs_0_) | copy-start | bytes 602116
  9.8 15.6 %copy-start.2 = (bf16[128,256]{1,0:T(8,128)(2,1)S(1)}, bf16[128,256]{1,0:T(8,128)(2,1)}, u32[]{:S(2)}) copy-start(bf16[128,256]{1,0:T(8,128)(2,1)} %constant.22.clone.rest_ref.refs_5_.refs_2_) | copy-start | bytes 196612
  9.8 15.6 %copy-start.4 = (bf16[128,256]{1,0:T(8,128)(2,1)S(1)}, bf16[128,256]{1,0:T(8,128)(2,1)}, u32[]{:S(2)}) copy-start(bf16[128,256]{1,0:T(8,128)(2,1)} %constant.21.clone.top_ref) | copy-start | bytes 196612
  9.8 15.7 %copy-start.6 = (s32[64]{0:T(128)S(1)}, s32[64]{0:T(128)}, u32[]{:S(2)}) copy-start(s32[64]{0:T(128)} %owner_ref.1) | copy-start | bytes 772
  9.8 18.1 %copy-start.5 = (s32[8]{0:T(128)S(1)}, s32[8]{0:T(128)}, u32[]{:S(2)}) copy-start(s32[8]{0:T(128)} %low_ref.11) | copy-start | bytes 100
  13.3 0.7 copy-start
  14.0 12.3 %copy-start.1 = (f32[392,128]{1,0:T(8,128)S(1)}, f32[392,128]{1,0:T(8,128)}, u32[]{:S(2)}) copy-start(f32[392,128]{1,0:T(8,128)} %copy-done) | copy-start | bytes 602116
  14.0 29.4 %all-to-all-start = ((f32[4,384,128]{2,1,0:T(8,128)}), f32[4,384,128]{2,1,0:T(8,128)S(1)}, u32[]{:S(2)}, u32[]{:S(2)}) async-start(f32[4,384,128]{2,1,0:T(8,128)} %hand_on.1), calls=%async_computation | async-start | bytes 1572864 | tf_op jit(solution)/shard_map/all_to_all | solution.py:741
  31.4 1.5 %collective-permute-start.3 = (f32[3,4,32,128]{3,2,1,0:T(8,128)S(1)}, f32[3,4,32,128]{3,2,1,0:T(8,128)S(1)}, u32[]{:S(2)}, u32[]{:S(2)}) collective-permute-start(f32[3,4,32,128]{3,2,1,0:T(8,128)S(1)} %get-tuple-element.45), channel_id=1, source_target_pairs={{0,1},{1,0},{2,3},{3,2},{4,5},{5,4},{6,7},{7,6},{8,9},{9,8},{10,11... | collective-permute-start | bytes 589832 | tf_op jit(solution)/shard_map/ppermute | solution.py:715
  32.9 7.0 %collective-permute-start.14 = (f32[3,4,32,128]{3,2,1,0:T(8,128)S(1)}, f32[3,4,32,128]{3,2,1,0:T(8,128)S(1)}, u32[]{:S(2)}, u32[]{:S(2)}) collective-permute-start(f32[3,4,32,128]{3,2,1,0:T(8,128)S(1)} %add.21.refs_4_.first_ref), channel_id=1, source_target_pairs={{0,2},{1,3},{2,0},{3,1},{4,6},{5,7},{6,4},{7,5},{8,10},{9,11},{10,... | collective-permute-start | bytes 589832 | tf_op jit(solution)/shard_map/ppermute | solution.py:715
  39.9 1.5 %collective-permute-start.15 = (f32[3,4,32,128]{3,2,1,0:T(8,128)S(1)}, f32[3,4,32,128]{3,2,1,0:T(8,128)S(1)}, u32[]{:S(2)}, u32[]{:S(2)}) collective-permute-start(f32[3,4,32,128]{3,2,1,0:T(8,128)S(1)} %ordered_sum.3.kept_ref), channel_id=1, source_target_pairs={{0,1},{1,0},{2,3},{3,2},{4,5},{5,4},{6,7},{7,6},{8,9},{9,8},{10,11... | collective-permute-start | bytes 589832 | tf_op jit(solution)/shard_map/ppermute | solution.py:715
  43.4 38.6 %all-to-all-start.1 = ((f32[8,8,24,128]{3,2,1,0:T(8,128)}), f32[8,8,24,128]{3,2,1,0:T(8,128)S(1)}, u32[]{:S(2)}, u32[]{:S(2)}) async-start(f32[8,8,24,128]{3,2,1,0:T(8,128)} %bitcast.13), calls=%async_computation.1 | async-start | bytes 1572864 | tf_op jit(solution)/shard_map/all_to_all | solution.py:772
  53.7 1.5 %collective-permute-start.4 = (f32[3,4,32,128]{3,2,1,0:T(8,128)S(1)}, f32[3,4,32,128]{3,2,1,0:T(8,128)S(1)}, u32[]{:S(2)}, u32[]{:S(2)}) collective-permute-start(f32[3,4,32,128]{3,2,1,0:T(8,128)S(1)} %get-tuple-element.49), channel_id=1, source_target_pairs={{0,1},{1,0},{2,3},{3,2},{4,5},{5,4},{6,7},{7,6},{8,9},{9,8},{10,11... | collective-permute-start | bytes 589832 | tf_op jit(solution)/shard_map/ppermute | solution.py:715
  55.3 7.0 %collective-permute-start.5 = (f32[3,4,32,128]{3,2,1,0:T(8,128)S(1)}, f32[3,4,32,128]{3,2,1,0:T(8,128)S(1)}, u32[]{:S(2)}, u32[]{:S(2)}) collective-permute-start(f32[3,4,32,128]{3,2,1,0:T(8,128)S(1)} %add.22.first_ref), channel_id=1, source_target_pairs={{0,2},{1,3},{2,0},{3,1},{4,6},{5,7},{6,4},{7,5},{8,10},{9,11},{10,... | collective-permute-start | bytes 589832 | tf_op jit(solution)/shard_map/ppermute | solution.py:715
  62.3 1.5 %collective-permute-start.6 = (f32[3,4,32,128]{3,2,1,0:T(8,128)S(1)}, f32[3,4,32,128]{3,2,1,0:T(8,128)S(1)}, u32[]{:S(2)}, u32[]{:S(2)}) collective-permute-start(f32[3,4,32,128]{3,2,1,0:T(8,128)S(1)} %ordered_sum.2.kept_ref), channel_id=1, source_target_pairs={{0,1},{1,0},{2,3},{3,2},{4,5},{5,4},{6,7},{7,6},{8,9},{9,8},{10,11... | collective-permute-start | bytes 589832 | tf_op jit(solution)/shard_map/ppermute | solution.py:715
  65.0 14.8 %collective-permute-start.7 = (f32[8,24,128]{2,1,0:T(8,128)S(1)}, f32[8,24,128]{2,1,0:T(8,128)S(1)}, u32[]{:S(2)}, u32[]{:S(2)}) collective-permute-start(f32[8,24,128]{2,1,0:T(8,128)S(1)} %bitcast.45), channel_id=1, source_target_pairs={{0,16},{1,21},{2,18},{3,23},{4,20},{5,17},{6,22},{7,19},{8,24},{9,... | collective-permute-start | bytes 294920 | tf_op jit(solution)/shard_map/ppermute | solution.py:693
  68.0 11.8 %collective-permute-start.8 = (f32[8,24,128]{2,1,0:T(8,128)S(1)}, f32[8,24,128]{2,1,0:T(8,128)S(1)}, u32[]{:S(2)}, u32[]{:S(2)}) collective-permute-start(f32[8,24,128]{2,1,0:T(8,128)S(1)} %bitcast.44), channel_id=1, source_target_pairs={{0,4},{1,17},{2,6},{3,19},{4,0},{5,21},{6,2},{7,23},{8,12},{9,25},... | collective-permute-start | bytes 294920 | tf_op jit(solution)/shard_map/ppermute | solution.py:693
  69.5 16.6 %collective-permute-start.9 = (f32[8,24,128]{2,1,0:T(8,128)S(1)}, f32[8,24,128]{2,1,0:T(8,128)S(1)}, u32[]{:S(2)}, u32[]{:S(2)}) collective-permute-start(f32[8,24,128]{2,1,0:T(8,128)S(1)} %bitcast.43), channel_id=1, source_target_pairs={{0,24},{1,5},{2,26},{3,7},{4,28},{5,1},{6,30},{7,3},{8,16},{9,13},... | collective-permute-start | bytes 294920 | tf_op jit(solution)/shard_map/ppermute | solution.py:693
  70.9 15.2 %collective-permute-start.10 = (f32[8,24,128]{2,1,0:T(8,128)S(1)}, f32[8,24,128]{2,1,0:T(8,128)S(1)}, u32[]{:S(2)}, u32[]{:S(2)}) collective-permute-start(f32[8,24,128]{2,1,0:T(8,128)S(1)} %bitcast.42), channel_id=1, source_target_pairs={{0,8},{1,25},{2,10},{3,27},{4,12},{5,29},{6,14},{7,31},{8,0},{9,17... | collective-permute-start | bytes 294920 | tf_op jit(solution)/shard_map/ppermute | solution.py:693
  70.9 15.6 %collective-permute-start.11 = (f32[8,24,128]{2,1,0:T(8,128)S(1)}, f32[8,24,128]{2,1,0:T(8,128)S(1)}, u32[]{:S(2)}, u32[]{:S(2)}) collective-permute-start(f32[8,24,128]{2,1,0:T(8,128)S(1)} %bitcast.41), channel_id=1, source_target_pairs={{0,20},{1,9},{2,22},{3,11},{4,16},{5,13},{6,18},{7,15},{8,28},{9,1... | collective-permute-start | bytes 294920 | tf_op jit(solution)/shard_map/ppermute | solution.py:693
  79.8 8.6 %collective-permute-start.12 = (f32[8,24,128]{2,1,0:T(8,128)S(1)}, f32[8,24,128]{2,1,0:T(8,128)S(1)}, u32[]{:S(2)}, u32[]{:S(2)}) collective-permute-start(f32[8,24,128]{2,1,0:T(8,128)S(1)} %bitcast.40), channel_id=1, source_target_pairs={{0,12},{1,29},{2,14},{3,31},{4,8},{5,25},{6,10},{7,27},{8,4},{9,21... | collective-permute-start | bytes 294920 | tf_op jit(solution)/shard_map/ppermute | solution.py:693
  79.8 8.6 %collective-permute-start.13 = (f32[8,24,128]{2,1,0:T(8,128)S(1)}, f32[8,24,128]{2,1,0:T(8,128)S(1)}, u32[]{:S(2)}, u32[]{:S(2)}) collective-permute-start(f32[8,24,128]{2,1,0:T(8,128)S(1)} %bitcast.39), channel_id=1, source_target_pairs={{0,28},{1,13},{2,30},{3,15},{4,24},{5,9},{6,26},{7,11},{8,20},{9,5... | collective-permute-start | bytes 294920 | tf_op jit(solution)/shard_map/ppermute | solution.py:693
  92.9 20.5 %collective-permute-start.16 = (f32[8,2,24,128]{3,2,1,0:T(8,128)S(1)}, f32[8,2,24,128]{3,2,1,0:T(8,128)S(1)}, u32[]{:S(2)}, u32[]{:S(2)}) collective-permute-start(f32[8,2,24,128]{3,2,1,0:T(8,128)S(1)} %get-tuple-element.61), channel_id=1, source_target_pairs={{0,16},{1,21},{2,18},{3,23},{4,20},{5,17},{6,22},{7,19},{8,24},{9,... | collective-permute-start | bytes 589832 | tf_op jit(solution)/shard_map/ppermute | solution.py:693
  93.6 19.7 %collective-permute-start.17 = (f32[8,2,24,128]{3,2,1,0:T(8,128)S(1)}, f32[8,2,24,128]{3,2,1,0:T(8,128)S(1)}, u32[]{:S(2)}, u32[]{:S(2)}) collective-permute-start(f32[8,2,24,128]{3,2,1,0:T(8,128)S(1)} %get-tuple-element.62), channel_id=1, source_target_pairs={{0,4},{1,17},{2,6},{3,19},{4,0},{5,21},{6,2},{7,23},{8,12},{9,25},... | collective-permute-start | bytes 589832 | tf_op jit(solution)/shard_map/ppermute | solution.py:693
  95.4 18.3 %collective-permute-start.18 = (f32[8,2,24,128]{3,2,1,0:T(8,128)S(1)}, f32[8,2,24,128]{3,2,1,0:T(8,128)S(1)}, u32[]{:S(2)}, u32[]{:S(2)}) collective-permute-start(f32[8,2,24,128]{3,2,1,0:T(8,128)S(1)} %get-tuple-element.63), channel_id=1, source_target_pairs={{0,24},{1,5},{2,26},{3,7},{4,28},{5,1},{6,30},{7,3},{8,16},{9,13},... | collective-permute-start | bytes 589832 | tf_op jit(solution)/shard_map/ppermute | solution.py:693
  96.8 16.9 %collective-permute-start.19 = (f32[8,2,24,128]{3,2,1,0:T(8,128)S(1)}, f32[8,2,24,128]{3,2,1,0:T(8,128)S(1)}, u32[]{:S(2)}, u32[]{:S(2)}) collective-permute-start(f32[8,2,24,128]{3,2,1,0:T(8,128)S(1)} %get-tuple-element.64), channel_id=1, source_target_pairs={{0,8},{1,25},{2,10},{3,27},{4,12},{5,29},{6,14},{7,31},{8,0},{9,17... | collective-permute-start | bytes 589832 | tf_op jit(solution)/shard_map/ppermute | solution.py:693
  97.4 29.6 %collective-permute-start.20 = (f32[8,2,24,128]{3,2,1,0:T(8,128)S(1)}, f32[8,2,24,128]{3,2,1,0:T(8,128)S(1)}, u32[]{:S(2)}, u32[]{:S(2)}) collective-permute-start(f32[8,2,24,128]{3,2,1,0:T(8,128)S(1)} %get-tuple-element.65), channel_id=1, source_target_pairs={{0,20},{1,9},{2,22},{3,11},{4,16},{5,13},{6,18},{7,15},{8,28},{9,1... | collective-permute-start | bytes 589832 | tf_op jit(solution)/shard_map/ppermute | solution.py:693
  113.4 14.6 %collective-permute-start.21 = (f32[8,2,24,128]{3,2,1,0:T(8,128)S(1)}, f32[8,2,24,128]{3,2,1,0:T(8,128)S(1)}, u32[]{:S(2)}, u32[]{:S(2)}) collective-permute-start(f32[8,2,24,128]{3,2,1,0:T(8,128)S(1)} %get-tuple-element.66), channel_id=1, source_target_pairs={{0,12},{1,29},{2,14},{3,31},{4,8},{5,25},{6,10},{7,27},{8,4},{9,21... | collective-permute-start | bytes 589832 | tf_op jit(solution)/shard_map/ppermute | solution.py:693
  113.4 14.6 %collective-permute-start.22 = (f32[8,2,24,128]{3,2,1,0:T(8,128)S(1)}, f32[8,2,24,128]{3,2,1,0:T(8,128)S(1)}, u32[]{:S(2)}, u32[]{:S(2)}) collective-permute-start(f32[8,2,24,128]{3,2,1,0:T(8,128)S(1)} %get-tuple-element.67), channel_id=1, source_target_pairs={{0,28},{1,13},{2,30},{3,15},{4,24},{5,9},{6,26},{7,11},{8,20},{9,5... | collective-permute-start | bytes 589832 | tf_op jit(solution)/shard_map/ppermute | solution.py:693

commit v19 on v16

--- a/solution.py
+++ b/solution.py
@@ -115,7 +115,7 @@
 
 
 def params():
-    return pltpu.CompilerParams(vmem_limit_bytes=48 * 1024 * 1024)
+    return pltpu.CompilerParams(vmem_limit_bytes=24 * 1024 * 1024)
 
 
 ORDERS = {4: (1, 3, 2), 8: (4, 1, 2, 6, 5, 3, 7)}

time: 130 us -> 130 us (level)
  waiting for transfers between devices: 47.4 us -> 42.7 us
  local copies, waits for them, and re-layouts: 1.56 us -> 4.95 us
  starting transfers between devices: 47.6 us -> 49.5 us
    ppermute x17, waiting for transfers between devices: 37 us -> 32.3 us  [exchange(): result[position] = lax.ppermute(blocks[position], axes + ('real',), pairs)]
    unnamed x14 -> x18, local copies, waits for them, and re-layouts: 0.71 us -> 4.1 us
    ppermute x17, starting transfers between devices: 26.4 us -> 28.3 us  [exchange(): result[position] = lax.ppermute(blocks[position], axes + ('real',), pairs)]
  transfers between devices with their start and end apart: 25 -> 25, of which waited for: 13 -> 13; matrix products, arithmetic and copies ran while one was open for 1% -> 1% of each run, Pallas kernels for 18% -> 17%
where the time goes in v19:
time: 130 us; the launch traced here: 128 us
  starting transfers between devices  49.5 us (38%)
  waiting for transfers between devices  42.7 us (33%)
  Pallas kernels  30.9 us (24%)
  local copies, waits for them, and re-layouts  4.95 us (4%)
    ppermute x17, waiting for transfers between devices, exchange(): result[position] = lax.ppermute(blocks[position], axes + ('real',), pairs)  32.3 us
    ppermute x17, starting transfers between devices, exchange(): result[position] = lax.ppermute(blocks[position], axes + ('real',), pairs)  28.3 us
    all_to_all x1, starting transfers between devices, local(): block = lax.all_to_all(block, 'kx', split_axis=0, concat_axis=0, tiled=True)  10.8 us
    ppermute x6, waiting for transfers between devices, swap(): return lax.ppermute(value, 'real', pairs)  10.4 us
    pallas_call x2, Pallas kernels, solve(): pl.pallas_call(functools.partial(solve_kernel, groups=groups, kx_count=kx...  7.79 us
    pallas_call x2, Pallas kernels, stress_terms(): pl.pallas_call(stress_kernel, out_shape=(jax.ShapeDtypeStruct(shape, jnp....  6.93 us
    all_to_all x1, starting transfers between devices, local(): lax.all_to_all(block, ('kx', 'ht'), split_axis=0, concat_axis=0, tiled=True)  6.91 us
    pallas_call x2, Pallas kernels, high_terms(): pl.pallas_call(products_kernel, out_shape=jax.ShapeDtypeStruct((component...  6 us
  transfers between devices with their start and end apart: 25, of which 13 were waited for; matrix products, arithmetic and copies ran while one was open for 1% of the time, Pallas kernels for 17%

profile of v19, /device:TPU:0, one launch (start us, length us, event | category | flops | bytes accessed | tf_op | source)
XLA Modules:
  0.0 128.4 jit_solution(15128790065995190548)
XLA Ops:
  0.0 2.1 %pack_first.1 = (f32[392,128]{1,0:T(8,128)}, f32[392,128]{1,0:T(8,128)}, f32[392,128]{1,0:T(8,128)}, f32[392,128]{1,0:T(8,128)}) custom-call(s32[4,8]{1,0:T(4,128)} %near_ref.1, s32[4]{0:T(128)} %count_ref.1, f32[12,2,4,32,128]{4,3,2,1,0:T(8,128)} %bitcast.46), custom_call_target="tpu_custom_call" | custom-call | bytes 1572864 | tf_op jit(solution)/shard_map/pack_first/pallas_call | solution.py:175
  2.1 5.0 %collective-permute-start.1 = (f32[392,128]{1,0:T(8,128)}, f32[392,128]{1,0:T(8,128)S(1)}, u32[]{:S(2)}, u32[]{:S(2)}) collective-permute-start(f32[392,128]{1,0:T(8,128)} %get-tuple-element.39), channel_id=1, source_target_pairs={{0,24},{1,9},{2,26},{3,11},{8,16},{9,1},{10,18},{11,3},{16,8},{17,... | collective-permute-start | bytes 602120 | tf_op jit(solution)/shard_map/ppermute | solution.py:693
  7.2 0.6 collective-permute-start.2
  7.7 2.1 %pack.1.value_ref = f32[4,384,128]{2,1,0:T(8,128)} custom-call(f32[12,2,4,32,128]{4,3,2,1,0:T(8,128)} %bitcast.47), custom_call_target="tpu_custom_call" | custom-call | bytes 1572864 | tf_op jit(solution)/shard_map/pack/pallas_call | solution.py:201
  9.8 0.0 copy-start.7
  9.8 3.5 %collective-permute-done.1.after_ref.refs_2_ = f32[392,128]{1,0:T(8,128)S(1)} collective-permute-done((f32[392,128]{1,0:T(8,128)}, f32[392,128]{1,0:T(8,128)S(1)}, u32[]{:S(2)}, u32[]{:S(2)}) %collective-permute-start.1) | collective-permute-done | bytes 200736 | tf_op jit(solution)/shard_map/ppermute | solution.py:693
  13.3 0.7 copy-done.2
  14.0 10.8 %all-to-all-start = ((f32[4,384,128]{2,1,0:T(8,128)}), f32[4,384,128]{2,1,0:T(8,128)S(1)}, u32[]{:S(2)}, u32[]{:S(2)}) async-start(f32[4,384,128]{2,1,0:T(8,128)} %hand_on.1), calls=%async_computation | async-start | bytes 1572864 | tf_op jit(solution)/shard_map/all_to_all | solution.py:741
  24.8 0.1 broadcast_in_dim.85
  24.8 0.1 broadcast_in_dim.86
  24.9 0.1 broadcast_in_dim.91
  25.0 0.1 broadcast_in_dim.92
  25.1 0.1 broadcast_in_dim.96
  25.2 0.1 broadcast_in_dim.97
  25.3 0.1 broadcast_in_dim.101
  25.4 0.1 broadcast_in_dim.102
  25.5 0.8 tables.1
  26.3 1.5 %collective-permute-done.2.refs_3_ = f32[392,128]{1,0:T(8,128)S(1)} collective-permute-done((f32[392,128]{1,0:T(8,128)}, f32[392,128]{1,0:T(8,128)S(1)}, u32[]{:S(2)}, u32[]{:S(2)}) %collective-permute-start.2) | collective-permute-done | bytes 200736 | tf_op jit(solution)/shard_map/ppermute | solution.py:693
  27.8 0.1 add_convert_fusion
  27.9 3.5 %stress.2 = (f32[3,16,32,128]{3,2,1,0:T(8,128)S(1)}, f32[3,16,32,256]{3,2,1,0:T(8,128)S(1)}, f32[3,4,32,128]{3,2,1,0:T(8,128)S(1)}, f32[3,4,32,128]{3,2,1,0:T(8,128)S(1)}) custom-call(s32[8]{0:T(128)S(1)} %copy-done.7, s32[16,8]{1,0:T(8,128)S(1)} %bitcast.26, f32[392,128]{1,0:T(8,128)S(1)} %copy-done.5, f32[392,128]{1,0:T(8,128)S(1)} %collective-permute-done.refs_1_, ...), custom_call_target="tpu_custom_call" | custom-call | bytes 12582912 | tf_op jit(solution)/shard_map/stress/pallas_call | solution.py:368
  31.4 0.1 collective-permute-start.3
  31.5 1.4 %collective-permute-done.3 = f32[3,4,32,128]{3,2,1,0:T(8,128)S(1)} collective-permute-done((f32[3,4,32,128]{3,2,1,0:T(8,128)S(1)}, f32[3,4,32,128]{3,2,1,0:T(8,128)S(1)}, u32[]{:S(2)}, u32[]{:S(2)}) %collective-permute-start.3) | collective-permute-done | bytes 196640 | tf_op jit(solution)/shard_map/ppermute | solution.py:715
  32.9 1.6 %collective-permute-start.14 = (f32[3,4,32,128]{3,2,1,0:T(8,128)S(1)}, f32[3,4,32,128]{3,2,1,0:T(8,128)S(1)}, u32[]{:S(2)}, u32[]{:S(2)}) collective-permute-start(f32[3,4,32,128]{3,2,1,0:T(8,128)S(1)} %add.21.refs_4_.first_ref), channel_id=1, source_target_pairs={{0,2},{1,3},{2,0},{3,1},{4,6},{5,7},{6,4},{7,5},{8,10},{9,11},{10,... | collective-permute-start | bytes 589832 | tf_op jit(solution)/shard_map/ppermute | solution.py:715
  34.5 0.2 slice_reduce_fusion.count_ref
  34.6 3.0 %products.3._.forcing_ref = f32[3,8,32,128]{3,2,1,0:T(8,128)S(1)} custom-call(s32[8]{0:T(128)S(1)} %copy-done.7, s32[16,8]{1,0:T(8,128)S(1)} %bitcast.27, s32[16]{0:T(128)S(1)} %slice_reduce_fusion.count_ref, f32[3,16,32,256]{3,2,1,0:T(8,128)S(1)} %get-tuple-element.59.physical, bf16[256,256]{1,0:T(8,128)(2,1)S(1)} %get-tuple-element.42.refs_6_.refs_3_.back_ref, ...), custom_call_target="tpu_custom_call" | custom-call | bytes 12582912 | tf_op jit(solution)/shard_map/products/pallas_call | solution.py:433
  37.6 2.3 %collective-permute-done.14.second_ref = f32[3,4,32,128]{3,2,1,0:T(8,128)S(1)} collective-permute-done((f32[3,4,32,128]{3,2,1,0:T(8,128)S(1)}, f32[3,4,32,128]{3,2,1,0:T(8,128)S(1)}, u32[]{:S(2)}, u32[]{:S(2)}) %collective-permute-start.14) | collective-permute-done | bytes 196640 | tf_op jit(solution)/shard_map/ppermute | solution.py:715
  39.9 0.1 collective-permute-start.15
  40.0 1.4 %collective-permute-done.15.other_ref = f32[3,4,32,128]{3,2,1,0:T(8,128)S(1)} collective-permute-done((f32[3,4,32,128]{3,2,1,0:T(8,128)S(1)}, f32[3,4,32,128]{3,2,1,0:T(8,128)S(1)}, u32[]{:S(2)}, u32[]{:S(2)}) %collective-permute-start.15) | collective-permute-done | bytes 196640 | tf_op jit(solution)/shard_map/ppermute | solution.py:715
  41.4 1.9 %outgoing.3 = f32[1536,128]{1,0:T(8,128)} custom-call(s32[8]{0:T(128)S(1)} %copy-done.7, s32[16]{0:T(128)S(1)} %slice_reduce_fusion.count_ref, f32[3,16,32,128]{3,2,1,0:T(8,128)S(1)} %get-tuple-element.58.slotted_ref, f32[3,8,32,128]{3,2,1,0:T(8,128)S(1)} %products.3._.forcing_ref, f32[3,4,32,128]{3,2,1,0:T(8,128)S(1)} %ordered_sum.3.kept_ref, ...), custom_call_target="tpu_custom_call" | custom-call | bytes 1572864 | tf_op jit(solution)/shard_map/outgoing/pallas_call | solution.py:499
  43.3 0.0 all-to-all-done.refs_0_
  43.3 6.9 %all-to-all-start.1 = ((f32[8,8,24,128]{3,2,1,0:T(8,128)}), f32[8,8,24,128]{3,2,1,0:T(8,128)S(1)}, u32[]{:S(2)}, u32[]{:S(2)}) async-start(f32[8,8,24,128]{3,2,1,0:T(8,128)} %bitcast.13), calls=%async_computation.1 | async-start | bytes 1572864 | tf_op jit(solution)/shard_map/all_to_all | solution.py:772
  50.3 3.5 %stress.3 = (f32[3,16,32,128]{3,2,1,0:T(8,128)S(1)}, f32[3,16,32,256]{3,2,1,0:T(8,128)S(1)}, f32[3,4,32,128]{3,2,1,0:T(8,128)S(1)}, f32[3,4,32,128]{3,2,1,0:T(8,128)S(1)}) custom-call(s32[8]{0:T(128)S(1)} %copy-done.7, s32[16,8]{1,0:T(8,128)S(1)} %bitcast.28, f32[4,384,128]{2,1,0:T(8,128)S(1)} %all-to-all-done.refs_0_, ...), custom_call_target="tpu_custom_call" | custom-call | bytes 12582912 | tf_op jit(solution)/shard_map/stress/pallas_call | solution.py:368
  53.7 0.1 collective-permute-start.4
  53.8 1.4 %collective-permute-done.4 = f32[3,4,32,128]{3,2,1,0:T(8,128)S(1)} collective-permute-done((f32[3,4,32,128]{3,2,1,0:T(8,128)S(1)}, f32[3,4,32,128]{3,2,1,0:T(8,128)S(1)}, u32[]{:S(2)}, u32[]{:S(2)}) %collective-permute-start.4) | collective-permute-done | bytes 196640 | tf_op jit(solution)/shard_map/ppermute | solution.py:715
  55.3 1.6 %collective-permute-start.5 = (f32[3,4,32,128]{3,2,1,0:T(8,128)S(1)}, f32[3,4,32,128]{3,2,1,0:T(8,128)S(1)}, u32[]{:S(2)}, u32[]{:S(2)}) collective-permute-start(f32[3,4,32,128]{3,2,1,0:T(8,128)S(1)} %add.22.first_ref), channel_id=1, source_target_pairs={{0,2},{1,3},{2,0},{3,1},{4,6},{5,7},{6,4},{7,5},{8,10},{9,11},{10,... | collective-permute-start | bytes 589832 | tf_op jit(solution)/shard_map/ppermute | solution.py:715
  56.8 3.0 %products.2._.forcing_ref = f32[3,8,32,128]{3,2,1,0:T(8,128)S(1)} custom-call(s32[8]{0:T(128)S(1)} %copy-done.7, s32[16,8]{1,0:T(8,128)S(1)} %bitcast.29, s32[16]{0:T(128)S(1)} %slice_reduce_fusion.count_ref, f32[3,16,32,256]{3,2,1,0:T(8,128)S(1)} %get-tuple-element.47.physical, bf16[256,256]{1,0:T(8,128)(2,1)S(1)} %get-tuple-element.42.refs_6_.refs_3_.back_ref, ...), custom_call_target="tpu_custom_call" | custom-call | bytes 12582912 | tf_op jit(solution)/shard_map/products/pallas_call | solution.py:433
  59.8 2.5 %collective-permute-done.5.second_ref = f32[3,4,32,128]{3,2,1,0:T(8,128)S(1)} collective-permute-done((f32[3,4,32,128]{3,2,1,0:T(8,128)S(1)}, f32[3,4,32,128]{3,2,1,0:T(8,128)S(1)}, u32[]{:S(2)}, u32[]{:S(2)}) %collective-permute-start.5) | collective-permute-done | bytes 196640 | tf_op jit(solution)/shard_map/ppermute | solution.py:715
  62.3 0.1 collective-permute-start.6
  62.4 1.4 %collective-permute-done.6.other_ref = f32[3,4,32,128]{3,2,1,0:T(8,128)S(1)} collective-permute-done((f32[3,4,32,128]{3,2,1,0:T(8,128)S(1)}, f32[3,4,32,128]{3,2,1,0:T(8,128)S(1)}, u32[]{:S(2)}, u32[]{:S(2)}) %collective-permute-start.6) | collective-permute-done | bytes 196640 | tf_op jit(solution)/shard_map/ppermute | solution.py:715
  63.8 1.2 outgoing.2
  65.0 3.0 %collective-permute-start.7 = (f32[8,24,128]{2,1,0:T(8,128)S(1)}, f32[8,24,128]{2,1,0:T(8,128)S(1)}, u32[]{:S(2)}, u32[]{:S(2)}) collective-permute-start(f32[8,24,128]{2,1,0:T(8,128)S(1)} %bitcast.45), channel_id=1, source_target_pairs={{0,16},{1,5},{2,18},{3,7},{4,20},{5,1},{6,22},{7,3},{8,24},{9,13},... | collective-permute-start | bytes 294920 | tf_op jit(solution)/shard_map/ppermute | solution.py:693
  68.0 1.5 %collective-permute-start.8 = (f32[8,24,128]{2,1,0:T(8,128)S(1)}, f32[8,24,128]{2,1,0:T(8,128)S(1)}, u32[]{:S(2)}, u32[]{:S(2)}) collective-permute-start(f32[8,24,128]{2,1,0:T(8,128)S(1)} %bitcast.44), channel_id=1, source_target_pairs={{0,4},{1,17},{2,6},{3,19},{4,0},{5,21},{6,2},{7,23},{8,12},{9,25},... | collective-permute-start | bytes 294920 | tf_op jit(solution)/shard_map/ppermute | solution.py:693
  69.5 1.5 %collective-permute-start.9 = (f32[8,24,128]{2,1,0:T(8,128)S(1)}, f32[8,24,128]{2,1,0:T(8,128)S(1)}, u32[]{:S(2)}, u32[]{:S(2)}) collective-permute-start(f32[8,24,128]{2,1,0:T(8,128)S(1)} %bitcast.43), channel_id=1, source_target_pairs={{0,8},{1,25},{2,10},{3,27},{4,12},{5,29},{6,14},{7,31},{8,0},{9,17... | collective-permute-start | bytes 294920 | tf_op jit(solution)/shard_map/ppermute | solution.py:693
  70.9 0.6 collective-permute-start.10
  71.5 1.5 %collective-permute-start.11 = (f32[8,24,128]{2,1,0:T(8,128)S(1)}, f32[8,24,128]{2,1,0:T(8,128)S(1)}, u32[]{:S(2)}, u32[]{:S(2)}) collective-permute-start(f32[8,24,128]{2,1,0:T(8,128)S(1)} %bitcast.41), channel_id=1, source_target_pairs={{0,20},{1,13},{2,22},{3,15},{4,16},{5,9},{6,18},{7,11},{8,28},{9,5... | collective-permute-start | bytes 294920 | tf_op jit(solution)/shard_map/ppermute | solution.py:693
  72.9 3.3 %collective-permute-done.7.refs_1_ = f32[8,24,128]{2,1,0:T(8,128)S(1)} collective-permute-done((f32[8,24,128]{2,1,0:T(8,128)S(1)}, f32[8,24,128]{2,1,0:T(8,128)S(1)}, u32[]{:S(2)}, u32[]{:S(2)}) %collective-permute-start.7) | collective-permute-done | bytes 98336 | tf_op jit(solution)/shard_map/ppermute | solution.py:693
  76.2 0.4 collective-permute-start.12
  76.7 3.1 %collective-permute-start.13 = (f32[8,24,128]{2,1,0:T(8,128)S(1)}, f32[8,24,128]{2,1,0:T(8,128)S(1)}, u32[]{:S(2)}, u32[]{:S(2)}) collective-permute-start(f32[8,24,128]{2,1,0:T(8,128)S(1)} %bitcast.39), channel_id=1, source_target_pairs={{0,28},{1,29},{2,30},{3,31},{4,24},{5,25},{6,26},{7,27},{8,20},{9,... | collective-permute-start | bytes 294920 | tf_op jit(solution)/shard_map/ppermute | solution.py:693
  79.8 3.4 %copy-done = f32[8,512,512]{2,1,0:T(8,128)S(1)} copy-done((f32[8,512,512]{2,1,0:T(8,128)S(1)}, f32[8,512,512]{2,1,0:T(8,128)}, u32[]{:S(2)}) %copy-start) | copy-done | bytes 8388632
  83.1 3.5 %solve.2.refs_9_ = f32[8,512,128]{2,1,0:T(8,128)S(1)} custom-call(f32[8,8,24,128]{3,2,1,0:T(8,128)S(1)} %all-to-all-done.1.refs_0_, f32[8,512,512]{2,1,0:T(8,128)S(1)} %copy-done), custom_call_target="tpu_custom_call" | custom-call | bytes 8388608 | tf_op jit(solution)/shard_map/solve/pallas_call | solution.py:631
  86.6 0.0 collective-permute-done.9.refs_3_
  86.7 0.7 collective-permute-done.11.refs_5_
  87.4 0.0 collective-permute-done.12.refs_6_
  87.4 0.0 collective-permute-done.13.refs_7_
  87.4 4.3 %solve.3 = (f32[8,2,24,128]{3,2,1,0:T(8,128)S(1)}, f32[8,2,24,128]{3,2,1,0:T(8,128)S(1)}, f32[8,2,24,128]{3,2,1,0:T(8,128)S(1)}, f32[8,2,24,128]{3,2,1,0:T(8,128...) custom-call(f32[8,24,128]{2,1,0:T(8,128)S(1)} %bitcast.38, ...), custom_call_target="tpu_custom_call" | custom-call | bytes 8388608 | tf_op jit(solution)/shard_map/solve/pallas_call | solution.py:631
  91.7 2.4 %collective-permute-start.16 = (f32[8,2,24,128]{3,2,1,0:T(8,128)S(1)}, f32[8,2,24,128]{3,2,1,0:T(8,128)S(1)}, u32[]{:S(2)}, u32[]{:S(2)}) collective-permute-start(f32[8,2,24,128]{3,2,1,0:T(8,128)S(1)} %get-tuple-element.61), channel_id=1, source_target_pairs={{0,16},{1,5},{2,18},{3,7},{4,20},{5,1},{6,22},{7,3},{8,24},{9,13},... | collective-permute-start | bytes 589832 | tf_op jit(solution)/shard_map/ppermute | solution.py:693
  94.1 3.2 %collective-permute-start.17 = (f32[8,2,24,128]{3,2,1,0:T(8,128)S(1)}, f32[8,2,24,128]{3,2,1,0:T(8,128)S(1)}, u32[]{:S(2)}, u32[]{:S(2)}) collective-permute-start(f32[8,2,24,128]{3,2,1,0:T(8,128)S(1)} %get-tuple-element.62), channel_id=1, source_target_pairs={{0,4},{1,17},{2,6},{3,19},{4,0},{5,21},{6,2},{7,23},{8,12},{9,25},... | collective-permute-start | bytes 589832 | tf_op jit(solution)/shard_map/ppermute | solution.py:693
  97.3 1.5 %collective-permute-start.19 = (f32[8,2,24,128]{3,2,1,0:T(8,128)S(1)}, f32[8,2,24,128]{3,2,1,0:T(8,128)S(1)}, u32[]{:S(2)}, u32[]{:S(2)}) collective-permute-start(f32[8,2,24,128]{3,2,1,0:T(8,128)S(1)} %get-tuple-element.64), channel_id=1, source_target_pairs={{0,24},{1,9},{2,26},{3,11},{4,28},{5,13},{6,30},{7,15},{8,16},{9,1... | collective-permute-start | bytes 589832 | tf_op jit(solution)/shard_map/ppermute | solution.py:693
  98.9 1.4 %collective-permute-start.20 = (f32[8,2,24,128]{3,2,1,0:T(8,128)S(1)}, f32[8,2,24,128]{3,2,1,0:T(8,128)S(1)}, u32[]{:S(2)}, u32[]{:S(2)}) collective-permute-start(f32[8,2,24,128]{3,2,1,0:T(8,128)S(1)} %get-tuple-element.65), channel_id=1, source_target_pairs={{0,20},{1,13},{2,22},{3,15},{4,16},{5,9},{6,18},{7,11},{8,28},{9,5... | collective-permute-start | bytes 589832 | tf_op jit(solution)/shard_map/ppermute | solution.py:693
  100.2 5.9 %collective-permute-done.16 = f32[8,2,24,128]{3,2,1,0:T(8,128)S(1)} collective-permute-done((f32[8,2,24,128]{3,2,1,0:T(8,128)S(1)}, f32[8,2,24,128]{3,2,1,0:T(8,128)S(1)}, u32[]{:S(2)}, u32[]{:S(2)}) %collective-permute-start.16) | collective-permute-done | bytes 196640 | tf_op jit(solution)/shard_map/ppermute | solution.py:693
  106.2 2.7 %collective-permute-start.22 = (f32[8,2,24,128]{3,2,1,0:T(8,128)S(1)}, f32[8,2,24,128]{3,2,1,0:T(8,128)S(1)}, u32[]{:S(2)}, u32[]{:S(2)}) collective-permute-start(f32[8,2,24,128]{3,2,1,0:T(8,128)S(1)} %get-tuple-element.67), channel_id=1, source_target_pairs={{0,28},{1,29},{2,30},{3,31},{4,24},{5,25},{6,26},{7,27},{8,20},{9,... | collective-permute-start | bytes 589832 | tf_op jit(solution)/shard_map/ppermute | solution.py:693
  108.9 3.1 %collective-permute-done.18 = f32[8,2,24,128]{3,2,1,0:T(8,128)S(1)} collective-permute-done((f32[8,2,24,128]{3,2,1,0:T(8,128)S(1)}, f32[8,2,24,128]{3,2,1,0:T(8,128)S(1)}, u32[]{:S(2)}, u32[]{:S(2)}) %collective-permute-start.18) | collective-permute-done | bytes 196640 | tf_op jit(solution)/shard_map/ppermute | solution.py:693
  112.0 14.3 %collective-permute-done.20 = f32[8,2,24,128]{3,2,1,0:T(8,128)S(1)} collective-permute-done((f32[8,2,24,128]{3,2,1,0:T(8,128)S(1)}, f32[8,2,24,128]{3,2,1,0:T(8,128)S(1)}, u32[]{:S(2)}, u32[]{:S(2)}) %collective-permute-start.20) | collective-permute-done | bytes 196640 | tf_op jit(solution)/shard_map/ppermute | solution.py:693
  126.3 2.1 %restore.1 = f32[3,4,256,128]{3,2,1,0:T(8,128)} custom-call(f32[384,128]{1,0:T(8,128)S(1)} %bitcast.30, f32[384,128]{1,0:T(8,128)S(1)} %bitcast.31, f32[384,128]{1,0:T(8,128)S(1)} %bitcast.32, f32[384,128]{1,0:T(8,128)S(1)} %bitcast.33, f32[384,128]{1,0:T(8,128)S(1)} %bitcast.34, f32[384,128]{1,0:T(8,128)S(1)} %bitcast.35, f32[384,128]{1,0:T(8,128)S(1)} %bitcast.36, ...), custom_call_target="tpu_custom_call" | custom-call | bytes 3145728 | tf_op jit(solution)/shard_map/restore/pallas_call | solution.py:671
  (43 shorter events, 0.2 us)
Async XLA Ops:
  2.1 11.2 %collective-permute-start.1 = (f32[392,128]{1,0:T(8,128)}, f32[392,128]{1,0:T(8,128)S(1)}, u32[]{:S(2)}, u32[]{:S(2)}) collective-permute-start(f32[392,128]{1,0:T(8,128)} %get-tuple-element.39), channel_id=1, source_target_pairs={{0,24},{1,9},{2,26},{3,11},{8,16},{9,1},{10,18},{11,3},{16,8},{17,... | collective-permute-start | bytes 602120 | tf_op jit(solution)/shard_map/ppermute | solution.py:693
  7.2 19.1 %collective-permute-start = (f32[392,128]{1,0:T(8,128)}, f32[392,128]{1,0:T(8,128)S(1)}, u32[]{:S(2)}, u32[]{:S(2)}) collective-permute-start(f32[392,128]{1,0:T(8,128)} %get-tuple-element.38), channel_id=1, source_target_pairs={{0,8},{1,25},{2,10},{3,27},{8,0},{9,17},{10,2},{11,19},{16,24},{17... | collective-permute-start | bytes 602120 | tf_op jit(solution)/shard_map/ppermute | solution.py:693
  7.2 20.6 %collective-permute-start.2 = (f32[392,128]{1,0:T(8,128)}, f32[392,128]{1,0:T(8,128)S(1)}, u32[]{:S(2)}, u32[]{:S(2)}) collective-permute-start(f32[392,128]{1,0:T(8,128)} %get-tuple-element.40), channel_id=1, source_target_pairs={{0,16},{1,17},{2,18},{3,19},{8,24},{9,25},{10,26},{11,27},{16,0},{... | collective-permute-start | bytes 602120 | tf_op jit(solution)/shard_map/ppermute | solution.py:693
  9.8 15.6 %copy-start.5 = (f32[392,128]{1,0:T(8,128)S(1)}, f32[392,128]{1,0:T(8,128)}, u32[]{:S(2)}) copy-start(f32[392,128]{1,0:T(8,128)} %get-tuple-element.37.refs_0_) | copy-start | bytes 602116
  9.8 15.6 %copy-start.4 = (bf16[128,256]{1,0:T(8,128)(2,1)S(1)}, bf16[128,256]{1,0:T(8,128)(2,1)}, u32[]{:S(2)}) copy-start(bf16[128,256]{1,0:T(8,128)(2,1)} %constant.22.clone.rest_ref.refs_5_.refs_2_) | copy-start | bytes 196612
  9.8 15.7 %copy-start.6 = (bf16[128,256]{1,0:T(8,128)(2,1)S(1)}, bf16[128,256]{1,0:T(8,128)(2,1)}, u32[]{:S(2)}) copy-start(bf16[128,256]{1,0:T(8,128)(2,1)} %constant.21.clone.top_ref) | copy-start | bytes 196612
  9.8 15.7 %copy-start.8 = (s32[64]{0:T(128)S(1)}, s32[64]{0:T(128)}, u32[]{:S(2)}) copy-start(s32[64]{0:T(128)} %owner_ref.1) | copy-start | bytes 772
  9.8 18.1 %copy-start.7 = (s32[8]{0:T(128)S(1)}, s32[8]{0:T(128)}, u32[]{:S(2)}) copy-start(s32[8]{0:T(128)} %low_ref.11) | copy-start | bytes 100
  13.3 0.7 copy-start.2
  14.0 12.3 %copy-start.3 = (f32[392,128]{1,0:T(8,128)S(1)}, f32[392,128]{1,0:T(8,128)}, u32[]{:S(2)}) copy-start(f32[392,128]{1,0:T(8,128)} %copy-done.2) | copy-start | bytes 602116
  14.0 29.4 %all-to-all-start = ((f32[4,384,128]{2,1,0:T(8,128)}), f32[4,384,128]{2,1,0:T(8,128)S(1)}, u32[]{:S(2)}, u32[]{:S(2)}) async-start(f32[4,384,128]{2,1,0:T(8,128)} %hand_on.1), calls=%async_computation | async-start | bytes 1572864 | tf_op jit(solution)/shard_map/all_to_all | solution.py:741
  31.4 1.5 %collective-permute-start.3 = (f32[3,4,32,128]{3,2,1,0:T(8,128)S(1)}, f32[3,4,32,128]{3,2,1,0:T(8,128)S(1)}, u32[]{:S(2)}, u32[]{:S(2)}) collective-permute-start(f32[3,4,32,128]{3,2,1,0:T(8,128)S(1)} %get-tuple-element.45), channel_id=1, source_target_pairs={{0,1},{1,0},{2,3},{3,2},{4,5},{5,4},{6,7},{7,6},{8,9},{9,8},{10,11... | collective-permute-start | bytes 589832 | tf_op jit(solution)/shard_map/ppermute | solution.py:715
  32.9 7.0 %collective-permute-start.14 = (f32[3,4,32,128]{3,2,1,0:T(8,128)S(1)}, f32[3,4,32,128]{3,2,1,0:T(8,128)S(1)}, u32[]{:S(2)}, u32[]{:S(2)}) collective-permute-start(f32[3,4,32,128]{3,2,1,0:T(8,128)S(1)} %add.21.refs_4_.first_ref), channel_id=1, source_target_pairs={{0,2},{1,3},{2,0},{3,1},{4,6},{5,7},{6,4},{7,5},{8,10},{9,11},{10,... | collective-permute-start | bytes 589832 | tf_op jit(solution)/shard_map/ppermute | solution.py:715
  39.9 1.5 %collective-permute-start.15 = (f32[3,4,32,128]{3,2,1,0:T(8,128)S(1)}, f32[3,4,32,128]{3,2,1,0:T(8,128)S(1)}, u32[]{:S(2)}, u32[]{:S(2)}) collective-permute-start(f32[3,4,32,128]{3,2,1,0:T(8,128)S(1)} %ordered_sum.3.kept_ref), channel_id=1, source_target_pairs={{0,1},{1,0},{2,3},{3,2},{4,5},{5,4},{6,7},{7,6},{8,9},{9,8},{10,11... | collective-permute-start | bytes 589832 | tf_op jit(solution)/shard_map/ppermute | solution.py:715
  43.3 36.4 %all-to-all-start.1 = ((f32[8,8,24,128]{3,2,1,0:T(8,128)}), f32[8,8,24,128]{3,2,1,0:T(8,128)S(1)}, u32[]{:S(2)}, u32[]{:S(2)}) async-start(f32[8,8,24,128]{3,2,1,0:T(8,128)} %bitcast.13), calls=%async_computation.1 | async-start | bytes 1572864 | tf_op jit(solution)/shard_map/all_to_all | solution.py:772
  53.7 1.5 %collective-permute-start.4 = (f32[3,4,32,128]{3,2,1,0:T(8,128)S(1)}, f32[3,4,32,128]{3,2,1,0:T(8,128)S(1)}, u32[]{:S(2)}, u32[]{:S(2)}) collective-permute-start(f32[3,4,32,128]{3,2,1,0:T(8,128)S(1)} %get-tuple-element.49), channel_id=1, source_target_pairs={{0,1},{1,0},{2,3},{3,2},{4,5},{5,4},{6,7},{7,6},{8,9},{9,8},{10,11... | collective-permute-start | bytes 589832 | tf_op jit(solution)/shard_map/ppermute | solution.py:715
  55.3 7.0 %collective-permute-start.5 = (f32[3,4,32,128]{3,2,1,0:T(8,128)S(1)}, f32[3,4,32,128]{3,2,1,0:T(8,128)S(1)}, u32[]{:S(2)}, u32[]{:S(2)}) collective-permute-start(f32[3,4,32,128]{3,2,1,0:T(8,128)S(1)} %add.22.first_ref), channel_id=1, source_target_pairs={{0,2},{1,3},{2,0},{3,1},{4,6},{5,7},{6,4},{7,5},{8,10},{9,11},{10,... | collective-permute-start | bytes 589832 | tf_op jit(solution)/shard_map/ppermute | solution.py:715
  62.3 1.5 %collective-permute-start.6 = (f32[3,4,32,128]{3,2,1,0:T(8,128)S(1)}, f32[3,4,32,128]{3,2,1,0:T(8,128)S(1)}, u32[]{:S(2)}, u32[]{:S(2)}) collective-permute-start(f32[3,4,32,128]{3,2,1,0:T(8,128)S(1)} %ordered_sum.2.kept_ref), channel_id=1, source_target_pairs={{0,1},{1,0},{2,3},{3,2},{4,5},{5,4},{6,7},{7,6},{8,9},{9,8},{10,11... | collective-permute-start | bytes 589832 | tf_op jit(solution)/shard_map/ppermute | solution.py:715
  65.0 11.2 %collective-permute-start.7 = (f32[8,24,128]{2,1,0:T(8,128)S(1)}, f32[8,24,128]{2,1,0:T(8,128)S(1)}, u32[]{:S(2)}, u32[]{:S(2)}) collective-permute-start(f32[8,24,128]{2,1,0:T(8,128)S(1)} %bitcast.45), channel_id=1, source_target_pairs={{0,16},{1,5},{2,18},{3,7},{4,20},{5,1},{6,22},{7,3},{8,24},{9,13},... | collective-permute-start | bytes 294920 | tf_op jit(solution)/shard_map/ppermute | solution.py:693
  68.0 8.7 %collective-permute-start.8 = (f32[8,24,128]{2,1,0:T(8,128)S(1)}, f32[8,24,128]{2,1,0:T(8,128)S(1)}, u32[]{:S(2)}, u32[]{:S(2)}) collective-permute-start(f32[8,24,128]{2,1,0:T(8,128)S(1)} %bitcast.44), channel_id=1, source_target_pairs={{0,4},{1,17},{2,6},{3,19},{4,0},{5,21},{6,2},{7,23},{8,12},{9,25},... | collective-permute-start | bytes 294920 | tf_op jit(solution)/shard_map/ppermute | solution.py:693
  69.5 17.2 %collective-permute-start.9 = (f32[8,24,128]{2,1,0:T(8,128)S(1)}, f32[8,24,128]{2,1,0:T(8,128)S(1)}, u32[]{:S(2)}, u32[]{:S(2)}) collective-permute-start(f32[8,24,128]{2,1,0:T(8,128)S(1)} %bitcast.43), channel_id=1, source_target_pairs={{0,8},{1,25},{2,10},{3,27},{4,12},{5,29},{6,14},{7,31},{8,0},{9,17... | collective-permute-start | bytes 294920 | tf_op jit(solution)/shard_map/ppermute | solution.py:693
  70.9 15.7 %collective-permute-start.10 = (f32[8,24,128]{2,1,0:T(8,128)S(1)}, f32[8,24,128]{2,1,0:T(8,128)S(1)}, u32[]{:S(2)}, u32[]{:S(2)}) collective-permute-start(f32[8,24,128]{2,1,0:T(8,128)S(1)} %bitcast.42), channel_id=1, source_target_pairs={{0,24},{1,9},{2,26},{3,11},{4,28},{5,13},{6,30},{7,15},{8,16},{9,1... | collective-permute-start | bytes 294920 | tf_op jit(solution)/shard_map/ppermute | solution.py:693
  71.5 15.9 %collective-permute-start.11 = (f32[8,24,128]{2,1,0:T(8,128)S(1)}, f32[8,24,128]{2,1,0:T(8,128)S(1)}, u32[]{:S(2)}, u32[]{:S(2)}) collective-permute-start(f32[8,24,128]{2,1,0:T(8,128)S(1)} %bitcast.41), channel_id=1, source_target_pairs={{0,20},{1,13},{2,22},{3,15},{4,16},{5,9},{6,18},{7,11},{8,28},{9,5... | collective-permute-start | bytes 294920 | tf_op jit(solution)/shard_map/ppermute | solution.py:693
  76.2 11.1 %collective-permute-start.12 = (f32[8,24,128]{2,1,0:T(8,128)S(1)}, f32[8,24,128]{2,1,0:T(8,128)S(1)}, u32[]{:S(2)}, u32[]{:S(2)}) collective-permute-start(f32[8,24,128]{2,1,0:T(8,128)S(1)} %bitcast.40), channel_id=1, source_target_pairs={{0,12},{1,21},{2,14},{3,23},{4,8},{5,17},{6,10},{7,19},{8,4},{9,29... | collective-permute-start | bytes 294920 | tf_op jit(solution)/shard_map/ppermute | solution.py:693
  76.7 10.7 %collective-permute-start.13 = (f32[8,24,128]{2,1,0:T(8,128)S(1)}, f32[8,24,128]{2,1,0:T(8,128)S(1)}, u32[]{:S(2)}, u32[]{:S(2)}) collective-permute-start(f32[8,24,128]{2,1,0:T(8,128)S(1)} %bitcast.39), channel_id=1, source_target_pairs={{0,28},{1,29},{2,30},{3,31},{4,24},{5,25},{6,26},{7,27},{8,20},{9,... | collective-permute-start | bytes 294920 | tf_op jit(solution)/shard_map/ppermute | solution.py:693
  79.7 3.4 %copy-start = (f32[8,512,512]{2,1,0:T(8,128)S(1)}, f32[8,512,512]{2,1,0:T(8,128)}, u32[]{:S(2)}) copy-start(f32[8,512,512]{2,1,0:T(8,128)} %refs_8_.1) | copy-start | bytes 25165828
  83.1 4.2 %copy-start.1 = (f32[8,512,512]{2,1,0:T(8,128)S(1)}, f32[8,512,512]{2,1,0:T(8,128)}, u32[]{:S(2)}) copy-start(f32[8,512,512]{2,1,0:T(8,128)} %refs_8_.1) | copy-start | bytes 25165828
  91.7 14.5 %collective-permute-start.16 = (f32[8,2,24,128]{3,2,1,0:T(8,128)S(1)}, f32[8,2,24,128]{3,2,1,0:T(8,128)S(1)}, u32[]{:S(2)}, u32[]{:S(2)}) collective-permute-start(f32[8,2,24,128]{3,2,1,0:T(8,128)S(1)} %get-tuple-element.61), channel_id=1, source_target_pairs={{0,16},{1,5},{2,18},{3,7},{4,20},{5,1},{6,22},{7,3},{8,24},{9,13},... | collective-permute-start | bytes 589832 | tf_op jit(solution)/shard_map/ppermute | solution.py:693
  94.1 12.0 %collective-permute-start.17 = (f32[8,2,24,128]{3,2,1,0:T(8,128)S(1)}, f32[8,2,24,128]{3,2,1,0:T(8,128)S(1)}, u32[]{:S(2)}, u32[]{:S(2)}) collective-permute-start(f32[8,2,24,128]{3,2,1,0:T(8,128)S(1)} %get-tuple-element.62), channel_id=1, source_target_pairs={{0,4},{1,17},{2,6},{3,19},{4,0},{5,21},{6,2},{7,23},{8,12},{9,25},... | collective-permute-start | bytes 589832 | tf_op jit(solution)/shard_map/ppermute | solution.py:693
  97.3 14.6 %collective-permute-start.18 = (f32[8,2,24,128]{3,2,1,0:T(8,128)S(1)}, f32[8,2,24,128]{3,2,1,0:T(8,128)S(1)}, u32[]{:S(2)}, u32[]{:S(2)}) collective-permute-start(f32[8,2,24,128]{3,2,1,0:T(8,128)S(1)} %get-tuple-element.63), channel_id=1, source_target_pairs={{0,8},{1,25},{2,10},{3,27},{4,12},{5,29},{6,14},{7,31},{8,0},{9,17... | collective-permute-start | bytes 589832 | tf_op jit(solution)/shard_map/ppermute | solution.py:693
  97.3 14.6 %collective-permute-start.19 = (f32[8,2,24,128]{3,2,1,0:T(8,128)S(1)}, f32[8,2,24,128]{3,2,1,0:T(8,128)S(1)}, u32[]{:S(2)}, u32[]{:S(2)}) collective-permute-start(f32[8,2,24,128]{3,2,1,0:T(8,128)S(1)} %get-tuple-element.64), channel_id=1, source_target_pairs={{0,24},{1,9},{2,26},{3,11},{4,28},{5,13},{6,30},{7,15},{8,16},{9,1... | collective-permute-start | bytes 589832 | tf_op jit(solution)/shard_map/ppermute | solution.py:693
  98.9 27.4 %collective-permute-start.20 = (f32[8,2,24,128]{3,2,1,0:T(8,128)S(1)}, f32[8,2,24,128]{3,2,1,0:T(8,128)S(1)}, u32[]{:S(2)}, u32[]{:S(2)}) collective-permute-start(f32[8,2,24,128]{3,2,1,0:T(8,128)S(1)} %get-tuple-element.65), channel_id=1, source_target_pairs={{0,20},{1,13},{2,22},{3,15},{4,16},{5,9},{6,18},{7,11},{8,28},{9,5... | collective-permute-start | bytes 589832 | tf_op jit(solution)/shard_map/ppermute | solution.py:693
  106.1 20.1 %collective-permute-start.21 = (f32[8,2,24,128]{3,2,1,0:T(8,128)S(1)}, f32[8,2,24,128]{3,2,1,0:T(8,128)S(1)}, u32[]{:S(2)}, u32[]{:S(2)}) collective-permute-start(f32[8,2,24,128]{3,2,1,0:T(8,128)S(1)} %get-tuple-element.66), channel_id=1, source_target_pairs={{0,12},{1,21},{2,14},{3,23},{4,8},{5,17},{6,10},{7,19},{8,4},{9,29... | collective-permute-start | bytes 589832 | tf_op jit(solution)/shard_map/ppermute | solution.py:693
  106.2 20.1 %collective-permute-start.22 = (f32[8,2,24,128]{3,2,1,0:T(8,128)S(1)}, f32[8,2,24,128]{3,2,1,0:T(8,128)S(1)}, u32[]{:S(2)}, u32[]{:S(2)}) collective-permute-start(f32[8,2,24,128]{3,2,1,0:T(8,128)S(1)} %get-tuple-element.67), channel_id=1, source_target_pairs={{0,28},{1,29},{2,30},{3,31},{4,24},{5,25},{6,26},{7,27},{8,20},{9,... | collective-permute-start | bytes 589832 | tf_op jit(solution)/shard_map/ppermute | solution.py:693

commit v20 on v19

--- a/solution.py
+++ b/solution.py
@@ -653,17 +653,17 @@
         ordered[me ^ step_at(owners, position)] = block_ref[...]
     for c in range(components):
         for mode in range(band_modes):
+            tiles = []
             for tile in range(rows // LANES):
                 parts = []
                 for p in range(2):
                     row = ((tile * 2 + p) * components + c) * band_modes + mode
                     for owner in range(owners):
                         parts.append(ordered[owner, pl.ds(row, slots, stride=per_slot), :])
-                top, rest = two_parts(jnp.concatenate(parts, axis=0))
-                both = jnp.concatenate([top, rest], axis=0)
-                out_ref[c, mode, pl.ds(tile * LANES, LANES)] = dot(
-                    both, order_ref[...], ((0,), (0,))
-                )
+                tiles.append(jnp.concatenate(parts, axis=0))
+            top, rest = two_parts(jnp.concatenate(tiles, axis=1))
+            both = jnp.concatenate([top, rest], axis=0)
+            out_ref[c, mode] = dot(both, order_ref[...], ((0,), (0,)))
 
 
 def restore(blocks, order, components, band_modes, rows, ht_count):

time: 130 us -> 130 us (level)
  no operation moved by 1% of the time
where the time goes in v20:
time: 130 us; the launch traced here: 128 us
  starting transfers between devices  49.5 us (38%)
  waiting for transfers between devices  42.7 us (33%)
  Pallas kernels  30.8 us (24%)
  local copies, waits for them, and re-layouts  4.95 us (4%)
    ppermute x17, waiting for transfers between devices, exchange(): result[position] = lax.ppermute(blocks[position], axes + ('real',), pairs)  32.3 us
    ppermute x17, starting transfers between devices, exchange(): result[position] = lax.ppermute(blocks[position], axes + ('real',), pairs)  28.4 us
    all_to_all x1, starting transfers between devices, local(): block = lax.all_to_all(block, 'kx', split_axis=0, concat_axis=0, tiled=True)  10.8 us
    ppermute x6, waiting for transfers between devices, swap(): return lax.ppermute(value, 'real', pairs)  10.4 us
    pallas_call x2, Pallas kernels, solve(): pl.pallas_call(functools.partial(solve_kernel, groups=groups, kx_count=kx...  7.79 us
    pallas_call x2, Pallas kernels, stress_terms(): pl.pallas_call(stress_kernel, out_shape=(jax.ShapeDtypeStruct(shape, jnp....  6.94 us
    all_to_all x1, starting transfers between devices, local(): lax.all_to_all(block, ('kx', 'ht'), split_axis=0, concat_axis=0, tiled=True)  6.91 us
    pallas_call x2, Pallas kernels, high_terms(): pl.pallas_call(products_kernel, out_shape=jax.ShapeDtypeStruct((component...  6 us
  transfers between devices with their start and end apart: 25, of which 13 were waited for; matrix products, arithmetic and copies ran while one was open for 1% of the time, Pallas kernels for 17%

profile of v20, /device:TPU:0, one launch (start us, length us, event | category | flops | bytes accessed | tf_op | source)
XLA Modules:
  0.0 128.4 jit_solution(3687452412836743182)
XLA Ops:
  0.0 2.1 %pack_first.1 = (f32[392,128]{1,0:T(8,128)}, f32[392,128]{1,0:T(8,128)}, f32[392,128]{1,0:T(8,128)}, f32[392,128]{1,0:T(8,128)}) custom-call(s32[4,8]{1,0:T(4,128)} %near_ref.1, s32[4]{0:T(128)} %count_ref.1, f32[12,2,4,32,128]{4,3,2,1,0:T(8,128)} %bitcast.46), custom_call_target="tpu_custom_call" | custom-call | bytes 1572864 | tf_op jit(solution)/shard_map/pack_first/pallas_call | solution.py:175
  2.1 5.0 %collective-permute-start.1 = (f32[392,128]{1,0:T(8,128)}, f32[392,128]{1,0:T(8,128)S(1)}, u32[]{:S(2)}, u32[]{:S(2)}) collective-permute-start(f32[392,128]{1,0:T(8,128)} %get-tuple-element.39), channel_id=1, source_target_pairs={{0,24},{1,9},{2,26},{3,11},{8,16},{9,1},{10,18},{11,3},{16,8},{17,... | collective-permute-start | bytes 602120 | tf_op jit(solution)/shard_map/ppermute | solution.py:693
  7.2 0.6 collective-permute-start.2
  7.7 2.1 %pack.1.value_ref = f32[4,384,128]{2,1,0:T(8,128)} custom-call(f32[12,2,4,32,128]{4,3,2,1,0:T(8,128)} %bitcast.47), custom_call_target="tpu_custom_call" | custom-call | bytes 1572864 | tf_op jit(solution)/shard_map/pack/pallas_call | solution.py:201
  9.8 0.0 copy-start.7
  9.8 3.5 %collective-permute-done.1.after_ref.refs_2_ = f32[392,128]{1,0:T(8,128)S(1)} collective-permute-done((f32[392,128]{1,0:T(8,128)}, f32[392,128]{1,0:T(8,128)S(1)}, u32[]{:S(2)}, u32[]{:S(2)}) %collective-permute-start.1) | collective-permute-done | bytes 200736 | tf_op jit(solution)/shard_map/ppermute | solution.py:693
  13.3 0.7 copy-done.2
  14.0 10.8 %all-to-all-start = ((f32[4,384,128]{2,1,0:T(8,128)}), f32[4,384,128]{2,1,0:T(8,128)S(1)}, u32[]{:S(2)}, u32[]{:S(2)}) async-start(f32[4,384,128]{2,1,0:T(8,128)} %hand_on.1), calls=%async_computation | async-start | bytes 1572864 | tf_op jit(solution)/shard_map/all_to_all | solution.py:741
  24.8 0.1 broadcast_in_dim.85
  24.8 0.1 broadcast_in_dim.86
  24.9 0.1 broadcast_in_dim.91
  25.0 0.1 broadcast_in_dim.92
  25.1 0.1 broadcast_in_dim.96
  25.2 0.1 broadcast_in_dim.97
  25.3 0.1 broadcast_in_dim.101
  25.4 0.1 broadcast_in_dim.102
  25.5 0.8 tables.1
  26.3 1.5 %collective-permute-done.2.refs_3_ = f32[392,128]{1,0:T(8,128)S(1)} collective-permute-done((f32[392,128]{1,0:T(8,128)}, f32[392,128]{1,0:T(8,128)S(1)}, u32[]{:S(2)}, u32[]{:S(2)}) %collective-permute-start.2) | collective-permute-done | bytes 200736 | tf_op jit(solution)/shard_map/ppermute | solution.py:693
  27.8 0.1 add_convert_fusion
  27.9 3.5 %stress.2 = (f32[3,16,32,128]{3,2,1,0:T(8,128)S(1)}, f32[3,16,32,256]{3,2,1,0:T(8,128)S(1)}, f32[3,4,32,128]{3,2,1,0:T(8,128)S(1)}, f32[3,4,32,128]{3,2,1,0:T(8,128)S(1)}) custom-call(s32[8]{0:T(128)S(1)} %copy-done.7, s32[16,8]{1,0:T(8,128)S(1)} %bitcast.26, f32[392,128]{1,0:T(8,128)S(1)} %copy-done.5, f32[392,128]{1,0:T(8,128)S(1)} %collective-permute-done.refs_1_, ...), custom_call_target="tpu_custom_call" | custom-call | bytes 12582912 | tf_op jit(solution)/shard_map/stress/pallas_call | solution.py:368
  31.4 0.1 collective-permute-start.3
  31.5 1.4 %collective-permute-done.3 = f32[3,4,32,128]{3,2,1,0:T(8,128)S(1)} collective-permute-done((f32[3,4,32,128]{3,2,1,0:T(8,128)S(1)}, f32[3,4,32,128]{3,2,1,0:T(8,128)S(1)}, u32[]{:S(2)}, u32[]{:S(2)}) %collective-permute-start.3) | collective-permute-done | bytes 196640 | tf_op jit(solution)/shard_map/ppermute | solution.py:715
  32.9 1.6 %collective-permute-start.14 = (f32[3,4,32,128]{3,2,1,0:T(8,128)S(1)}, f32[3,4,32,128]{3,2,1,0:T(8,128)S(1)}, u32[]{:S(2)}, u32[]{:S(2)}) collective-permute-start(f32[3,4,32,128]{3,2,1,0:T(8,128)S(1)} %add.21.refs_4_.first_ref), channel_id=1, source_target_pairs={{0,2},{1,3},{2,0},{3,1},{4,6},{5,7},{6,4},{7,5},{8,10},{9,11},{10,... | collective-permute-start | bytes 589832 | tf_op jit(solution)/shard_map/ppermute | solution.py:715
  34.5 0.2 slice_reduce_fusion.count_ref
  34.6 3.0 %products.3._.forcing_ref = f32[3,8,32,128]{3,2,1,0:T(8,128)S(1)} custom-call(s32[8]{0:T(128)S(1)} %copy-done.7, s32[16,8]{1,0:T(8,128)S(1)} %bitcast.27, s32[16]{0:T(128)S(1)} %slice_reduce_fusion.count_ref, f32[3,16,32,256]{3,2,1,0:T(8,128)S(1)} %get-tuple-element.59.physical, bf16[256,256]{1,0:T(8,128)(2,1)S(1)} %get-tuple-element.42.refs_6_.refs_3_.back_ref, ...), custom_call_target="tpu_custom_call" | custom-call | bytes 12582912 | tf_op jit(solution)/shard_map/products/pallas_call | solution.py:433
  37.6 2.3 %collective-permute-done.14.second_ref = f32[3,4,32,128]{3,2,1,0:T(8,128)S(1)} collective-permute-done((f32[3,4,32,128]{3,2,1,0:T(8,128)S(1)}, f32[3,4,32,128]{3,2,1,0:T(8,128)S(1)}, u32[]{:S(2)}, u32[]{:S(2)}) %collective-permute-start.14) | collective-permute-done | bytes 196640 | tf_op jit(solution)/shard_map/ppermute | solution.py:715
  39.9 0.1 collective-permute-start.15
  40.0 1.4 %collective-permute-done.15.other_ref = f32[3,4,32,128]{3,2,1,0:T(8,128)S(1)} collective-permute-done((f32[3,4,32,128]{3,2,1,0:T(8,128)S(1)}, f32[3,4,32,128]{3,2,1,0:T(8,128)S(1)}, u32[]{:S(2)}, u32[]{:S(2)}) %collective-permute-start.15) | collective-permute-done | bytes 196640 | tf_op jit(solution)/shard_map/ppermute | solution.py:715
  41.4 1.9 %outgoing.3 = f32[1536,128]{1,0:T(8,128)} custom-call(s32[8]{0:T(128)S(1)} %copy-done.7, s32[16]{0:T(128)S(1)} %slice_reduce_fusion.count_ref, f32[3,16,32,128]{3,2,1,0:T(8,128)S(1)} %get-tuple-element.58.slotted_ref, f32[3,8,32,128]{3,2,1,0:T(8,128)S(1)} %products.3._.forcing_ref, f32[3,4,32,128]{3,2,1,0:T(8,128)S(1)} %ordered_sum.3.kept_ref, ...), custom_call_target="tpu_custom_call" | custom-call | bytes 1572864 | tf_op jit(solution)/shard_map/outgoing/pallas_call | solution.py:499
  43.3 6.9 %all-to-all-start.1 = ((f32[8,8,24,128]{3,2,1,0:T(8,128)}), f32[8,8,24,128]{3,2,1,0:T(8,128)S(1)}, u32[]{:S(2)}, u32[]{:S(2)}) async-start(f32[8,8,24,128]{3,2,1,0:T(8,128)} %bitcast.13), calls=%async_computation.1 | async-start | bytes 1572864 | tf_op jit(solution)/shard_map/all_to_all | solution.py:772
  50.3 3.5 %stress.3 = (f32[3,16,32,128]{3,2,1,0:T(8,128)S(1)}, f32[3,16,32,256]{3,2,1,0:T(8,128)S(1)}, f32[3,4,32,128]{3,2,1,0:T(8,128)S(1)}, f32[3,4,32,128]{3,2,1,0:T(8,128)S(1)}) custom-call(s32[8]{0:T(128)S(1)} %copy-done.7, s32[16,8]{1,0:T(8,128)S(1)} %bitcast.28, f32[4,384,128]{2,1,0:T(8,128)S(1)} %all-to-all-done.refs_0_, ...), custom_call_target="tpu_custom_call" | custom-call | bytes 12582912 | tf_op jit(solution)/shard_map/stress/pallas_call | solution.py:368
  53.7 0.1 collective-permute-start.4
  53.8 1.4 %collective-permute-done.4 = f32[3,4,32,128]{3,2,1,0:T(8,128)S(1)} collective-permute-done((f32[3,4,32,128]{3,2,1,0:T(8,128)S(1)}, f32[3,4,32,128]{3,2,1,0:T(8,128)S(1)}, u32[]{:S(2)}, u32[]{:S(2)}) %collective-permute-start.4) | collective-permute-done | bytes 196640 | tf_op jit(solution)/shard_map/ppermute | solution.py:715
  55.3 1.6 %collective-permute-start.5 = (f32[3,4,32,128]{3,2,1,0:T(8,128)S(1)}, f32[3,4,32,128]{3,2,1,0:T(8,128)S(1)}, u32[]{:S(2)}, u32[]{:S(2)}) collective-permute-start(f32[3,4,32,128]{3,2,1,0:T(8,128)S(1)} %add.22.first_ref), channel_id=1, source_target_pairs={{0,2},{1,3},{2,0},{3,1},{4,6},{5,7},{6,4},{7,5},{8,10},{9,11},{10,... | collective-permute-start | bytes 589832 | tf_op jit(solution)/shard_map/ppermute | solution.py:715
  56.8 3.0 %products.2._.forcing_ref = f32[3,8,32,128]{3,2,1,0:T(8,128)S(1)} custom-call(s32[8]{0:T(128)S(1)} %copy-done.7, s32[16,8]{1,0:T(8,128)S(1)} %bitcast.29, s32[16]{0:T(128)S(1)} %slice_reduce_fusion.count_ref, f32[3,16,32,256]{3,2,1,0:T(8,128)S(1)} %get-tuple-element.47.physical, bf16[256,256]{1,0:T(8,128)(2,1)S(1)} %get-tuple-element.42.refs_6_.refs_3_.back_ref, ...), custom_call_target="tpu_custom_call" | custom-call | bytes 12582912 | tf_op jit(solution)/shard_map/products/pallas_call | solution.py:433
  59.8 2.5 %collective-permute-done.5.second_ref = f32[3,4,32,128]{3,2,1,0:T(8,128)S(1)} collective-permute-done((f32[3,4,32,128]{3,2,1,0:T(8,128)S(1)}, f32[3,4,32,128]{3,2,1,0:T(8,128)S(1)}, u32[]{:S(2)}, u32[]{:S(2)}) %collective-permute-start.5) | collective-permute-done | bytes 196640 | tf_op jit(solution)/shard_map/ppermute | solution.py:715
  62.3 0.1 collective-permute-start.6
  62.4 1.4 %collective-permute-done.6.other_ref = f32[3,4,32,128]{3,2,1,0:T(8,128)S(1)} collective-permute-done((f32[3,4,32,128]{3,2,1,0:T(8,128)S(1)}, f32[3,4,32,128]{3,2,1,0:T(8,128)S(1)}, u32[]{:S(2)}, u32[]{:S(2)}) %collective-permute-start.6) | collective-permute-done | bytes 196640 | tf_op jit(solution)/shard_map/ppermute | solution.py:715
  63.8 1.2 outgoing.2
  65.0 3.0 %collective-permute-start.7 = (f32[8,24,128]{2,1,0:T(8,128)S(1)}, f32[8,24,128]{2,1,0:T(8,128)S(1)}, u32[]{:S(2)}, u32[]{:S(2)}) collective-permute-start(f32[8,24,128]{2,1,0:T(8,128)S(1)} %bitcast.45), channel_id=1, source_target_pairs={{0,16},{1,5},{2,18},{3,7},{4,20},{5,1},{6,22},{7,3},{8,24},{9,13},... | collective-permute-start | bytes 294920 | tf_op jit(solution)/shard_map/ppermute | solution.py:693
  68.0 1.5 %collective-permute-start.8 = (f32[8,24,128]{2,1,0:T(8,128)S(1)}, f32[8,24,128]{2,1,0:T(8,128)S(1)}, u32[]{:S(2)}, u32[]{:S(2)}) collective-permute-start(f32[8,24,128]{2,1,0:T(8,128)S(1)} %bitcast.44), channel_id=1, source_target_pairs={{0,4},{1,17},{2,6},{3,19},{4,0},{5,21},{6,2},{7,23},{8,12},{9,25},... | collective-permute-start | bytes 294920 | tf_op jit(solution)/shard_map/ppermute | solution.py:693
  69.5 1.5 %collective-permute-start.9 = (f32[8,24,128]{2,1,0:T(8,128)S(1)}, f32[8,24,128]{2,1,0:T(8,128)S(1)}, u32[]{:S(2)}, u32[]{:S(2)}) collective-permute-start(f32[8,24,128]{2,1,0:T(8,128)S(1)} %bitcast.43), channel_id=1, source_target_pairs={{0,8},{1,25},{2,10},{3,27},{4,12},{5,29},{6,14},{7,31},{8,0},{9,17... | collective-permute-start | bytes 294920 | tf_op jit(solution)/shard_map/ppermute | solution.py:693
  70.9 0.6 collective-permute-start.10
  71.5 1.5 %collective-permute-start.11 = (f32[8,24,128]{2,1,0:T(8,128)S(1)}, f32[8,24,128]{2,1,0:T(8,128)S(1)}, u32[]{:S(2)}, u32[]{:S(2)}) collective-permute-start(f32[8,24,128]{2,1,0:T(8,128)S(1)} %bitcast.41), channel_id=1, source_target_pairs={{0,20},{1,13},{2,22},{3,15},{4,16},{5,9},{6,18},{7,11},{8,28},{9,5... | collective-permute-start | bytes 294920 | tf_op jit(solution)/shard_map/ppermute | solution.py:693
  72.9 3.3 %collective-permute-done.7.refs_1_ = f32[8,24,128]{2,1,0:T(8,128)S(1)} collective-permute-done((f32[8,24,128]{2,1,0:T(8,128)S(1)}, f32[8,24,128]{2,1,0:T(8,128)S(1)}, u32[]{:S(2)}, u32[]{:S(2)}) %collective-permute-start.7) | collective-permute-done | bytes 98336 | tf_op jit(solution)/shard_map/ppermute | solution.py:693
  76.2 0.4 collective-permute-start.12
  76.7 0.0 collective-permute-done.8.refs_2_
  76.7 3.1 %collective-permute-start.13 = (f32[8,24,128]{2,1,0:T(8,128)S(1)}, f32[8,24,128]{2,1,0:T(8,128)S(1)}, u32[]{:S(2)}, u32[]{:S(2)}) collective-permute-start(f32[8,24,128]{2,1,0:T(8,128)S(1)} %bitcast.39), channel_id=1, source_target_pairs={{0,28},{1,29},{2,30},{3,31},{4,24},{5,25},{6,26},{7,27},{8,20},{9,... | collective-permute-start | bytes 294920 | tf_op jit(solution)/shard_map/ppermute | solution.py:693
  79.7 3.4 %copy-done = f32[8,512,512]{2,1,0:T(8,128)S(1)} copy-done((f32[8,512,512]{2,1,0:T(8,128)S(1)}, f32[8,512,512]{2,1,0:T(8,128)}, u32[]{:S(2)}) %copy-start) | copy-done | bytes 8388632
  83.1 3.5 %solve.2.refs_9_ = f32[8,512,128]{2,1,0:T(8,128)S(1)} custom-call(f32[8,8,24,128]{3,2,1,0:T(8,128)S(1)} %all-to-all-done.1.refs_0_, f32[8,512,512]{2,1,0:T(8,128)S(1)} %copy-done), custom_call_target="tpu_custom_call" | custom-call | bytes 8388608 | tf_op jit(solution)/shard_map/solve/pallas_call | solution.py:631
  86.6 0.0 collective-permute-done.9.refs_3_
  86.6 0.0 collective-permute-done.10.refs_4_
  86.7 0.7 collective-permute-done.11.refs_5_
  87.4 4.3 %solve.3 = (f32[8,2,24,128]{3,2,1,0:T(8,128)S(1)}, f32[8,2,24,128]{3,2,1,0:T(8,128)S(1)}, f32[8,2,24,128]{3,2,1,0:T(8,128)S(1)}, f32[8,2,24,128]{3,2,1,0:T(8,128...) custom-call(f32[8,24,128]{2,1,0:T(8,128)S(1)} %bitcast.38, ...), custom_call_target="tpu_custom_call" | custom-call | bytes 8388608 | tf_op jit(solution)/shard_map/solve/pallas_call | solution.py:631
  91.7 2.4 %collective-permute-start.16 = (f32[8,2,24,128]{3,2,1,0:T(8,128)S(1)}, f32[8,2,24,128]{3,2,1,0:T(8,128)S(1)}, u32[]{:S(2)}, u32[]{:S(2)}) collective-permute-start(f32[8,2,24,128]{3,2,1,0:T(8,128)S(1)} %get-tuple-element.61), channel_id=1, source_target_pairs={{0,16},{1,5},{2,18},{3,7},{4,20},{5,1},{6,22},{7,3},{8,24},{9,13},... | collective-permute-start | bytes 589832 | tf_op jit(solution)/shard_map/ppermute | solution.py:693
  94.1 3.2 %collective-permute-start.17 = (f32[8,2,24,128]{3,2,1,0:T(8,128)S(1)}, f32[8,2,24,128]{3,2,1,0:T(8,128)S(1)}, u32[]{:S(2)}, u32[]{:S(2)}) collective-permute-start(f32[8,2,24,128]{3,2,1,0:T(8,128)S(1)} %get-tuple-element.62), channel_id=1, source_target_pairs={{0,4},{1,17},{2,6},{3,19},{4,0},{5,21},{6,2},{7,23},{8,12},{9,25},... | collective-permute-start | bytes 589832 | tf_op jit(solution)/shard_map/ppermute | solution.py:693
  97.3 1.5 %collective-permute-start.19 = (f32[8,2,24,128]{3,2,1,0:T(8,128)S(1)}, f32[8,2,24,128]{3,2,1,0:T(8,128)S(1)}, u32[]{:S(2)}, u32[]{:S(2)}) collective-permute-start(f32[8,2,24,128]{3,2,1,0:T(8,128)S(1)} %get-tuple-element.64), channel_id=1, source_target_pairs={{0,24},{1,9},{2,26},{3,11},{4,28},{5,13},{6,30},{7,15},{8,16},{9,1... | collective-permute-start | bytes 589832 | tf_op jit(solution)/shard_map/ppermute | solution.py:693
  98.9 1.4 %collective-permute-start.20 = (f32[8,2,24,128]{3,2,1,0:T(8,128)S(1)}, f32[8,2,24,128]{3,2,1,0:T(8,128)S(1)}, u32[]{:S(2)}, u32[]{:S(2)}) collective-permute-start(f32[8,2,24,128]{3,2,1,0:T(8,128)S(1)} %get-tuple-element.65), channel_id=1, source_target_pairs={{0,20},{1,13},{2,22},{3,15},{4,16},{5,9},{6,18},{7,11},{8,28},{9,5... | collective-permute-start | bytes 589832 | tf_op jit(solution)/shard_map/ppermute | solution.py:693
  100.3 5.9 %collective-permute-done.16 = f32[8,2,24,128]{3,2,1,0:T(8,128)S(1)} collective-permute-done((f32[8,2,24,128]{3,2,1,0:T(8,128)S(1)}, f32[8,2,24,128]{3,2,1,0:T(8,128)S(1)}, u32[]{:S(2)}, u32[]{:S(2)}) %collective-permute-start.16) | collective-permute-done | bytes 196640 | tf_op jit(solution)/shard_map/ppermute | solution.py:693
  106.1 2.7 %collective-permute-start.22 = (f32[8,2,24,128]{3,2,1,0:T(8,128)S(1)}, f32[8,2,24,128]{3,2,1,0:T(8,128)S(1)}, u32[]{:S(2)}, u32[]{:S(2)}) collective-permute-start(f32[8,2,24,128]{3,2,1,0:T(8,128)S(1)} %get-tuple-element.67), channel_id=1, source_target_pairs={{0,28},{1,29},{2,30},{3,31},{4,24},{5,25},{6,26},{7,27},{8,20},{9,... | collective-permute-start | bytes 589832 | tf_op jit(solution)/shard_map/ppermute | solution.py:693
  108.9 3.1 %collective-permute-done.18 = f32[8,2,24,128]{3,2,1,0:T(8,128)S(1)} collective-permute-done((f32[8,2,24,128]{3,2,1,0:T(8,128)S(1)}, f32[8,2,24,128]{3,2,1,0:T(8,128)S(1)}, u32[]{:S(2)}, u32[]{:S(2)}) %collective-permute-start.18) | collective-permute-done | bytes 196640 | tf_op jit(solution)/shard_map/ppermute | solution.py:693
  112.0 14.3 %collective-permute-done.20 = f32[8,2,24,128]{3,2,1,0:T(8,128)S(1)} collective-permute-done((f32[8,2,24,128]{3,2,1,0:T(8,128)S(1)}, f32[8,2,24,128]{3,2,1,0:T(8,128)S(1)}, u32[]{:S(2)}, u32[]{:S(2)}) %collective-permute-start.20) | collective-permute-done | bytes 196640 | tf_op jit(solution)/shard_map/ppermute | solution.py:693
  126.3 0.0 collective-permute-done.21
  126.3 2.0 %restore.1 = f32[3,4,256,128]{3,2,1,0:T(8,128)} custom-call(f32[384,128]{1,0:T(8,128)S(1)} %bitcast.30, f32[384,128]{1,0:T(8,128)S(1)} %bitcast.31, f32[384,128]{1,0:T(8,128)S(1)} %bitcast.32, f32[384,128]{1,0:T(8,128)S(1)} %bitcast.33, f32[384,128]{1,0:T(8,128)S(1)} %bitcast.34, f32[384,128]{1,0:T(8,128)S(1)} %bitcast.35, f32[384,128]{1,0:T(8,128)S(1)} %bitcast.36, ...), custom_call_target="tpu_custom_call" | custom-call | bytes 3145728 | tf_op jit(solution)/shard_map/restore/pallas_call | solution.py:671
  (43 shorter events, 0.2 us)
Async XLA Ops:
  2.1 11.2 %collective-permute-start.1 = (f32[392,128]{1,0:T(8,128)}, f32[392,128]{1,0:T(8,128)S(1)}, u32[]{:S(2)}, u32[]{:S(2)}) collective-permute-start(f32[392,128]{1,0:T(8,128)} %get-tuple-element.39), channel_id=1, source_target_pairs={{0,24},{1,9},{2,26},{3,11},{8,16},{9,1},{10,18},{11,3},{16,8},{17,... | collective-permute-start | bytes 602120 | tf_op jit(solution)/shard_map/ppermute | solution.py:693
  7.2 19.1 %collective-permute-start = (f32[392,128]{1,0:T(8,128)}, f32[392,128]{1,0:T(8,128)S(1)}, u32[]{:S(2)}, u32[]{:S(2)}) collective-permute-start(f32[392,128]{1,0:T(8,128)} %get-tuple-element.38), channel_id=1, source_target_pairs={{0,8},{1,25},{2,10},{3,27},{8,0},{9,17},{10,2},{11,19},{16,24},{17... | collective-permute-start | bytes 602120 | tf_op jit(solution)/shard_map/ppermute | solution.py:693
  7.2 20.6 %collective-permute-start.2 = (f32[392,128]{1,0:T(8,128)}, f32[392,128]{1,0:T(8,128)S(1)}, u32[]{:S(2)}, u32[]{:S(2)}) collective-permute-start(f32[392,128]{1,0:T(8,128)} %get-tuple-element.40), channel_id=1, source_target_pairs={{0,16},{1,17},{2,18},{3,19},{8,24},{9,25},{10,26},{11,27},{16,0},{... | collective-permute-start | bytes 602120 | tf_op jit(solution)/shard_map/ppermute | solution.py:693
  9.8 15.6 %copy-start.5 = (f32[392,128]{1,0:T(8,128)S(1)}, f32[392,128]{1,0:T(8,128)}, u32[]{:S(2)}) copy-start(f32[392,128]{1,0:T(8,128)} %get-tuple-element.37.refs_0_) | copy-start | bytes 602116
  9.8 15.6 %copy-start.4 = (bf16[128,256]{1,0:T(8,128)(2,1)S(1)}, bf16[128,256]{1,0:T(8,128)(2,1)}, u32[]{:S(2)}) copy-start(bf16[128,256]{1,0:T(8,128)(2,1)} %constant.22.clone.rest_ref.refs_5_.refs_2_) | copy-start | bytes 196612
  9.8 15.7 %copy-start.6 = (bf16[128,256]{1,0:T(8,128)(2,1)S(1)}, bf16[128,256]{1,0:T(8,128)(2,1)}, u32[]{:S(2)}) copy-start(bf16[128,256]{1,0:T(8,128)(2,1)} %constant.21.clone.top_ref) | copy-start | bytes 196612
  9.8 15.7 %copy-start.8 = (s32[64]{0:T(128)S(1)}, s32[64]{0:T(128)}, u32[]{:S(2)}) copy-start(s32[64]{0:T(128)} %owner_ref.1) | copy-start | bytes 772
  9.8 18.1 %copy-start.7 = (s32[8]{0:T(128)S(1)}, s32[8]{0:T(128)}, u32[]{:S(2)}) copy-start(s32[8]{0:T(128)} %low_ref.11) | copy-start | bytes 100
  13.3 0.7 copy-start.2
  14.0 12.3 %copy-start.3 = (f32[392,128]{1,0:T(8,128)S(1)}, f32[392,128]{1,0:T(8,128)}, u32[]{:S(2)}) copy-start(f32[392,128]{1,0:T(8,128)} %copy-done.2) | copy-start | bytes 602116
  14.0 29.4 %all-to-all-start = ((f32[4,384,128]{2,1,0:T(8,128)}), f32[4,384,128]{2,1,0:T(8,128)S(1)}, u32[]{:S(2)}, u32[]{:S(2)}) async-start(f32[4,384,128]{2,1,0:T(8,128)} %hand_on.1), calls=%async_computation | async-start | bytes 1572864 | tf_op jit(solution)/shard_map/all_to_all | solution.py:741
  31.4 1.5 %collective-permute-start.3 = (f32[3,4,32,128]{3,2,1,0:T(8,128)S(1)}, f32[3,4,32,128]{3,2,1,0:T(8,128)S(1)}, u32[]{:S(2)}, u32[]{:S(2)}) collective-permute-start(f32[3,4,32,128]{3,2,1,0:T(8,128)S(1)} %get-tuple-element.45), channel_id=1, source_target_pairs={{0,1},{1,0},{2,3},{3,2},{4,5},{5,4},{6,7},{7,6},{8,9},{9,8},{10,11... | collective-permute-start | bytes 589832 | tf_op jit(solution)/shard_map/ppermute | solution.py:715
  32.9 7.0 %collective-permute-start.14 = (f32[3,4,32,128]{3,2,1,0:T(8,128)S(1)}, f32[3,4,32,128]{3,2,1,0:T(8,128)S(1)}, u32[]{:S(2)}, u32[]{:S(2)}) collective-permute-start(f32[3,4,32,128]{3,2,1,0:T(8,128)S(1)} %add.21.refs_4_.first_ref), channel_id=1, source_target_pairs={{0,2},{1,3},{2,0},{3,1},{4,6},{5,7},{6,4},{7,5},{8,10},{9,11},{10,... | collective-permute-start | bytes 589832 | tf_op jit(solution)/shard_map/ppermute | solution.py:715
  39.9 1.5 %collective-permute-start.15 = (f32[3,4,32,128]{3,2,1,0:T(8,128)S(1)}, f32[3,4,32,128]{3,2,1,0:T(8,128)S(1)}, u32[]{:S(2)}, u32[]{:S(2)}) collective-permute-start(f32[3,4,32,128]{3,2,1,0:T(8,128)S(1)} %ordered_sum.3.kept_ref), channel_id=1, source_target_pairs={{0,1},{1,0},{2,3},{3,2},{4,5},{5,4},{6,7},{7,6},{8,9},{9,8},{10,11... | collective-permute-start | bytes 589832 | tf_op jit(solution)/shard_map/ppermute | solution.py:715
  43.3 36.4 %all-to-all-start.1 = ((f32[8,8,24,128]{3,2,1,0:T(8,128)}), f32[8,8,24,128]{3,2,1,0:T(8,128)S(1)}, u32[]{:S(2)}, u32[]{:S(2)}) async-start(f32[8,8,24,128]{3,2,1,0:T(8,128)} %bitcast.13), calls=%async_computation.1 | async-start | bytes 1572864 | tf_op jit(solution)/shard_map/all_to_all | solution.py:772
  53.7 1.5 %collective-permute-start.4 = (f32[3,4,32,128]{3,2,1,0:T(8,128)S(1)}, f32[3,4,32,128]{3,2,1,0:T(8,128)S(1)}, u32[]{:S(2)}, u32[]{:S(2)}) collective-permute-start(f32[3,4,32,128]{3,2,1,0:T(8,128)S(1)} %get-tuple-element.49), channel_id=1, source_target_pairs={{0,1},{1,0},{2,3},{3,2},{4,5},{5,4},{6,7},{7,6},{8,9},{9,8},{10,11... | collective-permute-start | bytes 589832 | tf_op jit(solution)/shard_map/ppermute | solution.py:715
  55.3 7.0 %collective-permute-start.5 = (f32[3,4,32,128]{3,2,1,0:T(8,128)S(1)}, f32[3,4,32,128]{3,2,1,0:T(8,128)S(1)}, u32[]{:S(2)}, u32[]{:S(2)}) collective-permute-start(f32[3,4,32,128]{3,2,1,0:T(8,128)S(1)} %add.22.first_ref), channel_id=1, source_target_pairs={{0,2},{1,3},{2,0},{3,1},{4,6},{5,7},{6,4},{7,5},{8,10},{9,11},{10,... | collective-permute-start | bytes 589832 | tf_op jit(solution)/shard_map/ppermute | solution.py:715
  62.3 1.5 %collective-permute-start.6 = (f32[3,4,32,128]{3,2,1,0:T(8,128)S(1)}, f32[3,4,32,128]{3,2,1,0:T(8,128)S(1)}, u32[]{:S(2)}, u32[]{:S(2)}) collective-permute-start(f32[3,4,32,128]{3,2,1,0:T(8,128)S(1)} %ordered_sum.2.kept_ref), channel_id=1, source_target_pairs={{0,1},{1,0},{2,3},{3,2},{4,5},{5,4},{6,7},{7,6},{8,9},{9,8},{10,11... | collective-permute-start | bytes 589832 | tf_op jit(solution)/shard_map/ppermute | solution.py:715
  65.0 11.2 %collective-permute-start.7 = (f32[8,24,128]{2,1,0:T(8,128)S(1)}, f32[8,24,128]{2,1,0:T(8,128)S(1)}, u32[]{:S(2)}, u32[]{:S(2)}) collective-permute-start(f32[8,24,128]{2,1,0:T(8,128)S(1)} %bitcast.45), channel_id=1, source_target_pairs={{0,16},{1,5},{2,18},{3,7},{4,20},{5,1},{6,22},{7,3},{8,24},{9,13},... | collective-permute-start | bytes 294920 | tf_op jit(solution)/shard_map/ppermute | solution.py:693
  68.0 8.7 %collective-permute-start.8 = (f32[8,24,128]{2,1,0:T(8,128)S(1)}, f32[8,24,128]{2,1,0:T(8,128)S(1)}, u32[]{:S(2)}, u32[]{:S(2)}) collective-permute-start(f32[8,24,128]{2,1,0:T(8,128)S(1)} %bitcast.44), channel_id=1, source_target_pairs={{0,4},{1,17},{2,6},{3,19},{4,0},{5,21},{6,2},{7,23},{8,12},{9,25},... | collective-permute-start | bytes 294920 | tf_op jit(solution)/shard_map/ppermute | solution.py:693
  69.5 17.2 %collective-permute-start.9 = (f32[8,24,128]{2,1,0:T(8,128)S(1)}, f32[8,24,128]{2,1,0:T(8,128)S(1)}, u32[]{:S(2)}, u32[]{:S(2)}) collective-permute-start(f32[8,24,128]{2,1,0:T(8,128)S(1)} %bitcast.43), channel_id=1, source_target_pairs={{0,8},{1,25},{2,10},{3,27},{4,12},{5,29},{6,14},{7,31},{8,0},{9,17... | collective-permute-start | bytes 294920 | tf_op jit(solution)/shard_map/ppermute | solution.py:693
  70.9 15.7 %collective-permute-start.10 = (f32[8,24,128]{2,1,0:T(8,128)S(1)}, f32[8,24,128]{2,1,0:T(8,128)S(1)}, u32[]{:S(2)}, u32[]{:S(2)}) collective-permute-start(f32[8,24,128]{2,1,0:T(8,128)S(1)} %bitcast.42), channel_id=1, source_target_pairs={{0,24},{1,9},{2,26},{3,11},{4,28},{5,13},{6,30},{7,15},{8,16},{9,1... | collective-permute-start | bytes 294920 | tf_op jit(solution)/shard_map/ppermute | solution.py:693
  71.5 15.9 %collective-permute-start.11 = (f32[8,24,128]{2,1,0:T(8,128)S(1)}, f32[8,24,128]{2,1,0:T(8,128)S(1)}, u32[]{:S(2)}, u32[]{:S(2)}) collective-permute-start(f32[8,24,128]{2,1,0:T(8,128)S(1)} %bitcast.41), channel_id=1, source_target_pairs={{0,20},{1,13},{2,22},{3,15},{4,16},{5,9},{6,18},{7,11},{8,28},{9,5... | collective-permute-start | bytes 294920 | tf_op jit(solution)/shard_map/ppermute | solution.py:693
  76.2 11.1 %collective-permute-start.12 = (f32[8,24,128]{2,1,0:T(8,128)S(1)}, f32[8,24,128]{2,1,0:T(8,128)S(1)}, u32[]{:S(2)}, u32[]{:S(2)}) collective-permute-start(f32[8,24,128]{2,1,0:T(8,128)S(1)} %bitcast.40), channel_id=1, source_target_pairs={{0,12},{1,21},{2,14},{3,23},{4,8},{5,17},{6,10},{7,19},{8,4},{9,29... | collective-permute-start | bytes 294920 | tf_op jit(solution)/shard_map/ppermute | solution.py:693
  76.7 10.7 %collective-permute-start.13 = (f32[8,24,128]{2,1,0:T(8,128)S(1)}, f32[8,24,128]{2,1,0:T(8,128)S(1)}, u32[]{:S(2)}, u32[]{:S(2)}) collective-permute-start(f32[8,24,128]{2,1,0:T(8,128)S(1)} %bitcast.39), channel_id=1, source_target_pairs={{0,28},{1,29},{2,30},{3,31},{4,24},{5,25},{6,26},{7,27},{8,20},{9,... | collective-permute-start | bytes 294920 | tf_op jit(solution)/shard_map/ppermute | solution.py:693
  79.7 3.4 %copy-start = (f32[8,512,512]{2,1,0:T(8,128)S(1)}, f32[8,512,512]{2,1,0:T(8,128)}, u32[]{:S(2)}) copy-start(f32[8,512,512]{2,1,0:T(8,128)} %refs_8_.1) | copy-start | bytes 25165828
  83.1 4.2 %copy-start.1 = (f32[8,512,512]{2,1,0:T(8,128)S(1)}, f32[8,512,512]{2,1,0:T(8,128)}, u32[]{:S(2)}) copy-start(f32[8,512,512]{2,1,0:T(8,128)} %refs_8_.1) | copy-start | bytes 25165828
  91.7 14.4 %collective-permute-start.16 = (f32[8,2,24,128]{3,2,1,0:T(8,128)S(1)}, f32[8,2,24,128]{3,2,1,0:T(8,128)S(1)}, u32[]{:S(2)}, u32[]{:S(2)}) collective-permute-start(f32[8,2,24,128]{3,2,1,0:T(8,128)S(1)} %get-tuple-element.61), channel_id=1, source_target_pairs={{0,16},{1,5},{2,18},{3,7},{4,20},{5,1},{6,22},{7,3},{8,24},{9,13},... | collective-permute-start | bytes 589832 | tf_op jit(solution)/shard_map/ppermute | solution.py:693
  94.1 12.0 %collective-permute-start.17 = (f32[8,2,24,128]{3,2,1,0:T(8,128)S(1)}, f32[8,2,24,128]{3,2,1,0:T(8,128)S(1)}, u32[]{:S(2)}, u32[]{:S(2)}) collective-permute-start(f32[8,2,24,128]{3,2,1,0:T(8,128)S(1)} %get-tuple-element.62), channel_id=1, source_target_pairs={{0,4},{1,17},{2,6},{3,19},{4,0},{5,21},{6,2},{7,23},{8,12},{9,25},... | collective-permute-start | bytes 589832 | tf_op jit(solution)/shard_map/ppermute | solution.py:693
  97.3 14.6 %collective-permute-start.18 = (f32[8,2,24,128]{3,2,1,0:T(8,128)S(1)}, f32[8,2,24,128]{3,2,1,0:T(8,128)S(1)}, u32[]{:S(2)}, u32[]{:S(2)}) collective-permute-start(f32[8,2,24,128]{3,2,1,0:T(8,128)S(1)} %get-tuple-element.63), channel_id=1, source_target_pairs={{0,8},{1,25},{2,10},{3,27},{4,12},{5,29},{6,14},{7,31},{8,0},{9,17... | collective-permute-start | bytes 589832 | tf_op jit(solution)/shard_map/ppermute | solution.py:693
  97.3 14.6 %collective-permute-start.19 = (f32[8,2,24,128]{3,2,1,0:T(8,128)S(1)}, f32[8,2,24,128]{3,2,1,0:T(8,128)S(1)}, u32[]{:S(2)}, u32[]{:S(2)}) collective-permute-start(f32[8,2,24,128]{3,2,1,0:T(8,128)S(1)} %get-tuple-element.64), channel_id=1, source_target_pairs={{0,24},{1,9},{2,26},{3,11},{4,28},{5,13},{6,30},{7,15},{8,16},{9,1... | collective-permute-start | bytes 589832 | tf_op jit(solution)/shard_map/ppermute | solution.py:693
  98.9 27.4 %collective-permute-start.20 = (f32[8,2,24,128]{3,2,1,0:T(8,128)S(1)}, f32[8,2,24,128]{3,2,1,0:T(8,128)S(1)}, u32[]{:S(2)}, u32[]{:S(2)}) collective-permute-start(f32[8,2,24,128]{3,2,1,0:T(8,128)S(1)} %get-tuple-element.65), channel_id=1, source_target_pairs={{0,20},{1,13},{2,22},{3,15},{4,16},{5,9},{6,18},{7,11},{8,28},{9,5... | collective-permute-start | bytes 589832 | tf_op jit(solution)/shard_map/ppermute | solution.py:693
  106.1 20.2 %collective-permute-start.21 = (f32[8,2,24,128]{3,2,1,0:T(8,128)S(1)}, f32[8,2,24,128]{3,2,1,0:T(8,128)S(1)}, u32[]{:S(2)}, u32[]{:S(2)}) collective-permute-start(f32[8,2,24,128]{3,2,1,0:T(8,128)S(1)} %get-tuple-element.66), channel_id=1, source_target_pairs={{0,12},{1,21},{2,14},{3,23},{4,8},{5,17},{6,10},{7,19},{8,4},{9,29... | collective-permute-start | bytes 589832 | tf_op jit(solution)/shard_map/ppermute | solution.py:693
  106.1 20.2 %collective-permute-start.22 = (f32[8,2,24,128]{3,2,1,0:T(8,128)S(1)}, f32[8,2,24,128]{3,2,1,0:T(8,128)S(1)}, u32[]{:S(2)}, u32[]{:S(2)}) collective-permute-start(f32[8,2,24,128]{3,2,1,0:T(8,128)S(1)} %get-tuple-element.67), channel_id=1, source_target_pairs={{0,28},{1,29},{2,30},{3,31},{4,24},{5,25},{6,26},{7,27},{8,20},{9,... | collective-permute-start | bytes 589832 | tf_op jit(solution)/shard_map/ppermute | solution.py:693
